TPU v7x, 32 devices: a whole 2x2x4 slice. The times are simulated.
32 devices in a mesh: kpt: 2 (over x), row: 16 (over z, y, core).
Axes of the slice: x: 2, y: 2, z: 4, core: 2. Of those that a mesh axis runs over, the one named last changes fastest.
Arguments:
- orbitals_zero: float32 [32768, 1024], P(('kpt', 'row')), parts along dimension 0, may hold values from -0.046875 to 0.046875
- orbitals_one: float32 [32768, 1024], P(('kpt', 'row')), parts along dimension 0, may hold values from -0.046875 to 0.046875
- correlation_zero: float32 [2048, 1024], P('kpt'), parts along dimension 0, as said below
- correlation_one: float32 [2048, 1024], P('kpt'), parts along dimension 0, as said below
- cotangent: float32 [32768, 1024], P(('kpt', 'row')), parts along dimension 0, may hold values from -6 to 6
Outputs:
- orbital_grad: float32 [32768, 1024], P(('kpt', 'row')), parts along dimension 0
There are 2 independent parts, one for each index of `kpt`. A program takes and returns all parts, laid end to end along the dimension named above; each array names one. Nothing has to cross between parts.
Inputs may be any that keep to these rules, and one draw needn't show every extreme that they name: `correlation_zero`: each correlation matrix is symmetric. `correlation_one`: each correlation matrix is symmetric.
All inputs are finite; a program needn't handle non-finite values.
Results may differ from a plain program's by a relative error of at most 0.000059.
Values sent between devices are 32-bit elements; how exact they have to be, the bound alone decides.
No kernel may reach another device: no remote copies, remote signals or barrier semaphores. Data moves between devices by JAX's collectives and lax.ppermute only.
A program may use at most 128 MiB of HBM per device.

v0:
```python
import functools
import jax
import jax.numpy as jnp
from jax import lax
from jax.experimental import pallas as pl
from jax.experimental.pallas import tpu as pltpu
from jax.sharding import PartitionSpec as P

F32 = jnp.float32
BF16 = jnp.bfloat16
B = 128
MIB = 1024 * 1024


def split(x):
    hi = x.astype(BF16)
    return hi, (x - hi.astype(F32)).astype(BF16)


def mm(a, b):
    (ah, al), (bh, bl) = a, b
    return jnp.dot(
        jnp.concatenate([ah, ah, al], axis=1),
        jnp.concatenate([bh, bl, bh], axis=0),
        preferred_element_type=F32,
    )


def call(kernel, name, out_shape, limit, products, arrays, **kw):
    size = 1024
    return pl.pallas_call(
        kernel,
        name=name,
        out_shape=out_shape,
        compiler_params=pltpu.CompilerParams(vmem_limit_bytes=limit * MIB),
        cost_estimate=pl.CostEstimate(
            flops=int(6 * products * size ** 3),
            bytes_accessed=int(4 * arrays * size * size),
            transcendentals=0,
        ),
        **kw,
    )


def struct(*shape, dtype=F32):
    return jax.ShapeDtypeStruct(shape, dtype)


SMEM = pl.BlockSpec(memory_space=pltpu.SMEM)
VMEM = pl.BlockSpec(memory_space=pltpu.VMEM)


def chunk_lines(size, chunk):
    half = size // B // 4
    return range(chunk * half, (chunk + 1) * half)


def line_blocks(size, i):
    n = size // B
    at = 0
    for top in (i, n - 1 - i):
        for j in range(top, n):
            yield at, slice(top * B, (top + 1) * B), slice(j * B, (j + 1) * B)
            at += B


def pack(g, packed, keep_ref, send_ref, me, shards, chunk):
    size = g.shape[0]
    rows = packed.shape[0] // shards
    per = B // rows
    for line, i in enumerate(chunk_lines(size, chunk)):
        for at, p, q in line_blocks(size, i):
            block = g[p, q] + g[q, p].T
            for s in range(per):
                slot = (line * per + s) ^ me
                packed[pl.ds(pl.multiple_of(slot * rows, rows), rows), at:at + B] = (
                    block[s * rows:(s + 1) * rows]
                )
    half = keep_ref.shape[0]
    keep_ref[...] = packed[:half]
    send_ref[...] = packed[half:]


def unpack(pieces, packed, hi, lo, me, shards, chunk):
    size = hi.shape[0]
    rows = packed.shape[0] // shards
    slot = 0
    for piece in pieces:
        for s in range(piece.shape[0] // rows):
            at = pl.multiple_of((slot ^ me) * rows, rows)
            packed[pl.ds(at, rows), :] = piece[s * rows:(s + 1) * rows, :]
            slot += 1
    for line, i in enumerate(chunk_lines(size, chunk)):
        for at, p, q in line_blocks(size, i):
            block = packed[line * B:(line + 1) * B, at:at + B]
            hi[p, q], lo[p, q] = split(block)
            if p.start != q.start:
                hi[q, p], lo[q, p] = split(block.T)


def packed_scratch(size):
    return pltpu.VMEM((size // 4, size + B), F32)


def halves(size):
    return [struct(size // 8, size + B)] * 2


def first_gram_kernel(
    shards, me_ref, a_hbm, b_hbm, keep_ref, send_ref, ah, al, bh, bl, a_buf, b_buf, sems, g, packed
):
    rows, size = a_buf.shape
    steps = sems.shape[1]
    tile = rows // steps
    copies = []
    for s in range(steps):
        r = slice(s * tile, (s + 1) * tile)
        pair = [
            pltpu.make_async_copy(src.at[r], dst.at[r], sems.at[k, s])
            for k, (src, dst) in enumerate([(a_hbm, a_buf), (b_hbm, b_buf)])
        ]
        for copy in pair:
            copy.start()
        copies.append((r, pair))
    for r, pair in copies:
        for copy in pair:
            copy.wait()
        ah[:, r], al[:, r] = split(a_buf[r].T)
        bh[r], bl[r] = split(b_buf[r])
    q = size // 4
    for r0, r1, c0, c1 in [(0, q, 0, size), (q, size, 0, q), (3 * q, size, 3 * q, size)]:
        g[r0:r1, c0:c1] = mm((ah[r0:r1, :], al[r0:r1, :]), (bh[:, c0:c1], bl[:, c0:c1]))
    pack(g, packed, keep_ref, send_ref, me_ref[0], shards, 0)


def first_gram(me, shards, a, b):
    rows, size = a.shape
    hbm = pl.BlockSpec(memory_space=pltpu.HBM)
    return call(
        functools.partial(first_gram_kernel, shards), "first_gram",
        halves(size) + [struct(size, rows, dtype=BF16)] * 2 + [struct(rows, size, dtype=BF16)] * 2,
        43, 0.5, 4,
        in_specs=[SMEM, hbm, hbm],
        out_specs=[VMEM] * 6,
        scratch_shapes=[
            pltpu.VMEM((rows, size), F32), pltpu.VMEM((rows, size), F32),
            pltpu.SemaphoreType.DMA((2, 4)),
            pltpu.VMEM((size, size), F32), packed_scratch(size),
        ],
    )(me, a, b)


def lower_product(g, ah, al, bh, bl):
    q = g.shape[0] // 4

    def step(r):
        t = pl.ds(pl.multiple_of(q + r.start, r.size), r.size)
        g[t, q:] = mm((ah[t], al[t]), (bh, bl))

    row_tiles(3 * q, q, step)


def other_gram_kernel(shards, me_ref, ah, al, bh, bl, keep_ref, send_ref, g, packed):
    q = g.shape[0] // 4
    lower_product(g, ah, al, bh[:, q:], bl[:, q:])
    pack(g, packed, keep_ref, send_ref, me_ref[0], shards, 1)


def other_gram(me, shards, ah, al, bh, bl):
    size = ah.shape[0]
    return call(
        functools.partial(other_gram_kernel, shards), "other_gram", halves(size), 22, 0.5, 2,
        in_specs=[SMEM] + [VMEM] * 4,
        out_specs=[VMEM, VMEM],
        scratch_shapes=[pltpu.VMEM((size, size), F32), packed_scratch(size)],
    )(me, ah, al, bh, bl)


def row_tiles(rows, tile, step):
    def body(t, _):
        step(pl.ds(pl.multiple_of(t * tile, tile), tile))
        return 0

    lax.fori_loop(0, rows // tile, body, 0)


def affine_kernel(a_ref, b_ref, out_ref, hi, lo):
    hi[...], lo[...] = split(b_ref[...])

    def step(r):
        a = a_ref[r]
        out_ref[r] = 1.5 * a - 0.5 * mm(split(a), (hi[...], lo[...]))

    row_tiles(a_ref.shape[0], 128, step)


def affine(a, b, part, parts):
    rows, size = a.shape
    height = rows // parts
    return call(
        affine_kernel, "affine", struct(height, size), 24, 1 / parts, 2,
        grid=(1,),
        in_specs=[
            pl.BlockSpec((height, size), lambda r: (part, 0)),
            pl.BlockSpec((size, size), lambda r: (0, 0)),
        ],
        out_specs=pl.BlockSpec((height, size), lambda r: (0, 0)),
        scratch_shapes=[pltpu.VMEM((size, size), BF16)] * 2,
    )(a, b)


def apply_first(a, base, hi, lo):
    size = hi.shape[0]
    q = size // 4
    part = lambda k0, k1, c0, c1: mm(
        (a[0][:, k0:k1], a[1][:, k0:k1]), (hi[k0:k1, c0:c1], lo[k0:k1, c0:c1])
    )
    wide = part(0, q, 0, size)
    left = part(q, size, 0, q)
    corner = part(3 * q, size, 3 * q, size)
    return jnp.concatenate(
        [
            base[:, :q] - 0.5 * (wide[:, :q] + left),
            base[:, q:3 * q] - 0.5 * wide[:, q:3 * q],
            base[:, 3 * q:] - 0.5 * (wide[:, 3 * q:] + corner),
        ],
        axis=1,
    )


def apply_parts(a_ref, base_refs, out_ref, hi, lo):
    at = 0
    for base_ref in base_refs:
        start = at

        def step(r):
            t = pl.ds(pl.multiple_of(start + r.start, r.size), r.size)
            out_ref[t] = apply_first(split(a_ref[t]), base_ref[r], hi, lo)

        row_tiles(base_ref.shape[0], 256, step)
        at += base_ref.shape[0]


def partial_kernel(shards, count, me_ref, *refs):
    pieces, refs = refs[:count], refs[count:]
    a_ref, base_refs, (out_ref, hi, lo, packed) = refs[0], refs[1:-4], refs[-4:]
    unpack(pieces, packed, hi, lo, me_ref[0], shards, 0)
    apply_parts(a_ref, base_refs, out_ref, hi, lo)


def partial_apply(me, shards, pieces, a, base):
    rows, size = a.shape
    return call(
        functools.partial(partial_kernel, shards, len(pieces)), "partial_apply",
        struct(rows, size), 20, 0.5, 3,
        in_specs=[SMEM] + [VMEM] * (len(pieces) + 1 + len(base)),
        out_specs=VMEM,
        scratch_shapes=[pltpu.VMEM((size, size), BF16)] * 2 + [packed_scratch(size)],
    )(me, *pieces, a, *base)


def early_kernel(shards, count, me_ref, *refs):
    pieces, refs = refs[:count], refs[count:]
    a_ref, base_refs, refs = refs[0], refs[1:-8], refs[-8:]
    x_ref, out_ref, xh, xl, col_ref, hi, lo, packed = refs
    unpack(pieces, packed, hi, lo, me_ref[0], shards, 0)
    apply_parts(a_ref, base_refs, out_ref, hi, lo)
    xh[...], xl[...] = split(x_ref[...].T)
    q = col_ref.shape[1]
    col = split(out_ref[:, :q])

    def step(r):
        col_ref[r] = mm((xh[r], xl[r]), col)

    row_tiles(col_ref.shape[0], 512, step)


def early_middle(me, shards, pieces, a, base, x):
    rows, size = a.shape
    part = struct(size, rows, dtype=BF16)
    return call(
        functools.partial(early_kernel, shards, len(pieces)), "early_middle",
        [struct(rows, size), part, part, struct(size, size // 4)], 22, 0.75, 5,
        in_specs=[SMEM] + [VMEM] * (len(pieces) + 2 + len(base)),
        out_specs=[VMEM] * 4,
        scratch_shapes=[pltpu.VMEM((size, size), BF16)] * 2 + [packed_scratch(size)],
    )(me, *pieces, a, *base, x)


def apply_second(a, base, hi, lo):
    size = hi.shape[0]
    q = size // 4
    part = lambda k1, c0, c1: mm(
        (a[0][:, q:k1], a[1][:, q:k1]), (hi[q:k1, c0:c1], lo[q:k1, c0:c1])
    )
    return jnp.concatenate(
        [base[:, q:3 * q] - 0.5 * part(size, q, 3 * q), base[:, 3 * q:] - 0.5 * part(3 * q, 3 * q, size)],
        axis=1,
    )


def second_gram_kernel(shards, count, me_ref, *refs):
    pieces, refs = refs[:count], refs[count:]
    a_ref, base_ref, xh, xl, col_ref, refs = refs[0], refs[1], refs[2], refs[3], refs[4], refs[5:]
    keep_ref, send_ref, mid_ref, mh, ml, hi, lo, g, packed = refs
    unpack(pieces, packed, hi, lo, me_ref[0], shards, 1)
    rows, size = a_ref.shape
    q = size // 4
    mid_ref[:, :q] = base_ref[:, :q]

    def step(t):
        mid = apply_second(split(a_ref[t]), base_ref[t], hi, lo)
        mid_ref[t, q:] = mid
        mh[t], ml[t] = split(mid)

    row_tiles(rows, 512, step)
    g[:, :q] = col_ref[...]
    g[:q, q:] = mm((xh[:q, :], xl[:q, :]), (mh[...], ml[...]))
    g[3 * q:, 3 * q:] = mm((xh[3 * q:, :], xl[3 * q:, :]), (mh[:, 2 * q:], ml[:, 2 * q:]))
    pack(g, packed, keep_ref, send_ref, me_ref[0], shards, 0)


def second_gram(me, shards, pieces, a, base, xh, xl, col):
    rows, size = a.shape
    part = struct(rows, size - size // 4, dtype=BF16)
    return call(
        functools.partial(second_gram_kernel, shards, len(pieces)), "second_gram",
        halves(size) + [struct(rows, size), part, part], 22, 0.8, 5,
        in_specs=[SMEM] + [VMEM] * (len(pieces) + 5),
        out_specs=[VMEM] * 5,
        scratch_shapes=[pltpu.VMEM((size, size), BF16)] * 2
        + [pltpu.VMEM((size, size), F32), packed_scratch(size)],
    )(me, *pieces, a, base, xh, xl, col)


def fourth_gram_kernel(shards, me_ref, xh, xl, mh, ml, keep_ref, send_ref, g, packed):
    lower_product(g, xh, xl, mh[...], ml[...])
    pack(g, packed, keep_ref, send_ref, me_ref[0], shards, 1)


def fourth_gram(me, shards, xh, xl, mh, ml):
    size = xh.shape[0]
    return call(
        functools.partial(fourth_gram_kernel, shards), "fourth_gram", halves(size), 22, 0.5, 2,
        in_specs=[SMEM] + [VMEM] * 4,
        out_specs=[VMEM, VMEM],
        scratch_shapes=[pltpu.VMEM((size, size), F32), packed_scratch(size)],
    )(me, xh, xl, mh, ml)


def last_kernel(shards, count, me_ref, *refs):
    pieces = refs[:count]
    x_ref, z_ref, out_ref, hi, lo, packed = refs[count:]
    size = hi.shape[0]
    q = size // 4

    @pl.when(pl.program_id(0) == 0)
    def _():
        unpack(pieces, packed, hi, lo, me_ref[0], shards, 1)

    a = split(x_ref[:, q:])
    out_ref[:, :q] = z_ref[:, :q]
    out_ref[:, q:3 * q] = z_ref[:, q:3 * q] - 0.5 * mm(a, (hi[q:, q:3 * q], lo[q:, q:3 * q]))
    a = (a[0][:, :2 * q], a[1][:, :2 * q])
    out_ref[:, 3 * q:] = z_ref[:, 3 * q:] - 0.5 * mm(a, (hi[q:3 * q, 3 * q:], lo[q:3 * q, 3 * q:]))


def last_step(me, shards, pieces, x, z):
    rows, size = x.shape
    tile = 256
    block = pl.BlockSpec((tile, size), lambda r: (r, 0))
    return call(
        functools.partial(last_kernel, shards, len(pieces)), "last", struct(rows, size), 20, 0.5, 3,
        grid=(rows // tile,),
        in_specs=[SMEM] + [pl.BlockSpec(p.shape, lambda r: (0, 0)) for p in pieces] + [block, block],
        out_specs=block,
        scratch_shapes=[pltpu.VMEM((size, size), BF16)] * 2 + [packed_scratch(size)],
    )(me, *pieces, x, z)


CORE = 1
PLANE = (2, 4, 6)
SHARDS = 2 * (1 + len(PLANE))


def slot_of(index):
    return (index % 2) * (SHARDS // 2) + (index // 2) % (SHARDS // 2)


class Sum:
    def __init__(self, count, keep, send):
        self.count, self.keep, self.send = count, keep, send

    def swap(self, x, offset):
        return lax.ppermute(x, "row", [(i, i ^ offset) for i in range(self.count)])

    def core(self):
        return self.swap(self.send, CORE)

    def plane(self, got):
        total = self.keep + got
        part = total.shape[0] // (1 + len(PLANE))
        self.keep, *sends = [total[k * part:(k + 1) * part] for k in range(1 + len(PLANE))]
        return [self.swap(x, offset) for x, offset in zip(sends, PLANE)]

    def own(self, got):
        self.keep = sum(got, self.keep)

    def exchange(self, offset):
        return self.swap(self.keep, offset)

    def gather_plane(self):
        return [self.swap(self.keep, offset) for offset in PLANE]

    def gather_core(self, got):
        self.mine = jnp.concatenate([self.keep, *got], axis=0)
        return self.swap(self.mine, CORE)


def close(env, *got):
    values = lax.optimization_barrier((*got, *env.values()))
    env.update(zip(env, values[len(got):]))
    return values[:len(got)]


def sum_chunks(count, env, first, second, works, late):
    beyond = [1 << s for s in range(3, count.bit_length() - 1)]
    works = list(works)

    def work():
        if works:
            works.pop(0)(env)

    a = Sum(count, *first)
    got_a = a.core()
    pair = second(env)
    got_a, *pair = close(env, got_a, *pair)
    b = Sum(count, *pair)

    got_a = a.plane(got_a)
    got_b = b.core()
    work()
    (got_b,) = close(env, got_b)

    got_b = b.plane(got_b)
    work()
    a.own(close(env, *got_a))

    for offset in beyond:
        got_a = a.exchange(offset)
        b.own(close(env, *got_b))
        got_b = [b.exchange(offset)]
        a.own(close(env, got_a))

    got_a = a.gather_plane()
    b.own(close(env, *got_b))

    got_b = b.gather_plane()
    work()
    *got_a, got_b[0] = close(env, *got_a, got_b[0])
    got_a = a.gather_core(got_a)
    pieces_a = [a.mine, *close(env, got_a)]
    late(env, pieces_a)
    got_b = b.gather_core(close(env, *got_b))
    return pieces_a, [b.mine, got_b]


def body(count, orbitals_zero, orbitals_one, correlation_zero, correlation_one, cotangent):
    me = slot_of(lax.axis_index("row")).astype(jnp.int32).reshape(1)
    env = dict(
        x0=orbitals_zero, x1=orbitals_one, s0=correlation_zero, s1=correlation_one, c=cotangent
    )

    def thirds(name, left, right):
        def put(at, part, parts):
            def work(env):
                env[f"{name}{at}"] = affine(env[left], env[right], part, parts)
            return work
        return [put(0, 0, 2), put(1, 2, 4), put(2, 3, 4)]

    def three(env, name):
        return [env[f"{name}{at}"] for at in range(3)]

    def early(env, pieces):
        env["mid"], env["xh"], env["xl"], env["col"] = early_middle(
            me, SHARDS, pieces, env["x1"], three(env, "m"), env["x0"]
        )

    keep, send, *parts = first_gram(me, SHARDS, env["x1"], env["c"])
    _, one = sum_chunks(
        count, env, (keep, send), lambda env: other_gram(me, SHARDS, *parts),
        thirds("m", "c", "s1"), early,
    )

    keep, send, env["mid"], mh, ml = second_gram(
        me, SHARDS, one, env["x1"], env["mid"], env["xh"], env["xl"], env["col"]
    )

    def late(env, pieces):
        env["z"] = partial_apply(me, SHARDS, pieces, env["x0"], three(env, "d"))

    _, two = sum_chunks(
        count, env, (keep, send),
        lambda env: fourth_gram(me, SHARDS, env["xh"], env["xl"], mh, ml),
        thirds("d", "mid", "s0"), late,
    )
    return last_step(me, SHARDS, two, env["x0"], env["z"])


def solution(mesh):
    in_specs = (
        P(("kpt", "row"), None),
        P(("kpt", "row"), None),
        P("kpt", None),
        P("kpt", None),
        P(("kpt", "row"), None),
    )
    out_specs = P(("kpt", "row"), None)
    return jax.shard_map(
        functools.partial(body, mesh.shape["row"]),
        mesh=mesh, in_specs=in_specs, out_specs=out_specs, check_vma=False,
    )
```

profile of v0, /device:TPU:0, one launch (start us, length us, event | category | flops | bytes accessed | tf_op | source)
XLA Modules:
  0.0 133.3 jit_solution(9995418231904861361)
XLA Ops:
  0.0 7.2 %first_gram.1 = (f32[128,1152]{1,0:T(8,128)S(1)}, f32[128,1152]{1,0:T(8,128)S(1)}, bf16[1024,1024]{1,0:T(8,128)(2,1)S(1)}, bf16[1024,1024]{1,0:T(8,128)(2,1)S(1)...) custom-call(s32[1]{0:T(128)} %bitcast.me_ref, f32[1024,1024]{1,0:T(8,128)} %refs_2_.1, f32[1024,1024]{1,0:T(8,128)} %a_ref.2), custom_call_target="tpu_custom_call" | custom-call | flops 3221225472 | bytes 16777216 | tf_op jit(solution)/shard_map/first_gram/pallas_call | solution.py:139
  7.8 5.1 %other_gram.1 = (f32[128,1152]{1,0:T(8,128)S(1)}, f32[128,1152]{1,0:T(8,128)S(1)}) custom-call(s32[1]{0:T(128)} %bitcast.me_ref, bf16[1024,1024]{1,0:T(8,128)(2,1)S(1)} %get-tuple-element.160.ah, bf16[1024,1024]{1,0:T(8,128)(2,1)S(1)} %get-tuple-element.161.al, bf16[1024,1024]{1,0:T(8,128)(2,1)S(1)} %get-tuple-element.162.bh, ...), custom_call_target="tpu_custom_call" | custom-call | flops 3221225472 | bytes 8388608 | tf_op jit(solution)/shard_map/other_gram/pallas_call | solution.py:171
  13.1 4.0 %collective-permute-start.7 = (f32[32,1152]{1,0:T(8,128)S(1)}, f32[32,1152]{1,0:T(8,128)S(1)}, u32[]{:S(2)}, u32[]{:S(2)}) collective-permute-start(f32[32,1152]{1,0:T(8,128)S(1)} %get-tuple-element.322), channel_id=1, source_target_pairs={{0,6},{1,7},{2,4},{3,5},{4,2},{5,3},{6,0},{7,1},{8,14},{9,15},{10,... | collective-permute-start | bytes 442376 | tf_op jit(solution)/shard_map/ppermute | solution.py:395
  17.8 4.7 %affine.6.refs_3_ = f32[512,1024]{1,0:T(8,128)S(1)} custom-call(f32[1024,1024]{1,0:T(8,128)S(1)} %copy-done, f32[1024,1024]{1,0:T(8,128)S(1)} %copy-done.1), custom_call_target="tpu_custom_call" | custom-call | flops 3221225472 | bytes 8388608 | tf_op jit(solution)/shard_map/affine/pallas_call | solution.py:200
  22.6 2.9 %collective-permute-start.4 = (f32[32,1152]{1,0:T(8,128)S(1)}, f32[32,1152]{1,0:T(8,128)S(1)}, u32[]{:S(2)}, u32[]{:S(2)}) collective-permute-start(f32[32,1152]{1,0:T(8,128)S(1)} %get-tuple-element.319), channel_id=1, source_target_pairs={{0,6},{1,7},{2,4},{3,5},{4,2},{5,3},{6,0},{7,1},{8,14},{9,15},{10,... | collective-permute-start | bytes 442376 | tf_op jit(solution)/shard_map/ppermute | solution.py:395
  26.0 2.7 %affine.7.refs_4_ = f32[256,1024]{1,0:T(8,128)S(1)} custom-call(f32[1024,1024]{1,0:T(8,128)S(1)} %copy-done, f32[1024,1024]{1,0:T(8,128)S(1)} %copy-done.1), custom_call_target="tpu_custom_call" | custom-call | flops 1610612736 | bytes 8388608 | tf_op jit(solution)/shard_map/affine/pallas_call | solution.py:200
  29.0 3.0 %collective-permute-start.9 = (f32[32,1152]{1,0:T(8,128)S(1)}, f32[32,1152]{1,0:T(8,128)S(1)}, u32[]{:S(2)}, u32[]{:S(2)}) collective-permute-start(f32[32,1152]{1,0:T(8,128)S(1)} %fusion.5), channel_id=1, source_target_pairs={{0,8},{1,9},{2,10},{3,11},{4,12},{5,13},{6,14},{7,15},{8,0},{9,1},... | collective-permute-start | bytes 442376 | tf_op jit(solution)/shard_map/ppermute | solution.py:395
  32.0 1.8 %collective-permute-done.3 = f32[32,1152]{1,0:T(8,128)S(1)} collective-permute-done((f32[32,1152]{1,0:T(8,128)S(1)}, f32[32,1152]{1,0:T(8,128)S(1)}, u32[]{:S(2)}, u32[]{:S(2)}) %collective-permute-start.3) | collective-permute-done | bytes 147488 | tf_op jit(solution)/shard_map/ppermute | solution.py:395
  33.9 2.6 %collective-permute-start.8 = (f32[32,1152]{1,0:T(8,128)S(1)}, f32[32,1152]{1,0:T(8,128)S(1)}, u32[]{:S(2)}, u32[]{:S(2)}) collective-permute-start(f32[32,1152]{1,0:T(8,128)S(1)} %fusion.7), channel_id=1, source_target_pairs={{0,8},{1,9},{2,10},{3,11},{4,12},{5,13},{6,14},{7,15},{8,0},{9,1},... | collective-permute-start | bytes 442376 | tf_op jit(solution)/shard_map/ppermute | solution.py:395
  36.6 4.7 %collective-permute-done.9 = f32[32,1152]{1,0:T(8,128)S(1)} collective-permute-done((f32[32,1152]{1,0:T(8,128)S(1)}, f32[32,1152]{1,0:T(8,128)S(1)}, u32[]{:S(2)}, u32[]{:S(2)}) %collective-permute-start.9) | collective-permute-done | bytes 147488 | tf_op jit(solution)/shard_map/ppermute | solution.py:395
  41.3 2.3 %collective-permute-start.12 = (f32[32,1152]{1,0:T(8,128)S(1)}, f32[32,1152]{1,0:T(8,128)S(1)}, u32[]{:S(2)}, u32[]{:S(2)}) collective-permute-start(f32[32,1152]{1,0:T(8,128)S(1)} %add.83), channel_id=1, source_target_pairs={{0,6},{1,7},{2,4},{3,5},{4,2},{5,3},{6,0},{7,1},{8,14},{9,15},{10,... | collective-permute-start | bytes 442376 | tf_op jit(solution)/shard_map/ppermute | solution.py:395
  43.6 1.9 %collective-permute-start.11 = (f32[32,1152]{1,0:T(8,128)S(1)}, f32[32,1152]{1,0:T(8,128)S(1)}, u32[]{:S(2)}, u32[]{:S(2)}) collective-permute-start(f32[32,1152]{1,0:T(8,128)S(1)} %add.83), channel_id=1, source_target_pairs={{0,4},{1,5},{2,6},{3,7},{4,0},{5,1},{6,2},{7,3},{8,12},{9,13},{10,... | collective-permute-start | bytes 442376 | tf_op jit(solution)/shard_map/ppermute | solution.py:395
  45.6 2.1 %collective-permute-start.13 = (f32[32,1152]{1,0:T(8,128)S(1)}, f32[32,1152]{1,0:T(8,128)S(1)}, u32[]{:S(2)}, u32[]{:S(2)}) collective-permute-start(f32[32,1152]{1,0:T(8,128)S(1)} %add.82), channel_id=1, source_target_pairs={{0,2},{1,3},{2,0},{3,1},{4,6},{5,7},{6,4},{7,5},{8,10},{9,11},{10,... | collective-permute-start | bytes 442376 | tf_op jit(solution)/shard_map/ppermute | solution.py:395
  47.7 2.7 %affine.8.refs_5_ = f32[256,1024]{1,0:T(8,128)S(1)} custom-call(f32[1024,1024]{1,0:T(8,128)S(1)} %copy-done, f32[1024,1024]{1,0:T(8,128)S(1)} %copy-done.1), custom_call_target="tpu_custom_call" | custom-call | flops 1610612736 | bytes 8388608 | tf_op jit(solution)/shard_map/affine/pallas_call | solution.py:200
  55.1 7.0 %early_middle.1 = (f32[1024,1024]{1,0:T(8,128)S(1)}, bf16[1024,1024]{1,0:T(8,128)(2,1)S(1)}, bf16[1024,1024]{1,0:T(8,128)(2,1)S(1)}, f32[1024,256]{1,0:T(8,128)S(1)}) custom-call(s32[1]{0:T(128)} %bitcast.me_ref, f32[128,1152]{1,0:T(8,128)S(1)} %pad_maximum_fusion.refs_0_, f32[128,1152]{1,0:T(8,128)S(1)} %collective-permute-done.16.refs_1_, ...), custom_call_target="tpu_custom_call" | custom-call | flops 4831838208 | bytes 20971520 | tf_op jit(solution)/shard_map/early_middle/pallas_call | solution.py:281
  62.6 2.0 %collective-permute-done.17.refs_1_ = f32[128,1152]{1,0:T(8,128)S(1)} collective-permute-done((f32[128,1152]{1,0:T(8,128)S(1)}, f32[128,1152]{1,0:T(8,128)S(1)}, u32[]{:S(2)}, u32[]{:S(2)}) %collective-permute-start.17) | collective-permute-done | bytes 589856 | tf_op jit(solution)/shard_map/ppermute | solution.py:395
  64.5 6.4 %second_gram.1 = (f32[128,1152]{1,0:T(8,128)S(1)}, f32[128,1152]{1,0:T(8,128)S(1)}, f32[1024,1024]{1,0:T(8,128)S(1)}, bf16[1024,768]{1,0:T(8,128)(2,1)S(1)}, bf16[1024,768]{1,0:T(8,128)(2,1)S(1)}) custom-call(s32[1]{0:T(128)} %bitcast.me_ref, f32[128,1152]{1,0:T(8,128)S(1)} %pad_maximum_fusion.1.refs_0_, f32[128,1152]{1,0:T(8,128)S(1)} %collective-permute-done.17.refs_1_, ...), custom_call_target="tpu_custom_call" | custom-call | flops 5153960960 | bytes 20971520 | tf_op jit(solution)/shard_map/second_gram/pallas_call | solution.py:326
  71.1 4.9 %fourth_gram.1 = (f32[128,1152]{1,0:T(8,128)S(1)}, f32[128,1152]{1,0:T(8,128)S(1)}) custom-call(s32[1]{0:T(128)} %bitcast.me_ref, bf16[1024,1024]{1,0:T(8,128)(2,1)S(1)} %get-tuple-element.244.refs_4_.xh, bf16[1024,1024]{1,0:T(8,128)(2,1)S(1)} %get-tuple-element.245.refs_5_.xl, bf16[1024,768]{1,0:T(8,128)(2,1)S(1)} %get-tuple-element.248.mh, ...), custom_call_target="tpu_custom_call" | custom-call | flops 3221225472 | bytes 8388608 | tf_op jit(solution)/shard_map/fourth_gram/pallas_call | solution.py:343
  77.4 1.7 %collective-permute-start.24 = (f32[32,1152]{1,0:T(8,128)S(1)}, f32[32,1152]{1,0:T(8,128)S(1)}, u32[]{:S(2)}, u32[]{:S(2)}) collective-permute-start(f32[32,1152]{1,0:T(8,128)S(1)} %get-tuple-element.317), channel_id=1, source_target_pairs={{0,4},{1,5},{2,6},{3,7},{4,0},{5,1},{6,2},{7,3},{8,12},{9,13},{10,... | collective-permute-start | bytes 442376 | tf_op jit(solution)/shard_map/ppermute | solution.py:395
  80.1 4.9 %affine.9.refs_3_ = f32[512,1024]{1,0:T(8,128)S(1)} custom-call(f32[1024,1024]{1,0:T(8,128)S(1)} %get-tuple-element.292.a_ref, f32[1024,1024]{1,0:T(8,128)S(1)} %copy-done.2), custom_call_target="tpu_custom_call" | custom-call | flops 3221225472 | bytes 8388608 | tf_op jit(solution)/shard_map/affine/pallas_call | solution.py:200
  86.0 1.7 %collective-permute-start.21 = (f32[32,1152]{1,0:T(8,128)S(1)}, f32[32,1152]{1,0:T(8,128)S(1)}, u32[]{:S(2)}, u32[]{:S(2)}) collective-permute-start(f32[32,1152]{1,0:T(8,128)S(1)} %get-tuple-element.314), channel_id=1, source_target_pairs={{0,4},{1,5},{2,6},{3,7},{4,0},{5,1},{6,2},{7,3},{8,12},{9,13},{10,... | collective-permute-start | bytes 442376 | tf_op jit(solution)/shard_map/ppermute | solution.py:395
  87.7 2.8 %affine.10.refs_4_ = f32[256,1024]{1,0:T(8,128)S(1)} custom-call(f32[1024,1024]{1,0:T(8,128)S(1)} %get-tuple-element.292.a_ref, f32[1024,1024]{1,0:T(8,128)S(1)} %copy-done.2), custom_call_target="tpu_custom_call" | custom-call | flops 1610612736 | bytes 8388608 | tf_op jit(solution)/shard_map/affine/pallas_call | solution.py:200
  91.6 3.6 %collective-permute-start.27 = (f32[32,1152]{1,0:T(8,128)S(1)}, f32[32,1152]{1,0:T(8,128)S(1)}, u32[]{:S(2)}, u32[]{:S(2)}) collective-permute-start(f32[32,1152]{1,0:T(8,128)S(1)} %fusion.1), channel_id=1, source_target_pairs={{0,8},{1,9},{2,10},{3,11},{4,12},{5,13},{6,14},{7,15},{8,0},{9,1},... | collective-permute-start | bytes 442376 | tf_op jit(solution)/shard_map/ppermute | solution.py:395
  95.7 3.7 %collective-permute-start.26 = (f32[32,1152]{1,0:T(8,128)S(1)}, f32[32,1152]{1,0:T(8,128)S(1)}, u32[]{:S(2)}, u32[]{:S(2)}) collective-permute-start(f32[32,1152]{1,0:T(8,128)S(1)} %fusion.3), channel_id=1, source_target_pairs={{0,8},{1,9},{2,10},{3,11},{4,12},{5,13},{6,14},{7,15},{8,0},{9,1},... | collective-permute-start | bytes 442376 | tf_op jit(solution)/shard_map/ppermute | solution.py:395
  99.5 5.3 %collective-permute-done.27 = f32[32,1152]{1,0:T(8,128)S(1)} collective-permute-done((f32[32,1152]{1,0:T(8,128)S(1)}, f32[32,1152]{1,0:T(8,128)S(1)}, u32[]{:S(2)}, u32[]{:S(2)}) %collective-permute-start.27) | collective-permute-done | bytes 147488 | tf_op jit(solution)/shard_map/ppermute | solution.py:395
  104.8 1.7 %collective-permute-start.30 = (f32[32,1152]{1,0:T(8,128)S(1)}, f32[32,1152]{1,0:T(8,128)S(1)}, u32[]{:S(2)}, u32[]{:S(2)}) collective-permute-start(f32[32,1152]{1,0:T(8,128)S(1)} %add.93), channel_id=1, source_target_pairs={{0,6},{1,7},{2,4},{3,5},{4,2},{5,3},{6,0},{7,1},{8,14},{9,15},{10,... | collective-permute-start | bytes 442376 | tf_op jit(solution)/shard_map/ppermute | solution.py:395
  108.3 1.9 %collective-permute-start.31 = (f32[32,1152]{1,0:T(8,128)S(1)}, f32[32,1152]{1,0:T(8,128)S(1)}, u32[]{:S(2)}, u32[]{:S(2)}) collective-permute-start(f32[32,1152]{1,0:T(8,128)S(1)} %add.92), channel_id=1, source_target_pairs={{0,2},{1,3},{2,0},{3,1},{4,6},{5,7},{6,4},{7,5},{8,10},{9,11},{10,... | collective-permute-start | bytes 442376 | tf_op jit(solution)/shard_map/ppermute | solution.py:395
  110.2 3.0 %affine.11.refs_5_ = f32[256,1024]{1,0:T(8,128)S(1)} custom-call(f32[1024,1024]{1,0:T(8,128)S(1)} %get-tuple-element.292.a_ref, f32[1024,1024]{1,0:T(8,128)S(1)} %copy-done.2), custom_call_target="tpu_custom_call" | custom-call | flops 1610612736 | bytes 8388608 | tf_op jit(solution)/shard_map/affine/pallas_call | solution.py:200
  113.3 1.9 %collective-permute-done.28 = f32[32,1152]{1,0:T(8,128)S(1)} collective-permute-done((f32[32,1152]{1,0:T(8,128)S(1)}, f32[32,1152]{1,0:T(8,128)S(1)}, u32[]{:S(2)}, u32[]{:S(2)}) %collective-permute-start.28) | collective-permute-done | bytes 147488 | tf_op jit(solution)/shard_map/ppermute | solution.py:395
  118.9 4.4 %partial_apply.1.refs_3_ = f32[1024,1024]{1,0:T(8,128)S(1)} custom-call(s32[1]{0:T(128)} %bitcast.me_ref, f32[128,1152]{1,0:T(8,128)S(1)} %pad_maximum_fusion.2.refs_0_, f32[128,1152]{1,0:T(8,128)S(1)} %collective-permute-done.34.refs_1_, f32[1024,1024]{1,0:T(8,128)S(1)} %copy-done.3, f32[512,1024]{1,0:T(8,128)S(1)} %affine.9.refs_3_, ...), custom_call_target="tpu_custom_call" | custom-call | flops 3221225472 | bytes 12582912 | tf_op jit(solution)/shard_map/partial_apply/pallas_call | solution.py:253
  125.8 2.0 %collective-permute-done.35.refs_1_ = f32[128,1152]{1,0:T(8,128)S(1)} collective-permute-done((f32[128,1152]{1,0:T(8,128)S(1)}, f32[128,1152]{1,0:T(8,128)S(1)}, u32[]{:S(2)}, u32[]{:S(2)}) %collective-permute-start.35) | collective-permute-done | bytes 589856 | tf_op jit(solution)/shard_map/ppermute | solution.py:395
  127.8 5.6 %last.1 = f32[1024,1024]{1,0:T(8,128)} custom-call(s32[1]{0:T(128)} %bitcast.me_ref, f32[128,1152]{1,0:T(8,128)S(1)} %pad_maximum_fusion.3.refs_0_, f32[128,1152]{1,0:T(8,128)S(1)} %collective-permute-done.35.refs_1_, f32[1024,1024]{1,0:T(8,128)S(1)} %copy-done.3, f32[1024,1024]{1,0:T(8,128)S(1)} %partial_apply.1.refs_3_), custom_call_target="tpu_custom_call" | custom-call | flops 3221225472 | bytes 12582912 | tf_op jit(solution)/shard_map/last/pallas_call | solution.py:372
  (83 shorter events, 20.8 us)
Async XLA Ops:
  7.2 5.6 %collective-permute-start = (f32[128,1152]{1,0:T(8,128)S(1)}, f32[128,1152]{1,0:T(8,128)S(1)}, u32[]{:S(2)}, u32[]{:S(2)}) collective-permute-start(f32[128,1152]{1,0:T(8,128)S(1)} %get-tuple-element.159), channel_id=1, source_target_pairs={{0,1},{1,0},{2,3},{3,2},{4,5},{5,4},{6,7},{7,6},{8,9},{9,8},{10,11... | collective-permute-start | bytes 1769480 | tf_op jit(solution)/shard_map/ppermute | solution.py:395
  12.8 9.6 %collective-permute-start.1 = (f32[128,1152]{1,0:T(8,128)S(1)}, f32[128,1152]{1,0:T(8,128)S(1)}, u32[]{:S(2)}, u32[]{:S(2)}) collective-permute-start(f32[128,1152]{1,0:T(8,128)S(1)} %get-tuple-element.167), channel_id=1, source_target_pairs={{0,1},{1,0},{2,3},{3,2},{4,5},{5,4},{6,7},{7,6},{8,9},{9,8},{10,11... | collective-permute-start | bytes 1769480 | tf_op jit(solution)/shard_map/ppermute | solution.py:395
  13.1 15.6 %collective-permute-start.7 = (f32[32,1152]{1,0:T(8,128)S(1)}, f32[32,1152]{1,0:T(8,128)S(1)}, u32[]{:S(2)}, u32[]{:S(2)}) collective-permute-start(f32[32,1152]{1,0:T(8,128)S(1)} %get-tuple-element.322), channel_id=1, source_target_pairs={{0,6},{1,7},{2,4},{3,5},{4,2},{5,3},{6,0},{7,1},{8,14},{9,15},{10,... | collective-permute-start | bytes 442376 | tf_op jit(solution)/shard_map/ppermute | solution.py:395
  17.1 11.8 %collective-permute-start.6 = (f32[32,1152]{1,0:T(8,128)S(1)}, f32[32,1152]{1,0:T(8,128)S(1)}, u32[]{:S(2)}, u32[]{:S(2)}) collective-permute-start(f32[32,1152]{1,0:T(8,128)S(1)} %get-tuple-element.323), channel_id=1, source_target_pairs={{0,4},{1,5},{2,6},{3,7},{4,0},{5,1},{6,2},{7,3},{8,12},{9,13},{10,... | collective-permute-start | bytes 442376 | tf_op jit(solution)/shard_map/ppermute | solution.py:395
  17.6 11.4 %collective-permute-start.5 = (f32[32,1152]{1,0:T(8,128)S(1)}, f32[32,1152]{1,0:T(8,128)S(1)}, u32[]{:S(2)}, u32[]{:S(2)}) collective-permute-start(f32[32,1152]{1,0:T(8,128)S(1)} %get-tuple-element.324), channel_id=1, source_target_pairs={{0,2},{1,3},{2,0},{3,1},{4,6},{5,7},{6,4},{7,5},{8,10},{9,11},{10,... | collective-permute-start | bytes 442376 | tf_op jit(solution)/shard_map/ppermute | solution.py:395
  22.6 9.4 %collective-permute-start.4 = (f32[32,1152]{1,0:T(8,128)S(1)}, f32[32,1152]{1,0:T(8,128)S(1)}, u32[]{:S(2)}, u32[]{:S(2)}) collective-permute-start(f32[32,1152]{1,0:T(8,128)S(1)} %get-tuple-element.319), channel_id=1, source_target_pairs={{0,6},{1,7},{2,4},{3,5},{4,2},{5,3},{6,0},{7,1},{8,14},{9,15},{10,... | collective-permute-start | bytes 442376 | tf_op jit(solution)/shard_map/ppermute | solution.py:395
  25.5 8.2 %collective-permute-start.3 = (f32[32,1152]{1,0:T(8,128)S(1)}, f32[32,1152]{1,0:T(8,128)S(1)}, u32[]{:S(2)}, u32[]{:S(2)}) collective-permute-start(f32[32,1152]{1,0:T(8,128)S(1)} %get-tuple-element.320), channel_id=1, source_target_pairs={{0,4},{1,5},{2,6},{3,7},{4,0},{5,1},{6,2},{7,3},{8,12},{9,13},{10,... | collective-permute-start | bytes 442376 | tf_op jit(solution)/shard_map/ppermute | solution.py:395
  28.7 5.2 %collective-permute-start.2 = (f32[32,1152]{1,0:T(8,128)S(1)}, f32[32,1152]{1,0:T(8,128)S(1)}, u32[]{:S(2)}, u32[]{:S(2)}) collective-permute-start(f32[32,1152]{1,0:T(8,128)S(1)} %get-tuple-element.321), channel_id=1, source_target_pairs={{0,2},{1,3},{2,0},{3,1},{4,6},{5,7},{6,4},{7,5},{8,10},{9,11},{10,... | collective-permute-start | bytes 442376 | tf_op jit(solution)/shard_map/ppermute | solution.py:395
  29.0 12.3 %collective-permute-start.9 = (f32[32,1152]{1,0:T(8,128)S(1)}, f32[32,1152]{1,0:T(8,128)S(1)}, u32[]{:S(2)}, u32[]{:S(2)}) collective-permute-start(f32[32,1152]{1,0:T(8,128)S(1)} %fusion.5), channel_id=1, source_target_pairs={{0,8},{1,9},{2,10},{3,11},{4,12},{5,13},{6,14},{7,15},{8,0},{9,1},... | collective-permute-start | bytes 442376 | tf_op jit(solution)/shard_map/ppermute | solution.py:395
  33.9 11.6 %collective-permute-start.8 = (f32[32,1152]{1,0:T(8,128)S(1)}, f32[32,1152]{1,0:T(8,128)S(1)}, u32[]{:S(2)}, u32[]{:S(2)}) collective-permute-start(f32[32,1152]{1,0:T(8,128)S(1)} %fusion.7), channel_id=1, source_target_pairs={{0,8},{1,9},{2,10},{3,11},{4,12},{5,13},{6,14},{7,15},{8,0},{9,1},... | collective-permute-start | bytes 442376 | tf_op jit(solution)/shard_map/ppermute | solution.py:395
  41.3 9.0 %collective-permute-start.12 = (f32[32,1152]{1,0:T(8,128)S(1)}, f32[32,1152]{1,0:T(8,128)S(1)}, u32[]{:S(2)}, u32[]{:S(2)}) collective-permute-start(f32[32,1152]{1,0:T(8,128)S(1)} %add.83), channel_id=1, source_target_pairs={{0,6},{1,7},{2,4},{3,5},{4,2},{5,3},{6,0},{7,1},{8,14},{9,15},{10,... | collective-permute-start | bytes 442376 | tf_op jit(solution)/shard_map/ppermute | solution.py:395
  43.6 6.8 %collective-permute-start.11 = (f32[32,1152]{1,0:T(8,128)S(1)}, f32[32,1152]{1,0:T(8,128)S(1)}, u32[]{:S(2)}, u32[]{:S(2)}) collective-permute-start(f32[32,1152]{1,0:T(8,128)S(1)} %add.83), channel_id=1, source_target_pairs={{0,4},{1,5},{2,6},{3,7},{4,0},{5,1},{6,2},{7,3},{8,12},{9,13},{10,... | collective-permute-start | bytes 442376 | tf_op jit(solution)/shard_map/ppermute | solution.py:395
  45.5 5.4 %collective-permute-start.10 = (f32[32,1152]{1,0:T(8,128)S(1)}, f32[32,1152]{1,0:T(8,128)S(1)}, u32[]{:S(2)}, u32[]{:S(2)}) collective-permute-start(f32[32,1152]{1,0:T(8,128)S(1)} %add.83), channel_id=1, source_target_pairs={{0,2},{1,3},{2,0},{3,1},{4,6},{5,7},{6,4},{7,5},{8,10},{9,11},{10,... | collective-permute-start | bytes 442376 | tf_op jit(solution)/shard_map/ppermute | solution.py:395
  45.6 6.9 %collective-permute-start.13 = (f32[32,1152]{1,0:T(8,128)S(1)}, f32[32,1152]{1,0:T(8,128)S(1)}, u32[]{:S(2)}, u32[]{:S(2)}) collective-permute-start(f32[32,1152]{1,0:T(8,128)S(1)} %add.82), channel_id=1, source_target_pairs={{0,2},{1,3},{2,0},{3,1},{4,6},{5,7},{6,4},{7,5},{8,10},{9,11},{10,... | collective-permute-start | bytes 442376 | tf_op jit(solution)/shard_map/ppermute | solution.py:395
  52.6 9.5 %collective-permute-start.15 = (f32[32,1152]{1,0:T(8,128)S(1)}, f32[32,1152]{1,0:T(8,128)S(1)}, u32[]{:S(2)}, u32[]{:S(2)}) collective-permute-start(f32[32,1152]{1,0:T(8,128)S(1)} %add.82), channel_id=1, source_target_pairs={{0,6},{1,7},{2,4},{3,5},{4,2},{5,3},{6,0},{7,1},{8,14},{9,15},{10,... | collective-permute-start | bytes 442376 | tf_op jit(solution)/shard_map/ppermute | solution.py:395
  53.7 8.8 %collective-permute-start.14 = (f32[32,1152]{1,0:T(8,128)S(1)}, f32[32,1152]{1,0:T(8,128)S(1)}, u32[]{:S(2)}, u32[]{:S(2)}) collective-permute-start(f32[32,1152]{1,0:T(8,128)S(1)} %add.82), channel_id=1, source_target_pairs={{0,4},{1,5},{2,6},{3,7},{4,0},{5,1},{6,2},{7,3},{8,12},{9,13},{10,... | collective-permute-start | bytes 442376 | tf_op jit(solution)/shard_map/ppermute | solution.py:395
  70.9 5.1 %collective-permute-start.18 = (f32[128,1152]{1,0:T(8,128)S(1)}, f32[128,1152]{1,0:T(8,128)S(1)}, u32[]{:S(2)}, u32[]{:S(2)}) collective-permute-start(f32[128,1152]{1,0:T(8,128)S(1)} %get-tuple-element.247), channel_id=1, source_target_pairs={{0,1},{1,0},{2,3},{3,2},{4,5},{5,4},{6,7},{7,6},{8,9},{9,8},{10,11... | collective-permute-start | bytes 1769480 | tf_op jit(solution)/shard_map/ppermute | solution.py:395
  76.0 9.0 %collective-permute-start.19 = (f32[128,1152]{1,0:T(8,128)S(1)}, f32[128,1152]{1,0:T(8,128)S(1)}, u32[]{:S(2)}, u32[]{:S(2)}) collective-permute-start(f32[128,1152]{1,0:T(8,128)S(1)} %get-tuple-element.256), channel_id=1, source_target_pairs={{0,1},{1,0},{2,3},{3,2},{4,5},{5,4},{6,7},{7,6},{8,9},{9,8},{10,11... | collective-permute-start | bytes 1769480 | tf_op jit(solution)/shard_map/ppermute | solution.py:395
  76.6 13.9 %collective-permute-start.25 = (f32[32,1152]{1,0:T(8,128)S(1)}, f32[32,1152]{1,0:T(8,128)S(1)}, u32[]{:S(2)}, u32[]{:S(2)}) collective-permute-start(f32[32,1152]{1,0:T(8,128)S(1)} %get-tuple-element.316), channel_id=1, source_target_pairs={{0,6},{1,7},{2,4},{3,5},{4,2},{5,3},{6,0},{7,1},{8,14},{9,15},{10,... | collective-permute-start | bytes 442376 | tf_op jit(solution)/shard_map/ppermute | solution.py:395
  77.4 14.1 %collective-permute-start.24 = (f32[32,1152]{1,0:T(8,128)S(1)}, f32[32,1152]{1,0:T(8,128)S(1)}, u32[]{:S(2)}, u32[]{:S(2)}) collective-permute-start(f32[32,1152]{1,0:T(8,128)S(1)} %get-tuple-element.317), channel_id=1, source_target_pairs={{0,4},{1,5},{2,6},{3,7},{4,0},{5,1},{6,2},{7,3},{8,12},{9,13},{10,... | collective-permute-start | bytes 442376 | tf_op jit(solution)/shard_map/ppermute | solution.py:395
  79.2 12.4 %collective-permute-start.23 = (f32[32,1152]{1,0:T(8,128)S(1)}, f32[32,1152]{1,0:T(8,128)S(1)}, u32[]{:S(2)}, u32[]{:S(2)}) collective-permute-start(f32[32,1152]{1,0:T(8,128)S(1)} %get-tuple-element.318), channel_id=1, source_target_pairs={{0,2},{1,3},{2,0},{3,1},{4,6},{5,7},{6,4},{7,5},{8,10},{9,11},{10,... | collective-permute-start | bytes 442376 | tf_op jit(solution)/shard_map/ppermute | solution.py:395
  85.1 10.1 %collective-permute-start.22 = (f32[32,1152]{1,0:T(8,128)S(1)}, f32[32,1152]{1,0:T(8,128)S(1)}, u32[]{:S(2)}, u32[]{:S(2)}) collective-permute-start(f32[32,1152]{1,0:T(8,128)S(1)} %get-tuple-element.313), channel_id=1, source_target_pairs={{0,6},{1,7},{2,4},{3,5},{4,2},{5,3},{6,0},{7,1},{8,14},{9,15},{10,... | collective-permute-start | bytes 442376 | tf_op jit(solution)/shard_map/ppermute | solution.py:395
  86.0 9.2 %collective-permute-start.21 = (f32[32,1152]{1,0:T(8,128)S(1)}, f32[32,1152]{1,0:T(8,128)S(1)}, u32[]{:S(2)}, u32[]{:S(2)}) collective-permute-start(f32[32,1152]{1,0:T(8,128)S(1)} %get-tuple-element.314), channel_id=1, source_target_pairs={{0,4},{1,5},{2,6},{3,7},{4,0},{5,1},{6,2},{7,3},{8,12},{9,13},{10,... | collective-permute-start | bytes 442376 | tf_op jit(solution)/shard_map/ppermute | solution.py:395
  90.5 5.2 %collective-permute-start.20 = (f32[32,1152]{1,0:T(8,128)S(1)}, f32[32,1152]{1,0:T(8,128)S(1)}, u32[]{:S(2)}, u32[]{:S(2)}) collective-permute-start(f32[32,1152]{1,0:T(8,128)S(1)} %get-tuple-element.315), channel_id=1, source_target_pairs={{0,2},{1,3},{2,0},{3,1},{4,6},{5,7},{6,4},{7,5},{8,10},{9,11},{10,... | collective-permute-start | bytes 442376 | tf_op jit(solution)/shard_map/ppermute | solution.py:395
  91.6 13.2 %collective-permute-start.27 = (f32[32,1152]{1,0:T(8,128)S(1)}, f32[32,1152]{1,0:T(8,128)S(1)}, u32[]{:S(2)}, u32[]{:S(2)}) collective-permute-start(f32[32,1152]{1,0:T(8,128)S(1)} %fusion.1), channel_id=1, source_target_pairs={{0,8},{1,9},{2,10},{3,11},{4,12},{5,13},{6,14},{7,15},{8,0},{9,1},... | collective-permute-start | bytes 442376 | tf_op jit(solution)/shard_map/ppermute | solution.py:395
  95.7 12.6 %collective-permute-start.26 = (f32[32,1152]{1,0:T(8,128)S(1)}, f32[32,1152]{1,0:T(8,128)S(1)}, u32[]{:S(2)}, u32[]{:S(2)}) collective-permute-start(f32[32,1152]{1,0:T(8,128)S(1)} %fusion.3), channel_id=1, source_target_pairs={{0,8},{1,9},{2,10},{3,11},{4,12},{5,13},{6,14},{7,15},{8,0},{9,1},... | collective-permute-start | bytes 442376 | tf_op jit(solution)/shard_map/ppermute | solution.py:395
  104.8 8.5 %collective-permute-start.30 = (f32[32,1152]{1,0:T(8,128)S(1)}, f32[32,1152]{1,0:T(8,128)S(1)}, u32[]{:S(2)}, u32[]{:S(2)}) collective-permute-start(f32[32,1152]{1,0:T(8,128)S(1)} %add.93), channel_id=1, source_target_pairs={{0,6},{1,7},{2,4},{3,5},{4,2},{5,3},{6,0},{7,1},{8,14},{9,15},{10,... | collective-permute-start | bytes 442376 | tf_op jit(solution)/shard_map/ppermute | solution.py:395
  106.5 6.8 %collective-permute-start.29 = (f32[32,1152]{1,0:T(8,128)S(1)}, f32[32,1152]{1,0:T(8,128)S(1)}, u32[]{:S(2)}, u32[]{:S(2)}) collective-permute-start(f32[32,1152]{1,0:T(8,128)S(1)} %add.93), channel_id=1, source_target_pairs={{0,4},{1,5},{2,6},{3,7},{4,0},{5,1},{6,2},{7,3},{8,12},{9,13},{10,... | collective-permute-start | bytes 442376 | tf_op jit(solution)/shard_map/ppermute | solution.py:395
  108.1 7.0 %collective-permute-start.28 = (f32[32,1152]{1,0:T(8,128)S(1)}, f32[32,1152]{1,0:T(8,128)S(1)}, u32[]{:S(2)}, u32[]{:S(2)}) collective-permute-start(f32[32,1152]{1,0:T(8,128)S(1)} %add.93), channel_id=1, source_target_pairs={{0,2},{1,3},{2,0},{3,1},{4,6},{5,7},{6,4},{7,5},{8,10},{9,11},{10,... | collective-permute-start | bytes 442376 | tf_op jit(solution)/shard_map/ppermute | solution.py:395
  108.3 8.4 %collective-permute-start.31 = (f32[32,1152]{1,0:T(8,128)S(1)}, f32[32,1152]{1,0:T(8,128)S(1)}, u32[]{:S(2)}, u32[]{:S(2)}) collective-permute-start(f32[32,1152]{1,0:T(8,128)S(1)} %add.92), channel_id=1, source_target_pairs={{0,2},{1,3},{2,0},{3,1},{4,6},{5,7},{6,4},{7,5},{8,10},{9,11},{10,... | collective-permute-start | bytes 442376 | tf_op jit(solution)/shard_map/ppermute | solution.py:395
  116.9 7.6 %collective-permute-start.33 = (f32[32,1152]{1,0:T(8,128)S(1)}, f32[32,1152]{1,0:T(8,128)S(1)}, u32[]{:S(2)}, u32[]{:S(2)}) collective-permute-start(f32[32,1152]{1,0:T(8,128)S(1)} %add.92), channel_id=1, source_target_pairs={{0,6},{1,7},{2,4},{3,5},{4,2},{5,3},{6,0},{7,1},{8,14},{9,15},{10,... | collective-permute-start | bytes 442376 | tf_op jit(solution)/shard_map/ppermute | solution.py:395
  118.2 7.4 %collective-permute-start.32 = (f32[32,1152]{1,0:T(8,128)S(1)}, f32[32,1152]{1,0:T(8,128)S(1)}, u32[]{:S(2)}, u32[]{:S(2)}) collective-permute-start(f32[32,1152]{1,0:T(8,128)S(1)} %add.92), channel_id=1, source_target_pairs={{0,4},{1,5},{2,6},{3,7},{4,0},{5,1},{6,2},{7,3},{8,12},{9,13},{10,... | collective-permute-start | bytes 442376 | tf_op jit(solution)/shard_map/ppermute | solution.py:395
  (9 other events, 56.8 us)
where the time goes:
time: 134 us; the launch traced here: 133 us
  Pallas kernels  61.3 us (46%)
  starting transfers between devices  45.7 us (34%)
  waiting for transfers between devices  25.3 us (19%)
    ppermute x36, starting transfers between devices, swap(): return lax.ppermute(x, 'row', [(i, i ^ offset) for i in range(self.count)])  45.7 us
    ppermute x36, waiting for transfers between devices, swap(): return lax.ppermute(x, 'row', [(i, i ^ offset) for i in range(self.count)])  25.3 us
    pallas_call x6, Pallas kernels, affine(): call(affine_kernel, 'affine', struct(height, size), 24, 1 / parts, 2, gri...  20.8 us
    pallas_call x1, Pallas kernels, first_gram(): call(functools.partial(first_gram_kernel, shards), 'first_gram', halves(s...  7.24 us
    pallas_call x1, Pallas kernels, early_middle(): call(functools.partial(early_kernel, shards, len(pieces)), 'early_middle'...  6.96 us
    pallas_call x1, Pallas kernels, second_gram(): call(functools.partial(second_gram_kernel, shards, len(pieces)), 'second_...  6.39 us
    pallas_call x1, Pallas kernels, last_step(): call(functools.partial(last_kernel, shards, len(pieces)), 'last', struct(...  5.57 us
    pallas_call x1, Pallas kernels, other_gram(): call(functools.partial(other_gram_kernel, shards), 'other_gram', halves(s...  5.05 us
  transfers between devices with their start and end apart: 36, of which 15 were waited for; matrix products, arithmetic and copies ran while one was open for 0% of the time, Pallas kernels for 32%

commit v1 on v0

--- a/solution.py
+++ b/solution.py
@@ -122,14 +122,17 @@
         for copy in pair:
             copy.start()
         copies.append((r, pair))
+    q = size // 4
     for r, pair in copies:
         for copy in pair:
             copy.wait()
         ah[:, r], al[:, r] = split(a_buf[r].T)
         bh[r], bl[r] = split(b_buf[r])
-    q = size // 4
-    for r0, r1, c0, c1 in [(0, q, 0, size), (q, size, 0, q), (3 * q, size, 3 * q, size)]:
-        g[r0:r1, c0:c1] = mm((ah[r0:r1, :], al[r0:r1, :]), (bh[:, c0:c1], bl[:, c0:c1]))
+        for r0, r1, c0, c1 in [(0, q, 0, size), (q, size, 0, q), (3 * q, size, 3 * q, size)]:
+            product = mm((ah[r0:r1, r], al[r0:r1, r]), (bh[r, c0:c1], bl[r, c0:c1]))
+            if r.start:
+                product += g[r0:r1, c0:c1]
+            g[r0:r1, c0:c1] = product
     pack(g, packed, keep_ref, send_ref, me_ref[0], shards, 0)
 
 
@@ -151,13 +154,11 @@
 
 
 def lower_product(g, ah, al, bh, bl):
-    q = g.shape[0] // 4
-
-    def step(r):
-        t = pl.ds(pl.multiple_of(q + r.start, r.size), r.size)
-        g[t, q:] = mm((ah[t], al[t]), (bh, bl))
-
-    row_tiles(3 * q, q, step)
+    size = g.shape[0]
+    q = size // 4
+    for r0, r1, c0, c1 in [(q, 3 * q, q, size), (3 * q, size, q, 3 * q)]:
+        c = slice(c0 - q, c1 - q)
+        g[r0:r1, c0:c1] = mm((ah[r0:r1, :], al[r0:r1, :]), (bh[:, c], bl[:, c]))
 
 
 def other_gram_kernel(shards, me_ref, ah, al, bh, bl, keep_ref, send_ref, g, packed):
@@ -176,22 +177,21 @@
     )(me, ah, al, bh, bl)
 
 
-def row_tiles(rows, tile, step):
+def tiles(count, tile, step):
     def body(t, _):
         step(pl.ds(pl.multiple_of(t * tile, tile), tile))
         return 0
 
-    lax.fori_loop(0, rows // tile, body, 0)
+    lax.fori_loop(0, count // tile, body, 0)
 
 
 def affine_kernel(a_ref, b_ref, out_ref, hi, lo):
-    hi[...], lo[...] = split(b_ref[...])
-
-    def step(r):
-        a = a_ref[r]
-        out_ref[r] = 1.5 * a - 0.5 * mm(split(a), (hi[...], lo[...]))
-
-    row_tiles(a_ref.shape[0], 128, step)
+    hi[...], lo[...] = split(a_ref[...])
+
+    def step(c):
+        out_ref[:, c] = 1.5 * a_ref[:, c] - 0.5 * mm((hi[...], lo[...]), split(b_ref[:, c]))
+
+    tiles(out_ref.shape[1], 256, step)
 
 
 def affine(a, b, part, parts):
@@ -205,115 +205,110 @@
             pl.BlockSpec((size, size), lambda r: (0, 0)),
         ],
         out_specs=pl.BlockSpec((height, size), lambda r: (0, 0)),
-        scratch_shapes=[pltpu.VMEM((size, size), BF16)] * 2,
+        scratch_shapes=[pltpu.VMEM((height, size), BF16)] * 2,
     )(a, b)
 
 
-def apply_first(a, base, hi, lo):
-    size = hi.shape[0]
-    q = size // 4
-    part = lambda k0, k1, c0, c1: mm(
-        (a[0][:, k0:k1], a[1][:, k0:k1]), (hi[k0:k1, c0:c1], lo[k0:k1, c0:c1])
-    )
-    wide = part(0, q, 0, size)
-    left = part(q, size, 0, q)
-    corner = part(3 * q, size, 3 * q, size)
-    return jnp.concatenate(
-        [
-            base[:, :q] - 0.5 * (wide[:, :q] + left),
-            base[:, q:3 * q] - 0.5 * wide[:, q:3 * q],
-            base[:, 3 * q:] - 0.5 * (wide[:, 3 * q:] + corner),
-        ],
-        axis=1,
-    )
-
-
-def apply_parts(a_ref, base_refs, out_ref, hi, lo):
-    at = 0
-    for base_ref in base_refs:
-        start = at
-
-        def step(r):
-            t = pl.ds(pl.multiple_of(start + r.start, r.size), r.size)
-            out_ref[t] = apply_first(split(a_ref[t]), base_ref[r], hi, lo)
-
-        row_tiles(base_ref.shape[0], 256, step)
-        at += base_ref.shape[0]
+SPANS = (
+    (((0, 4),), ((0, 1),), ((0, 1),), ((0, 1), (3, 4))),
+    ((), ((1, 4),), ((1, 4),), ((1, 3),)),
+)
+
+
+def sym_product(ah, al, hi, lo, chunk, column):
+    q = hi.shape[0] // 4
+    spans = [slice(k0 * q, k1 * q) for k0, k1 in SPANS[chunk][column]]
+    c = slice(column * q, (column + 1) * q)
+    a = [ref[:, k] for ref in (ah, ah, al) for k in spans]
+    b = [ref[k, c] for ref in (hi, lo, hi) for k in spans]
+    return c, jnp.dot(
+        jnp.concatenate(a, axis=1), jnp.concatenate(b, axis=0), preferred_element_type=F32
+    )
+
+
+def apply_first(a_ref, base_refs, out_ref, ah, al, hi, lo):
+    ah[...], al[...] = split(a_ref[...])
+    for column in range(4):
+        c, product = sym_product(ah, al, hi, lo, 0, column)
+        at = 0
+        for base_ref in base_refs:
+            end = at + base_ref.shape[0]
+            out_ref[at:end, c] = base_ref[:, c] - 0.5 * product[at:end]
+            at = end
+
+
+def sym_scratch(rows, size):
+    return (
+        [pltpu.VMEM((rows, size), BF16)] * 2
+        + [pltpu.VMEM((size, size), BF16)] * 2
+        + [packed_scratch(size)]
+    )
 
 
 def partial_kernel(shards, count, me_ref, *refs):
     pieces, refs = refs[:count], refs[count:]
-    a_ref, base_refs, (out_ref, hi, lo, packed) = refs[0], refs[1:-4], refs[-4:]
+    a_ref, base_refs, (out_ref, ah, al, hi, lo, packed) = refs[0], refs[1:-6], refs[-6:]
     unpack(pieces, packed, hi, lo, me_ref[0], shards, 0)
-    apply_parts(a_ref, base_refs, out_ref, hi, lo)
+    apply_first(a_ref, base_refs, out_ref, ah, al, hi, lo)
 
 
 def partial_apply(me, shards, pieces, a, base):
     rows, size = a.shape
     return call(
         functools.partial(partial_kernel, shards, len(pieces)), "partial_apply",
-        struct(rows, size), 20, 0.5, 3,
+        struct(rows, size), 22, 0.5, 3,
         in_specs=[SMEM] + [VMEM] * (len(pieces) + 1 + len(base)),
         out_specs=VMEM,
-        scratch_shapes=[pltpu.VMEM((size, size), BF16)] * 2 + [packed_scratch(size)],
+        scratch_shapes=sym_scratch(rows, size),
     )(me, *pieces, a, *base)
+
+
+def turn_kernel(x_ref, xh, xl):
+    xh[...], xl[...] = split(x_ref[...].T)
+
+
+def turn(x):
+    part = struct(*x.shape[::-1], dtype=BF16)
+    return call(
+        turn_kernel, "turn", [part, part], 16, 0.1, 2, in_specs=[VMEM], out_specs=[VMEM] * 2
+    )(x)
 
 
 def early_kernel(shards, count, me_ref, *refs):
     pieces, refs = refs[:count], refs[count:]
-    a_ref, base_refs, refs = refs[0], refs[1:-8], refs[-8:]
-    x_ref, out_ref, xh, xl, col_ref, hi, lo, packed = refs
+    a_ref, base_refs, refs = refs[0], refs[1:-9], refs[-9:]
+    xh, xl, out_ref, col_ref, ah, al, hi, lo, packed = refs
     unpack(pieces, packed, hi, lo, me_ref[0], shards, 0)
-    apply_parts(a_ref, base_refs, out_ref, hi, lo)
-    xh[...], xl[...] = split(x_ref[...].T)
-    q = col_ref.shape[1]
-    col = split(out_ref[:, :q])
-
-    def step(r):
-        col_ref[r] = mm((xh[r], xl[r]), col)
-
-    row_tiles(col_ref.shape[0], 512, step)
-
-
-def early_middle(me, shards, pieces, a, base, x):
+    apply_first(a_ref, base_refs, out_ref, ah, al, hi, lo)
+    col_ref[...] = mm((xh[...], xl[...]), split(out_ref[:, :col_ref.shape[1]]))
+
+
+def early_middle(me, shards, pieces, a, base, xh, xl):
     rows, size = a.shape
-    part = struct(size, rows, dtype=BF16)
     return call(
         functools.partial(early_kernel, shards, len(pieces)), "early_middle",
-        [struct(rows, size), part, part, struct(size, size // 4)], 22, 0.75, 5,
-        in_specs=[SMEM] + [VMEM] * (len(pieces) + 2 + len(base)),
-        out_specs=[VMEM] * 4,
-        scratch_shapes=[pltpu.VMEM((size, size), BF16)] * 2 + [packed_scratch(size)],
-    )(me, *pieces, a, *base, x)
-
-
-def apply_second(a, base, hi, lo):
-    size = hi.shape[0]
-    q = size // 4
-    part = lambda k1, c0, c1: mm(
-        (a[0][:, q:k1], a[1][:, q:k1]), (hi[q:k1, c0:c1], lo[q:k1, c0:c1])
-    )
-    return jnp.concatenate(
-        [base[:, q:3 * q] - 0.5 * part(size, q, 3 * q), base[:, 3 * q:] - 0.5 * part(3 * q, 3 * q, size)],
-        axis=1,
-    )
+        [struct(rows, size), struct(size, size // 4)], 24, 0.75, 5,
+        in_specs=[SMEM] + [VMEM] * (len(pieces) + 3 + len(base)),
+        out_specs=[VMEM] * 2,
+        scratch_shapes=sym_scratch(rows, size),
+    )(me, *pieces, a, *base, xh, xl)
 
 
 def second_gram_kernel(shards, count, me_ref, *refs):
     pieces, refs = refs[:count], refs[count:]
     a_ref, base_ref, xh, xl, col_ref, refs = refs[0], refs[1], refs[2], refs[3], refs[4], refs[5:]
-    keep_ref, send_ref, mid_ref, mh, ml, hi, lo, g, packed = refs
+    keep_ref, send_ref, mid_ref, mh, ml, ah, al, hi, lo, packed, g = refs
+    size = g.shape[0]
+    q = size // 4
+    ah[:, q:], al[:, q:] = split(a_ref[:, q:])
     unpack(pieces, packed, hi, lo, me_ref[0], shards, 1)
-    rows, size = a_ref.shape
-    q = size // 4
     mid_ref[:, :q] = base_ref[:, :q]
-
-    def step(t):
-        mid = apply_second(split(a_ref[t]), base_ref[t], hi, lo)
-        mid_ref[t, q:] = mid
-        mh[t], ml[t] = split(mid)
-
-    row_tiles(rows, 512, step)
+    for column in range(1, 4):
+        c, product = sym_product(ah, al, hi, lo, 1, column)
+        mid = base_ref[:, c] - 0.5 * product
+        mid_ref[:, c] = mid
+        c = slice(c.start - q, c.stop - q)
+        mh[:, c], ml[:, c] = split(mid)
     g[:, :q] = col_ref[...]
     g[:q, q:] = mm((xh[:q, :], xl[:q, :]), (mh[...], ml[...]))
     g[3 * q:, 3 * q:] = mm((xh[3 * q:, :], xl[3 * q:, :]), (mh[:, 2 * q:], ml[:, 2 * q:]))
@@ -325,11 +320,10 @@
     part = struct(rows, size - size // 4, dtype=BF16)
     return call(
         functools.partial(second_gram_kernel, shards, len(pieces)), "second_gram",
-        halves(size) + [struct(rows, size), part, part], 22, 0.8, 5,
+        halves(size) + [struct(rows, size), part, part], 26, 0.8, 5,
         in_specs=[SMEM] + [VMEM] * (len(pieces) + 5),
         out_specs=[VMEM] * 5,
-        scratch_shapes=[pltpu.VMEM((size, size), BF16)] * 2
-        + [pltpu.VMEM((size, size), F32), packed_scratch(size)],
+        scratch_shapes=sym_scratch(rows, size) + [pltpu.VMEM((size, size), F32)],
     )(me, *pieces, a, base, xh, xl, col)
 
 
@@ -350,31 +344,35 @@
 
 def last_kernel(shards, count, me_ref, *refs):
     pieces = refs[:count]
-    x_ref, z_ref, out_ref, hi, lo, packed = refs[count:]
-    size = hi.shape[0]
-    q = size // 4
-
-    @pl.when(pl.program_id(0) == 0)
-    def _():
-        unpack(pieces, packed, hi, lo, me_ref[0], shards, 1)
-
-    a = split(x_ref[:, q:])
-    out_ref[:, :q] = z_ref[:, :q]
-    out_ref[:, q:3 * q] = z_ref[:, q:3 * q] - 0.5 * mm(a, (hi[q:, q:3 * q], lo[q:, q:3 * q]))
-    a = (a[0][:, :2 * q], a[1][:, :2 * q])
-    out_ref[:, 3 * q:] = z_ref[:, 3 * q:] - 0.5 * mm(a, (hi[q:3 * q, 3 * q:], lo[q:3 * q, 3 * q:]))
+    x_ref, z_ref, out_hbm, ah, al, hi, lo, packed, out, sems = refs[count:]
+    q = hi.shape[0] // 4
+    copies = []
+
+    def send(src, column):
+        c = slice(column * q, (column + 1) * q)
+        copy = pltpu.make_async_copy(src.at[:, c], out_hbm.at[:, c], sems.at[column])
+        copy.start()
+        copies.append(copy)
+
+    send(z_ref, 0)
+    ah[:, q:], al[:, q:] = split(x_ref[:, q:])
+    unpack(pieces, packed, hi, lo, me_ref[0], shards, 1)
+    for column in (1, 2, 3):
+        c, product = sym_product(ah, al, hi, lo, 1, column)
+        out[:, c] = z_ref[:, c] - 0.5 * product
+        send(out, column)
+    for copy in copies:
+        copy.wait()
 
 
 def last_step(me, shards, pieces, x, z):
     rows, size = x.shape
-    tile = 256
-    block = pl.BlockSpec((tile, size), lambda r: (r, 0))
-    return call(
-        functools.partial(last_kernel, shards, len(pieces)), "last", struct(rows, size), 20, 0.5, 3,
-        grid=(rows // tile,),
-        in_specs=[SMEM] + [pl.BlockSpec(p.shape, lambda r: (0, 0)) for p in pieces] + [block, block],
-        out_specs=block,
-        scratch_shapes=[pltpu.VMEM((size, size), BF16)] * 2 + [packed_scratch(size)],
+    return call(
+        functools.partial(last_kernel, shards, len(pieces)), "last", struct(rows, size), 26, 0.5, 3,
+        in_specs=[SMEM] + [VMEM] * (len(pieces) + 2),
+        out_specs=pl.BlockSpec(memory_space=pltpu.HBM),
+        scratch_shapes=sym_scratch(rows, size)
+        + [pltpu.VMEM((rows, size), F32), pltpu.SemaphoreType.DMA((4,))],
     )(me, *pieces, x, z)
 
 
@@ -450,13 +448,13 @@
         got_a = a.exchange(offset)
         b.own(close(env, *got_b))
         got_b = [b.exchange(offset)]
+        work()
         a.own(close(env, got_a))
 
     got_a = a.gather_plane()
     b.own(close(env, *got_b))
 
     got_b = b.gather_plane()
-    work()
     *got_a, got_b[0] = close(env, *got_a, got_b[0])
     got_a = a.gather_core(got_a)
     pieces_a = [a.mine, *close(env, got_a)]
@@ -482,14 +480,20 @@
         return [env[f"{name}{at}"] for at in range(3)]
 
     def early(env, pieces):
-        env["mid"], env["xh"], env["xl"], env["col"] = early_middle(
-            me, SHARDS, pieces, env["x1"], three(env, "m"), env["x0"]
+        env["mid"], env["col"] = early_middle(
+            me, SHARDS, pieces, env["x1"], three(env, "m"), env["xh"], env["xl"]
         )
+
+    half, quarter, rest = thirds("m", "c", "s1")
+
+    def rest_and_turn(env):
+        rest(env)
+        env["xh"], env["xl"] = turn(env["x0"])
 
     keep, send, *parts = first_gram(me, SHARDS, env["x1"], env["c"])
     _, one = sum_chunks(
         count, env, (keep, send), lambda env: other_gram(me, SHARDS, *parts),
-        thirds("m", "c", "s1"), early,
+        [half, quarter, rest_and_turn], early,
     )
 
     keep, send, env["mid"], mh, ml = second_gram(

time: 134 us -> 129 us (0.963)
  Pallas kernels: 61.3 us -> 55.3 us
  waiting for transfers between devices: 25.3 us -> 27.6 us
    ppermute x36, waiting for transfers between devices: 25.3 us -> 27.6 us  [swap(): return lax.ppermute(x, 'row', [(i, i ^ offset) for i in range(self.count)])]
    pallas_call x6, Pallas kernels: 20.8 us -> 19.1 us  [affine(): call(affine_kernel, 'affine', struct(height, size), 24, 1 / parts, 2, gri...]
    pallas_call x1, Pallas kernels: 5.05 us -> 3.63 us  [other_gram(): call(functools.partial(other_gram_kernel, shards), 'other_gram', halves(s...]
    pallas_call x1, Pallas kernels: 6.96 us -> 5.55 us  [early_middle(): call(functools.partial(early_kernel, shards, len(pieces)), 'early_middle'...]
  transfers between devices with their start and end apart: 36 -> 36, of which waited for: 15 -> 18; matrix products, arithmetic and copies ran while one was open for 0% -> 0% of each run, Pallas kernels for 32% -> 29%
where the time goes in v1:
time: 129 us
  Pallas kernels  55.3 us (43%)
  starting transfers between devices  44.8 us (35%)
  waiting for transfers between devices  27.6 us (21%)
    ppermute x36, starting transfers between devices, swap(): return lax.ppermute(x, 'row', [(i, i ^ offset) for i in range(self.count)])  44.8 us
    ppermute x36, waiting for transfers between devices, swap(): return lax.ppermute(x, 'row', [(i, i ^ offset) for i in range(self.count)])  27.6 us
    pallas_call x6, Pallas kernels, affine(): call(affine_kernel, 'affine', struct(height, size), 24, 1 / parts, 2, gri...  19.1 us
    pallas_call x1, Pallas kernels, first_gram(): call(functools.partial(first_gram_kernel, shards), 'first_gram', halves(s...  6.92 us
    pallas_call x1, Pallas kernels, second_gram(): call(functools.partial(second_gram_kernel, shards, len(pieces)), 'second_...  5.9 us
    pallas_call x1, Pallas kernels, early_middle(): call(functools.partial(early_kernel, shards, len(pieces)), 'early_middle'...  5.55 us
    pallas_call x1, Pallas kernels, last_step(): call(functools.partial(last_kernel, shards, len(pieces)), 'last', struct(...  5.24 us
    pallas_call x1, Pallas kernels, fourth_gram(): call(functools.partial(fourth_gram_kernel, shards), 'fourth_gram', halves...  3.88 us
  transfers between devices with their start and end apart: 36, of which 18 were waited for; matrix products, arithmetic and copies ran while one was open for 0% of the time, Pallas kernels for 29%

profile of v1, /device:TPU:0, one launch (start us, length us, event | category | flops | bytes accessed | tf_op | source)
XLA Modules:
  0.0 128.9 jit_solution(6434897196412503924)
XLA Ops:
  0.0 6.9 %first_gram.1 = (f32[128,1152]{1,0:T(8,128)S(1)}, f32[128,1152]{1,0:T(8,128)S(1)}, bf16[1024,1024]{1,0:T(8,128)(2,1)S(1)}, bf16[1024,1024]{1,0:T(8,128)(2,1)S(1)...) custom-call(s32[1]{0:T(128)} %bitcast.me_ref, f32[1024,1024]{1,0:T(8,128)} %refs_2_.1, f32[1024,1024]{1,0:T(8,128)} %a_ref.2), custom_call_target="tpu_custom_call" | custom-call | flops 3221225472 | bytes 16777216 | tf_op jit(solution)/shard_map/first_gram/pallas_call | solution.py:142
  7.5 3.6 %other_gram.1 = (f32[128,1152]{1,0:T(8,128)S(1)}, f32[128,1152]{1,0:T(8,128)S(1)}) custom-call(s32[1]{0:T(128)} %bitcast.me_ref, bf16[1024,1024]{1,0:T(8,128)(2,1)S(1)} %get-tuple-element.164.ah, bf16[1024,1024]{1,0:T(8,128)(2,1)S(1)} %get-tuple-element.165.al, bf16[1024,1024]{1,0:T(8,128)(2,1)S(1)} %get-tuple-element.166.bh, ...), custom_call_target="tpu_custom_call" | custom-call | flops 3221225472 | bytes 8388608 | tf_op jit(solution)/shard_map/other_gram/pallas_call | solution.py:172
  11.3 4.1 %collective-permute-start.7 = (f32[32,1152]{1,0:T(8,128)S(1)}, f32[32,1152]{1,0:T(8,128)S(1)}, u32[]{:S(2)}, u32[]{:S(2)}) collective-permute-start(f32[32,1152]{1,0:T(8,128)S(1)} %get-tuple-element.330), channel_id=1, source_target_pairs={{0,6},{1,7},{2,4},{3,5},{4,2},{5,3},{6,0},{7,1},{8,14},{9,15},{10,... | collective-permute-start | bytes 442376 | tf_op jit(solution)/shard_map/ppermute | solution.py:393
  16.0 4.3 %affine.6.refs_3_ = f32[512,1024]{1,0:T(8,128)S(1)} custom-call(f32[1024,1024]{1,0:T(8,128)S(1)} %copy-done.1, f32[1024,1024]{1,0:T(8,128)S(1)} %copy-done.2), custom_call_target="tpu_custom_call" | custom-call | flops 3221225472 | bytes 8388608 | tf_op jit(solution)/shard_map/affine/pallas_call | solution.py:200
  20.5 2.9 %collective-permute-start.4 = (f32[32,1152]{1,0:T(8,128)S(1)}, f32[32,1152]{1,0:T(8,128)S(1)}, u32[]{:S(2)}, u32[]{:S(2)}) collective-permute-start(f32[32,1152]{1,0:T(8,128)S(1)} %get-tuple-element.327), channel_id=1, source_target_pairs={{0,6},{1,7},{2,4},{3,5},{4,2},{5,3},{6,0},{7,1},{8,14},{9,15},{10,... | collective-permute-start | bytes 442376 | tf_op jit(solution)/shard_map/ppermute | solution.py:393
  23.8 2.5 %affine.7.refs_4_ = f32[256,1024]{1,0:T(8,128)S(1)} custom-call(f32[1024,1024]{1,0:T(8,128)S(1)} %copy-done.1, f32[1024,1024]{1,0:T(8,128)S(1)} %copy-done.2), custom_call_target="tpu_custom_call" | custom-call | flops 1610612736 | bytes 8388608 | tf_op jit(solution)/shard_map/affine/pallas_call | solution.py:200
  26.7 3.0 %collective-permute-start.9 = (f32[32,1152]{1,0:T(8,128)S(1)}, f32[32,1152]{1,0:T(8,128)S(1)}, u32[]{:S(2)}, u32[]{:S(2)}) collective-permute-start(f32[32,1152]{1,0:T(8,128)S(1)} %fusion.5), channel_id=1, source_target_pairs={{0,8},{1,9},{2,10},{3,11},{4,12},{5,13},{6,14},{7,15},{8,0},{9,1},... | collective-permute-start | bytes 442376 | tf_op jit(solution)/shard_map/ppermute | solution.py:393
  29.7 2.1 %collective-permute-done.3 = f32[32,1152]{1,0:T(8,128)S(1)} collective-permute-done((f32[32,1152]{1,0:T(8,128)S(1)}, f32[32,1152]{1,0:T(8,128)S(1)}, u32[]{:S(2)}, u32[]{:S(2)}) %collective-permute-start.3) | collective-permute-done | bytes 147488 | tf_op jit(solution)/shard_map/ppermute | solution.py:393
  31.8 2.5 %collective-permute-start.8 = (f32[32,1152]{1,0:T(8,128)S(1)}, f32[32,1152]{1,0:T(8,128)S(1)}, u32[]{:S(2)}, u32[]{:S(2)}) collective-permute-start(f32[32,1152]{1,0:T(8,128)S(1)} %fusion.7), channel_id=1, source_target_pairs={{0,8},{1,9},{2,10},{3,11},{4,12},{5,13},{6,14},{7,15},{8,0},{9,1},... | collective-permute-start | bytes 442376 | tf_op jit(solution)/shard_map/ppermute | solution.py:393
  35.6 2.7 %affine.8.refs_5_ = f32[256,1024]{1,0:T(8,128)S(1)} custom-call(f32[1024,1024]{1,0:T(8,128)S(1)} %copy-done.1, f32[1024,1024]{1,0:T(8,128)S(1)} %copy-done.2), custom_call_target="tpu_custom_call" | custom-call | flops 1610612736 | bytes 8388608 | tf_op jit(solution)/shard_map/affine/pallas_call | solution.py:200
  39.0 2.3 %collective-permute-start.12 = (f32[32,1152]{1,0:T(8,128)S(1)}, f32[32,1152]{1,0:T(8,128)S(1)}, u32[]{:S(2)}, u32[]{:S(2)}) collective-permute-start(f32[32,1152]{1,0:T(8,128)S(1)} %add.83), channel_id=1, source_target_pairs={{0,6},{1,7},{2,4},{3,5},{4,2},{5,3},{6,0},{7,1},{8,14},{9,15},{10,... | collective-permute-start | bytes 442376 | tf_op jit(solution)/shard_map/ppermute | solution.py:393
  41.3 1.8 %collective-permute-start.11 = (f32[32,1152]{1,0:T(8,128)S(1)}, f32[32,1152]{1,0:T(8,128)S(1)}, u32[]{:S(2)}, u32[]{:S(2)}) collective-permute-start(f32[32,1152]{1,0:T(8,128)S(1)} %add.83), channel_id=1, source_target_pairs={{0,4},{1,5},{2,6},{3,7},{4,0},{5,1},{6,2},{7,3},{8,12},{9,13},{10,... | collective-permute-start | bytes 442376 | tf_op jit(solution)/shard_map/ppermute | solution.py:393
  43.2 2.1 %collective-permute-start.13 = (f32[32,1152]{1,0:T(8,128)S(1)}, f32[32,1152]{1,0:T(8,128)S(1)}, u32[]{:S(2)}, u32[]{:S(2)}) collective-permute-start(f32[32,1152]{1,0:T(8,128)S(1)} %add.82), channel_id=1, source_target_pairs={{0,2},{1,3},{2,0},{3,1},{4,6},{5,7},{6,4},{7,5},{8,10},{9,11},{10,... | collective-permute-start | bytes 442376 | tf_op jit(solution)/shard_map/ppermute | solution.py:393
  52.9 5.5 %early_middle.1 = (f32[1024,1024]{1,0:T(8,128)S(1)}, f32[1024,256]{1,0:T(8,128)S(1)}) custom-call(s32[1]{0:T(128)} %bitcast.me_ref, f32[128,1152]{1,0:T(8,128)S(1)} %pad_maximum_fusion.refs_0_, f32[128,1152]{1,0:T(8,128)S(1)} %collective-permute-done.16.refs_1_, f32[1024,1024]{1,0:T(8,128)S(1)} %copy-done.4, f32[512,1024]{1,0:T(8,128)S(1)} %affine.6.refs_3_, ...), custom_call_target="tpu_custom_call" | custom-call | flops 4831838208 | bytes 20971520 | tf_op jit(solution)/shard_map/early_middle/pallas_call | solution.py:288
  58.5 1.8 %collective-permute-done.14 = f32[32,1152]{1,0:T(8,128)S(1)} collective-permute-done((f32[32,1152]{1,0:T(8,128)S(1)}, f32[32,1152]{1,0:T(8,128)S(1)}, u32[]{:S(2)}, u32[]{:S(2)}) %collective-permute-start.14) | collective-permute-done | bytes 147488 | tf_op jit(solution)/shard_map/ppermute | solution.py:393
  60.4 2.0 %collective-permute-done.17.refs_1_ = f32[128,1152]{1,0:T(8,128)S(1)} collective-permute-done((f32[128,1152]{1,0:T(8,128)S(1)}, f32[128,1152]{1,0:T(8,128)S(1)}, u32[]{:S(2)}, u32[]{:S(2)}) %collective-permute-start.17) | collective-permute-done | bytes 589856 | tf_op jit(solution)/shard_map/ppermute | solution.py:393
  62.4 5.9 %second_gram.1 = (f32[128,1152]{1,0:T(8,128)S(1)}, f32[128,1152]{1,0:T(8,128)S(1)}, f32[1024,1024]{1,0:T(8,128)S(1)}, bf16[1024,768]{1,0:T(8,128)(2,1)S(1)}, bf16[1024,768]{1,0:T(8,128)(2,1)S(1)}) custom-call(s32[1]{0:T(128)} %bitcast.me_ref, f32[128,1152]{1,0:T(8,128)S(1)} %pad_maximum_fusion.1.refs_0_, f32[128,1152]{1,0:T(8,128)S(1)} %collective-permute-done.17.refs_1_, ...), custom_call_target="tpu_custom_call" | custom-call | flops 5153960960 | bytes 20971520 | tf_op jit(solution)/shard_map/second_gram/pallas_call | solution.py:321
  68.5 3.9 %fourth_gram.1 = (f32[128,1152]{1,0:T(8,128)S(1)}, f32[128,1152]{1,0:T(8,128)S(1)}) custom-call(s32[1]{0:T(128)} %bitcast.me_ref, bf16[1024,1024]{1,0:T(8,128)(2,1)S(1)} %get-tuple-element.254.refs_6_.refs_4_.xh, bf16[1024,1024]{1,0:T(8,128)(2,1)S(1)} %get-tuple-element.255.refs_7_.refs_5_.xl, bf16[1024,768]{1,0:T(8,128)(2,1)S(1)} %get-tuple-element.258.mh, ...), custom_call_target="tpu_custom_call" | custom-call | flops 3221225472 | bytes 8388608 | tf_op jit(solution)/shard_map/fourth_gram/pallas_call | solution.py:337
  74.1 1.8 %collective-permute-start.24 = (f32[32,1152]{1,0:T(8,128)S(1)}, f32[32,1152]{1,0:T(8,128)S(1)}, u32[]{:S(2)}, u32[]{:S(2)}) collective-permute-start(f32[32,1152]{1,0:T(8,128)S(1)} %get-tuple-element.325), channel_id=1, source_target_pairs={{0,4},{1,5},{2,6},{3,7},{4,0},{5,1},{6,2},{7,3},{8,12},{9,13},{10,... | collective-permute-start | bytes 442376 | tf_op jit(solution)/shard_map/ppermute | solution.py:393
  76.5 4.4 %affine.9.refs_3_ = f32[512,1024]{1,0:T(8,128)S(1)} custom-call(f32[1024,1024]{1,0:T(8,128)S(1)} %get-tuple-element.290.a_ref, f32[1024,1024]{1,0:T(8,128)S(1)} %copy-done.3), custom_call_target="tpu_custom_call" | custom-call | flops 3221225472 | bytes 8388608 | tf_op jit(solution)/shard_map/affine/pallas_call | solution.py:200
  82.1 1.8 %collective-permute-start.21 = (f32[32,1152]{1,0:T(8,128)S(1)}, f32[32,1152]{1,0:T(8,128)S(1)}, u32[]{:S(2)}, u32[]{:S(2)}) collective-permute-start(f32[32,1152]{1,0:T(8,128)S(1)} %get-tuple-element.322), channel_id=1, source_target_pairs={{0,4},{1,5},{2,6},{3,7},{4,0},{5,1},{6,2},{7,3},{8,12},{9,13},{10,... | collective-permute-start | bytes 442376 | tf_op jit(solution)/shard_map/ppermute | solution.py:393
  83.9 2.6 %affine.10.refs_4_ = f32[256,1024]{1,0:T(8,128)S(1)} custom-call(f32[1024,1024]{1,0:T(8,128)S(1)} %get-tuple-element.290.a_ref, f32[1024,1024]{1,0:T(8,128)S(1)} %copy-done.3), custom_call_target="tpu_custom_call" | custom-call | flops 1610612736 | bytes 8388608 | tf_op jit(solution)/shard_map/affine/pallas_call | solution.py:200
  87.2 3.5 %collective-permute-start.27 = (f32[32,1152]{1,0:T(8,128)S(1)}, f32[32,1152]{1,0:T(8,128)S(1)}, u32[]{:S(2)}, u32[]{:S(2)}) collective-permute-start(f32[32,1152]{1,0:T(8,128)S(1)} %fusion.1), channel_id=1, source_target_pairs={{0,8},{1,9},{2,10},{3,11},{4,12},{5,13},{6,14},{7,15},{8,0},{9,1},... | collective-permute-start | bytes 442376 | tf_op jit(solution)/shard_map/ppermute | solution.py:393
  91.7 3.4 %collective-permute-start.26 = (f32[32,1152]{1,0:T(8,128)S(1)}, f32[32,1152]{1,0:T(8,128)S(1)}, u32[]{:S(2)}, u32[]{:S(2)}) collective-permute-start(f32[32,1152]{1,0:T(8,128)S(1)} %fusion.3), channel_id=1, source_target_pairs={{0,8},{1,9},{2,10},{3,11},{4,12},{5,13},{6,14},{7,15},{8,0},{9,1},... | collective-permute-start | bytes 442376 | tf_op jit(solution)/shard_map/ppermute | solution.py:393
  95.1 2.6 %affine.11.refs_5_ = f32[256,1024]{1,0:T(8,128)S(1)} custom-call(f32[1024,1024]{1,0:T(8,128)S(1)} %get-tuple-element.290.a_ref, f32[1024,1024]{1,0:T(8,128)S(1)} %copy-done.3), custom_call_target="tpu_custom_call" | custom-call | flops 1610612736 | bytes 8388608 | tf_op jit(solution)/shard_map/affine/pallas_call | solution.py:200
  97.7 2.6 %collective-permute-done.27 = f32[32,1152]{1,0:T(8,128)S(1)} collective-permute-done((f32[32,1152]{1,0:T(8,128)S(1)}, f32[32,1152]{1,0:T(8,128)S(1)}, u32[]{:S(2)}, u32[]{:S(2)}) %collective-permute-start.27) | collective-permute-done | bytes 147488 | tf_op jit(solution)/shard_map/ppermute | solution.py:393
  105.5 2.6 %collective-permute-done.30 = f32[32,1152]{1,0:T(8,128)S(1)} collective-permute-done((f32[32,1152]{1,0:T(8,128)S(1)}, f32[32,1152]{1,0:T(8,128)S(1)}, u32[]{:S(2)}, u32[]{:S(2)}) %collective-permute-start.30) | collective-permute-done | bytes 147488 | tf_op jit(solution)/shard_map/ppermute | solution.py:393
  108.6 1.8 %collective-permute-done.28 = f32[32,1152]{1,0:T(8,128)S(1)} collective-permute-done((f32[32,1152]{1,0:T(8,128)S(1)}, f32[32,1152]{1,0:T(8,128)S(1)}, u32[]{:S(2)}, u32[]{:S(2)}) %collective-permute-start.28) | collective-permute-done | bytes 147488 | tf_op jit(solution)/shard_map/ppermute | solution.py:393
  114.1 3.8 %partial_apply.1.refs_3_ = f32[1024,1024]{1,0:T(8,128)S(1)} custom-call(s32[1]{0:T(128)} %bitcast.me_ref, f32[128,1152]{1,0:T(8,128)S(1)} %pad_maximum_fusion.2.refs_0_, f32[128,1152]{1,0:T(8,128)S(1)} %collective-permute-done.34.refs_1_, f32[1024,1024]{1,0:T(8,128)S(1)} %copy-done, f32[512,1024]{1,0:T(8,128)S(1)} %affine.9.refs_3_, ...), custom_call_target="tpu_custom_call" | custom-call | flops 3221225472 | bytes 12582912 | tf_op jit(solution)/shard_map/partial_apply/pallas_call | solution.py:257
  118.0 1.8 %collective-permute-done.33 = f32[32,1152]{1,0:T(8,128)S(1)} collective-permute-done((f32[32,1152]{1,0:T(8,128)S(1)}, f32[32,1152]{1,0:T(8,128)S(1)}, u32[]{:S(2)}, u32[]{:S(2)}) %collective-permute-start.33) | collective-permute-done | bytes 147488 | tf_op jit(solution)/shard_map/ppermute | solution.py:393
  121.5 2.0 %collective-permute-done.35.refs_1_ = f32[128,1152]{1,0:T(8,128)S(1)} collective-permute-done((f32[128,1152]{1,0:T(8,128)S(1)}, f32[128,1152]{1,0:T(8,128)S(1)}, u32[]{:S(2)}, u32[]{:S(2)}) %collective-permute-start.35) | collective-permute-done | bytes 589856 | tf_op jit(solution)/shard_map/ppermute | solution.py:393
  123.5 5.2 %last.1 = f32[1024,1024]{1,0:T(8,128)} custom-call(s32[1]{0:T(128)} %bitcast.me_ref, f32[128,1152]{1,0:T(8,128)S(1)} %pad_maximum_fusion.3.refs_0_, f32[128,1152]{1,0:T(8,128)S(1)} %collective-permute-done.35.refs_1_, f32[1024,1024]{1,0:T(8,128)S(1)} %copy-done, f32[1024,1024]{1,0:T(8,128)S(1)} %partial_apply.1.refs_3_), custom_call_target="tpu_custom_call" | custom-call | flops 3221225472 | bytes 12582912 | tf_op jit(solution)/shard_map/last/pallas_call | solution.py:370
  (84 shorter events, 28.7 us)
Async XLA Ops:
  6.9 4.2 %collective-permute-start = (f32[128,1152]{1,0:T(8,128)S(1)}, f32[128,1152]{1,0:T(8,128)S(1)}, u32[]{:S(2)}, u32[]{:S(2)}) collective-permute-start(f32[128,1152]{1,0:T(8,128)S(1)} %get-tuple-element.163), channel_id=1, source_target_pairs={{0,1},{1,0},{2,3},{3,2},{4,5},{5,4},{6,7},{7,6},{8,9},{9,8},{10,11... | collective-permute-start | bytes 1769480 | tf_op jit(solution)/shard_map/ppermute | solution.py:393
  11.1 9.3 %collective-permute-start.1 = (f32[128,1152]{1,0:T(8,128)S(1)}, f32[128,1152]{1,0:T(8,128)S(1)}, u32[]{:S(2)}, u32[]{:S(2)}) collective-permute-start(f32[128,1152]{1,0:T(8,128)S(1)} %get-tuple-element.171), channel_id=1, source_target_pairs={{0,1},{1,0},{2,3},{3,2},{4,5},{5,4},{6,7},{7,6},{8,9},{9,8},{10,11... | collective-permute-start | bytes 1769480 | tf_op jit(solution)/shard_map/ppermute | solution.py:393
  11.3 15.0 %collective-permute-start.7 = (f32[32,1152]{1,0:T(8,128)S(1)}, f32[32,1152]{1,0:T(8,128)S(1)}, u32[]{:S(2)}, u32[]{:S(2)}) collective-permute-start(f32[32,1152]{1,0:T(8,128)S(1)} %get-tuple-element.330), channel_id=1, source_target_pairs={{0,6},{1,7},{2,4},{3,5},{4,2},{5,3},{6,0},{7,1},{8,14},{9,15},{10,... | collective-permute-start | bytes 442376 | tf_op jit(solution)/shard_map/ppermute | solution.py:393
  15.4 11.3 %collective-permute-start.6 = (f32[32,1152]{1,0:T(8,128)S(1)}, f32[32,1152]{1,0:T(8,128)S(1)}, u32[]{:S(2)}, u32[]{:S(2)}) collective-permute-start(f32[32,1152]{1,0:T(8,128)S(1)} %get-tuple-element.331), channel_id=1, source_target_pairs={{0,4},{1,5},{2,6},{3,7},{4,0},{5,1},{6,2},{7,3},{8,12},{9,13},{10,... | collective-permute-start | bytes 442376 | tf_op jit(solution)/shard_map/ppermute | solution.py:393
  15.8 10.9 %collective-permute-start.5 = (f32[32,1152]{1,0:T(8,128)S(1)}, f32[32,1152]{1,0:T(8,128)S(1)}, u32[]{:S(2)}, u32[]{:S(2)}) collective-permute-start(f32[32,1152]{1,0:T(8,128)S(1)} %get-tuple-element.332), channel_id=1, source_target_pairs={{0,2},{1,3},{2,0},{3,1},{4,6},{5,7},{6,4},{7,5},{8,10},{9,11},{10,... | collective-permute-start | bytes 442376 | tf_op jit(solution)/shard_map/ppermute | solution.py:393
  20.5 9.2 %collective-permute-start.4 = (f32[32,1152]{1,0:T(8,128)S(1)}, f32[32,1152]{1,0:T(8,128)S(1)}, u32[]{:S(2)}, u32[]{:S(2)}) collective-permute-start(f32[32,1152]{1,0:T(8,128)S(1)} %get-tuple-element.327), channel_id=1, source_target_pairs={{0,6},{1,7},{2,4},{3,5},{4,2},{5,3},{6,0},{7,1},{8,14},{9,15},{10,... | collective-permute-start | bytes 442376 | tf_op jit(solution)/shard_map/ppermute | solution.py:393
  23.4 8.4 %collective-permute-start.3 = (f32[32,1152]{1,0:T(8,128)S(1)}, f32[32,1152]{1,0:T(8,128)S(1)}, u32[]{:S(2)}, u32[]{:S(2)}) collective-permute-start(f32[32,1152]{1,0:T(8,128)S(1)} %get-tuple-element.328), channel_id=1, source_target_pairs={{0,4},{1,5},{2,6},{3,7},{4,0},{5,1},{6,2},{7,3},{8,12},{9,13},{10,... | collective-permute-start | bytes 442376 | tf_op jit(solution)/shard_map/ppermute | solution.py:393
  26.4 5.4 %collective-permute-start.2 = (f32[32,1152]{1,0:T(8,128)S(1)}, f32[32,1152]{1,0:T(8,128)S(1)}, u32[]{:S(2)}, u32[]{:S(2)}) collective-permute-start(f32[32,1152]{1,0:T(8,128)S(1)} %get-tuple-element.329), channel_id=1, source_target_pairs={{0,2},{1,3},{2,0},{3,1},{4,6},{5,7},{6,4},{7,5},{8,10},{9,11},{10,... | collective-permute-start | bytes 442376 | tf_op jit(solution)/shard_map/ppermute | solution.py:393
  26.7 12.3 %collective-permute-start.9 = (f32[32,1152]{1,0:T(8,128)S(1)}, f32[32,1152]{1,0:T(8,128)S(1)}, u32[]{:S(2)}, u32[]{:S(2)}) collective-permute-start(f32[32,1152]{1,0:T(8,128)S(1)} %fusion.5), channel_id=1, source_target_pairs={{0,8},{1,9},{2,10},{3,11},{4,12},{5,13},{6,14},{7,15},{8,0},{9,1},... | collective-permute-start | bytes 442376 | tf_op jit(solution)/shard_map/ppermute | solution.py:393
  31.8 11.3 %collective-permute-start.8 = (f32[32,1152]{1,0:T(8,128)S(1)}, f32[32,1152]{1,0:T(8,128)S(1)}, u32[]{:S(2)}, u32[]{:S(2)}) collective-permute-start(f32[32,1152]{1,0:T(8,128)S(1)} %fusion.7), channel_id=1, source_target_pairs={{0,8},{1,9},{2,10},{3,11},{4,12},{5,13},{6,14},{7,15},{8,0},{9,1},... | collective-permute-start | bytes 442376 | tf_op jit(solution)/shard_map/ppermute | solution.py:393
  39.0 7.8 %collective-permute-start.12 = (f32[32,1152]{1,0:T(8,128)S(1)}, f32[32,1152]{1,0:T(8,128)S(1)}, u32[]{:S(2)}, u32[]{:S(2)}) collective-permute-start(f32[32,1152]{1,0:T(8,128)S(1)} %add.83), channel_id=1, source_target_pairs={{0,6},{1,7},{2,4},{3,5},{4,2},{5,3},{6,0},{7,1},{8,14},{9,15},{10,... | collective-permute-start | bytes 442376 | tf_op jit(solution)/shard_map/ppermute | solution.py:393
  41.3 6.8 %collective-permute-start.11 = (f32[32,1152]{1,0:T(8,128)S(1)}, f32[32,1152]{1,0:T(8,128)S(1)}, u32[]{:S(2)}, u32[]{:S(2)}) collective-permute-start(f32[32,1152]{1,0:T(8,128)S(1)} %add.83), channel_id=1, source_target_pairs={{0,4},{1,5},{2,6},{3,7},{4,0},{5,1},{6,2},{7,3},{8,12},{9,13},{10,... | collective-permute-start | bytes 442376 | tf_op jit(solution)/shard_map/ppermute | solution.py:393
  43.1 6.0 %collective-permute-start.10 = (f32[32,1152]{1,0:T(8,128)S(1)}, f32[32,1152]{1,0:T(8,128)S(1)}, u32[]{:S(2)}, u32[]{:S(2)}) collective-permute-start(f32[32,1152]{1,0:T(8,128)S(1)} %add.83), channel_id=1, source_target_pairs={{0,2},{1,3},{2,0},{3,1},{4,6},{5,7},{6,4},{7,5},{8,10},{9,11},{10,... | collective-permute-start | bytes 442376 | tf_op jit(solution)/shard_map/ppermute | solution.py:393
  43.2 7.5 %collective-permute-start.13 = (f32[32,1152]{1,0:T(8,128)S(1)}, f32[32,1152]{1,0:T(8,128)S(1)}, u32[]{:S(2)}, u32[]{:S(2)}) collective-permute-start(f32[32,1152]{1,0:T(8,128)S(1)} %add.82), channel_id=1, source_target_pairs={{0,2},{1,3},{2,0},{3,1},{4,6},{5,7},{6,4},{7,5},{8,10},{9,11},{10,... | collective-permute-start | bytes 442376 | tf_op jit(solution)/shard_map/ppermute | solution.py:393
  50.8 7.7 %collective-permute-start.15 = (f32[32,1152]{1,0:T(8,128)S(1)}, f32[32,1152]{1,0:T(8,128)S(1)}, u32[]{:S(2)}, u32[]{:S(2)}) collective-permute-start(f32[32,1152]{1,0:T(8,128)S(1)} %add.82), channel_id=1, source_target_pairs={{0,6},{1,7},{2,4},{3,5},{4,2},{5,3},{6,0},{7,1},{8,14},{9,15},{10,... | collective-permute-start | bytes 442376 | tf_op jit(solution)/shard_map/ppermute | solution.py:393
  51.7 8.6 %collective-permute-start.14 = (f32[32,1152]{1,0:T(8,128)S(1)}, f32[32,1152]{1,0:T(8,128)S(1)}, u32[]{:S(2)}, u32[]{:S(2)}) collective-permute-start(f32[32,1152]{1,0:T(8,128)S(1)} %add.82), channel_id=1, source_target_pairs={{0,4},{1,5},{2,6},{3,7},{4,0},{5,1},{6,2},{7,3},{8,12},{9,13},{10,... | collective-permute-start | bytes 442376 | tf_op jit(solution)/shard_map/ppermute | solution.py:393
  68.3 4.1 %collective-permute-start.18 = (f32[128,1152]{1,0:T(8,128)S(1)}, f32[128,1152]{1,0:T(8,128)S(1)}, u32[]{:S(2)}, u32[]{:S(2)}) collective-permute-start(f32[128,1152]{1,0:T(8,128)S(1)} %get-tuple-element.257), channel_id=1, source_target_pairs={{0,1},{1,0},{2,3},{3,2},{4,5},{5,4},{6,7},{7,6},{8,9},{9,8},{10,11... | collective-permute-start | bytes 1769480 | tf_op jit(solution)/shard_map/ppermute | solution.py:393
  72.4 8.5 %collective-permute-start.19 = (f32[128,1152]{1,0:T(8,128)S(1)}, f32[128,1152]{1,0:T(8,128)S(1)}, u32[]{:S(2)}, u32[]{:S(2)}) collective-permute-start(f32[128,1152]{1,0:T(8,128)S(1)} %get-tuple-element.266), channel_id=1, source_target_pairs={{0,1},{1,0},{2,3},{3,2},{4,5},{5,4},{6,7},{7,6},{8,9},{9,8},{10,11... | collective-permute-start | bytes 1769480 | tf_op jit(solution)/shard_map/ppermute | solution.py:393
  72.9 13.5 %collective-permute-start.25 = (f32[32,1152]{1,0:T(8,128)S(1)}, f32[32,1152]{1,0:T(8,128)S(1)}, u32[]{:S(2)}, u32[]{:S(2)}) collective-permute-start(f32[32,1152]{1,0:T(8,128)S(1)} %get-tuple-element.324), channel_id=1, source_target_pairs={{0,6},{1,7},{2,4},{3,5},{4,2},{5,3},{6,0},{7,1},{8,14},{9,15},{10,... | collective-permute-start | bytes 442376 | tf_op jit(solution)/shard_map/ppermute | solution.py:393
  74.1 13.1 %collective-permute-start.24 = (f32[32,1152]{1,0:T(8,128)S(1)}, f32[32,1152]{1,0:T(8,128)S(1)}, u32[]{:S(2)}, u32[]{:S(2)}) collective-permute-start(f32[32,1152]{1,0:T(8,128)S(1)} %get-tuple-element.325), channel_id=1, source_target_pairs={{0,4},{1,5},{2,6},{3,7},{4,0},{5,1},{6,2},{7,3},{8,12},{9,13},{10,... | collective-permute-start | bytes 442376 | tf_op jit(solution)/shard_map/ppermute | solution.py:393
  75.9 11.3 %collective-permute-start.23 = (f32[32,1152]{1,0:T(8,128)S(1)}, f32[32,1152]{1,0:T(8,128)S(1)}, u32[]{:S(2)}, u32[]{:S(2)}) collective-permute-start(f32[32,1152]{1,0:T(8,128)S(1)} %get-tuple-element.326), channel_id=1, source_target_pairs={{0,2},{1,3},{2,0},{3,1},{4,6},{5,7},{6,4},{7,5},{8,10},{9,11},{10,... | collective-permute-start | bytes 442376 | tf_op jit(solution)/shard_map/ppermute | solution.py:393
  81.0 9.7 %collective-permute-start.22 = (f32[32,1152]{1,0:T(8,128)S(1)}, f32[32,1152]{1,0:T(8,128)S(1)}, u32[]{:S(2)}, u32[]{:S(2)}) collective-permute-start(f32[32,1152]{1,0:T(8,128)S(1)} %get-tuple-element.321), channel_id=1, source_target_pairs={{0,6},{1,7},{2,4},{3,5},{4,2},{5,3},{6,0},{7,1},{8,14},{9,15},{10,... | collective-permute-start | bytes 442376 | tf_op jit(solution)/shard_map/ppermute | solution.py:393
  82.1 8.6 %collective-permute-start.21 = (f32[32,1152]{1,0:T(8,128)S(1)}, f32[32,1152]{1,0:T(8,128)S(1)}, u32[]{:S(2)}, u32[]{:S(2)}) collective-permute-start(f32[32,1152]{1,0:T(8,128)S(1)} %get-tuple-element.322), channel_id=1, source_target_pairs={{0,4},{1,5},{2,6},{3,7},{4,0},{5,1},{6,2},{7,3},{8,12},{9,13},{10,... | collective-permute-start | bytes 442376 | tf_op jit(solution)/shard_map/ppermute | solution.py:393
  86.5 5.2 %collective-permute-start.20 = (f32[32,1152]{1,0:T(8,128)S(1)}, f32[32,1152]{1,0:T(8,128)S(1)}, u32[]{:S(2)}, u32[]{:S(2)}) collective-permute-start(f32[32,1152]{1,0:T(8,128)S(1)} %get-tuple-element.323), channel_id=1, source_target_pairs={{0,2},{1,3},{2,0},{3,1},{4,6},{5,7},{6,4},{7,5},{8,10},{9,11},{10,... | collective-permute-start | bytes 442376 | tf_op jit(solution)/shard_map/ppermute | solution.py:393
  87.2 13.1 %collective-permute-start.27 = (f32[32,1152]{1,0:T(8,128)S(1)}, f32[32,1152]{1,0:T(8,128)S(1)}, u32[]{:S(2)}, u32[]{:S(2)}) collective-permute-start(f32[32,1152]{1,0:T(8,128)S(1)} %fusion.1), channel_id=1, source_target_pairs={{0,8},{1,9},{2,10},{3,11},{4,12},{5,13},{6,14},{7,15},{8,0},{9,1},... | collective-permute-start | bytes 442376 | tf_op jit(solution)/shard_map/ppermute | solution.py:393
  91.7 12.2 %collective-permute-start.26 = (f32[32,1152]{1,0:T(8,128)S(1)}, f32[32,1152]{1,0:T(8,128)S(1)}, u32[]{:S(2)}, u32[]{:S(2)}) collective-permute-start(f32[32,1152]{1,0:T(8,128)S(1)} %fusion.3), channel_id=1, source_target_pairs={{0,8},{1,9},{2,10},{3,11},{4,12},{5,13},{6,14},{7,15},{8,0},{9,1},... | collective-permute-start | bytes 442376 | tf_op jit(solution)/shard_map/ppermute | solution.py:393
  100.3 7.8 %collective-permute-start.30 = (f32[32,1152]{1,0:T(8,128)S(1)}, f32[32,1152]{1,0:T(8,128)S(1)}, u32[]{:S(2)}, u32[]{:S(2)}) collective-permute-start(f32[32,1152]{1,0:T(8,128)S(1)} %add.93), channel_id=1, source_target_pairs={{0,6},{1,7},{2,4},{3,5},{4,2},{5,3},{6,0},{7,1},{8,14},{9,15},{10,... | collective-permute-start | bytes 442376 | tf_op jit(solution)/shard_map/ppermute | solution.py:393
  102.0 6.6 %collective-permute-start.29 = (f32[32,1152]{1,0:T(8,128)S(1)}, f32[32,1152]{1,0:T(8,128)S(1)}, u32[]{:S(2)}, u32[]{:S(2)}) collective-permute-start(f32[32,1152]{1,0:T(8,128)S(1)} %add.93), channel_id=1, source_target_pairs={{0,4},{1,5},{2,6},{3,7},{4,0},{5,1},{6,2},{7,3},{8,12},{9,13},{10,... | collective-permute-start | bytes 442376 | tf_op jit(solution)/shard_map/ppermute | solution.py:393
  103.4 7.1 %collective-permute-start.28 = (f32[32,1152]{1,0:T(8,128)S(1)}, f32[32,1152]{1,0:T(8,128)S(1)}, u32[]{:S(2)}, u32[]{:S(2)}) collective-permute-start(f32[32,1152]{1,0:T(8,128)S(1)} %add.93), channel_id=1, source_target_pairs={{0,2},{1,3},{2,0},{3,1},{4,6},{5,7},{6,4},{7,5},{8,10},{9,11},{10,... | collective-permute-start | bytes 442376 | tf_op jit(solution)/shard_map/ppermute | solution.py:393
  103.9 8.1 %collective-permute-start.31 = (f32[32,1152]{1,0:T(8,128)S(1)}, f32[32,1152]{1,0:T(8,128)S(1)}, u32[]{:S(2)}, u32[]{:S(2)}) collective-permute-start(f32[32,1152]{1,0:T(8,128)S(1)} %add.92), channel_id=1, source_target_pairs={{0,2},{1,3},{2,0},{3,1},{4,6},{5,7},{6,4},{7,5},{8,10},{9,11},{10,... | collective-permute-start | bytes 442376 | tf_op jit(solution)/shard_map/ppermute | solution.py:393
  112.2 7.6 %collective-permute-start.33 = (f32[32,1152]{1,0:T(8,128)S(1)}, f32[32,1152]{1,0:T(8,128)S(1)}, u32[]{:S(2)}, u32[]{:S(2)}) collective-permute-start(f32[32,1152]{1,0:T(8,128)S(1)} %add.92), channel_id=1, source_target_pairs={{0,6},{1,7},{2,4},{3,5},{4,2},{5,3},{6,0},{7,1},{8,14},{9,15},{10,... | collective-permute-start | bytes 442376 | tf_op jit(solution)/shard_map/ppermute | solution.py:393
  113.5 7.9 %collective-permute-start.32 = (f32[32,1152]{1,0:T(8,128)S(1)}, f32[32,1152]{1,0:T(8,128)S(1)}, u32[]{:S(2)}, u32[]{:S(2)}) collective-permute-start(f32[32,1152]{1,0:T(8,128)S(1)} %add.92), channel_id=1, source_target_pairs={{0,4},{1,5},{2,6},{3,7},{4,0},{5,1},{6,2},{7,3},{8,12},{9,13},{10,... | collective-permute-start | bytes 442376 | tf_op jit(solution)/shard_map/ppermute | solution.py:393
  (9 other events, 61.4 us)

commit v2 on v1

--- a/solution.py
+++ b/solution.py
@@ -123,16 +123,24 @@
             copy.start()
         copies.append((r, pair))
     q = size // 4
-    for r, pair in copies:
-        for copy in pair:
-            copy.wait()
-        ah[:, r], al[:, r] = split(a_buf[r].T)
-        bh[r], bl[r] = split(b_buf[r])
+
+    def add_rows(r):
         for r0, r1, c0, c1 in [(0, q, 0, size), (q, size, 0, q), (3 * q, size, 3 * q, size)]:
             product = mm((ah[r0:r1, r], al[r0:r1, r]), (bh[r, c0:c1], bl[r, c0:c1]))
             if r.start:
                 product += g[r0:r1, c0:c1]
             g[r0:r1, c0:c1] = product
+
+    before = None
+    for r, pair in copies:
+        for copy in pair:
+            copy.wait()
+        if before:
+            add_rows(before)
+        ah[:, r], al[:, r] = split(a_buf[r].T)
+        bh[r], bl[r] = split(b_buf[r])
+        before = r
+    add_rows(before)
     pack(g, packed, keep_ref, send_ref, me_ref[0], shards, 0)
 
 
@@ -170,7 +178,7 @@
 def other_gram(me, shards, ah, al, bh, bl):
     size = ah.shape[0]
     return call(
-        functools.partial(other_gram_kernel, shards), "other_gram", halves(size), 22, 0.5, 2,
+        functools.partial(other_gram_kernel, shards), "other_gram", halves(size), 18, 0.5, 2,
         in_specs=[SMEM] + [VMEM] * 4,
         out_specs=[VMEM, VMEM],
         scratch_shapes=[pltpu.VMEM((size, size), F32), packed_scratch(size)],
@@ -198,7 +206,7 @@
     rows, size = a.shape
     height = rows // parts
     return call(
-        affine_kernel, "affine", struct(height, size), 24, 1 / parts, 2,
+        affine_kernel, "affine", struct(height, size), 18, 1 / parts, 2,
         grid=(1,),
         in_specs=[
             pl.BlockSpec((height, size), lambda r: (part, 0)),
@@ -226,8 +234,7 @@
     )
 
 
-def apply_first(a_ref, base_refs, out_ref, ah, al, hi, lo):
-    ah[...], al[...] = split(a_ref[...])
+def apply_first(base_refs, out_ref, ah, al, hi, lo):
     for column in range(4):
         c, product = sym_product(ah, al, hi, lo, 0, column)
         at = 0
@@ -247,20 +254,20 @@
 
 def partial_kernel(shards, count, me_ref, *refs):
     pieces, refs = refs[:count], refs[count:]
-    a_ref, base_refs, (out_ref, ah, al, hi, lo, packed) = refs[0], refs[1:-6], refs[-6:]
+    ah, al, base_refs, (out_ref, hi, lo, packed) = refs[0], refs[1], refs[2:-4], refs[-4:]
     unpack(pieces, packed, hi, lo, me_ref[0], shards, 0)
-    apply_first(a_ref, base_refs, out_ref, ah, al, hi, lo)
-
-
-def partial_apply(me, shards, pieces, a, base):
-    rows, size = a.shape
+    apply_first(base_refs, out_ref, ah, al, hi, lo)
+
+
+def partial_apply(me, shards, pieces, ah, al, base):
+    rows, size = ah.shape
     return call(
         functools.partial(partial_kernel, shards, len(pieces)), "partial_apply",
-        struct(rows, size), 22, 0.5, 3,
-        in_specs=[SMEM] + [VMEM] * (len(pieces) + 1 + len(base)),
+        struct(rows, size), 18, 0.5, 3,
+        in_specs=[SMEM] + [VMEM] * (len(pieces) + 2 + len(base)),
         out_specs=VMEM,
-        scratch_shapes=sym_scratch(rows, size),
-    )(me, *pieces, a, *base)
+        scratch_shapes=sym_scratch(rows, size)[2:],
+    )(me, *pieces, ah, al, *base)
 
 
 def turn_kernel(x_ref, xh, xl):
@@ -271,6 +278,17 @@
     part = struct(*x.shape[::-1], dtype=BF16)
     return call(
         turn_kernel, "turn", [part, part], 16, 0.1, 2, in_specs=[VMEM], out_specs=[VMEM] * 2
+    )(x)
+
+
+def cut_kernel(x_ref, hi, lo):
+    hi[...], lo[...] = split(x_ref[...])
+
+
+def cut(x):
+    part = struct(*x.shape, dtype=BF16)
+    return call(
+        cut_kernel, "cut", [part, part], 16, 0.1, 2, in_specs=[VMEM], out_specs=[VMEM] * 2
     )(x)
 
 
@@ -278,8 +296,9 @@
     pieces, refs = refs[:count], refs[count:]
     a_ref, base_refs, refs = refs[0], refs[1:-9], refs[-9:]
     xh, xl, out_ref, col_ref, ah, al, hi, lo, packed = refs
+    ah[...], al[...] = split(a_ref[...])
     unpack(pieces, packed, hi, lo, me_ref[0], shards, 0)
-    apply_first(a_ref, base_refs, out_ref, ah, al, hi, lo)
+    apply_first(base_refs, out_ref, ah, al, hi, lo)
     col_ref[...] = mm((xh[...], xl[...]), split(out_ref[:, :col_ref.shape[1]]))
 
 
@@ -287,7 +306,7 @@
     rows, size = a.shape
     return call(
         functools.partial(early_kernel, shards, len(pieces)), "early_middle",
-        [struct(rows, size), struct(size, size // 4)], 24, 0.75, 5,
+        [struct(rows, size), struct(size, size // 4)], 20, 0.75, 5,
         in_specs=[SMEM] + [VMEM] * (len(pieces) + 3 + len(base)),
         out_specs=[VMEM] * 2,
         scratch_shapes=sym_scratch(rows, size),
@@ -320,7 +339,7 @@
     part = struct(rows, size - size // 4, dtype=BF16)
     return call(
         functools.partial(second_gram_kernel, shards, len(pieces)), "second_gram",
-        halves(size) + [struct(rows, size), part, part], 26, 0.8, 5,
+        halves(size) + [struct(rows, size), part, part], 20, 0.8, 5,
         in_specs=[SMEM] + [VMEM] * (len(pieces) + 5),
         out_specs=[VMEM] * 5,
         scratch_shapes=sym_scratch(rows, size) + [pltpu.VMEM((size, size), F32)],
@@ -335,7 +354,7 @@
 def fourth_gram(me, shards, xh, xl, mh, ml):
     size = xh.shape[0]
     return call(
-        functools.partial(fourth_gram_kernel, shards), "fourth_gram", halves(size), 22, 0.5, 2,
+        functools.partial(fourth_gram_kernel, shards), "fourth_gram", halves(size), 18, 0.5, 2,
         in_specs=[SMEM] + [VMEM] * 4,
         out_specs=[VMEM, VMEM],
         scratch_shapes=[pltpu.VMEM((size, size), F32), packed_scratch(size)],
@@ -344,7 +363,7 @@
 
 def last_kernel(shards, count, me_ref, *refs):
     pieces = refs[:count]
-    x_ref, z_ref, out_hbm, ah, al, hi, lo, packed, out, sems = refs[count:]
+    ah, al, z_ref, out_hbm, hi, lo, packed, out, sems = refs[count:]
     q = hi.shape[0] // 4
     copies = []
 
@@ -355,7 +374,6 @@
         copies.append(copy)
 
     send(z_ref, 0)
-    ah[:, q:], al[:, q:] = split(x_ref[:, q:])
     unpack(pieces, packed, hi, lo, me_ref[0], shards, 1)
     for column in (1, 2, 3):
         c, product = sym_product(ah, al, hi, lo, 1, column)
@@ -365,15 +383,15 @@
         copy.wait()
 
 
-def last_step(me, shards, pieces, x, z):
-    rows, size = x.shape
-    return call(
-        functools.partial(last_kernel, shards, len(pieces)), "last", struct(rows, size), 26, 0.5, 3,
-        in_specs=[SMEM] + [VMEM] * (len(pieces) + 2),
+def last_step(me, shards, pieces, ah, al, z):
+    rows, size = z.shape
+    return call(
+        functools.partial(last_kernel, shards, len(pieces)), "last", struct(rows, size), 22, 0.5, 3,
+        in_specs=[SMEM] + [VMEM] * (len(pieces) + 3),
         out_specs=pl.BlockSpec(memory_space=pltpu.HBM),
-        scratch_shapes=sym_scratch(rows, size)
+        scratch_shapes=sym_scratch(rows, size)[2:]
         + [pltpu.VMEM((rows, size), F32), pltpu.SemaphoreType.DMA((4,))],
-    )(me, *pieces, x, z)
+    )(me, *pieces, ah, al, z)
 
 
 CORE = 1
@@ -455,7 +473,7 @@
     b.own(close(env, *got_b))
 
     got_b = b.gather_plane()
-    *got_a, got_b[0] = close(env, *got_a, got_b[0])
+    *got_a, got_b[2] = close(env, *got_a, got_b[2])
     got_a = a.gather_core(got_a)
     pieces_a = [a.mine, *close(env, got_a)]
     late(env, pieces_a)
@@ -469,31 +487,26 @@
         x0=orbitals_zero, x1=orbitals_one, s0=correlation_zero, s1=correlation_one, c=cotangent
     )
 
-    def thirds(name, left, right):
-        def put(at, part, parts):
-            def work(env):
-                env[f"{name}{at}"] = affine(env[left], env[right], part, parts)
-            return work
-        return [put(0, 0, 2), put(1, 2, 4), put(2, 3, 4)]
-
-    def three(env, name):
-        return [env[f"{name}{at}"] for at in range(3)]
+    def half(name, left, right, part):
+        def work(env):
+            env[f"{name}{part}"] = affine(env[left], env[right], part, 2)
+        return work
+
+    def turned(env):
+        env["xh"], env["xl"] = turn(env["x0"])
+
+    def parted(env):
+        env["x0h"], env["x0l"] = cut(env["x0"])
 
     def early(env, pieces):
         env["mid"], env["col"] = early_middle(
-            me, SHARDS, pieces, env["x1"], three(env, "m"), env["xh"], env["xl"]
+            me, SHARDS, pieces, env["x1"], [env["m0"], env["m1"]], env["xh"], env["xl"]
         )
-
-    half, quarter, rest = thirds("m", "c", "s1")
-
-    def rest_and_turn(env):
-        rest(env)
-        env["xh"], env["xl"] = turn(env["x0"])
 
     keep, send, *parts = first_gram(me, SHARDS, env["x1"], env["c"])
     _, one = sum_chunks(
         count, env, (keep, send), lambda env: other_gram(me, SHARDS, *parts),
-        [half, quarter, rest_and_turn], early,
+        [half("m", "c", "s1", 0), turned, half("m", "c", "s1", 1)], early,
     )
 
     keep, send, env["mid"], mh, ml = second_gram(
@@ -501,14 +514,14 @@
     )
 
     def late(env, pieces):
-        env["z"] = partial_apply(me, SHARDS, pieces, env["x0"], three(env, "d"))
+        env["z"] = partial_apply(me, SHARDS, pieces, env["x0h"], env["x0l"], [env["d0"], env["d1"]])
 
     _, two = sum_chunks(
         count, env, (keep, send),
         lambda env: fourth_gram(me, SHARDS, env["xh"], env["xl"], mh, ml),
-        thirds("d", "mid", "s0"), late,
-    )
-    return last_step(me, SHARDS, two, env["x0"], env["z"])
+        [half("d", "mid", "s0", 0), parted, half("d", "mid", "s0", 1)], late,
+    )
+    return last_step(me, SHARDS, two, env["x0h"], env["x0l"], env["z"])
 
 
 def solution(mesh):

time: 129 us -> 124 us (0.961)
  starting transfers between devices: 44.8 us -> 38.5 us
  waiting for transfers between devices: 27.6 us -> 29.2 us
    ppermute x36, starting transfers between devices: 44.8 us -> 38.5 us  [swap(): return lax.ppermute(x, 'row', [(i, i ^ offset) for i in range(self.count)])]
    ppermute x36, waiting for transfers between devices: 27.6 us -> 29.2 us  [swap(): return lax.ppermute(x, 'row', [(i, i ^ offset) for i in range(self.count)])]
    pallas_call x6 -> x5, Pallas kernels: 19.1 us -> 18.3 us  [the longest x4 17.5 us: affine(): call(affine_kernel, 'affine', struct(height, size), 18, 1 / parts, 2, gri...]
  transfers between devices with their start and end apart: 36 -> 36, of which waited for: 18 -> 14; matrix products, arithmetic and copies ran while one was open for 0% -> 0% of each run, Pallas kernels for 29% -> 29%
where the time goes in v2:
time: 124 us
  Pallas kernels  55.2 us (45%)
  starting transfers between devices  38.5 us (31%)
  waiting for transfers between devices  29.2 us (24%)
    ppermute x36, starting transfers between devices, swap(): return lax.ppermute(x, 'row', [(i, i ^ offset) for i in range(self.count)])  38.5 us
    ppermute x36, waiting for transfers between devices, swap(): return lax.ppermute(x, 'row', [(i, i ^ offset) for i in range(self.count)])  29.2 us
    pallas_call x4, Pallas kernels, affine(): call(affine_kernel, 'affine', struct(height, size), 18, 1 / parts, 2, gri...  17.5 us
    pallas_call x1, Pallas kernels, first_gram(): call(functools.partial(first_gram_kernel, shards), 'first_gram', halves(s...  7.72 us
    pallas_call x1, Pallas kernels, second_gram(): call(functools.partial(second_gram_kernel, shards, len(pieces)), 'second_...  5.9 us
    pallas_call x1, Pallas kernels, early_middle(): call(functools.partial(early_kernel, shards, len(pieces)), 'early_middle'...  5.54 us
    pallas_call x1, Pallas kernels, last_step(): call(functools.partial(last_kernel, shards, len(pieces)), 'last', struct(...  5.18 us
    pallas_call x1, Pallas kernels, fourth_gram(): call(functools.partial(fourth_gram_kernel, shards), 'fourth_gram', halves...  3.88 us
  transfers between devices with their start and end apart: 36, of which 14 were waited for; matrix products, arithmetic and copies ran while one was open for 0% of the time, Pallas kernels for 29%

profile of v2, /device:TPU:0, one launch (start us, length us, event | category | flops | bytes accessed | tf_op | source)
XLA Modules:
  0.0 124.2 jit_solution(10383075371928795892)
XLA Ops:
  0.0 7.7 %first_gram.1 = (f32[128,1152]{1,0:T(8,128)S(1)}, f32[128,1152]{1,0:T(8,128)S(1)}, bf16[1024,1024]{1,0:T(8,128)(2,1)S(1)}, bf16[1024,1024]{1,0:T(8,128)(2,1)S(1)...) custom-call(s32[1]{0:T(128)} %bitcast.me_ref, f32[1024,1024]{1,0:T(8,128)} %refs_2_.1, f32[1024,1024]{1,0:T(8,128)} %a_ref.1), custom_call_target="tpu_custom_call" | custom-call | flops 3221225472 | bytes 16777216 | tf_op jit(solution)/shard_map/first_gram/pallas_call | solution.py:150
  8.3 3.6 %other_gram.1 = (f32[128,1152]{1,0:T(8,128)S(1)}, f32[128,1152]{1,0:T(8,128)S(1)}) custom-call(s32[1]{0:T(128)} %bitcast.me_ref, bf16[1024,1024]{1,0:T(8,128)(2,1)S(1)} %get-tuple-element.165.ah, bf16[1024,1024]{1,0:T(8,128)(2,1)S(1)} %get-tuple-element.166.al, bf16[1024,1024]{1,0:T(8,128)(2,1)S(1)} %get-tuple-element.167.bh, ...), custom_call_target="tpu_custom_call" | custom-call | flops 3221225472 | bytes 8388608 | tf_op jit(solution)/shard_map/other_gram/pallas_call | solution.py:180
  12.1 4.0 %collective-permute-start.7 = (f32[32,1152]{1,0:T(8,128)S(1)}, f32[32,1152]{1,0:T(8,128)S(1)}, u32[]{:S(2)}, u32[]{:S(2)}) collective-permute-start(f32[32,1152]{1,0:T(8,128)S(1)} %get-tuple-element.329), channel_id=1, source_target_pairs={{0,6},{1,7},{2,4},{3,5},{4,2},{5,3},{6,0},{7,1},{8,14},{9,15},{10,... | collective-permute-start | bytes 442376 | tf_op jit(solution)/shard_map/ppermute | solution.py:411
  16.8 4.3 %affine.4.refs_3_ = f32[512,1024]{1,0:T(8,128)S(1)} custom-call(f32[1024,1024]{1,0:T(8,128)S(1)} %copy-done.1, f32[1024,1024]{1,0:T(8,128)S(1)} %copy-done.2), custom_call_target="tpu_custom_call" | custom-call | flops 3221225472 | bytes 8388608 | tf_op jit(solution)/shard_map/affine/pallas_call | solution.py:208
  21.3 2.9 %collective-permute-start.4 = (f32[32,1152]{1,0:T(8,128)S(1)}, f32[32,1152]{1,0:T(8,128)S(1)}, u32[]{:S(2)}, u32[]{:S(2)}) collective-permute-start(f32[32,1152]{1,0:T(8,128)S(1)} %get-tuple-element.332), channel_id=1, source_target_pairs={{0,6},{1,7},{2,4},{3,5},{4,2},{5,3},{6,0},{7,1},{8,14},{9,15},{10,... | collective-permute-start | bytes 442376 | tf_op jit(solution)/shard_map/ppermute | solution.py:411
  26.3 3.0 %collective-permute-start.9 = (f32[32,1152]{1,0:T(8,128)S(1)}, f32[32,1152]{1,0:T(8,128)S(1)}, u32[]{:S(2)}, u32[]{:S(2)}) collective-permute-start(f32[32,1152]{1,0:T(8,128)S(1)} %fusion.5), channel_id=1, source_target_pairs={{0,8},{1,9},{2,10},{3,11},{4,12},{5,13},{6,14},{7,15},{8,0},{9,1},... | collective-permute-start | bytes 442376 | tf_op jit(solution)/shard_map/ppermute | solution.py:411
  29.2 4.7 %collective-permute-done.3 = f32[32,1152]{1,0:T(8,128)S(1)} collective-permute-done((f32[32,1152]{1,0:T(8,128)S(1)}, f32[32,1152]{1,0:T(8,128)S(1)}, u32[]{:S(2)}, u32[]{:S(2)}) %collective-permute-start.3) | collective-permute-done | bytes 147488 | tf_op jit(solution)/shard_map/ppermute | solution.py:411
  35.0 4.5 %affine.5.refs_4_ = f32[512,1024]{1,0:T(8,128)S(1)} custom-call(f32[1024,1024]{1,0:T(8,128)S(1)} %copy-done.1, f32[1024,1024]{1,0:T(8,128)S(1)} %copy-done.2), custom_call_target="tpu_custom_call" | custom-call | flops 3221225472 | bytes 8388608 | tf_op jit(solution)/shard_map/affine/pallas_call | solution.py:208
  39.5 1.4 %collective-permute-start.14 = (f32[32,1152]{1,0:T(8,128)S(1)}, f32[32,1152]{1,0:T(8,128)S(1)}, u32[]{:S(2)}, u32[]{:S(2)}) collective-permute-start(f32[32,1152]{1,0:T(8,128)S(1)} %add.83), channel_id=1, source_target_pairs={{0,6},{1,7},{2,4},{3,5},{4,2},{5,3},{6,0},{7,1},{8,14},{9,15},{10,... | collective-permute-start | bytes 442376 | tf_op jit(solution)/shard_map/ppermute | solution.py:411
  43.2 1.5 %collective-permute-start.15 = (f32[32,1152]{1,0:T(8,128)S(1)}, f32[32,1152]{1,0:T(8,128)S(1)}, u32[]{:S(2)}, u32[]{:S(2)}) collective-permute-start(f32[32,1152]{1,0:T(8,128)S(1)} %add.82), channel_id=1, source_target_pairs={{0,6},{1,7},{2,4},{3,5},{4,2},{5,3},{6,0},{7,1},{8,14},{9,15},{10,... | collective-permute-start | bytes 442376 | tf_op jit(solution)/shard_map/ppermute | solution.py:411
  44.7 2.6 %collective-permute-done.14 = f32[32,1152]{1,0:T(8,128)S(1)} collective-permute-done((f32[32,1152]{1,0:T(8,128)S(1)}, f32[32,1152]{1,0:T(8,128)S(1)}, u32[]{:S(2)}, u32[]{:S(2)}) %collective-permute-start.14) | collective-permute-done | bytes 147488 | tf_op jit(solution)/shard_map/ppermute | solution.py:411
  47.3 2.3 %collective-permute-done.13 = f32[32,1152]{1,0:T(8,128)S(1)} collective-permute-done((f32[32,1152]{1,0:T(8,128)S(1)}, f32[32,1152]{1,0:T(8,128)S(1)}, u32[]{:S(2)}, u32[]{:S(2)}) %collective-permute-start.13) | collective-permute-done | bytes 147488 | tf_op jit(solution)/shard_map/ppermute | solution.py:411
  49.6 2.4 %collective-permute-done.15 = f32[32,1152]{1,0:T(8,128)S(1)} collective-permute-done((f32[32,1152]{1,0:T(8,128)S(1)}, f32[32,1152]{1,0:T(8,128)S(1)}, u32[]{:S(2)}, u32[]{:S(2)}) %collective-permute-start.15) | collective-permute-done | bytes 147488 | tf_op jit(solution)/shard_map/ppermute | solution.py:411
  54.1 5.5 %early_middle.1 = (f32[1024,1024]{1,0:T(8,128)S(1)}, f32[1024,256]{1,0:T(8,128)S(1)}) custom-call(s32[1]{0:T(128)} %bitcast.me_ref, f32[128,1152]{1,0:T(8,128)S(1)} %pad_maximum_fusion.refs_0_, f32[128,1152]{1,0:T(8,128)S(1)} %collective-permute-done.16.refs_1_, f32[1024,1024]{1,0:T(8,128)S(1)} %copy-done.3, f32[512,1024]{1,0:T(8,128)S(1)} %affine.4.refs_3_, ...), custom_call_target="tpu_custom_call" | custom-call | flops 4831838208 | bytes 20971520 | tf_op jit(solution)/shard_map/early_middle/pallas_call | solution.py:307
  60.0 1.9 %collective-permute-done.17.refs_1_ = f32[128,1152]{1,0:T(8,128)S(1)} collective-permute-done((f32[128,1152]{1,0:T(8,128)S(1)}, f32[128,1152]{1,0:T(8,128)S(1)}, u32[]{:S(2)}, u32[]{:S(2)}) %collective-permute-start.17) | collective-permute-done | bytes 589856 | tf_op jit(solution)/shard_map/ppermute | solution.py:411
  61.8 5.9 %second_gram.1 = (f32[128,1152]{1,0:T(8,128)S(1)}, f32[128,1152]{1,0:T(8,128)S(1)}, f32[1024,1024]{1,0:T(8,128)S(1)}, bf16[1024,768]{1,0:T(8,128)(2,1)S(1)}, bf16[1024,768]{1,0:T(8,128)(2,1)S(1)}) custom-call(s32[1]{0:T(128)} %bitcast.me_ref, f32[128,1152]{1,0:T(8,128)S(1)} %pad_maximum_fusion.1.refs_0_, f32[128,1152]{1,0:T(8,128)S(1)} %collective-permute-done.17.refs_1_, ...), custom_call_target="tpu_custom_call" | custom-call | flops 5153960960 | bytes 20971520 | tf_op jit(solution)/shard_map/second_gram/pallas_call | solution.py:340
  67.9 3.9 %fourth_gram.1 = (f32[128,1152]{1,0:T(8,128)S(1)}, f32[128,1152]{1,0:T(8,128)S(1)}) custom-call(s32[1]{0:T(128)} %bitcast.me_ref, bf16[1024,1024]{1,0:T(8,128)(2,1)S(1)} %get-tuple-element.253.refs_5_.refs_4_.xh, bf16[1024,1024]{1,0:T(8,128)(2,1)S(1)} %get-tuple-element.254.refs_6_.refs_5_.xl, bf16[1024,768]{1,0:T(8,128)(2,1)S(1)} %get-tuple-element.257.mh, ...), custom_call_target="tpu_custom_call" | custom-call | flops 3221225472 | bytes 8388608 | tf_op jit(solution)/shard_map/fourth_gram/pallas_call | solution.py:356
  72.4 1.6 %collective-permute-start.25 = (f32[32,1152]{1,0:T(8,128)S(1)}, f32[32,1152]{1,0:T(8,128)S(1)}, u32[]{:S(2)}, u32[]{:S(2)}) collective-permute-start(f32[32,1152]{1,0:T(8,128)S(1)} %get-tuple-element.323), channel_id=1, source_target_pairs={{0,6},{1,7},{2,4},{3,5},{4,2},{5,3},{6,0},{7,1},{8,14},{9,15},{10,... | collective-permute-start | bytes 442376 | tf_op jit(solution)/shard_map/ppermute | solution.py:411
  75.9 4.4 %affine.6.refs_4_ = f32[512,1024]{1,0:T(8,128)S(1)} custom-call(f32[1024,1024]{1,0:T(8,128)S(1)} %get-tuple-element.290.a_ref, f32[1024,1024]{1,0:T(8,128)S(1)} %copy-done.4), custom_call_target="tpu_custom_call" | custom-call | flops 3221225472 | bytes 8388608 | tf_op jit(solution)/shard_map/affine/pallas_call | solution.py:208
  80.4 1.6 %collective-permute-start.22 = (f32[32,1152]{1,0:T(8,128)S(1)}, f32[32,1152]{1,0:T(8,128)S(1)}, u32[]{:S(2)}, u32[]{:S(2)}) collective-permute-start(f32[32,1152]{1,0:T(8,128)S(1)} %get-tuple-element.326), channel_id=1, source_target_pairs={{0,6},{1,7},{2,4},{3,5},{4,2},{5,3},{6,0},{7,1},{8,14},{9,15},{10,... | collective-permute-start | bytes 442376 | tf_op jit(solution)/shard_map/ppermute | solution.py:411
  84.9 2.4 %collective-permute-start.27 = (f32[32,1152]{1,0:T(8,128)S(1)}, f32[32,1152]{1,0:T(8,128)S(1)}, u32[]{:S(2)}, u32[]{:S(2)}) collective-permute-start(f32[32,1152]{1,0:T(8,128)S(1)} %fusion.1), channel_id=1, source_target_pairs={{0,8},{1,9},{2,10},{3,11},{4,12},{5,13},{6,14},{7,15},{8,0},{9,1},... | collective-permute-start | bytes 442376 | tf_op jit(solution)/shard_map/ppermute | solution.py:411
  87.3 2.4 %collective-permute-done.22 = f32[32,1152]{1,0:T(8,128)S(1)} collective-permute-done((f32[32,1152]{1,0:T(8,128)S(1)}, f32[32,1152]{1,0:T(8,128)S(1)}, u32[]{:S(2)}, u32[]{:S(2)}) %collective-permute-start.22) | collective-permute-done | bytes 147488 | tf_op jit(solution)/shard_map/ppermute | solution.py:411
  89.7 2.5 %collective-permute-done.21 = f32[32,1152]{1,0:T(8,128)S(1)} collective-permute-done((f32[32,1152]{1,0:T(8,128)S(1)}, f32[32,1152]{1,0:T(8,128)S(1)}, u32[]{:S(2)}, u32[]{:S(2)}) %collective-permute-start.21) | collective-permute-done | bytes 147488 | tf_op jit(solution)/shard_map/ppermute | solution.py:411
  93.6 4.4 %affine.7.refs_5_ = f32[512,1024]{1,0:T(8,128)S(1)} custom-call(f32[1024,1024]{1,0:T(8,128)S(1)} %get-tuple-element.290.a_ref, f32[1024,1024]{1,0:T(8,128)S(1)} %copy-done.4), custom_call_target="tpu_custom_call" | custom-call | flops 3221225472 | bytes 8388608 | tf_op jit(solution)/shard_map/affine/pallas_call | solution.py:208
  98.0 2.2 %collective-permute-start.32 = (f32[32,1152]{1,0:T(8,128)S(1)}, f32[32,1152]{1,0:T(8,128)S(1)}, u32[]{:S(2)}, u32[]{:S(2)}) collective-permute-start(f32[32,1152]{1,0:T(8,128)S(1)} %add.93), channel_id=1, source_target_pairs={{0,6},{1,7},{2,4},{3,5},{4,2},{5,3},{6,0},{7,1},{8,14},{9,15},{10,... | collective-permute-start | bytes 442376 | tf_op jit(solution)/shard_map/ppermute | solution.py:411
  101.6 2.2 %collective-permute-start.33 = (f32[32,1152]{1,0:T(8,128)S(1)}, f32[32,1152]{1,0:T(8,128)S(1)}, u32[]{:S(2)}, u32[]{:S(2)}) collective-permute-start(f32[32,1152]{1,0:T(8,128)S(1)} %add.92), channel_id=1, source_target_pairs={{0,6},{1,7},{2,4},{3,5},{4,2},{5,3},{6,0},{7,1},{8,14},{9,15},{10,... | collective-permute-start | bytes 442376 | tf_op jit(solution)/shard_map/ppermute | solution.py:411
  103.8 2.0 %collective-permute-done.32 = f32[32,1152]{1,0:T(8,128)S(1)} collective-permute-done((f32[32,1152]{1,0:T(8,128)S(1)}, f32[32,1152]{1,0:T(8,128)S(1)}, u32[]{:S(2)}, u32[]{:S(2)}) %collective-permute-start.32) | collective-permute-done | bytes 147488 | tf_op jit(solution)/shard_map/ppermute | solution.py:411
  105.8 2.3 %collective-permute-done.31 = f32[32,1152]{1,0:T(8,128)S(1)} collective-permute-done((f32[32,1152]{1,0:T(8,128)S(1)}, f32[32,1152]{1,0:T(8,128)S(1)}, u32[]{:S(2)}, u32[]{:S(2)}) %collective-permute-start.31) | collective-permute-done | bytes 147488 | tf_op jit(solution)/shard_map/ppermute | solution.py:411
  108.1 2.3 %collective-permute-done.33 = f32[32,1152]{1,0:T(8,128)S(1)} collective-permute-done((f32[32,1152]{1,0:T(8,128)S(1)}, f32[32,1152]{1,0:T(8,128)S(1)}, u32[]{:S(2)}, u32[]{:S(2)}) %collective-permute-start.33) | collective-permute-done | bytes 147488 | tf_op jit(solution)/shard_map/ppermute | solution.py:411
  112.5 3.7 %partial_apply.1.refs_4_ = f32[1024,1024]{1,0:T(8,128)S(1)} custom-call(s32[1]{0:T(128)} %bitcast.me_ref, f32[128,1152]{1,0:T(8,128)S(1)} %pad_maximum_fusion.2.refs_0_, f32[128,1152]{1,0:T(8,128)S(1)} %collective-permute-done.34.refs_1_, bf16[1024,1024]{1,0:T(8,128)(2,1)S(1)} %get-tuple-element.320.refs_2_, ...), custom_call_target="tpu_custom_call" | custom-call | flops 3221225472 | bytes 12582912 | tf_op jit(solution)/shard_map/partial_apply/pallas_call | solution.py:264
  116.9 2.0 %collective-permute-done.35.refs_1_ = f32[128,1152]{1,0:T(8,128)S(1)} collective-permute-done((f32[128,1152]{1,0:T(8,128)S(1)}, f32[128,1152]{1,0:T(8,128)S(1)}, u32[]{:S(2)}, u32[]{:S(2)}) %collective-permute-start.35) | collective-permute-done | bytes 589856 | tf_op jit(solution)/shard_map/ppermute | solution.py:411
  118.9 5.2 %last.1 = f32[1024,1024]{1,0:T(8,128)} custom-call(s32[1]{0:T(128)} %bitcast.me_ref, f32[128,1152]{1,0:T(8,128)S(1)} %pad_maximum_fusion.3.refs_0_, f32[128,1152]{1,0:T(8,128)S(1)} %collective-permute-done.35.refs_1_, bf16[1024,1024]{1,0:T(8,128)(2,1)S(1)} %get-tuple-element.320.refs_2_, bf16[1024,1024]{1,0:T(8,128)(2,1)S(1)} %get-tuple-element.321.refs_3_, ...), custom_call_target="tpu_custom_call" | custom-call | flops 3221225472 | bytes 12582912 | tf_op jit(solution)/shard_map/last/pallas_call | solution.py:388
  (83 shorter events, 20.3 us)
Async XLA Ops:
  7.7 4.2 %collective-permute-start = (f32[128,1152]{1,0:T(8,128)S(1)}, f32[128,1152]{1,0:T(8,128)S(1)}, u32[]{:S(2)}, u32[]{:S(2)}) collective-permute-start(f32[128,1152]{1,0:T(8,128)S(1)} %get-tuple-element.164), channel_id=1, source_target_pairs={{0,1},{1,0},{2,3},{3,2},{4,5},{5,4},{6,7},{7,6},{8,9},{9,8},{10,11... | collective-permute-start | bytes 1769480 | tf_op jit(solution)/shard_map/ppermute | solution.py:411
  11.9 9.2 %collective-permute-start.1 = (f32[128,1152]{1,0:T(8,128)S(1)}, f32[128,1152]{1,0:T(8,128)S(1)}, u32[]{:S(2)}, u32[]{:S(2)}) collective-permute-start(f32[128,1152]{1,0:T(8,128)S(1)} %get-tuple-element.172), channel_id=1, source_target_pairs={{0,1},{1,0},{2,3},{3,2},{4,5},{5,4},{6,7},{7,6},{8,9},{9,8},{10,11... | collective-permute-start | bytes 1769480 | tf_op jit(solution)/shard_map/ppermute | solution.py:411
  12.1 13.8 %collective-permute-start.7 = (f32[32,1152]{1,0:T(8,128)S(1)}, f32[32,1152]{1,0:T(8,128)S(1)}, u32[]{:S(2)}, u32[]{:S(2)}) collective-permute-start(f32[32,1152]{1,0:T(8,128)S(1)} %get-tuple-element.329), channel_id=1, source_target_pairs={{0,6},{1,7},{2,4},{3,5},{4,2},{5,3},{6,0},{7,1},{8,14},{9,15},{10,... | collective-permute-start | bytes 442376 | tf_op jit(solution)/shard_map/ppermute | solution.py:411
  16.2 10.0 %collective-permute-start.6 = (f32[32,1152]{1,0:T(8,128)S(1)}, f32[32,1152]{1,0:T(8,128)S(1)}, u32[]{:S(2)}, u32[]{:S(2)}) collective-permute-start(f32[32,1152]{1,0:T(8,128)S(1)} %get-tuple-element.330), channel_id=1, source_target_pairs={{0,4},{1,5},{2,6},{3,7},{4,0},{5,1},{6,2},{7,3},{8,12},{9,13},{10,... | collective-permute-start | bytes 442376 | tf_op jit(solution)/shard_map/ppermute | solution.py:411
  16.6 9.6 %collective-permute-start.5 = (f32[32,1152]{1,0:T(8,128)S(1)}, f32[32,1152]{1,0:T(8,128)S(1)}, u32[]{:S(2)}, u32[]{:S(2)}) collective-permute-start(f32[32,1152]{1,0:T(8,128)S(1)} %get-tuple-element.331), channel_id=1, source_target_pairs={{0,2},{1,3},{2,0},{3,1},{4,6},{5,7},{6,4},{7,5},{8,10},{9,11},{10,... | collective-permute-start | bytes 442376 | tf_op jit(solution)/shard_map/ppermute | solution.py:411
  21.3 8.0 %collective-permute-start.4 = (f32[32,1152]{1,0:T(8,128)S(1)}, f32[32,1152]{1,0:T(8,128)S(1)}, u32[]{:S(2)}, u32[]{:S(2)}) collective-permute-start(f32[32,1152]{1,0:T(8,128)S(1)} %get-tuple-element.332), channel_id=1, source_target_pairs={{0,6},{1,7},{2,4},{3,5},{4,2},{5,3},{6,0},{7,1},{8,14},{9,15},{10,... | collective-permute-start | bytes 442376 | tf_op jit(solution)/shard_map/ppermute | solution.py:411
  24.2 9.7 %collective-permute-start.3 = (f32[32,1152]{1,0:T(8,128)S(1)}, f32[32,1152]{1,0:T(8,128)S(1)}, u32[]{:S(2)}, u32[]{:S(2)}) collective-permute-start(f32[32,1152]{1,0:T(8,128)S(1)} %get-tuple-element.333), channel_id=1, source_target_pairs={{0,4},{1,5},{2,6},{3,7},{4,0},{5,1},{6,2},{7,3},{8,12},{9,13},{10,... | collective-permute-start | bytes 442376 | tf_op jit(solution)/shard_map/ppermute | solution.py:411
  25.9 7.9 %collective-permute-start.2 = (f32[32,1152]{1,0:T(8,128)S(1)}, f32[32,1152]{1,0:T(8,128)S(1)}, u32[]{:S(2)}, u32[]{:S(2)}) collective-permute-start(f32[32,1152]{1,0:T(8,128)S(1)} %get-tuple-element.334), channel_id=1, source_target_pairs={{0,2},{1,3},{2,0},{3,1},{4,6},{5,7},{6,4},{7,5},{8,10},{9,11},{10,... | collective-permute-start | bytes 442376 | tf_op jit(solution)/shard_map/ppermute | solution.py:411
  26.3 13.3 %collective-permute-start.9 = (f32[32,1152]{1,0:T(8,128)S(1)}, f32[32,1152]{1,0:T(8,128)S(1)}, u32[]{:S(2)}, u32[]{:S(2)}) collective-permute-start(f32[32,1152]{1,0:T(8,128)S(1)} %fusion.5), channel_id=1, source_target_pairs={{0,8},{1,9},{2,10},{3,11},{4,12},{5,13},{6,14},{7,15},{8,0},{9,1},... | collective-permute-start | bytes 442376 | tf_op jit(solution)/shard_map/ppermute | solution.py:411
  33.9 9.2 %collective-permute-start.8 = (f32[32,1152]{1,0:T(8,128)S(1)}, f32[32,1152]{1,0:T(8,128)S(1)}, u32[]{:S(2)}, u32[]{:S(2)}) collective-permute-start(f32[32,1152]{1,0:T(8,128)S(1)} %fusion.7), channel_id=1, source_target_pairs={{0,8},{1,9},{2,10},{3,11},{4,12},{5,13},{6,14},{7,15},{8,0},{9,1},... | collective-permute-start | bytes 442376 | tf_op jit(solution)/shard_map/ppermute | solution.py:411
  39.5 7.8 %collective-permute-start.14 = (f32[32,1152]{1,0:T(8,128)S(1)}, f32[32,1152]{1,0:T(8,128)S(1)}, u32[]{:S(2)}, u32[]{:S(2)}) collective-permute-start(f32[32,1152]{1,0:T(8,128)S(1)} %add.83), channel_id=1, source_target_pairs={{0,6},{1,7},{2,4},{3,5},{4,2},{5,3},{6,0},{7,1},{8,14},{9,15},{10,... | collective-permute-start | bytes 442376 | tf_op jit(solution)/shard_map/ppermute | solution.py:411
  41.0 8.7 %collective-permute-start.13 = (f32[32,1152]{1,0:T(8,128)S(1)}, f32[32,1152]{1,0:T(8,128)S(1)}, u32[]{:S(2)}, u32[]{:S(2)}) collective-permute-start(f32[32,1152]{1,0:T(8,128)S(1)} %add.83), channel_id=1, source_target_pairs={{0,4},{1,5},{2,6},{3,7},{4,0},{5,1},{6,2},{7,3},{8,12},{9,13},{10,... | collective-permute-start | bytes 442376 | tf_op jit(solution)/shard_map/ppermute | solution.py:411
  41.8 7.8 %collective-permute-start.12 = (f32[32,1152]{1,0:T(8,128)S(1)}, f32[32,1152]{1,0:T(8,128)S(1)}, u32[]{:S(2)}, u32[]{:S(2)}) collective-permute-start(f32[32,1152]{1,0:T(8,128)S(1)} %add.83), channel_id=1, source_target_pairs={{0,2},{1,3},{2,0},{3,1},{4,6},{5,7},{6,4},{7,5},{8,10},{9,11},{10,... | collective-permute-start | bytes 442376 | tf_op jit(solution)/shard_map/ppermute | solution.py:411
  43.2 8.8 %collective-permute-start.15 = (f32[32,1152]{1,0:T(8,128)S(1)}, f32[32,1152]{1,0:T(8,128)S(1)}, u32[]{:S(2)}, u32[]{:S(2)}) collective-permute-start(f32[32,1152]{1,0:T(8,128)S(1)} %add.82), channel_id=1, source_target_pairs={{0,6},{1,7},{2,4},{3,5},{4,2},{5,3},{6,0},{7,1},{8,14},{9,15},{10,... | collective-permute-start | bytes 442376 | tf_op jit(solution)/shard_map/ppermute | solution.py:411
  52.1 7.5 %collective-permute-start.11 = (f32[32,1152]{1,0:T(8,128)S(1)}, f32[32,1152]{1,0:T(8,128)S(1)}, u32[]{:S(2)}, u32[]{:S(2)}) collective-permute-start(f32[32,1152]{1,0:T(8,128)S(1)} %add.82), channel_id=1, source_target_pairs={{0,4},{1,5},{2,6},{3,7},{4,0},{5,1},{6,2},{7,3},{8,12},{9,13},{10,... | collective-permute-start | bytes 442376 | tf_op jit(solution)/shard_map/ppermute | solution.py:411
  52.2 7.5 %collective-permute-start.10 = (f32[32,1152]{1,0:T(8,128)S(1)}, f32[32,1152]{1,0:T(8,128)S(1)}, u32[]{:S(2)}, u32[]{:S(2)}) collective-permute-start(f32[32,1152]{1,0:T(8,128)S(1)} %add.82), channel_id=1, source_target_pairs={{0,2},{1,3},{2,0},{3,1},{4,6},{5,7},{6,4},{7,5},{8,10},{9,11},{10,... | collective-permute-start | bytes 442376 | tf_op jit(solution)/shard_map/ppermute | solution.py:411
  67.7 4.1 %collective-permute-start.18 = (f32[128,1152]{1,0:T(8,128)S(1)}, f32[128,1152]{1,0:T(8,128)S(1)}, u32[]{:S(2)}, u32[]{:S(2)}) collective-permute-start(f32[128,1152]{1,0:T(8,128)S(1)} %get-tuple-element.256), channel_id=1, source_target_pairs={{0,1},{1,0},{2,3},{3,2},{4,5},{5,4},{6,7},{7,6},{8,9},{9,8},{10,11... | collective-permute-start | bytes 1769480 | tf_op jit(solution)/shard_map/ppermute | solution.py:411
  71.8 8.5 %collective-permute-start.19 = (f32[128,1152]{1,0:T(8,128)S(1)}, f32[128,1152]{1,0:T(8,128)S(1)}, u32[]{:S(2)}, u32[]{:S(2)}) collective-permute-start(f32[128,1152]{1,0:T(8,128)S(1)} %get-tuple-element.265), channel_id=1, source_target_pairs={{0,1},{1,0},{2,3},{3,2},{4,5},{5,4},{6,7},{7,6},{8,9},{9,8},{10,11... | collective-permute-start | bytes 1769480 | tf_op jit(solution)/shard_map/ppermute | solution.py:411
  72.4 11.4 %collective-permute-start.25 = (f32[32,1152]{1,0:T(8,128)S(1)}, f32[32,1152]{1,0:T(8,128)S(1)}, u32[]{:S(2)}, u32[]{:S(2)}) collective-permute-start(f32[32,1152]{1,0:T(8,128)S(1)} %get-tuple-element.323), channel_id=1, source_target_pairs={{0,6},{1,7},{2,4},{3,5},{4,2},{5,3},{6,0},{7,1},{8,14},{9,15},{10,... | collective-permute-start | bytes 442376 | tf_op jit(solution)/shard_map/ppermute | solution.py:411
  74.0 10.9 %collective-permute-start.24 = (f32[32,1152]{1,0:T(8,128)S(1)}, f32[32,1152]{1,0:T(8,128)S(1)}, u32[]{:S(2)}, u32[]{:S(2)}) collective-permute-start(f32[32,1152]{1,0:T(8,128)S(1)} %get-tuple-element.324), channel_id=1, source_target_pairs={{0,4},{1,5},{2,6},{3,7},{4,0},{5,1},{6,2},{7,3},{8,12},{9,13},{10,... | collective-permute-start | bytes 442376 | tf_op jit(solution)/shard_map/ppermute | solution.py:411
  75.0 9.9 %collective-permute-start.23 = (f32[32,1152]{1,0:T(8,128)S(1)}, f32[32,1152]{1,0:T(8,128)S(1)}, u32[]{:S(2)}, u32[]{:S(2)}) collective-permute-start(f32[32,1152]{1,0:T(8,128)S(1)} %get-tuple-element.325), channel_id=1, source_target_pairs={{0,2},{1,3},{2,0},{3,1},{4,6},{5,7},{6,4},{7,5},{8,10},{9,11},{10,... | collective-permute-start | bytes 442376 | tf_op jit(solution)/shard_map/ppermute | solution.py:411
  80.4 9.3 %collective-permute-start.22 = (f32[32,1152]{1,0:T(8,128)S(1)}, f32[32,1152]{1,0:T(8,128)S(1)}, u32[]{:S(2)}, u32[]{:S(2)}) collective-permute-start(f32[32,1152]{1,0:T(8,128)S(1)} %get-tuple-element.326), channel_id=1, source_target_pairs={{0,6},{1,7},{2,4},{3,5},{4,2},{5,3},{6,0},{7,1},{8,14},{9,15},{10,... | collective-permute-start | bytes 442376 | tf_op jit(solution)/shard_map/ppermute | solution.py:411
  82.1 10.2 %collective-permute-start.21 = (f32[32,1152]{1,0:T(8,128)S(1)}, f32[32,1152]{1,0:T(8,128)S(1)}, u32[]{:S(2)}, u32[]{:S(2)}) collective-permute-start(f32[32,1152]{1,0:T(8,128)S(1)} %get-tuple-element.327), channel_id=1, source_target_pairs={{0,4},{1,5},{2,6},{3,7},{4,0},{5,1},{6,2},{7,3},{8,12},{9,13},{10,... | collective-permute-start | bytes 442376 | tf_op jit(solution)/shard_map/ppermute | solution.py:411
  83.8 8.4 %collective-permute-start.20 = (f32[32,1152]{1,0:T(8,128)S(1)}, f32[32,1152]{1,0:T(8,128)S(1)}, u32[]{:S(2)}, u32[]{:S(2)}) collective-permute-start(f32[32,1152]{1,0:T(8,128)S(1)} %get-tuple-element.328), channel_id=1, source_target_pairs={{0,2},{1,3},{2,0},{3,1},{4,6},{5,7},{6,4},{7,5},{8,10},{9,11},{10,... | collective-permute-start | bytes 442376 | tf_op jit(solution)/shard_map/ppermute | solution.py:411
  84.9 13.1 %collective-permute-start.27 = (f32[32,1152]{1,0:T(8,128)S(1)}, f32[32,1152]{1,0:T(8,128)S(1)}, u32[]{:S(2)}, u32[]{:S(2)}) collective-permute-start(f32[32,1152]{1,0:T(8,128)S(1)} %fusion.1), channel_id=1, source_target_pairs={{0,8},{1,9},{2,10},{3,11},{4,12},{5,13},{6,14},{7,15},{8,0},{9,1},... | collective-permute-start | bytes 442376 | tf_op jit(solution)/shard_map/ppermute | solution.py:411
  92.3 9.3 %collective-permute-start.26 = (f32[32,1152]{1,0:T(8,128)S(1)}, f32[32,1152]{1,0:T(8,128)S(1)}, u32[]{:S(2)}, u32[]{:S(2)}) collective-permute-start(f32[32,1152]{1,0:T(8,128)S(1)} %fusion.3), channel_id=1, source_target_pairs={{0,8},{1,9},{2,10},{3,11},{4,12},{5,13},{6,14},{7,15},{8,0},{9,1},... | collective-permute-start | bytes 442376 | tf_op jit(solution)/shard_map/ppermute | solution.py:411
  98.0 7.8 %collective-permute-start.32 = (f32[32,1152]{1,0:T(8,128)S(1)}, f32[32,1152]{1,0:T(8,128)S(1)}, u32[]{:S(2)}, u32[]{:S(2)}) collective-permute-start(f32[32,1152]{1,0:T(8,128)S(1)} %add.93), channel_id=1, source_target_pairs={{0,6},{1,7},{2,4},{3,5},{4,2},{5,3},{6,0},{7,1},{8,14},{9,15},{10,... | collective-permute-start | bytes 442376 | tf_op jit(solution)/shard_map/ppermute | solution.py:411
  100.2 7.8 %collective-permute-start.31 = (f32[32,1152]{1,0:T(8,128)S(1)}, f32[32,1152]{1,0:T(8,128)S(1)}, u32[]{:S(2)}, u32[]{:S(2)}) collective-permute-start(f32[32,1152]{1,0:T(8,128)S(1)} %add.93), channel_id=1, source_target_pairs={{0,4},{1,5},{2,6},{3,7},{4,0},{5,1},{6,2},{7,3},{8,12},{9,13},{10,... | collective-permute-start | bytes 442376 | tf_op jit(solution)/shard_map/ppermute | solution.py:411
  100.2 7.8 %collective-permute-start.30 = (f32[32,1152]{1,0:T(8,128)S(1)}, f32[32,1152]{1,0:T(8,128)S(1)}, u32[]{:S(2)}, u32[]{:S(2)}) collective-permute-start(f32[32,1152]{1,0:T(8,128)S(1)} %add.93), channel_id=1, source_target_pairs={{0,2},{1,3},{2,0},{3,1},{4,6},{5,7},{6,4},{7,5},{8,10},{9,11},{10,... | collective-permute-start | bytes 442376 | tf_op jit(solution)/shard_map/ppermute | solution.py:411
  101.6 8.8 %collective-permute-start.33 = (f32[32,1152]{1,0:T(8,128)S(1)}, f32[32,1152]{1,0:T(8,128)S(1)}, u32[]{:S(2)}, u32[]{:S(2)}) collective-permute-start(f32[32,1152]{1,0:T(8,128)S(1)} %add.92), channel_id=1, source_target_pairs={{0,6},{1,7},{2,4},{3,5},{4,2},{5,3},{6,0},{7,1},{8,14},{9,15},{10,... | collective-permute-start | bytes 442376 | tf_op jit(solution)/shard_map/ppermute | solution.py:411
  110.5 6.3 %collective-permute-start.29 = (f32[32,1152]{1,0:T(8,128)S(1)}, f32[32,1152]{1,0:T(8,128)S(1)}, u32[]{:S(2)}, u32[]{:S(2)}) collective-permute-start(f32[32,1152]{1,0:T(8,128)S(1)} %add.92), channel_id=1, source_target_pairs={{0,4},{1,5},{2,6},{3,7},{4,0},{5,1},{6,2},{7,3},{8,12},{9,13},{10,... | collective-permute-start | bytes 442376 | tf_op jit(solution)/shard_map/ppermute | solution.py:411
  110.5 6.2 %collective-permute-start.28 = (f32[32,1152]{1,0:T(8,128)S(1)}, f32[32,1152]{1,0:T(8,128)S(1)}, u32[]{:S(2)}, u32[]{:S(2)}) collective-permute-start(f32[32,1152]{1,0:T(8,128)S(1)} %add.92), channel_id=1, source_target_pairs={{0,2},{1,3},{2,0},{3,1},{4,6},{5,7},{6,4},{7,5},{8,10},{9,11},{10,... | collective-permute-start | bytes 442376 | tf_op jit(solution)/shard_map/ppermute | solution.py:411
  (9 other events, 61.5 us)

commit v3 on v2

--- a/solution.py
+++ b/solution.py
@@ -81,15 +81,17 @@
     send_ref[...] = packed[half:]
 
 
+SLOTS = (range(8), (0, 3, 1, 2, 4, 7, 5, 6))
+
+
 def unpack(pieces, packed, hi, lo, me, shards, chunk):
     size = hi.shape[0]
     rows = packed.shape[0] // shards
-    slot = 0
+    slots = iter(SLOTS[chunk])
     for piece in pieces:
         for s in range(piece.shape[0] // rows):
-            at = pl.multiple_of((slot ^ me) * rows, rows)
+            at = pl.multiple_of((next(slots) ^ me) * rows, rows)
             packed[pl.ds(at, rows), :] = piece[s * rows:(s + 1) * rows, :]
-            slot += 1
     for line, i in enumerate(chunk_lines(size, chunk)):
         for at, p, q in line_blocks(size, i):
             block = packed[line * B:(line + 1) * B, at:at + B]
@@ -110,37 +112,36 @@
     shards, me_ref, a_hbm, b_hbm, keep_ref, send_ref, ah, al, bh, bl, a_buf, b_buf, sems, g, packed
 ):
     rows, size = a_buf.shape
+    q = size // 4
     steps = sems.shape[1]
     tile = rows // steps
-    copies = []
-    for s in range(steps):
-        r = slice(s * tile, (s + 1) * tile)
-        pair = [
-            pltpu.make_async_copy(src.at[r], dst.at[r], sems.at[k, s])
+
+    def copies(step):
+        r = slice(step * tile, (step + 1) * tile)
+        return [
+            pltpu.make_async_copy(src.at[r], dst.at[r], sems.at[k, step])
             for k, (src, dst) in enumerate([(a_hbm, a_buf), (b_hbm, b_buf)])
         ]
-        for copy in pair:
+
+    def start(step):
+        for copy in copies(step):
             copy.start()
-        copies.append((r, pair))
-    q = size // 4
-
-    def add_rows(r):
+
+    start(0)
+    start(1)
+    for step in range(steps):
+        r = slice(step * tile, (step + 1) * tile)
+        for copy in copies(step):
+            copy.wait()
+        if step + 2 < steps:
+            start(step + 2)
+        ah[:, r], al[:, r] = split(a_buf[r].T)
+        bh[r], bl[r] = split(b_buf[r])
         for r0, r1, c0, c1 in [(0, q, 0, size), (q, size, 0, q), (3 * q, size, 3 * q, size)]:
             product = mm((ah[r0:r1, r], al[r0:r1, r]), (bh[r, c0:c1], bl[r, c0:c1]))
-            if r.start:
+            if step:
                 product += g[r0:r1, c0:c1]
             g[r0:r1, c0:c1] = product
-
-    before = None
-    for r, pair in copies:
-        for copy in pair:
-            copy.wait()
-        if before:
-            add_rows(before)
-        ah[:, r], al[:, r] = split(a_buf[r].T)
-        bh[r], bl[r] = split(b_buf[r])
-        before = r
-    add_rows(before)
     pack(g, packed, keep_ref, send_ref, me_ref[0], shards, 0)
 
 
@@ -244,12 +245,8 @@
             at = end
 
 
-def sym_scratch(rows, size):
-    return (
-        [pltpu.VMEM((rows, size), BF16)] * 2
-        + [pltpu.VMEM((size, size), BF16)] * 2
-        + [packed_scratch(size)]
-    )
+def sym_scratch(size):
+    return [pltpu.VMEM((size, size), BF16)] * 2 + [packed_scratch(size)]
 
 
 def partial_kernel(shards, count, me_ref, *refs):
@@ -266,7 +263,7 @@
         struct(rows, size), 18, 0.5, 3,
         in_specs=[SMEM] + [VMEM] * (len(pieces) + 2 + len(base)),
         out_specs=VMEM,
-        scratch_shapes=sym_scratch(rows, size)[2:],
+        scratch_shapes=sym_scratch(size),
     )(me, *pieces, ah, al, *base)
 
 
@@ -281,45 +278,46 @@
     )(x)
 
 
-def cut_kernel(x_ref, hi, lo):
-    hi[...], lo[...] = split(x_ref[...])
-
-
-def cut(x):
-    part = struct(*x.shape, dtype=BF16)
-    return call(
-        cut_kernel, "cut", [part, part], 16, 0.1, 2, in_specs=[VMEM], out_specs=[VMEM] * 2
+def cut_kernel(which, x_ref, *out_refs):
+    parts = split(x_ref[...])
+    for out_ref, k in zip(out_refs, which):
+        out_ref[...] = parts[k]
+
+
+def cut(x, *which):
+    count = len(which)
+    return call(
+        functools.partial(cut_kernel, which), "cut", [struct(*x.shape, dtype=BF16)] * count,
+        16, 0.1, 2, in_specs=[VMEM], out_specs=[VMEM] * count,
     )(x)
 
 
 def early_kernel(shards, count, me_ref, *refs):
     pieces, refs = refs[:count], refs[count:]
-    a_ref, base_refs, refs = refs[0], refs[1:-9], refs[-9:]
-    xh, xl, out_ref, col_ref, ah, al, hi, lo, packed = refs
-    ah[...], al[...] = split(a_ref[...])
+    ah, al, base_refs, refs = refs[0], refs[1], refs[2:-7], refs[-7:]
+    xh, xl, out_ref, col_ref, hi, lo, packed = refs
     unpack(pieces, packed, hi, lo, me_ref[0], shards, 0)
     apply_first(base_refs, out_ref, ah, al, hi, lo)
     col_ref[...] = mm((xh[...], xl[...]), split(out_ref[:, :col_ref.shape[1]]))
 
 
-def early_middle(me, shards, pieces, a, base, xh, xl):
-    rows, size = a.shape
+def early_middle(me, shards, pieces, ah, al, base, xh, xl):
+    rows, size = ah.shape
     return call(
         functools.partial(early_kernel, shards, len(pieces)), "early_middle",
         [struct(rows, size), struct(size, size // 4)], 20, 0.75, 5,
-        in_specs=[SMEM] + [VMEM] * (len(pieces) + 3 + len(base)),
+        in_specs=[SMEM] + [VMEM] * (len(pieces) + 4 + len(base)),
         out_specs=[VMEM] * 2,
-        scratch_shapes=sym_scratch(rows, size),
-    )(me, *pieces, a, *base, xh, xl)
+        scratch_shapes=sym_scratch(size),
+    )(me, *pieces, ah, al, *base, xh, xl)
 
 
 def second_gram_kernel(shards, count, me_ref, *refs):
     pieces, refs = refs[:count], refs[count:]
-    a_ref, base_ref, xh, xl, col_ref, refs = refs[0], refs[1], refs[2], refs[3], refs[4], refs[5:]
-    keep_ref, send_ref, mid_ref, mh, ml, ah, al, hi, lo, packed, g = refs
+    (ah, al, base_ref, xh, xl, col_ref), refs = refs[:6], refs[6:]
+    keep_ref, send_ref, mid_ref, mh, ml, hi, lo, packed, g = refs
     size = g.shape[0]
     q = size // 4
-    ah[:, q:], al[:, q:] = split(a_ref[:, q:])
     unpack(pieces, packed, hi, lo, me_ref[0], shards, 1)
     mid_ref[:, :q] = base_ref[:, :q]
     for column in range(1, 4):
@@ -334,16 +332,16 @@
     pack(g, packed, keep_ref, send_ref, me_ref[0], shards, 0)
 
 
-def second_gram(me, shards, pieces, a, base, xh, xl, col):
-    rows, size = a.shape
+def second_gram(me, shards, pieces, ah, al, base, xh, xl, col):
+    rows, size = ah.shape
     part = struct(rows, size - size // 4, dtype=BF16)
     return call(
         functools.partial(second_gram_kernel, shards, len(pieces)), "second_gram",
         halves(size) + [struct(rows, size), part, part], 20, 0.8, 5,
-        in_specs=[SMEM] + [VMEM] * (len(pieces) + 5),
+        in_specs=[SMEM] + [VMEM] * (len(pieces) + 6),
         out_specs=[VMEM] * 5,
-        scratch_shapes=sym_scratch(rows, size) + [pltpu.VMEM((size, size), F32)],
-    )(me, *pieces, a, base, xh, xl, col)
+        scratch_shapes=sym_scratch(size) + [pltpu.VMEM((size, size), F32)],
+    )(me, *pieces, ah, al, base, xh, xl, col)
 
 
 def fourth_gram_kernel(shards, me_ref, xh, xl, mh, ml, keep_ref, send_ref, g, packed):
@@ -389,7 +387,7 @@
         functools.partial(last_kernel, shards, len(pieces)), "last", struct(rows, size), 22, 0.5, 3,
         in_specs=[SMEM] + [VMEM] * (len(pieces) + 3),
         out_specs=pl.BlockSpec(memory_space=pltpu.HBM),
-        scratch_shapes=sym_scratch(rows, size)[2:]
+        scratch_shapes=sym_scratch(size)
         + [pltpu.VMEM((rows, size), F32), pltpu.SemaphoreType.DMA((4,))],
     )(me, *pieces, ah, al, z)
 
@@ -464,21 +462,24 @@
 
     for offset in beyond:
         got_a = a.exchange(offset)
+        work()
         b.own(close(env, *got_b))
         got_b = [b.exchange(offset)]
-        work()
         a.own(close(env, got_a))
 
     got_a = a.gather_plane()
     b.own(close(env, *got_b))
 
-    got_b = b.gather_plane()
-    *got_a, got_b[2] = close(env, *got_a, got_b[2])
-    got_a = a.gather_core(got_a)
-    pieces_a = [a.mine, *close(env, got_a)]
-    late(env, pieces_a)
-    got_b = b.gather_core(close(env, *got_b))
-    return pieces_a, [b.mine, got_b]
+    side_b, near_b, diagonal_b = b.gather_plane()
+    got_a = a.gather_core(close(env, *got_a))
+    work()
+    got_a, diagonal_b = close(env, got_a, diagonal_b)
+    early_b = jnp.concatenate([b.keep, diagonal_b], axis=0)
+    core_b = b.swap(early_b, CORE)
+    late(env, [a.mine, got_a])
+    side_b, near_b, core_b = close(env, side_b, near_b, core_b)
+    late_b = jnp.concatenate([side_b, near_b], axis=0)
+    return [early_b, late_b, core_b, b.swap(late_b, CORE)]
 
 
 def body(count, orbitals_zero, orbitals_one, correlation_zero, correlation_one, cotangent):
@@ -495,31 +496,37 @@
     def turned(env):
         env["xh"], env["xl"] = turn(env["x0"])
 
-    def parted(env):
-        env["x0h"], env["x0l"] = cut(env["x0"])
+    def cut_one(env):
+        env["x1h"], env["x1l"] = cut(env["x1"], 0, 1)
+
+    def high(env):
+        (env["x0h"],) = cut(env["x0"], 0)
+
+    def low(env):
+        (env["x0l"],) = cut(env["x0"], 1)
 
     def early(env, pieces):
         env["mid"], env["col"] = early_middle(
-            me, SHARDS, pieces, env["x1"], [env["m0"], env["m1"]], env["xh"], env["xl"]
+            me, SHARDS, pieces, env["x1h"], env["x1l"], [env["m0"], env["m1"]], env["xh"], env["xl"]
         )
 
     keep, send, *parts = first_gram(me, SHARDS, env["x1"], env["c"])
-    _, one = sum_chunks(
+    one = sum_chunks(
         count, env, (keep, send), lambda env: other_gram(me, SHARDS, *parts),
-        [half("m", "c", "s1", 0), turned, half("m", "c", "s1", 1)], early,
+        [half("m", "c", "s1", 0), turned, half("m", "c", "s1", 1), cut_one], early,
     )
 
     keep, send, env["mid"], mh, ml = second_gram(
-        me, SHARDS, one, env["x1"], env["mid"], env["xh"], env["xl"], env["col"]
+        me, SHARDS, one, env["x1h"], env["x1l"], env["mid"], env["xh"], env["xl"], env["col"]
     )
 
     def late(env, pieces):
         env["z"] = partial_apply(me, SHARDS, pieces, env["x0h"], env["x0l"], [env["d0"], env["d1"]])
 
-    _, two = sum_chunks(
+    two = sum_chunks(
         count, env, (keep, send),
         lambda env: fourth_gram(me, SHARDS, env["xh"], env["xl"], mh, ml),
-        [half("d", "mid", "s0", 0), parted, half("d", "mid", "s0", 1)], late,
+        [half("d", "mid", "s0", 0), high, half("d", "mid", "s0", 1), low], late,
     )
     return last_step(me, SHARDS, two, env["x0h"], env["x0l"], env["z"])
 

time: 124 us -> 123 us (level)
  waiting for transfers between devices: 29.2 us -> 22 us
  starting transfers between devices: 38.5 us -> 44.9 us
    ppermute x36 -> x38, waiting for transfers between devices: 29.2 us -> 22 us  [swap(): return lax.ppermute(x, 'row', [(i, i ^ offset) for i in range(self.count)])]
    ppermute x36 -> x38, starting transfers between devices: 38.5 us -> 44.9 us  [swap(): return lax.ppermute(x, 'row', [(i, i ^ offset) for i in range(self.count)])]
  transfers between devices with their start and end apart: 36 -> 38, of which waited for: 14 -> 13; matrix products, arithmetic and copies ran while one was open for 0% -> 0% of each run, Pallas kernels for 29% -> 30%
where the time goes in v3:
time: 123 us
  Pallas kernels  54.9 us (45%)
  starting transfers between devices  44.9 us (37%)
  waiting for transfers between devices  22 us (18%)
    ppermute x38, starting transfers between devices, swap(): return lax.ppermute(x, 'row', [(i, i ^ offset) for i in range(self.count)])  44.9 us
    ppermute x38, waiting for transfers between devices, swap(): return lax.ppermute(x, 'row', [(i, i ^ offset) for i in range(self.count)])  22 us
    pallas_call x4, Pallas kernels, affine(): call(affine_kernel, 'affine', struct(height, size), 18, 1 / parts, 2, gri...  17.5 us
    pallas_call x1, Pallas kernels, first_gram(): call(functools.partial(first_gram_kernel, shards), 'first_gram', halves(s...  6.93 us
    pallas_call x1, Pallas kernels, second_gram(): call(functools.partial(second_gram_kernel, shards, len(pieces)), 'second_...  5.85 us
    pallas_call x1, Pallas kernels, early_middle(): call(functools.partial(early_kernel, shards, len(pieces)), 'early_middle'...  5.5 us
    pallas_call x1, Pallas kernels, last_step(): call(functools.partial(last_kernel, shards, len(pieces)), 'last', struct(...  5.2 us
    pallas_call x1, Pallas kernels, fourth_gram(): call(functools.partial(fourth_gram_kernel, shards), 'fourth_gram', halves...  3.88 us
  transfers between devices with their start and end apart: 38, of which 13 were waited for; matrix products, arithmetic and copies ran while one was open for 0% of the time, Pallas kernels for 30%

profile of v3, /device:TPU:0, one launch (start us, length us, event | category | flops | bytes accessed | tf_op | source)
XLA Modules:
  0.0 123.1 jit_solution(17865786058532005521)
XLA Ops:
  0.0 6.9 %first_gram.1 = (f32[128,1152]{1,0:T(8,128)S(1)}, f32[128,1152]{1,0:T(8,128)S(1)}, bf16[1024,1024]{1,0:T(8,128)(2,1)S(1)}, bf16[1024,1024]{1,0:T(8,128)(2,1)S(1)...) custom-call(s32[1]{0:T(128)} %bitcast.me_ref, f32[1024,1024]{1,0:T(8,128)} %x_ref.1, f32[1024,1024]{1,0:T(8,128)} %a_ref.1), custom_call_target="tpu_custom_call" | custom-call | flops 3221225472 | bytes 16777216 | tf_op jit(solution)/shard_map/first_gram/pallas_call | solution.py:151
  7.5 3.6 %other_gram.1 = (f32[128,1152]{1,0:T(8,128)S(1)}, f32[128,1152]{1,0:T(8,128)S(1)}) custom-call(s32[1]{0:T(128)} %bitcast.me_ref, bf16[1024,1024]{1,0:T(8,128)(2,1)S(1)} %get-tuple-element.165.ah, bf16[1024,1024]{1,0:T(8,128)(2,1)S(1)} %get-tuple-element.166.al, bf16[1024,1024]{1,0:T(8,128)(2,1)S(1)} %get-tuple-element.167.bh, ...), custom_call_target="tpu_custom_call" | custom-call | flops 3221225472 | bytes 8388608 | tf_op jit(solution)/shard_map/other_gram/pallas_call | solution.py:181
  11.3 4.0 %collective-permute-start.7 = (f32[32,1152]{1,0:T(8,128)S(1)}, f32[32,1152]{1,0:T(8,128)S(1)}, u32[]{:S(2)}, u32[]{:S(2)}) collective-permute-start(f32[32,1152]{1,0:T(8,128)S(1)} %get-tuple-element.332), channel_id=1, source_target_pairs={{0,6},{1,7},{2,4},{3,5},{4,2},{5,3},{6,0},{7,1},{8,14},{9,15},{10,... | collective-permute-start | bytes 442376 | tf_op jit(solution)/shard_map/ppermute | solution.py:409
  16.0 4.3 %affine.4.refs_4_ = f32[512,1024]{1,0:T(8,128)S(1)} custom-call(f32[1024,1024]{1,0:T(8,128)S(1)} %copy-done.2, f32[1024,1024]{1,0:T(8,128)S(1)} %copy-done.3), custom_call_target="tpu_custom_call" | custom-call | flops 3221225472 | bytes 8388608 | tf_op jit(solution)/shard_map/affine/pallas_call | solution.py:209
  20.5 2.9 %collective-permute-start.4 = (f32[32,1152]{1,0:T(8,128)S(1)}, f32[32,1152]{1,0:T(8,128)S(1)}, u32[]{:S(2)}, u32[]{:S(2)}) collective-permute-start(f32[32,1152]{1,0:T(8,128)S(1)} %get-tuple-element.329), channel_id=1, source_target_pairs={{0,6},{1,7},{2,4},{3,5},{4,2},{5,3},{6,0},{7,1},{8,14},{9,15},{10,... | collective-permute-start | bytes 442376 | tf_op jit(solution)/shard_map/ppermute | solution.py:409
  23.8 1.3 %turn.1 = (bf16[1024,1024]{1,0:T(8,128)(2,1)S(1)}, bf16[1024,1024]{1,0:T(8,128)(2,1)S(1)}) custom-call(f32[1024,1024]{1,0:T(8,128)S(1)} %copy-done), custom_call_target="tpu_custom_call" | custom-call | flops 644245120 | bytes 8388608 | tf_op jit(solution)/shard_map/turn/pallas_call | solution.py:276
  25.5 3.0 %collective-permute-start.9 = (f32[32,1152]{1,0:T(8,128)S(1)}, f32[32,1152]{1,0:T(8,128)S(1)}, u32[]{:S(2)}, u32[]{:S(2)}) collective-permute-start(f32[32,1152]{1,0:T(8,128)S(1)} %fusion.5), channel_id=1, source_target_pairs={{0,8},{1,9},{2,10},{3,11},{4,12},{5,13},{6,14},{7,15},{8,0},{9,1},... | collective-permute-start | bytes 442376 | tf_op jit(solution)/shard_map/ppermute | solution.py:409
  28.4 4.5 %affine.5.refs_5_ = f32[512,1024]{1,0:T(8,128)S(1)} custom-call(f32[1024,1024]{1,0:T(8,128)S(1)} %copy-done.2, f32[1024,1024]{1,0:T(8,128)S(1)} %copy-done.3), custom_call_target="tpu_custom_call" | custom-call | flops 3221225472 | bytes 8388608 | tf_op jit(solution)/shard_map/affine/pallas_call | solution.py:209
  34.2 5.5 %collective-permute-start.12 = (f32[32,1152]{1,0:T(8,128)S(1)}, f32[32,1152]{1,0:T(8,128)S(1)}, u32[]{:S(2)}, u32[]{:S(2)}) collective-permute-start(f32[32,1152]{1,0:T(8,128)S(1)} %add.83), channel_id=1, source_target_pairs={{0,6},{1,7},{2,4},{3,5},{4,2},{5,3},{6,0},{7,1},{8,14},{9,15},{10,... | collective-permute-start | bytes 442376 | tf_op jit(solution)/shard_map/ppermute | solution.py:409
  41.6 1.8 %collective-permute-done.12 = f32[32,1152]{1,0:T(8,128)S(1)} collective-permute-done((f32[32,1152]{1,0:T(8,128)S(1)}, f32[32,1152]{1,0:T(8,128)S(1)}, u32[]{:S(2)}, u32[]{:S(2)}) %collective-permute-start.12) | collective-permute-done | bytes 147488 | tf_op jit(solution)/shard_map/ppermute | solution.py:409
  43.4 1.4 %collective-permute-done.11 = f32[32,1152]{1,0:T(8,128)S(1)} collective-permute-done((f32[32,1152]{1,0:T(8,128)S(1)}, f32[32,1152]{1,0:T(8,128)S(1)}, u32[]{:S(2)}, u32[]{:S(2)}) %collective-permute-start.11) | collective-permute-done | bytes 147488 | tf_op jit(solution)/shard_map/ppermute | solution.py:409
  45.1 2.4 %collective-permute-start.14 = (f32[32,1152]{1,0:T(8,128)S(1)}, f32[32,1152]{1,0:T(8,128)S(1)}, u32[]{:S(2)}, u32[]{:S(2)}) collective-permute-start(f32[32,1152]{1,0:T(8,128)S(1)} %add.82), channel_id=1, source_target_pairs={{0,6},{1,7},{2,4},{3,5},{4,2},{5,3},{6,0},{7,1},{8,14},{9,15},{10,... | collective-permute-start | bytes 442376 | tf_op jit(solution)/shard_map/ppermute | solution.py:409
  49.4 3.3 %collective-permute-done.14 = f32[32,1152]{1,0:T(8,128)S(1)} collective-permute-done((f32[32,1152]{1,0:T(8,128)S(1)}, f32[32,1152]{1,0:T(8,128)S(1)}, u32[]{:S(2)}, u32[]{:S(2)}) %collective-permute-start.14) | collective-permute-done | bytes 147488 | tf_op jit(solution)/shard_map/ppermute | solution.py:409
  52.9 5.5 %early_middle.1 = (f32[1024,1024]{1,0:T(8,128)S(1)}, f32[1024,256]{1,0:T(8,128)S(1)}) custom-call(s32[1]{0:T(128)} %bitcast.me_ref, f32[128,1152]{1,0:T(8,128)S(1)} %pad_maximum_fusion.refs_0_, f32[128,1152]{1,0:T(8,128)S(1)} %collective-permute-done.13.refs_1_, bf16[1024,1024]{1,0:T(8,128)(2,1)S(1)} %get-tuple-element.253.refs_2_.refs_4_, ...), custom_call_target="tpu_custom_call" | custom-call | flops 4831838208 | bytes 20971520 | tf_op jit(solution)/shard_map/early_middle/pallas_call | solution.py:306
  59.0 1.2 collective-permute-done.18.refs_3_
  60.2 5.8 %second_gram.1 = (f32[128,1152]{1,0:T(8,128)S(1)}, f32[128,1152]{1,0:T(8,128)S(1)}, f32[1024,1024]{1,0:T(8,128)S(1)}, bf16[1024,768]{1,0:T(8,128)(2,1)S(1)}, bf16[1024,768]{1,0:T(8,128)(2,1)S(1)}) custom-call(s32[1]{0:T(128)} %bitcast.me_ref, f32[64,1152]{1,0:T(8,128)S(1)} %pad_maximum_fusion.2.refs_0_, ...), custom_call_target="tpu_custom_call" | custom-call | flops 5153960960 | bytes 20971520 | tf_op jit(solution)/shard_map/second_gram/pallas_call | solution.py:338
  66.5 3.9 %fourth_gram.1 = (f32[128,1152]{1,0:T(8,128)S(1)}, f32[128,1152]{1,0:T(8,128)S(1)}) custom-call(s32[1]{0:T(128)} %bitcast.me_ref, bf16[1024,1024]{1,0:T(8,128)(2,1)S(1)} %get-tuple-element.256.refs_6_.refs_7_.xh, bf16[1024,1024]{1,0:T(8,128)(2,1)S(1)} %get-tuple-element.257.refs_7_.refs_8_.xl, bf16[1024,768]{1,0:T(8,128)(2,1)S(1)} %get-tuple-element.260.mh, ...), custom_call_target="tpu_custom_call" | custom-call | flops 3221225472 | bytes 8388608 | tf_op jit(solution)/shard_map/fourth_gram/pallas_call | solution.py:354
  70.7 2.5 %collective-permute-start.26 = (f32[32,1152]{1,0:T(8,128)S(1)}, f32[32,1152]{1,0:T(8,128)S(1)}, u32[]{:S(2)}, u32[]{:S(2)}) collective-permute-start(f32[32,1152]{1,0:T(8,128)S(1)} %get-tuple-element.326), channel_id=1, source_target_pairs={{0,6},{1,7},{2,4},{3,5},{4,2},{5,3},{6,0},{7,1},{8,14},{9,15},{10,... | collective-permute-start | bytes 442376 | tf_op jit(solution)/shard_map/ppermute | solution.py:409
  74.3 4.4 %affine.6.refs_4_ = f32[512,1024]{1,0:T(8,128)S(1)} custom-call(f32[1024,1024]{1,0:T(8,128)S(1)} %get-tuple-element.281.a_ref, f32[1024,1024]{1,0:T(8,128)S(1)} %copy-done.4), custom_call_target="tpu_custom_call" | custom-call | flops 3221225472 | bytes 8388608 | tf_op jit(solution)/shard_map/affine/pallas_call | solution.py:209
  78.8 2.4 %collective-permute-start.23 = (f32[32,1152]{1,0:T(8,128)S(1)}, f32[32,1152]{1,0:T(8,128)S(1)}, u32[]{:S(2)}, u32[]{:S(2)}) collective-permute-start(f32[32,1152]{1,0:T(8,128)S(1)} %get-tuple-element.323), channel_id=1, source_target_pairs={{0,6},{1,7},{2,4},{3,5},{4,2},{5,3},{6,0},{7,1},{8,14},{9,15},{10,... | collective-permute-start | bytes 442376 | tf_op jit(solution)/shard_map/ppermute | solution.py:409
  82.7 3.8 %collective-permute-start.28 = (f32[32,1152]{1,0:T(8,128)S(1)}, f32[32,1152]{1,0:T(8,128)S(1)}, u32[]{:S(2)}, u32[]{:S(2)}) collective-permute-start(f32[32,1152]{1,0:T(8,128)S(1)} %fusion.1), channel_id=1, source_target_pairs={{0,8},{1,9},{2,10},{3,11},{4,12},{5,13},{6,14},{7,15},{8,0},{9,1},... | collective-permute-start | bytes 442376 | tf_op jit(solution)/shard_map/ppermute | solution.py:409
  86.5 4.4 %affine.7.refs_5_ = f32[512,1024]{1,0:T(8,128)S(1)} custom-call(f32[1024,1024]{1,0:T(8,128)S(1)} %get-tuple-element.281.a_ref, f32[1024,1024]{1,0:T(8,128)S(1)} %copy-done.4), custom_call_target="tpu_custom_call" | custom-call | flops 3221225472 | bytes 8388608 | tf_op jit(solution)/shard_map/affine/pallas_call | solution.py:209
  91.1 2.0 %collective-permute-start.27 = (f32[32,1152]{1,0:T(8,128)S(1)}, f32[32,1152]{1,0:T(8,128)S(1)}, u32[]{:S(2)}, u32[]{:S(2)}) collective-permute-start(f32[32,1152]{1,0:T(8,128)S(1)} %fusion.3), channel_id=1, source_target_pairs={{0,8},{1,9},{2,10},{3,11},{4,12},{5,13},{6,14},{7,15},{8,0},{9,1},... | collective-permute-start | bytes 442376 | tf_op jit(solution)/shard_map/ppermute | solution.py:409
  93.2 2.5 %collective-permute-start.31 = (f32[32,1152]{1,0:T(8,128)S(1)}, f32[32,1152]{1,0:T(8,128)S(1)}, u32[]{:S(2)}, u32[]{:S(2)}) collective-permute-start(f32[32,1152]{1,0:T(8,128)S(1)} %add.93), channel_id=1, source_target_pairs={{0,6},{1,7},{2,4},{3,5},{4,2},{5,3},{6,0},{7,1},{8,14},{9,15},{10,... | collective-permute-start | bytes 442376 | tf_op jit(solution)/shard_map/ppermute | solution.py:409
  96.8 4.0 %collective-permute-done.27 = f32[32,1152]{1,0:T(8,128)S(1)} collective-permute-done((f32[32,1152]{1,0:T(8,128)S(1)}, f32[32,1152]{1,0:T(8,128)S(1)}, u32[]{:S(2)}, u32[]{:S(2)}) %collective-permute-start.27) | collective-permute-done | bytes 147488 | tf_op jit(solution)/shard_map/ppermute | solution.py:409
  100.7 2.2 %collective-permute-done.31 = f32[32,1152]{1,0:T(8,128)S(1)} collective-permute-done((f32[32,1152]{1,0:T(8,128)S(1)}, f32[32,1152]{1,0:T(8,128)S(1)}, u32[]{:S(2)}, u32[]{:S(2)}) %collective-permute-start.31) | collective-permute-done | bytes 147488 | tf_op jit(solution)/shard_map/ppermute | solution.py:409
  102.9 1.3 %collective-permute-done.30 = f32[32,1152]{1,0:T(8,128)S(1)} collective-permute-done((f32[32,1152]{1,0:T(8,128)S(1)}, f32[32,1152]{1,0:T(8,128)S(1)}, u32[]{:S(2)}, u32[]{:S(2)}) %collective-permute-start.30) | collective-permute-done | bytes 147488 | tf_op jit(solution)/shard_map/ppermute | solution.py:409
  105.2 1.7 %collective-permute-start.35 = (f32[32,1152]{1,0:T(8,128)S(1)}, f32[32,1152]{1,0:T(8,128)S(1)}, u32[]{:S(2)}, u32[]{:S(2)}) collective-permute-start(f32[32,1152]{1,0:T(8,128)S(1)} %add.92), channel_id=1, source_target_pairs={{0,4},{1,5},{2,6},{3,7},{4,0},{5,1},{6,2},{7,3},{8,12},{9,13},{10,... | collective-permute-start | bytes 442376 | tf_op jit(solution)/shard_map/ppermute | solution.py:409
  108.3 3.7 %collective-permute-done.33 = f32[32,1152]{1,0:T(8,128)S(1)} collective-permute-done((f32[32,1152]{1,0:T(8,128)S(1)}, f32[32,1152]{1,0:T(8,128)S(1)}, u32[]{:S(2)}, u32[]{:S(2)}) %collective-permute-start.33) | collective-permute-done | bytes 147488 | tf_op jit(solution)/shard_map/ppermute | solution.py:409
  112.1 3.8 %partial_apply.1.refs_6_ = f32[1024,1024]{1,0:T(8,128)S(1)} custom-call(s32[1]{0:T(128)} %bitcast.me_ref, f32[128,1152]{1,0:T(8,128)S(1)} %pad_maximum_fusion.1.refs_0_, f32[128,1152]{1,0:T(8,128)S(1)} %collective-permute-done.32.refs_1_, bf16[1024,1024]{1,0:T(8,128)(2,1)S(1)} %cut.4.refs_2_.refs_4_, bf16[1024,1024]{1,0:T(8,128)(2,1)S(1)} %cut.5.refs_3_.refs_5_, ...), custom_call_target="tpu_custom_call" | custom-call | flops 3221225472 | bytes 12582912 | tf_op jit(solution)/shard_map/partial_apply/pallas_call | solution.py:261
  116.5 1.2 collective-permute-done.37.refs_3_
  117.7 5.2 %last.1 = f32[1024,1024]{1,0:T(8,128)} custom-call(s32[1]{0:T(128)} %bitcast.me_ref, f32[64,1152]{1,0:T(8,128)S(1)} %pad_maximum_fusion.3.refs_0_, f32[64,1152]{1,0:T(8,128)S(1)} %constant_dynamic-update-slice_fusion.2.refs_1_, f32[64,1152]{1,0:T(8,128)S(1)} %collective-permute-done.36.refs_2_, f32[64,1152]{1,0:T(8,128)S(1)} %collective-permute-done.37.refs_3_, ...), custom_call_target="tpu_custom_call" | custom-call | flops 3221225472 | bytes 12582912 | tf_op jit(solution)/shard_map/last/pallas_call | solution.py:386
  (93 shorter events, 16.0 us)
Async XLA Ops:
  11.1 9.2 %collective-permute-start.1 = (f32[128,1152]{1,0:T(8,128)S(1)}, f32[128,1152]{1,0:T(8,128)S(1)}, u32[]{:S(2)}, u32[]{:S(2)}) collective-permute-start(f32[128,1152]{1,0:T(8,128)S(1)} %get-tuple-element.172), channel_id=1, source_target_pairs={{0,1},{1,0},{2,3},{3,2},{4,5},{5,4},{6,7},{7,6},{8,9},{9,8},{10,11... | collective-permute-start | bytes 1769480 | tf_op jit(solution)/shard_map/ppermute | solution.py:409
  11.3 13.8 %collective-permute-start.7 = (f32[32,1152]{1,0:T(8,128)S(1)}, f32[32,1152]{1,0:T(8,128)S(1)}, u32[]{:S(2)}, u32[]{:S(2)}) collective-permute-start(f32[32,1152]{1,0:T(8,128)S(1)} %get-tuple-element.332), channel_id=1, source_target_pairs={{0,6},{1,7},{2,4},{3,5},{4,2},{5,3},{6,0},{7,1},{8,14},{9,15},{10,... | collective-permute-start | bytes 442376 | tf_op jit(solution)/shard_map/ppermute | solution.py:409
  15.4 10.0 %collective-permute-start.6 = (f32[32,1152]{1,0:T(8,128)S(1)}, f32[32,1152]{1,0:T(8,128)S(1)}, u32[]{:S(2)}, u32[]{:S(2)}) collective-permute-start(f32[32,1152]{1,0:T(8,128)S(1)} %get-tuple-element.333), channel_id=1, source_target_pairs={{0,4},{1,5},{2,6},{3,7},{4,0},{5,1},{6,2},{7,3},{8,12},{9,13},{10,... | collective-permute-start | bytes 442376 | tf_op jit(solution)/shard_map/ppermute | solution.py:409
  15.8 9.6 %collective-permute-start.5 = (f32[32,1152]{1,0:T(8,128)S(1)}, f32[32,1152]{1,0:T(8,128)S(1)}, u32[]{:S(2)}, u32[]{:S(2)}) collective-permute-start(f32[32,1152]{1,0:T(8,128)S(1)} %get-tuple-element.334), channel_id=1, source_target_pairs={{0,2},{1,3},{2,0},{3,1},{4,6},{5,7},{6,4},{7,5},{8,10},{9,11},{10,... | collective-permute-start | bytes 442376 | tf_op jit(solution)/shard_map/ppermute | solution.py:409
  20.5 12.5 %collective-permute-start.4 = (f32[32,1152]{1,0:T(8,128)S(1)}, f32[32,1152]{1,0:T(8,128)S(1)}, u32[]{:S(2)}, u32[]{:S(2)}) collective-permute-start(f32[32,1152]{1,0:T(8,128)S(1)} %get-tuple-element.329), channel_id=1, source_target_pairs={{0,6},{1,7},{2,4},{3,5},{4,2},{5,3},{6,0},{7,1},{8,14},{9,15},{10,... | collective-permute-start | bytes 442376 | tf_op jit(solution)/shard_map/ppermute | solution.py:409
  23.4 9.7 %collective-permute-start.3 = (f32[32,1152]{1,0:T(8,128)S(1)}, f32[32,1152]{1,0:T(8,128)S(1)}, u32[]{:S(2)}, u32[]{:S(2)}) collective-permute-start(f32[32,1152]{1,0:T(8,128)S(1)} %get-tuple-element.330), channel_id=1, source_target_pairs={{0,4},{1,5},{2,6},{3,7},{4,0},{5,1},{6,2},{7,3},{8,12},{9,13},{10,... | collective-permute-start | bytes 442376 | tf_op jit(solution)/shard_map/ppermute | solution.py:409
  25.2 7.9 %collective-permute-start.2 = (f32[32,1152]{1,0:T(8,128)S(1)}, f32[32,1152]{1,0:T(8,128)S(1)}, u32[]{:S(2)}, u32[]{:S(2)}) collective-permute-start(f32[32,1152]{1,0:T(8,128)S(1)} %get-tuple-element.331), channel_id=1, source_target_pairs={{0,2},{1,3},{2,0},{3,1},{4,6},{5,7},{6,4},{7,5},{8,10},{9,11},{10,... | collective-permute-start | bytes 442376 | tf_op jit(solution)/shard_map/ppermute | solution.py:409
  25.5 8.7 %collective-permute-start.9 = (f32[32,1152]{1,0:T(8,128)S(1)}, f32[32,1152]{1,0:T(8,128)S(1)}, u32[]{:S(2)}, u32[]{:S(2)}) collective-permute-start(f32[32,1152]{1,0:T(8,128)S(1)} %fusion.5), channel_id=1, source_target_pairs={{0,8},{1,9},{2,10},{3,11},{4,12},{5,13},{6,14},{7,15},{8,0},{9,1},... | collective-permute-start | bytes 442376 | tf_op jit(solution)/shard_map/ppermute | solution.py:409
  33.1 8.4 %collective-permute-start.8 = (f32[32,1152]{1,0:T(8,128)S(1)}, f32[32,1152]{1,0:T(8,128)S(1)}, u32[]{:S(2)}, u32[]{:S(2)}) collective-permute-start(f32[32,1152]{1,0:T(8,128)S(1)} %fusion.7), channel_id=1, source_target_pairs={{0,8},{1,9},{2,10},{3,11},{4,12},{5,13},{6,14},{7,15},{8,0},{9,1},... | collective-permute-start | bytes 442376 | tf_op jit(solution)/shard_map/ppermute | solution.py:409
  34.2 9.2 %collective-permute-start.12 = (f32[32,1152]{1,0:T(8,128)S(1)}, f32[32,1152]{1,0:T(8,128)S(1)}, u32[]{:S(2)}, u32[]{:S(2)}) collective-permute-start(f32[32,1152]{1,0:T(8,128)S(1)} %add.83), channel_id=1, source_target_pairs={{0,6},{1,7},{2,4},{3,5},{4,2},{5,3},{6,0},{7,1},{8,14},{9,15},{10,... | collective-permute-start | bytes 442376 | tf_op jit(solution)/shard_map/ppermute | solution.py:409
  39.7 5.3 %collective-permute-start.10 = (f32[32,1152]{1,0:T(8,128)S(1)}, f32[32,1152]{1,0:T(8,128)S(1)}, u32[]{:S(2)}, u32[]{:S(2)}) collective-permute-start(f32[32,1152]{1,0:T(8,128)S(1)} %add.83), channel_id=1, source_target_pairs={{0,2},{1,3},{2,0},{3,1},{4,6},{5,7},{6,4},{7,5},{8,10},{9,11},{10,... | collective-permute-start | bytes 442376 | tf_op jit(solution)/shard_map/ppermute | solution.py:409
  45.0 7.7 %collective-permute-start.13 = (f32[128,1152]{1,0:T(8,128)S(1)}, f32[128,1152]{1,0:T(8,128)S(1)}, u32[]{:S(2)}, u32[]{:S(2)}) collective-permute-start(f32[128,1152]{1,0:T(8,128)S(1)} %pad_maximum_fusion.refs_0_), channel_id=1, source_target_pairs={{0,1},{1,0},{2,3},{3,2},{4,5},{5,4},{6,7},{7,6},{8,9},{9,8},{10,11... | collective-permute-start | bytes 1769480 | tf_op jit(solution)/shard_map/ppermute | solution.py:409
  45.1 7.6 %collective-permute-start.14 = (f32[32,1152]{1,0:T(8,128)S(1)}, f32[32,1152]{1,0:T(8,128)S(1)}, u32[]{:S(2)}, u32[]{:S(2)}) collective-permute-start(f32[32,1152]{1,0:T(8,128)S(1)} %add.82), channel_id=1, source_target_pairs={{0,6},{1,7},{2,4},{3,5},{4,2},{5,3},{6,0},{7,1},{8,14},{9,15},{10,... | collective-permute-start | bytes 442376 | tf_op jit(solution)/shard_map/ppermute | solution.py:409
  47.6 10.8 %collective-permute-start.16 = (f32[32,1152]{1,0:T(8,128)S(1)}, f32[32,1152]{1,0:T(8,128)S(1)}, u32[]{:S(2)}, u32[]{:S(2)}) collective-permute-start(f32[32,1152]{1,0:T(8,128)S(1)} %add.82), channel_id=1, source_target_pairs={{0,4},{1,5},{2,6},{3,7},{4,0},{5,1},{6,2},{7,3},{8,12},{9,13},{10,... | collective-permute-start | bytes 442376 | tf_op jit(solution)/shard_map/ppermute | solution.py:409
  47.7 10.7 %collective-permute-start.15 = (f32[32,1152]{1,0:T(8,128)S(1)}, f32[32,1152]{1,0:T(8,128)S(1)}, u32[]{:S(2)}, u32[]{:S(2)}) collective-permute-start(f32[32,1152]{1,0:T(8,128)S(1)} %add.82), channel_id=1, source_target_pairs={{0,2},{1,3},{2,0},{3,1},{4,6},{5,7},{6,4},{7,5},{8,10},{9,11},{10,... | collective-permute-start | bytes 442376 | tf_op jit(solution)/shard_map/ppermute | solution.py:409
  52.8 5.6 %collective-permute-start.17 = (f32[64,1152]{1,0:T(8,128)S(1)}, f32[64,1152]{1,0:T(8,128)S(1)}, u32[]{:S(2)}, u32[]{:S(2)}) collective-permute-start(f32[64,1152]{1,0:T(8,128)S(1)} %pad_maximum_fusion.2.refs_0_), channel_id=1, source_target_pairs={{0,1},{1,0},{2,3},{3,2},{4,5},{5,4},{6,7},{7,6},{8,9},{9,8},{10,11... | collective-permute-start | bytes 884744 | tf_op jit(solution)/shard_map/ppermute | solution.py:409
  70.4 8.3 %collective-permute-start.20 = (f32[128,1152]{1,0:T(8,128)S(1)}, f32[128,1152]{1,0:T(8,128)S(1)}, u32[]{:S(2)}, u32[]{:S(2)}) collective-permute-start(f32[128,1152]{1,0:T(8,128)S(1)} %get-tuple-element.268), channel_id=1, source_target_pairs={{0,1},{1,0},{2,3},{3,2},{4,5},{5,4},{6,7},{7,6},{8,9},{9,8},{10,11... | collective-permute-start | bytes 1769480 | tf_op jit(solution)/shard_map/ppermute | solution.py:409
  70.7 10.8 %collective-permute-start.26 = (f32[32,1152]{1,0:T(8,128)S(1)}, f32[32,1152]{1,0:T(8,128)S(1)}, u32[]{:S(2)}, u32[]{:S(2)}) collective-permute-start(f32[32,1152]{1,0:T(8,128)S(1)} %get-tuple-element.326), channel_id=1, source_target_pairs={{0,6},{1,7},{2,4},{3,5},{4,2},{5,3},{6,0},{7,1},{8,14},{9,15},{10,... | collective-permute-start | bytes 442376 | tf_op jit(solution)/shard_map/ppermute | solution.py:409
  73.2 9.5 %collective-permute-start.25 = (f32[32,1152]{1,0:T(8,128)S(1)}, f32[32,1152]{1,0:T(8,128)S(1)}, u32[]{:S(2)}, u32[]{:S(2)}) collective-permute-start(f32[32,1152]{1,0:T(8,128)S(1)} %get-tuple-element.327), channel_id=1, source_target_pairs={{0,4},{1,5},{2,6},{3,7},{4,0},{5,1},{6,2},{7,3},{8,12},{9,13},{10,... | collective-permute-start | bytes 442376 | tf_op jit(solution)/shard_map/ppermute | solution.py:409
  73.2 9.4 %collective-permute-start.24 = (f32[32,1152]{1,0:T(8,128)S(1)}, f32[32,1152]{1,0:T(8,128)S(1)}, u32[]{:S(2)}, u32[]{:S(2)}) collective-permute-start(f32[32,1152]{1,0:T(8,128)S(1)} %get-tuple-element.328), channel_id=1, source_target_pairs={{0,2},{1,3},{2,0},{3,1},{4,6},{5,7},{6,4},{7,5},{8,10},{9,11},{10,... | collective-permute-start | bytes 442376 | tf_op jit(solution)/shard_map/ppermute | solution.py:409
  78.8 12.0 %collective-permute-start.23 = (f32[32,1152]{1,0:T(8,128)S(1)}, f32[32,1152]{1,0:T(8,128)S(1)}, u32[]{:S(2)}, u32[]{:S(2)}) collective-permute-start(f32[32,1152]{1,0:T(8,128)S(1)} %get-tuple-element.323), channel_id=1, source_target_pairs={{0,6},{1,7},{2,4},{3,5},{4,2},{5,3},{6,0},{7,1},{8,14},{9,15},{10,... | collective-permute-start | bytes 442376 | tf_op jit(solution)/shard_map/ppermute | solution.py:409
  81.2 9.8 %collective-permute-start.22 = (f32[32,1152]{1,0:T(8,128)S(1)}, f32[32,1152]{1,0:T(8,128)S(1)}, u32[]{:S(2)}, u32[]{:S(2)}) collective-permute-start(f32[32,1152]{1,0:T(8,128)S(1)} %get-tuple-element.324), channel_id=1, source_target_pairs={{0,4},{1,5},{2,6},{3,7},{4,0},{5,1},{6,2},{7,3},{8,12},{9,13},{10,... | collective-permute-start | bytes 442376 | tf_op jit(solution)/shard_map/ppermute | solution.py:409
  81.5 9.6 %collective-permute-start.21 = (f32[32,1152]{1,0:T(8,128)S(1)}, f32[32,1152]{1,0:T(8,128)S(1)}, u32[]{:S(2)}, u32[]{:S(2)}) collective-permute-start(f32[32,1152]{1,0:T(8,128)S(1)} %get-tuple-element.325), channel_id=1, source_target_pairs={{0,2},{1,3},{2,0},{3,1},{4,6},{5,7},{6,4},{7,5},{8,10},{9,11},{10,... | collective-permute-start | bytes 442376 | tf_op jit(solution)/shard_map/ppermute | solution.py:409
  82.7 10.5 %collective-permute-start.28 = (f32[32,1152]{1,0:T(8,128)S(1)}, f32[32,1152]{1,0:T(8,128)S(1)}, u32[]{:S(2)}, u32[]{:S(2)}) collective-permute-start(f32[32,1152]{1,0:T(8,128)S(1)} %fusion.1), channel_id=1, source_target_pairs={{0,8},{1,9},{2,10},{3,11},{4,12},{5,13},{6,14},{7,15},{8,0},{9,1},... | collective-permute-start | bytes 442376 | tf_op jit(solution)/shard_map/ppermute | solution.py:409
  91.1 9.6 %collective-permute-start.27 = (f32[32,1152]{1,0:T(8,128)S(1)}, f32[32,1152]{1,0:T(8,128)S(1)}, u32[]{:S(2)}, u32[]{:S(2)}) collective-permute-start(f32[32,1152]{1,0:T(8,128)S(1)} %fusion.3), channel_id=1, source_target_pairs={{0,8},{1,9},{2,10},{3,11},{4,12},{5,13},{6,14},{7,15},{8,0},{9,1},... | collective-permute-start | bytes 442376 | tf_op jit(solution)/shard_map/ppermute | solution.py:409
  93.2 9.7 %collective-permute-start.31 = (f32[32,1152]{1,0:T(8,128)S(1)}, f32[32,1152]{1,0:T(8,128)S(1)}, u32[]{:S(2)}, u32[]{:S(2)}) collective-permute-start(f32[32,1152]{1,0:T(8,128)S(1)} %add.93), channel_id=1, source_target_pairs={{0,6},{1,7},{2,4},{3,5},{4,2},{5,3},{6,0},{7,1},{8,14},{9,15},{10,... | collective-permute-start | bytes 442376 | tf_op jit(solution)/shard_map/ppermute | solution.py:409
  95.6 8.6 %collective-permute-start.30 = (f32[32,1152]{1,0:T(8,128)S(1)}, f32[32,1152]{1,0:T(8,128)S(1)}, u32[]{:S(2)}, u32[]{:S(2)}) collective-permute-start(f32[32,1152]{1,0:T(8,128)S(1)} %add.93), channel_id=1, source_target_pairs={{0,4},{1,5},{2,6},{3,7},{4,0},{5,1},{6,2},{7,3},{8,12},{9,13},{10,... | collective-permute-start | bytes 442376 | tf_op jit(solution)/shard_map/ppermute | solution.py:409
  95.6 8.6 %collective-permute-start.29 = (f32[32,1152]{1,0:T(8,128)S(1)}, f32[32,1152]{1,0:T(8,128)S(1)}, u32[]{:S(2)}, u32[]{:S(2)}) collective-permute-start(f32[32,1152]{1,0:T(8,128)S(1)} %add.93), channel_id=1, source_target_pairs={{0,2},{1,3},{2,0},{3,1},{4,6},{5,7},{6,4},{7,5},{8,10},{9,11},{10,... | collective-permute-start | bytes 442376 | tf_op jit(solution)/shard_map/ppermute | solution.py:409
  104.3 7.8 %collective-permute-start.32 = (f32[128,1152]{1,0:T(8,128)S(1)}, f32[128,1152]{1,0:T(8,128)S(1)}, u32[]{:S(2)}, u32[]{:S(2)}) collective-permute-start(f32[128,1152]{1,0:T(8,128)S(1)} %pad_maximum_fusion.1.refs_0_), channel_id=1, source_target_pairs={{0,1},{1,0},{2,3},{3,2},{4,5},{5,4},{6,7},{7,6},{8,9},{9,8},{10,11... | collective-permute-start | bytes 1769480 | tf_op jit(solution)/shard_map/ppermute | solution.py:409
  104.4 7.6 %collective-permute-start.33 = (f32[32,1152]{1,0:T(8,128)S(1)}, f32[32,1152]{1,0:T(8,128)S(1)}, u32[]{:S(2)}, u32[]{:S(2)}) collective-permute-start(f32[32,1152]{1,0:T(8,128)S(1)} %add.92), channel_id=1, source_target_pairs={{0,6},{1,7},{2,4},{3,5},{4,2},{5,3},{6,0},{7,1},{8,14},{9,15},{10,... | collective-permute-start | bytes 442376 | tf_op jit(solution)/shard_map/ppermute | solution.py:409
  105.2 10.7 %collective-permute-start.35 = (f32[32,1152]{1,0:T(8,128)S(1)}, f32[32,1152]{1,0:T(8,128)S(1)}, u32[]{:S(2)}, u32[]{:S(2)}) collective-permute-start(f32[32,1152]{1,0:T(8,128)S(1)} %add.92), channel_id=1, source_target_pairs={{0,4},{1,5},{2,6},{3,7},{4,0},{5,1},{6,2},{7,3},{8,12},{9,13},{10,... | collective-permute-start | bytes 442376 | tf_op jit(solution)/shard_map/ppermute | solution.py:409
  106.8 9.1 %collective-permute-start.34 = (f32[32,1152]{1,0:T(8,128)S(1)}, f32[32,1152]{1,0:T(8,128)S(1)}, u32[]{:S(2)}, u32[]{:S(2)}) collective-permute-start(f32[32,1152]{1,0:T(8,128)S(1)} %add.92), channel_id=1, source_target_pairs={{0,2},{1,3},{2,0},{3,1},{4,6},{5,7},{6,4},{7,5},{8,10},{9,11},{10,... | collective-permute-start | bytes 442376 | tf_op jit(solution)/shard_map/ppermute | solution.py:409
  (11 other events, 74.0 us)

commit v4 on v3

--- a/solution.py
+++ b/solution.py
@@ -10,6 +10,7 @@
 BF16 = jnp.bfloat16
 B = 128
 MIB = 1024 * 1024
+WEIGHT = 10
 
 
 def split(x):
@@ -34,8 +35,8 @@
         out_shape=out_shape,
         compiler_params=pltpu.CompilerParams(vmem_limit_bytes=limit * MIB),
         cost_estimate=pl.CostEstimate(
-            flops=int(6 * products * size ** 3),
-            bytes_accessed=int(4 * arrays * size * size),
+            flops=int(WEIGHT * 6 * products * size ** 3),
+            bytes_accessed=int(WEIGHT * 4 * arrays * size * size),
             transcendentals=0,
         ),
         **kw,
@@ -81,13 +82,10 @@
     send_ref[...] = packed[half:]
 
 
-SLOTS = (range(8), (0, 3, 1, 2, 4, 7, 5, 6))
-
-
 def unpack(pieces, packed, hi, lo, me, shards, chunk):
     size = hi.shape[0]
     rows = packed.shape[0] // shards
-    slots = iter(SLOTS[chunk])
+    slots = iter(range(shards))
     for piece in pieces:
         for s in range(piece.shape[0] // rows):
             at = pl.multiple_of((next(slots) ^ me) * rows, rows)
@@ -470,16 +468,13 @@
     got_a = a.gather_plane()
     b.own(close(env, *got_b))
 
-    side_b, near_b, diagonal_b = b.gather_plane()
+    got_b = b.gather_plane()
     got_a = a.gather_core(close(env, *got_a))
     work()
-    got_a, diagonal_b = close(env, got_a, diagonal_b)
-    early_b = jnp.concatenate([b.keep, diagonal_b], axis=0)
-    core_b = b.swap(early_b, CORE)
+    (got_a,) = close(env, got_a)
     late(env, [a.mine, got_a])
-    side_b, near_b, core_b = close(env, side_b, near_b, core_b)
-    late_b = jnp.concatenate([side_b, near_b], axis=0)
-    return [early_b, late_b, core_b, b.swap(late_b, CORE)]
+    got_b = b.gather_core(close(env, *got_b))
+    return [b.mine, got_b]
 
 
 def body(count, orbitals_zero, orbitals_one, correlation_zero, correlation_one, cotangent):

time: 123 us -> 120 us (0.976)
  waiting for transfers between devices: 22 us -> 16.7 us
  starting transfers between devices: 44.9 us -> 46.5 us
    ppermute x38 -> x36, waiting for transfers between devices: 22 us -> 16.7 us  [swap(): return lax.ppermute(x, 'row', [(i, i ^ offset) for i in range(self.count)])]
    ppermute x38 -> x36, starting transfers between devices: 44.9 us -> 46.5 us  [swap(): return lax.ppermute(x, 'row', [(i, i ^ offset) for i in range(self.count)])]
  transfers between devices with their start and end apart: 38 -> 36, of which waited for: 13 -> 11; matrix products, arithmetic and copies ran while one was open for 0% -> 0% of each run, Pallas kernels for 30% -> 31%
where the time goes in v4:
time: 120 us; the launch traced here: 119 us
  Pallas kernels  54.9 us (46%)
  starting transfers between devices  46.5 us (39%)
  waiting for transfers between devices  16.7 us (14%)
    ppermute x36, starting transfers between devices, swap(): return lax.ppermute(x, 'row', [(i, i ^ offset) for i in range(self.count)])  46.5 us
    pallas_call x4, Pallas kernels, affine(): call(affine_kernel, 'affine', struct(height, size), 18, 1 / parts, 2, gri...  17.5 us
    ppermute x36, waiting for transfers between devices, swap(): return lax.ppermute(x, 'row', [(i, i ^ offset) for i in range(self.count)])  16.7 us
    pallas_call x1, Pallas kernels, first_gram(): call(functools.partial(first_gram_kernel, shards), 'first_gram', halves(s...  6.93 us
    pallas_call x1, Pallas kernels, second_gram(): call(functools.partial(second_gram_kernel, shards, len(pieces)), 'second_...  5.85 us
    pallas_call x1, Pallas kernels, early_middle(): call(functools.partial(early_kernel, shards, len(pieces)), 'early_middle'...  5.51 us
    pallas_call x1, Pallas kernels, last_step(): call(functools.partial(last_kernel, shards, len(pieces)), 'last', struct(...  5.11 us
    pallas_call x1, Pallas kernels, fourth_gram(): call(functools.partial(fourth_gram_kernel, shards), 'fourth_gram', halves...  3.89 us
  transfers between devices with their start and end apart: 36, of which 11 were waited for; matrix products, arithmetic and copies ran while one was open for 0% of the time, Pallas kernels for 31%

profile of v4, /device:TPU:0, one launch (start us, length us, event | category | flops | bytes accessed | tf_op | source)
XLA Modules:
  0.0 119.4 jit_solution(6140559871150166792)
XLA Ops:
  0.0 6.9 %first_gram.1 = (f32[128,1152]{1,0:T(8,128)S(1)}, f32[128,1152]{1,0:T(8,128)S(1)}, bf16[1024,1024]{1,0:T(8,128)(2,1)S(1)}, bf16[1024,1024]{1,0:T(8,128)(2,1)S(1)...) custom-call(s32[1]{0:T(128)} %bitcast.me_ref, f32[1024,1024]{1,0:T(8,128)} %x_ref.1, f32[1024,1024]{1,0:T(8,128)} %a_ref.1), custom_call_target="tpu_custom_call" | custom-call | flops 32212254720 | bytes 167772160 | tf_op jit(solution)/shard_map/first_gram/pallas_call | solution.py:149
  7.5 3.6 %other_gram.1 = (f32[128,1152]{1,0:T(8,128)S(1)}, f32[128,1152]{1,0:T(8,128)S(1)}) custom-call(s32[1]{0:T(128)} %bitcast.me_ref, bf16[1024,1024]{1,0:T(8,128)(2,1)S(1)} %get-tuple-element.163.ah, bf16[1024,1024]{1,0:T(8,128)(2,1)S(1)} %get-tuple-element.164.al, bf16[1024,1024]{1,0:T(8,128)(2,1)S(1)} %get-tuple-element.165.bh, ...), custom_call_target="tpu_custom_call" | custom-call | flops 32212254720 | bytes 83886080 | tf_op jit(solution)/shard_map/other_gram/pallas_call | solution.py:179
  11.2 3.6 %collective-permute-start.7 = (f32[32,1152]{1,0:T(8,128)S(1)}, f32[32,1152]{1,0:T(8,128)S(1)}, u32[]{:S(2)}, u32[]{:S(2)}) collective-permute-start(f32[32,1152]{1,0:T(8,128)S(1)} %get-tuple-element.325), channel_id=1, source_target_pairs={{0,6},{1,7},{2,4},{3,5},{4,2},{5,3},{6,0},{7,1},{8,14},{9,15},{10,... | collective-permute-start | bytes 442376 | tf_op jit(solution)/shard_map/ppermute | solution.py:407
  15.5 4.3 %affine.4.refs_4_ = f32[512,1024]{1,0:T(8,128)S(1)} custom-call(f32[1024,1024]{1,0:T(8,128)S(1)} %copy-done, f32[1024,1024]{1,0:T(8,128)S(1)} %copy-done.1), custom_call_target="tpu_custom_call" | custom-call | flops 32212254720 | bytes 83886080 | tf_op jit(solution)/shard_map/affine/pallas_call | solution.py:207
  20.0 2.9 %collective-permute-start.4 = (f32[32,1152]{1,0:T(8,128)S(1)}, f32[32,1152]{1,0:T(8,128)S(1)}, u32[]{:S(2)}, u32[]{:S(2)}) collective-permute-start(f32[32,1152]{1,0:T(8,128)S(1)} %get-tuple-element.328), channel_id=1, source_target_pairs={{0,6},{1,7},{2,4},{3,5},{4,2},{5,3},{6,0},{7,1},{8,14},{9,15},{10,... | collective-permute-start | bytes 442376 | tf_op jit(solution)/shard_map/ppermute | solution.py:407
  25.0 3.0 %collective-permute-start.9 = (f32[32,1152]{1,0:T(8,128)S(1)}, f32[32,1152]{1,0:T(8,128)S(1)}, u32[]{:S(2)}, u32[]{:S(2)}) collective-permute-start(f32[32,1152]{1,0:T(8,128)S(1)} %fusion.5), channel_id=1, source_target_pairs={{0,8},{1,9},{2,10},{3,11},{4,12},{5,13},{6,14},{7,15},{8,0},{9,1},... | collective-permute-start | bytes 442376 | tf_op jit(solution)/shard_map/ppermute | solution.py:407
  27.9 4.5 %affine.5.refs_5_ = f32[512,1024]{1,0:T(8,128)S(1)} custom-call(f32[1024,1024]{1,0:T(8,128)S(1)} %copy-done, f32[1024,1024]{1,0:T(8,128)S(1)} %copy-done.1), custom_call_target="tpu_custom_call" | custom-call | flops 32212254720 | bytes 83886080 | tf_op jit(solution)/shard_map/affine/pallas_call | solution.py:207
  32.5 1.4 %collective-permute-done.3 = f32[32,1152]{1,0:T(8,128)S(1)} collective-permute-done((f32[32,1152]{1,0:T(8,128)S(1)}, f32[32,1152]{1,0:T(8,128)S(1)}, u32[]{:S(2)}, u32[]{:S(2)}) %collective-permute-start.3) | collective-permute-done | bytes 147488 | tf_op jit(solution)/shard_map/ppermute | solution.py:407
  34.6 5.7 %collective-permute-start.15 = (f32[32,1152]{1,0:T(8,128)S(1)}, f32[32,1152]{1,0:T(8,128)S(1)}, u32[]{:S(2)}, u32[]{:S(2)}) collective-permute-start(f32[32,1152]{1,0:T(8,128)S(1)} %add.83), channel_id=1, source_target_pairs={{0,6},{1,7},{2,4},{3,5},{4,2},{5,3},{6,0},{7,1},{8,14},{9,15},{10,... | collective-permute-start | bytes 442376 | tf_op jit(solution)/shard_map/ppermute | solution.py:407
  41.0 2.5 %collective-permute-done.8 = f32[32,1152]{1,0:T(8,128)S(1)} collective-permute-done((f32[32,1152]{1,0:T(8,128)S(1)}, f32[32,1152]{1,0:T(8,128)S(1)}, u32[]{:S(2)}, u32[]{:S(2)}) %collective-permute-start.8) | collective-permute-done | bytes 147488 | tf_op jit(solution)/shard_map/ppermute | solution.py:407
  43.9 1.8 %collective-permute-start.11 = (f32[32,1152]{1,0:T(8,128)S(1)}, f32[32,1152]{1,0:T(8,128)S(1)}, u32[]{:S(2)}, u32[]{:S(2)}) collective-permute-start(f32[32,1152]{1,0:T(8,128)S(1)} %add.82), channel_id=1, source_target_pairs={{0,4},{1,5},{2,6},{3,7},{4,0},{5,1},{6,2},{7,3},{8,12},{9,13},{10,... | collective-permute-start | bytes 442376 | tf_op jit(solution)/shard_map/ppermute | solution.py:407
  45.7 1.4 %collective-permute-start.10 = (f32[32,1152]{1,0:T(8,128)S(1)}, f32[32,1152]{1,0:T(8,128)S(1)}, u32[]{:S(2)}, u32[]{:S(2)}) collective-permute-start(f32[32,1152]{1,0:T(8,128)S(1)} %add.82), channel_id=1, source_target_pairs={{0,2},{1,3},{2,0},{3,1},{4,6},{5,7},{6,4},{7,5},{8,10},{9,11},{10,... | collective-permute-start | bytes 442376 | tf_op jit(solution)/shard_map/ppermute | solution.py:407
  49.9 5.5 %early_middle.1 = (f32[1024,1024]{1,0:T(8,128)S(1)}, f32[1024,256]{1,0:T(8,128)S(1)}) custom-call(s32[1]{0:T(128)} %bitcast.me_ref, f32[128,1152]{1,0:T(8,128)S(1)} %pad_maximum_fusion.refs_0_, f32[128,1152]{1,0:T(8,128)S(1)} %collective-permute-done.16.refs_1_, bf16[1024,1024]{1,0:T(8,128)(2,1)S(1)} %get-tuple-element.250.refs_2_, ...), custom_call_target="tpu_custom_call" | custom-call | flops 48318382080 | bytes 209715200 | tf_op jit(solution)/shard_map/early_middle/pallas_call | solution.py:304
  55.7 1.9 %collective-permute-done.17.refs_1_ = f32[128,1152]{1,0:T(8,128)S(1)} collective-permute-done((f32[128,1152]{1,0:T(8,128)S(1)}, f32[128,1152]{1,0:T(8,128)S(1)}, u32[]{:S(2)}, u32[]{:S(2)}) %collective-permute-start.17) | collective-permute-done | bytes 589856 | tf_op jit(solution)/shard_map/ppermute | solution.py:407
  57.6 5.9 %second_gram.1 = (f32[128,1152]{1,0:T(8,128)S(1)}, f32[128,1152]{1,0:T(8,128)S(1)}, f32[1024,1024]{1,0:T(8,128)S(1)}, bf16[1024,768]{1,0:T(8,128)(2,1)S(1)}, bf16[1024,768]{1,0:T(8,128)(2,1)S(1)}) custom-call(s32[1]{0:T(128)} %bitcast.me_ref, f32[128,1152]{1,0:T(8,128)S(1)} %pad_maximum_fusion.1.refs_0_, f32[128,1152]{1,0:T(8,128)S(1)} %collective-permute-done.17.refs_1_, ...), custom_call_target="tpu_custom_call" | custom-call | flops 51539607552 | bytes 209715200 | tf_op jit(solution)/shard_map/second_gram/pallas_call | solution.py:336
  63.6 3.9 %fourth_gram.1 = (f32[128,1152]{1,0:T(8,128)S(1)}, f32[128,1152]{1,0:T(8,128)S(1)}) custom-call(s32[1]{0:T(128)} %bitcast.me_ref, bf16[1024,1024]{1,0:T(8,128)(2,1)S(1)} %get-tuple-element.253.refs_6_.refs_5_.xh, bf16[1024,1024]{1,0:T(8,128)(2,1)S(1)} %get-tuple-element.254.refs_7_.refs_6_.xl, bf16[1024,768]{1,0:T(8,128)(2,1)S(1)} %get-tuple-element.257.mh, ...), custom_call_target="tpu_custom_call" | custom-call | flops 32212254720 | bytes 83886080 | tf_op jit(solution)/shard_map/fourth_gram/pallas_call | solution.py:352
  67.6 2.8 %collective-permute-start.25 = (f32[32,1152]{1,0:T(8,128)S(1)}, f32[32,1152]{1,0:T(8,128)S(1)}, u32[]{:S(2)}, u32[]{:S(2)}) collective-permute-start(f32[32,1152]{1,0:T(8,128)S(1)} %get-tuple-element.319), channel_id=1, source_target_pairs={{0,6},{1,7},{2,4},{3,5},{4,2},{5,3},{6,0},{7,1},{8,14},{9,15},{10,... | collective-permute-start | bytes 442376 | tf_op jit(solution)/shard_map/ppermute | solution.py:407
  71.6 1.4 %collective-permute-start.23 = (f32[32,1152]{1,0:T(8,128)S(1)}, f32[32,1152]{1,0:T(8,128)S(1)}, u32[]{:S(2)}, u32[]{:S(2)}) collective-permute-start(f32[32,1152]{1,0:T(8,128)S(1)} %get-tuple-element.321), channel_id=1, source_target_pairs={{0,2},{1,3},{2,0},{3,1},{4,6},{5,7},{6,4},{7,5},{8,10},{9,11},{10,... | collective-permute-start | bytes 442376 | tf_op jit(solution)/shard_map/ppermute | solution.py:407
  73.0 4.4 %affine.6.refs_4_ = f32[512,1024]{1,0:T(8,128)S(1)} custom-call(f32[1024,1024]{1,0:T(8,128)S(1)} %get-tuple-element.278.a_ref, f32[1024,1024]{1,0:T(8,128)S(1)} %copy-done.3), custom_call_target="tpu_custom_call" | custom-call | flops 32212254720 | bytes 83886080 | tf_op jit(solution)/shard_map/affine/pallas_call | solution.py:207
  77.5 1.5 %collective-permute-start.22 = (f32[32,1152]{1,0:T(8,128)S(1)}, f32[32,1152]{1,0:T(8,128)S(1)}, u32[]{:S(2)}, u32[]{:S(2)}) collective-permute-start(f32[32,1152]{1,0:T(8,128)S(1)} %get-tuple-element.322), channel_id=1, source_target_pairs={{0,6},{1,7},{2,4},{3,5},{4,2},{5,3},{6,0},{7,1},{8,14},{9,15},{10,... | collective-permute-start | bytes 442376 | tf_op jit(solution)/shard_map/ppermute | solution.py:407
  79.9 1.4 %collective-permute-start.20 = (f32[32,1152]{1,0:T(8,128)S(1)}, f32[32,1152]{1,0:T(8,128)S(1)}, u32[]{:S(2)}, u32[]{:S(2)}) collective-permute-start(f32[32,1152]{1,0:T(8,128)S(1)} %get-tuple-element.324), channel_id=1, source_target_pairs={{0,2},{1,3},{2,0},{3,1},{4,6},{5,7},{6,4},{7,5},{8,10},{9,11},{10,... | collective-permute-start | bytes 442376 | tf_op jit(solution)/shard_map/ppermute | solution.py:407
  81.4 3.8 %collective-permute-start.27 = (f32[32,1152]{1,0:T(8,128)S(1)}, f32[32,1152]{1,0:T(8,128)S(1)}, u32[]{:S(2)}, u32[]{:S(2)}) collective-permute-start(f32[32,1152]{1,0:T(8,128)S(1)} %fusion.1), channel_id=1, source_target_pairs={{0,8},{1,9},{2,10},{3,11},{4,12},{5,13},{6,14},{7,15},{8,0},{9,1},... | collective-permute-start | bytes 442376 | tf_op jit(solution)/shard_map/ppermute | solution.py:407
  85.1 4.4 %affine.7.refs_5_ = f32[512,1024]{1,0:T(8,128)S(1)} custom-call(f32[1024,1024]{1,0:T(8,128)S(1)} %get-tuple-element.278.a_ref, f32[1024,1024]{1,0:T(8,128)S(1)} %copy-done.3), custom_call_target="tpu_custom_call" | custom-call | flops 32212254720 | bytes 83886080 | tf_op jit(solution)/shard_map/affine/pallas_call | solution.py:207
  91.7 5.3 %collective-permute-start.33 = (f32[32,1152]{1,0:T(8,128)S(1)}, f32[32,1152]{1,0:T(8,128)S(1)}, u32[]{:S(2)}, u32[]{:S(2)}) collective-permute-start(f32[32,1152]{1,0:T(8,128)S(1)} %add.93), channel_id=1, source_target_pairs={{0,6},{1,7},{2,4},{3,5},{4,2},{5,3},{6,0},{7,1},{8,14},{9,15},{10,... | collective-permute-start | bytes 442376 | tf_op jit(solution)/shard_map/ppermute | solution.py:407
  97.6 2.6 %collective-permute-done.26 = f32[32,1152]{1,0:T(8,128)S(1)} collective-permute-done((f32[32,1152]{1,0:T(8,128)S(1)}, f32[32,1152]{1,0:T(8,128)S(1)}, u32[]{:S(2)}, u32[]{:S(2)}) %collective-permute-start.26) | collective-permute-done | bytes 147488 | tf_op jit(solution)/shard_map/ppermute | solution.py:407
  100.3 1.5 %collective-permute-start.30 = (f32[32,1152]{1,0:T(8,128)S(1)}, f32[32,1152]{1,0:T(8,128)S(1)}, u32[]{:S(2)}, u32[]{:S(2)}) collective-permute-start(f32[32,1152]{1,0:T(8,128)S(1)} %add.92), channel_id=1, source_target_pairs={{0,6},{1,7},{2,4},{3,5},{4,2},{5,3},{6,0},{7,1},{8,14},{9,15},{10,... | collective-permute-start | bytes 442376 | tf_op jit(solution)/shard_map/ppermute | solution.py:407
  102.6 1.8 %collective-permute-start.28 = (f32[32,1152]{1,0:T(8,128)S(1)}, f32[32,1152]{1,0:T(8,128)S(1)}, u32[]{:S(2)}, u32[]{:S(2)}) collective-permute-start(f32[32,1152]{1,0:T(8,128)S(1)} %add.92), channel_id=1, source_target_pairs={{0,2},{1,3},{2,0},{3,1},{4,6},{5,7},{6,4},{7,5},{8,10},{9,11},{10,... | collective-permute-start | bytes 442376 | tf_op jit(solution)/shard_map/ppermute | solution.py:407
  104.4 1.7 %collective-permute-done.32 = f32[32,1152]{1,0:T(8,128)S(1)} collective-permute-done((f32[32,1152]{1,0:T(8,128)S(1)}, f32[32,1152]{1,0:T(8,128)S(1)}, u32[]{:S(2)}, u32[]{:S(2)}) %collective-permute-start.32) | collective-permute-done | bytes 147488 | tf_op jit(solution)/shard_map/ppermute | solution.py:407
  106.6 1.6 %collective-permute-done.34.refs_1_ = f32[128,1152]{1,0:T(8,128)S(1)} collective-permute-done((f32[128,1152]{1,0:T(8,128)S(1)}, f32[128,1152]{1,0:T(8,128)S(1)}, u32[]{:S(2)}, u32[]{:S(2)}) %collective-permute-start.34) | collective-permute-done | bytes 589856 | tf_op jit(solution)/shard_map/ppermute | solution.py:407
  108.2 3.7 %partial_apply.1.refs_4_ = f32[1024,1024]{1,0:T(8,128)S(1)} custom-call(s32[1]{0:T(128)} %bitcast.me_ref, f32[128,1152]{1,0:T(8,128)S(1)} %pad_maximum_fusion.2.refs_0_, f32[128,1152]{1,0:T(8,128)S(1)} %collective-permute-done.34.refs_1_, bf16[1024,1024]{1,0:T(8,128)(2,1)S(1)} %cut.4.refs_2_, bf16[1024,1024]{1,0:T(8,128)(2,1)S(1)} %cut.5.refs_3_, ...), custom_call_target="tpu_custom_call" | custom-call | flops 32212254720 | bytes 125829120 | tf_op jit(solution)/shard_map/partial_apply/pallas_call | solution.py:259
  112.2 1.9 %collective-permute-done.35.refs_1_ = f32[128,1152]{1,0:T(8,128)S(1)} collective-permute-done((f32[128,1152]{1,0:T(8,128)S(1)}, f32[128,1152]{1,0:T(8,128)S(1)}, u32[]{:S(2)}, u32[]{:S(2)}) %collective-permute-start.35) | collective-permute-done | bytes 589856 | tf_op jit(solution)/shard_map/ppermute | solution.py:407
  114.1 5.1 %last.1 = f32[1024,1024]{1,0:T(8,128)} custom-call(s32[1]{0:T(128)} %bitcast.me_ref, f32[128,1152]{1,0:T(8,128)S(1)} %pad_maximum_fusion.3.refs_0_, f32[128,1152]{1,0:T(8,128)S(1)} %collective-permute-done.35.refs_1_, bf16[1024,1024]{1,0:T(8,128)(2,1)S(1)} %cut.4.refs_2_, bf16[1024,1024]{1,0:T(8,128)(2,1)S(1)} %cut.5.refs_3_, ...), custom_call_target="tpu_custom_call" | custom-call | flops 32212254720 | bytes 125829120 | tf_op jit(solution)/shard_map/last/pallas_call | solution.py:384
  (87 shorter events, 15.1 us)
Async XLA Ops:
  6.9 4.2 %collective-permute-start = (f32[128,1152]{1,0:T(8,128)S(1)}, f32[128,1152]{1,0:T(8,128)S(1)}, u32[]{:S(2)}, u32[]{:S(2)}) collective-permute-start(f32[128,1152]{1,0:T(8,128)S(1)} %get-tuple-element.162), channel_id=1, source_target_pairs={{0,1},{1,0},{2,3},{3,2},{4,5},{5,4},{6,7},{7,6},{8,9},{9,8},{10,11... | collective-permute-start | bytes 1769480 | tf_op jit(solution)/shard_map/ppermute | solution.py:407
  11.2 13.4 %collective-permute-start.7 = (f32[32,1152]{1,0:T(8,128)S(1)}, f32[32,1152]{1,0:T(8,128)S(1)}, u32[]{:S(2)}, u32[]{:S(2)}) collective-permute-start(f32[32,1152]{1,0:T(8,128)S(1)} %get-tuple-element.325), channel_id=1, source_target_pairs={{0,6},{1,7},{2,4},{3,5},{4,2},{5,3},{6,0},{7,1},{8,14},{9,15},{10,... | collective-permute-start | bytes 442376 | tf_op jit(solution)/shard_map/ppermute | solution.py:407
  14.8 10.1 %collective-permute-start.6 = (f32[32,1152]{1,0:T(8,128)S(1)}, f32[32,1152]{1,0:T(8,128)S(1)}, u32[]{:S(2)}, u32[]{:S(2)}) collective-permute-start(f32[32,1152]{1,0:T(8,128)S(1)} %get-tuple-element.326), channel_id=1, source_target_pairs={{0,4},{1,5},{2,6},{3,7},{4,0},{5,1},{6,2},{7,3},{8,12},{9,13},{10,... | collective-permute-start | bytes 442376 | tf_op jit(solution)/shard_map/ppermute | solution.py:407
  15.3 9.6 %collective-permute-start.5 = (f32[32,1152]{1,0:T(8,128)S(1)}, f32[32,1152]{1,0:T(8,128)S(1)}, u32[]{:S(2)}, u32[]{:S(2)}) collective-permute-start(f32[32,1152]{1,0:T(8,128)S(1)} %get-tuple-element.327), channel_id=1, source_target_pairs={{0,2},{1,3},{2,0},{3,1},{4,6},{5,7},{6,4},{7,5},{8,10},{9,11},{10,... | collective-permute-start | bytes 442376 | tf_op jit(solution)/shard_map/ppermute | solution.py:407
  15.5 4.4 %collective-permute-start.1 = (f32[128,1152]{1,0:T(8,128)S(1)}, f32[128,1152]{1,0:T(8,128)S(1)}, u32[]{:S(2)}, u32[]{:S(2)}) collective-permute-start(f32[128,1152]{1,0:T(8,128)S(1)} %get-tuple-element.170), channel_id=1, source_target_pairs={{0,1},{1,0},{2,3},{3,2},{4,5},{5,4},{6,7},{7,6},{8,9},{9,8},{10,11... | collective-permute-start | bytes 1769480 | tf_op jit(solution)/shard_map/ppermute | solution.py:407
  20.0 12.5 %collective-permute-start.4 = (f32[32,1152]{1,0:T(8,128)S(1)}, f32[32,1152]{1,0:T(8,128)S(1)}, u32[]{:S(2)}, u32[]{:S(2)}) collective-permute-start(f32[32,1152]{1,0:T(8,128)S(1)} %get-tuple-element.328), channel_id=1, source_target_pairs={{0,6},{1,7},{2,4},{3,5},{4,2},{5,3},{6,0},{7,1},{8,14},{9,15},{10,... | collective-permute-start | bytes 442376 | tf_op jit(solution)/shard_map/ppermute | solution.py:407
  22.9 11.0 %collective-permute-start.3 = (f32[32,1152]{1,0:T(8,128)S(1)}, f32[32,1152]{1,0:T(8,128)S(1)}, u32[]{:S(2)}, u32[]{:S(2)}) collective-permute-start(f32[32,1152]{1,0:T(8,128)S(1)} %get-tuple-element.329), channel_id=1, source_target_pairs={{0,4},{1,5},{2,6},{3,7},{4,0},{5,1},{6,2},{7,3},{8,12},{9,13},{10,... | collective-permute-start | bytes 442376 | tf_op jit(solution)/shard_map/ppermute | solution.py:407
  24.7 9.2 %collective-permute-start.2 = (f32[32,1152]{1,0:T(8,128)S(1)}, f32[32,1152]{1,0:T(8,128)S(1)}, u32[]{:S(2)}, u32[]{:S(2)}) collective-permute-start(f32[32,1152]{1,0:T(8,128)S(1)} %get-tuple-element.330), channel_id=1, source_target_pairs={{0,2},{1,3},{2,0},{3,1},{4,6},{5,7},{6,4},{7,5},{8,10},{9,11},{10,... | collective-permute-start | bytes 442376 | tf_op jit(solution)/shard_map/ppermute | solution.py:407
  25.0 9.6 %collective-permute-start.9 = (f32[32,1152]{1,0:T(8,128)S(1)}, f32[32,1152]{1,0:T(8,128)S(1)}, u32[]{:S(2)}, u32[]{:S(2)}) collective-permute-start(f32[32,1152]{1,0:T(8,128)S(1)} %fusion.5), channel_id=1, source_target_pairs={{0,8},{1,9},{2,10},{3,11},{4,12},{5,13},{6,14},{7,15},{8,0},{9,1},... | collective-permute-start | bytes 442376 | tf_op jit(solution)/shard_map/ppermute | solution.py:407
  33.9 9.6 %collective-permute-start.8 = (f32[32,1152]{1,0:T(8,128)S(1)}, f32[32,1152]{1,0:T(8,128)S(1)}, u32[]{:S(2)}, u32[]{:S(2)}) collective-permute-start(f32[32,1152]{1,0:T(8,128)S(1)} %fusion.7), channel_id=1, source_target_pairs={{0,8},{1,9},{2,10},{3,11},{4,12},{5,13},{6,14},{7,15},{8,0},{9,1},... | collective-permute-start | bytes 442376 | tf_op jit(solution)/shard_map/ppermute | solution.py:407
  34.6 11.1 %collective-permute-start.15 = (f32[32,1152]{1,0:T(8,128)S(1)}, f32[32,1152]{1,0:T(8,128)S(1)}, u32[]{:S(2)}, u32[]{:S(2)}) collective-permute-start(f32[32,1152]{1,0:T(8,128)S(1)} %add.83), channel_id=1, source_target_pairs={{0,6},{1,7},{2,4},{3,5},{4,2},{5,3},{6,0},{7,1},{8,14},{9,15},{10,... | collective-permute-start | bytes 442376 | tf_op jit(solution)/shard_map/ppermute | solution.py:407
  40.3 7.4 %collective-permute-start.14 = (f32[32,1152]{1,0:T(8,128)S(1)}, f32[32,1152]{1,0:T(8,128)S(1)}, u32[]{:S(2)}, u32[]{:S(2)}) collective-permute-start(f32[32,1152]{1,0:T(8,128)S(1)} %add.83), channel_id=1, source_target_pairs={{0,4},{1,5},{2,6},{3,7},{4,0},{5,1},{6,2},{7,3},{8,12},{9,13},{10,... | collective-permute-start | bytes 442376 | tf_op jit(solution)/shard_map/ppermute | solution.py:407
  40.3 7.4 %collective-permute-start.13 = (f32[32,1152]{1,0:T(8,128)S(1)}, f32[32,1152]{1,0:T(8,128)S(1)}, u32[]{:S(2)}, u32[]{:S(2)}) collective-permute-start(f32[32,1152]{1,0:T(8,128)S(1)} %add.83), channel_id=1, source_target_pairs={{0,2},{1,3},{2,0},{3,1},{4,6},{5,7},{6,4},{7,5},{8,10},{9,11},{10,... | collective-permute-start | bytes 442376 | tf_op jit(solution)/shard_map/ppermute | solution.py:407
  43.5 11.9 %collective-permute-start.12 = (f32[32,1152]{1,0:T(8,128)S(1)}, f32[32,1152]{1,0:T(8,128)S(1)}, u32[]{:S(2)}, u32[]{:S(2)}) collective-permute-start(f32[32,1152]{1,0:T(8,128)S(1)} %add.82), channel_id=1, source_target_pairs={{0,6},{1,7},{2,4},{3,5},{4,2},{5,3},{6,0},{7,1},{8,14},{9,15},{10,... | collective-permute-start | bytes 442376 | tf_op jit(solution)/shard_map/ppermute | solution.py:407
  43.9 11.5 %collective-permute-start.11 = (f32[32,1152]{1,0:T(8,128)S(1)}, f32[32,1152]{1,0:T(8,128)S(1)}, u32[]{:S(2)}, u32[]{:S(2)}) collective-permute-start(f32[32,1152]{1,0:T(8,128)S(1)} %add.82), channel_id=1, source_target_pairs={{0,4},{1,5},{2,6},{3,7},{4,0},{5,1},{6,2},{7,3},{8,12},{9,13},{10,... | collective-permute-start | bytes 442376 | tf_op jit(solution)/shard_map/ppermute | solution.py:407
  45.7 9.7 %collective-permute-start.10 = (f32[32,1152]{1,0:T(8,128)S(1)}, f32[32,1152]{1,0:T(8,128)S(1)}, u32[]{:S(2)}, u32[]{:S(2)}) collective-permute-start(f32[32,1152]{1,0:T(8,128)S(1)} %add.82), channel_id=1, source_target_pairs={{0,2},{1,3},{2,0},{3,1},{4,6},{5,7},{6,4},{7,5},{8,10},{9,11},{10,... | collective-permute-start | bytes 442376 | tf_op jit(solution)/shard_map/ppermute | solution.py:407
  63.4 4.1 %collective-permute-start.18 = (f32[128,1152]{1,0:T(8,128)S(1)}, f32[128,1152]{1,0:T(8,128)S(1)}, u32[]{:S(2)}, u32[]{:S(2)}) collective-permute-start(f32[128,1152]{1,0:T(8,128)S(1)} %get-tuple-element.256), channel_id=1, source_target_pairs={{0,1},{1,0},{2,3},{3,2},{4,5},{5,4},{6,7},{7,6},{8,9},{9,8},{10,11... | collective-permute-start | bytes 1769480 | tf_op jit(solution)/shard_map/ppermute | solution.py:407
  67.6 12.2 %collective-permute-start.25 = (f32[32,1152]{1,0:T(8,128)S(1)}, f32[32,1152]{1,0:T(8,128)S(1)}, u32[]{:S(2)}, u32[]{:S(2)}) collective-permute-start(f32[32,1152]{1,0:T(8,128)S(1)} %get-tuple-element.319), channel_id=1, source_target_pairs={{0,6},{1,7},{2,4},{3,5},{4,2},{5,3},{6,0},{7,1},{8,14},{9,15},{10,... | collective-permute-start | bytes 442376 | tf_op jit(solution)/shard_map/ppermute | solution.py:407
  70.5 10.8 %collective-permute-start.24 = (f32[32,1152]{1,0:T(8,128)S(1)}, f32[32,1152]{1,0:T(8,128)S(1)}, u32[]{:S(2)}, u32[]{:S(2)}) collective-permute-start(f32[32,1152]{1,0:T(8,128)S(1)} %get-tuple-element.320), channel_id=1, source_target_pairs={{0,4},{1,5},{2,6},{3,7},{4,0},{5,1},{6,2},{7,3},{8,12},{9,13},{10,... | collective-permute-start | bytes 442376 | tf_op jit(solution)/shard_map/ppermute | solution.py:407
  71.6 9.7 %collective-permute-start.23 = (f32[32,1152]{1,0:T(8,128)S(1)}, f32[32,1152]{1,0:T(8,128)S(1)}, u32[]{:S(2)}, u32[]{:S(2)}) collective-permute-start(f32[32,1152]{1,0:T(8,128)S(1)} %get-tuple-element.321), channel_id=1, source_target_pairs={{0,2},{1,3},{2,0},{3,1},{4,6},{5,7},{6,4},{7,5},{8,10},{9,11},{10,... | collective-permute-start | bytes 442376 | tf_op jit(solution)/shard_map/ppermute | solution.py:407
  73.0 4.4 %collective-permute-start.19 = (f32[128,1152]{1,0:T(8,128)S(1)}, f32[128,1152]{1,0:T(8,128)S(1)}, u32[]{:S(2)}, u32[]{:S(2)}) collective-permute-start(f32[128,1152]{1,0:T(8,128)S(1)} %get-tuple-element.265), channel_id=1, source_target_pairs={{0,1},{1,0},{2,3},{3,2},{4,5},{5,4},{6,7},{7,6},{8,9},{9,8},{10,11... | collective-permute-start | bytes 1769480 | tf_op jit(solution)/shard_map/ppermute | solution.py:407
  77.5 12.0 %collective-permute-start.22 = (f32[32,1152]{1,0:T(8,128)S(1)}, f32[32,1152]{1,0:T(8,128)S(1)}, u32[]{:S(2)}, u32[]{:S(2)}) collective-permute-start(f32[32,1152]{1,0:T(8,128)S(1)} %get-tuple-element.322), channel_id=1, source_target_pairs={{0,6},{1,7},{2,4},{3,5},{4,2},{5,3},{6,0},{7,1},{8,14},{9,15},{10,... | collective-permute-start | bytes 442376 | tf_op jit(solution)/shard_map/ppermute | solution.py:407
  79.0 11.4 %collective-permute-start.21 = (f32[32,1152]{1,0:T(8,128)S(1)}, f32[32,1152]{1,0:T(8,128)S(1)}, u32[]{:S(2)}, u32[]{:S(2)}) collective-permute-start(f32[32,1152]{1,0:T(8,128)S(1)} %get-tuple-element.323), channel_id=1, source_target_pairs={{0,4},{1,5},{2,6},{3,7},{4,0},{5,1},{6,2},{7,3},{8,12},{9,13},{10,... | collective-permute-start | bytes 442376 | tf_op jit(solution)/shard_map/ppermute | solution.py:407
  79.9 10.5 %collective-permute-start.20 = (f32[32,1152]{1,0:T(8,128)S(1)}, f32[32,1152]{1,0:T(8,128)S(1)}, u32[]{:S(2)}, u32[]{:S(2)}) collective-permute-start(f32[32,1152]{1,0:T(8,128)S(1)} %get-tuple-element.324), channel_id=1, source_target_pairs={{0,2},{1,3},{2,0},{3,1},{4,6},{5,7},{6,4},{7,5},{8,10},{9,11},{10,... | collective-permute-start | bytes 442376 | tf_op jit(solution)/shard_map/ppermute | solution.py:407
  81.4 10.3 %collective-permute-start.27 = (f32[32,1152]{1,0:T(8,128)S(1)}, f32[32,1152]{1,0:T(8,128)S(1)}, u32[]{:S(2)}, u32[]{:S(2)}) collective-permute-start(f32[32,1152]{1,0:T(8,128)S(1)} %fusion.1), channel_id=1, source_target_pairs={{0,8},{1,9},{2,10},{3,11},{4,12},{5,13},{6,14},{7,15},{8,0},{9,1},... | collective-permute-start | bytes 442376 | tf_op jit(solution)/shard_map/ppermute | solution.py:407
  90.4 9.8 %collective-permute-start.26 = (f32[32,1152]{1,0:T(8,128)S(1)}, f32[32,1152]{1,0:T(8,128)S(1)}, u32[]{:S(2)}, u32[]{:S(2)}) collective-permute-start(f32[32,1152]{1,0:T(8,128)S(1)} %fusion.3), channel_id=1, source_target_pairs={{0,8},{1,9},{2,10},{3,11},{4,12},{5,13},{6,14},{7,15},{8,0},{9,1},... | collective-permute-start | bytes 442376 | tf_op jit(solution)/shard_map/ppermute | solution.py:407
  91.7 10.9 %collective-permute-start.33 = (f32[32,1152]{1,0:T(8,128)S(1)}, f32[32,1152]{1,0:T(8,128)S(1)}, u32[]{:S(2)}, u32[]{:S(2)}) collective-permute-start(f32[32,1152]{1,0:T(8,128)S(1)} %add.93), channel_id=1, source_target_pairs={{0,6},{1,7},{2,4},{3,5},{4,2},{5,3},{6,0},{7,1},{8,14},{9,15},{10,... | collective-permute-start | bytes 442376 | tf_op jit(solution)/shard_map/ppermute | solution.py:407
  97.0 9.1 %collective-permute-start.32 = (f32[32,1152]{1,0:T(8,128)S(1)}, f32[32,1152]{1,0:T(8,128)S(1)}, u32[]{:S(2)}, u32[]{:S(2)}) collective-permute-start(f32[32,1152]{1,0:T(8,128)S(1)} %add.93), channel_id=1, source_target_pairs={{0,4},{1,5},{2,6},{3,7},{4,0},{5,1},{6,2},{7,3},{8,12},{9,13},{10,... | collective-permute-start | bytes 442376 | tf_op jit(solution)/shard_map/ppermute | solution.py:407
  97.0 9.1 %collective-permute-start.31 = (f32[32,1152]{1,0:T(8,128)S(1)}, f32[32,1152]{1,0:T(8,128)S(1)}, u32[]{:S(2)}, u32[]{:S(2)}) collective-permute-start(f32[32,1152]{1,0:T(8,128)S(1)} %add.93), channel_id=1, source_target_pairs={{0,2},{1,3},{2,0},{3,1},{4,6},{5,7},{6,4},{7,5},{8,10},{9,11},{10,... | collective-permute-start | bytes 442376 | tf_op jit(solution)/shard_map/ppermute | solution.py:407
  100.3 11.7 %collective-permute-start.30 = (f32[32,1152]{1,0:T(8,128)S(1)}, f32[32,1152]{1,0:T(8,128)S(1)}, u32[]{:S(2)}, u32[]{:S(2)}) collective-permute-start(f32[32,1152]{1,0:T(8,128)S(1)} %add.92), channel_id=1, source_target_pairs={{0,6},{1,7},{2,4},{3,5},{4,2},{5,3},{6,0},{7,1},{8,14},{9,15},{10,... | collective-permute-start | bytes 442376 | tf_op jit(solution)/shard_map/ppermute | solution.py:407
  101.7 10.2 %collective-permute-start.29 = (f32[32,1152]{1,0:T(8,128)S(1)}, f32[32,1152]{1,0:T(8,128)S(1)}, u32[]{:S(2)}, u32[]{:S(2)}) collective-permute-start(f32[32,1152]{1,0:T(8,128)S(1)} %add.92), channel_id=1, source_target_pairs={{0,4},{1,5},{2,6},{3,7},{4,0},{5,1},{6,2},{7,3},{8,12},{9,13},{10,... | collective-permute-start | bytes 442376 | tf_op jit(solution)/shard_map/ppermute | solution.py:407
  102.6 9.4 %collective-permute-start.28 = (f32[32,1152]{1,0:T(8,128)S(1)}, f32[32,1152]{1,0:T(8,128)S(1)}, u32[]{:S(2)}, u32[]{:S(2)}) collective-permute-start(f32[32,1152]{1,0:T(8,128)S(1)} %add.92), channel_id=1, source_target_pairs={{0,2},{1,3},{2,0},{3,1},{4,6},{5,7},{6,4},{7,5},{8,10},{9,11},{10,... | collective-permute-start | bytes 442376 | tf_op jit(solution)/shard_map/ppermute | solution.py:407
  (10 other events, 68.2 us)

commit v5 on v4

--- a/solution.py
+++ b/solution.py
@@ -58,25 +58,50 @@
 
 def line_blocks(size, i):
     n = size // B
-    at = 0
-    for top in (i, n - 1 - i):
-        for j in range(top, n):
-            yield at, slice(top * B, (top + 1) * B), slice(j * B, (j + 1) * B)
-            at += B
+    block = lambda k: slice(k * B, (k + 1) * B)
+    return [(block(top), block(j)) for top in (i, n - 1 - i) for j in range(top + 1, n)]
+
+
+def diagonal_blocks(size, i):
+    n = size // B
+    return [slice(k * B, (k + 1) * B) for k in (i, n - 1 - i)]
+
+
+def part_rows(size, shards):
+    return size // 4 // shards
+
+
+def shard_rows(size, shards):
+    return part_rows(size, shards) * (size // B) + 8
+
+
+def places():
+    row = lax.broadcasted_iota(jnp.int32, (B, B), 0)
+    column = lax.broadcasted_iota(jnp.int32, (B, B), 1)
+    return row, column
 
 
 def pack(g, packed, keep_ref, send_ref, me, shards, chunk):
     size = g.shape[0]
-    rows = packed.shape[0] // shards
+    rows, height = part_rows(size, shards), shard_rows(size, shards)
     per = B // rows
+    row, column = places()
+    whole = lambda p, q: g[p, q] + g[q, p].T
     for line, i in enumerate(chunk_lines(size, chunk)):
-        for at, p, q in line_blocks(size, i):
-            block = g[p, q] + g[q, p].T
+        starts = [((line * per + s) ^ me) * height for s in range(per)]
+
+        def put(at, s, value):
+            start = pl.multiple_of(starts[s] + at, 8)
+            packed[pl.ds(start, value.shape[0]), :] = value
+
+        upper, lower = [whole(p, p) for p in diagonal_blocks(size, i)]
+        for k, place in enumerate([None] + line_blocks(size, i)):
+            block = whole(*place) if place else jnp.where(column >= row, upper, lower)
             for s in range(per):
-                slot = (line * per + s) ^ me
-                packed[pl.ds(pl.multiple_of(slot * rows, rows), rows), at:at + B] = (
-                    block[s * rows:(s + 1) * rows]
-                )
+                put(k * rows, s, block[s * rows:(s + 1) * rows])
+        element = jnp.sum(jnp.where(column == row, lower, 0.0), axis=0, keepdims=True)
+        for s in range(per):
+            put(height - 8, s, jnp.broadcast_to(element, (8, B)))
     half = keep_ref.shape[0]
     keep_ref[...] = packed[:half]
     send_ref[...] = packed[half:]
@@ -84,26 +109,50 @@
 
 def unpack(pieces, packed, hi, lo, me, shards, chunk):
     size = hi.shape[0]
-    rows = packed.shape[0] // shards
-    slots = iter(range(shards))
+    rows, height = part_rows(size, shards), shard_rows(size, shards)
+    per = B // rows
+    row, column = places()
+    slot = 0
     for piece in pieces:
-        for s in range(piece.shape[0] // rows):
-            at = pl.multiple_of((next(slots) ^ me) * rows, rows)
-            packed[pl.ds(at, rows), :] = piece[s * rows:(s + 1) * rows, :]
+        for s in range(piece.shape[0] // height):
+            at = pl.multiple_of((slot ^ me) * height, 8)
+            packed[pl.ds(at, height), :] = piece[s * height:(s + 1) * height, :]
+            slot += 1
+
+    def put(p, q, block):
+        hi[p, q], lo[p, q] = split(block)
+
     for line, i in enumerate(chunk_lines(size, chunk)):
-        for at, p, q in line_blocks(size, i):
-            block = packed[line * B:(line + 1) * B, at:at + B]
-            hi[p, q], lo[p, q] = split(block)
-            if p.start != q.start:
-                hi[q, p], lo[q, p] = split(block.T)
-
-
-def packed_scratch(size):
-    return pltpu.VMEM((size // 4, size + B), F32)
-
-
-def halves(size):
-    return [struct(size // 8, size + B)] * 2
+        start = line * per * height
+
+        def get(k):
+            return jnp.concatenate(
+                [
+                    packed[start + s * height + k * rows:start + s * height + (k + 1) * rows, :]
+                    for s in range(per)
+                ],
+                axis=0,
+            )
+
+        first, last = diagonal_blocks(size, i)
+        block = get(0)
+        turned = block.T
+        element = packed[start + height - 8:start + height - 7, :]
+        put(first, first, jnp.where(column >= row, block, turned))
+        below = jnp.where(column < row, block, turned)
+        put(last, last, jnp.where(column == row, jnp.broadcast_to(element, (B, B)), below))
+        for k, (p, q) in enumerate(line_blocks(size, i)):
+            block = get(k + 1)
+            put(p, q, block)
+            put(q, p, block.T)
+
+
+def packed_scratch(size, shards):
+    return pltpu.VMEM((shards * shard_rows(size, shards), B), F32)
+
+
+def halves(size, shards):
+    return [struct(shards // 2 * shard_rows(size, shards), B)] * 2
 
 
 def first_gram_kernel(
@@ -148,14 +197,14 @@
     hbm = pl.BlockSpec(memory_space=pltpu.HBM)
     return call(
         functools.partial(first_gram_kernel, shards), "first_gram",
-        halves(size) + [struct(size, rows, dtype=BF16)] * 2 + [struct(rows, size, dtype=BF16)] * 2,
+        halves(size, shards) + [struct(size, rows, dtype=BF16)] * 2 + [struct(rows, size, dtype=BF16)] * 2,
         43, 0.5, 4,
         in_specs=[SMEM, hbm, hbm],
         out_specs=[VMEM] * 6,
         scratch_shapes=[
             pltpu.VMEM((rows, size), F32), pltpu.VMEM((rows, size), F32),
             pltpu.SemaphoreType.DMA((2, 4)),
-            pltpu.VMEM((size, size), F32), packed_scratch(size),
+            pltpu.VMEM((size, size), F32), packed_scratch(size, shards),
         ],
     )(me, a, b)
 
@@ -177,10 +226,10 @@
 def other_gram(me, shards, ah, al, bh, bl):
     size = ah.shape[0]
     return call(
-        functools.partial(other_gram_kernel, shards), "other_gram", halves(size), 18, 0.5, 2,
+        functools.partial(other_gram_kernel, shards), "other_gram", halves(size, shards), 18, 0.5, 2,
         in_specs=[SMEM] + [VMEM] * 4,
         out_specs=[VMEM, VMEM],
-        scratch_shapes=[pltpu.VMEM((size, size), F32), packed_scratch(size)],
+        scratch_shapes=[pltpu.VMEM((size, size), F32), packed_scratch(size, shards)],
     )(me, ah, al, bh, bl)
 
 
@@ -243,8 +292,8 @@
             at = end
 
 
-def sym_scratch(size):
-    return [pltpu.VMEM((size, size), BF16)] * 2 + [packed_scratch(size)]
+def sym_scratch(size, shards):
+    return [pltpu.VMEM((size, size), BF16)] * 2 + [packed_scratch(size, shards)]
 
 
 def partial_kernel(shards, count, me_ref, *refs):
@@ -261,7 +310,7 @@
         struct(rows, size), 18, 0.5, 3,
         in_specs=[SMEM] + [VMEM] * (len(pieces) + 2 + len(base)),
         out_specs=VMEM,
-        scratch_shapes=sym_scratch(size),
+        scratch_shapes=sym_scratch(size, shards),
     )(me, *pieces, ah, al, *base)
 
 
@@ -306,7 +355,7 @@
         [struct(rows, size), struct(size, size // 4)], 20, 0.75, 5,
         in_specs=[SMEM] + [VMEM] * (len(pieces) + 4 + len(base)),
         out_specs=[VMEM] * 2,
-        scratch_shapes=sym_scratch(size),
+        scratch_shapes=sym_scratch(size, shards),
     )(me, *pieces, ah, al, *base, xh, xl)
 
 
@@ -335,10 +384,10 @@
     part = struct(rows, size - size // 4, dtype=BF16)
     return call(
         functools.partial(second_gram_kernel, shards, len(pieces)), "second_gram",
-        halves(size) + [struct(rows, size), part, part], 20, 0.8, 5,
+        halves(size, shards) + [struct(rows, size), part, part], 20, 0.8, 5,
         in_specs=[SMEM] + [VMEM] * (len(pieces) + 6),
         out_specs=[VMEM] * 5,
-        scratch_shapes=sym_scratch(size) + [pltpu.VMEM((size, size), F32)],
+        scratch_shapes=sym_scratch(size, shards) + [pltpu.VMEM((size, size), F32)],
     )(me, *pieces, ah, al, base, xh, xl, col)
 
 
@@ -350,10 +399,10 @@
 def fourth_gram(me, shards, xh, xl, mh, ml):
     size = xh.shape[0]
     return call(
-        functools.partial(fourth_gram_kernel, shards), "fourth_gram", halves(size), 18, 0.5, 2,
+        functools.partial(fourth_gram_kernel, shards), "fourth_gram", halves(size, shards), 18, 0.5, 2,
         in_specs=[SMEM] + [VMEM] * 4,
         out_specs=[VMEM, VMEM],
-        scratch_shapes=[pltpu.VMEM((size, size), F32), packed_scratch(size)],
+        scratch_shapes=[pltpu.VMEM((size, size), F32), packed_scratch(size, shards)],
     )(me, xh, xl, mh, ml)
 
 
@@ -385,7 +434,7 @@
         functools.partial(last_kernel, shards, len(pieces)), "last", struct(rows, size), 22, 0.5, 3,
         in_specs=[SMEM] + [VMEM] * (len(pieces) + 3),
         out_specs=pl.BlockSpec(memory_space=pltpu.HBM),
-        scratch_shapes=sym_scratch(size)
+        scratch_shapes=sym_scratch(size, shards)
         + [pltpu.VMEM((rows, size), F32), pltpu.SemaphoreType.DMA((4,))],
     )(me, *pieces, ah, al, z)
 

time: 120 us -> 117 us (0.975)
  waiting for transfers between devices: 16.7 us -> 13.2 us
    ppermute x36, waiting for transfers between devices: 16.7 us -> 13.2 us  [swap(): return lax.ppermute(x, 'row', [(i, i ^ offset) for i in range(self.count)])]
  transfers between devices with their start and end apart: 36 -> 36, of which waited for: 11 -> 10; matrix products, arithmetic and copies ran while one was open for 0% -> 0% of each run, Pallas kernels for 31% -> 32%
where the time goes in v5:
time: 117 us; the launch traced here: 116 us
  Pallas kernels  54.8 us (47%)
  starting transfers between devices  47.1 us (40%)
  waiting for transfers between devices  13.2 us (11%)
    ppermute x36, starting transfers between devices, swap(): return lax.ppermute(x, 'row', [(i, i ^ offset) for i in range(self.count)])  47.1 us
    pallas_call x4, Pallas kernels, affine(): call(affine_kernel, 'affine', struct(height, size), 18, 1 / parts, 2, gri...  17.5 us
    ppermute x36, waiting for transfers between devices, swap(): return lax.ppermute(x, 'row', [(i, i ^ offset) for i in range(self.count)])  13.2 us
    pallas_call x1, Pallas kernels, first_gram(): call(functools.partial(first_gram_kernel, shards), 'first_gram', halves(s...  6.9 us
    pallas_call x1, Pallas kernels, second_gram(): call(functools.partial(second_gram_kernel, shards, len(pieces)), 'second_...  5.82 us
    pallas_call x1, Pallas kernels, early_middle(): call(functools.partial(early_kernel, shards, len(pieces)), 'early_middle'...  5.51 us
    pallas_call x1, Pallas kernels, last_step(): call(functools.partial(last_kernel, shards, len(pieces)), 'last', struct(...  5.08 us
    pallas_call x1, Pallas kernels, fourth_gram(): call(functools.partial(fourth_gram_kernel, shards), 'fourth_gram', halves...  3.88 us
  transfers between devices with their start and end apart: 36, of which 10 were waited for; matrix products, arithmetic and copies ran while one was open for 0% of the time, Pallas kernels for 32%

profile of v5, /device:TPU:0, one launch (start us, length us, event | category | flops | bytes accessed | tf_op | source)
XLA Modules:
  0.0 116.4 jit_solution(12965032135305735533)
XLA Ops:
  0.0 6.9 %first_gram.1 = (f32[1056,128]{1,0:T(8,128)S(1)}, f32[1056,128]{1,0:T(8,128)S(1)}, bf16[1024,1024]{1,0:T(8,128)(2,1)S(1)}, bf16[1024,1024]{1,0:T(8,128)(2,1)S(1)...) custom-call(s32[1]{0:T(128)} %bitcast.me_ref, f32[1024,1024]{1,0:T(8,128)} %x_ref.1, f32[1024,1024]{1,0:T(8,128)} %a_ref.1), custom_call_target="tpu_custom_call" | custom-call | flops 32212254720 | bytes 167772160 | tf_op jit(solution)/shard_map/first_gram/pallas_call | solution.py:198
  7.4 3.6 %other_gram.1 = (f32[1056,128]{1,0:T(8,128)S(1)}, f32[1056,128]{1,0:T(8,128)S(1)}) custom-call(s32[1]{0:T(128)} %bitcast.me_ref, bf16[1024,1024]{1,0:T(8,128)(2,1)S(1)} %get-tuple-element.163.ah, bf16[1024,1024]{1,0:T(8,128)(2,1)S(1)} %get-tuple-element.164.al, bf16[1024,1024]{1,0:T(8,128)(2,1)S(1)} %get-tuple-element.165.bh, ...), custom_call_target="tpu_custom_call" | custom-call | flops 32212254720 | bytes 83886080 | tf_op jit(solution)/shard_map/other_gram/pallas_call | solution.py:228
  11.2 3.6 %collective-permute-start.7 = (f32[264,128]{1,0:T(8,128)S(1)}, f32[264,128]{1,0:T(8,128)S(1)}, u32[]{:S(2)}, u32[]{:S(2)}) collective-permute-start(f32[264,128]{1,0:T(8,128)S(1)} %get-tuple-element.325), channel_id=1, source_target_pairs={{0,6},{1,7},{2,4},{3,5},{4,2},{5,3},{6,0},{7,1},{8,14},{9,15},{10,... | collective-permute-start | bytes 405512 | tf_op jit(solution)/shard_map/ppermute | solution.py:456
  15.5 4.3 %affine.4.refs_4_ = f32[512,1024]{1,0:T(8,128)S(1)} custom-call(f32[1024,1024]{1,0:T(8,128)S(1)} %copy-done, f32[1024,1024]{1,0:T(8,128)S(1)} %copy-done.1), custom_call_target="tpu_custom_call" | custom-call | flops 32212254720 | bytes 83886080 | tf_op jit(solution)/shard_map/affine/pallas_call | solution.py:256
  19.9 2.9 %collective-permute-start.4 = (f32[264,128]{1,0:T(8,128)S(1)}, f32[264,128]{1,0:T(8,128)S(1)}, u32[]{:S(2)}, u32[]{:S(2)}) collective-permute-start(f32[264,128]{1,0:T(8,128)S(1)} %get-tuple-element.328), channel_id=1, source_target_pairs={{0,6},{1,7},{2,4},{3,5},{4,2},{5,3},{6,0},{7,1},{8,14},{9,15},{10,... | collective-permute-start | bytes 405512 | tf_op jit(solution)/shard_map/ppermute | solution.py:456
  23.3 1.3 %turn.1 = (bf16[1024,1024]{1,0:T(8,128)(2,1)S(1)}, bf16[1024,1024]{1,0:T(8,128)(2,1)S(1)}) custom-call(f32[1024,1024]{1,0:T(8,128)S(1)} %copy-done.4), custom_call_target="tpu_custom_call" | custom-call | flops 6442450944 | bytes 83886080 | tf_op jit(solution)/shard_map/turn/pallas_call | solution.py:323
  24.9 3.0 %collective-permute-start.9 = (f32[264,128]{1,0:T(8,128)S(1)}, f32[264,128]{1,0:T(8,128)S(1)}, u32[]{:S(2)}, u32[]{:S(2)}) collective-permute-start(f32[264,128]{1,0:T(8,128)S(1)} %fusion.5), channel_id=1, source_target_pairs={{0,8},{1,9},{2,10},{3,11},{4,12},{5,13},{6,14},{7,15},{8,0},{9,1},... | collective-permute-start | bytes 405512 | tf_op jit(solution)/shard_map/ppermute | solution.py:456
  27.9 4.5 %affine.5.refs_5_ = f32[512,1024]{1,0:T(8,128)S(1)} custom-call(f32[1024,1024]{1,0:T(8,128)S(1)} %copy-done, f32[1024,1024]{1,0:T(8,128)S(1)} %copy-done.1), custom_call_target="tpu_custom_call" | custom-call | flops 32212254720 | bytes 83886080 | tf_op jit(solution)/shard_map/affine/pallas_call | solution.py:256
  33.5 6.1 %collective-permute-start.15 = (f32[264,128]{1,0:T(8,128)S(1)}, f32[264,128]{1,0:T(8,128)S(1)}, u32[]{:S(2)}, u32[]{:S(2)}) collective-permute-start(f32[264,128]{1,0:T(8,128)S(1)} %add.83), channel_id=1, source_target_pairs={{0,6},{1,7},{2,4},{3,5},{4,2},{5,3},{6,0},{7,1},{8,14},{9,15},{10,... | collective-permute-start | bytes 405512 | tf_op jit(solution)/shard_map/ppermute | solution.py:456
  40.2 1.9 %collective-permute-done.8 = f32[264,128]{1,0:T(8,128)S(1)} collective-permute-done((f32[264,128]{1,0:T(8,128)S(1)}, f32[264,128]{1,0:T(8,128)S(1)}, u32[]{:S(2)}, u32[]{:S(2)}) %collective-permute-start.8) | collective-permute-done | bytes 135200 | tf_op jit(solution)/shard_map/ppermute | solution.py:456
  44.3 1.4 %collective-permute-start.10 = (f32[264,128]{1,0:T(8,128)S(1)}, f32[264,128]{1,0:T(8,128)S(1)}, u32[]{:S(2)}, u32[]{:S(2)}) collective-permute-start(f32[264,128]{1,0:T(8,128)S(1)} %add.82), channel_id=1, source_target_pairs={{0,2},{1,3},{2,0},{3,1},{4,6},{5,7},{6,4},{7,5},{8,10},{9,11},{10,... | collective-permute-start | bytes 405512 | tf_op jit(solution)/shard_map/ppermute | solution.py:456
  48.3 5.5 %early_middle.1 = (f32[1024,1024]{1,0:T(8,128)S(1)}, f32[1024,256]{1,0:T(8,128)S(1)}) custom-call(s32[1]{0:T(128)} %bitcast.me_ref, f32[1056,128]{1,0:T(8,128)S(1)} %pad_maximum_fusion.refs_0_, f32[1056,128]{1,0:T(8,128)S(1)} %collective-permute-done.16.refs_1_, bf16[1024,1024]{1,0:T(8,128)(2,1)S(1)} %get-tuple-element.250.refs_2_, ...), custom_call_target="tpu_custom_call" | custom-call | flops 48318382080 | bytes 209715200 | tf_op jit(solution)/shard_map/early_middle/pallas_call | solution.py:353
  54.1 1.8 %collective-permute-done.17.refs_1_ = f32[1056,128]{1,0:T(8,128)S(1)} collective-permute-done((f32[1056,128]{1,0:T(8,128)S(1)}, f32[1056,128]{1,0:T(8,128)S(1)}, u32[]{:S(2)}, u32[]{:S(2)}) %collective-permute-start.17) | collective-permute-done | bytes 540704 | tf_op jit(solution)/shard_map/ppermute | solution.py:456
  55.9 5.8 %second_gram.1 = (f32[1056,128]{1,0:T(8,128)S(1)}, f32[1056,128]{1,0:T(8,128)S(1)}, f32[1024,1024]{1,0:T(8,128)S(1)}, bf16[1024,768]{1,0:T(8,128)(2,1)S(1)}, bf16[1024,768]{1,0:T(8,128)(2,1)S(1)}) custom-call(s32[1]{0:T(128)} %bitcast.me_ref, f32[1056,128]{1,0:T(8,128)S(1)} %pad_maximum_fusion.1.refs_0_, f32[1056,128]{1,0:T(8,128)S(1)} %collective-permute-done.17.refs_1_, ...), custom_call_target="tpu_custom_call" | custom-call | flops 51539607552 | bytes 209715200 | tf_op jit(solution)/shard_map/second_gram/pallas_call | solution.py:385
  62.0 3.9 %fourth_gram.1 = (f32[1056,128]{1,0:T(8,128)S(1)}, f32[1056,128]{1,0:T(8,128)S(1)}) custom-call(s32[1]{0:T(128)} %bitcast.me_ref, bf16[1024,1024]{1,0:T(8,128)(2,1)S(1)} %get-tuple-element.253.refs_6_.refs_5_.xh, bf16[1024,1024]{1,0:T(8,128)(2,1)S(1)} %get-tuple-element.254.refs_7_.refs_6_.xl, bf16[1024,768]{1,0:T(8,128)(2,1)S(1)} %get-tuple-element.257.mh, ...), custom_call_target="tpu_custom_call" | custom-call | flops 32212254720 | bytes 83886080 | tf_op jit(solution)/shard_map/fourth_gram/pallas_call | solution.py:401
  66.0 3.2 %collective-permute-start.25 = (f32[264,128]{1,0:T(8,128)S(1)}, f32[264,128]{1,0:T(8,128)S(1)}, u32[]{:S(2)}, u32[]{:S(2)}) collective-permute-start(f32[264,128]{1,0:T(8,128)S(1)} %get-tuple-element.319), channel_id=1, source_target_pairs={{0,6},{1,7},{2,4},{3,5},{4,2},{5,3},{6,0},{7,1},{8,14},{9,15},{10,... | collective-permute-start | bytes 405512 | tf_op jit(solution)/shard_map/ppermute | solution.py:456
  70.3 1.4 %collective-permute-start.23 = (f32[264,128]{1,0:T(8,128)S(1)}, f32[264,128]{1,0:T(8,128)S(1)}, u32[]{:S(2)}, u32[]{:S(2)}) collective-permute-start(f32[264,128]{1,0:T(8,128)S(1)} %get-tuple-element.321), channel_id=1, source_target_pairs={{0,2},{1,3},{2,0},{3,1},{4,6},{5,7},{6,4},{7,5},{8,10},{9,11},{10,... | collective-permute-start | bytes 405512 | tf_op jit(solution)/shard_map/ppermute | solution.py:456
  71.6 4.3 %affine.6.refs_4_ = f32[512,1024]{1,0:T(8,128)S(1)} custom-call(f32[1024,1024]{1,0:T(8,128)S(1)} %get-tuple-element.278.a_ref, f32[1024,1024]{1,0:T(8,128)S(1)} %copy-done.3), custom_call_target="tpu_custom_call" | custom-call | flops 32212254720 | bytes 83886080 | tf_op jit(solution)/shard_map/affine/pallas_call | solution.py:256
  76.1 1.5 %collective-permute-start.22 = (f32[264,128]{1,0:T(8,128)S(1)}, f32[264,128]{1,0:T(8,128)S(1)}, u32[]{:S(2)}, u32[]{:S(2)}) collective-permute-start(f32[264,128]{1,0:T(8,128)S(1)} %get-tuple-element.322), channel_id=1, source_target_pairs={{0,6},{1,7},{2,4},{3,5},{4,2},{5,3},{6,0},{7,1},{8,14},{9,15},{10,... | collective-permute-start | bytes 405512 | tf_op jit(solution)/shard_map/ppermute | solution.py:456
  78.5 1.5 %collective-permute-start.20 = (f32[264,128]{1,0:T(8,128)S(1)}, f32[264,128]{1,0:T(8,128)S(1)}, u32[]{:S(2)}, u32[]{:S(2)}) collective-permute-start(f32[264,128]{1,0:T(8,128)S(1)} %get-tuple-element.324), channel_id=1, source_target_pairs={{0,2},{1,3},{2,0},{3,1},{4,6},{5,7},{6,4},{7,5},{8,10},{9,11},{10,... | collective-permute-start | bytes 405512 | tf_op jit(solution)/shard_map/ppermute | solution.py:456
  80.0 4.1 %collective-permute-start.27 = (f32[264,128]{1,0:T(8,128)S(1)}, f32[264,128]{1,0:T(8,128)S(1)}, u32[]{:S(2)}, u32[]{:S(2)}) collective-permute-start(f32[264,128]{1,0:T(8,128)S(1)} %fusion.1), channel_id=1, source_target_pairs={{0,8},{1,9},{2,10},{3,11},{4,12},{5,13},{6,14},{7,15},{8,0},{9,1},... | collective-permute-start | bytes 405512 | tf_op jit(solution)/shard_map/ppermute | solution.py:456
  84.2 4.4 %affine.7.refs_5_ = f32[512,1024]{1,0:T(8,128)S(1)} custom-call(f32[1024,1024]{1,0:T(8,128)S(1)} %get-tuple-element.278.a_ref, f32[1024,1024]{1,0:T(8,128)S(1)} %copy-done.3), custom_call_target="tpu_custom_call" | custom-call | flops 32212254720 | bytes 83886080 | tf_op jit(solution)/shard_map/affine/pallas_call | solution.py:256
  88.6 1.6 %collective-permute-start.26 = (f32[264,128]{1,0:T(8,128)S(1)}, f32[264,128]{1,0:T(8,128)S(1)}, u32[]{:S(2)}, u32[]{:S(2)}) collective-permute-start(f32[264,128]{1,0:T(8,128)S(1)} %fusion.3), channel_id=1, source_target_pairs={{0,8},{1,9},{2,10},{3,11},{4,12},{5,13},{6,14},{7,15},{8,0},{9,1},... | collective-permute-start | bytes 405512 | tf_op jit(solution)/shard_map/ppermute | solution.py:456
  90.2 5.0 %collective-permute-start.33 = (f32[264,128]{1,0:T(8,128)S(1)}, f32[264,128]{1,0:T(8,128)S(1)}, u32[]{:S(2)}, u32[]{:S(2)}) collective-permute-start(f32[264,128]{1,0:T(8,128)S(1)} %add.93), channel_id=1, source_target_pairs={{0,6},{1,7},{2,4},{3,5},{4,2},{5,3},{6,0},{7,1},{8,14},{9,15},{10,... | collective-permute-start | bytes 405512 | tf_op jit(solution)/shard_map/ppermute | solution.py:456
  95.9 1.7 %collective-permute-done.26 = f32[264,128]{1,0:T(8,128)S(1)} collective-permute-done((f32[264,128]{1,0:T(8,128)S(1)}, f32[264,128]{1,0:T(8,128)S(1)}, u32[]{:S(2)}, u32[]{:S(2)}) %collective-permute-start.26) | collective-permute-done | bytes 135200 | tf_op jit(solution)/shard_map/ppermute | solution.py:456
  97.6 1.3 %collective-permute-start.30 = (f32[264,128]{1,0:T(8,128)S(1)}, f32[264,128]{1,0:T(8,128)S(1)}, u32[]{:S(2)}, u32[]{:S(2)}) collective-permute-start(f32[264,128]{1,0:T(8,128)S(1)} %add.92), channel_id=1, source_target_pairs={{0,6},{1,7},{2,4},{3,5},{4,2},{5,3},{6,0},{7,1},{8,14},{9,15},{10,... | collective-permute-start | bytes 405512 | tf_op jit(solution)/shard_map/ppermute | solution.py:456
  98.9 1.4 %collective-permute-start.29 = (f32[264,128]{1,0:T(8,128)S(1)}, f32[264,128]{1,0:T(8,128)S(1)}, u32[]{:S(2)}, u32[]{:S(2)}) collective-permute-start(f32[264,128]{1,0:T(8,128)S(1)} %add.92), channel_id=1, source_target_pairs={{0,4},{1,5},{2,6},{3,7},{4,0},{5,1},{6,2},{7,3},{8,12},{9,13},{10,... | collective-permute-start | bytes 405512 | tf_op jit(solution)/shard_map/ppermute | solution.py:456
  101.7 1.6 %collective-permute-done.31 = f32[264,128]{1,0:T(8,128)S(1)} collective-permute-done((f32[264,128]{1,0:T(8,128)S(1)}, f32[264,128]{1,0:T(8,128)S(1)}, u32[]{:S(2)}, u32[]{:S(2)}) %collective-permute-start.31) | collective-permute-done | bytes 135200 | tf_op jit(solution)/shard_map/ppermute | solution.py:456
  103.8 1.5 %collective-permute-done.34.refs_1_ = f32[1056,128]{1,0:T(8,128)S(1)} collective-permute-done((f32[1056,128]{1,0:T(8,128)S(1)}, f32[1056,128]{1,0:T(8,128)S(1)}, u32[]{:S(2)}, u32[]{:S(2)}) %collective-permute-start.34) | collective-permute-done | bytes 540704 | tf_op jit(solution)/shard_map/ppermute | solution.py:456
  105.3 3.8 %partial_apply.1.refs_4_ = f32[1024,1024]{1,0:T(8,128)S(1)} custom-call(s32[1]{0:T(128)} %bitcast.me_ref, f32[1056,128]{1,0:T(8,128)S(1)} %pad_maximum_fusion.2.refs_0_, f32[1056,128]{1,0:T(8,128)S(1)} %collective-permute-done.34.refs_1_, bf16[1024,1024]{1,0:T(8,128)(2,1)S(1)} %cut.4.refs_2_, bf16[1024,1024]{1,0:T(8,128)(2,1)S(1)} %cut.5.refs_3_, ...), custom_call_target="tpu_custom_call" | custom-call | flops 32212254720 | bytes 125829120 | tf_op jit(solution)/shard_map/partial_apply/pallas_call | solution.py:308
  109.4 1.8 %collective-permute-done.35.refs_1_ = f32[1056,128]{1,0:T(8,128)S(1)} collective-permute-done((f32[1056,128]{1,0:T(8,128)S(1)}, f32[1056,128]{1,0:T(8,128)S(1)}, u32[]{:S(2)}, u32[]{:S(2)}) %collective-permute-start.35) | collective-permute-done | bytes 540704 | tf_op jit(solution)/shard_map/ppermute | solution.py:456
  111.2 5.1 %last.1 = f32[1024,1024]{1,0:T(8,128)} custom-call(s32[1]{0:T(128)} %bitcast.me_ref, f32[1056,128]{1,0:T(8,128)S(1)} %pad_maximum_fusion.3.refs_0_, f32[1056,128]{1,0:T(8,128)S(1)} %collective-permute-done.35.refs_1_, bf16[1024,1024]{1,0:T(8,128)(2,1)S(1)} %cut.4.refs_2_, bf16[1024,1024]{1,0:T(8,128)(2,1)S(1)} %cut.5.refs_3_, ...), custom_call_target="tpu_custom_call" | custom-call | flops 32212254720 | bytes 125829120 | tf_op jit(solution)/shard_map/last/pallas_call | solution.py:433
  (87 shorter events, 14.2 us)
Async XLA Ops:
  6.9 4.2 %collective-permute-start = (f32[1056,128]{1,0:T(8,128)S(1)}, f32[1056,128]{1,0:T(8,128)S(1)}, u32[]{:S(2)}, u32[]{:S(2)}) collective-permute-start(f32[1056,128]{1,0:T(8,128)S(1)} %get-tuple-element.162), channel_id=1, source_target_pairs={{0,1},{1,0},{2,3},{3,2},{4,5},{5,4},{6,7},{7,6},{8,9},{9,8},{10,11... | collective-permute-start | bytes 1622024 | tf_op jit(solution)/shard_map/ppermute | solution.py:456
  11.2 13.4 %collective-permute-start.7 = (f32[264,128]{1,0:T(8,128)S(1)}, f32[264,128]{1,0:T(8,128)S(1)}, u32[]{:S(2)}, u32[]{:S(2)}) collective-permute-start(f32[264,128]{1,0:T(8,128)S(1)} %get-tuple-element.325), channel_id=1, source_target_pairs={{0,6},{1,7},{2,4},{3,5},{4,2},{5,3},{6,0},{7,1},{8,14},{9,15},{10,... | collective-permute-start | bytes 405512 | tf_op jit(solution)/shard_map/ppermute | solution.py:456
  14.8 10.0 %collective-permute-start.6 = (f32[264,128]{1,0:T(8,128)S(1)}, f32[264,128]{1,0:T(8,128)S(1)}, u32[]{:S(2)}, u32[]{:S(2)}) collective-permute-start(f32[264,128]{1,0:T(8,128)S(1)} %get-tuple-element.326), channel_id=1, source_target_pairs={{0,4},{1,5},{2,6},{3,7},{4,0},{5,1},{6,2},{7,3},{8,12},{9,13},{10,... | collective-permute-start | bytes 405512 | tf_op jit(solution)/shard_map/ppermute | solution.py:456
  15.3 9.6 %collective-permute-start.5 = (f32[264,128]{1,0:T(8,128)S(1)}, f32[264,128]{1,0:T(8,128)S(1)}, u32[]{:S(2)}, u32[]{:S(2)}) collective-permute-start(f32[264,128]{1,0:T(8,128)S(1)} %get-tuple-element.327), channel_id=1, source_target_pairs={{0,2},{1,3},{2,0},{3,1},{4,6},{5,7},{6,4},{7,5},{8,10},{9,11},{10,... | collective-permute-start | bytes 405512 | tf_op jit(solution)/shard_map/ppermute | solution.py:456
  15.5 4.3 %collective-permute-start.1 = (f32[1056,128]{1,0:T(8,128)S(1)}, f32[1056,128]{1,0:T(8,128)S(1)}, u32[]{:S(2)}, u32[]{:S(2)}) collective-permute-start(f32[1056,128]{1,0:T(8,128)S(1)} %get-tuple-element.170), channel_id=1, source_target_pairs={{0,1},{1,0},{2,3},{3,2},{4,5},{5,4},{6,7},{7,6},{8,9},{9,8},{10,11... | collective-permute-start | bytes 1622024 | tf_op jit(solution)/shard_map/ppermute | solution.py:456
  19.9 12.5 %collective-permute-start.4 = (f32[264,128]{1,0:T(8,128)S(1)}, f32[264,128]{1,0:T(8,128)S(1)}, u32[]{:S(2)}, u32[]{:S(2)}) collective-permute-start(f32[264,128]{1,0:T(8,128)S(1)} %get-tuple-element.328), channel_id=1, source_target_pairs={{0,6},{1,7},{2,4},{3,5},{4,2},{5,3},{6,0},{7,1},{8,14},{9,15},{10,... | collective-permute-start | bytes 405512 | tf_op jit(solution)/shard_map/ppermute | solution.py:456
  22.8 10.2 %collective-permute-start.3 = (f32[264,128]{1,0:T(8,128)S(1)}, f32[264,128]{1,0:T(8,128)S(1)}, u32[]{:S(2)}, u32[]{:S(2)}) collective-permute-start(f32[264,128]{1,0:T(8,128)S(1)} %get-tuple-element.329), channel_id=1, source_target_pairs={{0,4},{1,5},{2,6},{3,7},{4,0},{5,1},{6,2},{7,3},{8,12},{9,13},{10,... | collective-permute-start | bytes 405512 | tf_op jit(solution)/shard_map/ppermute | solution.py:456
  24.6 8.4 %collective-permute-start.2 = (f32[264,128]{1,0:T(8,128)S(1)}, f32[264,128]{1,0:T(8,128)S(1)}, u32[]{:S(2)}, u32[]{:S(2)}) collective-permute-start(f32[264,128]{1,0:T(8,128)S(1)} %get-tuple-element.330), channel_id=1, source_target_pairs={{0,2},{1,3},{2,0},{3,1},{4,6},{5,7},{6,4},{7,5},{8,10},{9,11},{10,... | collective-permute-start | bytes 405512 | tf_op jit(solution)/shard_map/ppermute | solution.py:456
  24.9 8.6 %collective-permute-start.9 = (f32[264,128]{1,0:T(8,128)S(1)}, f32[264,128]{1,0:T(8,128)S(1)}, u32[]{:S(2)}, u32[]{:S(2)}) collective-permute-start(f32[264,128]{1,0:T(8,128)S(1)} %fusion.5), channel_id=1, source_target_pairs={{0,8},{1,9},{2,10},{3,11},{4,12},{5,13},{6,14},{7,15},{8,0},{9,1},... | collective-permute-start | bytes 405512 | tf_op jit(solution)/shard_map/ppermute | solution.py:456
  33.1 9.1 %collective-permute-start.8 = (f32[264,128]{1,0:T(8,128)S(1)}, f32[264,128]{1,0:T(8,128)S(1)}, u32[]{:S(2)}, u32[]{:S(2)}) collective-permute-start(f32[264,128]{1,0:T(8,128)S(1)} %fusion.7), channel_id=1, source_target_pairs={{0,8},{1,9},{2,10},{3,11},{4,12},{5,13},{6,14},{7,15},{8,0},{9,1},... | collective-permute-start | bytes 405512 | tf_op jit(solution)/shard_map/ppermute | solution.py:456
  33.5 10.8 %collective-permute-start.15 = (f32[264,128]{1,0:T(8,128)S(1)}, f32[264,128]{1,0:T(8,128)S(1)}, u32[]{:S(2)}, u32[]{:S(2)}) collective-permute-start(f32[264,128]{1,0:T(8,128)S(1)} %add.83), channel_id=1, source_target_pairs={{0,6},{1,7},{2,4},{3,5},{4,2},{5,3},{6,0},{7,1},{8,14},{9,15},{10,... | collective-permute-start | bytes 405512 | tf_op jit(solution)/shard_map/ppermute | solution.py:456
  39.6 6.7 %collective-permute-start.14 = (f32[264,128]{1,0:T(8,128)S(1)}, f32[264,128]{1,0:T(8,128)S(1)}, u32[]{:S(2)}, u32[]{:S(2)}) collective-permute-start(f32[264,128]{1,0:T(8,128)S(1)} %add.83), channel_id=1, source_target_pairs={{0,4},{1,5},{2,6},{3,7},{4,0},{5,1},{6,2},{7,3},{8,12},{9,13},{10,... | collective-permute-start | bytes 405512 | tf_op jit(solution)/shard_map/ppermute | solution.py:456
  39.6 6.7 %collective-permute-start.13 = (f32[264,128]{1,0:T(8,128)S(1)}, f32[264,128]{1,0:T(8,128)S(1)}, u32[]{:S(2)}, u32[]{:S(2)}) collective-permute-start(f32[264,128]{1,0:T(8,128)S(1)} %add.83), channel_id=1, source_target_pairs={{0,2},{1,3},{2,0},{3,1},{4,6},{5,7},{6,4},{7,5},{8,10},{9,11},{10,... | collective-permute-start | bytes 405512 | tf_op jit(solution)/shard_map/ppermute | solution.py:456
  42.2 11.7 %collective-permute-start.12 = (f32[264,128]{1,0:T(8,128)S(1)}, f32[264,128]{1,0:T(8,128)S(1)}, u32[]{:S(2)}, u32[]{:S(2)}) collective-permute-start(f32[264,128]{1,0:T(8,128)S(1)} %add.82), channel_id=1, source_target_pairs={{0,6},{1,7},{2,4},{3,5},{4,2},{5,3},{6,0},{7,1},{8,14},{9,15},{10,... | collective-permute-start | bytes 405512 | tf_op jit(solution)/shard_map/ppermute | solution.py:456
  43.2 10.7 %collective-permute-start.11 = (f32[264,128]{1,0:T(8,128)S(1)}, f32[264,128]{1,0:T(8,128)S(1)}, u32[]{:S(2)}, u32[]{:S(2)}) collective-permute-start(f32[264,128]{1,0:T(8,128)S(1)} %add.82), channel_id=1, source_target_pairs={{0,4},{1,5},{2,6},{3,7},{4,0},{5,1},{6,2},{7,3},{8,12},{9,13},{10,... | collective-permute-start | bytes 405512 | tf_op jit(solution)/shard_map/ppermute | solution.py:456
  44.3 9.5 %collective-permute-start.10 = (f32[264,128]{1,0:T(8,128)S(1)}, f32[264,128]{1,0:T(8,128)S(1)}, u32[]{:S(2)}, u32[]{:S(2)}) collective-permute-start(f32[264,128]{1,0:T(8,128)S(1)} %add.82), channel_id=1, source_target_pairs={{0,2},{1,3},{2,0},{3,1},{4,6},{5,7},{6,4},{7,5},{8,10},{9,11},{10,... | collective-permute-start | bytes 405512 | tf_op jit(solution)/shard_map/ppermute | solution.py:456
  61.8 4.1 %collective-permute-start.18 = (f32[1056,128]{1,0:T(8,128)S(1)}, f32[1056,128]{1,0:T(8,128)S(1)}, u32[]{:S(2)}, u32[]{:S(2)}) collective-permute-start(f32[1056,128]{1,0:T(8,128)S(1)} %get-tuple-element.256), channel_id=1, source_target_pairs={{0,1},{1,0},{2,3},{3,2},{4,5},{5,4},{6,7},{7,6},{8,9},{9,8},{10,11... | collective-permute-start | bytes 1622024 | tf_op jit(solution)/shard_map/ppermute | solution.py:456
  66.0 12.5 %collective-permute-start.25 = (f32[264,128]{1,0:T(8,128)S(1)}, f32[264,128]{1,0:T(8,128)S(1)}, u32[]{:S(2)}, u32[]{:S(2)}) collective-permute-start(f32[264,128]{1,0:T(8,128)S(1)} %get-tuple-element.319), channel_id=1, source_target_pairs={{0,6},{1,7},{2,4},{3,5},{4,2},{5,3},{6,0},{7,1},{8,14},{9,15},{10,... | collective-permute-start | bytes 405512 | tf_op jit(solution)/shard_map/ppermute | solution.py:456
  69.2 10.8 %collective-permute-start.24 = (f32[264,128]{1,0:T(8,128)S(1)}, f32[264,128]{1,0:T(8,128)S(1)}, u32[]{:S(2)}, u32[]{:S(2)}) collective-permute-start(f32[264,128]{1,0:T(8,128)S(1)} %get-tuple-element.320), channel_id=1, source_target_pairs={{0,4},{1,5},{2,6},{3,7},{4,0},{5,1},{6,2},{7,3},{8,12},{9,13},{10,... | collective-permute-start | bytes 405512 | tf_op jit(solution)/shard_map/ppermute | solution.py:456
  70.3 9.7 %collective-permute-start.23 = (f32[264,128]{1,0:T(8,128)S(1)}, f32[264,128]{1,0:T(8,128)S(1)}, u32[]{:S(2)}, u32[]{:S(2)}) collective-permute-start(f32[264,128]{1,0:T(8,128)S(1)} %get-tuple-element.321), channel_id=1, source_target_pairs={{0,2},{1,3},{2,0},{3,1},{4,6},{5,7},{6,4},{7,5},{8,10},{9,11},{10,... | collective-permute-start | bytes 405512 | tf_op jit(solution)/shard_map/ppermute | solution.py:456
  71.6 4.4 %collective-permute-start.19 = (f32[1056,128]{1,0:T(8,128)S(1)}, f32[1056,128]{1,0:T(8,128)S(1)}, u32[]{:S(2)}, u32[]{:S(2)}) collective-permute-start(f32[1056,128]{1,0:T(8,128)S(1)} %get-tuple-element.265), channel_id=1, source_target_pairs={{0,1},{1,0},{2,3},{3,2},{4,5},{5,4},{6,7},{7,6},{8,9},{9,8},{10,11... | collective-permute-start | bytes 1622024 | tf_op jit(solution)/shard_map/ppermute | solution.py:456
  76.1 12.4 %collective-permute-start.22 = (f32[264,128]{1,0:T(8,128)S(1)}, f32[264,128]{1,0:T(8,128)S(1)}, u32[]{:S(2)}, u32[]{:S(2)}) collective-permute-start(f32[264,128]{1,0:T(8,128)S(1)} %get-tuple-element.322), channel_id=1, source_target_pairs={{0,6},{1,7},{2,4},{3,5},{4,2},{5,3},{6,0},{7,1},{8,14},{9,15},{10,... | collective-permute-start | bytes 405512 | tf_op jit(solution)/shard_map/ppermute | solution.py:456
  77.7 10.9 %collective-permute-start.21 = (f32[264,128]{1,0:T(8,128)S(1)}, f32[264,128]{1,0:T(8,128)S(1)}, u32[]{:S(2)}, u32[]{:S(2)}) collective-permute-start(f32[264,128]{1,0:T(8,128)S(1)} %get-tuple-element.323), channel_id=1, source_target_pairs={{0,4},{1,5},{2,6},{3,7},{4,0},{5,1},{6,2},{7,3},{8,12},{9,13},{10,... | collective-permute-start | bytes 405512 | tf_op jit(solution)/shard_map/ppermute | solution.py:456
  78.5 10.0 %collective-permute-start.20 = (f32[264,128]{1,0:T(8,128)S(1)}, f32[264,128]{1,0:T(8,128)S(1)}, u32[]{:S(2)}, u32[]{:S(2)}) collective-permute-start(f32[264,128]{1,0:T(8,128)S(1)} %get-tuple-element.324), channel_id=1, source_target_pairs={{0,2},{1,3},{2,0},{3,1},{4,6},{5,7},{6,4},{7,5},{8,10},{9,11},{10,... | collective-permute-start | bytes 405512 | tf_op jit(solution)/shard_map/ppermute | solution.py:456
  80.0 10.2 %collective-permute-start.27 = (f32[264,128]{1,0:T(8,128)S(1)}, f32[264,128]{1,0:T(8,128)S(1)}, u32[]{:S(2)}, u32[]{:S(2)}) collective-permute-start(f32[264,128]{1,0:T(8,128)S(1)} %fusion.1), channel_id=1, source_target_pairs={{0,8},{1,9},{2,10},{3,11},{4,12},{5,13},{6,14},{7,15},{8,0},{9,1},... | collective-permute-start | bytes 405512 | tf_op jit(solution)/shard_map/ppermute | solution.py:456
  88.6 9.0 %collective-permute-start.26 = (f32[264,128]{1,0:T(8,128)S(1)}, f32[264,128]{1,0:T(8,128)S(1)}, u32[]{:S(2)}, u32[]{:S(2)}) collective-permute-start(f32[264,128]{1,0:T(8,128)S(1)} %fusion.3), channel_id=1, source_target_pairs={{0,8},{1,9},{2,10},{3,11},{4,12},{5,13},{6,14},{7,15},{8,0},{9,1},... | collective-permute-start | bytes 405512 | tf_op jit(solution)/shard_map/ppermute | solution.py:456
  90.2 10.1 %collective-permute-start.33 = (f32[264,128]{1,0:T(8,128)S(1)}, f32[264,128]{1,0:T(8,128)S(1)}, u32[]{:S(2)}, u32[]{:S(2)}) collective-permute-start(f32[264,128]{1,0:T(8,128)S(1)} %add.93), channel_id=1, source_target_pairs={{0,6},{1,7},{2,4},{3,5},{4,2},{5,3},{6,0},{7,1},{8,14},{9,15},{10,... | collective-permute-start | bytes 405512 | tf_op jit(solution)/shard_map/ppermute | solution.py:456
  95.2 6.5 %collective-permute-start.32 = (f32[264,128]{1,0:T(8,128)S(1)}, f32[264,128]{1,0:T(8,128)S(1)}, u32[]{:S(2)}, u32[]{:S(2)}) collective-permute-start(f32[264,128]{1,0:T(8,128)S(1)} %add.93), channel_id=1, source_target_pairs={{0,4},{1,5},{2,6},{3,7},{4,0},{5,1},{6,2},{7,3},{8,12},{9,13},{10,... | collective-permute-start | bytes 405512 | tf_op jit(solution)/shard_map/ppermute | solution.py:456
  95.2 8.1 %collective-permute-start.31 = (f32[264,128]{1,0:T(8,128)S(1)}, f32[264,128]{1,0:T(8,128)S(1)}, u32[]{:S(2)}, u32[]{:S(2)}) collective-permute-start(f32[264,128]{1,0:T(8,128)S(1)} %add.93), channel_id=1, source_target_pairs={{0,2},{1,3},{2,0},{3,1},{4,6},{5,7},{6,4},{7,5},{8,10},{9,11},{10,... | collective-permute-start | bytes 405512 | tf_op jit(solution)/shard_map/ppermute | solution.py:456
  97.6 11.5 %collective-permute-start.30 = (f32[264,128]{1,0:T(8,128)S(1)}, f32[264,128]{1,0:T(8,128)S(1)}, u32[]{:S(2)}, u32[]{:S(2)}) collective-permute-start(f32[264,128]{1,0:T(8,128)S(1)} %add.92), channel_id=1, source_target_pairs={{0,6},{1,7},{2,4},{3,5},{4,2},{5,3},{6,0},{7,1},{8,14},{9,15},{10,... | collective-permute-start | bytes 405512 | tf_op jit(solution)/shard_map/ppermute | solution.py:456
  98.9 10.2 %collective-permute-start.29 = (f32[264,128]{1,0:T(8,128)S(1)}, f32[264,128]{1,0:T(8,128)S(1)}, u32[]{:S(2)}, u32[]{:S(2)}) collective-permute-start(f32[264,128]{1,0:T(8,128)S(1)} %add.92), channel_id=1, source_target_pairs={{0,4},{1,5},{2,6},{3,7},{4,0},{5,1},{6,2},{7,3},{8,12},{9,13},{10,... | collective-permute-start | bytes 405512 | tf_op jit(solution)/shard_map/ppermute | solution.py:456
  100.3 8.8 %collective-permute-start.28 = (f32[264,128]{1,0:T(8,128)S(1)}, f32[264,128]{1,0:T(8,128)S(1)}, u32[]{:S(2)}, u32[]{:S(2)}) collective-permute-start(f32[264,128]{1,0:T(8,128)S(1)} %add.92), channel_id=1, source_target_pairs={{0,2},{1,3},{2,0},{3,1},{4,6},{5,7},{6,4},{7,5},{8,10},{9,11},{10,... | collective-permute-start | bytes 405512 | tf_op jit(solution)/shard_map/ppermute | solution.py:456
  (10 other events, 66.8 us)

commit v6 on v5

--- a/solution.py
+++ b/solution.py
@@ -250,19 +250,36 @@
     tiles(out_ref.shape[1], 256, step)
 
 
-def affine(a, b, part, parts):
+def affine(a, b, half):
     rows, size = a.shape
-    height = rows // parts
-    return call(
-        affine_kernel, "affine", struct(height, size), 18, 1 / parts, 2,
+    block = lambda at: pl.BlockSpec((rows // 2, size), lambda r: (at, 0))
+    return call(
+        affine_kernel, "affine", struct(rows // 2, size), 18, 0.5, 2,
         grid=(1,),
-        in_specs=[
-            pl.BlockSpec((height, size), lambda r: (part, 0)),
-            pl.BlockSpec((size, size), lambda r: (0, 0)),
-        ],
-        out_specs=pl.BlockSpec((height, size), lambda r: (0, 0)),
-        scratch_shapes=[pltpu.VMEM((height, size), BF16)] * 2,
+        in_specs=[block(half), pl.BlockSpec((size, size), lambda r: (0, 0))],
+        out_specs=block(0),
+        scratch_shapes=[pltpu.VMEM((rows // 2, size), BF16)] * 2,
     )(a, b)
+
+
+def affine_parts_kernel(a_ref, ah, al, bh, bl, out_ref):
+    def step(c):
+        product = mm((ah[...], al[...]), (bh[:, c], bl[:, c]))
+        out_ref[:, c] = 1.5 * a_ref[:, c] - 0.5 * product
+
+    tiles(out_ref.shape[1], 256, step)
+
+
+def affine_parts(a, ah, al, bh, bl, half):
+    rows, size = a.shape
+    block = lambda at: pl.BlockSpec((rows // 2, size), lambda r: (at, 0))
+    whole = pl.BlockSpec((size, size), lambda r: (0, 0))
+    return call(
+        affine_parts_kernel, "affine_parts", struct(rows // 2, size), 18, 0.5, 2,
+        grid=(1,),
+        in_specs=[block(half)] * 3 + [whole] * 2,
+        out_specs=block(0),
+    )(a, ah, al, bh, bl)
 
 
 SPANS = (
@@ -282,13 +299,15 @@
     )
 
 
-def apply_first(base_refs, out_ref, ah, al, hi, lo):
-    for column in range(4):
+def apply_first(base_refs, out_ref, ah, al, hi, lo, columns):
+    q = hi.shape[0] // 4
+    for column in columns:
         c, product = sym_product(ah, al, hi, lo, 0, column)
+        out = slice(c.start - columns[0] * q, c.stop - columns[0] * q)
         at = 0
         for base_ref in base_refs:
             end = at + base_ref.shape[0]
-            out_ref[at:end, c] = base_ref[:, c] - 0.5 * product[at:end]
+            out_ref[at:end, out] = base_ref[:, c] - 0.5 * product[at:end]
             at = end
 
 
@@ -296,26 +315,60 @@
     return [pltpu.VMEM((size, size), BF16)] * 2 + [packed_scratch(size, shards)]
 
 
-def partial_kernel(shards, count, me_ref, *refs):
+def first_part_kernel(shards, count, columns, me_ref, *refs):
     pieces, refs = refs[:count], refs[count:]
     ah, al, base_refs, (out_ref, hi, lo, packed) = refs[0], refs[1], refs[2:-4], refs[-4:]
     unpack(pieces, packed, hi, lo, me_ref[0], shards, 0)
-    apply_first(base_refs, out_ref, ah, al, hi, lo)
-
-
-def partial_apply(me, shards, pieces, ah, al, base):
+    apply_first(base_refs, out_ref, ah, al, hi, lo, columns)
+
+
+def first_part(me, shards, pieces, ah, al, base, columns):
     rows, size = ah.shape
-    return call(
-        functools.partial(partial_kernel, shards, len(pieces)), "partial_apply",
-        struct(rows, size), 18, 0.5, 3,
+    part = struct(size, size, dtype=BF16)
+    more = len(columns) < 4
+    scratch = sym_scratch(size, shards)
+    return call(
+        functools.partial(first_part_kernel, shards, len(pieces), columns), "first_part",
+        [struct(rows, len(columns) * size // 4)] + [part, part] * more, 18, 0.5, 3,
         in_specs=[SMEM] + [VMEM] * (len(pieces) + 2 + len(base)),
+        out_specs=[VMEM] * (1 + 2 * more),
+        scratch_shapes=scratch[2 * more:],
+    )(me, *pieces, ah, al, *base)
+
+
+def other_part_kernel(columns, ah, al, hi, lo, *refs):
+    apply_first(refs[:-1], refs[-1], ah, al, hi, lo, columns)
+
+
+def other_part(ah, al, hi, lo, base, columns):
+    rows, size = ah.shape
+    return call(
+        functools.partial(other_part_kernel, columns), "other_part",
+        struct(rows, len(columns) * size // 4), 16, 0.25, 3,
+        in_specs=[VMEM] * (4 + len(base)),
         out_specs=VMEM,
-        scratch_shapes=sym_scratch(size, shards),
-    )(me, *pieces, ah, al, *base)
+    )(ah, al, hi, lo, *base)
+
+
+def column_kernel(xh, xl, mid_ref, col_ref):
+    col_ref[...] = mm((xh[...], xl[...]), split(mid_ref[...]))
+
+
+def column_product(xh, xl, mid):
+    size, rows = xh.shape
+    block = pl.BlockSpec((rows, size // 4), lambda r: (0, 0))
+    whole = pl.BlockSpec((size, rows), lambda r: (0, 0))
+    return call(
+        column_kernel, "column_product", struct(size, size // 4), 16, 0.25, 2,
+        grid=(1,), in_specs=[whole, whole, block], out_specs=block,
+    )(xh, xl, mid)
 
 
 def turn_kernel(x_ref, xh, xl):
-    xh[...], xl[...] = split(x_ref[...].T)
+    def step(r):
+        xh[:, r], xl[:, r] = split(x_ref[r].T)
+
+    tiles(x_ref.shape[0], 256, step)
 
 
 def turn(x):
@@ -326,9 +379,12 @@
 
 
 def cut_kernel(which, x_ref, *out_refs):
-    parts = split(x_ref[...])
-    for out_ref, k in zip(out_refs, which):
-        out_ref[...] = parts[k]
+    def step(r):
+        parts = split(x_ref[r])
+        for out_ref, k in zip(out_refs, which):
+            out_ref[r] = parts[k]
+
+    tiles(x_ref.shape[0], 128, step)
 
 
 def cut(x, *which):
@@ -337,26 +393,6 @@
         functools.partial(cut_kernel, which), "cut", [struct(*x.shape, dtype=BF16)] * count,
         16, 0.1, 2, in_specs=[VMEM], out_specs=[VMEM] * count,
     )(x)
-
-
-def early_kernel(shards, count, me_ref, *refs):
-    pieces, refs = refs[:count], refs[count:]
-    ah, al, base_refs, refs = refs[0], refs[1], refs[2:-7], refs[-7:]
-    xh, xl, out_ref, col_ref, hi, lo, packed = refs
-    unpack(pieces, packed, hi, lo, me_ref[0], shards, 0)
-    apply_first(base_refs, out_ref, ah, al, hi, lo)
-    col_ref[...] = mm((xh[...], xl[...]), split(out_ref[:, :col_ref.shape[1]]))
-
-
-def early_middle(me, shards, pieces, ah, al, base, xh, xl):
-    rows, size = ah.shape
-    return call(
-        functools.partial(early_kernel, shards, len(pieces)), "early_middle",
-        [struct(rows, size), struct(size, size // 4)], 20, 0.75, 5,
-        in_specs=[SMEM] + [VMEM] * (len(pieces) + 4 + len(base)),
-        out_specs=[VMEM] * 2,
-        scratch_shapes=sym_scratch(size, shards),
-    )(me, *pieces, ah, al, *base, xh, xl)
 
 
 def second_gram_kernel(shards, count, me_ref, *refs):
@@ -367,21 +403,21 @@
     q = size // 4
     unpack(pieces, packed, hi, lo, me_ref[0], shards, 1)
     mid_ref[:, :q] = base_ref[:, :q]
+    mh[:, :q], ml[:, :q] = split(base_ref[:, :q])
     for column in range(1, 4):
         c, product = sym_product(ah, al, hi, lo, 1, column)
         mid = base_ref[:, c] - 0.5 * product
         mid_ref[:, c] = mid
-        c = slice(c.start - q, c.stop - q)
         mh[:, c], ml[:, c] = split(mid)
     g[:, :q] = col_ref[...]
-    g[:q, q:] = mm((xh[:q, :], xl[:q, :]), (mh[...], ml[...]))
-    g[3 * q:, 3 * q:] = mm((xh[3 * q:, :], xl[3 * q:, :]), (mh[:, 2 * q:], ml[:, 2 * q:]))
+    g[:q, q:] = mm((xh[:q, :], xl[:q, :]), (mh[:, q:], ml[:, q:]))
+    g[3 * q:, 3 * q:] = mm((xh[3 * q:, :], xl[3 * q:, :]), (mh[:, 3 * q:], ml[:, 3 * q:]))
     pack(g, packed, keep_ref, send_ref, me_ref[0], shards, 0)
 
 
 def second_gram(me, shards, pieces, ah, al, base, xh, xl, col):
     rows, size = ah.shape
-    part = struct(rows, size - size // 4, dtype=BF16)
+    part = struct(rows, size, dtype=BF16)
     return call(
         functools.partial(second_gram_kernel, shards, len(pieces)), "second_gram",
         halves(size, shards) + [struct(rows, size), part, part], 20, 0.8, 5,
@@ -392,7 +428,8 @@
 
 
 def fourth_gram_kernel(shards, me_ref, xh, xl, mh, ml, keep_ref, send_ref, g, packed):
-    lower_product(g, xh, xl, mh[...], ml[...])
+    q = g.shape[0] // 4
+    lower_product(g, xh, xl, mh[:, q:], ml[:, q:])
     pack(g, packed, keep_ref, send_ref, me_ref[0], shards, 1)
 
 
@@ -408,13 +445,13 @@
 
 def last_kernel(shards, count, me_ref, *refs):
     pieces = refs[:count]
-    ah, al, z_ref, out_hbm, hi, lo, packed, out, sems = refs[count:]
+    ah, al, z_ref, rest_ref, out_hbm, hi, lo, packed, out, sems = refs[count:]
     q = hi.shape[0] // 4
     copies = []
 
     def send(src, column):
         c = slice(column * q, (column + 1) * q)
-        copy = pltpu.make_async_copy(src.at[:, c], out_hbm.at[:, c], sems.at[column])
+        copy = pltpu.make_async_copy(src, out_hbm.at[:, c], sems.at[column])
         copy.start()
         copies.append(copy)
 
@@ -422,21 +459,21 @@
     unpack(pieces, packed, hi, lo, me_ref[0], shards, 1)
     for column in (1, 2, 3):
         c, product = sym_product(ah, al, hi, lo, 1, column)
-        out[:, c] = z_ref[:, c] - 0.5 * product
-        send(out, column)
+        out[:, c] = rest_ref[:, c.start - q:c.stop - q] - 0.5 * product
+        send(out.at[:, c], column)
     for copy in copies:
         copy.wait()
 
 
-def last_step(me, shards, pieces, ah, al, z):
-    rows, size = z.shape
+def last_step(me, shards, pieces, ah, al, z, rest):
+    rows, size = ah.shape
     return call(
         functools.partial(last_kernel, shards, len(pieces)), "last", struct(rows, size), 22, 0.5, 3,
-        in_specs=[SMEM] + [VMEM] * (len(pieces) + 3),
+        in_specs=[SMEM] + [VMEM] * (len(pieces) + 4),
         out_specs=pl.BlockSpec(memory_space=pltpu.HBM),
         scratch_shapes=sym_scratch(size, shards)
         + [pltpu.VMEM((rows, size), F32), pltpu.SemaphoreType.DMA((4,))],
-    )(me, *pieces, ah, al, z)
+    )(me, *pieces, ah, al, z, rest)
 
 
 CORE = 1
@@ -521,8 +558,10 @@
     got_a = a.gather_core(close(env, *got_a))
     work()
     (got_a,) = close(env, got_a)
-    late(env, [a.mine, got_a])
+    late[0](env, [a.mine, got_a])
     got_b = b.gather_core(close(env, *got_b))
+    late[1](env)
+    (got_b,) = close(env, got_b)
     return [b.mine, got_b]
 
 
@@ -532,47 +571,65 @@
         x0=orbitals_zero, x1=orbitals_one, s0=correlation_zero, s1=correlation_one, c=cotangent
     )
 
-    def half(name, left, right, part):
+    def half(part):
         def work(env):
-            env[f"{name}{part}"] = affine(env[left], env[right], part, 2)
+            env[f"m{part}"] = affine(env["c"], env["s1"], part)
         return work
 
     def turned(env):
         env["xh"], env["xl"] = turn(env["x0"])
 
-    def cut_one(env):
+    def cut_two(env):
         env["x1h"], env["x1l"] = cut(env["x1"], 0, 1)
-
-    def high(env):
-        (env["x0h"],) = cut(env["x0"], 0)
-
-    def low(env):
-        (env["x0l"],) = cut(env["x0"], 1)
-
-    def early(env, pieces):
-        env["mid"], env["col"] = early_middle(
-            me, SHARDS, pieces, env["x1h"], env["x1l"], [env["m0"], env["m1"]], env["xh"], env["xl"]
+        env["s0h"], env["s0l"] = cut(env["s0"], 0, 1)
+
+    def middle(env, pieces):
+        (env["mid"],) = first_part(
+            me, SHARDS, pieces, env["x1h"], env["x1l"], [env["m0"], env["m1"]], (0, 1, 2, 3)
         )
+
+    def column(env):
+        env["col"] = column_product(env["xh"], env["xl"], env["mid"])
 
     keep, send, *parts = first_gram(me, SHARDS, env["x1"], env["c"])
     one = sum_chunks(
         count, env, (keep, send), lambda env: other_gram(me, SHARDS, *parts),
-        [half("m", "c", "s1", 0), turned, half("m", "c", "s1", 1), cut_one], early,
-    )
-
-    keep, send, env["mid"], mh, ml = second_gram(
+        [half(0), turned, half(1), cut_two], [middle, column],
+    )
+
+    keep, send, env["mid"], env["mh"], env["ml"] = second_gram(
         me, SHARDS, one, env["x1h"], env["x1l"], env["mid"], env["xh"], env["xl"], env["col"]
     )
 
-    def late(env, pieces):
-        env["z"] = partial_apply(me, SHARDS, pieces, env["x0h"], env["x0l"], [env["d0"], env["d1"]])
+    def half_parts(part):
+        def work(env):
+            env[f"d{part}"] = affine_parts(
+                env["mid"], env["mh"], env["ml"], env["s0h"], env["s0l"], part
+            )
+        return work
+
+    def high(env):
+        (env["x0h"],) = cut(env["x0"], 0)
+
+    def low(env):
+        (env["x0l"],) = cut(env["x0"], 1)
+
+    def result(env, pieces):
+        env["z"], env["symh"], env["syml"] = first_part(
+            me, SHARDS, pieces, env["x0h"], env["x0l"], [env["d0"], env["d1"]], (0,)
+        )
+
+    def rest(env):
+        env["rest"] = other_part(
+            env["x0h"], env["x0l"], env["symh"], env["syml"], [env["d0"], env["d1"]], (1, 2, 3)
+        )
 
     two = sum_chunks(
         count, env, (keep, send),
-        lambda env: fourth_gram(me, SHARDS, env["xh"], env["xl"], mh, ml),
-        [half("d", "mid", "s0", 0), high, half("d", "mid", "s0", 1), low], late,
-    )
-    return last_step(me, SHARDS, two, env["x0h"], env["x0l"], env["z"])
+        lambda env: fourth_gram(me, SHARDS, env["xh"], env["xl"], env["mh"], env["ml"]),
+        [half_parts(0), high, half_parts(1), low], [result, rest],
+    )
+    return last_step(me, SHARDS, two, env["x0h"], env["x0l"], env["z"], env["rest"])
 
 
 def solution(mesh):

time: 117 us -> 114 us (0.974)
  starting transfers between devices: 47.1 us -> 44.3 us
  waiting for transfers between devices: 13.2 us -> 11.1 us
  local copies, waits for them, and re-layouts: 0.14 us -> 1.48 us
    ppermute x36, starting transfers between devices: 47.1 us -> 44.3 us  [swap(): return lax.ppermute(x, 'row', [(i, i ^ offset) for i in range(self.count)])]
    ppermute x36, waiting for transfers between devices: 13.2 us -> 11.1 us  [swap(): return lax.ppermute(x, 'row', [(i, i ^ offset) for i in range(self.count)])]
    unnamed x12, local copies, waits for them, and re-layouts: 0.02 us -> 1.36 us
    pallas_call x6 -> x8, Pallas kernels: 26.8 us -> 26.3 us  [the longest x2 8.64 us: affine(): call(affine_kernel, 'affine', struct(rows // 2, size), 18, 0.5, 2, grid=(...]
  transfers between devices with their start and end apart: 36 -> 36, of which waited for: 10 -> 11; matrix products, arithmetic and copies ran while one was open for 0% -> 0% of each run, Pallas kernels for 32% -> 33%
where the time goes in v6:
time: 114 us
  Pallas kernels  55.9 us (49%)
  starting transfers between devices  44.3 us (39%)
  waiting for transfers between devices  11.1 us (10%)
  local copies, waits for them, and re-layouts  1.48 us (1%)
    ppermute x36, starting transfers between devices, swap(): return lax.ppermute(x, 'row', [(i, i ^ offset) for i in range(self.count)])  44.3 us
    ppermute x36, waiting for transfers between devices, swap(): return lax.ppermute(x, 'row', [(i, i ^ offset) for i in range(self.count)])  11.1 us
    pallas_call x2, Pallas kernels, affine(): call(affine_kernel, 'affine', struct(rows // 2, size), 18, 0.5, 2, grid=(...  8.64 us
    pallas_call x2, Pallas kernels, affine_parts(): call(affine_parts_kernel, 'affine_parts', struct(rows // 2, size), 18, 0....  8.08 us
    pallas_call x1, Pallas kernels, first_gram(): call(functools.partial(first_gram_kernel, shards), 'first_gram', halves(s...  6.9 us
    pallas_call x1, Pallas kernels, second_gram(): call(functools.partial(second_gram_kernel, shards, len(pieces)), 'second_...  6.18 us
    pallas_call x2, Pallas kernels, first_part(): call(functools.partial(first_part_kernel, shards, len(pieces), columns),...  5.99 us
    pallas_call x1, Pallas kernels, last_step(): call(functools.partial(last_kernel, shards, len(pieces)), 'last', struct(...  5.13 us
  transfers between devices with their start and end apart: 36, of which 11 were waited for; matrix products, arithmetic and copies ran while one was open for 0% of the time, Pallas kernels for 33%

profile of v6, /device:TPU:0, one launch (start us, length us, event | category | flops | bytes accessed | tf_op | source)
XLA Modules:
  0.0 114.0 jit_solution(10398171485554905144)
XLA Ops:
  0.0 6.9 %first_gram.1 = (f32[1056,128]{1,0:T(8,128)S(1)}, f32[1056,128]{1,0:T(8,128)S(1)}, bf16[1024,1024]{1,0:T(8,128)(2,1)S(1)}, bf16[1024,1024]{1,0:T(8,128)(2,1)S(1)...) custom-call(s32[1]{0:T(128)} %bitcast.me_ref, f32[1024,1024]{1,0:T(8,128)} %x_ref.1, f32[1024,1024]{1,0:T(8,128)} %a_ref.1), custom_call_target="tpu_custom_call" | custom-call | flops 32212254720 | bytes 167772160 | tf_op jit(solution)/shard_map/first_gram/pallas_call | solution.py:198
  7.4 3.6 %other_gram.1 = (f32[1056,128]{1,0:T(8,128)S(1)}, f32[1056,128]{1,0:T(8,128)S(1)}) custom-call(s32[1]{0:T(128)} %bitcast.me_ref, bf16[1024,1024]{1,0:T(8,128)(2,1)S(1)} %get-tuple-element.199.ah, bf16[1024,1024]{1,0:T(8,128)(2,1)S(1)} %get-tuple-element.200.al, bf16[1024,1024]{1,0:T(8,128)(2,1)S(1)} %get-tuple-element.201.bh, ...), custom_call_target="tpu_custom_call" | custom-call | flops 32212254720 | bytes 83886080 | tf_op jit(solution)/shard_map/other_gram/pallas_call | solution.py:228
  11.2 3.6 %collective-permute-start.7 = (f32[264,128]{1,0:T(8,128)S(1)}, f32[264,128]{1,0:T(8,128)S(1)}, u32[]{:S(2)}, u32[]{:S(2)}) collective-permute-start(f32[264,128]{1,0:T(8,128)S(1)} %get-tuple-element.397), channel_id=1, source_target_pairs={{0,6},{1,7},{2,4},{3,5},{4,2},{5,3},{6,0},{7,1},{8,14},{9,15},{10,... | collective-permute-start | bytes 405512 | tf_op jit(solution)/shard_map/ppermute | solution.py:493
  15.5 4.3 %affine.2.refs_4_ = f32[512,1024]{1,0:T(8,128)S(1)} custom-call(f32[1024,1024]{1,0:T(8,128)S(1)} %copy-done, f32[1024,1024]{1,0:T(8,128)S(1)} %copy-done.1), custom_call_target="tpu_custom_call" | custom-call | flops 32212254720 | bytes 83886080 | tf_op jit(solution)/shard_map/affine/pallas_call | solution.py:256
  19.9 2.9 %collective-permute-start.4 = (f32[264,128]{1,0:T(8,128)S(1)}, f32[264,128]{1,0:T(8,128)S(1)}, u32[]{:S(2)}, u32[]{:S(2)}) collective-permute-start(f32[264,128]{1,0:T(8,128)S(1)} %get-tuple-element.400), channel_id=1, source_target_pairs={{0,6},{1,7},{2,4},{3,5},{4,2},{5,3},{6,0},{7,1},{8,14},{9,15},{10,... | collective-permute-start | bytes 405512 | tf_op jit(solution)/shard_map/ppermute | solution.py:493
  23.3 1.5 %turn.1 = (bf16[1024,1024]{1,0:T(8,128)(2,1)S(1)}, bf16[1024,1024]{1,0:T(8,128)(2,1)S(1)}) custom-call(f32[1024,1024]{1,0:T(8,128)S(1)} %copy-done.4), custom_call_target="tpu_custom_call" | custom-call | flops 6442450944 | bytes 83886080 | tf_op jit(solution)/shard_map/turn/pallas_call | solution.py:376
  25.1 3.0 %collective-permute-start.9 = (f32[264,128]{1,0:T(8,128)S(1)}, f32[264,128]{1,0:T(8,128)S(1)}, u32[]{:S(2)}, u32[]{:S(2)}) collective-permute-start(f32[264,128]{1,0:T(8,128)S(1)} %fusion.5), channel_id=1, source_target_pairs={{0,8},{1,9},{2,10},{3,11},{4,12},{5,13},{6,14},{7,15},{8,0},{9,1},... | collective-permute-start | bytes 405512 | tf_op jit(solution)/shard_map/ppermute | solution.py:493
  28.1 4.3 %affine.3.refs_5_ = f32[512,1024]{1,0:T(8,128)S(1)} custom-call(f32[1024,1024]{1,0:T(8,128)S(1)} %copy-done, f32[1024,1024]{1,0:T(8,128)S(1)} %copy-done.1), custom_call_target="tpu_custom_call" | custom-call | flops 32212254720 | bytes 83886080 | tf_op jit(solution)/shard_map/affine/pallas_call | solution.py:256
  33.3 6.3 %collective-permute-start.15 = (f32[264,128]{1,0:T(8,128)S(1)}, f32[264,128]{1,0:T(8,128)S(1)}, u32[]{:S(2)}, u32[]{:S(2)}) collective-permute-start(f32[264,128]{1,0:T(8,128)S(1)} %add.83), channel_id=1, source_target_pairs={{0,6},{1,7},{2,4},{3,5},{4,2},{5,3},{6,0},{7,1},{8,14},{9,15},{10,... | collective-permute-start | bytes 405512 | tf_op jit(solution)/shard_map/ppermute | solution.py:493
  40.2 2.0 %collective-permute-done.8 = f32[264,128]{1,0:T(8,128)S(1)} collective-permute-done((f32[264,128]{1,0:T(8,128)S(1)}, f32[264,128]{1,0:T(8,128)S(1)}, u32[]{:S(2)}, u32[]{:S(2)}) %collective-permute-start.8) | collective-permute-done | bytes 135200 | tf_op jit(solution)/shard_map/ppermute | solution.py:493
  43.2 1.2 %collective-permute-start.11 = (f32[264,128]{1,0:T(8,128)S(1)}, f32[264,128]{1,0:T(8,128)S(1)}, u32[]{:S(2)}, u32[]{:S(2)}) collective-permute-start(f32[264,128]{1,0:T(8,128)S(1)} %add.82), channel_id=1, source_target_pairs={{0,4},{1,5},{2,6},{3,7},{4,0},{5,1},{6,2},{7,3},{8,12},{9,13},{10,... | collective-permute-start | bytes 405512 | tf_op jit(solution)/shard_map/ppermute | solution.py:493
  45.8 1.0 collective-permute-done.14
  47.7 1.3 %copy-done.3 = f32[1024,1024]{1,0:T(8,128)S(1)} copy-done((f32[1024,1024]{1,0:T(8,128)S(1)}, f32[1024,1024]{1,0:T(8,128)}, u32[]{:S(2)}) %copy-start.3) | copy-done | bytes 4194328
  50.0 3.8 %first_part.2.mid_ref.refs_4_ = f32[1024,1024]{1,0:T(8,128)S(1)} custom-call(s32[1]{0:T(128)} %bitcast.me_ref, f32[1056,128]{1,0:T(8,128)S(1)} %pad_maximum_fusion.refs_0_, f32[1056,128]{1,0:T(8,128)S(1)} %collective-permute-done.16.refs_1_, bf16[1024,1024]{1,0:T(8,128)(2,1)S(1)} %get-tuple-element.300.refs_2_, ...), custom_call_target="tpu_custom_call" | custom-call | flops 32212254720 | bytes 125829120 | tf_op jit(solution)/shard_map/first_part/pallas_call | solution.py:330
  54.0 1.8 %column_product.1.refs_7_ = f32[1024,256]{1,0:T(8,128)S(1)} custom-call(bf16[1024,1024]{1,0:T(8,128)(2,1)S(1)} %get-tuple-element.303.xh.refs_5_, bf16[1024,1024]{1,0:T(8,128)(2,1)S(1)} %get-tuple-element.304.xl.refs_6_, f32[1024,1024]{1,0:T(8,128)S(1)} %first_part.2.mid_ref.refs_4_), custom_call_target="tpu_custom_call" | custom-call | flops 16106127360 | bytes 83886080 | tf_op jit(solution)/shard_map/column_product/pallas_call | solution.py:361
  55.9 6.2 %second_gram.1 = (f32[1056,128]{1,0:T(8,128)S(1)}, f32[1056,128]{1,0:T(8,128)S(1)}, f32[1024,1024]{1,0:T(8,128)S(1)}, bf16[1024,1024]{1,0:T(8,128)(2,1)S(1)}, bf16[1024,1024]{1,0:T(8,128)(2,1)S(1)}) custom-call(s32[1]{0:T(128)} %bitcast.me_ref, f32[1056,128]{1,0:T(8,128)S(1)} %pad_maximum_fusion.1.refs_0_, f32[1056,128]{1,0:T(8,128)S(1)} %collective-permute-done.17.refs_1_, ...), custom_call_target="tpu_custom_call" | custom-call | flops 51539607552 | bytes 209715200 | tf_op jit(solution)/shard_map/second_gram/pallas_call | solution.py:421
  62.6 3.9 %fourth_gram.1 = (f32[1056,128]{1,0:T(8,128)S(1)}, f32[1056,128]{1,0:T(8,128)S(1)}) custom-call(s32[1]{0:T(128)} %bitcast.me_ref, bf16[1024,1024]{1,0:T(8,128)(2,1)S(1)} %get-tuple-element.303.xh.refs_5_, bf16[1024,1024]{1,0:T(8,128)(2,1)S(1)} %get-tuple-element.304.xl.refs_6_, bf16[1024,1024]{1,0:T(8,128)(2,1)S(1)} %get-tuple-element.337.mh.ah, ...), custom_call_target="tpu_custom_call" | custom-call | flops 32212254720 | bytes 83886080 | tf_op jit(solution)/shard_map/fourth_gram/pallas_call | solution.py:438
  66.5 4.0 %collective-permute-start.25 = (f32[264,128]{1,0:T(8,128)S(1)}, f32[264,128]{1,0:T(8,128)S(1)}, u32[]{:S(2)}, u32[]{:S(2)}) collective-permute-start(f32[264,128]{1,0:T(8,128)S(1)} %get-tuple-element.391), channel_id=1, source_target_pairs={{0,6},{1,7},{2,4},{3,5},{4,2},{5,3},{6,0},{7,1},{8,14},{9,15},{10,... | collective-permute-start | bytes 405512 | tf_op jit(solution)/shard_map/ppermute | solution.py:493
  70.6 1.3 %collective-permute-start.23 = (f32[264,128]{1,0:T(8,128)S(1)}, f32[264,128]{1,0:T(8,128)S(1)}, u32[]{:S(2)}, u32[]{:S(2)}) collective-permute-start(f32[264,128]{1,0:T(8,128)S(1)} %get-tuple-element.393), channel_id=1, source_target_pairs={{0,2},{1,3},{2,0},{3,1},{4,6},{5,7},{6,4},{7,5},{8,10},{9,11},{10,... | collective-permute-start | bytes 405512 | tf_op jit(solution)/shard_map/ppermute | solution.py:493
  71.9 4.0 %affine_parts.2.refs_4_.refs_0_ = f32[512,1024]{1,0:T(8,128)S(1)} custom-call(f32[1024,1024]{1,0:T(8,128)S(1)} %get-tuple-element.336.a_ref, bf16[1024,1024]{1,0:T(8,128)(2,1)S(1)} %get-tuple-element.337.mh.ah, bf16[1024,1024]{1,0:T(8,128)(2,1)S(1)} %get-tuple-element.338.ml.al, bf16[1024,1024]{1,0:T(8,128)(2,1)S(1)} %get-tuple-element.334.bh, ...), custom_call_target="tpu_custom_call" | custom-call | flops 32212254720 | bytes 83886080 | tf_op jit(solution)/shard_map/affine_parts/pallas_call | solution.py:277
  76.1 2.2 %collective-permute-start.22 = (f32[264,128]{1,0:T(8,128)S(1)}, f32[264,128]{1,0:T(8,128)S(1)}, u32[]{:S(2)}, u32[]{:S(2)}) collective-permute-start(f32[264,128]{1,0:T(8,128)S(1)} %get-tuple-element.394), channel_id=1, source_target_pairs={{0,6},{1,7},{2,4},{3,5},{4,2},{5,3},{6,0},{7,1},{8,14},{9,15},{10,... | collective-permute-start | bytes 405512 | tf_op jit(solution)/shard_map/ppermute | solution.py:493
  78.5 1.4 %collective-permute-start.20 = (f32[264,128]{1,0:T(8,128)S(1)}, f32[264,128]{1,0:T(8,128)S(1)}, u32[]{:S(2)}, u32[]{:S(2)}) collective-permute-start(f32[264,128]{1,0:T(8,128)S(1)} %get-tuple-element.396), channel_id=1, source_target_pairs={{0,2},{1,3},{2,0},{3,1},{4,6},{5,7},{6,4},{7,5},{8,10},{9,11},{10,... | collective-permute-start | bytes 405512 | tf_op jit(solution)/shard_map/ppermute | solution.py:493
  80.0 3.9 %collective-permute-start.27 = (f32[264,128]{1,0:T(8,128)S(1)}, f32[264,128]{1,0:T(8,128)S(1)}, u32[]{:S(2)}, u32[]{:S(2)}) collective-permute-start(f32[264,128]{1,0:T(8,128)S(1)} %fusion.1), channel_id=1, source_target_pairs={{0,8},{1,9},{2,10},{3,11},{4,12},{5,13},{6,14},{7,15},{8,0},{9,1},... | collective-permute-start | bytes 405512 | tf_op jit(solution)/shard_map/ppermute | solution.py:493
  83.9 4.0 %affine_parts.3.refs_5_.refs_1_ = f32[512,1024]{1,0:T(8,128)S(1)} custom-call(f32[1024,1024]{1,0:T(8,128)S(1)} %get-tuple-element.336.a_ref, bf16[1024,1024]{1,0:T(8,128)(2,1)S(1)} %get-tuple-element.337.mh.ah, bf16[1024,1024]{1,0:T(8,128)(2,1)S(1)} %get-tuple-element.338.ml.al, bf16[1024,1024]{1,0:T(8,128)(2,1)S(1)} %get-tuple-element.334.bh, ...), custom_call_target="tpu_custom_call" | custom-call | flops 32212254720 | bytes 83886080 | tf_op jit(solution)/shard_map/affine_parts/pallas_call | solution.py:277
  88.3 1.7 %collective-permute-start.26 = (f32[264,128]{1,0:T(8,128)S(1)}, f32[264,128]{1,0:T(8,128)S(1)}, u32[]{:S(2)}, u32[]{:S(2)}) collective-permute-start(f32[264,128]{1,0:T(8,128)S(1)} %fusion.3), channel_id=1, source_target_pairs={{0,8},{1,9},{2,10},{3,11},{4,12},{5,13},{6,14},{7,15},{8,0},{9,1},... | collective-permute-start | bytes 405512 | tf_op jit(solution)/shard_map/ppermute | solution.py:493
  89.9 3.6 %collective-permute-start.33 = (f32[264,128]{1,0:T(8,128)S(1)}, f32[264,128]{1,0:T(8,128)S(1)}, u32[]{:S(2)}, u32[]{:S(2)}) collective-permute-start(f32[264,128]{1,0:T(8,128)S(1)} %add.93), channel_id=1, source_target_pairs={{0,6},{1,7},{2,4},{3,5},{4,2},{5,3},{6,0},{7,1},{8,14},{9,15},{10,... | collective-permute-start | bytes 405512 | tf_op jit(solution)/shard_map/ppermute | solution.py:493
  94.2 3.2 %collective-permute-done.26 = f32[264,128]{1,0:T(8,128)S(1)} collective-permute-done((f32[264,128]{1,0:T(8,128)S(1)}, f32[264,128]{1,0:T(8,128)S(1)}, u32[]{:S(2)}, u32[]{:S(2)}) %collective-permute-start.26) | collective-permute-done | bytes 135200 | tf_op jit(solution)/shard_map/ppermute | solution.py:493
  98.2 2.0 %collective-permute-start.29 = (f32[264,128]{1,0:T(8,128)S(1)}, f32[264,128]{1,0:T(8,128)S(1)}, u32[]{:S(2)}, u32[]{:S(2)}) collective-permute-start(f32[264,128]{1,0:T(8,128)S(1)} %add.92), channel_id=1, source_target_pairs={{0,4},{1,5},{2,6},{3,7},{4,0},{5,1},{6,2},{7,3},{8,12},{9,13},{10,... | collective-permute-start | bytes 405512 | tf_op jit(solution)/shard_map/ppermute | solution.py:493
  102.6 1.5 %collective-permute-done.34.refs_1_ = f32[1056,128]{1,0:T(8,128)S(1)} collective-permute-done((f32[1056,128]{1,0:T(8,128)S(1)}, f32[1056,128]{1,0:T(8,128)S(1)}, u32[]{:S(2)}, u32[]{:S(2)}) %collective-permute-start.34) | collective-permute-done | bytes 540704 | tf_op jit(solution)/shard_map/ppermute | solution.py:493
  104.0 2.2 %first_part.3 = (f32[1024,256]{1,0:T(8,128)S(1)}, bf16[1024,1024]{1,0:T(8,128)(2,1)S(1)}, bf16[1024,1024]{1,0:T(8,128)(2,1)S(1)}) custom-call(s32[1]{0:T(128)} %bitcast.me_ref, f32[1056,128]{1,0:T(8,128)S(1)} %pad_maximum_fusion.2.refs_0_, f32[1056,128]{1,0:T(8,128)S(1)} %collective-permute-done.34.refs_1_, bf16[1024,1024]{1,0:T(8,128)(2,1)S(1)} %cut.6.refs_2_.ah, ...), custom_call_target="tpu_custom_call" | custom-call | flops 32212254720 | bytes 125829120 | tf_op jit(solution)/shard_map/first_part/pallas_call | solution.py:330
  106.8 1.8 %other_part.1.refs_5_ = f32[1024,768]{1,0:T(8,128)S(1)} custom-call(bf16[1024,1024]{1,0:T(8,128)(2,1)S(1)} %cut.6.refs_2_.ah, bf16[1024,1024]{1,0:T(8,128)(2,1)S(1)} %cut.7.refs_3_.al, bf16[1024,1024]{1,0:T(8,128)(2,1)S(1)} %get-tuple-element.384.hi, bf16[1024,1024]{1,0:T(8,128)(2,1)S(1)} %get-tuple-element.385.lo, ...), custom_call_target="tpu_custom_call" | custom-call | flops 16106127360 | bytes 125829120 | tf_op jit(solution)/shard_map/other_part/pallas_call | solution.py:345
  108.7 5.1 %last.1 = f32[1024,1024]{1,0:T(8,128)} custom-call(s32[1]{0:T(128)} %bitcast.me_ref, f32[1056,128]{1,0:T(8,128)S(1)} %pad_maximum_fusion.3.refs_0_, f32[1056,128]{1,0:T(8,128)S(1)} %collective-permute-done.35.refs_1_, bf16[1024,1024]{1,0:T(8,128)(2,1)S(1)} %cut.6.refs_2_.ah, bf16[1024,1024]{1,0:T(8,128)(2,1)S(1)} %cut.7.refs_3_.al, ...), custom_call_target="tpu_custom_call" | custom-call | flops 32212254720 | bytes 125829120 | tf_op jit(solution)/shard_map/last/pallas_call | solution.py:470
  (90 shorter events, 13.7 us)
Async XLA Ops:
  6.9 4.2 %collective-permute-start = (f32[1056,128]{1,0:T(8,128)S(1)}, f32[1056,128]{1,0:T(8,128)S(1)}, u32[]{:S(2)}, u32[]{:S(2)}) collective-permute-start(f32[1056,128]{1,0:T(8,128)S(1)} %get-tuple-element.198), channel_id=1, source_target_pairs={{0,1},{1,0},{2,3},{3,2},{4,5},{5,4},{6,7},{7,6},{8,9},{9,8},{10,11... | collective-permute-start | bytes 1622024 | tf_op jit(solution)/shard_map/ppermute | solution.py:493
  11.2 13.6 %collective-permute-start.7 = (f32[264,128]{1,0:T(8,128)S(1)}, f32[264,128]{1,0:T(8,128)S(1)}, u32[]{:S(2)}, u32[]{:S(2)}) collective-permute-start(f32[264,128]{1,0:T(8,128)S(1)} %get-tuple-element.397), channel_id=1, source_target_pairs={{0,6},{1,7},{2,4},{3,5},{4,2},{5,3},{6,0},{7,1},{8,14},{9,15},{10,... | collective-permute-start | bytes 405512 | tf_op jit(solution)/shard_map/ppermute | solution.py:493
  14.8 10.2 %collective-permute-start.6 = (f32[264,128]{1,0:T(8,128)S(1)}, f32[264,128]{1,0:T(8,128)S(1)}, u32[]{:S(2)}, u32[]{:S(2)}) collective-permute-start(f32[264,128]{1,0:T(8,128)S(1)} %get-tuple-element.398), channel_id=1, source_target_pairs={{0,4},{1,5},{2,6},{3,7},{4,0},{5,1},{6,2},{7,3},{8,12},{9,13},{10,... | collective-permute-start | bytes 405512 | tf_op jit(solution)/shard_map/ppermute | solution.py:493
  15.3 9.8 %collective-permute-start.5 = (f32[264,128]{1,0:T(8,128)S(1)}, f32[264,128]{1,0:T(8,128)S(1)}, u32[]{:S(2)}, u32[]{:S(2)}) collective-permute-start(f32[264,128]{1,0:T(8,128)S(1)} %get-tuple-element.399), channel_id=1, source_target_pairs={{0,2},{1,3},{2,0},{3,1},{4,6},{5,7},{6,4},{7,5},{8,10},{9,11},{10,... | collective-permute-start | bytes 405512 | tf_op jit(solution)/shard_map/ppermute | solution.py:493
  15.5 4.3 %collective-permute-start.1 = (f32[1056,128]{1,0:T(8,128)S(1)}, f32[1056,128]{1,0:T(8,128)S(1)}, u32[]{:S(2)}, u32[]{:S(2)}) collective-permute-start(f32[1056,128]{1,0:T(8,128)S(1)} %get-tuple-element.206), channel_id=1, source_target_pairs={{0,1},{1,0},{2,3},{3,2},{4,5},{5,4},{6,7},{7,6},{8,9},{9,8},{10,11... | collective-permute-start | bytes 1622024 | tf_op jit(solution)/shard_map/ppermute | solution.py:493
  19.9 12.5 %collective-permute-start.4 = (f32[264,128]{1,0:T(8,128)S(1)}, f32[264,128]{1,0:T(8,128)S(1)}, u32[]{:S(2)}, u32[]{:S(2)}) collective-permute-start(f32[264,128]{1,0:T(8,128)S(1)} %get-tuple-element.400), channel_id=1, source_target_pairs={{0,6},{1,7},{2,4},{3,5},{4,2},{5,3},{6,0},{7,1},{8,14},{9,15},{10,... | collective-permute-start | bytes 405512 | tf_op jit(solution)/shard_map/ppermute | solution.py:493
  22.8 10.2 %collective-permute-start.3 = (f32[264,128]{1,0:T(8,128)S(1)}, f32[264,128]{1,0:T(8,128)S(1)}, u32[]{:S(2)}, u32[]{:S(2)}) collective-permute-start(f32[264,128]{1,0:T(8,128)S(1)} %get-tuple-element.401), channel_id=1, source_target_pairs={{0,4},{1,5},{2,6},{3,7},{4,0},{5,1},{6,2},{7,3},{8,12},{9,13},{10,... | collective-permute-start | bytes 405512 | tf_op jit(solution)/shard_map/ppermute | solution.py:493
  24.8 8.2 %collective-permute-start.2 = (f32[264,128]{1,0:T(8,128)S(1)}, f32[264,128]{1,0:T(8,128)S(1)}, u32[]{:S(2)}, u32[]{:S(2)}) collective-permute-start(f32[264,128]{1,0:T(8,128)S(1)} %get-tuple-element.402), channel_id=1, source_target_pairs={{0,2},{1,3},{2,0},{3,1},{4,6},{5,7},{6,4},{7,5},{8,10},{9,11},{10,... | collective-permute-start | bytes 405512 | tf_op jit(solution)/shard_map/ppermute | solution.py:493
  25.1 8.2 %collective-permute-start.9 = (f32[264,128]{1,0:T(8,128)S(1)}, f32[264,128]{1,0:T(8,128)S(1)}, u32[]{:S(2)}, u32[]{:S(2)}) collective-permute-start(f32[264,128]{1,0:T(8,128)S(1)} %fusion.5), channel_id=1, source_target_pairs={{0,8},{1,9},{2,10},{3,11},{4,12},{5,13},{6,14},{7,15},{8,0},{9,1},... | collective-permute-start | bytes 405512 | tf_op jit(solution)/shard_map/ppermute | solution.py:493
  33.1 9.2 %collective-permute-start.8 = (f32[264,128]{1,0:T(8,128)S(1)}, f32[264,128]{1,0:T(8,128)S(1)}, u32[]{:S(2)}, u32[]{:S(2)}) collective-permute-start(f32[264,128]{1,0:T(8,128)S(1)} %fusion.7), channel_id=1, source_target_pairs={{0,8},{1,9},{2,10},{3,11},{4,12},{5,13},{6,14},{7,15},{8,0},{9,1},... | collective-permute-start | bytes 405512 | tf_op jit(solution)/shard_map/ppermute | solution.py:493
  33.3 11.9 %collective-permute-start.15 = (f32[264,128]{1,0:T(8,128)S(1)}, f32[264,128]{1,0:T(8,128)S(1)}, u32[]{:S(2)}, u32[]{:S(2)}) collective-permute-start(f32[264,128]{1,0:T(8,128)S(1)} %add.83), channel_id=1, source_target_pairs={{0,6},{1,7},{2,4},{3,5},{4,2},{5,3},{6,0},{7,1},{8,14},{9,15},{10,... | collective-permute-start | bytes 405512 | tf_op jit(solution)/shard_map/ppermute | solution.py:493
  39.6 7.3 %collective-permute-start.14 = (f32[264,128]{1,0:T(8,128)S(1)}, f32[264,128]{1,0:T(8,128)S(1)}, u32[]{:S(2)}, u32[]{:S(2)}) collective-permute-start(f32[264,128]{1,0:T(8,128)S(1)} %add.83), channel_id=1, source_target_pairs={{0,4},{1,5},{2,6},{3,7},{4,0},{5,1},{6,2},{7,3},{8,12},{9,13},{10,... | collective-permute-start | bytes 405512 | tf_op jit(solution)/shard_map/ppermute | solution.py:493
  39.6 7.3 %collective-permute-start.13 = (f32[264,128]{1,0:T(8,128)S(1)}, f32[264,128]{1,0:T(8,128)S(1)}, u32[]{:S(2)}, u32[]{:S(2)}) collective-permute-start(f32[264,128]{1,0:T(8,128)S(1)} %add.83), channel_id=1, source_target_pairs={{0,2},{1,3},{2,0},{3,1},{4,6},{5,7},{6,4},{7,5},{8,10},{9,11},{10,... | collective-permute-start | bytes 405512 | tf_op jit(solution)/shard_map/ppermute | solution.py:493
  42.3 11.5 %collective-permute-start.12 = (f32[264,128]{1,0:T(8,128)S(1)}, f32[264,128]{1,0:T(8,128)S(1)}, u32[]{:S(2)}, u32[]{:S(2)}) collective-permute-start(f32[264,128]{1,0:T(8,128)S(1)} %add.82), channel_id=1, source_target_pairs={{0,6},{1,7},{2,4},{3,5},{4,2},{5,3},{6,0},{7,1},{8,14},{9,15},{10,... | collective-permute-start | bytes 405512 | tf_op jit(solution)/shard_map/ppermute | solution.py:493
  43.2 10.7 %collective-permute-start.11 = (f32[264,128]{1,0:T(8,128)S(1)}, f32[264,128]{1,0:T(8,128)S(1)}, u32[]{:S(2)}, u32[]{:S(2)}) collective-permute-start(f32[264,128]{1,0:T(8,128)S(1)} %add.82), channel_id=1, source_target_pairs={{0,4},{1,5},{2,6},{3,7},{4,0},{5,1},{6,2},{7,3},{8,12},{9,13},{10,... | collective-permute-start | bytes 405512 | tf_op jit(solution)/shard_map/ppermute | solution.py:493
  45.2 8.6 %collective-permute-start.10 = (f32[264,128]{1,0:T(8,128)S(1)}, f32[264,128]{1,0:T(8,128)S(1)}, u32[]{:S(2)}, u32[]{:S(2)}) collective-permute-start(f32[264,128]{1,0:T(8,128)S(1)} %add.82), channel_id=1, source_target_pairs={{0,2},{1,3},{2,0},{3,1},{4,6},{5,7},{6,4},{7,5},{8,10},{9,11},{10,... | collective-permute-start | bytes 405512 | tf_op jit(solution)/shard_map/ppermute | solution.py:493
  62.1 4.3 %collective-permute-start.18 = (f32[1056,128]{1,0:T(8,128)S(1)}, f32[1056,128]{1,0:T(8,128)S(1)}, u32[]{:S(2)}, u32[]{:S(2)}) collective-permute-start(f32[1056,128]{1,0:T(8,128)S(1)} %get-tuple-element.306), channel_id=1, source_target_pairs={{0,1},{1,0},{2,3},{3,2},{4,5},{5,4},{6,7},{7,6},{8,9},{9,8},{10,11... | collective-permute-start | bytes 1622024 | tf_op jit(solution)/shard_map/ppermute | solution.py:493
  66.5 12.0 %collective-permute-start.25 = (f32[264,128]{1,0:T(8,128)S(1)}, f32[264,128]{1,0:T(8,128)S(1)}, u32[]{:S(2)}, u32[]{:S(2)}) collective-permute-start(f32[264,128]{1,0:T(8,128)S(1)} %get-tuple-element.391), channel_id=1, source_target_pairs={{0,6},{1,7},{2,4},{3,5},{4,2},{5,3},{6,0},{7,1},{8,14},{9,15},{10,... | collective-permute-start | bytes 405512 | tf_op jit(solution)/shard_map/ppermute | solution.py:493
  70.6 9.4 %collective-permute-start.24 = (f32[264,128]{1,0:T(8,128)S(1)}, f32[264,128]{1,0:T(8,128)S(1)}, u32[]{:S(2)}, u32[]{:S(2)}) collective-permute-start(f32[264,128]{1,0:T(8,128)S(1)} %get-tuple-element.392), channel_id=1, source_target_pairs={{0,4},{1,5},{2,6},{3,7},{4,0},{5,1},{6,2},{7,3},{8,12},{9,13},{10,... | collective-permute-start | bytes 405512 | tf_op jit(solution)/shard_map/ppermute | solution.py:493
  70.6 9.4 %collective-permute-start.23 = (f32[264,128]{1,0:T(8,128)S(1)}, f32[264,128]{1,0:T(8,128)S(1)}, u32[]{:S(2)}, u32[]{:S(2)}) collective-permute-start(f32[264,128]{1,0:T(8,128)S(1)} %get-tuple-element.393), channel_id=1, source_target_pairs={{0,2},{1,3},{2,0},{3,1},{4,6},{5,7},{6,4},{7,5},{8,10},{9,11},{10,... | collective-permute-start | bytes 405512 | tf_op jit(solution)/shard_map/ppermute | solution.py:493
  71.9 4.1 %collective-permute-start.19 = (f32[1056,128]{1,0:T(8,128)S(1)}, f32[1056,128]{1,0:T(8,128)S(1)}, u32[]{:S(2)}, u32[]{:S(2)}) collective-permute-start(f32[1056,128]{1,0:T(8,128)S(1)} %get-tuple-element.316), channel_id=1, source_target_pairs={{0,1},{1,0},{2,3},{3,2},{4,5},{5,4},{6,7},{7,6},{8,9},{9,8},{10,11... | collective-permute-start | bytes 1622024 | tf_op jit(solution)/shard_map/ppermute | solution.py:493
  76.1 11.9 %collective-permute-start.22 = (f32[264,128]{1,0:T(8,128)S(1)}, f32[264,128]{1,0:T(8,128)S(1)}, u32[]{:S(2)}, u32[]{:S(2)}) collective-permute-start(f32[264,128]{1,0:T(8,128)S(1)} %get-tuple-element.394), channel_id=1, source_target_pairs={{0,6},{1,7},{2,4},{3,5},{4,2},{5,3},{6,0},{7,1},{8,14},{9,15},{10,... | collective-permute-start | bytes 405512 | tf_op jit(solution)/shard_map/ppermute | solution.py:493
  78.3 9.9 %collective-permute-start.21 = (f32[264,128]{1,0:T(8,128)S(1)}, f32[264,128]{1,0:T(8,128)S(1)}, u32[]{:S(2)}, u32[]{:S(2)}) collective-permute-start(f32[264,128]{1,0:T(8,128)S(1)} %get-tuple-element.395), channel_id=1, source_target_pairs={{0,4},{1,5},{2,6},{3,7},{4,0},{5,1},{6,2},{7,3},{8,12},{9,13},{10,... | collective-permute-start | bytes 405512 | tf_op jit(solution)/shard_map/ppermute | solution.py:493
  78.5 9.7 %collective-permute-start.20 = (f32[264,128]{1,0:T(8,128)S(1)}, f32[264,128]{1,0:T(8,128)S(1)}, u32[]{:S(2)}, u32[]{:S(2)}) collective-permute-start(f32[264,128]{1,0:T(8,128)S(1)} %get-tuple-element.396), channel_id=1, source_target_pairs={{0,2},{1,3},{2,0},{3,1},{4,6},{5,7},{6,4},{7,5},{8,10},{9,11},{10,... | collective-permute-start | bytes 405512 | tf_op jit(solution)/shard_map/ppermute | solution.py:493
  80.0 9.9 %collective-permute-start.27 = (f32[264,128]{1,0:T(8,128)S(1)}, f32[264,128]{1,0:T(8,128)S(1)}, u32[]{:S(2)}, u32[]{:S(2)}) collective-permute-start(f32[264,128]{1,0:T(8,128)S(1)} %fusion.1), channel_id=1, source_target_pairs={{0,8},{1,9},{2,10},{3,11},{4,12},{5,13},{6,14},{7,15},{8,0},{9,1},... | collective-permute-start | bytes 405512 | tf_op jit(solution)/shard_map/ppermute | solution.py:493
  88.3 9.2 %collective-permute-start.26 = (f32[264,128]{1,0:T(8,128)S(1)}, f32[264,128]{1,0:T(8,128)S(1)}, u32[]{:S(2)}, u32[]{:S(2)}) collective-permute-start(f32[264,128]{1,0:T(8,128)S(1)} %fusion.3), channel_id=1, source_target_pairs={{0,8},{1,9},{2,10},{3,11},{4,12},{5,13},{6,14},{7,15},{8,0},{9,1},... | collective-permute-start | bytes 405512 | tf_op jit(solution)/shard_map/ppermute | solution.py:493
  89.9 10.3 %collective-permute-start.33 = (f32[264,128]{1,0:T(8,128)S(1)}, f32[264,128]{1,0:T(8,128)S(1)}, u32[]{:S(2)}, u32[]{:S(2)}) collective-permute-start(f32[264,128]{1,0:T(8,128)S(1)} %add.93), channel_id=1, source_target_pairs={{0,6},{1,7},{2,4},{3,5},{4,2},{5,3},{6,0},{7,1},{8,14},{9,15},{10,... | collective-permute-start | bytes 405512 | tf_op jit(solution)/shard_map/ppermute | solution.py:493
  93.5 8.4 %collective-permute-start.32 = (f32[264,128]{1,0:T(8,128)S(1)}, f32[264,128]{1,0:T(8,128)S(1)}, u32[]{:S(2)}, u32[]{:S(2)}) collective-permute-start(f32[264,128]{1,0:T(8,128)S(1)} %add.93), channel_id=1, source_target_pairs={{0,4},{1,5},{2,6},{3,7},{4,0},{5,1},{6,2},{7,3},{8,12},{9,13},{10,... | collective-permute-start | bytes 405512 | tf_op jit(solution)/shard_map/ppermute | solution.py:493
  93.5 8.4 %collective-permute-start.31 = (f32[264,128]{1,0:T(8,128)S(1)}, f32[264,128]{1,0:T(8,128)S(1)}, u32[]{:S(2)}, u32[]{:S(2)}) collective-permute-start(f32[264,128]{1,0:T(8,128)S(1)} %add.93), channel_id=1, source_target_pairs={{0,2},{1,3},{2,0},{3,1},{4,6},{5,7},{6,4},{7,5},{8,10},{9,11},{10,... | collective-permute-start | bytes 405512 | tf_op jit(solution)/shard_map/ppermute | solution.py:493
  97.4 8.8 %collective-permute-start.30 = (f32[264,128]{1,0:T(8,128)S(1)}, f32[264,128]{1,0:T(8,128)S(1)}, u32[]{:S(2)}, u32[]{:S(2)}) collective-permute-start(f32[264,128]{1,0:T(8,128)S(1)} %add.92), channel_id=1, source_target_pairs={{0,6},{1,7},{2,4},{3,5},{4,2},{5,3},{6,0},{7,1},{8,14},{9,15},{10,... | collective-permute-start | bytes 405512 | tf_op jit(solution)/shard_map/ppermute | solution.py:493
  98.2 8.5 %collective-permute-start.29 = (f32[264,128]{1,0:T(8,128)S(1)}, f32[264,128]{1,0:T(8,128)S(1)}, u32[]{:S(2)}, u32[]{:S(2)}) collective-permute-start(f32[264,128]{1,0:T(8,128)S(1)} %add.92), channel_id=1, source_target_pairs={{0,4},{1,5},{2,6},{3,7},{4,0},{5,1},{6,2},{7,3},{8,12},{9,13},{10,... | collective-permute-start | bytes 405512 | tf_op jit(solution)/shard_map/ppermute | solution.py:493
  100.2 6.5 %collective-permute-start.28 = (f32[264,128]{1,0:T(8,128)S(1)}, f32[264,128]{1,0:T(8,128)S(1)}, u32[]{:S(2)}, u32[]{:S(2)}) collective-permute-start(f32[264,128]{1,0:T(8,128)S(1)} %add.92), channel_id=1, source_target_pairs={{0,2},{1,3},{2,0},{3,1},{4,6},{5,7},{6,4},{7,5},{8,10},{9,11},{10,... | collective-permute-start | bytes 405512 | tf_op jit(solution)/shard_map/ppermute | solution.py:493
  (10 other events, 60.5 us)

commit v7 on v6

--- a/solution.py
+++ b/solution.py
@@ -492,6 +492,9 @@
     def swap(self, x, offset):
         return lax.ppermute(x, "row", [(i, i ^ offset) for i in range(self.count)])
 
+    def swaps(self, values):
+        return [self.swap(x, offset) for x, offset in zip(values, PLANE)]
+
     def core(self):
         return self.swap(self.send, CORE)
 
@@ -499,7 +502,7 @@
         total = self.keep + got
         part = total.shape[0] // (1 + len(PLANE))
         self.keep, *sends = [total[k * part:(k + 1) * part] for k in range(1 + len(PLANE))]
-        return [self.swap(x, offset) for x, offset in zip(sends, PLANE)]
+        return self.swaps(sends)
 
     def own(self, got):
         self.keep = sum(got, self.keep)
@@ -508,7 +511,7 @@
         return self.swap(self.keep, offset)
 
     def gather_plane(self):
-        return [self.swap(self.keep, offset) for offset in PLANE]
+        return self.swaps([self.keep] * len(PLANE))
 
     def gather_core(self, got):
         self.mine = jnp.concatenate([self.keep, *got], axis=0)
@@ -516,9 +519,9 @@
 
 
 def close(env, *got):
-    values = lax.optimization_barrier((*got, *env.values()))
-    env.update(zip(env, values[len(got):]))
-    return values[:len(got)]
+    values = lax.optimization_barrier((*env.values(), *got[::-1]))
+    env.update(zip(env, values))
+    return values[len(env):][::-1]
 
 
 def sum_chunks(count, env, first, second, works, late):
@@ -579,9 +582,12 @@
     def turned(env):
         env["xh"], env["xl"] = turn(env["x0"])
 
-    def cut_two(env):
+    def half_and_cut(env):
+        half(1)(env)
+        env["s0h"], env["s0l"] = cut(env["s0"], 0, 1)
+
+    def cut_orbitals(env):
         env["x1h"], env["x1l"] = cut(env["x1"], 0, 1)
-        env["s0h"], env["s0l"] = cut(env["s0"], 0, 1)
 
     def middle(env, pieces):
         (env["mid"],) = first_part(
@@ -594,7 +600,7 @@
     keep, send, *parts = first_gram(me, SHARDS, env["x1"], env["c"])
     one = sum_chunks(
         count, env, (keep, send), lambda env: other_gram(me, SHARDS, *parts),
-        [half(0), turned, half(1), cut_two], [middle, column],
+        [half(0), turned, half_and_cut, cut_orbitals], [middle, column],
     )
 
     keep, send, env["mid"], env["mh"], env["ml"] = second_gram(

time: 114 us -> 113 us (level)
  waiting for transfers between devices: 11.1 us -> 13.8 us
  starting transfers between devices: 44.3 us -> 42 us
  local copies, waits for them, and re-layouts: 1.48 us -> 0.14 us
    ppermute x36, waiting for transfers between devices: 11.1 us -> 13.8 us  [swap(): return lax.ppermute(x, 'row', [(i, i ^ offset) for i in range(self.count)])]
    ppermute x36, starting transfers between devices: 44.3 us -> 42 us  [swap(): return lax.ppermute(x, 'row', [(i, i ^ offset) for i in range(self.count)])]
    unnamed x12, local copies, waits for them, and re-layouts: 1.36 us -> 0.03 us
  transfers between devices with their start and end apart: 36 -> 36, of which waited for: 11 -> 9; matrix products, arithmetic and copies ran while one was open for 0% -> 0% of each run, Pallas kernels for 33% -> 33%
where the time goes in v7:
time: 113 us
  Pallas kernels  55.9 us (49%)
  starting transfers between devices  42 us (37%)
  waiting for transfers between devices  13.8 us (12%)
    ppermute x36, starting transfers between devices, swap(): return lax.ppermute(x, 'row', [(i, i ^ offset) for i in range(self.count)])  42 us
    ppermute x36, waiting for transfers between devices, swap(): return lax.ppermute(x, 'row', [(i, i ^ offset) for i in range(self.count)])  13.8 us
    pallas_call x2, Pallas kernels, affine(): call(affine_kernel, 'affine', struct(rows // 2, size), 18, 0.5, 2, grid=(...  8.63 us
    pallas_call x2, Pallas kernels, affine_parts(): call(affine_parts_kernel, 'affine_parts', struct(rows // 2, size), 18, 0....  8.09 us
    pallas_call x1, Pallas kernels, first_gram(): call(functools.partial(first_gram_kernel, shards), 'first_gram', halves(s...  6.9 us
    pallas_call x1, Pallas kernels, second_gram(): call(functools.partial(second_gram_kernel, shards, len(pieces)), 'second_...  6.19 us
    pallas_call x2, Pallas kernels, first_part(): call(functools.partial(first_part_kernel, shards, len(pieces), columns),...  5.98 us
    pallas_call x1, Pallas kernels, last_step(): call(functools.partial(last_kernel, shards, len(pieces)), 'last', struct(...  5.13 us
  transfers between devices with their start and end apart: 36, of which 9 were waited for; matrix products, arithmetic and copies ran while one was open for 0% of the time, Pallas kernels for 33%

profile of v7, /device:TPU:0, one launch (start us, length us, event | category | flops | bytes accessed | tf_op | source)
XLA Modules:
  0.0 113.1 jit_solution(3530014592698868339)
XLA Ops:
  0.0 6.9 %first_gram.1 = (f32[1056,128]{1,0:T(8,128)S(1)}, f32[1056,128]{1,0:T(8,128)S(1)}, bf16[1024,1024]{1,0:T(8,128)(2,1)S(1)}, bf16[1024,1024]{1,0:T(8,128)(2,1)S(1)...) custom-call(s32[1]{0:T(128)} %bitcast.me_ref, f32[1024,1024]{1,0:T(8,128)} %x_ref.2, f32[1024,1024]{1,0:T(8,128)} %a_ref.1), custom_call_target="tpu_custom_call" | custom-call | flops 32212254720 | bytes 167772160 | tf_op jit(solution)/shard_map/first_gram/pallas_call | solution.py:198
  7.4 3.6 %other_gram.1 = (f32[1056,128]{1,0:T(8,128)S(1)}, f32[1056,128]{1,0:T(8,128)S(1)}) custom-call(s32[1]{0:T(128)} %bitcast.me_ref, bf16[1024,1024]{1,0:T(8,128)(2,1)S(1)} %get-tuple-element.204.ah, bf16[1024,1024]{1,0:T(8,128)(2,1)S(1)} %get-tuple-element.205.al, bf16[1024,1024]{1,0:T(8,128)(2,1)S(1)} %get-tuple-element.206.bh, ...), custom_call_target="tpu_custom_call" | custom-call | flops 32212254720 | bytes 83886080 | tf_op jit(solution)/shard_map/other_gram/pallas_call | solution.py:228
  11.2 2.6 %collective-permute-start.4 = (f32[264,128]{1,0:T(8,128)S(1)}, f32[264,128]{1,0:T(8,128)S(1)}, u32[]{:S(2)}, u32[]{:S(2)}) collective-permute-start(f32[264,128]{1,0:T(8,128)S(1)} %get-tuple-element.412), channel_id=1, source_target_pairs={{0,2},{1,3},{2,0},{3,1},{4,6},{5,7},{6,4},{7,5},{8,10},{9,11},{10,... | collective-permute-start | bytes 405512 | tf_op jit(solution)/shard_map/ppermute | solution.py:493
  13.8 1.6 %collective-permute-start.3 = (f32[264,128]{1,0:T(8,128)S(1)}, f32[264,128]{1,0:T(8,128)S(1)}, u32[]{:S(2)}, u32[]{:S(2)}) collective-permute-start(f32[264,128]{1,0:T(8,128)S(1)} %get-tuple-element.413), channel_id=1, source_target_pairs={{0,4},{1,5},{2,6},{3,7},{4,0},{5,1},{6,2},{7,3},{8,12},{9,13},{10,... | collective-permute-start | bytes 405512 | tf_op jit(solution)/shard_map/ppermute | solution.py:493
  15.4 4.3 %affine.2.refs_4_ = f32[512,1024]{1,0:T(8,128)S(1)} custom-call(f32[1024,1024]{1,0:T(8,128)S(1)} %copy-done, f32[1024,1024]{1,0:T(8,128)S(1)} %copy-done.1), custom_call_target="tpu_custom_call" | custom-call | flops 32212254720 | bytes 83886080 | tf_op jit(solution)/shard_map/affine/pallas_call | solution.py:256
  19.8 2.0 %collective-permute-start.7 = (f32[264,128]{1,0:T(8,128)S(1)}, f32[264,128]{1,0:T(8,128)S(1)}, u32[]{:S(2)}, u32[]{:S(2)}) collective-permute-start(f32[264,128]{1,0:T(8,128)S(1)} %get-tuple-element.409), channel_id=1, source_target_pairs={{0,2},{1,3},{2,0},{3,1},{4,6},{5,7},{6,4},{7,5},{8,10},{9,11},{10,... | collective-permute-start | bytes 405512 | tf_op jit(solution)/shard_map/ppermute | solution.py:493
  21.8 1.6 %collective-permute-start.6 = (f32[264,128]{1,0:T(8,128)S(1)}, f32[264,128]{1,0:T(8,128)S(1)}, u32[]{:S(2)}, u32[]{:S(2)}) collective-permute-start(f32[264,128]{1,0:T(8,128)S(1)} %get-tuple-element.410), channel_id=1, source_target_pairs={{0,4},{1,5},{2,6},{3,7},{4,0},{5,1},{6,2},{7,3},{8,12},{9,13},{10,... | collective-permute-start | bytes 405512 | tf_op jit(solution)/shard_map/ppermute | solution.py:493
  23.4 1.5 %turn.1 = (bf16[1024,1024]{1,0:T(8,128)(2,1)S(1)}, bf16[1024,1024]{1,0:T(8,128)(2,1)S(1)}) custom-call(f32[1024,1024]{1,0:T(8,128)S(1)} %copy-done.4), custom_call_target="tpu_custom_call" | custom-call | flops 6442450944 | bytes 83886080 | tf_op jit(solution)/shard_map/turn/pallas_call | solution.py:376
  25.1 3.0 %collective-permute-start.8 = (f32[264,128]{1,0:T(8,128)S(1)}, f32[264,128]{1,0:T(8,128)S(1)}, u32[]{:S(2)}, u32[]{:S(2)}) collective-permute-start(f32[264,128]{1,0:T(8,128)S(1)} %fusion.7), channel_id=1, source_target_pairs={{0,8},{1,9},{2,10},{3,11},{4,12},{5,13},{6,14},{7,15},{8,0},{9,1},... | collective-permute-start | bytes 405512 | tf_op jit(solution)/shard_map/ppermute | solution.py:493
  28.1 4.3 %affine.3.refs_5_ = f32[512,1024]{1,0:T(8,128)S(1)} custom-call(f32[1024,1024]{1,0:T(8,128)S(1)} %copy-done, f32[1024,1024]{1,0:T(8,128)S(1)} %copy-done.1), custom_call_target="tpu_custom_call" | custom-call | flops 32212254720 | bytes 83886080 | tf_op jit(solution)/shard_map/affine/pallas_call | solution.py:256
  35.6 3.5 %collective-permute-start.11 = (f32[264,128]{1,0:T(8,128)S(1)}, f32[264,128]{1,0:T(8,128)S(1)}, u32[]{:S(2)}, u32[]{:S(2)}) collective-permute-start(f32[264,128]{1,0:T(8,128)S(1)} %add.82), channel_id=1, source_target_pairs={{0,4},{1,5},{2,6},{3,7},{4,0},{5,1},{6,2},{7,3},{8,12},{9,13},{10,... | collective-permute-start | bytes 405512 | tf_op jit(solution)/shard_map/ppermute | solution.py:493
  39.2 3.5 %collective-permute-done.9 = f32[264,128]{1,0:T(8,128)S(1)} collective-permute-done((f32[264,128]{1,0:T(8,128)S(1)}, f32[264,128]{1,0:T(8,128)S(1)}, u32[]{:S(2)}, u32[]{:S(2)}) %collective-permute-start.9) | collective-permute-done | bytes 135200 | tf_op jit(solution)/shard_map/ppermute | solution.py:493
  44.0 2.9 %collective-permute-start.14 = (f32[264,128]{1,0:T(8,128)S(1)}, f32[264,128]{1,0:T(8,128)S(1)}, u32[]{:S(2)}, u32[]{:S(2)}) collective-permute-start(f32[264,128]{1,0:T(8,128)S(1)} %add.83), channel_id=1, source_target_pairs={{0,6},{1,7},{2,4},{3,5},{4,2},{5,3},{6,0},{7,1},{8,14},{9,15},{10,... | collective-permute-start | bytes 405512 | tf_op jit(solution)/shard_map/ppermute | solution.py:493
  48.9 3.8 %first_part.2.mid_ref.refs_4_ = f32[1024,1024]{1,0:T(8,128)S(1)} custom-call(s32[1]{0:T(128)} %bitcast.me_ref, f32[1056,128]{1,0:T(8,128)S(1)} %pad_maximum_fusion.refs_0_, f32[1056,128]{1,0:T(8,128)S(1)} %collective-permute-done.13.refs_1_, bf16[1024,1024]{1,0:T(8,128)(2,1)S(1)} %get-tuple-element.316.refs_2_, ...), custom_call_target="tpu_custom_call" | custom-call | flops 32212254720 | bytes 125829120 | tf_op jit(solution)/shard_map/first_part/pallas_call | solution.py:330
  53.0 1.8 %column_product.1.refs_7_ = f32[1024,256]{1,0:T(8,128)S(1)} custom-call(bf16[1024,1024]{1,0:T(8,128)(2,1)S(1)} %get-tuple-element.312.xh.refs_5_, bf16[1024,1024]{1,0:T(8,128)(2,1)S(1)} %get-tuple-element.313.xl.refs_6_, f32[1024,1024]{1,0:T(8,128)S(1)} %first_part.2.mid_ref.refs_4_), custom_call_target="tpu_custom_call" | custom-call | flops 16106127360 | bytes 83886080 | tf_op jit(solution)/shard_map/column_product/pallas_call | solution.py:361
  54.8 6.2 %second_gram.1 = (f32[1056,128]{1,0:T(8,128)S(1)}, f32[1056,128]{1,0:T(8,128)S(1)}, f32[1024,1024]{1,0:T(8,128)S(1)}, bf16[1024,1024]{1,0:T(8,128)(2,1)S(1)}, bf16[1024,1024]{1,0:T(8,128)(2,1)S(1)}) custom-call(s32[1]{0:T(128)} %bitcast.me_ref, f32[1056,128]{1,0:T(8,128)S(1)} %pad_maximum_fusion.1.refs_0_, f32[1056,128]{1,0:T(8,128)S(1)} %collective-permute-done.17.refs_1_, ...), custom_call_target="tpu_custom_call" | custom-call | flops 51539607552 | bytes 209715200 | tf_op jit(solution)/shard_map/second_gram/pallas_call | solution.py:421
  61.4 3.9 %fourth_gram.1 = (f32[1056,128]{1,0:T(8,128)S(1)}, f32[1056,128]{1,0:T(8,128)S(1)}) custom-call(s32[1]{0:T(128)} %bitcast.me_ref, bf16[1024,1024]{1,0:T(8,128)(2,1)S(1)} %get-tuple-element.312.xh.refs_5_, bf16[1024,1024]{1,0:T(8,128)(2,1)S(1)} %get-tuple-element.313.xl.refs_6_, bf16[1024,1024]{1,0:T(8,128)(2,1)S(1)} %get-tuple-element.349.mh.ah, ...), custom_call_target="tpu_custom_call" | custom-call | flops 32212254720 | bytes 83886080 | tf_op jit(solution)/shard_map/fourth_gram/pallas_call | solution.py:438
  66.6 2.3 %collective-permute-start.20 = (f32[264,128]{1,0:T(8,128)S(1)}, f32[264,128]{1,0:T(8,128)S(1)}, u32[]{:S(2)}, u32[]{:S(2)}) collective-permute-start(f32[264,128]{1,0:T(8,128)S(1)} %get-tuple-element.408), channel_id=1, source_target_pairs={{0,6},{1,7},{2,4},{3,5},{4,2},{5,3},{6,0},{7,1},{8,14},{9,15},{10,... | collective-permute-start | bytes 405512 | tf_op jit(solution)/shard_map/ppermute | solution.py:493
  69.0 4.0 %affine_parts.2.refs_4_.refs_0_ = f32[512,1024]{1,0:T(8,128)S(1)} custom-call(f32[1024,1024]{1,0:T(8,128)S(1)} %get-tuple-element.348.a_ref, bf16[1024,1024]{1,0:T(8,128)(2,1)S(1)} %get-tuple-element.349.mh.ah, bf16[1024,1024]{1,0:T(8,128)(2,1)S(1)} %get-tuple-element.350.ml.al, bf16[1024,1024]{1,0:T(8,128)(2,1)S(1)} %get-tuple-element.346.bh, ...), custom_call_target="tpu_custom_call" | custom-call | flops 32212254720 | bytes 83886080 | tf_op jit(solution)/shard_map/affine_parts/pallas_call | solution.py:277
  74.6 2.4 %collective-permute-start.23 = (f32[264,128]{1,0:T(8,128)S(1)}, f32[264,128]{1,0:T(8,128)S(1)}, u32[]{:S(2)}, u32[]{:S(2)}) collective-permute-start(f32[264,128]{1,0:T(8,128)S(1)} %get-tuple-element.405), channel_id=1, source_target_pairs={{0,6},{1,7},{2,4},{3,5},{4,2},{5,3},{6,0},{7,1},{8,14},{9,15},{10,... | collective-permute-start | bytes 405512 | tf_op jit(solution)/shard_map/ppermute | solution.py:493
  77.1 4.3 %collective-permute-start.26 = (f32[264,128]{1,0:T(8,128)S(1)}, f32[264,128]{1,0:T(8,128)S(1)}, u32[]{:S(2)}, u32[]{:S(2)}) collective-permute-start(f32[264,128]{1,0:T(8,128)S(1)} %fusion.1), channel_id=1, source_target_pairs={{0,8},{1,9},{2,10},{3,11},{4,12},{5,13},{6,14},{7,15},{8,0},{9,1},... | collective-permute-start | bytes 405512 | tf_op jit(solution)/shard_map/ppermute | solution.py:493
  81.4 4.0 %affine_parts.3.refs_5_.refs_1_ = f32[512,1024]{1,0:T(8,128)S(1)} custom-call(f32[1024,1024]{1,0:T(8,128)S(1)} %get-tuple-element.348.a_ref, bf16[1024,1024]{1,0:T(8,128)(2,1)S(1)} %get-tuple-element.349.mh.ah, bf16[1024,1024]{1,0:T(8,128)(2,1)S(1)} %get-tuple-element.350.ml.al, bf16[1024,1024]{1,0:T(8,128)(2,1)S(1)} %get-tuple-element.346.bh, ...), custom_call_target="tpu_custom_call" | custom-call | flops 32212254720 | bytes 83886080 | tf_op jit(solution)/shard_map/affine_parts/pallas_call | solution.py:277
  86.2 2.1 %collective-permute-start.27 = (f32[264,128]{1,0:T(8,128)S(1)}, f32[264,128]{1,0:T(8,128)S(1)}, u32[]{:S(2)}, u32[]{:S(2)}) collective-permute-start(f32[264,128]{1,0:T(8,128)S(1)} %fusion.3), channel_id=1, source_target_pairs={{0,8},{1,9},{2,10},{3,11},{4,12},{5,13},{6,14},{7,15},{8,0},{9,1},... | collective-permute-start | bytes 405512 | tf_op jit(solution)/shard_map/ppermute | solution.py:493
  88.5 3.4 %collective-permute-start.29 = (f32[264,128]{1,0:T(8,128)S(1)}, f32[264,128]{1,0:T(8,128)S(1)}, u32[]{:S(2)}, u32[]{:S(2)}) collective-permute-start(f32[264,128]{1,0:T(8,128)S(1)} %add.93), channel_id=1, source_target_pairs={{0,4},{1,5},{2,6},{3,7},{4,0},{5,1},{6,2},{7,3},{8,12},{9,13},{10,... | collective-permute-start | bytes 405512 | tf_op jit(solution)/shard_map/ppermute | solution.py:493
  91.9 2.8 %collective-permute-done.27 = f32[264,128]{1,0:T(8,128)S(1)} collective-permute-done((f32[264,128]{1,0:T(8,128)S(1)}, f32[264,128]{1,0:T(8,128)S(1)}, u32[]{:S(2)}, u32[]{:S(2)}) %collective-permute-start.27) | collective-permute-done | bytes 135200 | tf_op jit(solution)/shard_map/ppermute | solution.py:493
  94.7 1.7 %collective-permute-start.34 = (f32[264,128]{1,0:T(8,128)S(1)}, f32[264,128]{1,0:T(8,128)S(1)}, u32[]{:S(2)}, u32[]{:S(2)}) collective-permute-start(f32[264,128]{1,0:T(8,128)S(1)} %add.92), channel_id=1, source_target_pairs={{0,2},{1,3},{2,0},{3,1},{4,6},{5,7},{6,4},{7,5},{8,10},{9,11},{10,... | collective-permute-start | bytes 405512 | tf_op jit(solution)/shard_map/ppermute | solution.py:493
  96.4 1.9 %collective-permute-start.32 = (f32[264,128]{1,0:T(8,128)S(1)}, f32[264,128]{1,0:T(8,128)S(1)}, u32[]{:S(2)}, u32[]{:S(2)}) collective-permute-start(f32[264,128]{1,0:T(8,128)S(1)} %add.92), channel_id=1, source_target_pairs={{0,6},{1,7},{2,4},{3,5},{4,2},{5,3},{6,0},{7,1},{8,14},{9,15},{10,... | collective-permute-start | bytes 405512 | tf_op jit(solution)/shard_map/ppermute | solution.py:493
  98.3 3.2 %collective-permute-done.28 = f32[264,128]{1,0:T(8,128)S(1)} collective-permute-done((f32[264,128]{1,0:T(8,128)S(1)}, f32[264,128]{1,0:T(8,128)S(1)}, u32[]{:S(2)}, u32[]{:S(2)}) %collective-permute-start.28) | collective-permute-done | bytes 135200 | tf_op jit(solution)/shard_map/ppermute | solution.py:493
  102.0 1.5 %collective-permute-done.31.refs_1_ = f32[1056,128]{1,0:T(8,128)S(1)} collective-permute-done((f32[1056,128]{1,0:T(8,128)S(1)}, f32[1056,128]{1,0:T(8,128)S(1)}, u32[]{:S(2)}, u32[]{:S(2)}) %collective-permute-start.31) | collective-permute-done | bytes 540704 | tf_op jit(solution)/shard_map/ppermute | solution.py:493
  103.5 2.2 %first_part.3 = (f32[1024,256]{1,0:T(8,128)S(1)}, bf16[1024,1024]{1,0:T(8,128)(2,1)S(1)}, bf16[1024,1024]{1,0:T(8,128)(2,1)S(1)}) custom-call(s32[1]{0:T(128)} %bitcast.me_ref, f32[1056,128]{1,0:T(8,128)S(1)} %pad_maximum_fusion.2.refs_0_, f32[1056,128]{1,0:T(8,128)S(1)} %collective-permute-done.31.refs_1_, bf16[1024,1024]{1,0:T(8,128)(2,1)S(1)} %cut.6.refs_2_.ah, ...), custom_call_target="tpu_custom_call" | custom-call | flops 32212254720 | bytes 125829120 | tf_op jit(solution)/shard_map/first_part/pallas_call | solution.py:330
  106.0 1.8 %other_part.1.refs_5_ = f32[1024,768]{1,0:T(8,128)S(1)} custom-call(bf16[1024,1024]{1,0:T(8,128)(2,1)S(1)} %cut.6.refs_2_.ah, bf16[1024,1024]{1,0:T(8,128)(2,1)S(1)} %cut.7.refs_3_.al, bf16[1024,1024]{1,0:T(8,128)(2,1)S(1)} %get-tuple-element.396.hi, bf16[1024,1024]{1,0:T(8,128)(2,1)S(1)} %get-tuple-element.397.lo, ...), custom_call_target="tpu_custom_call" | custom-call | flops 16106127360 | bytes 125829120 | tf_op jit(solution)/shard_map/other_part/pallas_call | solution.py:345
  107.8 5.1 %last.1 = f32[1024,1024]{1,0:T(8,128)} custom-call(s32[1]{0:T(128)} %bitcast.me_ref, f32[1056,128]{1,0:T(8,128)S(1)} %pad_maximum_fusion.3.refs_0_, f32[1056,128]{1,0:T(8,128)S(1)} %collective-permute-done.35.refs_1_, bf16[1024,1024]{1,0:T(8,128)(2,1)S(1)} %cut.6.refs_2_.ah, bf16[1024,1024]{1,0:T(8,128)(2,1)S(1)} %cut.7.refs_3_.al, ...), custom_call_target="tpu_custom_call" | custom-call | flops 32212254720 | bytes 125829120 | tf_op jit(solution)/shard_map/last/pallas_call | solution.py:470
  (90 shorter events, 12.8 us)
Async XLA Ops:
  6.9 4.2 %collective-permute-start = (f32[1056,128]{1,0:T(8,128)S(1)}, f32[1056,128]{1,0:T(8,128)S(1)}, u32[]{:S(2)}, u32[]{:S(2)}) collective-permute-start(f32[1056,128]{1,0:T(8,128)S(1)} %get-tuple-element.210), channel_id=1, source_target_pairs={{0,1},{1,0},{2,3},{3,2},{4,5},{5,4},{6,7},{7,6},{8,9},{9,8},{10,11... | collective-permute-start | bytes 1622024 | tf_op jit(solution)/shard_map/ppermute | solution.py:493
  11.2 13.7 %collective-permute-start.4 = (f32[264,128]{1,0:T(8,128)S(1)}, f32[264,128]{1,0:T(8,128)S(1)}, u32[]{:S(2)}, u32[]{:S(2)}) collective-permute-start(f32[264,128]{1,0:T(8,128)S(1)} %get-tuple-element.412), channel_id=1, source_target_pairs={{0,2},{1,3},{2,0},{3,1},{4,6},{5,7},{6,4},{7,5},{8,10},{9,11},{10,... | collective-permute-start | bytes 405512 | tf_op jit(solution)/shard_map/ppermute | solution.py:493
  13.8 11.2 %collective-permute-start.3 = (f32[264,128]{1,0:T(8,128)S(1)}, f32[264,128]{1,0:T(8,128)S(1)}, u32[]{:S(2)}, u32[]{:S(2)}) collective-permute-start(f32[264,128]{1,0:T(8,128)S(1)} %get-tuple-element.413), channel_id=1, source_target_pairs={{0,4},{1,5},{2,6},{3,7},{4,0},{5,1},{6,2},{7,3},{8,12},{9,13},{10,... | collective-permute-start | bytes 405512 | tf_op jit(solution)/shard_map/ppermute | solution.py:493
  15.4 9.6 %collective-permute-start.2 = (f32[264,128]{1,0:T(8,128)S(1)}, f32[264,128]{1,0:T(8,128)S(1)}, u32[]{:S(2)}, u32[]{:S(2)}) collective-permute-start(f32[264,128]{1,0:T(8,128)S(1)} %get-tuple-element.414), channel_id=1, source_target_pairs={{0,6},{1,7},{2,4},{3,5},{4,2},{5,3},{6,0},{7,1},{8,14},{9,15},{10,... | collective-permute-start | bytes 405512 | tf_op jit(solution)/shard_map/ppermute | solution.py:493
  15.4 4.4 %collective-permute-start.1 = (f32[1056,128]{1,0:T(8,128)S(1)}, f32[1056,128]{1,0:T(8,128)S(1)}, u32[]{:S(2)}, u32[]{:S(2)}) collective-permute-start(f32[1056,128]{1,0:T(8,128)S(1)} %get-tuple-element.216), channel_id=1, source_target_pairs={{0,1},{1,0},{2,3},{3,2},{4,5},{5,4},{6,7},{7,6},{8,9},{9,8},{10,11... | collective-permute-start | bytes 1622024 | tf_op jit(solution)/shard_map/ppermute | solution.py:493
  19.8 13.4 %collective-permute-start.7 = (f32[264,128]{1,0:T(8,128)S(1)}, f32[264,128]{1,0:T(8,128)S(1)}, u32[]{:S(2)}, u32[]{:S(2)}) collective-permute-start(f32[264,128]{1,0:T(8,128)S(1)} %get-tuple-element.409), channel_id=1, source_target_pairs={{0,2},{1,3},{2,0},{3,1},{4,6},{5,7},{6,4},{7,5},{8,10},{9,11},{10,... | collective-permute-start | bytes 405512 | tf_op jit(solution)/shard_map/ppermute | solution.py:493
  21.8 11.4 %collective-permute-start.6 = (f32[264,128]{1,0:T(8,128)S(1)}, f32[264,128]{1,0:T(8,128)S(1)}, u32[]{:S(2)}, u32[]{:S(2)}) collective-permute-start(f32[264,128]{1,0:T(8,128)S(1)} %get-tuple-element.410), channel_id=1, source_target_pairs={{0,4},{1,5},{2,6},{3,7},{4,0},{5,1},{6,2},{7,3},{8,12},{9,13},{10,... | collective-permute-start | bytes 405512 | tf_op jit(solution)/shard_map/ppermute | solution.py:493
  24.9 9.3 %collective-permute-start.5 = (f32[264,128]{1,0:T(8,128)S(1)}, f32[264,128]{1,0:T(8,128)S(1)}, u32[]{:S(2)}, u32[]{:S(2)}) collective-permute-start(f32[264,128]{1,0:T(8,128)S(1)} %get-tuple-element.411), channel_id=1, source_target_pairs={{0,6},{1,7},{2,4},{3,5},{4,2},{5,3},{6,0},{7,1},{8,14},{9,15},{10,... | collective-permute-start | bytes 405512 | tf_op jit(solution)/shard_map/ppermute | solution.py:493
  25.1 10.0 %collective-permute-start.8 = (f32[264,128]{1,0:T(8,128)S(1)}, f32[264,128]{1,0:T(8,128)S(1)}, u32[]{:S(2)}, u32[]{:S(2)}) collective-permute-start(f32[264,128]{1,0:T(8,128)S(1)} %fusion.7), channel_id=1, source_target_pairs={{0,8},{1,9},{2,10},{3,11},{4,12},{5,13},{6,14},{7,15},{8,0},{9,1},... | collective-permute-start | bytes 405512 | tf_op jit(solution)/shard_map/ppermute | solution.py:493
  34.2 8.4 %collective-permute-start.9 = (f32[264,128]{1,0:T(8,128)S(1)}, f32[264,128]{1,0:T(8,128)S(1)}, u32[]{:S(2)}, u32[]{:S(2)}) collective-permute-start(f32[264,128]{1,0:T(8,128)S(1)} %fusion.5), channel_id=1, source_target_pairs={{0,8},{1,9},{2,10},{3,11},{4,12},{5,13},{6,14},{7,15},{8,0},{9,1},... | collective-permute-start | bytes 405512 | tf_op jit(solution)/shard_map/ppermute | solution.py:493
  35.1 8.9 %collective-permute-start.12 = (f32[264,128]{1,0:T(8,128)S(1)}, f32[264,128]{1,0:T(8,128)S(1)}, u32[]{:S(2)}, u32[]{:S(2)}) collective-permute-start(f32[264,128]{1,0:T(8,128)S(1)} %add.82), channel_id=1, source_target_pairs={{0,2},{1,3},{2,0},{3,1},{4,6},{5,7},{6,4},{7,5},{8,10},{9,11},{10,... | collective-permute-start | bytes 405512 | tf_op jit(solution)/shard_map/ppermute | solution.py:493
  35.6 11.2 %collective-permute-start.11 = (f32[264,128]{1,0:T(8,128)S(1)}, f32[264,128]{1,0:T(8,128)S(1)}, u32[]{:S(2)}, u32[]{:S(2)}) collective-permute-start(f32[264,128]{1,0:T(8,128)S(1)} %add.82), channel_id=1, source_target_pairs={{0,4},{1,5},{2,6},{3,7},{4,0},{5,1},{6,2},{7,3},{8,12},{9,13},{10,... | collective-permute-start | bytes 405512 | tf_op jit(solution)/shard_map/ppermute | solution.py:493
  39.2 7.7 %collective-permute-start.10 = (f32[264,128]{1,0:T(8,128)S(1)}, f32[264,128]{1,0:T(8,128)S(1)}, u32[]{:S(2)}, u32[]{:S(2)}) collective-permute-start(f32[264,128]{1,0:T(8,128)S(1)} %add.82), channel_id=1, source_target_pairs={{0,6},{1,7},{2,4},{3,5},{4,2},{5,3},{6,0},{7,1},{8,14},{9,15},{10,... | collective-permute-start | bytes 405512 | tf_op jit(solution)/shard_map/ppermute | solution.py:493
  42.7 10.0 %collective-permute-start.16 = (f32[264,128]{1,0:T(8,128)S(1)}, f32[264,128]{1,0:T(8,128)S(1)}, u32[]{:S(2)}, u32[]{:S(2)}) collective-permute-start(f32[264,128]{1,0:T(8,128)S(1)} %add.83), channel_id=1, source_target_pairs={{0,2},{1,3},{2,0},{3,1},{4,6},{5,7},{6,4},{7,5},{8,10},{9,11},{10,... | collective-permute-start | bytes 405512 | tf_op jit(solution)/shard_map/ppermute | solution.py:493
  43.7 9.0 %collective-permute-start.15 = (f32[264,128]{1,0:T(8,128)S(1)}, f32[264,128]{1,0:T(8,128)S(1)}, u32[]{:S(2)}, u32[]{:S(2)}) collective-permute-start(f32[264,128]{1,0:T(8,128)S(1)} %add.83), channel_id=1, source_target_pairs={{0,4},{1,5},{2,6},{3,7},{4,0},{5,1},{6,2},{7,3},{8,12},{9,13},{10,... | collective-permute-start | bytes 405512 | tf_op jit(solution)/shard_map/ppermute | solution.py:493
  44.0 8.7 %collective-permute-start.14 = (f32[264,128]{1,0:T(8,128)S(1)}, f32[264,128]{1,0:T(8,128)S(1)}, u32[]{:S(2)}, u32[]{:S(2)}) collective-permute-start(f32[264,128]{1,0:T(8,128)S(1)} %add.83), channel_id=1, source_target_pairs={{0,6},{1,7},{2,4},{3,5},{4,2},{5,3},{6,0},{7,1},{8,14},{9,15},{10,... | collective-permute-start | bytes 405512 | tf_op jit(solution)/shard_map/ppermute | solution.py:493
  61.0 4.3 %collective-permute-start.18 = (f32[1056,128]{1,0:T(8,128)S(1)}, f32[1056,128]{1,0:T(8,128)S(1)}, u32[]{:S(2)}, u32[]{:S(2)}) collective-permute-start(f32[1056,128]{1,0:T(8,128)S(1)} %get-tuple-element.326), channel_id=1, source_target_pairs={{0,1},{1,0},{2,3},{3,2},{4,5},{5,4},{6,7},{7,6},{8,9},{9,8},{10,11... | collective-permute-start | bytes 1622024 | tf_op jit(solution)/shard_map/ppermute | solution.py:493
  65.4 9.2 %collective-permute-start.22 = (f32[264,128]{1,0:T(8,128)S(1)}, f32[264,128]{1,0:T(8,128)S(1)}, u32[]{:S(2)}, u32[]{:S(2)}) collective-permute-start(f32[264,128]{1,0:T(8,128)S(1)} %get-tuple-element.406), channel_id=1, source_target_pairs={{0,2},{1,3},{2,0},{3,1},{4,6},{5,7},{6,4},{7,5},{8,10},{9,11},{10,... | collective-permute-start | bytes 405512 | tf_op jit(solution)/shard_map/ppermute | solution.py:493
  66.6 10.4 %collective-permute-start.21 = (f32[264,128]{1,0:T(8,128)S(1)}, f32[264,128]{1,0:T(8,128)S(1)}, u32[]{:S(2)}, u32[]{:S(2)}) collective-permute-start(f32[264,128]{1,0:T(8,128)S(1)} %get-tuple-element.407), channel_id=1, source_target_pairs={{0,4},{1,5},{2,6},{3,7},{4,0},{5,1},{6,2},{7,3},{8,12},{9,13},{10,... | collective-permute-start | bytes 405512 | tf_op jit(solution)/shard_map/ppermute | solution.py:493
  66.6 10.4 %collective-permute-start.20 = (f32[264,128]{1,0:T(8,128)S(1)}, f32[264,128]{1,0:T(8,128)S(1)}, u32[]{:S(2)}, u32[]{:S(2)}) collective-permute-start(f32[264,128]{1,0:T(8,128)S(1)} %get-tuple-element.408), channel_id=1, source_target_pairs={{0,6},{1,7},{2,4},{3,5},{4,2},{5,3},{6,0},{7,1},{8,14},{9,15},{10,... | collective-permute-start | bytes 405512 | tf_op jit(solution)/shard_map/ppermute | solution.py:493
  69.0 4.1 %collective-permute-start.19 = (f32[1056,128]{1,0:T(8,128)S(1)}, f32[1056,128]{1,0:T(8,128)S(1)}, u32[]{:S(2)}, u32[]{:S(2)}) collective-permute-start(f32[1056,128]{1,0:T(8,128)S(1)} %get-tuple-element.334), channel_id=1, source_target_pairs={{0,1},{1,0},{2,3},{3,2},{4,5},{5,4},{6,7},{7,6},{8,9},{9,8},{10,11... | collective-permute-start | bytes 1622024 | tf_op jit(solution)/shard_map/ppermute | solution.py:493
  73.1 12.3 %collective-permute-start.25 = (f32[264,128]{1,0:T(8,128)S(1)}, f32[264,128]{1,0:T(8,128)S(1)}, u32[]{:S(2)}, u32[]{:S(2)}) collective-permute-start(f32[264,128]{1,0:T(8,128)S(1)} %get-tuple-element.403), channel_id=1, source_target_pairs={{0,2},{1,3},{2,0},{3,1},{4,6},{5,7},{6,4},{7,5},{8,10},{9,11},{10,... | collective-permute-start | bytes 405512 | tf_op jit(solution)/shard_map/ppermute | solution.py:493
  74.4 11.1 %collective-permute-start.24 = (f32[264,128]{1,0:T(8,128)S(1)}, f32[264,128]{1,0:T(8,128)S(1)}, u32[]{:S(2)}, u32[]{:S(2)}) collective-permute-start(f32[264,128]{1,0:T(8,128)S(1)} %get-tuple-element.404), channel_id=1, source_target_pairs={{0,4},{1,5},{2,6},{3,7},{4,0},{5,1},{6,2},{7,3},{8,12},{9,13},{10,... | collective-permute-start | bytes 405512 | tf_op jit(solution)/shard_map/ppermute | solution.py:493
  74.6 11.6 %collective-permute-start.23 = (f32[264,128]{1,0:T(8,128)S(1)}, f32[264,128]{1,0:T(8,128)S(1)}, u32[]{:S(2)}, u32[]{:S(2)}) collective-permute-start(f32[264,128]{1,0:T(8,128)S(1)} %get-tuple-element.405), channel_id=1, source_target_pairs={{0,6},{1,7},{2,4},{3,5},{4,2},{5,3},{6,0},{7,1},{8,14},{9,15},{10,... | collective-permute-start | bytes 405512 | tf_op jit(solution)/shard_map/ppermute | solution.py:493
  77.1 11.3 %collective-permute-start.26 = (f32[264,128]{1,0:T(8,128)S(1)}, f32[264,128]{1,0:T(8,128)S(1)}, u32[]{:S(2)}, u32[]{:S(2)}) collective-permute-start(f32[264,128]{1,0:T(8,128)S(1)} %fusion.1), channel_id=1, source_target_pairs={{0,8},{1,9},{2,10},{3,11},{4,12},{5,13},{6,14},{7,15},{8,0},{9,1},... | collective-permute-start | bytes 405512 | tf_op jit(solution)/shard_map/ppermute | solution.py:493
  86.2 8.5 %collective-permute-start.27 = (f32[264,128]{1,0:T(8,128)S(1)}, f32[264,128]{1,0:T(8,128)S(1)}, u32[]{:S(2)}, u32[]{:S(2)}) collective-permute-start(f32[264,128]{1,0:T(8,128)S(1)} %fusion.3), channel_id=1, source_target_pairs={{0,8},{1,9},{2,10},{3,11},{4,12},{5,13},{6,14},{7,15},{8,0},{9,1},... | collective-permute-start | bytes 405512 | tf_op jit(solution)/shard_map/ppermute | solution.py:493
  88.4 8.0 %collective-permute-start.30 = (f32[264,128]{1,0:T(8,128)S(1)}, f32[264,128]{1,0:T(8,128)S(1)}, u32[]{:S(2)}, u32[]{:S(2)}) collective-permute-start(f32[264,128]{1,0:T(8,128)S(1)} %add.93), channel_id=1, source_target_pairs={{0,2},{1,3},{2,0},{3,1},{4,6},{5,7},{6,4},{7,5},{8,10},{9,11},{10,... | collective-permute-start | bytes 405512 | tf_op jit(solution)/shard_map/ppermute | solution.py:493
  88.5 9.8 %collective-permute-start.29 = (f32[264,128]{1,0:T(8,128)S(1)}, f32[264,128]{1,0:T(8,128)S(1)}, u32[]{:S(2)}, u32[]{:S(2)}) collective-permute-start(f32[264,128]{1,0:T(8,128)S(1)} %add.93), channel_id=1, source_target_pairs={{0,4},{1,5},{2,6},{3,7},{4,0},{5,1},{6,2},{7,3},{8,12},{9,13},{10,... | collective-permute-start | bytes 405512 | tf_op jit(solution)/shard_map/ppermute | solution.py:493
  91.9 9.6 %collective-permute-start.28 = (f32[264,128]{1,0:T(8,128)S(1)}, f32[264,128]{1,0:T(8,128)S(1)}, u32[]{:S(2)}, u32[]{:S(2)}) collective-permute-start(f32[264,128]{1,0:T(8,128)S(1)} %add.93), channel_id=1, source_target_pairs={{0,6},{1,7},{2,4},{3,5},{4,2},{5,3},{6,0},{7,1},{8,14},{9,15},{10,... | collective-permute-start | bytes 405512 | tf_op jit(solution)/shard_map/ppermute | solution.py:493
  94.7 11.0 %collective-permute-start.34 = (f32[264,128]{1,0:T(8,128)S(1)}, f32[264,128]{1,0:T(8,128)S(1)}, u32[]{:S(2)}, u32[]{:S(2)}) collective-permute-start(f32[264,128]{1,0:T(8,128)S(1)} %add.92), channel_id=1, source_target_pairs={{0,2},{1,3},{2,0},{3,1},{4,6},{5,7},{6,4},{7,5},{8,10},{9,11},{10,... | collective-permute-start | bytes 405512 | tf_op jit(solution)/shard_map/ppermute | solution.py:493
  96.4 9.3 %collective-permute-start.33 = (f32[264,128]{1,0:T(8,128)S(1)}, f32[264,128]{1,0:T(8,128)S(1)}, u32[]{:S(2)}, u32[]{:S(2)}) collective-permute-start(f32[264,128]{1,0:T(8,128)S(1)} %add.92), channel_id=1, source_target_pairs={{0,4},{1,5},{2,6},{3,7},{4,0},{5,1},{6,2},{7,3},{8,12},{9,13},{10,... | collective-permute-start | bytes 405512 | tf_op jit(solution)/shard_map/ppermute | solution.py:493
  96.4 9.4 %collective-permute-start.32 = (f32[264,128]{1,0:T(8,128)S(1)}, f32[264,128]{1,0:T(8,128)S(1)}, u32[]{:S(2)}, u32[]{:S(2)}) collective-permute-start(f32[264,128]{1,0:T(8,128)S(1)} %add.92), channel_id=1, source_target_pairs={{0,6},{1,7},{2,4},{3,5},{4,2},{5,3},{6,0},{7,1},{8,14},{9,15},{10,... | collective-permute-start | bytes 405512 | tf_op jit(solution)/shard_map/ppermute | solution.py:493
  (10 other events, 59.2 us)

commit v8 on v7

--- a/solution.py
+++ b/solution.py
@@ -250,36 +250,44 @@
     tiles(out_ref.shape[1], 256, step)
 
 
-def affine(a, b, half):
+THIRDS = ((0, 4), (1, 4), (1, 2))
+
+
+def row_part(part, rows, size):
+    at, parts = THIRDS[part]
+    return pl.BlockSpec((rows // parts, size), lambda r: (at, 0))
+
+
+def affine(a, b, part):
     rows, size = a.shape
-    block = lambda at: pl.BlockSpec((rows // 2, size), lambda r: (at, 0))
-    return call(
-        affine_kernel, "affine", struct(rows // 2, size), 18, 0.5, 2,
+    height = rows // THIRDS[part][1]
+    return call(
+        affine_kernel, "affine", struct(height, size), 18, height / rows, 2,
         grid=(1,),
-        in_specs=[block(half), pl.BlockSpec((size, size), lambda r: (0, 0))],
-        out_specs=block(0),
-        scratch_shapes=[pltpu.VMEM((rows // 2, size), BF16)] * 2,
+        in_specs=[row_part(part, rows, size), pl.BlockSpec((size, size), lambda r: (0, 0))],
+        out_specs=pl.BlockSpec((height, size), lambda r: (0, 0)),
+        scratch_shapes=[pltpu.VMEM((height, size), BF16)] * 2,
     )(a, b)
 
 
-def affine_parts_kernel(a_ref, ah, al, bh, bl, out_ref):
+def affine_parts_kernel(ah, al, b_ref, out_ref):
     def step(c):
-        product = mm((ah[...], al[...]), (bh[:, c], bl[:, c]))
-        out_ref[:, c] = 1.5 * a_ref[:, c] - 0.5 * product
+        product = mm((ah[...], al[...]), split(b_ref[:, c]))
+        out_ref[:, c] = 1.5 * (ah[:, c].astype(F32) + al[:, c].astype(F32)) - 0.5 * product
 
     tiles(out_ref.shape[1], 256, step)
 
 
-def affine_parts(a, ah, al, bh, bl, half):
-    rows, size = a.shape
-    block = lambda at: pl.BlockSpec((rows // 2, size), lambda r: (at, 0))
-    whole = pl.BlockSpec((size, size), lambda r: (0, 0))
-    return call(
-        affine_parts_kernel, "affine_parts", struct(rows // 2, size), 18, 0.5, 2,
+def affine_parts(ah, al, b, part):
+    rows, size = ah.shape
+    height = rows // THIRDS[part][1]
+    return call(
+        affine_parts_kernel, "affine_parts", struct(height, size), 18, height / rows, 2,
         grid=(1,),
-        in_specs=[block(half)] * 3 + [whole] * 2,
-        out_specs=block(0),
-    )(a, ah, al, bh, bl)
+        in_specs=[row_part(part, rows, size)] * 2
+        + [pl.BlockSpec((size, size), lambda r: (0, 0))],
+        out_specs=pl.BlockSpec((height, size), lambda r: (0, 0)),
+    )(ah, al, b)
 
 
 SPANS = (
@@ -378,36 +386,31 @@
     )(x)
 
 
-def cut_kernel(which, x_ref, *out_refs):
+def cut_kernel(x_ref, hi, lo):
     def step(r):
-        parts = split(x_ref[r])
-        for out_ref, k in zip(out_refs, which):
-            out_ref[r] = parts[k]
+        hi[r], lo[r] = split(x_ref[r])
 
     tiles(x_ref.shape[0], 128, step)
 
 
-def cut(x, *which):
-    count = len(which)
-    return call(
-        functools.partial(cut_kernel, which), "cut", [struct(*x.shape, dtype=BF16)] * count,
-        16, 0.1, 2, in_specs=[VMEM], out_specs=[VMEM] * count,
+def cut(x):
+    part = struct(*x.shape, dtype=BF16)
+    return call(
+        cut_kernel, "cut", [part, part], 16, 0.1, 2, in_specs=[VMEM], out_specs=[VMEM] * 2
     )(x)
 
 
 def second_gram_kernel(shards, count, me_ref, *refs):
     pieces, refs = refs[:count], refs[count:]
     (ah, al, base_ref, xh, xl, col_ref), refs = refs[:6], refs[6:]
-    keep_ref, send_ref, mid_ref, mh, ml, hi, lo, packed, g = refs
+    keep_ref, send_ref, mh, ml, hi, lo, packed, g = refs
     size = g.shape[0]
     q = size // 4
     unpack(pieces, packed, hi, lo, me_ref[0], shards, 1)
-    mid_ref[:, :q] = base_ref[:, :q]
     mh[:, :q], ml[:, :q] = split(base_ref[:, :q])
     for column in range(1, 4):
         c, product = sym_product(ah, al, hi, lo, 1, column)
         mid = base_ref[:, c] - 0.5 * product
-        mid_ref[:, c] = mid
         mh[:, c], ml[:, c] = split(mid)
     g[:, :q] = col_ref[...]
     g[:q, q:] = mm((xh[:q, :], xl[:q, :]), (mh[:, q:], ml[:, q:]))
@@ -420,9 +423,9 @@
     part = struct(rows, size, dtype=BF16)
     return call(
         functools.partial(second_gram_kernel, shards, len(pieces)), "second_gram",
-        halves(size, shards) + [struct(rows, size), part, part], 20, 0.8, 5,
+        halves(size, shards) + [part, part], 20, 0.8, 5,
         in_specs=[SMEM] + [VMEM] * (len(pieces) + 6),
-        out_specs=[VMEM] * 5,
+        out_specs=[VMEM] * 4,
         scratch_shapes=sym_scratch(size, shards) + [pltpu.VMEM((size, size), F32)],
     )(me, *pieces, ah, al, base, xh, xl, col)
 
@@ -574,24 +577,21 @@
         x0=orbitals_zero, x1=orbitals_one, s0=correlation_zero, s1=correlation_one, c=cotangent
     )
 
-    def half(part):
+    def direct(part):
         def work(env):
             env[f"m{part}"] = affine(env["c"], env["s1"], part)
         return work
 
-    def turned(env):
+    def direct_and_turn(env):
+        direct(2)(env)
         env["xh"], env["xl"] = turn(env["x0"])
 
-    def half_and_cut(env):
-        half(1)(env)
-        env["s0h"], env["s0l"] = cut(env["s0"], 0, 1)
-
-    def cut_orbitals(env):
-        env["x1h"], env["x1l"] = cut(env["x1"], 0, 1)
+    def cut_one(env):
+        env["x1h"], env["x1l"] = cut(env["x1"])
 
     def middle(env, pieces):
         (env["mid"],) = first_part(
-            me, SHARDS, pieces, env["x1h"], env["x1l"], [env["m0"], env["m1"]], (0, 1, 2, 3)
+            me, SHARDS, pieces, env["x1h"], env["x1l"], [env["m0"], env["m1"], env["m2"]], (0, 1, 2, 3)
         )
 
     def column(env):
@@ -600,40 +600,38 @@
     keep, send, *parts = first_gram(me, SHARDS, env["x1"], env["c"])
     one = sum_chunks(
         count, env, (keep, send), lambda env: other_gram(me, SHARDS, *parts),
-        [half(0), turned, half_and_cut, cut_orbitals], [middle, column],
-    )
-
-    keep, send, env["mid"], env["mh"], env["ml"] = second_gram(
+        [direct(0), direct(1), direct_and_turn, cut_one], [middle, column],
+    )
+
+    keep, send, env["mh"], env["ml"] = second_gram(
         me, SHARDS, one, env["x1h"], env["x1l"], env["mid"], env["xh"], env["xl"], env["col"]
     )
 
-    def half_parts(part):
+    def last_direct(part):
         def work(env):
-            env[f"d{part}"] = affine_parts(
-                env["mid"], env["mh"], env["ml"], env["s0h"], env["s0l"], part
-            )
+            env[f"d{part}"] = affine_parts(env["mh"], env["ml"], env["s0"], part)
         return work
 
-    def high(env):
-        (env["x0h"],) = cut(env["x0"], 0)
-
-    def low(env):
-        (env["x0l"],) = cut(env["x0"], 1)
+    def cut_zero(env):
+        env["x0h"], env["x0l"] = cut(env["x0"])
+
+    def three(name):
+        return [env[f"{name}{part}"] for part in range(3)]
 
     def result(env, pieces):
         env["z"], env["symh"], env["syml"] = first_part(
-            me, SHARDS, pieces, env["x0h"], env["x0l"], [env["d0"], env["d1"]], (0,)
+            me, SHARDS, pieces, env["x0h"], env["x0l"], three("d"), (0,)
         )
 
     def rest(env):
         env["rest"] = other_part(
-            env["x0h"], env["x0l"], env["symh"], env["syml"], [env["d0"], env["d1"]], (1, 2, 3)
+            env["x0h"], env["x0l"], env["symh"], env["syml"], three("d"), (1, 2, 3)
         )
 
     two = sum_chunks(
         count, env, (keep, send),
         lambda env: fourth_gram(me, SHARDS, env["xh"], env["xl"], env["mh"], env["ml"]),
-        [half_parts(0), high, half_parts(1), low], [result, rest],
+        [last_direct(0), last_direct(1), last_direct(2), cut_zero], [result, rest],
     )
     return last_step(me, SHARDS, two, env["x0h"], env["x0l"], env["z"], env["rest"])
 

time: 113 us -> 111 us (0.982)
  waiting for transfers between devices: 13.8 us -> 11.2 us
    ppermute x36, waiting for transfers between devices: 13.8 us -> 11.2 us  [swap(): return lax.ppermute(x, 'row', [(i, i ^ offset) for i in range(self.count)])]
  transfers between devices with their start and end apart: 36 -> 36, of which waited for: 9 -> 7; matrix products, arithmetic and copies ran while one was open for 0% -> 0% of each run, Pallas kernels for 33% -> 35%
where the time goes in v8:
time: 111 us
  Pallas kernels  56.7 us (51%)
  starting transfers between devices  41.2 us (37%)
  waiting for transfers between devices  11.2 us (10%)
    ppermute x36, starting transfers between devices, swap(): return lax.ppermute(x, 'row', [(i, i ^ offset) for i in range(self.count)])  41.2 us
    ppermute x36, waiting for transfers between devices, swap(): return lax.ppermute(x, 'row', [(i, i ^ offset) for i in range(self.count)])  11.2 us
    pallas_call x3, Pallas kernels, affine(): call(affine_kernel, 'affine', struct(height, size), 18, height / rows, 2,...  9.44 us
    pallas_call x3, Pallas kernels, affine_parts(): call(affine_parts_kernel, 'affine_parts', struct(height, size), 18, heigh...  8.96 us
    pallas_call x1, Pallas kernels, first_gram(): call(functools.partial(first_gram_kernel, shards), 'first_gram', halves(s...  6.9 us
    pallas_call x1, Pallas kernels, second_gram(): call(functools.partial(second_gram_kernel, shards, len(pieces)), 'second_...  6.04 us
    pallas_call x2, Pallas kernels, first_part(): call(functools.partial(first_part_kernel, shards, len(pieces), columns),...  5.99 us
    pallas_call x1, Pallas kernels, last_step(): call(functools.partial(last_kernel, shards, len(pieces)), 'last', struct(...  5.13 us
  transfers between devices with their start and end apart: 36, of which 7 were waited for; matrix products, arithmetic and copies ran while one was open for 0% of the time, Pallas kernels for 35%

profile of v8, /device:TPU:0, one launch (start us, length us, event | category | flops | bytes accessed | tf_op | source)
XLA Modules:
  0.0 110.5 jit_solution(16055214369202078659)
XLA Ops:
  0.0 6.9 %first_gram.1 = (f32[1056,128]{1,0:T(8,128)S(1)}, f32[1056,128]{1,0:T(8,128)S(1)}, bf16[1024,1024]{1,0:T(8,128)(2,1)S(1)}, bf16[1024,1024]{1,0:T(8,128)(2,1)S(1)...) custom-call(s32[1]{0:T(128)} %bitcast.me_ref, f32[1024,1024]{1,0:T(8,128)} %x_ref.1, f32[1024,1024]{1,0:T(8,128)} %a_ref.2), custom_call_target="tpu_custom_call" | custom-call | flops 32212254720 | bytes 167772160 | tf_op jit(solution)/shard_map/first_gram/pallas_call | solution.py:198
  7.4 3.6 %other_gram.1 = (f32[1056,128]{1,0:T(8,128)S(1)}, f32[1056,128]{1,0:T(8,128)S(1)}) custom-call(s32[1]{0:T(128)} %bitcast.me_ref, bf16[1024,1024]{1,0:T(8,128)(2,1)S(1)} %get-tuple-element.194.ah, bf16[1024,1024]{1,0:T(8,128)(2,1)S(1)} %get-tuple-element.195.al, bf16[1024,1024]{1,0:T(8,128)(2,1)S(1)} %get-tuple-element.196.bh, ...), custom_call_target="tpu_custom_call" | custom-call | flops 32212254720 | bytes 83886080 | tf_op jit(solution)/shard_map/other_gram/pallas_call | solution.py:228
  11.2 2.6 %collective-permute-start.4 = (f32[264,128]{1,0:T(8,128)S(1)}, f32[264,128]{1,0:T(8,128)S(1)}, u32[]{:S(2)}, u32[]{:S(2)}) collective-permute-start(f32[264,128]{1,0:T(8,128)S(1)} %get-tuple-element.392), channel_id=1, source_target_pairs={{0,2},{1,3},{2,0},{3,1},{4,6},{5,7},{6,4},{7,5},{8,10},{9,11},{10,... | collective-permute-start | bytes 405512 | tf_op jit(solution)/shard_map/ppermute | solution.py:496
  13.8 1.6 %collective-permute-start.3 = (f32[264,128]{1,0:T(8,128)S(1)}, f32[264,128]{1,0:T(8,128)S(1)}, u32[]{:S(2)}, u32[]{:S(2)}) collective-permute-start(f32[264,128]{1,0:T(8,128)S(1)} %get-tuple-element.393), channel_id=1, source_target_pairs={{0,4},{1,5},{2,6},{3,7},{4,0},{5,1},{6,2},{7,3},{8,12},{9,13},{10,... | collective-permute-start | bytes 405512 | tf_op jit(solution)/shard_map/ppermute | solution.py:496
  15.4 2.6 %affine.3.refs_4_ = f32[256,1024]{1,0:T(8,128)S(1)} custom-call(f32[1024,1024]{1,0:T(8,128)S(1)} %copy-done, f32[1024,1024]{1,0:T(8,128)S(1)} %copy-done.1), custom_call_target="tpu_custom_call" | custom-call | flops 16106127360 | bytes 83886080 | tf_op jit(solution)/shard_map/affine/pallas_call | solution.py:264
  18.1 1.9 %collective-permute-start.7 = (f32[264,128]{1,0:T(8,128)S(1)}, f32[264,128]{1,0:T(8,128)S(1)}, u32[]{:S(2)}, u32[]{:S(2)}) collective-permute-start(f32[264,128]{1,0:T(8,128)S(1)} %get-tuple-element.389), channel_id=1, source_target_pairs={{0,2},{1,3},{2,0},{3,1},{4,6},{5,7},{6,4},{7,5},{8,10},{9,11},{10,... | collective-permute-start | bytes 405512 | tf_op jit(solution)/shard_map/ppermute | solution.py:496
  20.0 1.6 %collective-permute-start.6 = (f32[264,128]{1,0:T(8,128)S(1)}, f32[264,128]{1,0:T(8,128)S(1)}, u32[]{:S(2)}, u32[]{:S(2)}) collective-permute-start(f32[264,128]{1,0:T(8,128)S(1)} %get-tuple-element.390), channel_id=1, source_target_pairs={{0,4},{1,5},{2,6},{3,7},{4,0},{5,1},{6,2},{7,3},{8,12},{9,13},{10,... | collective-permute-start | bytes 405512 | tf_op jit(solution)/shard_map/ppermute | solution.py:496
  21.6 2.6 %affine.4.refs_5_ = f32[256,1024]{1,0:T(8,128)S(1)} custom-call(f32[1024,1024]{1,0:T(8,128)S(1)} %copy-done, f32[1024,1024]{1,0:T(8,128)S(1)} %copy-done.1), custom_call_target="tpu_custom_call" | custom-call | flops 16106127360 | bytes 83886080 | tf_op jit(solution)/shard_map/affine/pallas_call | solution.py:264
  24.4 3.0 %collective-permute-start.8 = (f32[264,128]{1,0:T(8,128)S(1)}, f32[264,128]{1,0:T(8,128)S(1)}, u32[]{:S(2)}, u32[]{:S(2)}) collective-permute-start(f32[264,128]{1,0:T(8,128)S(1)} %fusion.7), channel_id=1, source_target_pairs={{0,8},{1,9},{2,10},{3,11},{4,12},{5,13},{6,14},{7,15},{8,0},{9,1},... | collective-permute-start | bytes 405512 | tf_op jit(solution)/shard_map/ppermute | solution.py:496
  27.4 4.3 %affine.5.refs_6_ = f32[512,1024]{1,0:T(8,128)S(1)} custom-call(f32[1024,1024]{1,0:T(8,128)S(1)} %copy-done, f32[1024,1024]{1,0:T(8,128)S(1)} %copy-done.1), custom_call_target="tpu_custom_call" | custom-call | flops 32212254720 | bytes 83886080 | tf_op jit(solution)/shard_map/affine/pallas_call | solution.py:264
  35.3 1.6 %collective-permute-start.11 = (f32[264,128]{1,0:T(8,128)S(1)}, f32[264,128]{1,0:T(8,128)S(1)}, u32[]{:S(2)}, u32[]{:S(2)}) collective-permute-start(f32[264,128]{1,0:T(8,128)S(1)} %add.82), channel_id=1, source_target_pairs={{0,4},{1,5},{2,6},{3,7},{4,0},{5,1},{6,2},{7,3},{8,12},{9,13},{10,... | collective-permute-start | bytes 405512 | tf_op jit(solution)/shard_map/ppermute | solution.py:496
  37.9 4.1 %collective-permute-done.9 = f32[264,128]{1,0:T(8,128)S(1)} collective-permute-done((f32[264,128]{1,0:T(8,128)S(1)}, f32[264,128]{1,0:T(8,128)S(1)}, u32[]{:S(2)}, u32[]{:S(2)}) %collective-permute-start.9) | collective-permute-done | bytes 135200 | tf_op jit(solution)/shard_map/ppermute | solution.py:496
  42.1 1.6 %collective-permute-start.16 = (f32[264,128]{1,0:T(8,128)S(1)}, f32[264,128]{1,0:T(8,128)S(1)}, u32[]{:S(2)}, u32[]{:S(2)}) collective-permute-start(f32[264,128]{1,0:T(8,128)S(1)} %add.83), channel_id=1, source_target_pairs={{0,2},{1,3},{2,0},{3,1},{4,6},{5,7},{6,4},{7,5},{8,10},{9,11},{10,... | collective-permute-start | bytes 405512 | tf_op jit(solution)/shard_map/ppermute | solution.py:496
  44.0 1.6 %collective-permute-start.14 = (f32[264,128]{1,0:T(8,128)S(1)}, f32[264,128]{1,0:T(8,128)S(1)}, u32[]{:S(2)}, u32[]{:S(2)}) collective-permute-start(f32[264,128]{1,0:T(8,128)S(1)} %add.83), channel_id=1, source_target_pairs={{0,6},{1,7},{2,4},{3,5},{4,2},{5,3},{6,0},{7,1},{8,14},{9,15},{10,... | collective-permute-start | bytes 405512 | tf_op jit(solution)/shard_map/ppermute | solution.py:496
  48.5 3.8 %first_part.2.mid_ref.refs_4_ = f32[1024,1024]{1,0:T(8,128)S(1)} custom-call(s32[1]{0:T(128)} %bitcast.me_ref, f32[1056,128]{1,0:T(8,128)S(1)} %pad_maximum_fusion.refs_0_, f32[1056,128]{1,0:T(8,128)S(1)} %collective-permute-done.13.refs_1_, bf16[1024,1024]{1,0:T(8,128)(2,1)S(1)} %get-tuple-element.299.refs_2_, ...), custom_call_target="tpu_custom_call" | custom-call | flops 32212254720 | bytes 125829120 | tf_op jit(solution)/shard_map/first_part/pallas_call | solution.py:338
  52.6 1.8 %column_product.1.refs_7_ = f32[1024,256]{1,0:T(8,128)S(1)} custom-call(bf16[1024,1024]{1,0:T(8,128)(2,1)S(1)} %get-tuple-element.297.xh.refs_5_, bf16[1024,1024]{1,0:T(8,128)(2,1)S(1)} %get-tuple-element.298.xl.refs_6_, f32[1024,1024]{1,0:T(8,128)S(1)} %first_part.2.mid_ref.refs_4_), custom_call_target="tpu_custom_call" | custom-call | flops 16106127360 | bytes 83886080 | tf_op jit(solution)/shard_map/column_product/pallas_call | solution.py:369
  54.4 6.0 %second_gram.1 = (f32[1056,128]{1,0:T(8,128)S(1)}, f32[1056,128]{1,0:T(8,128)S(1)}, bf16[1024,1024]{1,0:T(8,128)(2,1)S(1)}, bf16[1024,1024]{1,0:T(8,128)(2,1)S(1)}) custom-call(s32[1]{0:T(128)} %bitcast.me_ref, f32[1056,128]{1,0:T(8,128)S(1)} %pad_maximum_fusion.1.refs_0_, f32[1056,128]{1,0:T(8,128)S(1)} %collective-permute-done.17.refs_1_, ...), custom_call_target="tpu_custom_call" | custom-call | flops 51539607552 | bytes 209715200 | tf_op jit(solution)/shard_map/second_gram/pallas_call | solution.py:424
  60.9 3.8 %fourth_gram.1 = (f32[1056,128]{1,0:T(8,128)S(1)}, f32[1056,128]{1,0:T(8,128)S(1)}) custom-call(s32[1]{0:T(128)} %bitcast.me_ref, bf16[1024,1024]{1,0:T(8,128)(2,1)S(1)} %get-tuple-element.297.xh.refs_5_, bf16[1024,1024]{1,0:T(8,128)(2,1)S(1)} %get-tuple-element.298.xl.refs_6_, bf16[1024,1024]{1,0:T(8,128)(2,1)S(1)} %get-tuple-element.325.mh.ah, ...), custom_call_target="tpu_custom_call" | custom-call | flops 32212254720 | bytes 83886080 | tf_op jit(solution)/shard_map/fourth_gram/pallas_call | solution.py:441
  65.9 2.4 %collective-permute-start.20 = (f32[264,128]{1,0:T(8,128)S(1)}, f32[264,128]{1,0:T(8,128)S(1)}, u32[]{:S(2)}, u32[]{:S(2)}) collective-permute-start(f32[264,128]{1,0:T(8,128)S(1)} %get-tuple-element.388), channel_id=1, source_target_pairs={{0,6},{1,7},{2,4},{3,5},{4,2},{5,3},{6,0},{7,1},{8,14},{9,15},{10,... | collective-permute-start | bytes 405512 | tf_op jit(solution)/shard_map/ppermute | solution.py:496
  68.4 2.4 %affine_parts.3.refs_4_.refs_0_ = f32[256,1024]{1,0:T(8,128)S(1)} custom-call(bf16[1024,1024]{1,0:T(8,128)(2,1)S(1)} %get-tuple-element.325.mh.ah, bf16[1024,1024]{1,0:T(8,128)(2,1)S(1)} %get-tuple-element.326.ml.al, f32[1024,1024]{1,0:T(8,128)S(1)} %copy-done.3), custom_call_target="tpu_custom_call" | custom-call | flops 16106127360 | bytes 83886080 | tf_op jit(solution)/shard_map/affine_parts/pallas_call | solution.py:284
  72.0 2.5 %affine_parts.4.refs_5_.refs_1_ = f32[256,1024]{1,0:T(8,128)S(1)} custom-call(bf16[1024,1024]{1,0:T(8,128)(2,1)S(1)} %get-tuple-element.325.mh.ah, bf16[1024,1024]{1,0:T(8,128)(2,1)S(1)} %get-tuple-element.326.ml.al, f32[1024,1024]{1,0:T(8,128)S(1)} %copy-done.3), custom_call_target="tpu_custom_call" | custom-call | flops 16106127360 | bytes 83886080 | tf_op jit(solution)/shard_map/affine_parts/pallas_call | solution.py:284
  74.5 2.5 %collective-permute-start.23 = (f32[264,128]{1,0:T(8,128)S(1)}, f32[264,128]{1,0:T(8,128)S(1)}, u32[]{:S(2)}, u32[]{:S(2)}) collective-permute-start(f32[264,128]{1,0:T(8,128)S(1)} %get-tuple-element.385), channel_id=1, source_target_pairs={{0,6},{1,7},{2,4},{3,5},{4,2},{5,3},{6,0},{7,1},{8,14},{9,15},{10,... | collective-permute-start | bytes 405512 | tf_op jit(solution)/shard_map/ppermute | solution.py:496
  77.1 2.8 %collective-permute-start.26 = (f32[264,128]{1,0:T(8,128)S(1)}, f32[264,128]{1,0:T(8,128)S(1)}, u32[]{:S(2)}, u32[]{:S(2)}) collective-permute-start(f32[264,128]{1,0:T(8,128)S(1)} %fusion.1), channel_id=1, source_target_pairs={{0,8},{1,9},{2,10},{3,11},{4,12},{5,13},{6,14},{7,15},{8,0},{9,1},... | collective-permute-start | bytes 405512 | tf_op jit(solution)/shard_map/ppermute | solution.py:496
  79.8 4.1 %affine_parts.5.refs_6_.refs_2_ = f32[512,1024]{1,0:T(8,128)S(1)} custom-call(bf16[1024,1024]{1,0:T(8,128)(2,1)S(1)} %get-tuple-element.325.mh.ah, bf16[1024,1024]{1,0:T(8,128)(2,1)S(1)} %get-tuple-element.326.ml.al, f32[1024,1024]{1,0:T(8,128)S(1)} %copy-done.3), custom_call_target="tpu_custom_call" | custom-call | flops 32212254720 | bytes 83886080 | tf_op jit(solution)/shard_map/affine_parts/pallas_call | solution.py:284
  84.0 1.8 %collective-permute-start.27 = (f32[264,128]{1,0:T(8,128)S(1)}, f32[264,128]{1,0:T(8,128)S(1)}, u32[]{:S(2)}, u32[]{:S(2)}) collective-permute-start(f32[264,128]{1,0:T(8,128)S(1)} %fusion.3), channel_id=1, source_target_pairs={{0,8},{1,9},{2,10},{3,11},{4,12},{5,13},{6,14},{7,15},{8,0},{9,1},... | collective-permute-start | bytes 405512 | tf_op jit(solution)/shard_map/ppermute | solution.py:496
  87.2 2.7 %collective-permute-start.29 = (f32[264,128]{1,0:T(8,128)S(1)}, f32[264,128]{1,0:T(8,128)S(1)}, u32[]{:S(2)}, u32[]{:S(2)}) collective-permute-start(f32[264,128]{1,0:T(8,128)S(1)} %add.93), channel_id=1, source_target_pairs={{0,4},{1,5},{2,6},{3,7},{4,0},{5,1},{6,2},{7,3},{8,12},{9,13},{10,... | collective-permute-start | bytes 405512 | tf_op jit(solution)/shard_map/ppermute | solution.py:496
  91.2 1.6 %collective-permute-done.27 = f32[264,128]{1,0:T(8,128)S(1)} collective-permute-done((f32[264,128]{1,0:T(8,128)S(1)}, f32[264,128]{1,0:T(8,128)S(1)}, u32[]{:S(2)}, u32[]{:S(2)}) %collective-permute-start.27) | collective-permute-done | bytes 135200 | tf_op jit(solution)/shard_map/ppermute | solution.py:496
  93.6 3.2 %collective-permute-start.32 = (f32[264,128]{1,0:T(8,128)S(1)}, f32[264,128]{1,0:T(8,128)S(1)}, u32[]{:S(2)}, u32[]{:S(2)}) collective-permute-start(f32[264,128]{1,0:T(8,128)S(1)} %add.92), channel_id=1, source_target_pairs={{0,6},{1,7},{2,4},{3,5},{4,2},{5,3},{6,0},{7,1},{8,14},{9,15},{10,... | collective-permute-start | bytes 405512 | tf_op jit(solution)/shard_map/ppermute | solution.py:496
  96.7 2.1 %collective-permute-done.28 = f32[264,128]{1,0:T(8,128)S(1)} collective-permute-done((f32[264,128]{1,0:T(8,128)S(1)}, f32[264,128]{1,0:T(8,128)S(1)}, u32[]{:S(2)}, u32[]{:S(2)}) %collective-permute-start.28) | collective-permute-done | bytes 135200 | tf_op jit(solution)/shard_map/ppermute | solution.py:496
  100.9 2.2 %first_part.3 = (f32[1024,256]{1,0:T(8,128)S(1)}, bf16[1024,1024]{1,0:T(8,128)(2,1)S(1)}, bf16[1024,1024]{1,0:T(8,128)(2,1)S(1)}) custom-call(s32[1]{0:T(128)} %bitcast.me_ref, f32[1056,128]{1,0:T(8,128)S(1)} %pad_maximum_fusion.2.refs_0_, f32[1056,128]{1,0:T(8,128)S(1)} %collective-permute-done.31.refs_1_, ...), custom_call_target="tpu_custom_call" | custom-call | flops 32212254720 | bytes 125829120 | tf_op jit(solution)/shard_map/first_part/pallas_call | solution.py:338
  103.4 1.8 %other_part.1.refs_5_ = f32[1024,768]{1,0:T(8,128)S(1)} custom-call(bf16[1024,1024]{1,0:T(8,128)(2,1)S(1)} %get-tuple-element.379.refs_2_.ah, bf16[1024,1024]{1,0:T(8,128)(2,1)S(1)} %get-tuple-element.380.refs_3_.al, bf16[1024,1024]{1,0:T(8,128)(2,1)S(1)} %get-tuple-element.376.hi, bf16[1024,1024]{1,0:T(8,128)(2,1)S(1)} %get-tuple-element.377.lo, ...), custom_call_target="tpu_custom_call" | custom-call | flops 16106127360 | bytes 125829120 | tf_op jit(solution)/shard_map/other_part/pallas_call | solution.py:353
  105.2 5.1 %last.1 = f32[1024,1024]{1,0:T(8,128)} custom-call(s32[1]{0:T(128)} %bitcast.me_ref, f32[1056,128]{1,0:T(8,128)S(1)} %pad_maximum_fusion.3.refs_0_, f32[1056,128]{1,0:T(8,128)S(1)} %collective-permute-done.35.refs_1_, bf16[1024,1024]{1,0:T(8,128)(2,1)S(1)} %get-tuple-element.379.refs_2_.ah, bf16[1024,1024]{1,0:T(8,128)(2,1)S(1)} %get-tuple-element.380.refs_3_.al, ...), custom_call_target="tpu_custom_call" | custom-call | flops 32212254720 | bytes 125829120 | tf_op jit(solution)/shard_map/last/pallas_call | solution.py:473
  (90 shorter events, 17.5 us)
Async XLA Ops:
  6.9 4.2 %collective-permute-start = (f32[1056,128]{1,0:T(8,128)S(1)}, f32[1056,128]{1,0:T(8,128)S(1)}, u32[]{:S(2)}, u32[]{:S(2)}) collective-permute-start(f32[1056,128]{1,0:T(8,128)S(1)} %get-tuple-element.200), channel_id=1, source_target_pairs={{0,1},{1,0},{2,3},{3,2},{4,5},{5,4},{6,7},{7,6},{8,9},{9,8},{10,11... | collective-permute-start | bytes 1622024 | tf_op jit(solution)/shard_map/ppermute | solution.py:496
  11.2 13.0 %collective-permute-start.4 = (f32[264,128]{1,0:T(8,128)S(1)}, f32[264,128]{1,0:T(8,128)S(1)}, u32[]{:S(2)}, u32[]{:S(2)}) collective-permute-start(f32[264,128]{1,0:T(8,128)S(1)} %get-tuple-element.392), channel_id=1, source_target_pairs={{0,2},{1,3},{2,0},{3,1},{4,6},{5,7},{6,4},{7,5},{8,10},{9,11},{10,... | collective-permute-start | bytes 405512 | tf_op jit(solution)/shard_map/ppermute | solution.py:496
  13.8 10.5 %collective-permute-start.3 = (f32[264,128]{1,0:T(8,128)S(1)}, f32[264,128]{1,0:T(8,128)S(1)}, u32[]{:S(2)}, u32[]{:S(2)}) collective-permute-start(f32[264,128]{1,0:T(8,128)S(1)} %get-tuple-element.393), channel_id=1, source_target_pairs={{0,4},{1,5},{2,6},{3,7},{4,0},{5,1},{6,2},{7,3},{8,12},{9,13},{10,... | collective-permute-start | bytes 405512 | tf_op jit(solution)/shard_map/ppermute | solution.py:496
  15.4 8.9 %collective-permute-start.2 = (f32[264,128]{1,0:T(8,128)S(1)}, f32[264,128]{1,0:T(8,128)S(1)}, u32[]{:S(2)}, u32[]{:S(2)}) collective-permute-start(f32[264,128]{1,0:T(8,128)S(1)} %get-tuple-element.394), channel_id=1, source_target_pairs={{0,6},{1,7},{2,4},{3,5},{4,2},{5,3},{6,0},{7,1},{8,14},{9,15},{10,... | collective-permute-start | bytes 405512 | tf_op jit(solution)/shard_map/ppermute | solution.py:496
  15.4 2.6 %collective-permute-start.1 = (f32[1056,128]{1,0:T(8,128)S(1)}, f32[1056,128]{1,0:T(8,128)S(1)}, u32[]{:S(2)}, u32[]{:S(2)}) collective-permute-start(f32[1056,128]{1,0:T(8,128)S(1)} %get-tuple-element.206), channel_id=1, source_target_pairs={{0,1},{1,0},{2,3},{3,2},{4,5},{5,4},{6,7},{7,6},{8,9},{9,8},{10,11... | collective-permute-start | bytes 1622024 | tf_op jit(solution)/shard_map/ppermute | solution.py:496
  18.1 15.2 %collective-permute-start.7 = (f32[264,128]{1,0:T(8,128)S(1)}, f32[264,128]{1,0:T(8,128)S(1)}, u32[]{:S(2)}, u32[]{:S(2)}) collective-permute-start(f32[264,128]{1,0:T(8,128)S(1)} %get-tuple-element.389), channel_id=1, source_target_pairs={{0,2},{1,3},{2,0},{3,1},{4,6},{5,7},{6,4},{7,5},{8,10},{9,11},{10,... | collective-permute-start | bytes 405512 | tf_op jit(solution)/shard_map/ppermute | solution.py:496
  20.0 13.2 %collective-permute-start.6 = (f32[264,128]{1,0:T(8,128)S(1)}, f32[264,128]{1,0:T(8,128)S(1)}, u32[]{:S(2)}, u32[]{:S(2)}) collective-permute-start(f32[264,128]{1,0:T(8,128)S(1)} %get-tuple-element.390), channel_id=1, source_target_pairs={{0,4},{1,5},{2,6},{3,7},{4,0},{5,1},{6,2},{7,3},{8,12},{9,13},{10,... | collective-permute-start | bytes 405512 | tf_op jit(solution)/shard_map/ppermute | solution.py:496
  24.2 9.3 %collective-permute-start.5 = (f32[264,128]{1,0:T(8,128)S(1)}, f32[264,128]{1,0:T(8,128)S(1)}, u32[]{:S(2)}, u32[]{:S(2)}) collective-permute-start(f32[264,128]{1,0:T(8,128)S(1)} %get-tuple-element.391), channel_id=1, source_target_pairs={{0,6},{1,7},{2,4},{3,5},{4,2},{5,3},{6,0},{7,1},{8,14},{9,15},{10,... | collective-permute-start | bytes 405512 | tf_op jit(solution)/shard_map/ppermute | solution.py:496
  24.4 10.0 %collective-permute-start.8 = (f32[264,128]{1,0:T(8,128)S(1)}, f32[264,128]{1,0:T(8,128)S(1)}, u32[]{:S(2)}, u32[]{:S(2)}) collective-permute-start(f32[264,128]{1,0:T(8,128)S(1)} %fusion.7), channel_id=1, source_target_pairs={{0,8},{1,9},{2,10},{3,11},{4,12},{5,13},{6,14},{7,15},{8,0},{9,1},... | collective-permute-start | bytes 405512 | tf_op jit(solution)/shard_map/ppermute | solution.py:496
  33.6 8.5 %collective-permute-start.9 = (f32[264,128]{1,0:T(8,128)S(1)}, f32[264,128]{1,0:T(8,128)S(1)}, u32[]{:S(2)}, u32[]{:S(2)}) collective-permute-start(f32[264,128]{1,0:T(8,128)S(1)} %fusion.5), channel_id=1, source_target_pairs={{0,8},{1,9},{2,10},{3,11},{4,12},{5,13},{6,14},{7,15},{8,0},{9,1},... | collective-permute-start | bytes 405512 | tf_op jit(solution)/shard_map/ppermute | solution.py:496
  34.4 9.6 %collective-permute-start.12 = (f32[264,128]{1,0:T(8,128)S(1)}, f32[264,128]{1,0:T(8,128)S(1)}, u32[]{:S(2)}, u32[]{:S(2)}) collective-permute-start(f32[264,128]{1,0:T(8,128)S(1)} %add.82), channel_id=1, source_target_pairs={{0,2},{1,3},{2,0},{3,1},{4,6},{5,7},{6,4},{7,5},{8,10},{9,11},{10,... | collective-permute-start | bytes 405512 | tf_op jit(solution)/shard_map/ppermute | solution.py:496
  35.3 10.3 %collective-permute-start.11 = (f32[264,128]{1,0:T(8,128)S(1)}, f32[264,128]{1,0:T(8,128)S(1)}, u32[]{:S(2)}, u32[]{:S(2)}) collective-permute-start(f32[264,128]{1,0:T(8,128)S(1)} %add.82), channel_id=1, source_target_pairs={{0,4},{1,5},{2,6},{3,7},{4,0},{5,1},{6,2},{7,3},{8,12},{9,13},{10,... | collective-permute-start | bytes 405512 | tf_op jit(solution)/shard_map/ppermute | solution.py:496
  36.9 9.6 %collective-permute-start.10 = (f32[264,128]{1,0:T(8,128)S(1)}, f32[264,128]{1,0:T(8,128)S(1)}, u32[]{:S(2)}, u32[]{:S(2)}) collective-permute-start(f32[264,128]{1,0:T(8,128)S(1)} %add.82), channel_id=1, source_target_pairs={{0,6},{1,7},{2,4},{3,5},{4,2},{5,3},{6,0},{7,1},{8,14},{9,15},{10,... | collective-permute-start | bytes 405512 | tf_op jit(solution)/shard_map/ppermute | solution.py:496
  42.1 10.2 %collective-permute-start.16 = (f32[264,128]{1,0:T(8,128)S(1)}, f32[264,128]{1,0:T(8,128)S(1)}, u32[]{:S(2)}, u32[]{:S(2)}) collective-permute-start(f32[264,128]{1,0:T(8,128)S(1)} %add.83), channel_id=1, source_target_pairs={{0,2},{1,3},{2,0},{3,1},{4,6},{5,7},{6,4},{7,5},{8,10},{9,11},{10,... | collective-permute-start | bytes 405512 | tf_op jit(solution)/shard_map/ppermute | solution.py:496
  43.7 8.6 %collective-permute-start.15 = (f32[264,128]{1,0:T(8,128)S(1)}, f32[264,128]{1,0:T(8,128)S(1)}, u32[]{:S(2)}, u32[]{:S(2)}) collective-permute-start(f32[264,128]{1,0:T(8,128)S(1)} %add.83), channel_id=1, source_target_pairs={{0,4},{1,5},{2,6},{3,7},{4,0},{5,1},{6,2},{7,3},{8,12},{9,13},{10,... | collective-permute-start | bytes 405512 | tf_op jit(solution)/shard_map/ppermute | solution.py:496
  44.0 8.3 %collective-permute-start.14 = (f32[264,128]{1,0:T(8,128)S(1)}, f32[264,128]{1,0:T(8,128)S(1)}, u32[]{:S(2)}, u32[]{:S(2)}) collective-permute-start(f32[264,128]{1,0:T(8,128)S(1)} %add.83), channel_id=1, source_target_pairs={{0,6},{1,7},{2,4},{3,5},{4,2},{5,3},{6,0},{7,1},{8,14},{9,15},{10,... | collective-permute-start | bytes 405512 | tf_op jit(solution)/shard_map/ppermute | solution.py:496
  60.4 4.3 %collective-permute-start.18 = (f32[1056,128]{1,0:T(8,128)S(1)}, f32[1056,128]{1,0:T(8,128)S(1)}, u32[]{:S(2)}, u32[]{:S(2)}) collective-permute-start(f32[1056,128]{1,0:T(8,128)S(1)} %get-tuple-element.308), channel_id=1, source_target_pairs={{0,1},{1,0},{2,3},{3,2},{4,5},{5,4},{6,7},{7,6},{8,9},{9,8},{10,11... | collective-permute-start | bytes 1622024 | tf_op jit(solution)/shard_map/ppermute | solution.py:496
  64.8 9.7 %collective-permute-start.22 = (f32[264,128]{1,0:T(8,128)S(1)}, f32[264,128]{1,0:T(8,128)S(1)}, u32[]{:S(2)}, u32[]{:S(2)}) collective-permute-start(f32[264,128]{1,0:T(8,128)S(1)} %get-tuple-element.386), channel_id=1, source_target_pairs={{0,2},{1,3},{2,0},{3,1},{4,6},{5,7},{6,4},{7,5},{8,10},{9,11},{10,... | collective-permute-start | bytes 405512 | tf_op jit(solution)/shard_map/ppermute | solution.py:496
  65.6 11.4 %collective-permute-start.21 = (f32[264,128]{1,0:T(8,128)S(1)}, f32[264,128]{1,0:T(8,128)S(1)}, u32[]{:S(2)}, u32[]{:S(2)}) collective-permute-start(f32[264,128]{1,0:T(8,128)S(1)} %get-tuple-element.387), channel_id=1, source_target_pairs={{0,4},{1,5},{2,6},{3,7},{4,0},{5,1},{6,2},{7,3},{8,12},{9,13},{10,... | collective-permute-start | bytes 405512 | tf_op jit(solution)/shard_map/ppermute | solution.py:496
  65.9 11.1 %collective-permute-start.20 = (f32[264,128]{1,0:T(8,128)S(1)}, f32[264,128]{1,0:T(8,128)S(1)}, u32[]{:S(2)}, u32[]{:S(2)}) collective-permute-start(f32[264,128]{1,0:T(8,128)S(1)} %get-tuple-element.388), channel_id=1, source_target_pairs={{0,6},{1,7},{2,4},{3,5},{4,2},{5,3},{6,0},{7,1},{8,14},{9,15},{10,... | collective-permute-start | bytes 405512 | tf_op jit(solution)/shard_map/ppermute | solution.py:496
  68.4 2.5 %collective-permute-start.19 = (f32[1056,128]{1,0:T(8,128)S(1)}, f32[1056,128]{1,0:T(8,128)S(1)}, u32[]{:S(2)}, u32[]{:S(2)}) collective-permute-start(f32[1056,128]{1,0:T(8,128)S(1)} %get-tuple-element.314), channel_id=1, source_target_pairs={{0,1},{1,0},{2,3},{3,2},{4,5},{5,4},{6,7},{7,6},{8,9},{9,8},{10,11... | collective-permute-start | bytes 1622024 | tf_op jit(solution)/shard_map/ppermute | solution.py:496
  70.9 13.0 %collective-permute-start.25 = (f32[264,128]{1,0:T(8,128)S(1)}, f32[264,128]{1,0:T(8,128)S(1)}, u32[]{:S(2)}, u32[]{:S(2)}) collective-permute-start(f32[264,128]{1,0:T(8,128)S(1)} %get-tuple-element.383), channel_id=1, source_target_pairs={{0,2},{1,3},{2,0},{3,1},{4,6},{5,7},{6,4},{7,5},{8,10},{9,11},{10,... | collective-permute-start | bytes 405512 | tf_op jit(solution)/shard_map/ppermute | solution.py:496
  71.8 12.2 %collective-permute-start.24 = (f32[264,128]{1,0:T(8,128)S(1)}, f32[264,128]{1,0:T(8,128)S(1)}, u32[]{:S(2)}, u32[]{:S(2)}) collective-permute-start(f32[264,128]{1,0:T(8,128)S(1)} %get-tuple-element.384), channel_id=1, source_target_pairs={{0,4},{1,5},{2,6},{3,7},{4,0},{5,1},{6,2},{7,3},{8,12},{9,13},{10,... | collective-permute-start | bytes 405512 | tf_op jit(solution)/shard_map/ppermute | solution.py:496
  74.5 9.5 %collective-permute-start.23 = (f32[264,128]{1,0:T(8,128)S(1)}, f32[264,128]{1,0:T(8,128)S(1)}, u32[]{:S(2)}, u32[]{:S(2)}) collective-permute-start(f32[264,128]{1,0:T(8,128)S(1)} %get-tuple-element.385), channel_id=1, source_target_pairs={{0,6},{1,7},{2,4},{3,5},{4,2},{5,3},{6,0},{7,1},{8,14},{9,15},{10,... | collective-permute-start | bytes 405512 | tf_op jit(solution)/shard_map/ppermute | solution.py:496
  77.1 8.7 %collective-permute-start.26 = (f32[264,128]{1,0:T(8,128)S(1)}, f32[264,128]{1,0:T(8,128)S(1)}, u32[]{:S(2)}, u32[]{:S(2)}) collective-permute-start(f32[264,128]{1,0:T(8,128)S(1)} %fusion.1), channel_id=1, source_target_pairs={{0,8},{1,9},{2,10},{3,11},{4,12},{5,13},{6,14},{7,15},{8,0},{9,1},... | collective-permute-start | bytes 405512 | tf_op jit(solution)/shard_map/ppermute | solution.py:496
  84.0 8.8 %collective-permute-start.27 = (f32[264,128]{1,0:T(8,128)S(1)}, f32[264,128]{1,0:T(8,128)S(1)}, u32[]{:S(2)}, u32[]{:S(2)}) collective-permute-start(f32[264,128]{1,0:T(8,128)S(1)} %fusion.3), channel_id=1, source_target_pairs={{0,8},{1,9},{2,10},{3,11},{4,12},{5,13},{6,14},{7,15},{8,0},{9,1},... | collective-permute-start | bytes 405512 | tf_op jit(solution)/shard_map/ppermute | solution.py:496
  85.8 7.7 %collective-permute-start.30 = (f32[264,128]{1,0:T(8,128)S(1)}, f32[264,128]{1,0:T(8,128)S(1)}, u32[]{:S(2)}, u32[]{:S(2)}) collective-permute-start(f32[264,128]{1,0:T(8,128)S(1)} %add.93), channel_id=1, source_target_pairs={{0,2},{1,3},{2,0},{3,1},{4,6},{5,7},{6,4},{7,5},{8,10},{9,11},{10,... | collective-permute-start | bytes 405512 | tf_op jit(solution)/shard_map/ppermute | solution.py:496
  87.2 9.6 %collective-permute-start.29 = (f32[264,128]{1,0:T(8,128)S(1)}, f32[264,128]{1,0:T(8,128)S(1)}, u32[]{:S(2)}, u32[]{:S(2)}) collective-permute-start(f32[264,128]{1,0:T(8,128)S(1)} %add.93), channel_id=1, source_target_pairs={{0,4},{1,5},{2,6},{3,7},{4,0},{5,1},{6,2},{7,3},{8,12},{9,13},{10,... | collective-permute-start | bytes 405512 | tf_op jit(solution)/shard_map/ppermute | solution.py:496
  89.8 9.0 %collective-permute-start.28 = (f32[264,128]{1,0:T(8,128)S(1)}, f32[264,128]{1,0:T(8,128)S(1)}, u32[]{:S(2)}, u32[]{:S(2)}) collective-permute-start(f32[264,128]{1,0:T(8,128)S(1)} %add.93), channel_id=1, source_target_pairs={{0,6},{1,7},{2,4},{3,5},{4,2},{5,3},{6,0},{7,1},{8,14},{9,15},{10,... | collective-permute-start | bytes 405512 | tf_op jit(solution)/shard_map/ppermute | solution.py:496
  92.9 10.3 %collective-permute-start.34 = (f32[264,128]{1,0:T(8,128)S(1)}, f32[264,128]{1,0:T(8,128)S(1)}, u32[]{:S(2)}, u32[]{:S(2)}) collective-permute-start(f32[264,128]{1,0:T(8,128)S(1)} %add.92), channel_id=1, source_target_pairs={{0,2},{1,3},{2,0},{3,1},{4,6},{5,7},{6,4},{7,5},{8,10},{9,11},{10,... | collective-permute-start | bytes 405512 | tf_op jit(solution)/shard_map/ppermute | solution.py:496
  93.6 9.6 %collective-permute-start.33 = (f32[264,128]{1,0:T(8,128)S(1)}, f32[264,128]{1,0:T(8,128)S(1)}, u32[]{:S(2)}, u32[]{:S(2)}) collective-permute-start(f32[264,128]{1,0:T(8,128)S(1)} %add.92), channel_id=1, source_target_pairs={{0,4},{1,5},{2,6},{3,7},{4,0},{5,1},{6,2},{7,3},{8,12},{9,13},{10,... | collective-permute-start | bytes 405512 | tf_op jit(solution)/shard_map/ppermute | solution.py:496
  93.6 9.6 %collective-permute-start.32 = (f32[264,128]{1,0:T(8,128)S(1)}, f32[264,128]{1,0:T(8,128)S(1)}, u32[]{:S(2)}, u32[]{:S(2)}) collective-permute-start(f32[264,128]{1,0:T(8,128)S(1)} %add.92), channel_id=1, source_target_pairs={{0,6},{1,7},{2,4},{3,5},{4,2},{5,3},{6,0},{7,1},{8,14},{9,15},{10,... | collective-permute-start | bytes 405512 | tf_op jit(solution)/shard_map/ppermute | solution.py:496
  (10 other events, 72.9 us)

commit v9 on v8

--- a/solution.py
+++ b/solution.py
@@ -247,7 +247,7 @@
     def step(c):
         out_ref[:, c] = 1.5 * a_ref[:, c] - 0.5 * mm((hi[...], lo[...]), split(b_ref[:, c]))
 
-    tiles(out_ref.shape[1], 256, step)
+    tiles(out_ref.shape[1], min(512, out_ref.shape[0]), step)
 
 
 THIRDS = ((0, 4), (1, 4), (1, 2))
@@ -275,7 +275,7 @@
         product = mm((ah[...], al[...]), split(b_ref[:, c]))
         out_ref[:, c] = 1.5 * (ah[:, c].astype(F32) + al[:, c].astype(F32)) - 0.5 * product
 
-    tiles(out_ref.shape[1], 256, step)
+    tiles(out_ref.shape[1], min(512, out_ref.shape[0]), step)
 
 
 def affine_parts(ah, al, b, part):
@@ -296,11 +296,11 @@
 )
 
 
-def sym_product(ah, al, hi, lo, chunk, column):
+def sym_product(ah, al, hi, lo, chunk, column, rows=slice(None)):
     q = hi.shape[0] // 4
     spans = [slice(k0 * q, k1 * q) for k0, k1 in SPANS[chunk][column]]
     c = slice(column * q, (column + 1) * q)
-    a = [ref[:, k] for ref in (ah, ah, al) for k in spans]
+    a = [ref[rows, k] for ref in (ah, ah, al) for k in spans]
     b = [ref[k, c] for ref in (hi, lo, hi) for k in spans]
     return c, jnp.dot(
         jnp.concatenate(a, axis=1), jnp.concatenate(b, axis=0), preferred_element_type=F32
@@ -412,8 +412,8 @@
         c, product = sym_product(ah, al, hi, lo, 1, column)
         mid = base_ref[:, c] - 0.5 * product
         mh[:, c], ml[:, c] = split(mid)
+        g[:q, c] = mm((xh[:q, :], xl[:q, :]), (mh[:, c], ml[:, c]))
     g[:, :q] = col_ref[...]
-    g[:q, q:] = mm((xh[:q, :], xl[:q, :]), (mh[:, q:], ml[:, q:]))
     g[3 * q:, 3 * q:] = mm((xh[3 * q:, :], xl[3 * q:, :]), (mh[:, 3 * q:], ml[:, 3 * q:]))
     pack(g, packed, keep_ref, send_ref, me_ref[0], shards, 0)
 
@@ -452,18 +452,21 @@
     q = hi.shape[0] // 4
     copies = []
 
-    def send(src, column):
-        c = slice(column * q, (column + 1) * q)
-        copy = pltpu.make_async_copy(src, out_hbm.at[:, c], sems.at[column])
+    def send(src, rows, c):
+        copy = pltpu.make_async_copy(src, out_hbm.at[rows, c], sems.at[len(copies)])
         copy.start()
         copies.append(copy)
 
-    send(z_ref, 0)
+    count = out.shape[0]
+    send(z_ref, slice(0, count), slice(0, q))
     unpack(pieces, packed, hi, lo, me_ref[0], shards, 1)
     for column in (1, 2, 3):
-        c, product = sym_product(ah, al, hi, lo, 1, column)
-        out[:, c] = rest_ref[:, c.start - q:c.stop - q] - 0.5 * product
-        send(out.at[:, c], column)
+        parts = 2 if column == 3 else 1
+        for part in range(parts):
+            r = slice(part * count // parts, (part + 1) * count // parts)
+            c, product = sym_product(ah, al, hi, lo, 1, column, r)
+            out[r, c] = rest_ref[r, c.start - q:c.stop - q] - 0.5 * product
+            send(out.at[r, c], r, c)
     for copy in copies:
         copy.wait()
 
@@ -475,7 +478,7 @@
         in_specs=[SMEM] + [VMEM] * (len(pieces) + 4),
         out_specs=pl.BlockSpec(memory_space=pltpu.HBM),
         scratch_shapes=sym_scratch(size, shards)
-        + [pltpu.VMEM((rows, size), F32), pltpu.SemaphoreType.DMA((4,))],
+        + [pltpu.VMEM((rows, size), F32), pltpu.SemaphoreType.DMA((5,))],
     )(me, *pieces, ah, al, z, rest)
 
 

time: 111 us -> 116 us (1.045)
  Pallas kernels: 56.7 us -> 60.1 us
  waiting for transfers between devices: 11.2 us -> 14.1 us
    pallas_call x1, Pallas kernels: 6.04 us -> 10.5 us  [second_gram(): call(functools.partial(second_gram_kernel, shards, len(pieces)), 'second_...]
    ppermute x36, waiting for transfers between devices: 11.2 us -> 14.1 us  [swap(): return lax.ppermute(x, 'row', [(i, i ^ offset) for i in range(self.count)])]
  transfers between devices with their start and end apart: 36 -> 36, of which waited for: 7 -> 9; matrix products, arithmetic and copies ran while one was open for 0% -> 0% of each run, Pallas kernels for 35% -> 33%
where the time goes in v9:
time: 116 us
  Pallas kernels  60.1 us (52%)
  starting transfers between devices  40.1 us (35%)
  waiting for transfers between devices  14.1 us (12%)
    ppermute x36, starting transfers between devices, swap(): return lax.ppermute(x, 'row', [(i, i ^ offset) for i in range(self.count)])  40.1 us
    ppermute x36, waiting for transfers between devices, swap(): return lax.ppermute(x, 'row', [(i, i ^ offset) for i in range(self.count)])  14.1 us
    pallas_call x1, Pallas kernels, second_gram(): call(functools.partial(second_gram_kernel, shards, len(pieces)), 'second_...  10.5 us
    pallas_call x3, Pallas kernels, affine(): call(affine_kernel, 'affine', struct(height, size), 18, height / rows, 2,...  9.01 us
    pallas_call x3, Pallas kernels, affine_parts(): call(affine_parts_kernel, 'affine_parts', struct(height, size), 18, heigh...  8.55 us
    pallas_call x1, Pallas kernels, first_gram(): call(functools.partial(first_gram_kernel, shards), 'first_gram', halves(s...  6.9 us
    pallas_call x2, Pallas kernels, first_part(): call(functools.partial(first_part_kernel, shards, len(pieces), columns),...  5.99 us
    pallas_call x1, Pallas kernels, last_step(): call(functools.partial(last_kernel, shards, len(pieces)), 'last', struct(...  4.94 us
  transfers between devices with their start and end apart: 36, of which 9 were waited for; matrix products, arithmetic and copies ran while one was open for 0% of the time, Pallas kernels for 33%

profile of v9, /device:TPU:0, one launch (start us, length us, event | category | flops | bytes accessed | tf_op | source)
XLA Modules:
  0.0 115.7 jit_solution(2194614567324880511)
XLA Ops:
  0.0 6.9 %first_gram.1 = (f32[1056,128]{1,0:T(8,128)S(1)}, f32[1056,128]{1,0:T(8,128)S(1)}, bf16[1024,1024]{1,0:T(8,128)(2,1)S(1)}, bf16[1024,1024]{1,0:T(8,128)(2,1)S(1)...) custom-call(s32[1]{0:T(128)} %bitcast.me_ref, f32[1024,1024]{1,0:T(8,128)} %x_ref.1, f32[1024,1024]{1,0:T(8,128)} %a_ref.2), custom_call_target="tpu_custom_call" | custom-call | flops 32212254720 | bytes 167772160 | tf_op jit(solution)/shard_map/first_gram/pallas_call | solution.py:198
  7.4 3.6 %other_gram.1 = (f32[1056,128]{1,0:T(8,128)S(1)}, f32[1056,128]{1,0:T(8,128)S(1)}) custom-call(s32[1]{0:T(128)} %bitcast.me_ref, bf16[1024,1024]{1,0:T(8,128)(2,1)S(1)} %get-tuple-element.194.ah, bf16[1024,1024]{1,0:T(8,128)(2,1)S(1)} %get-tuple-element.195.al, bf16[1024,1024]{1,0:T(8,128)(2,1)S(1)} %get-tuple-element.196.bh, ...), custom_call_target="tpu_custom_call" | custom-call | flops 32212254720 | bytes 83886080 | tf_op jit(solution)/shard_map/other_gram/pallas_call | solution.py:228
  11.2 2.6 %collective-permute-start.4 = (f32[264,128]{1,0:T(8,128)S(1)}, f32[264,128]{1,0:T(8,128)S(1)}, u32[]{:S(2)}, u32[]{:S(2)}) collective-permute-start(f32[264,128]{1,0:T(8,128)S(1)} %get-tuple-element.392), channel_id=1, source_target_pairs={{0,2},{1,3},{2,0},{3,1},{4,6},{5,7},{6,4},{7,5},{8,10},{9,11},{10,... | collective-permute-start | bytes 405512 | tf_op jit(solution)/shard_map/ppermute | solution.py:499
  15.4 2.6 %affine.3.refs_4_ = f32[256,1024]{1,0:T(8,128)S(1)} custom-call(f32[1024,1024]{1,0:T(8,128)S(1)} %copy-done, f32[1024,1024]{1,0:T(8,128)S(1)} %copy-done.1), custom_call_target="tpu_custom_call" | custom-call | flops 16106127360 | bytes 83886080 | tf_op jit(solution)/shard_map/affine/pallas_call | solution.py:264
  18.1 1.9 %collective-permute-start.7 = (f32[264,128]{1,0:T(8,128)S(1)}, f32[264,128]{1,0:T(8,128)S(1)}, u32[]{:S(2)}, u32[]{:S(2)}) collective-permute-start(f32[264,128]{1,0:T(8,128)S(1)} %get-tuple-element.389), channel_id=1, source_target_pairs={{0,2},{1,3},{2,0},{3,1},{4,6},{5,7},{6,4},{7,5},{8,10},{9,11},{10,... | collective-permute-start | bytes 405512 | tf_op jit(solution)/shard_map/ppermute | solution.py:499
  20.0 1.6 %collective-permute-start.6 = (f32[264,128]{1,0:T(8,128)S(1)}, f32[264,128]{1,0:T(8,128)S(1)}, u32[]{:S(2)}, u32[]{:S(2)}) collective-permute-start(f32[264,128]{1,0:T(8,128)S(1)} %get-tuple-element.390), channel_id=1, source_target_pairs={{0,4},{1,5},{2,6},{3,7},{4,0},{5,1},{6,2},{7,3},{8,12},{9,13},{10,... | collective-permute-start | bytes 405512 | tf_op jit(solution)/shard_map/ppermute | solution.py:499
  21.6 2.6 %affine.4.refs_5_ = f32[256,1024]{1,0:T(8,128)S(1)} custom-call(f32[1024,1024]{1,0:T(8,128)S(1)} %copy-done, f32[1024,1024]{1,0:T(8,128)S(1)} %copy-done.1), custom_call_target="tpu_custom_call" | custom-call | flops 16106127360 | bytes 83886080 | tf_op jit(solution)/shard_map/affine/pallas_call | solution.py:264
  24.4 3.0 %collective-permute-start.8 = (f32[264,128]{1,0:T(8,128)S(1)}, f32[264,128]{1,0:T(8,128)S(1)}, u32[]{:S(2)}, u32[]{:S(2)}) collective-permute-start(f32[264,128]{1,0:T(8,128)S(1)} %fusion.7), channel_id=1, source_target_pairs={{0,8},{1,9},{2,10},{3,11},{4,12},{5,13},{6,14},{7,15},{8,0},{9,1},... | collective-permute-start | bytes 405512 | tf_op jit(solution)/shard_map/ppermute | solution.py:499
  27.4 3.9 %affine.5.refs_6_ = f32[512,1024]{1,0:T(8,128)S(1)} custom-call(f32[1024,1024]{1,0:T(8,128)S(1)} %copy-done, f32[1024,1024]{1,0:T(8,128)S(1)} %copy-done.1), custom_call_target="tpu_custom_call" | custom-call | flops 32212254720 | bytes 83886080 | tf_op jit(solution)/shard_map/affine/pallas_call | solution.py:264
  34.9 1.8 %collective-permute-start.11 = (f32[264,128]{1,0:T(8,128)S(1)}, f32[264,128]{1,0:T(8,128)S(1)}, u32[]{:S(2)}, u32[]{:S(2)}) collective-permute-start(f32[264,128]{1,0:T(8,128)S(1)} %add.82), channel_id=1, source_target_pairs={{0,4},{1,5},{2,6},{3,7},{4,0},{5,1},{6,2},{7,3},{8,12},{9,13},{10,... | collective-permute-start | bytes 405512 | tf_op jit(solution)/shard_map/ppermute | solution.py:499
  37.9 4.1 %collective-permute-done.9 = f32[264,128]{1,0:T(8,128)S(1)} collective-permute-done((f32[264,128]{1,0:T(8,128)S(1)}, f32[264,128]{1,0:T(8,128)S(1)}, u32[]{:S(2)}, u32[]{:S(2)}) %collective-permute-start.9) | collective-permute-done | bytes 135200 | tf_op jit(solution)/shard_map/ppermute | solution.py:499
  43.6 2.0 %collective-permute-start.14 = (f32[264,128]{1,0:T(8,128)S(1)}, f32[264,128]{1,0:T(8,128)S(1)}, u32[]{:S(2)}, u32[]{:S(2)}) collective-permute-start(f32[264,128]{1,0:T(8,128)S(1)} %add.83), channel_id=1, source_target_pairs={{0,6},{1,7},{2,4},{3,5},{4,2},{5,3},{6,0},{7,1},{8,14},{9,15},{10,... | collective-permute-start | bytes 405512 | tf_op jit(solution)/shard_map/ppermute | solution.py:499
  47.6 3.8 %first_part.2.mid_ref.refs_4_ = f32[1024,1024]{1,0:T(8,128)S(1)} custom-call(s32[1]{0:T(128)} %bitcast.me_ref, f32[1056,128]{1,0:T(8,128)S(1)} %pad_maximum_fusion.refs_0_, f32[1056,128]{1,0:T(8,128)S(1)} %collective-permute-done.13.refs_1_, bf16[1024,1024]{1,0:T(8,128)(2,1)S(1)} %get-tuple-element.299.refs_2_, ...), custom_call_target="tpu_custom_call" | custom-call | flops 32212254720 | bytes 125829120 | tf_op jit(solution)/shard_map/first_part/pallas_call | solution.py:338
  51.7 1.8 %column_product.1.refs_7_ = f32[1024,256]{1,0:T(8,128)S(1)} custom-call(bf16[1024,1024]{1,0:T(8,128)(2,1)S(1)} %get-tuple-element.297.xh.refs_5_, bf16[1024,1024]{1,0:T(8,128)(2,1)S(1)} %get-tuple-element.298.xl.refs_6_, f32[1024,1024]{1,0:T(8,128)S(1)} %first_part.2.mid_ref.refs_4_), custom_call_target="tpu_custom_call" | custom-call | flops 16106127360 | bytes 83886080 | tf_op jit(solution)/shard_map/column_product/pallas_call | solution.py:369
  53.5 10.5 %second_gram.1 = (f32[1056,128]{1,0:T(8,128)S(1)}, f32[1056,128]{1,0:T(8,128)S(1)}, bf16[1024,1024]{1,0:T(8,128)(2,1)S(1)}, bf16[1024,1024]{1,0:T(8,128)(2,1)S(1)}) custom-call(s32[1]{0:T(128)} %bitcast.me_ref, f32[1056,128]{1,0:T(8,128)S(1)} %pad_maximum_fusion.1.refs_0_, f32[1056,128]{1,0:T(8,128)S(1)} %collective-permute-done.17.refs_1_, ...), custom_call_target="tpu_custom_call" | custom-call | flops 51539607552 | bytes 209715200 | tf_op jit(solution)/shard_map/second_gram/pallas_call | solution.py:424
  64.4 3.8 %fourth_gram.1 = (f32[1056,128]{1,0:T(8,128)S(1)}, f32[1056,128]{1,0:T(8,128)S(1)}) custom-call(s32[1]{0:T(128)} %bitcast.me_ref, bf16[1024,1024]{1,0:T(8,128)(2,1)S(1)} %get-tuple-element.297.xh.refs_5_, bf16[1024,1024]{1,0:T(8,128)(2,1)S(1)} %get-tuple-element.298.xl.refs_6_, bf16[1024,1024]{1,0:T(8,128)(2,1)S(1)} %get-tuple-element.325.mh.ah, ...), custom_call_target="tpu_custom_call" | custom-call | flops 32212254720 | bytes 83886080 | tf_op jit(solution)/shard_map/fourth_gram/pallas_call | solution.py:441
  68.4 1.6 %collective-permute-start.22 = (f32[264,128]{1,0:T(8,128)S(1)}, f32[264,128]{1,0:T(8,128)S(1)}, u32[]{:S(2)}, u32[]{:S(2)}) collective-permute-start(f32[264,128]{1,0:T(8,128)S(1)} %get-tuple-element.386), channel_id=1, source_target_pairs={{0,2},{1,3},{2,0},{3,1},{4,6},{5,7},{6,4},{7,5},{8,10},{9,11},{10,... | collective-permute-start | bytes 405512 | tf_op jit(solution)/shard_map/ppermute | solution.py:499
  70.2 1.7 %collective-permute-start.20 = (f32[264,128]{1,0:T(8,128)S(1)}, f32[264,128]{1,0:T(8,128)S(1)}, u32[]{:S(2)}, u32[]{:S(2)}) collective-permute-start(f32[264,128]{1,0:T(8,128)S(1)} %get-tuple-element.388), channel_id=1, source_target_pairs={{0,6},{1,7},{2,4},{3,5},{4,2},{5,3},{6,0},{7,1},{8,14},{9,15},{10,... | collective-permute-start | bytes 405512 | tf_op jit(solution)/shard_map/ppermute | solution.py:499
  71.9 2.4 %affine_parts.3.refs_4_.refs_0_ = f32[256,1024]{1,0:T(8,128)S(1)} custom-call(bf16[1024,1024]{1,0:T(8,128)(2,1)S(1)} %get-tuple-element.325.mh.ah, bf16[1024,1024]{1,0:T(8,128)(2,1)S(1)} %get-tuple-element.326.ml.al, f32[1024,1024]{1,0:T(8,128)S(1)} %copy-done.3), custom_call_target="tpu_custom_call" | custom-call | flops 16106127360 | bytes 83886080 | tf_op jit(solution)/shard_map/affine_parts/pallas_call | solution.py:284
  74.5 1.6 %collective-permute-start.25 = (f32[264,128]{1,0:T(8,128)S(1)}, f32[264,128]{1,0:T(8,128)S(1)}, u32[]{:S(2)}, u32[]{:S(2)}) collective-permute-start(f32[264,128]{1,0:T(8,128)S(1)} %get-tuple-element.383), channel_id=1, source_target_pairs={{0,2},{1,3},{2,0},{3,1},{4,6},{5,7},{6,4},{7,5},{8,10},{9,11},{10,... | collective-permute-start | bytes 405512 | tf_op jit(solution)/shard_map/ppermute | solution.py:499
  76.3 2.5 %affine_parts.4.refs_5_.refs_1_ = f32[256,1024]{1,0:T(8,128)S(1)} custom-call(bf16[1024,1024]{1,0:T(8,128)(2,1)S(1)} %get-tuple-element.325.mh.ah, bf16[1024,1024]{1,0:T(8,128)(2,1)S(1)} %get-tuple-element.326.ml.al, f32[1024,1024]{1,0:T(8,128)S(1)} %copy-done.3), custom_call_target="tpu_custom_call" | custom-call | flops 16106127360 | bytes 83886080 | tf_op jit(solution)/shard_map/affine_parts/pallas_call | solution.py:284
  78.8 1.8 %collective-permute-start.23 = (f32[264,128]{1,0:T(8,128)S(1)}, f32[264,128]{1,0:T(8,128)S(1)}, u32[]{:S(2)}, u32[]{:S(2)}) collective-permute-start(f32[264,128]{1,0:T(8,128)S(1)} %get-tuple-element.385), channel_id=1, source_target_pairs={{0,6},{1,7},{2,4},{3,5},{4,2},{5,3},{6,0},{7,1},{8,14},{9,15},{10,... | collective-permute-start | bytes 405512 | tf_op jit(solution)/shard_map/ppermute | solution.py:499
  80.6 3.4 %collective-permute-start.26 = (f32[264,128]{1,0:T(8,128)S(1)}, f32[264,128]{1,0:T(8,128)S(1)}, u32[]{:S(2)}, u32[]{:S(2)}) collective-permute-start(f32[264,128]{1,0:T(8,128)S(1)} %fusion.1), channel_id=1, source_target_pairs={{0,8},{1,9},{2,10},{3,11},{4,12},{5,13},{6,14},{7,15},{8,0},{9,1},... | collective-permute-start | bytes 405512 | tf_op jit(solution)/shard_map/ppermute | solution.py:499
  84.0 3.7 %affine_parts.5.refs_6_.refs_2_ = f32[512,1024]{1,0:T(8,128)S(1)} custom-call(bf16[1024,1024]{1,0:T(8,128)(2,1)S(1)} %get-tuple-element.325.mh.ah, bf16[1024,1024]{1,0:T(8,128)(2,1)S(1)} %get-tuple-element.326.ml.al, f32[1024,1024]{1,0:T(8,128)S(1)} %copy-done.3), custom_call_target="tpu_custom_call" | custom-call | flops 32212254720 | bytes 83886080 | tf_op jit(solution)/shard_map/affine_parts/pallas_call | solution.py:284
  88.2 2.0 %collective-permute-start.27 = (f32[264,128]{1,0:T(8,128)S(1)}, f32[264,128]{1,0:T(8,128)S(1)}, u32[]{:S(2)}, u32[]{:S(2)}) collective-permute-start(f32[264,128]{1,0:T(8,128)S(1)} %fusion.3), channel_id=1, source_target_pairs={{0,8},{1,9},{2,10},{3,11},{4,12},{5,13},{6,14},{7,15},{8,0},{9,1},... | collective-permute-start | bytes 405512 | tf_op jit(solution)/shard_map/ppermute | solution.py:499
  91.7 2.3 %collective-permute-start.29 = (f32[264,128]{1,0:T(8,128)S(1)}, f32[264,128]{1,0:T(8,128)S(1)}, u32[]{:S(2)}, u32[]{:S(2)}) collective-permute-start(f32[264,128]{1,0:T(8,128)S(1)} %add.93), channel_id=1, source_target_pairs={{0,4},{1,5},{2,6},{3,7},{4,0},{5,1},{6,2},{7,3},{8,12},{9,13},{10,... | collective-permute-start | bytes 405512 | tf_op jit(solution)/shard_map/ppermute | solution.py:499
  94.1 3.1 %collective-permute-done.27 = f32[264,128]{1,0:T(8,128)S(1)} collective-permute-done((f32[264,128]{1,0:T(8,128)S(1)}, f32[264,128]{1,0:T(8,128)S(1)}, u32[]{:S(2)}, u32[]{:S(2)}) %collective-permute-start.27) | collective-permute-done | bytes 135200 | tf_op jit(solution)/shard_map/ppermute | solution.py:499
  97.9 2.9 %collective-permute-start.32 = (f32[264,128]{1,0:T(8,128)S(1)}, f32[264,128]{1,0:T(8,128)S(1)}, u32[]{:S(2)}, u32[]{:S(2)}) collective-permute-start(f32[264,128]{1,0:T(8,128)S(1)} %add.92), channel_id=1, source_target_pairs={{0,6},{1,7},{2,4},{3,5},{4,2},{5,3},{6,0},{7,1},{8,14},{9,15},{10,... | collective-permute-start | bytes 405512 | tf_op jit(solution)/shard_map/ppermute | solution.py:499
  100.8 2.3 %collective-permute-done.28 = f32[264,128]{1,0:T(8,128)S(1)} collective-permute-done((f32[264,128]{1,0:T(8,128)S(1)}, f32[264,128]{1,0:T(8,128)S(1)}, u32[]{:S(2)}, u32[]{:S(2)}) %collective-permute-start.28) | collective-permute-done | bytes 135200 | tf_op jit(solution)/shard_map/ppermute | solution.py:499
  105.2 2.2 %first_part.3 = (f32[1024,256]{1,0:T(8,128)S(1)}, bf16[1024,1024]{1,0:T(8,128)(2,1)S(1)}, bf16[1024,1024]{1,0:T(8,128)(2,1)S(1)}) custom-call(s32[1]{0:T(128)} %bitcast.me_ref, f32[1056,128]{1,0:T(8,128)S(1)} %pad_maximum_fusion.2.refs_0_, f32[1056,128]{1,0:T(8,128)S(1)} %collective-permute-done.31.refs_1_, ...), custom_call_target="tpu_custom_call" | custom-call | flops 32212254720 | bytes 125829120 | tf_op jit(solution)/shard_map/first_part/pallas_call | solution.py:338
  108.6 1.8 %other_part.1.refs_5_ = f32[1024,768]{1,0:T(8,128)S(1)} custom-call(bf16[1024,1024]{1,0:T(8,128)(2,1)S(1)} %get-tuple-element.379.refs_2_.ah, bf16[1024,1024]{1,0:T(8,128)(2,1)S(1)} %get-tuple-element.380.refs_3_.al, bf16[1024,1024]{1,0:T(8,128)(2,1)S(1)} %get-tuple-element.376.hi, bf16[1024,1024]{1,0:T(8,128)(2,1)S(1)} %get-tuple-element.377.lo, ...), custom_call_target="tpu_custom_call" | custom-call | flops 16106127360 | bytes 125829120 | tf_op jit(solution)/shard_map/other_part/pallas_call | solution.py:353
  110.5 4.9 %last.1 = f32[1024,1024]{1,0:T(8,128)} custom-call(s32[1]{0:T(128)} %bitcast.me_ref, f32[1056,128]{1,0:T(8,128)S(1)} %pad_maximum_fusion.3.refs_0_, f32[1056,128]{1,0:T(8,128)S(1)} %collective-permute-done.35.refs_1_, bf16[1024,1024]{1,0:T(8,128)(2,1)S(1)} %get-tuple-element.379.refs_2_.ah, bf16[1024,1024]{1,0:T(8,128)(2,1)S(1)} %get-tuple-element.380.refs_3_.al, ...), custom_call_target="tpu_custom_call" | custom-call | flops 32212254720 | bytes 125829120 | tf_op jit(solution)/shard_map/last/pallas_call | solution.py:476
  (90 shorter events, 18.3 us)
Async XLA Ops:
  6.9 4.2 %collective-permute-start = (f32[1056,128]{1,0:T(8,128)S(1)}, f32[1056,128]{1,0:T(8,128)S(1)}, u32[]{:S(2)}, u32[]{:S(2)}) collective-permute-start(f32[1056,128]{1,0:T(8,128)S(1)} %get-tuple-element.200), channel_id=1, source_target_pairs={{0,1},{1,0},{2,3},{3,2},{4,5},{5,4},{6,7},{7,6},{8,9},{9,8},{10,11... | collective-permute-start | bytes 1622024 | tf_op jit(solution)/shard_map/ppermute | solution.py:499
  11.2 13.0 %collective-permute-start.4 = (f32[264,128]{1,0:T(8,128)S(1)}, f32[264,128]{1,0:T(8,128)S(1)}, u32[]{:S(2)}, u32[]{:S(2)}) collective-permute-start(f32[264,128]{1,0:T(8,128)S(1)} %get-tuple-element.392), channel_id=1, source_target_pairs={{0,2},{1,3},{2,0},{3,1},{4,6},{5,7},{6,4},{7,5},{8,10},{9,11},{10,... | collective-permute-start | bytes 405512 | tf_op jit(solution)/shard_map/ppermute | solution.py:499
  13.8 10.5 %collective-permute-start.3 = (f32[264,128]{1,0:T(8,128)S(1)}, f32[264,128]{1,0:T(8,128)S(1)}, u32[]{:S(2)}, u32[]{:S(2)}) collective-permute-start(f32[264,128]{1,0:T(8,128)S(1)} %get-tuple-element.393), channel_id=1, source_target_pairs={{0,4},{1,5},{2,6},{3,7},{4,0},{5,1},{6,2},{7,3},{8,12},{9,13},{10,... | collective-permute-start | bytes 405512 | tf_op jit(solution)/shard_map/ppermute | solution.py:499
  15.4 8.9 %collective-permute-start.2 = (f32[264,128]{1,0:T(8,128)S(1)}, f32[264,128]{1,0:T(8,128)S(1)}, u32[]{:S(2)}, u32[]{:S(2)}) collective-permute-start(f32[264,128]{1,0:T(8,128)S(1)} %get-tuple-element.394), channel_id=1, source_target_pairs={{0,6},{1,7},{2,4},{3,5},{4,2},{5,3},{6,0},{7,1},{8,14},{9,15},{10,... | collective-permute-start | bytes 405512 | tf_op jit(solution)/shard_map/ppermute | solution.py:499
  15.4 2.6 %collective-permute-start.1 = (f32[1056,128]{1,0:T(8,128)S(1)}, f32[1056,128]{1,0:T(8,128)S(1)}, u32[]{:S(2)}, u32[]{:S(2)}) collective-permute-start(f32[1056,128]{1,0:T(8,128)S(1)} %get-tuple-element.206), channel_id=1, source_target_pairs={{0,1},{1,0},{2,3},{3,2},{4,5},{5,4},{6,7},{7,6},{8,9},{9,8},{10,11... | collective-permute-start | bytes 1622024 | tf_op jit(solution)/shard_map/ppermute | solution.py:499
  18.1 14.7 %collective-permute-start.7 = (f32[264,128]{1,0:T(8,128)S(1)}, f32[264,128]{1,0:T(8,128)S(1)}, u32[]{:S(2)}, u32[]{:S(2)}) collective-permute-start(f32[264,128]{1,0:T(8,128)S(1)} %get-tuple-element.389), channel_id=1, source_target_pairs={{0,2},{1,3},{2,0},{3,1},{4,6},{5,7},{6,4},{7,5},{8,10},{9,11},{10,... | collective-permute-start | bytes 405512 | tf_op jit(solution)/shard_map/ppermute | solution.py:499
  20.0 12.8 %collective-permute-start.6 = (f32[264,128]{1,0:T(8,128)S(1)}, f32[264,128]{1,0:T(8,128)S(1)}, u32[]{:S(2)}, u32[]{:S(2)}) collective-permute-start(f32[264,128]{1,0:T(8,128)S(1)} %get-tuple-element.390), channel_id=1, source_target_pairs={{0,4},{1,5},{2,6},{3,7},{4,0},{5,1},{6,2},{7,3},{8,12},{9,13},{10,... | collective-permute-start | bytes 405512 | tf_op jit(solution)/shard_map/ppermute | solution.py:499
  24.2 9.3 %collective-permute-start.5 = (f32[264,128]{1,0:T(8,128)S(1)}, f32[264,128]{1,0:T(8,128)S(1)}, u32[]{:S(2)}, u32[]{:S(2)}) collective-permute-start(f32[264,128]{1,0:T(8,128)S(1)} %get-tuple-element.391), channel_id=1, source_target_pairs={{0,6},{1,7},{2,4},{3,5},{4,2},{5,3},{6,0},{7,1},{8,14},{9,15},{10,... | collective-permute-start | bytes 405512 | tf_op jit(solution)/shard_map/ppermute | solution.py:499
  24.4 10.0 %collective-permute-start.8 = (f32[264,128]{1,0:T(8,128)S(1)}, f32[264,128]{1,0:T(8,128)S(1)}, u32[]{:S(2)}, u32[]{:S(2)}) collective-permute-start(f32[264,128]{1,0:T(8,128)S(1)} %fusion.7), channel_id=1, source_target_pairs={{0,8},{1,9},{2,10},{3,11},{4,12},{5,13},{6,14},{7,15},{8,0},{9,1},... | collective-permute-start | bytes 405512 | tf_op jit(solution)/shard_map/ppermute | solution.py:499
  33.6 8.4 %collective-permute-start.9 = (f32[264,128]{1,0:T(8,128)S(1)}, f32[264,128]{1,0:T(8,128)S(1)}, u32[]{:S(2)}, u32[]{:S(2)}) collective-permute-start(f32[264,128]{1,0:T(8,128)S(1)} %fusion.5), channel_id=1, source_target_pairs={{0,8},{1,9},{2,10},{3,11},{4,12},{5,13},{6,14},{7,15},{8,0},{9,1},... | collective-permute-start | bytes 405512 | tf_op jit(solution)/shard_map/ppermute | solution.py:499
  34.4 9.2 %collective-permute-start.12 = (f32[264,128]{1,0:T(8,128)S(1)}, f32[264,128]{1,0:T(8,128)S(1)}, u32[]{:S(2)}, u32[]{:S(2)}) collective-permute-start(f32[264,128]{1,0:T(8,128)S(1)} %add.82), channel_id=1, source_target_pairs={{0,2},{1,3},{2,0},{3,1},{4,6},{5,7},{6,4},{7,5},{8,10},{9,11},{10,... | collective-permute-start | bytes 405512 | tf_op jit(solution)/shard_map/ppermute | solution.py:499
  34.9 10.7 %collective-permute-start.11 = (f32[264,128]{1,0:T(8,128)S(1)}, f32[264,128]{1,0:T(8,128)S(1)}, u32[]{:S(2)}, u32[]{:S(2)}) collective-permute-start(f32[264,128]{1,0:T(8,128)S(1)} %add.82), channel_id=1, source_target_pairs={{0,4},{1,5},{2,6},{3,7},{4,0},{5,1},{6,2},{7,3},{8,12},{9,13},{10,... | collective-permute-start | bytes 405512 | tf_op jit(solution)/shard_map/ppermute | solution.py:499
  36.7 8.8 %collective-permute-start.10 = (f32[264,128]{1,0:T(8,128)S(1)}, f32[264,128]{1,0:T(8,128)S(1)}, u32[]{:S(2)}, u32[]{:S(2)}) collective-permute-start(f32[264,128]{1,0:T(8,128)S(1)} %add.82), channel_id=1, source_target_pairs={{0,6},{1,7},{2,4},{3,5},{4,2},{5,3},{6,0},{7,1},{8,14},{9,15},{10,... | collective-permute-start | bytes 405512 | tf_op jit(solution)/shard_map/ppermute | solution.py:499
  42.0 9.4 %collective-permute-start.16 = (f32[264,128]{1,0:T(8,128)S(1)}, f32[264,128]{1,0:T(8,128)S(1)}, u32[]{:S(2)}, u32[]{:S(2)}) collective-permute-start(f32[264,128]{1,0:T(8,128)S(1)} %add.83), channel_id=1, source_target_pairs={{0,2},{1,3},{2,0},{3,1},{4,6},{5,7},{6,4},{7,5},{8,10},{9,11},{10,... | collective-permute-start | bytes 405512 | tf_op jit(solution)/shard_map/ppermute | solution.py:499
  43.3 8.1 %collective-permute-start.15 = (f32[264,128]{1,0:T(8,128)S(1)}, f32[264,128]{1,0:T(8,128)S(1)}, u32[]{:S(2)}, u32[]{:S(2)}) collective-permute-start(f32[264,128]{1,0:T(8,128)S(1)} %add.83), channel_id=1, source_target_pairs={{0,4},{1,5},{2,6},{3,7},{4,0},{5,1},{6,2},{7,3},{8,12},{9,13},{10,... | collective-permute-start | bytes 405512 | tf_op jit(solution)/shard_map/ppermute | solution.py:499
  43.6 7.9 %collective-permute-start.14 = (f32[264,128]{1,0:T(8,128)S(1)}, f32[264,128]{1,0:T(8,128)S(1)}, u32[]{:S(2)}, u32[]{:S(2)}) collective-permute-start(f32[264,128]{1,0:T(8,128)S(1)} %add.83), channel_id=1, source_target_pairs={{0,6},{1,7},{2,4},{3,5},{4,2},{5,3},{6,0},{7,1},{8,14},{9,15},{10,... | collective-permute-start | bytes 405512 | tf_op jit(solution)/shard_map/ppermute | solution.py:499
  64.0 4.3 %collective-permute-start.18 = (f32[1056,128]{1,0:T(8,128)S(1)}, f32[1056,128]{1,0:T(8,128)S(1)}, u32[]{:S(2)}, u32[]{:S(2)}) collective-permute-start(f32[1056,128]{1,0:T(8,128)S(1)} %get-tuple-element.308), channel_id=1, source_target_pairs={{0,1},{1,0},{2,3},{3,2},{4,5},{5,4},{6,7},{7,6},{8,9},{9,8},{10,11... | collective-permute-start | bytes 1622024 | tf_op jit(solution)/shard_map/ppermute | solution.py:499
  68.4 10.4 %collective-permute-start.22 = (f32[264,128]{1,0:T(8,128)S(1)}, f32[264,128]{1,0:T(8,128)S(1)}, u32[]{:S(2)}, u32[]{:S(2)}) collective-permute-start(f32[264,128]{1,0:T(8,128)S(1)} %get-tuple-element.386), channel_id=1, source_target_pairs={{0,2},{1,3},{2,0},{3,1},{4,6},{5,7},{6,4},{7,5},{8,10},{9,11},{10,... | collective-permute-start | bytes 405512 | tf_op jit(solution)/shard_map/ppermute | solution.py:499
  70.0 10.6 %collective-permute-start.21 = (f32[264,128]{1,0:T(8,128)S(1)}, f32[264,128]{1,0:T(8,128)S(1)}, u32[]{:S(2)}, u32[]{:S(2)}) collective-permute-start(f32[264,128]{1,0:T(8,128)S(1)} %get-tuple-element.387), channel_id=1, source_target_pairs={{0,4},{1,5},{2,6},{3,7},{4,0},{5,1},{6,2},{7,3},{8,12},{9,13},{10,... | collective-permute-start | bytes 405512 | tf_op jit(solution)/shard_map/ppermute | solution.py:499
  70.2 10.4 %collective-permute-start.20 = (f32[264,128]{1,0:T(8,128)S(1)}, f32[264,128]{1,0:T(8,128)S(1)}, u32[]{:S(2)}, u32[]{:S(2)}) collective-permute-start(f32[264,128]{1,0:T(8,128)S(1)} %get-tuple-element.388), channel_id=1, source_target_pairs={{0,6},{1,7},{2,4},{3,5},{4,2},{5,3},{6,0},{7,1},{8,14},{9,15},{10,... | collective-permute-start | bytes 405512 | tf_op jit(solution)/shard_map/ppermute | solution.py:499
  71.9 2.5 %collective-permute-start.19 = (f32[1056,128]{1,0:T(8,128)S(1)}, f32[1056,128]{1,0:T(8,128)S(1)}, u32[]{:S(2)}, u32[]{:S(2)}) collective-permute-start(f32[1056,128]{1,0:T(8,128)S(1)} %get-tuple-element.314), channel_id=1, source_target_pairs={{0,1},{1,0},{2,3},{3,2},{4,5},{5,4},{6,7},{7,6},{8,9},{9,8},{10,11... | collective-permute-start | bytes 1622024 | tf_op jit(solution)/shard_map/ppermute | solution.py:499
  74.5 13.2 %collective-permute-start.25 = (f32[264,128]{1,0:T(8,128)S(1)}, f32[264,128]{1,0:T(8,128)S(1)}, u32[]{:S(2)}, u32[]{:S(2)}) collective-permute-start(f32[264,128]{1,0:T(8,128)S(1)} %get-tuple-element.383), channel_id=1, source_target_pairs={{0,2},{1,3},{2,0},{3,1},{4,6},{5,7},{6,4},{7,5},{8,10},{9,11},{10,... | collective-permute-start | bytes 405512 | tf_op jit(solution)/shard_map/ppermute | solution.py:499
  76.1 11.6 %collective-permute-start.24 = (f32[264,128]{1,0:T(8,128)S(1)}, f32[264,128]{1,0:T(8,128)S(1)}, u32[]{:S(2)}, u32[]{:S(2)}) collective-permute-start(f32[264,128]{1,0:T(8,128)S(1)} %get-tuple-element.384), channel_id=1, source_target_pairs={{0,4},{1,5},{2,6},{3,7},{4,0},{5,1},{6,2},{7,3},{8,12},{9,13},{10,... | collective-permute-start | bytes 405512 | tf_op jit(solution)/shard_map/ppermute | solution.py:499
  78.8 9.4 %collective-permute-start.23 = (f32[264,128]{1,0:T(8,128)S(1)}, f32[264,128]{1,0:T(8,128)S(1)}, u32[]{:S(2)}, u32[]{:S(2)}) collective-permute-start(f32[264,128]{1,0:T(8,128)S(1)} %get-tuple-element.385), channel_id=1, source_target_pairs={{0,6},{1,7},{2,4},{3,5},{4,2},{5,3},{6,0},{7,1},{8,14},{9,15},{10,... | collective-permute-start | bytes 405512 | tf_op jit(solution)/shard_map/ppermute | solution.py:499
  80.6 9.6 %collective-permute-start.26 = (f32[264,128]{1,0:T(8,128)S(1)}, f32[264,128]{1,0:T(8,128)S(1)}, u32[]{:S(2)}, u32[]{:S(2)}) collective-permute-start(f32[264,128]{1,0:T(8,128)S(1)} %fusion.1), channel_id=1, source_target_pairs={{0,8},{1,9},{2,10},{3,11},{4,12},{5,13},{6,14},{7,15},{8,0},{9,1},... | collective-permute-start | bytes 405512 | tf_op jit(solution)/shard_map/ppermute | solution.py:499
  88.2 9.0 %collective-permute-start.27 = (f32[264,128]{1,0:T(8,128)S(1)}, f32[264,128]{1,0:T(8,128)S(1)}, u32[]{:S(2)}, u32[]{:S(2)}) collective-permute-start(f32[264,128]{1,0:T(8,128)S(1)} %fusion.3), channel_id=1, source_target_pairs={{0,8},{1,9},{2,10},{3,11},{4,12},{5,13},{6,14},{7,15},{8,0},{9,1},... | collective-permute-start | bytes 405512 | tf_op jit(solution)/shard_map/ppermute | solution.py:499
  90.2 7.7 %collective-permute-start.30 = (f32[264,128]{1,0:T(8,128)S(1)}, f32[264,128]{1,0:T(8,128)S(1)}, u32[]{:S(2)}, u32[]{:S(2)}) collective-permute-start(f32[264,128]{1,0:T(8,128)S(1)} %add.93), channel_id=1, source_target_pairs={{0,2},{1,3},{2,0},{3,1},{4,6},{5,7},{6,4},{7,5},{8,10},{9,11},{10,... | collective-permute-start | bytes 405512 | tf_op jit(solution)/shard_map/ppermute | solution.py:499
  91.7 9.1 %collective-permute-start.29 = (f32[264,128]{1,0:T(8,128)S(1)}, f32[264,128]{1,0:T(8,128)S(1)}, u32[]{:S(2)}, u32[]{:S(2)}) collective-permute-start(f32[264,128]{1,0:T(8,128)S(1)} %add.93), channel_id=1, source_target_pairs={{0,4},{1,5},{2,6},{3,7},{4,0},{5,1},{6,2},{7,3},{8,12},{9,13},{10,... | collective-permute-start | bytes 405512 | tf_op jit(solution)/shard_map/ppermute | solution.py:499
  94.0 9.1 %collective-permute-start.28 = (f32[264,128]{1,0:T(8,128)S(1)}, f32[264,128]{1,0:T(8,128)S(1)}, u32[]{:S(2)}, u32[]{:S(2)}) collective-permute-start(f32[264,128]{1,0:T(8,128)S(1)} %add.93), channel_id=1, source_target_pairs={{0,6},{1,7},{2,4},{3,5},{4,2},{5,3},{6,0},{7,1},{8,14},{9,15},{10,... | collective-permute-start | bytes 405512 | tf_op jit(solution)/shard_map/ppermute | solution.py:499
  97.3 10.1 %collective-permute-start.34 = (f32[264,128]{1,0:T(8,128)S(1)}, f32[264,128]{1,0:T(8,128)S(1)}, u32[]{:S(2)}, u32[]{:S(2)}) collective-permute-start(f32[264,128]{1,0:T(8,128)S(1)} %add.92), channel_id=1, source_target_pairs={{0,2},{1,3},{2,0},{3,1},{4,6},{5,7},{6,4},{7,5},{8,10},{9,11},{10,... | collective-permute-start | bytes 405512 | tf_op jit(solution)/shard_map/ppermute | solution.py:499
  97.9 9.5 %collective-permute-start.33 = (f32[264,128]{1,0:T(8,128)S(1)}, f32[264,128]{1,0:T(8,128)S(1)}, u32[]{:S(2)}, u32[]{:S(2)}) collective-permute-start(f32[264,128]{1,0:T(8,128)S(1)} %add.92), channel_id=1, source_target_pairs={{0,4},{1,5},{2,6},{3,7},{4,0},{5,1},{6,2},{7,3},{8,12},{9,13},{10,... | collective-permute-start | bytes 405512 | tf_op jit(solution)/shard_map/ppermute | solution.py:499
  97.9 10.6 %collective-permute-start.32 = (f32[264,128]{1,0:T(8,128)S(1)}, f32[264,128]{1,0:T(8,128)S(1)}, u32[]{:S(2)}, u32[]{:S(2)}) collective-permute-start(f32[264,128]{1,0:T(8,128)S(1)} %add.92), channel_id=1, source_target_pairs={{0,6},{1,7},{2,4},{3,5},{4,2},{5,3},{6,0},{7,1},{8,14},{9,15},{10,... | collective-permute-start | bytes 405512 | tf_op jit(solution)/shard_map/ppermute | solution.py:499
  (10 other events, 72.1 us)

commit v10 on v9

--- a/solution.py
+++ b/solution.py
@@ -412,8 +412,8 @@
         c, product = sym_product(ah, al, hi, lo, 1, column)
         mid = base_ref[:, c] - 0.5 * product
         mh[:, c], ml[:, c] = split(mid)
-        g[:q, c] = mm((xh[:q, :], xl[:q, :]), (mh[:, c], ml[:, c]))
     g[:, :q] = col_ref[...]
+    g[:q, q:] = mm((xh[:q, :], xl[:q, :]), (mh[:, q:], ml[:, q:]))
     g[3 * q:, 3 * q:] = mm((xh[3 * q:, :], xl[3 * q:, :]), (mh[:, 3 * q:], ml[:, 3 * q:]))
     pack(g, packed, keep_ref, send_ref, me_ref[0], shards, 0)
 

time: 116 us -> 111 us (0.957)
  Pallas kernels: 60.1 us -> 55.7 us
    pallas_call x1, Pallas kernels: 10.5 us -> 6.04 us  [second_gram(): call(functools.partial(second_gram_kernel, shards, len(pieces)), 'second_...]
  transfers between devices with their start and end apart: 36 -> 36, of which waited for: 9 -> 9; matrix products, arithmetic and copies ran while one was open for 0% -> 0% of each run, Pallas kernels for 33% -> 34%
where the time goes in v10:
time: 111 us
  Pallas kernels  55.7 us (50%)
  starting transfers between devices  40.1 us (36%)
  waiting for transfers between devices  14 us (13%)
    ppermute x36, starting transfers between devices, swap(): return lax.ppermute(x, 'row', [(i, i ^ offset) for i in range(self.count)])  40.1 us
    ppermute x36, waiting for transfers between devices, swap(): return lax.ppermute(x, 'row', [(i, i ^ offset) for i in range(self.count)])  14 us
    pallas_call x3, Pallas kernels, affine(): call(affine_kernel, 'affine', struct(height, size), 18, height / rows, 2,...  9.01 us
    pallas_call x3, Pallas kernels, affine_parts(): call(affine_parts_kernel, 'affine_parts', struct(height, size), 18, heigh...  8.54 us
    pallas_call x1, Pallas kernels, first_gram(): call(functools.partial(first_gram_kernel, shards), 'first_gram', halves(s...  6.9 us
    pallas_call x1, Pallas kernels, second_gram(): call(functools.partial(second_gram_kernel, shards, len(pieces)), 'second_...  6.04 us
    pallas_call x2, Pallas kernels, first_part(): call(functools.partial(first_part_kernel, shards, len(pieces), columns),...  5.99 us
    pallas_call x1, Pallas kernels, last_step(): call(functools.partial(last_kernel, shards, len(pieces)), 'last', struct(...  4.95 us
  transfers between devices with their start and end apart: 36, of which 9 were waited for; matrix products, arithmetic and copies ran while one was open for 0% of the time, Pallas kernels for 34%

profile of v10, /device:TPU:0, one launch (start us, length us, event | category | flops | bytes accessed | tf_op | source)
XLA Modules:
  0.0 111.2 jit_solution(2898799048769404280)
XLA Ops:
  0.0 6.9 %first_gram.1 = (f32[1056,128]{1,0:T(8,128)S(1)}, f32[1056,128]{1,0:T(8,128)S(1)}, bf16[1024,1024]{1,0:T(8,128)(2,1)S(1)}, bf16[1024,1024]{1,0:T(8,128)(2,1)S(1)...) custom-call(s32[1]{0:T(128)} %bitcast.me_ref, f32[1024,1024]{1,0:T(8,128)} %x_ref.1, f32[1024,1024]{1,0:T(8,128)} %a_ref.2), custom_call_target="tpu_custom_call" | custom-call | flops 32212254720 | bytes 167772160 | tf_op jit(solution)/shard_map/first_gram/pallas_call | solution.py:198
  7.4 3.6 %other_gram.1 = (f32[1056,128]{1,0:T(8,128)S(1)}, f32[1056,128]{1,0:T(8,128)S(1)}) custom-call(s32[1]{0:T(128)} %bitcast.me_ref, bf16[1024,1024]{1,0:T(8,128)(2,1)S(1)} %get-tuple-element.194.ah, bf16[1024,1024]{1,0:T(8,128)(2,1)S(1)} %get-tuple-element.195.al, bf16[1024,1024]{1,0:T(8,128)(2,1)S(1)} %get-tuple-element.196.bh, ...), custom_call_target="tpu_custom_call" | custom-call | flops 32212254720 | bytes 83886080 | tf_op jit(solution)/shard_map/other_gram/pallas_call | solution.py:228
  11.2 2.6 %collective-permute-start.4 = (f32[264,128]{1,0:T(8,128)S(1)}, f32[264,128]{1,0:T(8,128)S(1)}, u32[]{:S(2)}, u32[]{:S(2)}) collective-permute-start(f32[264,128]{1,0:T(8,128)S(1)} %get-tuple-element.392), channel_id=1, source_target_pairs={{0,2},{1,3},{2,0},{3,1},{4,6},{5,7},{6,4},{7,5},{8,10},{9,11},{10,... | collective-permute-start | bytes 405512 | tf_op jit(solution)/shard_map/ppermute | solution.py:499
  15.4 2.6 %affine.3.refs_4_ = f32[256,1024]{1,0:T(8,128)S(1)} custom-call(f32[1024,1024]{1,0:T(8,128)S(1)} %copy-done, f32[1024,1024]{1,0:T(8,128)S(1)} %copy-done.1), custom_call_target="tpu_custom_call" | custom-call | flops 16106127360 | bytes 83886080 | tf_op jit(solution)/shard_map/affine/pallas_call | solution.py:264
  18.1 1.9 %collective-permute-start.7 = (f32[264,128]{1,0:T(8,128)S(1)}, f32[264,128]{1,0:T(8,128)S(1)}, u32[]{:S(2)}, u32[]{:S(2)}) collective-permute-start(f32[264,128]{1,0:T(8,128)S(1)} %get-tuple-element.389), channel_id=1, source_target_pairs={{0,2},{1,3},{2,0},{3,1},{4,6},{5,7},{6,4},{7,5},{8,10},{9,11},{10,... | collective-permute-start | bytes 405512 | tf_op jit(solution)/shard_map/ppermute | solution.py:499
  20.0 1.6 %collective-permute-start.6 = (f32[264,128]{1,0:T(8,128)S(1)}, f32[264,128]{1,0:T(8,128)S(1)}, u32[]{:S(2)}, u32[]{:S(2)}) collective-permute-start(f32[264,128]{1,0:T(8,128)S(1)} %get-tuple-element.390), channel_id=1, source_target_pairs={{0,4},{1,5},{2,6},{3,7},{4,0},{5,1},{6,2},{7,3},{8,12},{9,13},{10,... | collective-permute-start | bytes 405512 | tf_op jit(solution)/shard_map/ppermute | solution.py:499
  21.6 2.6 %affine.4.refs_5_ = f32[256,1024]{1,0:T(8,128)S(1)} custom-call(f32[1024,1024]{1,0:T(8,128)S(1)} %copy-done, f32[1024,1024]{1,0:T(8,128)S(1)} %copy-done.1), custom_call_target="tpu_custom_call" | custom-call | flops 16106127360 | bytes 83886080 | tf_op jit(solution)/shard_map/affine/pallas_call | solution.py:264
  24.4 3.0 %collective-permute-start.8 = (f32[264,128]{1,0:T(8,128)S(1)}, f32[264,128]{1,0:T(8,128)S(1)}, u32[]{:S(2)}, u32[]{:S(2)}) collective-permute-start(f32[264,128]{1,0:T(8,128)S(1)} %fusion.7), channel_id=1, source_target_pairs={{0,8},{1,9},{2,10},{3,11},{4,12},{5,13},{6,14},{7,15},{8,0},{9,1},... | collective-permute-start | bytes 405512 | tf_op jit(solution)/shard_map/ppermute | solution.py:499
  27.4 3.9 %affine.5.refs_6_ = f32[512,1024]{1,0:T(8,128)S(1)} custom-call(f32[1024,1024]{1,0:T(8,128)S(1)} %copy-done, f32[1024,1024]{1,0:T(8,128)S(1)} %copy-done.1), custom_call_target="tpu_custom_call" | custom-call | flops 32212254720 | bytes 83886080 | tf_op jit(solution)/shard_map/affine/pallas_call | solution.py:264
  34.9 1.8 %collective-permute-start.11 = (f32[264,128]{1,0:T(8,128)S(1)}, f32[264,128]{1,0:T(8,128)S(1)}, u32[]{:S(2)}, u32[]{:S(2)}) collective-permute-start(f32[264,128]{1,0:T(8,128)S(1)} %add.82), channel_id=1, source_target_pairs={{0,4},{1,5},{2,6},{3,7},{4,0},{5,1},{6,2},{7,3},{8,12},{9,13},{10,... | collective-permute-start | bytes 405512 | tf_op jit(solution)/shard_map/ppermute | solution.py:499
  37.9 4.1 %collective-permute-done.9 = f32[264,128]{1,0:T(8,128)S(1)} collective-permute-done((f32[264,128]{1,0:T(8,128)S(1)}, f32[264,128]{1,0:T(8,128)S(1)}, u32[]{:S(2)}, u32[]{:S(2)}) %collective-permute-start.9) | collective-permute-done | bytes 135200 | tf_op jit(solution)/shard_map/ppermute | solution.py:499
  43.6 2.0 %collective-permute-start.14 = (f32[264,128]{1,0:T(8,128)S(1)}, f32[264,128]{1,0:T(8,128)S(1)}, u32[]{:S(2)}, u32[]{:S(2)}) collective-permute-start(f32[264,128]{1,0:T(8,128)S(1)} %add.83), channel_id=1, source_target_pairs={{0,6},{1,7},{2,4},{3,5},{4,2},{5,3},{6,0},{7,1},{8,14},{9,15},{10,... | collective-permute-start | bytes 405512 | tf_op jit(solution)/shard_map/ppermute | solution.py:499
  47.6 3.8 %first_part.2.mid_ref.refs_4_ = f32[1024,1024]{1,0:T(8,128)S(1)} custom-call(s32[1]{0:T(128)} %bitcast.me_ref, f32[1056,128]{1,0:T(8,128)S(1)} %pad_maximum_fusion.refs_0_, f32[1056,128]{1,0:T(8,128)S(1)} %collective-permute-done.13.refs_1_, bf16[1024,1024]{1,0:T(8,128)(2,1)S(1)} %get-tuple-element.299.refs_2_, ...), custom_call_target="tpu_custom_call" | custom-call | flops 32212254720 | bytes 125829120 | tf_op jit(solution)/shard_map/first_part/pallas_call | solution.py:338
  51.7 1.8 %column_product.1.refs_7_ = f32[1024,256]{1,0:T(8,128)S(1)} custom-call(bf16[1024,1024]{1,0:T(8,128)(2,1)S(1)} %get-tuple-element.297.xh.refs_5_, bf16[1024,1024]{1,0:T(8,128)(2,1)S(1)} %get-tuple-element.298.xl.refs_6_, f32[1024,1024]{1,0:T(8,128)S(1)} %first_part.2.mid_ref.refs_4_), custom_call_target="tpu_custom_call" | custom-call | flops 16106127360 | bytes 83886080 | tf_op jit(solution)/shard_map/column_product/pallas_call | solution.py:369
  53.5 6.0 %second_gram.1 = (f32[1056,128]{1,0:T(8,128)S(1)}, f32[1056,128]{1,0:T(8,128)S(1)}, bf16[1024,1024]{1,0:T(8,128)(2,1)S(1)}, bf16[1024,1024]{1,0:T(8,128)(2,1)S(1)}) custom-call(s32[1]{0:T(128)} %bitcast.me_ref, f32[1056,128]{1,0:T(8,128)S(1)} %pad_maximum_fusion.1.refs_0_, f32[1056,128]{1,0:T(8,128)S(1)} %collective-permute-done.17.refs_1_, ...), custom_call_target="tpu_custom_call" | custom-call | flops 51539607552 | bytes 209715200 | tf_op jit(solution)/shard_map/second_gram/pallas_call | solution.py:424
  60.0 3.8 %fourth_gram.1 = (f32[1056,128]{1,0:T(8,128)S(1)}, f32[1056,128]{1,0:T(8,128)S(1)}) custom-call(s32[1]{0:T(128)} %bitcast.me_ref, bf16[1024,1024]{1,0:T(8,128)(2,1)S(1)} %get-tuple-element.297.xh.refs_5_, bf16[1024,1024]{1,0:T(8,128)(2,1)S(1)} %get-tuple-element.298.xl.refs_6_, bf16[1024,1024]{1,0:T(8,128)(2,1)S(1)} %get-tuple-element.325.mh.ah, ...), custom_call_target="tpu_custom_call" | custom-call | flops 32212254720 | bytes 83886080 | tf_op jit(solution)/shard_map/fourth_gram/pallas_call | solution.py:441
  63.9 1.6 %collective-permute-start.22 = (f32[264,128]{1,0:T(8,128)S(1)}, f32[264,128]{1,0:T(8,128)S(1)}, u32[]{:S(2)}, u32[]{:S(2)}) collective-permute-start(f32[264,128]{1,0:T(8,128)S(1)} %get-tuple-element.386), channel_id=1, source_target_pairs={{0,2},{1,3},{2,0},{3,1},{4,6},{5,7},{6,4},{7,5},{8,10},{9,11},{10,... | collective-permute-start | bytes 405512 | tf_op jit(solution)/shard_map/ppermute | solution.py:499
  65.8 1.7 %collective-permute-start.20 = (f32[264,128]{1,0:T(8,128)S(1)}, f32[264,128]{1,0:T(8,128)S(1)}, u32[]{:S(2)}, u32[]{:S(2)}) collective-permute-start(f32[264,128]{1,0:T(8,128)S(1)} %get-tuple-element.388), channel_id=1, source_target_pairs={{0,6},{1,7},{2,4},{3,5},{4,2},{5,3},{6,0},{7,1},{8,14},{9,15},{10,... | collective-permute-start | bytes 405512 | tf_op jit(solution)/shard_map/ppermute | solution.py:499
  67.5 2.4 %affine_parts.3.refs_4_.refs_0_ = f32[256,1024]{1,0:T(8,128)S(1)} custom-call(bf16[1024,1024]{1,0:T(8,128)(2,1)S(1)} %get-tuple-element.325.mh.ah, bf16[1024,1024]{1,0:T(8,128)(2,1)S(1)} %get-tuple-element.326.ml.al, f32[1024,1024]{1,0:T(8,128)S(1)} %copy-done.3), custom_call_target="tpu_custom_call" | custom-call | flops 16106127360 | bytes 83886080 | tf_op jit(solution)/shard_map/affine_parts/pallas_call | solution.py:284
  70.1 1.6 %collective-permute-start.25 = (f32[264,128]{1,0:T(8,128)S(1)}, f32[264,128]{1,0:T(8,128)S(1)}, u32[]{:S(2)}, u32[]{:S(2)}) collective-permute-start(f32[264,128]{1,0:T(8,128)S(1)} %get-tuple-element.383), channel_id=1, source_target_pairs={{0,2},{1,3},{2,0},{3,1},{4,6},{5,7},{6,4},{7,5},{8,10},{9,11},{10,... | collective-permute-start | bytes 405512 | tf_op jit(solution)/shard_map/ppermute | solution.py:499
  71.9 2.4 %affine_parts.4.refs_5_.refs_1_ = f32[256,1024]{1,0:T(8,128)S(1)} custom-call(bf16[1024,1024]{1,0:T(8,128)(2,1)S(1)} %get-tuple-element.325.mh.ah, bf16[1024,1024]{1,0:T(8,128)(2,1)S(1)} %get-tuple-element.326.ml.al, f32[1024,1024]{1,0:T(8,128)S(1)} %copy-done.3), custom_call_target="tpu_custom_call" | custom-call | flops 16106127360 | bytes 83886080 | tf_op jit(solution)/shard_map/affine_parts/pallas_call | solution.py:284
  74.4 1.8 %collective-permute-start.23 = (f32[264,128]{1,0:T(8,128)S(1)}, f32[264,128]{1,0:T(8,128)S(1)}, u32[]{:S(2)}, u32[]{:S(2)}) collective-permute-start(f32[264,128]{1,0:T(8,128)S(1)} %get-tuple-element.385), channel_id=1, source_target_pairs={{0,6},{1,7},{2,4},{3,5},{4,2},{5,3},{6,0},{7,1},{8,14},{9,15},{10,... | collective-permute-start | bytes 405512 | tf_op jit(solution)/shard_map/ppermute | solution.py:499
  76.2 3.4 %collective-permute-start.26 = (f32[264,128]{1,0:T(8,128)S(1)}, f32[264,128]{1,0:T(8,128)S(1)}, u32[]{:S(2)}, u32[]{:S(2)}) collective-permute-start(f32[264,128]{1,0:T(8,128)S(1)} %fusion.1), channel_id=1, source_target_pairs={{0,8},{1,9},{2,10},{3,11},{4,12},{5,13},{6,14},{7,15},{8,0},{9,1},... | collective-permute-start | bytes 405512 | tf_op jit(solution)/shard_map/ppermute | solution.py:499
  79.6 3.7 %affine_parts.5.refs_6_.refs_2_ = f32[512,1024]{1,0:T(8,128)S(1)} custom-call(bf16[1024,1024]{1,0:T(8,128)(2,1)S(1)} %get-tuple-element.325.mh.ah, bf16[1024,1024]{1,0:T(8,128)(2,1)S(1)} %get-tuple-element.326.ml.al, f32[1024,1024]{1,0:T(8,128)S(1)} %copy-done.3), custom_call_target="tpu_custom_call" | custom-call | flops 32212254720 | bytes 83886080 | tf_op jit(solution)/shard_map/affine_parts/pallas_call | solution.py:284
  83.8 2.0 %collective-permute-start.27 = (f32[264,128]{1,0:T(8,128)S(1)}, f32[264,128]{1,0:T(8,128)S(1)}, u32[]{:S(2)}, u32[]{:S(2)}) collective-permute-start(f32[264,128]{1,0:T(8,128)S(1)} %fusion.3), channel_id=1, source_target_pairs={{0,8},{1,9},{2,10},{3,11},{4,12},{5,13},{6,14},{7,15},{8,0},{9,1},... | collective-permute-start | bytes 405512 | tf_op jit(solution)/shard_map/ppermute | solution.py:499
  87.3 2.3 %collective-permute-start.29 = (f32[264,128]{1,0:T(8,128)S(1)}, f32[264,128]{1,0:T(8,128)S(1)}, u32[]{:S(2)}, u32[]{:S(2)}) collective-permute-start(f32[264,128]{1,0:T(8,128)S(1)} %add.93), channel_id=1, source_target_pairs={{0,4},{1,5},{2,6},{3,7},{4,0},{5,1},{6,2},{7,3},{8,12},{9,13},{10,... | collective-permute-start | bytes 405512 | tf_op jit(solution)/shard_map/ppermute | solution.py:499
  89.7 3.1 %collective-permute-done.27 = f32[264,128]{1,0:T(8,128)S(1)} collective-permute-done((f32[264,128]{1,0:T(8,128)S(1)}, f32[264,128]{1,0:T(8,128)S(1)}, u32[]{:S(2)}, u32[]{:S(2)}) %collective-permute-start.27) | collective-permute-done | bytes 135200 | tf_op jit(solution)/shard_map/ppermute | solution.py:499
  93.5 2.9 %collective-permute-start.32 = (f32[264,128]{1,0:T(8,128)S(1)}, f32[264,128]{1,0:T(8,128)S(1)}, u32[]{:S(2)}, u32[]{:S(2)}) collective-permute-start(f32[264,128]{1,0:T(8,128)S(1)} %add.92), channel_id=1, source_target_pairs={{0,6},{1,7},{2,4},{3,5},{4,2},{5,3},{6,0},{7,1},{8,14},{9,15},{10,... | collective-permute-start | bytes 405512 | tf_op jit(solution)/shard_map/ppermute | solution.py:499
  96.4 2.3 %collective-permute-done.28 = f32[264,128]{1,0:T(8,128)S(1)} collective-permute-done((f32[264,128]{1,0:T(8,128)S(1)}, f32[264,128]{1,0:T(8,128)S(1)}, u32[]{:S(2)}, u32[]{:S(2)}) %collective-permute-start.28) | collective-permute-done | bytes 135200 | tf_op jit(solution)/shard_map/ppermute | solution.py:499
  100.7 2.2 %first_part.3 = (f32[1024,256]{1,0:T(8,128)S(1)}, bf16[1024,1024]{1,0:T(8,128)(2,1)S(1)}, bf16[1024,1024]{1,0:T(8,128)(2,1)S(1)}) custom-call(s32[1]{0:T(128)} %bitcast.me_ref, f32[1056,128]{1,0:T(8,128)S(1)} %pad_maximum_fusion.2.refs_0_, f32[1056,128]{1,0:T(8,128)S(1)} %collective-permute-done.31.refs_1_, ...), custom_call_target="tpu_custom_call" | custom-call | flops 32212254720 | bytes 125829120 | tf_op jit(solution)/shard_map/first_part/pallas_call | solution.py:338
  104.2 1.8 %other_part.1.refs_5_ = f32[1024,768]{1,0:T(8,128)S(1)} custom-call(bf16[1024,1024]{1,0:T(8,128)(2,1)S(1)} %get-tuple-element.379.refs_2_.ah, bf16[1024,1024]{1,0:T(8,128)(2,1)S(1)} %get-tuple-element.380.refs_3_.al, bf16[1024,1024]{1,0:T(8,128)(2,1)S(1)} %get-tuple-element.376.hi, bf16[1024,1024]{1,0:T(8,128)(2,1)S(1)} %get-tuple-element.377.lo, ...), custom_call_target="tpu_custom_call" | custom-call | flops 16106127360 | bytes 125829120 | tf_op jit(solution)/shard_map/other_part/pallas_call | solution.py:353
  106.1 4.9 %last.1 = f32[1024,1024]{1,0:T(8,128)} custom-call(s32[1]{0:T(128)} %bitcast.me_ref, f32[1056,128]{1,0:T(8,128)S(1)} %pad_maximum_fusion.3.refs_0_, f32[1056,128]{1,0:T(8,128)S(1)} %collective-permute-done.35.refs_1_, bf16[1024,1024]{1,0:T(8,128)(2,1)S(1)} %get-tuple-element.379.refs_2_.ah, bf16[1024,1024]{1,0:T(8,128)(2,1)S(1)} %get-tuple-element.380.refs_3_.al, ...), custom_call_target="tpu_custom_call" | custom-call | flops 32212254720 | bytes 125829120 | tf_op jit(solution)/shard_map/last/pallas_call | solution.py:476
  (90 shorter events, 18.3 us)
Async XLA Ops:
  6.9 4.2 %collective-permute-start = (f32[1056,128]{1,0:T(8,128)S(1)}, f32[1056,128]{1,0:T(8,128)S(1)}, u32[]{:S(2)}, u32[]{:S(2)}) collective-permute-start(f32[1056,128]{1,0:T(8,128)S(1)} %get-tuple-element.200), channel_id=1, source_target_pairs={{0,1},{1,0},{2,3},{3,2},{4,5},{5,4},{6,7},{7,6},{8,9},{9,8},{10,11... | collective-permute-start | bytes 1622024 | tf_op jit(solution)/shard_map/ppermute | solution.py:499
  11.2 13.0 %collective-permute-start.4 = (f32[264,128]{1,0:T(8,128)S(1)}, f32[264,128]{1,0:T(8,128)S(1)}, u32[]{:S(2)}, u32[]{:S(2)}) collective-permute-start(f32[264,128]{1,0:T(8,128)S(1)} %get-tuple-element.392), channel_id=1, source_target_pairs={{0,2},{1,3},{2,0},{3,1},{4,6},{5,7},{6,4},{7,5},{8,10},{9,11},{10,... | collective-permute-start | bytes 405512 | tf_op jit(solution)/shard_map/ppermute | solution.py:499
  13.8 10.5 %collective-permute-start.3 = (f32[264,128]{1,0:T(8,128)S(1)}, f32[264,128]{1,0:T(8,128)S(1)}, u32[]{:S(2)}, u32[]{:S(2)}) collective-permute-start(f32[264,128]{1,0:T(8,128)S(1)} %get-tuple-element.393), channel_id=1, source_target_pairs={{0,4},{1,5},{2,6},{3,7},{4,0},{5,1},{6,2},{7,3},{8,12},{9,13},{10,... | collective-permute-start | bytes 405512 | tf_op jit(solution)/shard_map/ppermute | solution.py:499
  15.4 8.9 %collective-permute-start.2 = (f32[264,128]{1,0:T(8,128)S(1)}, f32[264,128]{1,0:T(8,128)S(1)}, u32[]{:S(2)}, u32[]{:S(2)}) collective-permute-start(f32[264,128]{1,0:T(8,128)S(1)} %get-tuple-element.394), channel_id=1, source_target_pairs={{0,6},{1,7},{2,4},{3,5},{4,2},{5,3},{6,0},{7,1},{8,14},{9,15},{10,... | collective-permute-start | bytes 405512 | tf_op jit(solution)/shard_map/ppermute | solution.py:499
  15.4 2.6 %collective-permute-start.1 = (f32[1056,128]{1,0:T(8,128)S(1)}, f32[1056,128]{1,0:T(8,128)S(1)}, u32[]{:S(2)}, u32[]{:S(2)}) collective-permute-start(f32[1056,128]{1,0:T(8,128)S(1)} %get-tuple-element.206), channel_id=1, source_target_pairs={{0,1},{1,0},{2,3},{3,2},{4,5},{5,4},{6,7},{7,6},{8,9},{9,8},{10,11... | collective-permute-start | bytes 1622024 | tf_op jit(solution)/shard_map/ppermute | solution.py:499
  18.1 14.7 %collective-permute-start.7 = (f32[264,128]{1,0:T(8,128)S(1)}, f32[264,128]{1,0:T(8,128)S(1)}, u32[]{:S(2)}, u32[]{:S(2)}) collective-permute-start(f32[264,128]{1,0:T(8,128)S(1)} %get-tuple-element.389), channel_id=1, source_target_pairs={{0,2},{1,3},{2,0},{3,1},{4,6},{5,7},{6,4},{7,5},{8,10},{9,11},{10,... | collective-permute-start | bytes 405512 | tf_op jit(solution)/shard_map/ppermute | solution.py:499
  20.0 12.8 %collective-permute-start.6 = (f32[264,128]{1,0:T(8,128)S(1)}, f32[264,128]{1,0:T(8,128)S(1)}, u32[]{:S(2)}, u32[]{:S(2)}) collective-permute-start(f32[264,128]{1,0:T(8,128)S(1)} %get-tuple-element.390), channel_id=1, source_target_pairs={{0,4},{1,5},{2,6},{3,7},{4,0},{5,1},{6,2},{7,3},{8,12},{9,13},{10,... | collective-permute-start | bytes 405512 | tf_op jit(solution)/shard_map/ppermute | solution.py:499
  24.2 9.3 %collective-permute-start.5 = (f32[264,128]{1,0:T(8,128)S(1)}, f32[264,128]{1,0:T(8,128)S(1)}, u32[]{:S(2)}, u32[]{:S(2)}) collective-permute-start(f32[264,128]{1,0:T(8,128)S(1)} %get-tuple-element.391), channel_id=1, source_target_pairs={{0,6},{1,7},{2,4},{3,5},{4,2},{5,3},{6,0},{7,1},{8,14},{9,15},{10,... | collective-permute-start | bytes 405512 | tf_op jit(solution)/shard_map/ppermute | solution.py:499
  24.4 10.0 %collective-permute-start.8 = (f32[264,128]{1,0:T(8,128)S(1)}, f32[264,128]{1,0:T(8,128)S(1)}, u32[]{:S(2)}, u32[]{:S(2)}) collective-permute-start(f32[264,128]{1,0:T(8,128)S(1)} %fusion.7), channel_id=1, source_target_pairs={{0,8},{1,9},{2,10},{3,11},{4,12},{5,13},{6,14},{7,15},{8,0},{9,1},... | collective-permute-start | bytes 405512 | tf_op jit(solution)/shard_map/ppermute | solution.py:499
  33.6 8.4 %collective-permute-start.9 = (f32[264,128]{1,0:T(8,128)S(1)}, f32[264,128]{1,0:T(8,128)S(1)}, u32[]{:S(2)}, u32[]{:S(2)}) collective-permute-start(f32[264,128]{1,0:T(8,128)S(1)} %fusion.5), channel_id=1, source_target_pairs={{0,8},{1,9},{2,10},{3,11},{4,12},{5,13},{6,14},{7,15},{8,0},{9,1},... | collective-permute-start | bytes 405512 | tf_op jit(solution)/shard_map/ppermute | solution.py:499
  34.4 9.2 %collective-permute-start.12 = (f32[264,128]{1,0:T(8,128)S(1)}, f32[264,128]{1,0:T(8,128)S(1)}, u32[]{:S(2)}, u32[]{:S(2)}) collective-permute-start(f32[264,128]{1,0:T(8,128)S(1)} %add.82), channel_id=1, source_target_pairs={{0,2},{1,3},{2,0},{3,1},{4,6},{5,7},{6,4},{7,5},{8,10},{9,11},{10,... | collective-permute-start | bytes 405512 | tf_op jit(solution)/shard_map/ppermute | solution.py:499
  34.9 10.7 %collective-permute-start.11 = (f32[264,128]{1,0:T(8,128)S(1)}, f32[264,128]{1,0:T(8,128)S(1)}, u32[]{:S(2)}, u32[]{:S(2)}) collective-permute-start(f32[264,128]{1,0:T(8,128)S(1)} %add.82), channel_id=1, source_target_pairs={{0,4},{1,5},{2,6},{3,7},{4,0},{5,1},{6,2},{7,3},{8,12},{9,13},{10,... | collective-permute-start | bytes 405512 | tf_op jit(solution)/shard_map/ppermute | solution.py:499
  36.7 8.8 %collective-permute-start.10 = (f32[264,128]{1,0:T(8,128)S(1)}, f32[264,128]{1,0:T(8,128)S(1)}, u32[]{:S(2)}, u32[]{:S(2)}) collective-permute-start(f32[264,128]{1,0:T(8,128)S(1)} %add.82), channel_id=1, source_target_pairs={{0,6},{1,7},{2,4},{3,5},{4,2},{5,3},{6,0},{7,1},{8,14},{9,15},{10,... | collective-permute-start | bytes 405512 | tf_op jit(solution)/shard_map/ppermute | solution.py:499
  42.0 9.4 %collective-permute-start.16 = (f32[264,128]{1,0:T(8,128)S(1)}, f32[264,128]{1,0:T(8,128)S(1)}, u32[]{:S(2)}, u32[]{:S(2)}) collective-permute-start(f32[264,128]{1,0:T(8,128)S(1)} %add.83), channel_id=1, source_target_pairs={{0,2},{1,3},{2,0},{3,1},{4,6},{5,7},{6,4},{7,5},{8,10},{9,11},{10,... | collective-permute-start | bytes 405512 | tf_op jit(solution)/shard_map/ppermute | solution.py:499
  43.3 8.1 %collective-permute-start.15 = (f32[264,128]{1,0:T(8,128)S(1)}, f32[264,128]{1,0:T(8,128)S(1)}, u32[]{:S(2)}, u32[]{:S(2)}) collective-permute-start(f32[264,128]{1,0:T(8,128)S(1)} %add.83), channel_id=1, source_target_pairs={{0,4},{1,5},{2,6},{3,7},{4,0},{5,1},{6,2},{7,3},{8,12},{9,13},{10,... | collective-permute-start | bytes 405512 | tf_op jit(solution)/shard_map/ppermute | solution.py:499
  43.6 7.9 %collective-permute-start.14 = (f32[264,128]{1,0:T(8,128)S(1)}, f32[264,128]{1,0:T(8,128)S(1)}, u32[]{:S(2)}, u32[]{:S(2)}) collective-permute-start(f32[264,128]{1,0:T(8,128)S(1)} %add.83), channel_id=1, source_target_pairs={{0,6},{1,7},{2,4},{3,5},{4,2},{5,3},{6,0},{7,1},{8,14},{9,15},{10,... | collective-permute-start | bytes 405512 | tf_op jit(solution)/shard_map/ppermute | solution.py:499
  59.6 4.3 %collective-permute-start.18 = (f32[1056,128]{1,0:T(8,128)S(1)}, f32[1056,128]{1,0:T(8,128)S(1)}, u32[]{:S(2)}, u32[]{:S(2)}) collective-permute-start(f32[1056,128]{1,0:T(8,128)S(1)} %get-tuple-element.308), channel_id=1, source_target_pairs={{0,1},{1,0},{2,3},{3,2},{4,5},{5,4},{6,7},{7,6},{8,9},{9,8},{10,11... | collective-permute-start | bytes 1622024 | tf_op jit(solution)/shard_map/ppermute | solution.py:499
  63.9 10.4 %collective-permute-start.22 = (f32[264,128]{1,0:T(8,128)S(1)}, f32[264,128]{1,0:T(8,128)S(1)}, u32[]{:S(2)}, u32[]{:S(2)}) collective-permute-start(f32[264,128]{1,0:T(8,128)S(1)} %get-tuple-element.386), channel_id=1, source_target_pairs={{0,2},{1,3},{2,0},{3,1},{4,6},{5,7},{6,4},{7,5},{8,10},{9,11},{10,... | collective-permute-start | bytes 405512 | tf_op jit(solution)/shard_map/ppermute | solution.py:499
  65.6 10.6 %collective-permute-start.21 = (f32[264,128]{1,0:T(8,128)S(1)}, f32[264,128]{1,0:T(8,128)S(1)}, u32[]{:S(2)}, u32[]{:S(2)}) collective-permute-start(f32[264,128]{1,0:T(8,128)S(1)} %get-tuple-element.387), channel_id=1, source_target_pairs={{0,4},{1,5},{2,6},{3,7},{4,0},{5,1},{6,2},{7,3},{8,12},{9,13},{10,... | collective-permute-start | bytes 405512 | tf_op jit(solution)/shard_map/ppermute | solution.py:499
  65.8 10.4 %collective-permute-start.20 = (f32[264,128]{1,0:T(8,128)S(1)}, f32[264,128]{1,0:T(8,128)S(1)}, u32[]{:S(2)}, u32[]{:S(2)}) collective-permute-start(f32[264,128]{1,0:T(8,128)S(1)} %get-tuple-element.388), channel_id=1, source_target_pairs={{0,6},{1,7},{2,4},{3,5},{4,2},{5,3},{6,0},{7,1},{8,14},{9,15},{10,... | collective-permute-start | bytes 405512 | tf_op jit(solution)/shard_map/ppermute | solution.py:499
  67.5 2.5 %collective-permute-start.19 = (f32[1056,128]{1,0:T(8,128)S(1)}, f32[1056,128]{1,0:T(8,128)S(1)}, u32[]{:S(2)}, u32[]{:S(2)}) collective-permute-start(f32[1056,128]{1,0:T(8,128)S(1)} %get-tuple-element.314), channel_id=1, source_target_pairs={{0,1},{1,0},{2,3},{3,2},{4,5},{5,4},{6,7},{7,6},{8,9},{9,8},{10,11... | collective-permute-start | bytes 1622024 | tf_op jit(solution)/shard_map/ppermute | solution.py:499
  70.1 13.2 %collective-permute-start.25 = (f32[264,128]{1,0:T(8,128)S(1)}, f32[264,128]{1,0:T(8,128)S(1)}, u32[]{:S(2)}, u32[]{:S(2)}) collective-permute-start(f32[264,128]{1,0:T(8,128)S(1)} %get-tuple-element.383), channel_id=1, source_target_pairs={{0,2},{1,3},{2,0},{3,1},{4,6},{5,7},{6,4},{7,5},{8,10},{9,11},{10,... | collective-permute-start | bytes 405512 | tf_op jit(solution)/shard_map/ppermute | solution.py:499
  71.7 11.6 %collective-permute-start.24 = (f32[264,128]{1,0:T(8,128)S(1)}, f32[264,128]{1,0:T(8,128)S(1)}, u32[]{:S(2)}, u32[]{:S(2)}) collective-permute-start(f32[264,128]{1,0:T(8,128)S(1)} %get-tuple-element.384), channel_id=1, source_target_pairs={{0,4},{1,5},{2,6},{3,7},{4,0},{5,1},{6,2},{7,3},{8,12},{9,13},{10,... | collective-permute-start | bytes 405512 | tf_op jit(solution)/shard_map/ppermute | solution.py:499
  74.4 9.3 %collective-permute-start.23 = (f32[264,128]{1,0:T(8,128)S(1)}, f32[264,128]{1,0:T(8,128)S(1)}, u32[]{:S(2)}, u32[]{:S(2)}) collective-permute-start(f32[264,128]{1,0:T(8,128)S(1)} %get-tuple-element.385), channel_id=1, source_target_pairs={{0,6},{1,7},{2,4},{3,5},{4,2},{5,3},{6,0},{7,1},{8,14},{9,15},{10,... | collective-permute-start | bytes 405512 | tf_op jit(solution)/shard_map/ppermute | solution.py:499
  76.2 9.6 %collective-permute-start.26 = (f32[264,128]{1,0:T(8,128)S(1)}, f32[264,128]{1,0:T(8,128)S(1)}, u32[]{:S(2)}, u32[]{:S(2)}) collective-permute-start(f32[264,128]{1,0:T(8,128)S(1)} %fusion.1), channel_id=1, source_target_pairs={{0,8},{1,9},{2,10},{3,11},{4,12},{5,13},{6,14},{7,15},{8,0},{9,1},... | collective-permute-start | bytes 405512 | tf_op jit(solution)/shard_map/ppermute | solution.py:499
  83.8 9.0 %collective-permute-start.27 = (f32[264,128]{1,0:T(8,128)S(1)}, f32[264,128]{1,0:T(8,128)S(1)}, u32[]{:S(2)}, u32[]{:S(2)}) collective-permute-start(f32[264,128]{1,0:T(8,128)S(1)} %fusion.3), channel_id=1, source_target_pairs={{0,8},{1,9},{2,10},{3,11},{4,12},{5,13},{6,14},{7,15},{8,0},{9,1},... | collective-permute-start | bytes 405512 | tf_op jit(solution)/shard_map/ppermute | solution.py:499
  85.8 7.7 %collective-permute-start.30 = (f32[264,128]{1,0:T(8,128)S(1)}, f32[264,128]{1,0:T(8,128)S(1)}, u32[]{:S(2)}, u32[]{:S(2)}) collective-permute-start(f32[264,128]{1,0:T(8,128)S(1)} %add.93), channel_id=1, source_target_pairs={{0,2},{1,3},{2,0},{3,1},{4,6},{5,7},{6,4},{7,5},{8,10},{9,11},{10,... | collective-permute-start | bytes 405512 | tf_op jit(solution)/shard_map/ppermute | solution.py:499
  87.3 9.1 %collective-permute-start.29 = (f32[264,128]{1,0:T(8,128)S(1)}, f32[264,128]{1,0:T(8,128)S(1)}, u32[]{:S(2)}, u32[]{:S(2)}) collective-permute-start(f32[264,128]{1,0:T(8,128)S(1)} %add.93), channel_id=1, source_target_pairs={{0,4},{1,5},{2,6},{3,7},{4,0},{5,1},{6,2},{7,3},{8,12},{9,13},{10,... | collective-permute-start | bytes 405512 | tf_op jit(solution)/shard_map/ppermute | solution.py:499
  89.6 9.1 %collective-permute-start.28 = (f32[264,128]{1,0:T(8,128)S(1)}, f32[264,128]{1,0:T(8,128)S(1)}, u32[]{:S(2)}, u32[]{:S(2)}) collective-permute-start(f32[264,128]{1,0:T(8,128)S(1)} %add.93), channel_id=1, source_target_pairs={{0,6},{1,7},{2,4},{3,5},{4,2},{5,3},{6,0},{7,1},{8,14},{9,15},{10,... | collective-permute-start | bytes 405512 | tf_op jit(solution)/shard_map/ppermute | solution.py:499
  92.8 10.1 %collective-permute-start.34 = (f32[264,128]{1,0:T(8,128)S(1)}, f32[264,128]{1,0:T(8,128)S(1)}, u32[]{:S(2)}, u32[]{:S(2)}) collective-permute-start(f32[264,128]{1,0:T(8,128)S(1)} %add.92), channel_id=1, source_target_pairs={{0,2},{1,3},{2,0},{3,1},{4,6},{5,7},{6,4},{7,5},{8,10},{9,11},{10,... | collective-permute-start | bytes 405512 | tf_op jit(solution)/shard_map/ppermute | solution.py:499
  93.5 9.5 %collective-permute-start.33 = (f32[264,128]{1,0:T(8,128)S(1)}, f32[264,128]{1,0:T(8,128)S(1)}, u32[]{:S(2)}, u32[]{:S(2)}) collective-permute-start(f32[264,128]{1,0:T(8,128)S(1)} %add.92), channel_id=1, source_target_pairs={{0,4},{1,5},{2,6},{3,7},{4,0},{5,1},{6,2},{7,3},{8,12},{9,13},{10,... | collective-permute-start | bytes 405512 | tf_op jit(solution)/shard_map/ppermute | solution.py:499
  93.5 10.6 %collective-permute-start.32 = (f32[264,128]{1,0:T(8,128)S(1)}, f32[264,128]{1,0:T(8,128)S(1)}, u32[]{:S(2)}, u32[]{:S(2)}) collective-permute-start(f32[264,128]{1,0:T(8,128)S(1)} %add.92), channel_id=1, source_target_pairs={{0,6},{1,7},{2,4},{3,5},{4,2},{5,3},{6,0},{7,1},{8,14},{9,15},{10,... | collective-permute-start | bytes 405512 | tf_op jit(solution)/shard_map/ppermute | solution.py:499
  (10 other events, 72.1 us)

commit v11 on v10

--- a/solution.py
+++ b/solution.py
@@ -155,8 +155,18 @@
     return [struct(shards // 2 * shard_rows(size, shards), B)] * 2
 
 
+def outer_rows(ah, al, columns=slice(None)):
+    q = ah.shape[0] // 4
+    return [jnp.concatenate([x[:q, columns], x[3 * q:, columns]], axis=0) for x in (ah, al)]
+
+
+def rest_shape(size):
+    return struct(size // 4, size // 2)
+
+
 def first_gram_kernel(
-    shards, me_ref, a_hbm, b_hbm, keep_ref, send_ref, ah, al, bh, bl, a_buf, b_buf, sems, g, packed
+    shards, me_ref, a_hbm, b_hbm, keep_ref, send_ref, rest_ref, ah, al, bh, bl,
+    a_buf, b_buf, sems, g, packed
 ):
     rows, size = a_buf.shape
     q = size // 4
@@ -184,11 +194,15 @@
             start(step + 2)
         ah[:, r], al[:, r] = split(a_buf[r].T)
         bh[r], bl[r] = split(b_buf[r])
-        for r0, r1, c0, c1 in [(0, q, 0, size), (q, size, 0, q), (3 * q, size, 3 * q, size)]:
-            product = mm((ah[r0:r1, r], al[r0:r1, r]), (bh[r, c0:c1], bl[r, c0:c1]))
-            if step:
-                product += g[r0:r1, c0:c1]
-            g[r0:r1, c0:c1] = product
+        left = mm((ah[:, r], al[:, r]), (bh[r, :q], bl[r, :q]))
+        outer = mm(outer_rows(ah, al, r), (bh[r, q:], bl[r, q:]))
+        if step:
+            left += g[:, :q]
+            outer += jnp.concatenate([g[:q, q:], g[3 * q:, q:]], axis=0)
+        g[:, :q] = left
+        g[:q, q:] = outer[:q]
+        g[3 * q:, q:] = outer[q:]
+    rest_ref[...] = g[3 * q:, q:3 * q]
     pack(g, packed, keep_ref, send_ref, me_ref[0], shards, 0)
 
 
@@ -197,10 +211,11 @@
     hbm = pl.BlockSpec(memory_space=pltpu.HBM)
     return call(
         functools.partial(first_gram_kernel, shards), "first_gram",
-        halves(size, shards) + [struct(size, rows, dtype=BF16)] * 2 + [struct(rows, size, dtype=BF16)] * 2,
+        halves(size, shards) + [rest_shape(size)]
+        + [struct(size, rows, dtype=BF16)] * 2 + [struct(rows, size, dtype=BF16)] * 2,
         43, 0.5, 4,
         in_specs=[SMEM, hbm, hbm],
-        out_specs=[VMEM] * 6,
+        out_specs=[VMEM] * 7,
         scratch_shapes=[
             pltpu.VMEM((rows, size), F32), pltpu.VMEM((rows, size), F32),
             pltpu.SemaphoreType.DMA((2, 4)),
@@ -209,28 +224,21 @@
     )(me, a, b)
 
 
-def lower_product(g, ah, al, bh, bl):
-    size = g.shape[0]
-    q = size // 4
-    for r0, r1, c0, c1 in [(q, 3 * q, q, size), (3 * q, size, q, 3 * q)]:
-        c = slice(c0 - q, c1 - q)
-        g[r0:r1, c0:c1] = mm((ah[r0:r1, :], al[r0:r1, :]), (bh[:, c], bl[:, c]))
-
-
-def other_gram_kernel(shards, me_ref, ah, al, bh, bl, keep_ref, send_ref, g, packed):
+def inner_kernel(shards, me_ref, rest_ref, ah, al, bh, bl, keep_ref, send_ref, g, packed):
     q = g.shape[0] // 4
-    lower_product(g, ah, al, bh[:, q:], bl[:, q:])
+    g[q:3 * q, q:] = mm((ah[q:3 * q, :], al[q:3 * q, :]), (bh[:, q:], bl[:, q:]))
+    g[3 * q:, q:3 * q] = rest_ref[...]
     pack(g, packed, keep_ref, send_ref, me_ref[0], shards, 1)
 
 
-def other_gram(me, shards, ah, al, bh, bl):
+def inner_gram(me, shards, rest, ah, al, bh, bl):
     size = ah.shape[0]
     return call(
-        functools.partial(other_gram_kernel, shards), "other_gram", halves(size, shards), 18, 0.5, 2,
-        in_specs=[SMEM] + [VMEM] * 4,
+        functools.partial(inner_kernel, shards), "inner_gram", halves(size, shards), 18, 0.4, 2,
+        in_specs=[SMEM] + [VMEM] * 5,
         out_specs=[VMEM, VMEM],
         scratch_shapes=[pltpu.VMEM((size, size), F32), packed_scratch(size, shards)],
-    )(me, ah, al, bh, bl)
+    )(me, rest, ah, al, bh, bl)
 
 
 def tiles(count, tile, step):
@@ -403,7 +411,7 @@
 def second_gram_kernel(shards, count, me_ref, *refs):
     pieces, refs = refs[:count], refs[count:]
     (ah, al, base_ref, xh, xl, col_ref), refs = refs[:6], refs[6:]
-    keep_ref, send_ref, mh, ml, hi, lo, packed, g = refs
+    keep_ref, send_ref, rest_ref, mh, ml, hi, lo, packed, g = refs
     size = g.shape[0]
     q = size // 4
     unpack(pieces, packed, hi, lo, me_ref[0], shards, 1)
@@ -413,8 +421,10 @@
         mid = base_ref[:, c] - 0.5 * product
         mh[:, c], ml[:, c] = split(mid)
     g[:, :q] = col_ref[...]
-    g[:q, q:] = mm((xh[:q, :], xl[:q, :]), (mh[:, q:], ml[:, q:]))
-    g[3 * q:, 3 * q:] = mm((xh[3 * q:, :], xl[3 * q:, :]), (mh[:, 3 * q:], ml[:, 3 * q:]))
+    outer = mm(outer_rows(xh, xl), (mh[:, q:], ml[:, q:]))
+    g[:q, q:] = outer[:q]
+    g[3 * q:, q:] = outer[q:]
+    rest_ref[...] = outer[q:, :2 * q]
     pack(g, packed, keep_ref, send_ref, me_ref[0], shards, 0)
 
 
@@ -423,27 +433,11 @@
     part = struct(rows, size, dtype=BF16)
     return call(
         functools.partial(second_gram_kernel, shards, len(pieces)), "second_gram",
-        halves(size, shards) + [part, part], 20, 0.8, 5,
+        halves(size, shards) + [rest_shape(size), part, part], 20, 0.8, 5,
         in_specs=[SMEM] + [VMEM] * (len(pieces) + 6),
-        out_specs=[VMEM] * 4,
+        out_specs=[VMEM] * 5,
         scratch_shapes=sym_scratch(size, shards) + [pltpu.VMEM((size, size), F32)],
     )(me, *pieces, ah, al, base, xh, xl, col)
-
-
-def fourth_gram_kernel(shards, me_ref, xh, xl, mh, ml, keep_ref, send_ref, g, packed):
-    q = g.shape[0] // 4
-    lower_product(g, xh, xl, mh[:, q:], ml[:, q:])
-    pack(g, packed, keep_ref, send_ref, me_ref[0], shards, 1)
-
-
-def fourth_gram(me, shards, xh, xl, mh, ml):
-    size = xh.shape[0]
-    return call(
-        functools.partial(fourth_gram_kernel, shards), "fourth_gram", halves(size, shards), 18, 0.5, 2,
-        in_specs=[SMEM] + [VMEM] * 4,
-        out_specs=[VMEM, VMEM],
-        scratch_shapes=[pltpu.VMEM((size, size), F32), packed_scratch(size, shards)],
-    )(me, xh, xl, mh, ml)
 
 
 def last_kernel(shards, count, me_ref, *refs):
@@ -602,11 +596,11 @@
 
     keep, send, *parts = first_gram(me, SHARDS, env["x1"], env["c"])
     one = sum_chunks(
-        count, env, (keep, send), lambda env: other_gram(me, SHARDS, *parts),
+        count, env, (keep, send), lambda env: inner_gram(me, SHARDS, *parts),
         [direct(0), direct(1), direct_and_turn, cut_one], [middle, column],
     )
 
-    keep, send, env["mh"], env["ml"] = second_gram(
+    keep, send, rest_two, env["mh"], env["ml"] = second_gram(
         me, SHARDS, one, env["x1h"], env["x1l"], env["mid"], env["xh"], env["xl"], env["col"]
     )
 
@@ -633,7 +627,9 @@
 
     two = sum_chunks(
         count, env, (keep, send),
-        lambda env: fourth_gram(me, SHARDS, env["xh"], env["xl"], env["mh"], env["ml"]),
+        lambda env: inner_gram(
+            me, SHARDS, rest_two, env["xh"], env["xl"], env["mh"], env["ml"]
+        ),
         [last_direct(0), last_direct(1), last_direct(2), cut_zero], [result, rest],
     )
     return last_step(me, SHARDS, two, env["x0h"], env["x0l"], env["z"], env["rest"])

time: 111 us -> 112 us (level)
    pallas_call x2, Pallas kernels: 7.48 us -> 5.98 us  [inner_gram(): call(functools.partial(inner_kernel, shards), 'inner_gram', halves(size,...]
  transfers between devices with their start and end apart: 36 -> 36, of which waited for: 9 -> 9; matrix products, arithmetic and copies ran while one was open for 0% -> 0% of each run, Pallas kernels for 34% -> 33%
where the time goes in v11:
time: 112 us
  Pallas kernels  56.4 us (50%)
  starting transfers between devices  39.9 us (36%)
  waiting for transfers between devices  14 us (12%)
    ppermute x36, starting transfers between devices, swap(): return lax.ppermute(x, 'row', [(i, i ^ offset) for i in range(self.count)])  39.9 us
    ppermute x36, waiting for transfers between devices, swap(): return lax.ppermute(x, 'row', [(i, i ^ offset) for i in range(self.count)])  14 us
    pallas_call x3, Pallas kernels, affine(): call(affine_kernel, 'affine', struct(height, size), 18, height / rows, 2,...  9.18 us
    pallas_call x3, Pallas kernels, affine_parts(): call(affine_parts_kernel, 'affine_parts', struct(height, size), 18, heigh...  8.69 us
    pallas_call x1, Pallas kernels, first_gram(): call(functools.partial(first_gram_kernel, shards), 'first_gram', halves(s...  8 us
    pallas_call x1, Pallas kernels, second_gram(): call(functools.partial(second_gram_kernel, shards, len(pieces)), 'second_...  6.89 us
    pallas_call x2, Pallas kernels, inner_gram(): call(functools.partial(inner_kernel, shards), 'inner_gram', halves(size,...  5.98 us
    pallas_call x2, Pallas kernels, first_part(): call(functools.partial(first_part_kernel, shards, len(pieces), columns),...  5.95 us
  transfers between devices with their start and end apart: 36, of which 9 were waited for; matrix products, arithmetic and copies ran while one was open for 0% of the time, Pallas kernels for 33%

profile of v11, /device:TPU:0, one launch (start us, length us, event | category | flops | bytes accessed | tf_op | source)
XLA Modules:
  0.0 111.7 jit_solution(2506581362702733783)
XLA Ops:
  0.0 8.0 %first_gram.1 = (f32[1056,128]{1,0:T(8,128)S(1)}, f32[1056,128]{1,0:T(8,128)S(1)}, f32[256,512]{1,0:T(8,128)S(1)}, bf16[1024,1024]{1,0:T(8,128)(2,1)S(1)}, bf16[...) custom-call(s32[1]{0:T(128)} %bitcast.me_ref, f32[1024,1024]{1,0:T(8,128)} %x_ref.1, ...), custom_call_target="tpu_custom_call" | custom-call | flops 32212254720 | bytes 167772160 | tf_op jit(solution)/shard_map/first_gram/pallas_call | solution.py:212
  8.5 2.9 %inner_gram.2 = (f32[1056,128]{1,0:T(8,128)S(1)}, f32[1056,128]{1,0:T(8,128)S(1)}) custom-call(s32[1]{0:T(128)} %bitcast.me_ref, f32[256,512]{1,0:T(8,128)S(1)} %get-tuple-element.196.rest_ref, bf16[1024,1024]{1,0:T(8,128)(2,1)S(1)} %get-tuple-element.197.ah, bf16[1024,1024]{1,0:T(8,128)(2,1)S(1)} %get-tuple-element.198.al, ...), custom_call_target="tpu_custom_call" | custom-call | flops 25769803776 | bytes 83886080 | tf_op jit(solution)/shard_map/inner_gram/pallas_call | solution.py:236
  11.5 2.6 %collective-permute-start.4 = (f32[264,128]{1,0:T(8,128)S(1)}, f32[264,128]{1,0:T(8,128)S(1)}, u32[]{:S(2)}, u32[]{:S(2)}) collective-permute-start(f32[264,128]{1,0:T(8,128)S(1)} %get-tuple-element.396), channel_id=1, source_target_pairs={{0,2},{1,3},{2,0},{3,1},{4,6},{5,7},{6,4},{7,5},{8,10},{9,11},{10,... | collective-permute-start | bytes 405512 | tf_op jit(solution)/shard_map/ppermute | solution.py:493
  15.7 2.6 %affine.3.refs_4_ = f32[256,1024]{1,0:T(8,128)S(1)} custom-call(f32[1024,1024]{1,0:T(8,128)S(1)} %copy-done, f32[1024,1024]{1,0:T(8,128)S(1)} %copy-done.1), custom_call_target="tpu_custom_call" | custom-call | flops 16106127360 | bytes 83886080 | tf_op jit(solution)/shard_map/affine/pallas_call | solution.py:272
  18.4 2.0 %collective-permute-start.7 = (f32[264,128]{1,0:T(8,128)S(1)}, f32[264,128]{1,0:T(8,128)S(1)}, u32[]{:S(2)}, u32[]{:S(2)}) collective-permute-start(f32[264,128]{1,0:T(8,128)S(1)} %get-tuple-element.393), channel_id=1, source_target_pairs={{0,2},{1,3},{2,0},{3,1},{4,6},{5,7},{6,4},{7,5},{8,10},{9,11},{10,... | collective-permute-start | bytes 405512 | tf_op jit(solution)/shard_map/ppermute | solution.py:493
  20.4 1.6 %collective-permute-start.6 = (f32[264,128]{1,0:T(8,128)S(1)}, f32[264,128]{1,0:T(8,128)S(1)}, u32[]{:S(2)}, u32[]{:S(2)}) collective-permute-start(f32[264,128]{1,0:T(8,128)S(1)} %get-tuple-element.394), channel_id=1, source_target_pairs={{0,4},{1,5},{2,6},{3,7},{4,0},{5,1},{6,2},{7,3},{8,12},{9,13},{10,... | collective-permute-start | bytes 405512 | tf_op jit(solution)/shard_map/ppermute | solution.py:493
  22.0 2.6 %affine.4.refs_5_ = f32[256,1024]{1,0:T(8,128)S(1)} custom-call(f32[1024,1024]{1,0:T(8,128)S(1)} %copy-done, f32[1024,1024]{1,0:T(8,128)S(1)} %copy-done.1), custom_call_target="tpu_custom_call" | custom-call | flops 16106127360 | bytes 83886080 | tf_op jit(solution)/shard_map/affine/pallas_call | solution.py:272
  24.7 3.0 %collective-permute-start.8 = (f32[264,128]{1,0:T(8,128)S(1)}, f32[264,128]{1,0:T(8,128)S(1)}, u32[]{:S(2)}, u32[]{:S(2)}) collective-permute-start(f32[264,128]{1,0:T(8,128)S(1)} %fusion.7), channel_id=1, source_target_pairs={{0,8},{1,9},{2,10},{3,11},{4,12},{5,13},{6,14},{7,15},{8,0},{9,1},... | collective-permute-start | bytes 405512 | tf_op jit(solution)/shard_map/ppermute | solution.py:493
  27.8 4.0 %affine.5.refs_6_ = f32[512,1024]{1,0:T(8,128)S(1)} custom-call(f32[1024,1024]{1,0:T(8,128)S(1)} %copy-done, f32[1024,1024]{1,0:T(8,128)S(1)} %copy-done.1), custom_call_target="tpu_custom_call" | custom-call | flops 32212254720 | bytes 83886080 | tf_op jit(solution)/shard_map/affine/pallas_call | solution.py:272
  35.4 1.7 %collective-permute-start.11 = (f32[264,128]{1,0:T(8,128)S(1)}, f32[264,128]{1,0:T(8,128)S(1)}, u32[]{:S(2)}, u32[]{:S(2)}) collective-permute-start(f32[264,128]{1,0:T(8,128)S(1)} %add.82), channel_id=1, source_target_pairs={{0,4},{1,5},{2,6},{3,7},{4,0},{5,1},{6,2},{7,3},{8,12},{9,13},{10,... | collective-permute-start | bytes 405512 | tf_op jit(solution)/shard_map/ppermute | solution.py:493
  38.3 4.1 %collective-permute-done.9 = f32[264,128]{1,0:T(8,128)S(1)} collective-permute-done((f32[264,128]{1,0:T(8,128)S(1)}, f32[264,128]{1,0:T(8,128)S(1)}, u32[]{:S(2)}, u32[]{:S(2)}) %collective-permute-start.9) | collective-permute-done | bytes 135200 | tf_op jit(solution)/shard_map/ppermute | solution.py:493
  44.1 1.9 %collective-permute-start.14 = (f32[264,128]{1,0:T(8,128)S(1)}, f32[264,128]{1,0:T(8,128)S(1)}, u32[]{:S(2)}, u32[]{:S(2)}) collective-permute-start(f32[264,128]{1,0:T(8,128)S(1)} %add.83), channel_id=1, source_target_pairs={{0,6},{1,7},{2,4},{3,5},{4,2},{5,3},{6,0},{7,1},{8,14},{9,15},{10,... | collective-permute-start | bytes 405512 | tf_op jit(solution)/shard_map/ppermute | solution.py:493
  48.0 3.8 %first_part.2.mid_ref.refs_4_ = f32[1024,1024]{1,0:T(8,128)S(1)} custom-call(s32[1]{0:T(128)} %bitcast.me_ref, f32[1056,128]{1,0:T(8,128)S(1)} %pad_maximum_fusion.refs_0_, f32[1056,128]{1,0:T(8,128)S(1)} %collective-permute-done.13.refs_1_, bf16[1024,1024]{1,0:T(8,128)(2,1)S(1)} %get-tuple-element.302.refs_2_, ...), custom_call_target="tpu_custom_call" | custom-call | flops 32212254720 | bytes 125829120 | tf_op jit(solution)/shard_map/first_part/pallas_call | solution.py:346
  52.0 1.8 %column_product.1.refs_7_ = f32[1024,256]{1,0:T(8,128)S(1)} custom-call(bf16[1024,1024]{1,0:T(8,128)(2,1)S(1)} %get-tuple-element.300.xh.refs_5_.ah, bf16[1024,1024]{1,0:T(8,128)(2,1)S(1)} %get-tuple-element.301.xl.refs_6_.al, f32[1024,1024]{1,0:T(8,128)S(1)} %first_part.2.mid_ref.refs_4_), custom_call_target="tpu_custom_call" | custom-call | flops 16106127360 | bytes 83886080 | tf_op jit(solution)/shard_map/column_product/pallas_call | solution.py:377
  53.9 6.9 %second_gram.1 = (f32[1056,128]{1,0:T(8,128)S(1)}, f32[1056,128]{1,0:T(8,128)S(1)}, f32[256,512]{1,0:T(8,128)S(1)}, bf16[1024,1024]{1,0:T(8,128)(2,1)S(1)}, bf16[1024,1024]{1,0:T(8,128)(2,1)S(1)}) custom-call(s32[1]{0:T(128)} %bitcast.me_ref, f32[1056,128]{1,0:T(8,128)S(1)} %pad_maximum_fusion.1.refs_0_, f32[1056,128]{1,0:T(8,128)S(1)} %collective-permute-done.17.refs_1_, ...), custom_call_target="tpu_custom_call" | custom-call | flops 51539607552 | bytes 209715200 | tf_op jit(solution)/shard_map/second_gram/pallas_call | solution.py:434
  61.2 3.1 %inner_gram.3 = (f32[1056,128]{1,0:T(8,128)S(1)}, f32[1056,128]{1,0:T(8,128)S(1)}) custom-call(s32[1]{0:T(128)} %bitcast.me_ref, f32[256,512]{1,0:T(8,128)S(1)} %get-tuple-element.309.rest_ref, bf16[1024,1024]{1,0:T(8,128)(2,1)S(1)} %get-tuple-element.300.xh.refs_5_.ah, bf16[1024,1024]{1,0:T(8,128)(2,1)S(1)} %get-tuple-element.301.xl.refs_6_.al, ...), custom_call_target="tpu_custom_call" | custom-call | flops 25769803776 | bytes 83886080 | tf_op jit(solution)/shard_map/inner_gram/pallas_call | solution.py:236
  64.4 1.7 %collective-permute-start.22 = (f32[264,128]{1,0:T(8,128)S(1)}, f32[264,128]{1,0:T(8,128)S(1)}, u32[]{:S(2)}, u32[]{:S(2)}) collective-permute-start(f32[264,128]{1,0:T(8,128)S(1)} %get-tuple-element.390), channel_id=1, source_target_pairs={{0,2},{1,3},{2,0},{3,1},{4,6},{5,7},{6,4},{7,5},{8,10},{9,11},{10,... | collective-permute-start | bytes 405512 | tf_op jit(solution)/shard_map/ppermute | solution.py:493
  66.3 1.7 %collective-permute-start.20 = (f32[264,128]{1,0:T(8,128)S(1)}, f32[264,128]{1,0:T(8,128)S(1)}, u32[]{:S(2)}, u32[]{:S(2)}) collective-permute-start(f32[264,128]{1,0:T(8,128)S(1)} %get-tuple-element.392), channel_id=1, source_target_pairs={{0,6},{1,7},{2,4},{3,5},{4,2},{5,3},{6,0},{7,1},{8,14},{9,15},{10,... | collective-permute-start | bytes 405512 | tf_op jit(solution)/shard_map/ppermute | solution.py:493
  68.0 2.5 %affine_parts.3.refs_4_.refs_0_ = f32[256,1024]{1,0:T(8,128)S(1)} custom-call(bf16[1024,1024]{1,0:T(8,128)(2,1)S(1)} %get-tuple-element.329.bh.ah, bf16[1024,1024]{1,0:T(8,128)(2,1)S(1)} %get-tuple-element.330.bl.al, f32[1024,1024]{1,0:T(8,128)S(1)} %copy-done.3), custom_call_target="tpu_custom_call" | custom-call | flops 16106127360 | bytes 83886080 | tf_op jit(solution)/shard_map/affine_parts/pallas_call | solution.py:292
  70.6 1.7 %collective-permute-start.25 = (f32[264,128]{1,0:T(8,128)S(1)}, f32[264,128]{1,0:T(8,128)S(1)}, u32[]{:S(2)}, u32[]{:S(2)}) collective-permute-start(f32[264,128]{1,0:T(8,128)S(1)} %get-tuple-element.387), channel_id=1, source_target_pairs={{0,2},{1,3},{2,0},{3,1},{4,6},{5,7},{6,4},{7,5},{8,10},{9,11},{10,... | collective-permute-start | bytes 405512 | tf_op jit(solution)/shard_map/ppermute | solution.py:493
  72.4 2.5 %affine_parts.4.refs_5_.refs_1_ = f32[256,1024]{1,0:T(8,128)S(1)} custom-call(bf16[1024,1024]{1,0:T(8,128)(2,1)S(1)} %get-tuple-element.329.bh.ah, bf16[1024,1024]{1,0:T(8,128)(2,1)S(1)} %get-tuple-element.330.bl.al, f32[1024,1024]{1,0:T(8,128)S(1)} %copy-done.3), custom_call_target="tpu_custom_call" | custom-call | flops 16106127360 | bytes 83886080 | tf_op jit(solution)/shard_map/affine_parts/pallas_call | solution.py:292
  74.9 1.8 %collective-permute-start.23 = (f32[264,128]{1,0:T(8,128)S(1)}, f32[264,128]{1,0:T(8,128)S(1)}, u32[]{:S(2)}, u32[]{:S(2)}) collective-permute-start(f32[264,128]{1,0:T(8,128)S(1)} %get-tuple-element.389), channel_id=1, source_target_pairs={{0,6},{1,7},{2,4},{3,5},{4,2},{5,3},{6,0},{7,1},{8,14},{9,15},{10,... | collective-permute-start | bytes 405512 | tf_op jit(solution)/shard_map/ppermute | solution.py:493
  76.8 3.1 %collective-permute-start.26 = (f32[264,128]{1,0:T(8,128)S(1)}, f32[264,128]{1,0:T(8,128)S(1)}, u32[]{:S(2)}, u32[]{:S(2)}) collective-permute-start(f32[264,128]{1,0:T(8,128)S(1)} %fusion.1), channel_id=1, source_target_pairs={{0,8},{1,9},{2,10},{3,11},{4,12},{5,13},{6,14},{7,15},{8,0},{9,1},... | collective-permute-start | bytes 405512 | tf_op jit(solution)/shard_map/ppermute | solution.py:493
  79.9 3.7 %affine_parts.5.refs_6_.refs_2_ = f32[512,1024]{1,0:T(8,128)S(1)} custom-call(bf16[1024,1024]{1,0:T(8,128)(2,1)S(1)} %get-tuple-element.329.bh.ah, bf16[1024,1024]{1,0:T(8,128)(2,1)S(1)} %get-tuple-element.330.bl.al, f32[1024,1024]{1,0:T(8,128)S(1)} %copy-done.3), custom_call_target="tpu_custom_call" | custom-call | flops 32212254720 | bytes 83886080 | tf_op jit(solution)/shard_map/affine_parts/pallas_call | solution.py:292
  84.3 1.9 %collective-permute-start.27 = (f32[264,128]{1,0:T(8,128)S(1)}, f32[264,128]{1,0:T(8,128)S(1)}, u32[]{:S(2)}, u32[]{:S(2)}) collective-permute-start(f32[264,128]{1,0:T(8,128)S(1)} %fusion.3), channel_id=1, source_target_pairs={{0,8},{1,9},{2,10},{3,11},{4,12},{5,13},{6,14},{7,15},{8,0},{9,1},... | collective-permute-start | bytes 405512 | tf_op jit(solution)/shard_map/ppermute | solution.py:493
  87.8 2.3 %collective-permute-start.29 = (f32[264,128]{1,0:T(8,128)S(1)}, f32[264,128]{1,0:T(8,128)S(1)}, u32[]{:S(2)}, u32[]{:S(2)}) collective-permute-start(f32[264,128]{1,0:T(8,128)S(1)} %add.93), channel_id=1, source_target_pairs={{0,4},{1,5},{2,6},{3,7},{4,0},{5,1},{6,2},{7,3},{8,12},{9,13},{10,... | collective-permute-start | bytes 405512 | tf_op jit(solution)/shard_map/ppermute | solution.py:493
  90.2 3.1 %collective-permute-done.27 = f32[264,128]{1,0:T(8,128)S(1)} collective-permute-done((f32[264,128]{1,0:T(8,128)S(1)}, f32[264,128]{1,0:T(8,128)S(1)}, u32[]{:S(2)}, u32[]{:S(2)}) %collective-permute-start.27) | collective-permute-done | bytes 135200 | tf_op jit(solution)/shard_map/ppermute | solution.py:493
  94.0 3.0 %collective-permute-start.32 = (f32[264,128]{1,0:T(8,128)S(1)}, f32[264,128]{1,0:T(8,128)S(1)}, u32[]{:S(2)}, u32[]{:S(2)}) collective-permute-start(f32[264,128]{1,0:T(8,128)S(1)} %add.92), channel_id=1, source_target_pairs={{0,6},{1,7},{2,4},{3,5},{4,2},{5,3},{6,0},{7,1},{8,14},{9,15},{10,... | collective-permute-start | bytes 405512 | tf_op jit(solution)/shard_map/ppermute | solution.py:493
  97.0 2.2 %collective-permute-done.28 = f32[264,128]{1,0:T(8,128)S(1)} collective-permute-done((f32[264,128]{1,0:T(8,128)S(1)}, f32[264,128]{1,0:T(8,128)S(1)}, u32[]{:S(2)}, u32[]{:S(2)}) %collective-permute-start.28) | collective-permute-done | bytes 135200 | tf_op jit(solution)/shard_map/ppermute | solution.py:493
  101.2 2.2 %first_part.3 = (f32[1024,256]{1,0:T(8,128)S(1)}, bf16[1024,1024]{1,0:T(8,128)(2,1)S(1)}, bf16[1024,1024]{1,0:T(8,128)(2,1)S(1)}) custom-call(s32[1]{0:T(128)} %bitcast.me_ref, f32[1056,128]{1,0:T(8,128)S(1)} %pad_maximum_fusion.2.refs_0_, f32[1056,128]{1,0:T(8,128)S(1)} %collective-permute-done.31.refs_1_, ...), custom_call_target="tpu_custom_call" | custom-call | flops 32212254720 | bytes 125829120 | tf_op jit(solution)/shard_map/first_part/pallas_call | solution.py:346
  104.6 1.8 %other_part.1.refs_5_ = f32[1024,768]{1,0:T(8,128)S(1)} custom-call(bf16[1024,1024]{1,0:T(8,128)(2,1)S(1)} %get-tuple-element.383.refs_2_.ah, bf16[1024,1024]{1,0:T(8,128)(2,1)S(1)} %get-tuple-element.384.refs_3_.al, bf16[1024,1024]{1,0:T(8,128)(2,1)S(1)} %get-tuple-element.380.hi, bf16[1024,1024]{1,0:T(8,128)(2,1)S(1)} %get-tuple-element.381.lo, ...), custom_call_target="tpu_custom_call" | custom-call | flops 16106127360 | bytes 125829120 | tf_op jit(solution)/shard_map/other_part/pallas_call | solution.py:361
  106.6 4.9 %last.1 = f32[1024,1024]{1,0:T(8,128)} custom-call(s32[1]{0:T(128)} %bitcast.me_ref, f32[1056,128]{1,0:T(8,128)S(1)} %pad_maximum_fusion.3.refs_0_, f32[1056,128]{1,0:T(8,128)S(1)} %collective-permute-done.35.refs_1_, bf16[1024,1024]{1,0:T(8,128)(2,1)S(1)} %get-tuple-element.383.refs_2_.ah, bf16[1024,1024]{1,0:T(8,128)(2,1)S(1)} %get-tuple-element.384.refs_3_.al, ...), custom_call_target="tpu_custom_call" | custom-call | flops 32212254720 | bytes 125829120 | tf_op jit(solution)/shard_map/last/pallas_call | solution.py:470
  (90 shorter events, 18.4 us)
Async XLA Ops:
  8.0 3.4 %collective-permute-start = (f32[1056,128]{1,0:T(8,128)S(1)}, f32[1056,128]{1,0:T(8,128)S(1)}, u32[]{:S(2)}, u32[]{:S(2)}) collective-permute-start(f32[1056,128]{1,0:T(8,128)S(1)} %get-tuple-element.203), channel_id=1, source_target_pairs={{0,1},{1,0},{2,3},{3,2},{4,5},{5,4},{6,7},{7,6},{8,9},{9,8},{10,11... | collective-permute-start | bytes 1622024 | tf_op jit(solution)/shard_map/ppermute | solution.py:493
  11.5 13.1 %collective-permute-start.4 = (f32[264,128]{1,0:T(8,128)S(1)}, f32[264,128]{1,0:T(8,128)S(1)}, u32[]{:S(2)}, u32[]{:S(2)}) collective-permute-start(f32[264,128]{1,0:T(8,128)S(1)} %get-tuple-element.396), channel_id=1, source_target_pairs={{0,2},{1,3},{2,0},{3,1},{4,6},{5,7},{6,4},{7,5},{8,10},{9,11},{10,... | collective-permute-start | bytes 405512 | tf_op jit(solution)/shard_map/ppermute | solution.py:493
  14.1 10.5 %collective-permute-start.3 = (f32[264,128]{1,0:T(8,128)S(1)}, f32[264,128]{1,0:T(8,128)S(1)}, u32[]{:S(2)}, u32[]{:S(2)}) collective-permute-start(f32[264,128]{1,0:T(8,128)S(1)} %get-tuple-element.397), channel_id=1, source_target_pairs={{0,4},{1,5},{2,6},{3,7},{4,0},{5,1},{6,2},{7,3},{8,12},{9,13},{10,... | collective-permute-start | bytes 405512 | tf_op jit(solution)/shard_map/ppermute | solution.py:493
  15.7 9.0 %collective-permute-start.2 = (f32[264,128]{1,0:T(8,128)S(1)}, f32[264,128]{1,0:T(8,128)S(1)}, u32[]{:S(2)}, u32[]{:S(2)}) collective-permute-start(f32[264,128]{1,0:T(8,128)S(1)} %get-tuple-element.398), channel_id=1, source_target_pairs={{0,6},{1,7},{2,4},{3,5},{4,2},{5,3},{6,0},{7,1},{8,14},{9,15},{10,... | collective-permute-start | bytes 405512 | tf_op jit(solution)/shard_map/ppermute | solution.py:493
  15.7 2.6 %collective-permute-start.1 = (f32[1056,128]{1,0:T(8,128)S(1)}, f32[1056,128]{1,0:T(8,128)S(1)}, u32[]{:S(2)}, u32[]{:S(2)}) collective-permute-start(f32[1056,128]{1,0:T(8,128)S(1)} %get-tuple-element.209), channel_id=1, source_target_pairs={{0,1},{1,0},{2,3},{3,2},{4,5},{5,4},{6,7},{7,6},{8,9},{9,8},{10,11... | collective-permute-start | bytes 1622024 | tf_op jit(solution)/shard_map/ppermute | solution.py:493
  18.4 14.9 %collective-permute-start.7 = (f32[264,128]{1,0:T(8,128)S(1)}, f32[264,128]{1,0:T(8,128)S(1)}, u32[]{:S(2)}, u32[]{:S(2)}) collective-permute-start(f32[264,128]{1,0:T(8,128)S(1)} %get-tuple-element.393), channel_id=1, source_target_pairs={{0,2},{1,3},{2,0},{3,1},{4,6},{5,7},{6,4},{7,5},{8,10},{9,11},{10,... | collective-permute-start | bytes 405512 | tf_op jit(solution)/shard_map/ppermute | solution.py:493
  20.4 12.9 %collective-permute-start.6 = (f32[264,128]{1,0:T(8,128)S(1)}, f32[264,128]{1,0:T(8,128)S(1)}, u32[]{:S(2)}, u32[]{:S(2)}) collective-permute-start(f32[264,128]{1,0:T(8,128)S(1)} %get-tuple-element.394), channel_id=1, source_target_pairs={{0,4},{1,5},{2,6},{3,7},{4,0},{5,1},{6,2},{7,3},{8,12},{9,13},{10,... | collective-permute-start | bytes 405512 | tf_op jit(solution)/shard_map/ppermute | solution.py:493
  24.6 9.3 %collective-permute-start.5 = (f32[264,128]{1,0:T(8,128)S(1)}, f32[264,128]{1,0:T(8,128)S(1)}, u32[]{:S(2)}, u32[]{:S(2)}) collective-permute-start(f32[264,128]{1,0:T(8,128)S(1)} %get-tuple-element.395), channel_id=1, source_target_pairs={{0,6},{1,7},{2,4},{3,5},{4,2},{5,3},{6,0},{7,1},{8,14},{9,15},{10,... | collective-permute-start | bytes 405512 | tf_op jit(solution)/shard_map/ppermute | solution.py:493
  24.7 10.0 %collective-permute-start.8 = (f32[264,128]{1,0:T(8,128)S(1)}, f32[264,128]{1,0:T(8,128)S(1)}, u32[]{:S(2)}, u32[]{:S(2)}) collective-permute-start(f32[264,128]{1,0:T(8,128)S(1)} %fusion.7), channel_id=1, source_target_pairs={{0,8},{1,9},{2,10},{3,11},{4,12},{5,13},{6,14},{7,15},{8,0},{9,1},... | collective-permute-start | bytes 405512 | tf_op jit(solution)/shard_map/ppermute | solution.py:493
  33.9 8.4 %collective-permute-start.9 = (f32[264,128]{1,0:T(8,128)S(1)}, f32[264,128]{1,0:T(8,128)S(1)}, u32[]{:S(2)}, u32[]{:S(2)}) collective-permute-start(f32[264,128]{1,0:T(8,128)S(1)} %fusion.5), channel_id=1, source_target_pairs={{0,8},{1,9},{2,10},{3,11},{4,12},{5,13},{6,14},{7,15},{8,0},{9,1},... | collective-permute-start | bytes 405512 | tf_op jit(solution)/shard_map/ppermute | solution.py:493
  34.7 9.3 %collective-permute-start.12 = (f32[264,128]{1,0:T(8,128)S(1)}, f32[264,128]{1,0:T(8,128)S(1)}, u32[]{:S(2)}, u32[]{:S(2)}) collective-permute-start(f32[264,128]{1,0:T(8,128)S(1)} %add.82), channel_id=1, source_target_pairs={{0,2},{1,3},{2,0},{3,1},{4,6},{5,7},{6,4},{7,5},{8,10},{9,11},{10,... | collective-permute-start | bytes 405512 | tf_op jit(solution)/shard_map/ppermute | solution.py:493
  35.4 10.5 %collective-permute-start.11 = (f32[264,128]{1,0:T(8,128)S(1)}, f32[264,128]{1,0:T(8,128)S(1)}, u32[]{:S(2)}, u32[]{:S(2)}) collective-permute-start(f32[264,128]{1,0:T(8,128)S(1)} %add.82), channel_id=1, source_target_pairs={{0,4},{1,5},{2,6},{3,7},{4,0},{5,1},{6,2},{7,3},{8,12},{9,13},{10,... | collective-permute-start | bytes 405512 | tf_op jit(solution)/shard_map/ppermute | solution.py:493
  37.1 8.8 %collective-permute-start.10 = (f32[264,128]{1,0:T(8,128)S(1)}, f32[264,128]{1,0:T(8,128)S(1)}, u32[]{:S(2)}, u32[]{:S(2)}) collective-permute-start(f32[264,128]{1,0:T(8,128)S(1)} %add.82), channel_id=1, source_target_pairs={{0,6},{1,7},{2,4},{3,5},{4,2},{5,3},{6,0},{7,1},{8,14},{9,15},{10,... | collective-permute-start | bytes 405512 | tf_op jit(solution)/shard_map/ppermute | solution.py:493
  42.4 9.4 %collective-permute-start.16 = (f32[264,128]{1,0:T(8,128)S(1)}, f32[264,128]{1,0:T(8,128)S(1)}, u32[]{:S(2)}, u32[]{:S(2)}) collective-permute-start(f32[264,128]{1,0:T(8,128)S(1)} %add.83), channel_id=1, source_target_pairs={{0,2},{1,3},{2,0},{3,1},{4,6},{5,7},{6,4},{7,5},{8,10},{9,11},{10,... | collective-permute-start | bytes 405512 | tf_op jit(solution)/shard_map/ppermute | solution.py:493
  43.8 8.0 %collective-permute-start.15 = (f32[264,128]{1,0:T(8,128)S(1)}, f32[264,128]{1,0:T(8,128)S(1)}, u32[]{:S(2)}, u32[]{:S(2)}) collective-permute-start(f32[264,128]{1,0:T(8,128)S(1)} %add.83), channel_id=1, source_target_pairs={{0,4},{1,5},{2,6},{3,7},{4,0},{5,1},{6,2},{7,3},{8,12},{9,13},{10,... | collective-permute-start | bytes 405512 | tf_op jit(solution)/shard_map/ppermute | solution.py:493
  44.1 7.7 %collective-permute-start.14 = (f32[264,128]{1,0:T(8,128)S(1)}, f32[264,128]{1,0:T(8,128)S(1)}, u32[]{:S(2)}, u32[]{:S(2)}) collective-permute-start(f32[264,128]{1,0:T(8,128)S(1)} %add.83), channel_id=1, source_target_pairs={{0,6},{1,7},{2,4},{3,5},{4,2},{5,3},{6,0},{7,1},{8,14},{9,15},{10,... | collective-permute-start | bytes 405512 | tf_op jit(solution)/shard_map/ppermute | solution.py:493
  60.8 3.5 %collective-permute-start.18 = (f32[1056,128]{1,0:T(8,128)S(1)}, f32[1056,128]{1,0:T(8,128)S(1)}, u32[]{:S(2)}, u32[]{:S(2)}) collective-permute-start(f32[1056,128]{1,0:T(8,128)S(1)} %get-tuple-element.312), channel_id=1, source_target_pairs={{0,1},{1,0},{2,3},{3,2},{4,5},{5,4},{6,7},{7,6},{8,9},{9,8},{10,11... | collective-permute-start | bytes 1622024 | tf_op jit(solution)/shard_map/ppermute | solution.py:493
  64.4 10.5 %collective-permute-start.22 = (f32[264,128]{1,0:T(8,128)S(1)}, f32[264,128]{1,0:T(8,128)S(1)}, u32[]{:S(2)}, u32[]{:S(2)}) collective-permute-start(f32[264,128]{1,0:T(8,128)S(1)} %get-tuple-element.390), channel_id=1, source_target_pairs={{0,2},{1,3},{2,0},{3,1},{4,6},{5,7},{6,4},{7,5},{8,10},{9,11},{10,... | collective-permute-start | bytes 405512 | tf_op jit(solution)/shard_map/ppermute | solution.py:493
  66.2 10.6 %collective-permute-start.21 = (f32[264,128]{1,0:T(8,128)S(1)}, f32[264,128]{1,0:T(8,128)S(1)}, u32[]{:S(2)}, u32[]{:S(2)}) collective-permute-start(f32[264,128]{1,0:T(8,128)S(1)} %get-tuple-element.391), channel_id=1, source_target_pairs={{0,4},{1,5},{2,6},{3,7},{4,0},{5,1},{6,2},{7,3},{8,12},{9,13},{10,... | collective-permute-start | bytes 405512 | tf_op jit(solution)/shard_map/ppermute | solution.py:493
  66.3 10.4 %collective-permute-start.20 = (f32[264,128]{1,0:T(8,128)S(1)}, f32[264,128]{1,0:T(8,128)S(1)}, u32[]{:S(2)}, u32[]{:S(2)}) collective-permute-start(f32[264,128]{1,0:T(8,128)S(1)} %get-tuple-element.392), channel_id=1, source_target_pairs={{0,6},{1,7},{2,4},{3,5},{4,2},{5,3},{6,0},{7,1},{8,14},{9,15},{10,... | collective-permute-start | bytes 405512 | tf_op jit(solution)/shard_map/ppermute | solution.py:493
  68.0 2.5 %collective-permute-start.19 = (f32[1056,128]{1,0:T(8,128)S(1)}, f32[1056,128]{1,0:T(8,128)S(1)}, u32[]{:S(2)}, u32[]{:S(2)}) collective-permute-start(f32[1056,128]{1,0:T(8,128)S(1)} %get-tuple-element.318), channel_id=1, source_target_pairs={{0,1},{1,0},{2,3},{3,2},{4,5},{5,4},{6,7},{7,6},{8,9},{9,8},{10,11... | collective-permute-start | bytes 1622024 | tf_op jit(solution)/shard_map/ppermute | solution.py:493
  70.6 13.0 %collective-permute-start.25 = (f32[264,128]{1,0:T(8,128)S(1)}, f32[264,128]{1,0:T(8,128)S(1)}, u32[]{:S(2)}, u32[]{:S(2)}) collective-permute-start(f32[264,128]{1,0:T(8,128)S(1)} %get-tuple-element.387), channel_id=1, source_target_pairs={{0,2},{1,3},{2,0},{3,1},{4,6},{5,7},{6,4},{7,5},{8,10},{9,11},{10,... | collective-permute-start | bytes 405512 | tf_op jit(solution)/shard_map/ppermute | solution.py:493
  72.3 11.3 %collective-permute-start.24 = (f32[264,128]{1,0:T(8,128)S(1)}, f32[264,128]{1,0:T(8,128)S(1)}, u32[]{:S(2)}, u32[]{:S(2)}) collective-permute-start(f32[264,128]{1,0:T(8,128)S(1)} %get-tuple-element.388), channel_id=1, source_target_pairs={{0,4},{1,5},{2,6},{3,7},{4,0},{5,1},{6,2},{7,3},{8,12},{9,13},{10,... | collective-permute-start | bytes 405512 | tf_op jit(solution)/shard_map/ppermute | solution.py:493
  74.9 9.3 %collective-permute-start.23 = (f32[264,128]{1,0:T(8,128)S(1)}, f32[264,128]{1,0:T(8,128)S(1)}, u32[]{:S(2)}, u32[]{:S(2)}) collective-permute-start(f32[264,128]{1,0:T(8,128)S(1)} %get-tuple-element.389), channel_id=1, source_target_pairs={{0,6},{1,7},{2,4},{3,5},{4,2},{5,3},{6,0},{7,1},{8,14},{9,15},{10,... | collective-permute-start | bytes 405512 | tf_op jit(solution)/shard_map/ppermute | solution.py:493
  76.8 9.5 %collective-permute-start.26 = (f32[264,128]{1,0:T(8,128)S(1)}, f32[264,128]{1,0:T(8,128)S(1)}, u32[]{:S(2)}, u32[]{:S(2)}) collective-permute-start(f32[264,128]{1,0:T(8,128)S(1)} %fusion.1), channel_id=1, source_target_pairs={{0,8},{1,9},{2,10},{3,11},{4,12},{5,13},{6,14},{7,15},{8,0},{9,1},... | collective-permute-start | bytes 405512 | tf_op jit(solution)/shard_map/ppermute | solution.py:493
  84.3 9.1 %collective-permute-start.27 = (f32[264,128]{1,0:T(8,128)S(1)}, f32[264,128]{1,0:T(8,128)S(1)}, u32[]{:S(2)}, u32[]{:S(2)}) collective-permute-start(f32[264,128]{1,0:T(8,128)S(1)} %fusion.3), channel_id=1, source_target_pairs={{0,8},{1,9},{2,10},{3,11},{4,12},{5,13},{6,14},{7,15},{8,0},{9,1},... | collective-permute-start | bytes 405512 | tf_op jit(solution)/shard_map/ppermute | solution.py:493
  86.3 7.7 %collective-permute-start.30 = (f32[264,128]{1,0:T(8,128)S(1)}, f32[264,128]{1,0:T(8,128)S(1)}, u32[]{:S(2)}, u32[]{:S(2)}) collective-permute-start(f32[264,128]{1,0:T(8,128)S(1)} %add.93), channel_id=1, source_target_pairs={{0,2},{1,3},{2,0},{3,1},{4,6},{5,7},{6,4},{7,5},{8,10},{9,11},{10,... | collective-permute-start | bytes 405512 | tf_op jit(solution)/shard_map/ppermute | solution.py:493
  87.8 9.2 %collective-permute-start.29 = (f32[264,128]{1,0:T(8,128)S(1)}, f32[264,128]{1,0:T(8,128)S(1)}, u32[]{:S(2)}, u32[]{:S(2)}) collective-permute-start(f32[264,128]{1,0:T(8,128)S(1)} %add.93), channel_id=1, source_target_pairs={{0,4},{1,5},{2,6},{3,7},{4,0},{5,1},{6,2},{7,3},{8,12},{9,13},{10,... | collective-permute-start | bytes 405512 | tf_op jit(solution)/shard_map/ppermute | solution.py:493
  90.1 9.1 %collective-permute-start.28 = (f32[264,128]{1,0:T(8,128)S(1)}, f32[264,128]{1,0:T(8,128)S(1)}, u32[]{:S(2)}, u32[]{:S(2)}) collective-permute-start(f32[264,128]{1,0:T(8,128)S(1)} %add.93), channel_id=1, source_target_pairs={{0,6},{1,7},{2,4},{3,5},{4,2},{5,3},{6,0},{7,1},{8,14},{9,15},{10,... | collective-permute-start | bytes 405512 | tf_op jit(solution)/shard_map/ppermute | solution.py:493
  93.4 10.0 %collective-permute-start.34 = (f32[264,128]{1,0:T(8,128)S(1)}, f32[264,128]{1,0:T(8,128)S(1)}, u32[]{:S(2)}, u32[]{:S(2)}) collective-permute-start(f32[264,128]{1,0:T(8,128)S(1)} %add.92), channel_id=1, source_target_pairs={{0,2},{1,3},{2,0},{3,1},{4,6},{5,7},{6,4},{7,5},{8,10},{9,11},{10,... | collective-permute-start | bytes 405512 | tf_op jit(solution)/shard_map/ppermute | solution.py:493
  94.0 9.4 %collective-permute-start.33 = (f32[264,128]{1,0:T(8,128)S(1)}, f32[264,128]{1,0:T(8,128)S(1)}, u32[]{:S(2)}, u32[]{:S(2)}) collective-permute-start(f32[264,128]{1,0:T(8,128)S(1)} %add.92), channel_id=1, source_target_pairs={{0,4},{1,5},{2,6},{3,7},{4,0},{5,1},{6,2},{7,3},{8,12},{9,13},{10,... | collective-permute-start | bytes 405512 | tf_op jit(solution)/shard_map/ppermute | solution.py:493
  94.0 10.5 %collective-permute-start.32 = (f32[264,128]{1,0:T(8,128)S(1)}, f32[264,128]{1,0:T(8,128)S(1)}, u32[]{:S(2)}, u32[]{:S(2)}) collective-permute-start(f32[264,128]{1,0:T(8,128)S(1)} %add.92), channel_id=1, source_target_pairs={{0,6},{1,7},{2,4},{3,5},{4,2},{5,3},{6,0},{7,1},{8,14},{9,15},{10,... | collective-permute-start | bytes 405512 | tf_op jit(solution)/shard_map/ppermute | solution.py:493
  (10 other events, 70.0 us)

commit v12 on v10

--- a/solution.py
+++ b/solution.py
@@ -549,7 +549,7 @@
     work()
     (got_b,) = close(env, got_b)
 
-    got_b = b.plane(got_b)
+    got_b = b.plane(got_b)[::-1]
     work()
     a.own(close(env, *got_a))
 
@@ -563,12 +563,12 @@
     got_a = a.gather_plane()
     b.own(close(env, *got_b))
 
-    got_b = b.gather_plane()
+    got_b = b.gather_plane()[::-1]
     got_a = a.gather_core(close(env, *got_a))
     work()
     (got_a,) = close(env, got_a)
     late[0](env, [a.mine, got_a])
-    got_b = b.gather_core(close(env, *got_b))
+    got_b = b.gather_core(close(env, *got_b)[::-1])
     late[1](env)
     (got_b,) = close(env, got_b)
     return [b.mine, got_b]

time: 111 us -> 112 us (level)
  waiting for transfers between devices: 14 us -> 15.3 us
    ppermute x36, waiting for transfers between devices: 14 us -> 15.3 us  [swap(): return lax.ppermute(x, 'row', [(i, i ^ offset) for i in range(self.count)])]
  transfers between devices with their start and end apart: 36 -> 36, of which waited for: 9 -> 10; matrix products, arithmetic and copies ran while one was open for 0% -> 0% of each run, Pallas kernels for 34% -> 34%
where the time goes in v12:
time: 112 us
  Pallas kernels  55.7 us (50%)
  starting transfers between devices  39.7 us (35%)
  waiting for transfers between devices  15.3 us (14%)
    ppermute x36, starting transfers between devices, swap(): return lax.ppermute(x, 'row', [(i, i ^ offset) for i in range(self.count)])  39.7 us
    ppermute x36, waiting for transfers between devices, swap(): return lax.ppermute(x, 'row', [(i, i ^ offset) for i in range(self.count)])  15.3 us
    pallas_call x3, Pallas kernels, affine(): call(affine_kernel, 'affine', struct(height, size), 18, height / rows, 2,...  8.99 us
    pallas_call x3, Pallas kernels, affine_parts(): call(affine_parts_kernel, 'affine_parts', struct(height, size), 18, heigh...  8.54 us
    pallas_call x1, Pallas kernels, first_gram(): call(functools.partial(first_gram_kernel, shards), 'first_gram', halves(s...  6.9 us
    pallas_call x1, Pallas kernels, second_gram(): call(functools.partial(second_gram_kernel, shards, len(pieces)), 'second_...  6.04 us
    pallas_call x2, Pallas kernels, first_part(): call(functools.partial(first_part_kernel, shards, len(pieces), columns),...  5.99 us
    pallas_call x1, Pallas kernels, last_step(): call(functools.partial(last_kernel, shards, len(pieces)), 'last', struct(...  4.94 us
  transfers between devices with their start and end apart: 36, of which 10 were waited for; matrix products, arithmetic and copies ran while one was open for 0% of the time, Pallas kernels for 34%

profile of v12, /device:TPU:0, one launch (start us, length us, event | category | flops | bytes accessed | tf_op | source)
XLA Modules:
  0.0 112.1 jit_solution(10075548119779368434)
XLA Ops:
  0.0 6.9 %first_gram.1 = (f32[1056,128]{1,0:T(8,128)S(1)}, f32[1056,128]{1,0:T(8,128)S(1)}, bf16[1024,1024]{1,0:T(8,128)(2,1)S(1)}, bf16[1024,1024]{1,0:T(8,128)(2,1)S(1)...) custom-call(s32[1]{0:T(128)} %bitcast.me_ref, f32[1024,1024]{1,0:T(8,128)} %x_ref.1, f32[1024,1024]{1,0:T(8,128)} %a_ref.2), custom_call_target="tpu_custom_call" | custom-call | flops 32212254720 | bytes 167772160 | tf_op jit(solution)/shard_map/first_gram/pallas_call | solution.py:198
  7.4 3.6 %other_gram.1 = (f32[1056,128]{1,0:T(8,128)S(1)}, f32[1056,128]{1,0:T(8,128)S(1)}) custom-call(s32[1]{0:T(128)} %bitcast.me_ref, bf16[1024,1024]{1,0:T(8,128)(2,1)S(1)} %get-tuple-element.194.ah, bf16[1024,1024]{1,0:T(8,128)(2,1)S(1)} %get-tuple-element.195.al, bf16[1024,1024]{1,0:T(8,128)(2,1)S(1)} %get-tuple-element.196.bh, ...), custom_call_target="tpu_custom_call" | custom-call | flops 32212254720 | bytes 83886080 | tf_op jit(solution)/shard_map/other_gram/pallas_call | solution.py:228
  11.2 2.6 %collective-permute-start.4 = (f32[264,128]{1,0:T(8,128)S(1)}, f32[264,128]{1,0:T(8,128)S(1)}, u32[]{:S(2)}, u32[]{:S(2)}) collective-permute-start(f32[264,128]{1,0:T(8,128)S(1)} %get-tuple-element.392), channel_id=1, source_target_pairs={{0,2},{1,3},{2,0},{3,1},{4,6},{5,7},{6,4},{7,5},{8,10},{9,11},{10,... | collective-permute-start | bytes 405512 | tf_op jit(solution)/shard_map/ppermute | solution.py:499
  13.8 1.6 %collective-permute-start.3 = (f32[264,128]{1,0:T(8,128)S(1)}, f32[264,128]{1,0:T(8,128)S(1)}, u32[]{:S(2)}, u32[]{:S(2)}) collective-permute-start(f32[264,128]{1,0:T(8,128)S(1)} %get-tuple-element.393), channel_id=1, source_target_pairs={{0,4},{1,5},{2,6},{3,7},{4,0},{5,1},{6,2},{7,3},{8,12},{9,13},{10,... | collective-permute-start | bytes 405512 | tf_op jit(solution)/shard_map/ppermute | solution.py:499
  15.4 2.6 %affine.3.refs_4_ = f32[256,1024]{1,0:T(8,128)S(1)} custom-call(f32[1024,1024]{1,0:T(8,128)S(1)} %copy-done, f32[1024,1024]{1,0:T(8,128)S(1)} %copy-done.1), custom_call_target="tpu_custom_call" | custom-call | flops 16106127360 | bytes 83886080 | tf_op jit(solution)/shard_map/affine/pallas_call | solution.py:264
  18.1 3.0 %collective-permute-start.7 = (f32[264,128]{1,0:T(8,128)S(1)}, f32[264,128]{1,0:T(8,128)S(1)}, u32[]{:S(2)}, u32[]{:S(2)}) collective-permute-start(f32[264,128]{1,0:T(8,128)S(1)} %get-tuple-element.389), channel_id=1, source_target_pairs={{0,6},{1,7},{2,4},{3,5},{4,2},{5,3},{6,0},{7,1},{8,14},{9,15},{10,... | collective-permute-start | bytes 405512 | tf_op jit(solution)/shard_map/ppermute | solution.py:499
  21.5 2.5 %affine.4.refs_5_ = f32[256,1024]{1,0:T(8,128)S(1)} custom-call(f32[1024,1024]{1,0:T(8,128)S(1)} %copy-done, f32[1024,1024]{1,0:T(8,128)S(1)} %copy-done.1), custom_call_target="tpu_custom_call" | custom-call | flops 16106127360 | bytes 83886080 | tf_op jit(solution)/shard_map/affine/pallas_call | solution.py:264
  24.4 3.0 %collective-permute-start.8 = (f32[264,128]{1,0:T(8,128)S(1)}, f32[264,128]{1,0:T(8,128)S(1)}, u32[]{:S(2)}, u32[]{:S(2)}) collective-permute-start(f32[264,128]{1,0:T(8,128)S(1)} %fusion.7), channel_id=1, source_target_pairs={{0,8},{1,9},{2,10},{3,11},{4,12},{5,13},{6,14},{7,15},{8,0},{9,1},... | collective-permute-start | bytes 405512 | tf_op jit(solution)/shard_map/ppermute | solution.py:499
  27.4 3.9 %affine.5.refs_6_ = f32[512,1024]{1,0:T(8,128)S(1)} custom-call(f32[1024,1024]{1,0:T(8,128)S(1)} %copy-done, f32[1024,1024]{1,0:T(8,128)S(1)} %copy-done.1), custom_call_target="tpu_custom_call" | custom-call | flops 32212254720 | bytes 83886080 | tf_op jit(solution)/shard_map/affine/pallas_call | solution.py:264
  31.3 1.5 %turn.1 = (bf16[1024,1024]{1,0:T(8,128)(2,1)S(1)}, bf16[1024,1024]{1,0:T(8,128)(2,1)S(1)}) custom-call(f32[1024,1024]{1,0:T(8,128)S(1)} %copy-done.4), custom_call_target="tpu_custom_call" | custom-call | flops 6442450944 | bytes 83886080 | tf_op jit(solution)/shard_map/turn/pallas_call | solution.py:384
  33.8 1.6 %collective-permute-start.12 = (f32[264,128]{1,0:T(8,128)S(1)}, f32[264,128]{1,0:T(8,128)S(1)}, u32[]{:S(2)}, u32[]{:S(2)}) collective-permute-start(f32[264,128]{1,0:T(8,128)S(1)} %add.82), channel_id=1, source_target_pairs={{0,2},{1,3},{2,0},{3,1},{4,6},{5,7},{6,4},{7,5},{8,10},{9,11},{10,... | collective-permute-start | bytes 405512 | tf_op jit(solution)/shard_map/ppermute | solution.py:499
  37.3 4.3 %collective-permute-done.9 = f32[264,128]{1,0:T(8,128)S(1)} collective-permute-done((f32[264,128]{1,0:T(8,128)S(1)}, f32[264,128]{1,0:T(8,128)S(1)}, u32[]{:S(2)}, u32[]{:S(2)}) %collective-permute-start.9) | collective-permute-done | bytes 135200 | tf_op jit(solution)/shard_map/ppermute | solution.py:499
  41.6 1.4 %collective-permute-start.16 = (f32[264,128]{1,0:T(8,128)S(1)}, f32[264,128]{1,0:T(8,128)S(1)}, u32[]{:S(2)}, u32[]{:S(2)}) collective-permute-start(f32[264,128]{1,0:T(8,128)S(1)} %add.83), channel_id=1, source_target_pairs={{0,6},{1,7},{2,4},{3,5},{4,2},{5,3},{6,0},{7,1},{8,14},{9,15},{10,... | collective-permute-start | bytes 405512 | tf_op jit(solution)/shard_map/ppermute | solution.py:499
  43.0 1.7 %collective-permute-start.15 = (f32[264,128]{1,0:T(8,128)S(1)}, f32[264,128]{1,0:T(8,128)S(1)}, u32[]{:S(2)}, u32[]{:S(2)}) collective-permute-start(f32[264,128]{1,0:T(8,128)S(1)} %add.83), channel_id=1, source_target_pairs={{0,4},{1,5},{2,6},{3,7},{4,0},{5,1},{6,2},{7,3},{8,12},{9,13},{10,... | collective-permute-start | bytes 405512 | tf_op jit(solution)/shard_map/ppermute | solution.py:499
  48.2 3.8 %first_part.2.mid_ref.refs_4_ = f32[1024,1024]{1,0:T(8,128)S(1)} custom-call(s32[1]{0:T(128)} %bitcast.me_ref, f32[1056,128]{1,0:T(8,128)S(1)} %pad_maximum_fusion.refs_0_, f32[1056,128]{1,0:T(8,128)S(1)} %collective-permute-done.13.refs_1_, bf16[1024,1024]{1,0:T(8,128)(2,1)S(1)} %get-tuple-element.299.refs_2_, ...), custom_call_target="tpu_custom_call" | custom-call | flops 32212254720 | bytes 125829120 | tf_op jit(solution)/shard_map/first_part/pallas_call | solution.py:338
  52.2 1.8 %column_product.1.refs_7_ = f32[1024,256]{1,0:T(8,128)S(1)} custom-call(bf16[1024,1024]{1,0:T(8,128)(2,1)S(1)} %get-tuple-element.297.xh.refs_5_, bf16[1024,1024]{1,0:T(8,128)(2,1)S(1)} %get-tuple-element.298.xl.refs_6_, f32[1024,1024]{1,0:T(8,128)S(1)} %first_part.2.mid_ref.refs_4_), custom_call_target="tpu_custom_call" | custom-call | flops 16106127360 | bytes 83886080 | tf_op jit(solution)/shard_map/column_product/pallas_call | solution.py:369
  54.0 6.0 %second_gram.1 = (f32[1056,128]{1,0:T(8,128)S(1)}, f32[1056,128]{1,0:T(8,128)S(1)}, bf16[1024,1024]{1,0:T(8,128)(2,1)S(1)}, bf16[1024,1024]{1,0:T(8,128)(2,1)S(1)}) custom-call(s32[1]{0:T(128)} %bitcast.me_ref, f32[1056,128]{1,0:T(8,128)S(1)} %pad_maximum_fusion.1.refs_0_, f32[1056,128]{1,0:T(8,128)S(1)} %collective-permute-done.17.refs_1_, ...), custom_call_target="tpu_custom_call" | custom-call | flops 51539607552 | bytes 209715200 | tf_op jit(solution)/shard_map/second_gram/pallas_call | solution.py:424
  60.5 3.8 %fourth_gram.1 = (f32[1056,128]{1,0:T(8,128)S(1)}, f32[1056,128]{1,0:T(8,128)S(1)}) custom-call(s32[1]{0:T(128)} %bitcast.me_ref, bf16[1024,1024]{1,0:T(8,128)(2,1)S(1)} %get-tuple-element.297.xh.refs_5_, bf16[1024,1024]{1,0:T(8,128)(2,1)S(1)} %get-tuple-element.298.xl.refs_6_, bf16[1024,1024]{1,0:T(8,128)(2,1)S(1)} %get-tuple-element.325.mh.ah, ...), custom_call_target="tpu_custom_call" | custom-call | flops 32212254720 | bytes 83886080 | tf_op jit(solution)/shard_map/fourth_gram/pallas_call | solution.py:441
  65.6 2.4 %collective-permute-start.20 = (f32[264,128]{1,0:T(8,128)S(1)}, f32[264,128]{1,0:T(8,128)S(1)}, u32[]{:S(2)}, u32[]{:S(2)}) collective-permute-start(f32[264,128]{1,0:T(8,128)S(1)} %get-tuple-element.388), channel_id=1, source_target_pairs={{0,6},{1,7},{2,4},{3,5},{4,2},{5,3},{6,0},{7,1},{8,14},{9,15},{10,... | collective-permute-start | bytes 405512 | tf_op jit(solution)/shard_map/ppermute | solution.py:499
  68.0 2.4 %affine_parts.3.refs_4_.refs_0_ = f32[256,1024]{1,0:T(8,128)S(1)} custom-call(bf16[1024,1024]{1,0:T(8,128)(2,1)S(1)} %get-tuple-element.325.mh.ah, bf16[1024,1024]{1,0:T(8,128)(2,1)S(1)} %get-tuple-element.326.ml.al, f32[1024,1024]{1,0:T(8,128)S(1)} %copy-done.3), custom_call_target="tpu_custom_call" | custom-call | flops 16106127360 | bytes 83886080 | tf_op jit(solution)/shard_map/affine_parts/pallas_call | solution.py:284
  71.1 2.0 %collective-permute-start.24 = (f32[264,128]{1,0:T(8,128)S(1)}, f32[264,128]{1,0:T(8,128)S(1)}, u32[]{:S(2)}, u32[]{:S(2)}) collective-permute-start(f32[264,128]{1,0:T(8,128)S(1)} %get-tuple-element.384), channel_id=1, source_target_pairs={{0,4},{1,5},{2,6},{3,7},{4,0},{5,1},{6,2},{7,3},{8,12},{9,13},{10,... | collective-permute-start | bytes 405512 | tf_op jit(solution)/shard_map/ppermute | solution.py:499
  73.2 2.4 %affine_parts.4.refs_5_.refs_1_ = f32[256,1024]{1,0:T(8,128)S(1)} custom-call(bf16[1024,1024]{1,0:T(8,128)(2,1)S(1)} %get-tuple-element.325.mh.ah, bf16[1024,1024]{1,0:T(8,128)(2,1)S(1)} %get-tuple-element.326.ml.al, f32[1024,1024]{1,0:T(8,128)S(1)} %copy-done.3), custom_call_target="tpu_custom_call" | custom-call | flops 16106127360 | bytes 83886080 | tf_op jit(solution)/shard_map/affine_parts/pallas_call | solution.py:284
  76.7 3.8 %collective-permute-start.26 = (f32[264,128]{1,0:T(8,128)S(1)}, f32[264,128]{1,0:T(8,128)S(1)}, u32[]{:S(2)}, u32[]{:S(2)}) collective-permute-start(f32[264,128]{1,0:T(8,128)S(1)} %fusion.1), channel_id=1, source_target_pairs={{0,8},{1,9},{2,10},{3,11},{4,12},{5,13},{6,14},{7,15},{8,0},{9,1},... | collective-permute-start | bytes 405512 | tf_op jit(solution)/shard_map/ppermute | solution.py:499
  80.5 3.7 %affine_parts.5.refs_6_.refs_2_ = f32[512,1024]{1,0:T(8,128)S(1)} custom-call(bf16[1024,1024]{1,0:T(8,128)(2,1)S(1)} %get-tuple-element.325.mh.ah, bf16[1024,1024]{1,0:T(8,128)(2,1)S(1)} %get-tuple-element.326.ml.al, f32[1024,1024]{1,0:T(8,128)S(1)} %copy-done.3), custom_call_target="tpu_custom_call" | custom-call | flops 32212254720 | bytes 83886080 | tf_op jit(solution)/shard_map/affine_parts/pallas_call | solution.py:284
  84.8 2.3 %collective-permute-done.26 = f32[264,128]{1,0:T(8,128)S(1)} collective-permute-done((f32[264,128]{1,0:T(8,128)S(1)}, f32[264,128]{1,0:T(8,128)S(1)}, u32[]{:S(2)}, u32[]{:S(2)}) %collective-permute-start.26) | collective-permute-done | bytes 135200 | tf_op jit(solution)/shard_map/ppermute | solution.py:499
  87.8 3.7 %collective-permute-start.29 = (f32[264,128]{1,0:T(8,128)S(1)}, f32[264,128]{1,0:T(8,128)S(1)}, u32[]{:S(2)}, u32[]{:S(2)}) collective-permute-start(f32[264,128]{1,0:T(8,128)S(1)} %add.93), channel_id=1, source_target_pairs={{0,4},{1,5},{2,6},{3,7},{4,0},{5,1},{6,2},{7,3},{8,12},{9,13},{10,... | collective-permute-start | bytes 405512 | tf_op jit(solution)/shard_map/ppermute | solution.py:499
  95.5 1.5 %collective-permute-start.32 = (f32[264,128]{1,0:T(8,128)S(1)}, f32[264,128]{1,0:T(8,128)S(1)}, u32[]{:S(2)}, u32[]{:S(2)}) collective-permute-start(f32[264,128]{1,0:T(8,128)S(1)} %add.92), channel_id=1, source_target_pairs={{0,2},{1,3},{2,0},{3,1},{4,6},{5,7},{6,4},{7,5},{8,10},{9,11},{10,... | collective-permute-start | bytes 405512 | tf_op jit(solution)/shard_map/ppermute | solution.py:499
  97.0 2.8 %collective-permute-done.28 = f32[264,128]{1,0:T(8,128)S(1)} collective-permute-done((f32[264,128]{1,0:T(8,128)S(1)}, f32[264,128]{1,0:T(8,128)S(1)}, u32[]{:S(2)}, u32[]{:S(2)}) %collective-permute-start.28) | collective-permute-done | bytes 135200 | tf_op jit(solution)/shard_map/ppermute | solution.py:499
  100.7 1.2 %collective-permute-done.31.refs_1_ = f32[1056,128]{1,0:T(8,128)S(1)} collective-permute-done((f32[1056,128]{1,0:T(8,128)S(1)}, f32[1056,128]{1,0:T(8,128)S(1)}, u32[]{:S(2)}, u32[]{:S(2)}) %collective-permute-start.31) | collective-permute-done | bytes 540704 | tf_op jit(solution)/shard_map/ppermute | solution.py:499
  101.8 2.2 %first_part.3 = (f32[1024,256]{1,0:T(8,128)S(1)}, bf16[1024,1024]{1,0:T(8,128)(2,1)S(1)}, bf16[1024,1024]{1,0:T(8,128)(2,1)S(1)}) custom-call(s32[1]{0:T(128)} %bitcast.me_ref, f32[1056,128]{1,0:T(8,128)S(1)} %pad_maximum_fusion.2.refs_0_, f32[1056,128]{1,0:T(8,128)S(1)} %collective-permute-done.31.refs_1_, ...), custom_call_target="tpu_custom_call" | custom-call | flops 32212254720 | bytes 125829120 | tf_op jit(solution)/shard_map/first_part/pallas_call | solution.py:338
  105.0 1.8 %other_part.1.refs_5_ = f32[1024,768]{1,0:T(8,128)S(1)} custom-call(bf16[1024,1024]{1,0:T(8,128)(2,1)S(1)} %get-tuple-element.379.refs_2_.ah, bf16[1024,1024]{1,0:T(8,128)(2,1)S(1)} %get-tuple-element.380.refs_3_.al, bf16[1024,1024]{1,0:T(8,128)(2,1)S(1)} %get-tuple-element.376.hi, bf16[1024,1024]{1,0:T(8,128)(2,1)S(1)} %get-tuple-element.377.lo, ...), custom_call_target="tpu_custom_call" | custom-call | flops 16106127360 | bytes 125829120 | tf_op jit(solution)/shard_map/other_part/pallas_call | solution.py:353
  107.0 4.9 %last.1 = f32[1024,1024]{1,0:T(8,128)} custom-call(s32[1]{0:T(128)} %bitcast.me_ref, f32[1056,128]{1,0:T(8,128)S(1)} %pad_maximum_fusion.3.refs_0_, f32[1056,128]{1,0:T(8,128)S(1)} %collective-permute-done.35.refs_1_, bf16[1024,1024]{1,0:T(8,128)(2,1)S(1)} %get-tuple-element.379.refs_2_.ah, bf16[1024,1024]{1,0:T(8,128)(2,1)S(1)} %get-tuple-element.380.refs_3_.al, ...), custom_call_target="tpu_custom_call" | custom-call | flops 32212254720 | bytes 125829120 | tf_op jit(solution)/shard_map/last/pallas_call | solution.py:476
  (90 shorter events, 18.7 us)
Async XLA Ops:
  6.9 4.2 %collective-permute-start = (f32[1056,128]{1,0:T(8,128)S(1)}, f32[1056,128]{1,0:T(8,128)S(1)}, u32[]{:S(2)}, u32[]{:S(2)}) collective-permute-start(f32[1056,128]{1,0:T(8,128)S(1)} %get-tuple-element.200), channel_id=1, source_target_pairs={{0,1},{1,0},{2,3},{3,2},{4,5},{5,4},{6,7},{7,6},{8,9},{9,8},{10,11... | collective-permute-start | bytes 1622024 | tf_op jit(solution)/shard_map/ppermute | solution.py:499
  11.2 12.9 %collective-permute-start.4 = (f32[264,128]{1,0:T(8,128)S(1)}, f32[264,128]{1,0:T(8,128)S(1)}, u32[]{:S(2)}, u32[]{:S(2)}) collective-permute-start(f32[264,128]{1,0:T(8,128)S(1)} %get-tuple-element.392), channel_id=1, source_target_pairs={{0,2},{1,3},{2,0},{3,1},{4,6},{5,7},{6,4},{7,5},{8,10},{9,11},{10,... | collective-permute-start | bytes 405512 | tf_op jit(solution)/shard_map/ppermute | solution.py:499
  13.8 10.5 %collective-permute-start.3 = (f32[264,128]{1,0:T(8,128)S(1)}, f32[264,128]{1,0:T(8,128)S(1)}, u32[]{:S(2)}, u32[]{:S(2)}) collective-permute-start(f32[264,128]{1,0:T(8,128)S(1)} %get-tuple-element.393), channel_id=1, source_target_pairs={{0,4},{1,5},{2,6},{3,7},{4,0},{5,1},{6,2},{7,3},{8,12},{9,13},{10,... | collective-permute-start | bytes 405512 | tf_op jit(solution)/shard_map/ppermute | solution.py:499
  15.4 9.0 %collective-permute-start.2 = (f32[264,128]{1,0:T(8,128)S(1)}, f32[264,128]{1,0:T(8,128)S(1)}, u32[]{:S(2)}, u32[]{:S(2)}) collective-permute-start(f32[264,128]{1,0:T(8,128)S(1)} %get-tuple-element.394), channel_id=1, source_target_pairs={{0,6},{1,7},{2,4},{3,5},{4,2},{5,3},{6,0},{7,1},{8,14},{9,15},{10,... | collective-permute-start | bytes 405512 | tf_op jit(solution)/shard_map/ppermute | solution.py:499
  15.4 2.6 %collective-permute-start.1 = (f32[1056,128]{1,0:T(8,128)S(1)}, f32[1056,128]{1,0:T(8,128)S(1)}, u32[]{:S(2)}, u32[]{:S(2)}) collective-permute-start(f32[1056,128]{1,0:T(8,128)S(1)} %get-tuple-element.206), channel_id=1, source_target_pairs={{0,1},{1,0},{2,3},{3,2},{4,5},{5,4},{6,7},{7,6},{8,9},{9,8},{10,11... | collective-permute-start | bytes 1622024 | tf_op jit(solution)/shard_map/ppermute | solution.py:499
  18.1 14.7 %collective-permute-start.7 = (f32[264,128]{1,0:T(8,128)S(1)}, f32[264,128]{1,0:T(8,128)S(1)}, u32[]{:S(2)}, u32[]{:S(2)}) collective-permute-start(f32[264,128]{1,0:T(8,128)S(1)} %get-tuple-element.389), channel_id=1, source_target_pairs={{0,6},{1,7},{2,4},{3,5},{4,2},{5,3},{6,0},{7,1},{8,14},{9,15},{10,... | collective-permute-start | bytes 405512 | tf_op jit(solution)/shard_map/ppermute | solution.py:499
  21.1 11.7 %collective-permute-start.6 = (f32[264,128]{1,0:T(8,128)S(1)}, f32[264,128]{1,0:T(8,128)S(1)}, u32[]{:S(2)}, u32[]{:S(2)}) collective-permute-start(f32[264,128]{1,0:T(8,128)S(1)} %get-tuple-element.390), channel_id=1, source_target_pairs={{0,4},{1,5},{2,6},{3,7},{4,0},{5,1},{6,2},{7,3},{8,12},{9,13},{10,... | collective-permute-start | bytes 405512 | tf_op jit(solution)/shard_map/ppermute | solution.py:499
  24.1 8.8 %collective-permute-start.5 = (f32[264,128]{1,0:T(8,128)S(1)}, f32[264,128]{1,0:T(8,128)S(1)}, u32[]{:S(2)}, u32[]{:S(2)}) collective-permute-start(f32[264,128]{1,0:T(8,128)S(1)} %get-tuple-element.391), channel_id=1, source_target_pairs={{0,2},{1,3},{2,0},{3,1},{4,6},{5,7},{6,4},{7,5},{8,10},{9,11},{10,... | collective-permute-start | bytes 405512 | tf_op jit(solution)/shard_map/ppermute | solution.py:499
  24.4 9.4 %collective-permute-start.8 = (f32[264,128]{1,0:T(8,128)S(1)}, f32[264,128]{1,0:T(8,128)S(1)}, u32[]{:S(2)}, u32[]{:S(2)}) collective-permute-start(f32[264,128]{1,0:T(8,128)S(1)} %fusion.7), channel_id=1, source_target_pairs={{0,8},{1,9},{2,10},{3,11},{4,12},{5,13},{6,14},{7,15},{8,0},{9,1},... | collective-permute-start | bytes 405512 | tf_op jit(solution)/shard_map/ppermute | solution.py:499
  32.9 8.7 %collective-permute-start.9 = (f32[264,128]{1,0:T(8,128)S(1)}, f32[264,128]{1,0:T(8,128)S(1)}, u32[]{:S(2)}, u32[]{:S(2)}) collective-permute-start(f32[264,128]{1,0:T(8,128)S(1)} %fusion.5), channel_id=1, source_target_pairs={{0,8},{1,9},{2,10},{3,11},{4,12},{5,13},{6,14},{7,15},{8,0},{9,1},... | collective-permute-start | bytes 405512 | tf_op jit(solution)/shard_map/ppermute | solution.py:499
  33.8 11.0 %collective-permute-start.12 = (f32[264,128]{1,0:T(8,128)S(1)}, f32[264,128]{1,0:T(8,128)S(1)}, u32[]{:S(2)}, u32[]{:S(2)}) collective-permute-start(f32[264,128]{1,0:T(8,128)S(1)} %add.82), channel_id=1, source_target_pairs={{0,2},{1,3},{2,0},{3,1},{4,6},{5,7},{6,4},{7,5},{8,10},{9,11},{10,... | collective-permute-start | bytes 405512 | tf_op jit(solution)/shard_map/ppermute | solution.py:499
  35.3 9.9 %collective-permute-start.11 = (f32[264,128]{1,0:T(8,128)S(1)}, f32[264,128]{1,0:T(8,128)S(1)}, u32[]{:S(2)}, u32[]{:S(2)}) collective-permute-start(f32[264,128]{1,0:T(8,128)S(1)} %add.82), channel_id=1, source_target_pairs={{0,4},{1,5},{2,6},{3,7},{4,0},{5,1},{6,2},{7,3},{8,12},{9,13},{10,... | collective-permute-start | bytes 405512 | tf_op jit(solution)/shard_map/ppermute | solution.py:499
  36.5 9.6 %collective-permute-start.10 = (f32[264,128]{1,0:T(8,128)S(1)}, f32[264,128]{1,0:T(8,128)S(1)}, u32[]{:S(2)}, u32[]{:S(2)}) collective-permute-start(f32[264,128]{1,0:T(8,128)S(1)} %add.82), channel_id=1, source_target_pairs={{0,6},{1,7},{2,4},{3,5},{4,2},{5,3},{6,0},{7,1},{8,14},{9,15},{10,... | collective-permute-start | bytes 405512 | tf_op jit(solution)/shard_map/ppermute | solution.py:499
  41.6 10.3 %collective-permute-start.16 = (f32[264,128]{1,0:T(8,128)S(1)}, f32[264,128]{1,0:T(8,128)S(1)}, u32[]{:S(2)}, u32[]{:S(2)}) collective-permute-start(f32[264,128]{1,0:T(8,128)S(1)} %add.83), channel_id=1, source_target_pairs={{0,6},{1,7},{2,4},{3,5},{4,2},{5,3},{6,0},{7,1},{8,14},{9,15},{10,... | collective-permute-start | bytes 405512 | tf_op jit(solution)/shard_map/ppermute | solution.py:499
  43.0 8.9 %collective-permute-start.15 = (f32[264,128]{1,0:T(8,128)S(1)}, f32[264,128]{1,0:T(8,128)S(1)}, u32[]{:S(2)}, u32[]{:S(2)}) collective-permute-start(f32[264,128]{1,0:T(8,128)S(1)} %add.83), channel_id=1, source_target_pairs={{0,4},{1,5},{2,6},{3,7},{4,0},{5,1},{6,2},{7,3},{8,12},{9,13},{10,... | collective-permute-start | bytes 405512 | tf_op jit(solution)/shard_map/ppermute | solution.py:499
  44.7 7.2 %collective-permute-start.14 = (f32[264,128]{1,0:T(8,128)S(1)}, f32[264,128]{1,0:T(8,128)S(1)}, u32[]{:S(2)}, u32[]{:S(2)}) collective-permute-start(f32[264,128]{1,0:T(8,128)S(1)} %add.83), channel_id=1, source_target_pairs={{0,2},{1,3},{2,0},{3,1},{4,6},{5,7},{6,4},{7,5},{8,10},{9,11},{10,... | collective-permute-start | bytes 405512 | tf_op jit(solution)/shard_map/ppermute | solution.py:499
  60.1 4.3 %collective-permute-start.18 = (f32[1056,128]{1,0:T(8,128)S(1)}, f32[1056,128]{1,0:T(8,128)S(1)}, u32[]{:S(2)}, u32[]{:S(2)}) collective-permute-start(f32[1056,128]{1,0:T(8,128)S(1)} %get-tuple-element.308), channel_id=1, source_target_pairs={{0,1},{1,0},{2,3},{3,2},{4,5},{5,4},{6,7},{7,6},{8,9},{9,8},{10,11... | collective-permute-start | bytes 1622024 | tf_op jit(solution)/shard_map/ppermute | solution.py:499
  64.5 11.1 %collective-permute-start.22 = (f32[264,128]{1,0:T(8,128)S(1)}, f32[264,128]{1,0:T(8,128)S(1)}, u32[]{:S(2)}, u32[]{:S(2)}) collective-permute-start(f32[264,128]{1,0:T(8,128)S(1)} %get-tuple-element.386), channel_id=1, source_target_pairs={{0,2},{1,3},{2,0},{3,1},{4,6},{5,7},{6,4},{7,5},{8,10},{9,11},{10,... | collective-permute-start | bytes 405512 | tf_op jit(solution)/shard_map/ppermute | solution.py:499
  65.6 11.1 %collective-permute-start.21 = (f32[264,128]{1,0:T(8,128)S(1)}, f32[264,128]{1,0:T(8,128)S(1)}, u32[]{:S(2)}, u32[]{:S(2)}) collective-permute-start(f32[264,128]{1,0:T(8,128)S(1)} %get-tuple-element.387), channel_id=1, source_target_pairs={{0,4},{1,5},{2,6},{3,7},{4,0},{5,1},{6,2},{7,3},{8,12},{9,13},{10,... | collective-permute-start | bytes 405512 | tf_op jit(solution)/shard_map/ppermute | solution.py:499
  65.6 11.1 %collective-permute-start.20 = (f32[264,128]{1,0:T(8,128)S(1)}, f32[264,128]{1,0:T(8,128)S(1)}, u32[]{:S(2)}, u32[]{:S(2)}) collective-permute-start(f32[264,128]{1,0:T(8,128)S(1)} %get-tuple-element.388), channel_id=1, source_target_pairs={{0,6},{1,7},{2,4},{3,5},{4,2},{5,3},{6,0},{7,1},{8,14},{9,15},{10,... | collective-permute-start | bytes 405512 | tf_op jit(solution)/shard_map/ppermute | solution.py:499
  68.0 2.5 %collective-permute-start.19 = (f32[1056,128]{1,0:T(8,128)S(1)}, f32[1056,128]{1,0:T(8,128)S(1)}, u32[]{:S(2)}, u32[]{:S(2)}) collective-permute-start(f32[1056,128]{1,0:T(8,128)S(1)} %get-tuple-element.314), channel_id=1, source_target_pairs={{0,1},{1,0},{2,3},{3,2},{4,5},{5,4},{6,7},{7,6},{8,9},{9,8},{10,11... | collective-permute-start | bytes 1622024 | tf_op jit(solution)/shard_map/ppermute | solution.py:499
  70.6 13.6 %collective-permute-start.25 = (f32[264,128]{1,0:T(8,128)S(1)}, f32[264,128]{1,0:T(8,128)S(1)}, u32[]{:S(2)}, u32[]{:S(2)}) collective-permute-start(f32[264,128]{1,0:T(8,128)S(1)} %get-tuple-element.383), channel_id=1, source_target_pairs={{0,6},{1,7},{2,4},{3,5},{4,2},{5,3},{6,0},{7,1},{8,14},{9,15},{10,... | collective-permute-start | bytes 405512 | tf_op jit(solution)/shard_map/ppermute | solution.py:499
  71.1 13.1 %collective-permute-start.24 = (f32[264,128]{1,0:T(8,128)S(1)}, f32[264,128]{1,0:T(8,128)S(1)}, u32[]{:S(2)}, u32[]{:S(2)}) collective-permute-start(f32[264,128]{1,0:T(8,128)S(1)} %get-tuple-element.384), channel_id=1, source_target_pairs={{0,4},{1,5},{2,6},{3,7},{4,0},{5,1},{6,2},{7,3},{8,12},{9,13},{10,... | collective-permute-start | bytes 405512 | tf_op jit(solution)/shard_map/ppermute | solution.py:499
  75.6 8.6 %collective-permute-start.23 = (f32[264,128]{1,0:T(8,128)S(1)}, f32[264,128]{1,0:T(8,128)S(1)}, u32[]{:S(2)}, u32[]{:S(2)}) collective-permute-start(f32[264,128]{1,0:T(8,128)S(1)} %get-tuple-element.385), channel_id=1, source_target_pairs={{0,2},{1,3},{2,0},{3,1},{4,6},{5,7},{6,4},{7,5},{8,10},{9,11},{10,... | collective-permute-start | bytes 405512 | tf_op jit(solution)/shard_map/ppermute | solution.py:499
  76.7 10.4 %collective-permute-start.26 = (f32[264,128]{1,0:T(8,128)S(1)}, f32[264,128]{1,0:T(8,128)S(1)}, u32[]{:S(2)}, u32[]{:S(2)}) collective-permute-start(f32[264,128]{1,0:T(8,128)S(1)} %fusion.1), channel_id=1, source_target_pairs={{0,8},{1,9},{2,10},{3,11},{4,12},{5,13},{6,14},{7,15},{8,0},{9,1},... | collective-permute-start | bytes 405512 | tf_op jit(solution)/shard_map/ppermute | solution.py:499
  84.3 9.1 %collective-permute-start.27 = (f32[264,128]{1,0:T(8,128)S(1)}, f32[264,128]{1,0:T(8,128)S(1)}, u32[]{:S(2)}, u32[]{:S(2)}) collective-permute-start(f32[264,128]{1,0:T(8,128)S(1)} %fusion.3), channel_id=1, source_target_pairs={{0,8},{1,9},{2,10},{3,11},{4,12},{5,13},{6,14},{7,15},{8,0},{9,1},... | collective-permute-start | bytes 405512 | tf_op jit(solution)/shard_map/ppermute | solution.py:499
  87.1 8.4 %collective-permute-start.30 = (f32[264,128]{1,0:T(8,128)S(1)}, f32[264,128]{1,0:T(8,128)S(1)}, u32[]{:S(2)}, u32[]{:S(2)}) collective-permute-start(f32[264,128]{1,0:T(8,128)S(1)} %add.93), channel_id=1, source_target_pairs={{0,2},{1,3},{2,0},{3,1},{4,6},{5,7},{6,4},{7,5},{8,10},{9,11},{10,... | collective-permute-start | bytes 405512 | tf_op jit(solution)/shard_map/ppermute | solution.py:499
  87.8 9.2 %collective-permute-start.29 = (f32[264,128]{1,0:T(8,128)S(1)}, f32[264,128]{1,0:T(8,128)S(1)}, u32[]{:S(2)}, u32[]{:S(2)}) collective-permute-start(f32[264,128]{1,0:T(8,128)S(1)} %add.93), channel_id=1, source_target_pairs={{0,4},{1,5},{2,6},{3,7},{4,0},{5,1},{6,2},{7,3},{8,12},{9,13},{10,... | collective-permute-start | bytes 405512 | tf_op jit(solution)/shard_map/ppermute | solution.py:499
  91.5 8.3 %collective-permute-start.28 = (f32[264,128]{1,0:T(8,128)S(1)}, f32[264,128]{1,0:T(8,128)S(1)}, u32[]{:S(2)}, u32[]{:S(2)}) collective-permute-start(f32[264,128]{1,0:T(8,128)S(1)} %add.93), channel_id=1, source_target_pairs={{0,6},{1,7},{2,4},{3,5},{4,2},{5,3},{6,0},{7,1},{8,14},{9,15},{10,... | collective-permute-start | bytes 405512 | tf_op jit(solution)/shard_map/ppermute | solution.py:499
  93.4 10.7 %collective-permute-start.34 = (f32[264,128]{1,0:T(8,128)S(1)}, f32[264,128]{1,0:T(8,128)S(1)}, u32[]{:S(2)}, u32[]{:S(2)}) collective-permute-start(f32[264,128]{1,0:T(8,128)S(1)} %add.92), channel_id=1, source_target_pairs={{0,6},{1,7},{2,4},{3,5},{4,2},{5,3},{6,0},{7,1},{8,14},{9,15},{10,... | collective-permute-start | bytes 405512 | tf_op jit(solution)/shard_map/ppermute | solution.py:499
  94.5 10.4 %collective-permute-start.33 = (f32[264,128]{1,0:T(8,128)S(1)}, f32[264,128]{1,0:T(8,128)S(1)}, u32[]{:S(2)}, u32[]{:S(2)}) collective-permute-start(f32[264,128]{1,0:T(8,128)S(1)} %add.92), channel_id=1, source_target_pairs={{0,4},{1,5},{2,6},{3,7},{4,0},{5,1},{6,2},{7,3},{8,12},{9,13},{10,... | collective-permute-start | bytes 405512 | tf_op jit(solution)/shard_map/ppermute | solution.py:499
  95.5 9.4 %collective-permute-start.32 = (f32[264,128]{1,0:T(8,128)S(1)}, f32[264,128]{1,0:T(8,128)S(1)}, u32[]{:S(2)}, u32[]{:S(2)}) collective-permute-start(f32[264,128]{1,0:T(8,128)S(1)} %add.92), channel_id=1, source_target_pairs={{0,2},{1,3},{2,0},{3,1},{4,6},{5,7},{6,4},{7,5},{8,10},{9,11},{10,... | collective-permute-start | bytes 405512 | tf_op jit(solution)/shard_map/ppermute | solution.py:499
  (10 other events, 72.7 us)

commit v13 on v10

--- a/solution.py
+++ b/solution.py
@@ -241,52 +241,50 @@
     lax.fori_loop(0, count // tile, body, 0)
 
 
-def affine_kernel(a_ref, b_ref, out_ref, hi, lo):
-    hi[...], lo[...] = split(a_ref[...])
+def row_part(part, rows):
+    return slice(0, rows // 4) if part == 0 else slice(rows // 4, rows)
+
+
+def affine_kernel(part, a_ref, b_ref, out_ref, hi, lo):
+    r = row_part(part, a_ref.shape[0])
+    hi[...], lo[...] = split(a_ref[r])
 
     def step(c):
-        out_ref[:, c] = 1.5 * a_ref[:, c] - 0.5 * mm((hi[...], lo[...]), split(b_ref[:, c]))
-
-    tiles(out_ref.shape[1], min(512, out_ref.shape[0]), step)
-
-
-THIRDS = ((0, 4), (1, 4), (1, 2))
-
-
-def row_part(part, rows, size):
-    at, parts = THIRDS[part]
-    return pl.BlockSpec((rows // parts, size), lambda r: (at, 0))
+        out_ref[:, c] = 1.5 * a_ref[r, c] - 0.5 * mm((hi[...], lo[...]), split(b_ref[:, c]))
+
+    tiles(out_ref.shape[1], 256, step)
 
 
 def affine(a, b, part):
     rows, size = a.shape
-    height = rows // THIRDS[part][1]
-    return call(
-        affine_kernel, "affine", struct(height, size), 18, height / rows, 2,
-        grid=(1,),
-        in_specs=[row_part(part, rows, size), pl.BlockSpec((size, size), lambda r: (0, 0))],
-        out_specs=pl.BlockSpec((height, size), lambda r: (0, 0)),
+    height = rows // 4 if part == 0 else 3 * rows // 4
+    return call(
+        functools.partial(affine_kernel, part), "affine", struct(height, size), 18,
+        height / rows, 2,
+        in_specs=[VMEM, VMEM],
+        out_specs=VMEM,
         scratch_shapes=[pltpu.VMEM((height, size), BF16)] * 2,
     )(a, b)
 
 
-def affine_parts_kernel(ah, al, b_ref, out_ref):
+def affine_parts_kernel(part, ah, al, b_ref, out_ref):
+    r = row_part(part, ah.shape[0])
+
     def step(c):
-        product = mm((ah[...], al[...]), split(b_ref[:, c]))
-        out_ref[:, c] = 1.5 * (ah[:, c].astype(F32) + al[:, c].astype(F32)) - 0.5 * product
-
-    tiles(out_ref.shape[1], min(512, out_ref.shape[0]), step)
+        product = mm((ah[r], al[r]), split(b_ref[:, c]))
+        out_ref[:, c] = 1.5 * (ah[r, c].astype(F32) + al[r, c].astype(F32)) - 0.5 * product
+
+    tiles(out_ref.shape[1], 256, step)
 
 
 def affine_parts(ah, al, b, part):
     rows, size = ah.shape
-    height = rows // THIRDS[part][1]
-    return call(
-        affine_parts_kernel, "affine_parts", struct(height, size), 18, height / rows, 2,
-        grid=(1,),
-        in_specs=[row_part(part, rows, size)] * 2
-        + [pl.BlockSpec((size, size), lambda r: (0, 0))],
-        out_specs=pl.BlockSpec((height, size), lambda r: (0, 0)),
+    height = rows // 4 if part == 0 else 3 * rows // 4
+    return call(
+        functools.partial(affine_parts_kernel, part), "affine_parts", struct(height, size), 18,
+        height / rows, 2,
+        in_specs=[VMEM] * 3,
+        out_specs=VMEM,
     )(ah, al, b)
 
 
@@ -386,17 +384,20 @@
     )(x)
 
 
-def cut_kernel(x_ref, hi, lo):
+def cut_kernel(which, x_ref, *out_refs):
     def step(r):
-        hi[r], lo[r] = split(x_ref[r])
+        parts = split(x_ref[r])
+        for out_ref, k in zip(out_refs, which):
+            out_ref[r] = parts[k]
 
     tiles(x_ref.shape[0], 128, step)
 
 
-def cut(x):
-    part = struct(*x.shape, dtype=BF16)
-    return call(
-        cut_kernel, "cut", [part, part], 16, 0.1, 2, in_specs=[VMEM], out_specs=[VMEM] * 2
+def cut(x, *which):
+    count = len(which)
+    return call(
+        functools.partial(cut_kernel, which), "cut", [struct(*x.shape, dtype=BF16)] * count,
+        16, 0.25, 2, in_specs=[VMEM], out_specs=[VMEM] * count,
     )(x)
 
 
@@ -585,16 +586,15 @@
             env[f"m{part}"] = affine(env["c"], env["s1"], part)
         return work
 
-    def direct_and_turn(env):
-        direct(2)(env)
+    def turned(env):
         env["xh"], env["xl"] = turn(env["x0"])
 
     def cut_one(env):
-        env["x1h"], env["x1l"] = cut(env["x1"])
+        env["x1h"], env["x1l"] = cut(env["x1"], 0, 1)
 
     def middle(env, pieces):
         (env["mid"],) = first_part(
-            me, SHARDS, pieces, env["x1h"], env["x1l"], [env["m0"], env["m1"], env["m2"]], (0, 1, 2, 3)
+            me, SHARDS, pieces, env["x1h"], env["x1l"], [env["m0"], env["m1"]], (0, 1, 2, 3)
         )
 
     def column(env):
@@ -603,7 +603,7 @@
     keep, send, *parts = first_gram(me, SHARDS, env["x1"], env["c"])
     one = sum_chunks(
         count, env, (keep, send), lambda env: other_gram(me, SHARDS, *parts),
-        [direct(0), direct(1), direct_and_turn, cut_one], [middle, column],
+        [direct(0), cut_one, direct(1), turned], [middle, column],
     )
 
     keep, send, env["mh"], env["ml"] = second_gram(
@@ -615,26 +615,26 @@
             env[f"d{part}"] = affine_parts(env["mh"], env["ml"], env["s0"], part)
         return work
 
-    def cut_zero(env):
-        env["x0h"], env["x0l"] = cut(env["x0"])
-
-    def three(name):
-        return [env[f"{name}{part}"] for part in range(3)]
+    def high(env):
+        (env["x0h"],) = cut(env["x0"], 0)
+
+    def low(env):
+        (env["x0l"],) = cut(env["x0"], 1)
 
     def result(env, pieces):
         env["z"], env["symh"], env["syml"] = first_part(
-            me, SHARDS, pieces, env["x0h"], env["x0l"], three("d"), (0,)
+            me, SHARDS, pieces, env["x0h"], env["x0l"], [env["d0"], env["d1"]], (0,)
         )
 
     def rest(env):
         env["rest"] = other_part(
-            env["x0h"], env["x0l"], env["symh"], env["syml"], three("d"), (1, 2, 3)
+            env["x0h"], env["x0l"], env["symh"], env["syml"], [env["d0"], env["d1"]], (1, 2, 3)
         )
 
     two = sum_chunks(
         count, env, (keep, send),
         lambda env: fourth_gram(me, SHARDS, env["xh"], env["xl"], env["mh"], env["ml"]),
-        [last_direct(0), last_direct(1), last_direct(2), cut_zero], [result, rest],
+        [last_direct(0), high, last_direct(1), low], [result, rest],
     )
     return last_step(me, SHARDS, two, env["x0h"], env["x0l"], env["z"], env["rest"])
 

time: 111 us -> 109 us (0.982)
    pallas_call x8 -> x7, Pallas kernels: 19.2 us -> 18.4 us  [the longest x2 8.84 us: affine(): call(functools.partial(affine_kernel, part), 'affine', struct(height, siz...]
where the time goes in v13:
time: 109 us
  Pallas kernels  55.1 us (51%)
  starting transfers between devices  39 us (36%)
  waiting for transfers between devices  13.4 us (12%)
    ppermute x36, starting transfers between devices, swap(): return lax.ppermute(x, 'row', [(i, i ^ offset) for i in range(self.count)])  39 us
    ppermute x36, waiting for transfers between devices, swap(): return lax.ppermute(x, 'row', [(i, i ^ offset) for i in range(self.count)])  13.4 us
    pallas_call x2, Pallas kernels, affine(): call(functools.partial(affine_kernel, part), 'affine', struct(height, siz...  8.84 us
    pallas_call x2, Pallas kernels, affine_parts(): call(functools.partial(affine_parts_kernel, part), 'affine_parts', struct...  8.17 us
    pallas_call x1, Pallas kernels, first_gram(): call(functools.partial(first_gram_kernel, shards), 'first_gram', halves(s...  6.9 us
    pallas_call x1, Pallas kernels, second_gram(): call(functools.partial(second_gram_kernel, shards, len(pieces)), 'second_...  6.15 us
    pallas_call x2, Pallas kernels, first_part(): call(functools.partial(first_part_kernel, shards, len(pieces), columns),...  5.92 us
    pallas_call x1, Pallas kernels, last_step(): call(functools.partial(last_kernel, shards, len(pieces)), 'last', struct(...  4.89 us
  transfers between devices with their start and end apart: 36, of which 9 were waited for; matrix products, arithmetic and copies ran while one was open for 0% of the time, Pallas kernels for 34%

profile of v13, /device:TPU:0, one launch (start us, length us, event | category | flops | bytes accessed | tf_op | source)
XLA Modules:
  0.0 108.8 jit_solution(254078454855177117)
XLA Ops:
  0.0 6.9 %first_gram.1 = (f32[1056,128]{1,0:T(8,128)S(1)}, f32[1056,128]{1,0:T(8,128)S(1)}, bf16[1024,1024]{1,0:T(8,128)(2,1)S(1)}, bf16[1024,1024]{1,0:T(8,128)(2,1)S(1)...) custom-call(s32[1]{0:T(128)} %bitcast.me_ref, f32[1024,1024]{1,0:T(8,128)} %x_ref, f32[1024,1024]{1,0:T(8,128)} %a_ref.1), custom_call_target="tpu_custom_call" | custom-call | flops 32212254720 | bytes 167772160 | tf_op jit(solution)/shard_map/first_gram/pallas_call | solution.py:198
  7.4 3.6 %other_gram.1 = (f32[1056,128]{1,0:T(8,128)S(1)}, f32[1056,128]{1,0:T(8,128)S(1)}) custom-call(s32[1]{0:T(128)} %bitcast.me_ref, bf16[1024,1024]{1,0:T(8,128)(2,1)S(1)} %get-tuple-element.184.ah, bf16[1024,1024]{1,0:T(8,128)(2,1)S(1)} %get-tuple-element.185.al, bf16[1024,1024]{1,0:T(8,128)(2,1)S(1)} %get-tuple-element.186.bh, ...), custom_call_target="tpu_custom_call" | custom-call | flops 32212254720 | bytes 83886080 | tf_op jit(solution)/shard_map/other_gram/pallas_call | solution.py:228
  11.2 2.6 %collective-permute-start.4 = (f32[264,128]{1,0:T(8,128)S(1)}, f32[264,128]{1,0:T(8,128)S(1)}, u32[]{:S(2)}, u32[]{:S(2)}) collective-permute-start(f32[264,128]{1,0:T(8,128)S(1)} %get-tuple-element.372), channel_id=1, source_target_pairs={{0,2},{1,3},{2,0},{3,1},{4,6},{5,7},{6,4},{7,5},{8,10},{9,11},{10,... | collective-permute-start | bytes 405512 | tf_op jit(solution)/shard_map/ppermute | solution.py:500
  13.8 1.6 %collective-permute-start.3 = (f32[264,128]{1,0:T(8,128)S(1)}, f32[264,128]{1,0:T(8,128)S(1)}, u32[]{:S(2)}, u32[]{:S(2)}) collective-permute-start(f32[264,128]{1,0:T(8,128)S(1)} %get-tuple-element.373), channel_id=1, source_target_pairs={{0,4},{1,5},{2,6},{3,7},{4,0},{5,1},{6,2},{7,3},{8,12},{9,13},{10,... | collective-permute-start | bytes 405512 | tf_op jit(solution)/shard_map/ppermute | solution.py:500
  15.4 2.6 %affine.2.refs_4_ = f32[256,1024]{1,0:T(8,128)S(1)} custom-call(f32[1024,1024]{1,0:T(8,128)S(1)} %copy-done.1, f32[1024,1024]{1,0:T(8,128)S(1)} %copy-done.2), custom_call_target="tpu_custom_call" | custom-call | flops 16106127360 | bytes 83886080 | tf_op jit(solution)/shard_map/affine/pallas_call | solution.py:261
  18.1 2.0 %collective-permute-start.7 = (f32[264,128]{1,0:T(8,128)S(1)}, f32[264,128]{1,0:T(8,128)S(1)}, u32[]{:S(2)}, u32[]{:S(2)}) collective-permute-start(f32[264,128]{1,0:T(8,128)S(1)} %get-tuple-element.369), channel_id=1, source_target_pairs={{0,2},{1,3},{2,0},{3,1},{4,6},{5,7},{6,4},{7,5},{8,10},{9,11},{10,... | collective-permute-start | bytes 405512 | tf_op jit(solution)/shard_map/ppermute | solution.py:500
  20.1 1.6 %collective-permute-start.6 = (f32[264,128]{1,0:T(8,128)S(1)}, f32[264,128]{1,0:T(8,128)S(1)}, u32[]{:S(2)}, u32[]{:S(2)}) collective-permute-start(f32[264,128]{1,0:T(8,128)S(1)} %get-tuple-element.370), channel_id=1, source_target_pairs={{0,4},{1,5},{2,6},{3,7},{4,0},{5,1},{6,2},{7,3},{8,12},{9,13},{10,... | collective-permute-start | bytes 405512 | tf_op jit(solution)/shard_map/ppermute | solution.py:500
  22.6 3.0 %collective-permute-start.8 = (f32[264,128]{1,0:T(8,128)S(1)}, f32[264,128]{1,0:T(8,128)S(1)}, u32[]{:S(2)}, u32[]{:S(2)}) collective-permute-start(f32[264,128]{1,0:T(8,128)S(1)} %fusion.7), channel_id=1, source_target_pairs={{0,8},{1,9},{2,10},{3,11},{4,12},{5,13},{6,14},{7,15},{8,0},{9,1},... | collective-permute-start | bytes 405512 | tf_op jit(solution)/shard_map/ppermute | solution.py:500
  25.6 6.3 %affine.3.refs_5_ = f32[768,1024]{1,0:T(8,128)S(1)} custom-call(f32[1024,1024]{1,0:T(8,128)S(1)} %copy-done.1, f32[1024,1024]{1,0:T(8,128)S(1)} %copy-done.2), custom_call_target="tpu_custom_call" | custom-call | flops 48318382080 | bytes 83886080 | tf_op jit(solution)/shard_map/affine/pallas_call | solution.py:261
  33.9 2.9 %collective-permute-start.11 = (f32[264,128]{1,0:T(8,128)S(1)}, f32[264,128]{1,0:T(8,128)S(1)}, u32[]{:S(2)}, u32[]{:S(2)}) collective-permute-start(f32[264,128]{1,0:T(8,128)S(1)} %add.82), channel_id=1, source_target_pairs={{0,4},{1,5},{2,6},{3,7},{4,0},{5,1},{6,2},{7,3},{8,12},{9,13},{10,... | collective-permute-start | bytes 405512 | tf_op jit(solution)/shard_map/ppermute | solution.py:500
  36.9 3.8 %collective-permute-done.9 = f32[264,128]{1,0:T(8,128)S(1)} collective-permute-done((f32[264,128]{1,0:T(8,128)S(1)}, f32[264,128]{1,0:T(8,128)S(1)}, u32[]{:S(2)}, u32[]{:S(2)}) %collective-permute-start.9) | collective-permute-done | bytes 135200 | tf_op jit(solution)/shard_map/ppermute | solution.py:500
  40.7 1.6 %collective-permute-start.16 = (f32[264,128]{1,0:T(8,128)S(1)}, f32[264,128]{1,0:T(8,128)S(1)}, u32[]{:S(2)}, u32[]{:S(2)}) collective-permute-start(f32[264,128]{1,0:T(8,128)S(1)} %add.83), channel_id=1, source_target_pairs={{0,2},{1,3},{2,0},{3,1},{4,6},{5,7},{6,4},{7,5},{8,10},{9,11},{10,... | collective-permute-start | bytes 405512 | tf_op jit(solution)/shard_map/ppermute | solution.py:500
  42.6 1.6 %collective-permute-start.14 = (f32[264,128]{1,0:T(8,128)S(1)}, f32[264,128]{1,0:T(8,128)S(1)}, u32[]{:S(2)}, u32[]{:S(2)}) collective-permute-start(f32[264,128]{1,0:T(8,128)S(1)} %add.83), channel_id=1, source_target_pairs={{0,6},{1,7},{2,4},{3,5},{4,2},{5,3},{6,0},{7,1},{8,14},{9,15},{10,... | collective-permute-start | bytes 405512 | tf_op jit(solution)/shard_map/ppermute | solution.py:500
  45.7 1.7 %turn.1 = (bf16[1024,1024]{1,0:T(8,128)(2,1)S(1)}, bf16[1024,1024]{1,0:T(8,128)(2,1)S(1)}) custom-call(f32[1024,1024]{1,0:T(8,128)S(1)} %copy-done.4), custom_call_target="tpu_custom_call" | custom-call | flops 6442450944 | bytes 83886080 | tf_op jit(solution)/shard_map/turn/pallas_call | solution.py:382
  47.6 3.8 %first_part.2.mid_ref.refs_4_ = f32[1024,1024]{1,0:T(8,128)S(1)} custom-call(s32[1]{0:T(128)} %bitcast.me_ref, f32[1056,128]{1,0:T(8,128)S(1)} %pad_maximum_fusion.refs_0_, f32[1056,128]{1,0:T(8,128)S(1)} %collective-permute-done.13.refs_1_, bf16[1024,1024]{1,0:T(8,128)(2,1)S(1)} %get-tuple-element.281.refs_2_, ...), custom_call_target="tpu_custom_call" | custom-call | flops 32212254720 | bytes 125829120 | tf_op jit(solution)/shard_map/first_part/pallas_call | solution.py:336
  51.8 1.8 %column_product.1.refs_7_ = f32[1024,256]{1,0:T(8,128)S(1)} custom-call(bf16[1024,1024]{1,0:T(8,128)(2,1)S(1)} %get-tuple-element.283.xh.refs_5_, bf16[1024,1024]{1,0:T(8,128)(2,1)S(1)} %get-tuple-element.284.xl.refs_6_, f32[1024,1024]{1,0:T(8,128)S(1)} %first_part.2.mid_ref.refs_4_), custom_call_target="tpu_custom_call" | custom-call | flops 16106127360 | bytes 83886080 | tf_op jit(solution)/shard_map/column_product/pallas_call | solution.py:367
  53.7 6.1 %second_gram.1 = (f32[1056,128]{1,0:T(8,128)S(1)}, f32[1056,128]{1,0:T(8,128)S(1)}, bf16[1024,1024]{1,0:T(8,128)(2,1)S(1)}, bf16[1024,1024]{1,0:T(8,128)(2,1)S(1)}) custom-call(s32[1]{0:T(128)} %bitcast.me_ref, f32[1056,128]{1,0:T(8,128)S(1)} %pad_maximum_fusion.1.refs_0_, f32[1056,128]{1,0:T(8,128)S(1)} %collective-permute-done.17.refs_1_, ...), custom_call_target="tpu_custom_call" | custom-call | flops 51539607552 | bytes 209715200 | tf_op jit(solution)/shard_map/second_gram/pallas_call | solution.py:425
  60.1 3.9 %fourth_gram.1 = (f32[1056,128]{1,0:T(8,128)S(1)}, f32[1056,128]{1,0:T(8,128)S(1)}) custom-call(s32[1]{0:T(128)} %bitcast.me_ref, bf16[1024,1024]{1,0:T(8,128)(2,1)S(1)} %get-tuple-element.283.xh.refs_5_, bf16[1024,1024]{1,0:T(8,128)(2,1)S(1)} %get-tuple-element.284.xl.refs_6_, bf16[1024,1024]{1,0:T(8,128)(2,1)S(1)} %get-tuple-element.309.mh.ah, ...), custom_call_target="tpu_custom_call" | custom-call | flops 32212254720 | bytes 83886080 | tf_op jit(solution)/shard_map/fourth_gram/pallas_call | solution.py:442
  64.1 1.5 %collective-permute-start.22 = (f32[264,128]{1,0:T(8,128)S(1)}, f32[264,128]{1,0:T(8,128)S(1)}, u32[]{:S(2)}, u32[]{:S(2)}) collective-permute-start(f32[264,128]{1,0:T(8,128)S(1)} %get-tuple-element.366), channel_id=1, source_target_pairs={{0,2},{1,3},{2,0},{3,1},{4,6},{5,7},{6,4},{7,5},{8,10},{9,11},{10,... | collective-permute-start | bytes 405512 | tf_op jit(solution)/shard_map/ppermute | solution.py:500
  65.6 2.1 %collective-permute-start.20 = (f32[264,128]{1,0:T(8,128)S(1)}, f32[264,128]{1,0:T(8,128)S(1)}, u32[]{:S(2)}, u32[]{:S(2)}) collective-permute-start(f32[264,128]{1,0:T(8,128)S(1)} %get-tuple-element.368), channel_id=1, source_target_pairs={{0,6},{1,7},{2,4},{3,5},{4,2},{5,3},{6,0},{7,1},{8,14},{9,15},{10,... | collective-permute-start | bytes 405512 | tf_op jit(solution)/shard_map/ppermute | solution.py:500
  67.7 2.4 %affine_parts.2.refs_4_.refs_0_ = f32[256,1024]{1,0:T(8,128)S(1)} custom-call(bf16[1024,1024]{1,0:T(8,128)(2,1)S(1)} %get-tuple-element.309.mh.ah, bf16[1024,1024]{1,0:T(8,128)(2,1)S(1)} %get-tuple-element.310.ml.al, f32[1024,1024]{1,0:T(8,128)S(1)} %copy-done.3), custom_call_target="tpu_custom_call" | custom-call | flops 16106127360 | bytes 83886080 | tf_op jit(solution)/shard_map/affine_parts/pallas_call | solution.py:283
  72.0 2.1 %collective-permute-start.23 = (f32[264,128]{1,0:T(8,128)S(1)}, f32[264,128]{1,0:T(8,128)S(1)}, u32[]{:S(2)}, u32[]{:S(2)}) collective-permute-start(f32[264,128]{1,0:T(8,128)S(1)} %get-tuple-element.365), channel_id=1, source_target_pairs={{0,6},{1,7},{2,4},{3,5},{4,2},{5,3},{6,0},{7,1},{8,14},{9,15},{10,... | collective-permute-start | bytes 405512 | tf_op jit(solution)/shard_map/ppermute | solution.py:500
  74.2 1.6 %collective-permute-start.26 = (f32[264,128]{1,0:T(8,128)S(1)}, f32[264,128]{1,0:T(8,128)S(1)}, u32[]{:S(2)}, u32[]{:S(2)}) collective-permute-start(f32[264,128]{1,0:T(8,128)S(1)} %fusion.1), channel_id=1, source_target_pairs={{0,8},{1,9},{2,10},{3,11},{4,12},{5,13},{6,14},{7,15},{8,0},{9,1},... | collective-permute-start | bytes 405512 | tf_op jit(solution)/shard_map/ppermute | solution.py:500
  75.8 5.7 %affine_parts.3.refs_5_.refs_1_ = f32[768,1024]{1,0:T(8,128)S(1)} custom-call(bf16[1024,1024]{1,0:T(8,128)(2,1)S(1)} %get-tuple-element.309.mh.ah, bf16[1024,1024]{1,0:T(8,128)(2,1)S(1)} %get-tuple-element.310.ml.al, f32[1024,1024]{1,0:T(8,128)S(1)} %copy-done.3), custom_call_target="tpu_custom_call" | custom-call | flops 48318382080 | bytes 83886080 | tf_op jit(solution)/shard_map/affine_parts/pallas_call | solution.py:283
  81.6 1.7 %collective-permute-done.23 = f32[264,128]{1,0:T(8,128)S(1)} collective-permute-done((f32[264,128]{1,0:T(8,128)S(1)}, f32[264,128]{1,0:T(8,128)S(1)}, u32[]{:S(2)}, u32[]{:S(2)}) %collective-permute-start.23) | collective-permute-done | bytes 135200 | tf_op jit(solution)/shard_map/ppermute | solution.py:500
  84.9 3.4 %collective-permute-start.29 = (f32[264,128]{1,0:T(8,128)S(1)}, f32[264,128]{1,0:T(8,128)S(1)}, u32[]{:S(2)}, u32[]{:S(2)}) collective-permute-start(f32[264,128]{1,0:T(8,128)S(1)} %add.93), channel_id=1, source_target_pairs={{0,4},{1,5},{2,6},{3,7},{4,0},{5,1},{6,2},{7,3},{8,12},{9,13},{10,... | collective-permute-start | bytes 405512 | tf_op jit(solution)/shard_map/ppermute | solution.py:500
  88.3 3.3 %collective-permute-done.27 = f32[264,128]{1,0:T(8,128)S(1)} collective-permute-done((f32[264,128]{1,0:T(8,128)S(1)}, f32[264,128]{1,0:T(8,128)S(1)}, u32[]{:S(2)}, u32[]{:S(2)}) %collective-permute-start.27) | collective-permute-done | bytes 135200 | tf_op jit(solution)/shard_map/ppermute | solution.py:500
  91.7 1.6 %collective-permute-start.34 = (f32[264,128]{1,0:T(8,128)S(1)}, f32[264,128]{1,0:T(8,128)S(1)}, u32[]{:S(2)}, u32[]{:S(2)}) collective-permute-start(f32[264,128]{1,0:T(8,128)S(1)} %add.92), channel_id=1, source_target_pairs={{0,2},{1,3},{2,0},{3,1},{4,6},{5,7},{6,4},{7,5},{8,10},{9,11},{10,... | collective-permute-start | bytes 405512 | tf_op jit(solution)/shard_map/ppermute | solution.py:500
  93.2 2.9 %collective-permute-start.32 = (f32[264,128]{1,0:T(8,128)S(1)}, f32[264,128]{1,0:T(8,128)S(1)}, u32[]{:S(2)}, u32[]{:S(2)}) collective-permute-start(f32[264,128]{1,0:T(8,128)S(1)} %add.92), channel_id=1, source_target_pairs={{0,6},{1,7},{2,4},{3,5},{4,2},{5,3},{6,0},{7,1},{8,14},{9,15},{10,... | collective-permute-start | bytes 405512 | tf_op jit(solution)/shard_map/ppermute | solution.py:500
  98.5 2.2 %first_part.3 = (f32[1024,256]{1,0:T(8,128)S(1)}, bf16[1024,1024]{1,0:T(8,128)(2,1)S(1)}, bf16[1024,1024]{1,0:T(8,128)(2,1)S(1)}) custom-call(s32[1]{0:T(128)} %bitcast.me_ref, f32[1056,128]{1,0:T(8,128)S(1)} %pad_maximum_fusion.2.refs_0_, f32[1056,128]{1,0:T(8,128)S(1)} %collective-permute-done.31.refs_1_, bf16[1024,1024]{1,0:T(8,128)(2,1)S(1)} %cut.4.refs_2_.ah, ...), custom_call_target="tpu_custom_call" | custom-call | flops 32212254720 | bytes 125829120 | tf_op jit(solution)/shard_map/first_part/pallas_call | solution.py:336
  101.9 1.8 %other_part.1.refs_5_ = f32[1024,768]{1,0:T(8,128)S(1)} custom-call(bf16[1024,1024]{1,0:T(8,128)(2,1)S(1)} %cut.4.refs_2_.ah, bf16[1024,1024]{1,0:T(8,128)(2,1)S(1)} %cut.5.refs_3_.al, bf16[1024,1024]{1,0:T(8,128)(2,1)S(1)} %get-tuple-element.356.hi, bf16[1024,1024]{1,0:T(8,128)(2,1)S(1)} %get-tuple-element.357.lo, ...), custom_call_target="tpu_custom_call" | custom-call | flops 16106127360 | bytes 125829120 | tf_op jit(solution)/shard_map/other_part/pallas_call | solution.py:351
  103.8 4.9 %last.1 = f32[1024,1024]{1,0:T(8,128)} custom-call(s32[1]{0:T(128)} %bitcast.me_ref, f32[1056,128]{1,0:T(8,128)S(1)} %pad_maximum_fusion.3.refs_0_, f32[1056,128]{1,0:T(8,128)S(1)} %collective-permute-done.35.refs_1_, bf16[1024,1024]{1,0:T(8,128)(2,1)S(1)} %cut.4.refs_2_.ah, bf16[1024,1024]{1,0:T(8,128)(2,1)S(1)} %cut.5.refs_3_.al, ...), custom_call_target="tpu_custom_call" | custom-call | flops 32212254720 | bytes 125829120 | tf_op jit(solution)/shard_map/last/pallas_call | solution.py:477
  (89 shorter events, 13.6 us)
Async XLA Ops:
  6.9 4.2 %collective-permute-start = (f32[1056,128]{1,0:T(8,128)S(1)}, f32[1056,128]{1,0:T(8,128)S(1)}, u32[]{:S(2)}, u32[]{:S(2)}) collective-permute-start(f32[1056,128]{1,0:T(8,128)S(1)} %get-tuple-element.190), channel_id=1, source_target_pairs={{0,1},{1,0},{2,3},{3,2},{4,5},{5,4},{6,7},{7,6},{8,9},{9,8},{10,11... | collective-permute-start | bytes 1622024 | tf_op jit(solution)/shard_map/ppermute | solution.py:500
  11.2 11.2 %collective-permute-start.4 = (f32[264,128]{1,0:T(8,128)S(1)}, f32[264,128]{1,0:T(8,128)S(1)}, u32[]{:S(2)}, u32[]{:S(2)}) collective-permute-start(f32[264,128]{1,0:T(8,128)S(1)} %get-tuple-element.372), channel_id=1, source_target_pairs={{0,2},{1,3},{2,0},{3,1},{4,6},{5,7},{6,4},{7,5},{8,10},{9,11},{10,... | collective-permute-start | bytes 405512 | tf_op jit(solution)/shard_map/ppermute | solution.py:500
  13.8 8.7 %collective-permute-start.3 = (f32[264,128]{1,0:T(8,128)S(1)}, f32[264,128]{1,0:T(8,128)S(1)}, u32[]{:S(2)}, u32[]{:S(2)}) collective-permute-start(f32[264,128]{1,0:T(8,128)S(1)} %get-tuple-element.373), channel_id=1, source_target_pairs={{0,4},{1,5},{2,6},{3,7},{4,0},{5,1},{6,2},{7,3},{8,12},{9,13},{10,... | collective-permute-start | bytes 405512 | tf_op jit(solution)/shard_map/ppermute | solution.py:500
  15.4 7.1 %collective-permute-start.2 = (f32[264,128]{1,0:T(8,128)S(1)}, f32[264,128]{1,0:T(8,128)S(1)}, u32[]{:S(2)}, u32[]{:S(2)}) collective-permute-start(f32[264,128]{1,0:T(8,128)S(1)} %get-tuple-element.374), channel_id=1, source_target_pairs={{0,6},{1,7},{2,4},{3,5},{4,2},{5,3},{6,0},{7,1},{8,14},{9,15},{10,... | collective-permute-start | bytes 405512 | tf_op jit(solution)/shard_map/ppermute | solution.py:500
  15.4 2.6 %collective-permute-start.1 = (f32[1056,128]{1,0:T(8,128)S(1)}, f32[1056,128]{1,0:T(8,128)S(1)}, u32[]{:S(2)}, u32[]{:S(2)}) collective-permute-start(f32[1056,128]{1,0:T(8,128)S(1)} %get-tuple-element.196), channel_id=1, source_target_pairs={{0,1},{1,0},{2,3},{3,2},{4,5},{5,4},{6,7},{7,6},{8,9},{9,8},{10,11... | collective-permute-start | bytes 1622024 | tf_op jit(solution)/shard_map/ppermute | solution.py:500
  18.1 13.7 %collective-permute-start.7 = (f32[264,128]{1,0:T(8,128)S(1)}, f32[264,128]{1,0:T(8,128)S(1)}, u32[]{:S(2)}, u32[]{:S(2)}) collective-permute-start(f32[264,128]{1,0:T(8,128)S(1)} %get-tuple-element.369), channel_id=1, source_target_pairs={{0,2},{1,3},{2,0},{3,1},{4,6},{5,7},{6,4},{7,5},{8,10},{9,11},{10,... | collective-permute-start | bytes 405512 | tf_op jit(solution)/shard_map/ppermute | solution.py:500
  20.1 11.8 %collective-permute-start.6 = (f32[264,128]{1,0:T(8,128)S(1)}, f32[264,128]{1,0:T(8,128)S(1)}, u32[]{:S(2)}, u32[]{:S(2)}) collective-permute-start(f32[264,128]{1,0:T(8,128)S(1)} %get-tuple-element.370), channel_id=1, source_target_pairs={{0,4},{1,5},{2,6},{3,7},{4,0},{5,1},{6,2},{7,3},{8,12},{9,13},{10,... | collective-permute-start | bytes 405512 | tf_op jit(solution)/shard_map/ppermute | solution.py:500
  22.4 9.5 %collective-permute-start.5 = (f32[264,128]{1,0:T(8,128)S(1)}, f32[264,128]{1,0:T(8,128)S(1)}, u32[]{:S(2)}, u32[]{:S(2)}) collective-permute-start(f32[264,128]{1,0:T(8,128)S(1)} %get-tuple-element.371), channel_id=1, source_target_pairs={{0,6},{1,7},{2,4},{3,5},{4,2},{5,3},{6,0},{7,1},{8,14},{9,15},{10,... | collective-permute-start | bytes 405512 | tf_op jit(solution)/shard_map/ppermute | solution.py:500
  22.6 10.3 %collective-permute-start.8 = (f32[264,128]{1,0:T(8,128)S(1)}, f32[264,128]{1,0:T(8,128)S(1)}, u32[]{:S(2)}, u32[]{:S(2)}) collective-permute-start(f32[264,128]{1,0:T(8,128)S(1)} %fusion.7), channel_id=1, source_target_pairs={{0,8},{1,9},{2,10},{3,11},{4,12},{5,13},{6,14},{7,15},{8,0},{9,1},... | collective-permute-start | bytes 405512 | tf_op jit(solution)/shard_map/ppermute | solution.py:500
  31.9 8.7 %collective-permute-start.9 = (f32[264,128]{1,0:T(8,128)S(1)}, f32[264,128]{1,0:T(8,128)S(1)}, u32[]{:S(2)}, u32[]{:S(2)}) collective-permute-start(f32[264,128]{1,0:T(8,128)S(1)} %fusion.5), channel_id=1, source_target_pairs={{0,8},{1,9},{2,10},{3,11},{4,12},{5,13},{6,14},{7,15},{8,0},{9,1},... | collective-permute-start | bytes 405512 | tf_op jit(solution)/shard_map/ppermute | solution.py:500
  32.9 9.7 %collective-permute-start.12 = (f32[264,128]{1,0:T(8,128)S(1)}, f32[264,128]{1,0:T(8,128)S(1)}, u32[]{:S(2)}, u32[]{:S(2)}) collective-permute-start(f32[264,128]{1,0:T(8,128)S(1)} %add.82), channel_id=1, source_target_pairs={{0,2},{1,3},{2,0},{3,1},{4,6},{5,7},{6,4},{7,5},{8,10},{9,11},{10,... | collective-permute-start | bytes 405512 | tf_op jit(solution)/shard_map/ppermute | solution.py:500
  33.9 10.3 %collective-permute-start.11 = (f32[264,128]{1,0:T(8,128)S(1)}, f32[264,128]{1,0:T(8,128)S(1)}, u32[]{:S(2)}, u32[]{:S(2)}) collective-permute-start(f32[264,128]{1,0:T(8,128)S(1)} %add.82), channel_id=1, source_target_pairs={{0,4},{1,5},{2,6},{3,7},{4,0},{5,1},{6,2},{7,3},{8,12},{9,13},{10,... | collective-permute-start | bytes 405512 | tf_op jit(solution)/shard_map/ppermute | solution.py:500
  36.9 8.7 %collective-permute-start.10 = (f32[264,128]{1,0:T(8,128)S(1)}, f32[264,128]{1,0:T(8,128)S(1)}, u32[]{:S(2)}, u32[]{:S(2)}) collective-permute-start(f32[264,128]{1,0:T(8,128)S(1)} %add.82), channel_id=1, source_target_pairs={{0,6},{1,7},{2,4},{3,5},{4,2},{5,3},{6,0},{7,1},{8,14},{9,15},{10,... | collective-permute-start | bytes 405512 | tf_op jit(solution)/shard_map/ppermute | solution.py:500
  40.7 10.7 %collective-permute-start.16 = (f32[264,128]{1,0:T(8,128)S(1)}, f32[264,128]{1,0:T(8,128)S(1)}, u32[]{:S(2)}, u32[]{:S(2)}) collective-permute-start(f32[264,128]{1,0:T(8,128)S(1)} %add.83), channel_id=1, source_target_pairs={{0,2},{1,3},{2,0},{3,1},{4,6},{5,7},{6,4},{7,5},{8,10},{9,11},{10,... | collective-permute-start | bytes 405512 | tf_op jit(solution)/shard_map/ppermute | solution.py:500
  42.2 9.2 %collective-permute-start.15 = (f32[264,128]{1,0:T(8,128)S(1)}, f32[264,128]{1,0:T(8,128)S(1)}, u32[]{:S(2)}, u32[]{:S(2)}) collective-permute-start(f32[264,128]{1,0:T(8,128)S(1)} %add.83), channel_id=1, source_target_pairs={{0,4},{1,5},{2,6},{3,7},{4,0},{5,1},{6,2},{7,3},{8,12},{9,13},{10,... | collective-permute-start | bytes 405512 | tf_op jit(solution)/shard_map/ppermute | solution.py:500
  42.6 8.8 %collective-permute-start.14 = (f32[264,128]{1,0:T(8,128)S(1)}, f32[264,128]{1,0:T(8,128)S(1)}, u32[]{:S(2)}, u32[]{:S(2)}) collective-permute-start(f32[264,128]{1,0:T(8,128)S(1)} %add.83), channel_id=1, source_target_pairs={{0,6},{1,7},{2,4},{3,5},{4,2},{5,3},{6,0},{7,1},{8,14},{9,15},{10,... | collective-permute-start | bytes 405512 | tf_op jit(solution)/shard_map/ppermute | solution.py:500
  59.8 4.2 %collective-permute-start.18 = (f32[1056,128]{1,0:T(8,128)S(1)}, f32[1056,128]{1,0:T(8,128)S(1)}, u32[]{:S(2)}, u32[]{:S(2)}) collective-permute-start(f32[1056,128]{1,0:T(8,128)S(1)} %get-tuple-element.292), channel_id=1, source_target_pairs={{0,1},{1,0},{2,3},{3,2},{4,5},{5,4},{6,7},{7,6},{8,9},{9,8},{10,11... | collective-permute-start | bytes 1622024 | tf_op jit(solution)/shard_map/ppermute | solution.py:500
  64.1 7.9 %collective-permute-start.22 = (f32[264,128]{1,0:T(8,128)S(1)}, f32[264,128]{1,0:T(8,128)S(1)}, u32[]{:S(2)}, u32[]{:S(2)}) collective-permute-start(f32[264,128]{1,0:T(8,128)S(1)} %get-tuple-element.366), channel_id=1, source_target_pairs={{0,2},{1,3},{2,0},{3,1},{4,6},{5,7},{6,4},{7,5},{8,10},{9,11},{10,... | collective-permute-start | bytes 405512 | tf_op jit(solution)/shard_map/ppermute | solution.py:500
  65.6 8.5 %collective-permute-start.21 = (f32[264,128]{1,0:T(8,128)S(1)}, f32[264,128]{1,0:T(8,128)S(1)}, u32[]{:S(2)}, u32[]{:S(2)}) collective-permute-start(f32[264,128]{1,0:T(8,128)S(1)} %get-tuple-element.367), channel_id=1, source_target_pairs={{0,4},{1,5},{2,6},{3,7},{4,0},{5,1},{6,2},{7,3},{8,12},{9,13},{10,... | collective-permute-start | bytes 405512 | tf_op jit(solution)/shard_map/ppermute | solution.py:500
  65.6 8.5 %collective-permute-start.20 = (f32[264,128]{1,0:T(8,128)S(1)}, f32[264,128]{1,0:T(8,128)S(1)}, u32[]{:S(2)}, u32[]{:S(2)}) collective-permute-start(f32[264,128]{1,0:T(8,128)S(1)} %get-tuple-element.368), channel_id=1, source_target_pairs={{0,6},{1,7},{2,4},{3,5},{4,2},{5,3},{6,0},{7,1},{8,14},{9,15},{10,... | collective-permute-start | bytes 405512 | tf_op jit(solution)/shard_map/ppermute | solution.py:500
  67.7 2.5 %collective-permute-start.19 = (f32[1056,128]{1,0:T(8,128)S(1)}, f32[1056,128]{1,0:T(8,128)S(1)}, u32[]{:S(2)}, u32[]{:S(2)}) collective-permute-start(f32[1056,128]{1,0:T(8,128)S(1)} %get-tuple-element.298), channel_id=1, source_target_pairs={{0,1},{1,0},{2,3},{3,2},{4,5},{5,4},{6,7},{7,6},{8,9},{9,8},{10,11... | collective-permute-start | bytes 1622024 | tf_op jit(solution)/shard_map/ppermute | solution.py:500
  70.2 11.3 %collective-permute-start.25 = (f32[264,128]{1,0:T(8,128)S(1)}, f32[264,128]{1,0:T(8,128)S(1)}, u32[]{:S(2)}, u32[]{:S(2)}) collective-permute-start(f32[264,128]{1,0:T(8,128)S(1)} %get-tuple-element.363), channel_id=1, source_target_pairs={{0,2},{1,3},{2,0},{3,1},{4,6},{5,7},{6,4},{7,5},{8,10},{9,11},{10,... | collective-permute-start | bytes 405512 | tf_op jit(solution)/shard_map/ppermute | solution.py:500
  71.7 9.8 %collective-permute-start.24 = (f32[264,128]{1,0:T(8,128)S(1)}, f32[264,128]{1,0:T(8,128)S(1)}, u32[]{:S(2)}, u32[]{:S(2)}) collective-permute-start(f32[264,128]{1,0:T(8,128)S(1)} %get-tuple-element.364), channel_id=1, source_target_pairs={{0,4},{1,5},{2,6},{3,7},{4,0},{5,1},{6,2},{7,3},{8,12},{9,13},{10,... | collective-permute-start | bytes 405512 | tf_op jit(solution)/shard_map/ppermute | solution.py:500
  72.0 11.3 %collective-permute-start.23 = (f32[264,128]{1,0:T(8,128)S(1)}, f32[264,128]{1,0:T(8,128)S(1)}, u32[]{:S(2)}, u32[]{:S(2)}) collective-permute-start(f32[264,128]{1,0:T(8,128)S(1)} %get-tuple-element.365), channel_id=1, source_target_pairs={{0,6},{1,7},{2,4},{3,5},{4,2},{5,3},{6,0},{7,1},{8,14},{9,15},{10,... | collective-permute-start | bytes 405512 | tf_op jit(solution)/shard_map/ppermute | solution.py:500
  74.2 9.6 %collective-permute-start.26 = (f32[264,128]{1,0:T(8,128)S(1)}, f32[264,128]{1,0:T(8,128)S(1)}, u32[]{:S(2)}, u32[]{:S(2)}) collective-permute-start(f32[264,128]{1,0:T(8,128)S(1)} %fusion.1), channel_id=1, source_target_pairs={{0,8},{1,9},{2,10},{3,11},{4,12},{5,13},{6,14},{7,15},{8,0},{9,1},... | collective-permute-start | bytes 405512 | tf_op jit(solution)/shard_map/ppermute | solution.py:500
  83.3 8.3 %collective-permute-start.27 = (f32[264,128]{1,0:T(8,128)S(1)}, f32[264,128]{1,0:T(8,128)S(1)}, u32[]{:S(2)}, u32[]{:S(2)}) collective-permute-start(f32[264,128]{1,0:T(8,128)S(1)} %fusion.3), channel_id=1, source_target_pairs={{0,8},{1,9},{2,10},{3,11},{4,12},{5,13},{6,14},{7,15},{8,0},{9,1},... | collective-permute-start | bytes 405512 | tf_op jit(solution)/shard_map/ppermute | solution.py:500
  83.8 9.4 %collective-permute-start.30 = (f32[264,128]{1,0:T(8,128)S(1)}, f32[264,128]{1,0:T(8,128)S(1)}, u32[]{:S(2)}, u32[]{:S(2)}) collective-permute-start(f32[264,128]{1,0:T(8,128)S(1)} %add.93), channel_id=1, source_target_pairs={{0,2},{1,3},{2,0},{3,1},{4,6},{5,7},{6,4},{7,5},{8,10},{9,11},{10,... | collective-permute-start | bytes 405512 | tf_op jit(solution)/shard_map/ppermute | solution.py:500
  84.9 11.2 %collective-permute-start.29 = (f32[264,128]{1,0:T(8,128)S(1)}, f32[264,128]{1,0:T(8,128)S(1)}, u32[]{:S(2)}, u32[]{:S(2)}) collective-permute-start(f32[264,128]{1,0:T(8,128)S(1)} %add.93), channel_id=1, source_target_pairs={{0,4},{1,5},{2,6},{3,7},{4,0},{5,1},{6,2},{7,3},{8,12},{9,13},{10,... | collective-permute-start | bytes 405512 | tf_op jit(solution)/shard_map/ppermute | solution.py:500
  88.3 8.1 %collective-permute-start.28 = (f32[264,128]{1,0:T(8,128)S(1)}, f32[264,128]{1,0:T(8,128)S(1)}, u32[]{:S(2)}, u32[]{:S(2)}) collective-permute-start(f32[264,128]{1,0:T(8,128)S(1)} %add.93), channel_id=1, source_target_pairs={{0,6},{1,7},{2,4},{3,5},{4,2},{5,3},{6,0},{7,1},{8,14},{9,15},{10,... | collective-permute-start | bytes 405512 | tf_op jit(solution)/shard_map/ppermute | solution.py:500
  91.7 9.0 %collective-permute-start.34 = (f32[264,128]{1,0:T(8,128)S(1)}, f32[264,128]{1,0:T(8,128)S(1)}, u32[]{:S(2)}, u32[]{:S(2)}) collective-permute-start(f32[264,128]{1,0:T(8,128)S(1)} %add.92), channel_id=1, source_target_pairs={{0,2},{1,3},{2,0},{3,1},{4,6},{5,7},{6,4},{7,5},{8,10},{9,11},{10,... | collective-permute-start | bytes 405512 | tf_op jit(solution)/shard_map/ppermute | solution.py:500
  93.2 7.4 %collective-permute-start.33 = (f32[264,128]{1,0:T(8,128)S(1)}, f32[264,128]{1,0:T(8,128)S(1)}, u32[]{:S(2)}, u32[]{:S(2)}) collective-permute-start(f32[264,128]{1,0:T(8,128)S(1)} %add.92), channel_id=1, source_target_pairs={{0,4},{1,5},{2,6},{3,7},{4,0},{5,1},{6,2},{7,3},{8,12},{9,13},{10,... | collective-permute-start | bytes 405512 | tf_op jit(solution)/shard_map/ppermute | solution.py:500
  93.2 8.5 %collective-permute-start.32 = (f32[264,128]{1,0:T(8,128)S(1)}, f32[264,128]{1,0:T(8,128)S(1)}, u32[]{:S(2)}, u32[]{:S(2)}) collective-permute-start(f32[264,128]{1,0:T(8,128)S(1)} %add.92), channel_id=1, source_target_pairs={{0,6},{1,7},{2,4},{3,5},{4,2},{5,3},{6,0},{7,1},{8,14},{9,15},{10,... | collective-permute-start | bytes 405512 | tf_op jit(solution)/shard_map/ppermute | solution.py:500
  (10 other events, 62.1 us)

commit v14 on v13

--- a/solution.py
+++ b/solution.py
@@ -252,7 +252,7 @@
     def step(c):
         out_ref[:, c] = 1.5 * a_ref[r, c] - 0.5 * mm((hi[...], lo[...]), split(b_ref[:, c]))
 
-    tiles(out_ref.shape[1], 256, step)
+    tiles(out_ref.shape[1], 512 if part else 256, step)
 
 
 def affine(a, b, part):
@@ -274,7 +274,7 @@
         product = mm((ah[r], al[r]), split(b_ref[:, c]))
         out_ref[:, c] = 1.5 * (ah[r, c].astype(F32) + al[r, c].astype(F32)) - 0.5 * product
 
-    tiles(out_ref.shape[1], 256, step)
+    tiles(out_ref.shape[1], 512 if part else 256, step)
 
 
 def affine_parts(ah, al, b, part):
@@ -550,7 +550,7 @@
     work()
     (got_b,) = close(env, got_b)
 
-    got_b = b.plane(got_b)
+    got_b = b.plane(got_b)[::-1]
     work()
     a.own(close(env, *got_a))
 

time: 109 us -> 108 us (level)
  no operation moved by 1% of the time
where the time goes in v14:
time: 108 us
  Pallas kernels  54.3 us (50%)
  starting transfers between devices  38.9 us (36%)
  waiting for transfers between devices  12.9 us (12%)
    ppermute x36, starting transfers between devices, swap(): return lax.ppermute(x, 'row', [(i, i ^ offset) for i in range(self.count)])  38.9 us
    ppermute x36, waiting for transfers between devices, swap(): return lax.ppermute(x, 'row', [(i, i ^ offset) for i in range(self.count)])  12.9 us
    pallas_call x2, Pallas kernels, affine(): call(functools.partial(affine_kernel, part), 'affine', struct(height, siz...  8.39 us
    pallas_call x2, Pallas kernels, affine_parts(): call(functools.partial(affine_parts_kernel, part), 'affine_parts', struct...  7.87 us
    pallas_call x1, Pallas kernels, first_gram(): call(functools.partial(first_gram_kernel, shards), 'first_gram', halves(s...  6.9 us
    pallas_call x1, Pallas kernels, second_gram(): call(functools.partial(second_gram_kernel, shards, len(pieces)), 'second_...  6.15 us
    pallas_call x2, Pallas kernels, first_part(): call(functools.partial(first_part_kernel, shards, len(pieces), columns),...  5.92 us
    pallas_call x1, Pallas kernels, last_step(): call(functools.partial(last_kernel, shards, len(pieces)), 'last', struct(...  4.89 us
  transfers between devices with their start and end apart: 36, of which 9 were waited for; matrix products, arithmetic and copies ran while one was open for 0% of the time, Pallas kernels for 34%

profile of v14, /device:TPU:0, one launch (start us, length us, event | category | flops | bytes accessed | tf_op | source)
XLA Modules:
  0.0 107.5 jit_solution(4170410911025791430)
XLA Ops:
  0.0 6.9 %first_gram.1 = (f32[1056,128]{1,0:T(8,128)S(1)}, f32[1056,128]{1,0:T(8,128)S(1)}, bf16[1024,1024]{1,0:T(8,128)(2,1)S(1)}, bf16[1024,1024]{1,0:T(8,128)(2,1)S(1)...) custom-call(s32[1]{0:T(128)} %bitcast.me_ref, f32[1024,1024]{1,0:T(8,128)} %x_ref, f32[1024,1024]{1,0:T(8,128)} %a_ref.1), custom_call_target="tpu_custom_call" | custom-call | flops 32212254720 | bytes 167772160 | tf_op jit(solution)/shard_map/first_gram/pallas_call | solution.py:198
  7.4 3.6 %other_gram.1 = (f32[1056,128]{1,0:T(8,128)S(1)}, f32[1056,128]{1,0:T(8,128)S(1)}) custom-call(s32[1]{0:T(128)} %bitcast.me_ref, bf16[1024,1024]{1,0:T(8,128)(2,1)S(1)} %get-tuple-element.184.ah, bf16[1024,1024]{1,0:T(8,128)(2,1)S(1)} %get-tuple-element.185.al, bf16[1024,1024]{1,0:T(8,128)(2,1)S(1)} %get-tuple-element.186.bh, ...), custom_call_target="tpu_custom_call" | custom-call | flops 32212254720 | bytes 83886080 | tf_op jit(solution)/shard_map/other_gram/pallas_call | solution.py:228
  11.2 2.6 %collective-permute-start.4 = (f32[264,128]{1,0:T(8,128)S(1)}, f32[264,128]{1,0:T(8,128)S(1)}, u32[]{:S(2)}, u32[]{:S(2)}) collective-permute-start(f32[264,128]{1,0:T(8,128)S(1)} %get-tuple-element.372), channel_id=1, source_target_pairs={{0,2},{1,3},{2,0},{3,1},{4,6},{5,7},{6,4},{7,5},{8,10},{9,11},{10,... | collective-permute-start | bytes 405512 | tf_op jit(solution)/shard_map/ppermute | solution.py:500
  13.8 1.6 %collective-permute-start.3 = (f32[264,128]{1,0:T(8,128)S(1)}, f32[264,128]{1,0:T(8,128)S(1)}, u32[]{:S(2)}, u32[]{:S(2)}) collective-permute-start(f32[264,128]{1,0:T(8,128)S(1)} %get-tuple-element.373), channel_id=1, source_target_pairs={{0,4},{1,5},{2,6},{3,7},{4,0},{5,1},{6,2},{7,3},{8,12},{9,13},{10,... | collective-permute-start | bytes 405512 | tf_op jit(solution)/shard_map/ppermute | solution.py:500
  15.4 2.6 %affine.2.refs_4_ = f32[256,1024]{1,0:T(8,128)S(1)} custom-call(f32[1024,1024]{1,0:T(8,128)S(1)} %copy-done.1, f32[1024,1024]{1,0:T(8,128)S(1)} %copy-done.2), custom_call_target="tpu_custom_call" | custom-call | flops 16106127360 | bytes 83886080 | tf_op jit(solution)/shard_map/affine/pallas_call | solution.py:261
  18.1 3.0 %collective-permute-start.7 = (f32[264,128]{1,0:T(8,128)S(1)}, f32[264,128]{1,0:T(8,128)S(1)}, u32[]{:S(2)}, u32[]{:S(2)}) collective-permute-start(f32[264,128]{1,0:T(8,128)S(1)} %get-tuple-element.369), channel_id=1, source_target_pairs={{0,6},{1,7},{2,4},{3,5},{4,2},{5,3},{6,0},{7,1},{8,14},{9,15},{10,... | collective-permute-start | bytes 405512 | tf_op jit(solution)/shard_map/ppermute | solution.py:500
  22.6 3.0 %collective-permute-start.8 = (f32[264,128]{1,0:T(8,128)S(1)}, f32[264,128]{1,0:T(8,128)S(1)}, u32[]{:S(2)}, u32[]{:S(2)}) collective-permute-start(f32[264,128]{1,0:T(8,128)S(1)} %fusion.7), channel_id=1, source_target_pairs={{0,8},{1,9},{2,10},{3,11},{4,12},{5,13},{6,14},{7,15},{8,0},{9,1},... | collective-permute-start | bytes 405512 | tf_op jit(solution)/shard_map/ppermute | solution.py:500
  25.6 5.8 %affine.3.refs_5_ = f32[768,1024]{1,0:T(8,128)S(1)} custom-call(f32[1024,1024]{1,0:T(8,128)S(1)} %copy-done.1, f32[1024,1024]{1,0:T(8,128)S(1)} %copy-done.2), custom_call_target="tpu_custom_call" | custom-call | flops 48318382080 | bytes 83886080 | tf_op jit(solution)/shard_map/affine/pallas_call | solution.py:261
  33.5 1.5 %collective-permute-start.11 = (f32[264,128]{1,0:T(8,128)S(1)}, f32[264,128]{1,0:T(8,128)S(1)}, u32[]{:S(2)}, u32[]{:S(2)}) collective-permute-start(f32[264,128]{1,0:T(8,128)S(1)} %add.82), channel_id=1, source_target_pairs={{0,4},{1,5},{2,6},{3,7},{4,0},{5,1},{6,2},{7,3},{8,12},{9,13},{10,... | collective-permute-start | bytes 405512 | tf_op jit(solution)/shard_map/ppermute | solution.py:500
  36.3 4.2 %collective-permute-done.9 = f32[264,128]{1,0:T(8,128)S(1)} collective-permute-done((f32[264,128]{1,0:T(8,128)S(1)}, f32[264,128]{1,0:T(8,128)S(1)}, u32[]{:S(2)}, u32[]{:S(2)}) %collective-permute-start.9) | collective-permute-done | bytes 135200 | tf_op jit(solution)/shard_map/ppermute | solution.py:500
  40.5 1.3 %collective-permute-start.16 = (f32[264,128]{1,0:T(8,128)S(1)}, f32[264,128]{1,0:T(8,128)S(1)}, u32[]{:S(2)}, u32[]{:S(2)}) collective-permute-start(f32[264,128]{1,0:T(8,128)S(1)} %add.83), channel_id=1, source_target_pairs={{0,2},{1,3},{2,0},{3,1},{4,6},{5,7},{6,4},{7,5},{8,10},{9,11},{10,... | collective-permute-start | bytes 405512 | tf_op jit(solution)/shard_map/ppermute | solution.py:500
  42.2 1.9 %collective-permute-start.14 = (f32[264,128]{1,0:T(8,128)S(1)}, f32[264,128]{1,0:T(8,128)S(1)}, u32[]{:S(2)}, u32[]{:S(2)}) collective-permute-start(f32[264,128]{1,0:T(8,128)S(1)} %add.83), channel_id=1, source_target_pairs={{0,6},{1,7},{2,4},{3,5},{4,2},{5,3},{6,0},{7,1},{8,14},{9,15},{10,... | collective-permute-start | bytes 405512 | tf_op jit(solution)/shard_map/ppermute | solution.py:500
  45.2 1.7 %turn.1 = (bf16[1024,1024]{1,0:T(8,128)(2,1)S(1)}, bf16[1024,1024]{1,0:T(8,128)(2,1)S(1)}) custom-call(f32[1024,1024]{1,0:T(8,128)S(1)} %copy-done.4), custom_call_target="tpu_custom_call" | custom-call | flops 6442450944 | bytes 83886080 | tf_op jit(solution)/shard_map/turn/pallas_call | solution.py:382
  47.1 3.8 %first_part.2.mid_ref.refs_4_ = f32[1024,1024]{1,0:T(8,128)S(1)} custom-call(s32[1]{0:T(128)} %bitcast.me_ref, f32[1056,128]{1,0:T(8,128)S(1)} %pad_maximum_fusion.refs_0_, f32[1056,128]{1,0:T(8,128)S(1)} %collective-permute-done.13.refs_1_, bf16[1024,1024]{1,0:T(8,128)(2,1)S(1)} %get-tuple-element.281.refs_2_, ...), custom_call_target="tpu_custom_call" | custom-call | flops 32212254720 | bytes 125829120 | tf_op jit(solution)/shard_map/first_part/pallas_call | solution.py:336
  51.3 1.8 %column_product.1.refs_7_ = f32[1024,256]{1,0:T(8,128)S(1)} custom-call(bf16[1024,1024]{1,0:T(8,128)(2,1)S(1)} %get-tuple-element.283.xh.refs_5_, bf16[1024,1024]{1,0:T(8,128)(2,1)S(1)} %get-tuple-element.284.xl.refs_6_, f32[1024,1024]{1,0:T(8,128)S(1)} %first_part.2.mid_ref.refs_4_), custom_call_target="tpu_custom_call" | custom-call | flops 16106127360 | bytes 83886080 | tf_op jit(solution)/shard_map/column_product/pallas_call | solution.py:367
  53.2 6.1 %second_gram.1 = (f32[1056,128]{1,0:T(8,128)S(1)}, f32[1056,128]{1,0:T(8,128)S(1)}, bf16[1024,1024]{1,0:T(8,128)(2,1)S(1)}, bf16[1024,1024]{1,0:T(8,128)(2,1)S(1)}) custom-call(s32[1]{0:T(128)} %bitcast.me_ref, f32[1056,128]{1,0:T(8,128)S(1)} %pad_maximum_fusion.1.refs_0_, f32[1056,128]{1,0:T(8,128)S(1)} %collective-permute-done.17.refs_1_, ...), custom_call_target="tpu_custom_call" | custom-call | flops 51539607552 | bytes 209715200 | tf_op jit(solution)/shard_map/second_gram/pallas_call | solution.py:425
  59.6 3.9 %fourth_gram.1 = (f32[1056,128]{1,0:T(8,128)S(1)}, f32[1056,128]{1,0:T(8,128)S(1)}) custom-call(s32[1]{0:T(128)} %bitcast.me_ref, bf16[1024,1024]{1,0:T(8,128)(2,1)S(1)} %get-tuple-element.283.xh.refs_5_, bf16[1024,1024]{1,0:T(8,128)(2,1)S(1)} %get-tuple-element.284.xl.refs_6_, bf16[1024,1024]{1,0:T(8,128)(2,1)S(1)} %get-tuple-element.309.mh.ah, ...), custom_call_target="tpu_custom_call" | custom-call | flops 32212254720 | bytes 83886080 | tf_op jit(solution)/shard_map/fourth_gram/pallas_call | solution.py:442
  64.5 2.6 %collective-permute-start.20 = (f32[264,128]{1,0:T(8,128)S(1)}, f32[264,128]{1,0:T(8,128)S(1)}, u32[]{:S(2)}, u32[]{:S(2)}) collective-permute-start(f32[264,128]{1,0:T(8,128)S(1)} %get-tuple-element.368), channel_id=1, source_target_pairs={{0,6},{1,7},{2,4},{3,5},{4,2},{5,3},{6,0},{7,1},{8,14},{9,15},{10,... | collective-permute-start | bytes 405512 | tf_op jit(solution)/shard_map/ppermute | solution.py:500
  67.1 2.5 %affine_parts.2.refs_4_.refs_0_ = f32[256,1024]{1,0:T(8,128)S(1)} custom-call(bf16[1024,1024]{1,0:T(8,128)(2,1)S(1)} %get-tuple-element.309.mh.ah, bf16[1024,1024]{1,0:T(8,128)(2,1)S(1)} %get-tuple-element.310.ml.al, f32[1024,1024]{1,0:T(8,128)S(1)} %copy-done.3), custom_call_target="tpu_custom_call" | custom-call | flops 16106127360 | bytes 83886080 | tf_op jit(solution)/shard_map/affine_parts/pallas_call | solution.py:283
  70.1 2.0 %collective-permute-start.24 = (f32[264,128]{1,0:T(8,128)S(1)}, f32[264,128]{1,0:T(8,128)S(1)}, u32[]{:S(2)}, u32[]{:S(2)}) collective-permute-start(f32[264,128]{1,0:T(8,128)S(1)} %get-tuple-element.364), channel_id=1, source_target_pairs={{0,4},{1,5},{2,6},{3,7},{4,0},{5,1},{6,2},{7,3},{8,12},{9,13},{10,... | collective-permute-start | bytes 405512 | tf_op jit(solution)/shard_map/ppermute | solution.py:500
  73.6 1.7 %collective-permute-start.26 = (f32[264,128]{1,0:T(8,128)S(1)}, f32[264,128]{1,0:T(8,128)S(1)}, u32[]{:S(2)}, u32[]{:S(2)}) collective-permute-start(f32[264,128]{1,0:T(8,128)S(1)} %fusion.1), channel_id=1, source_target_pairs={{0,8},{1,9},{2,10},{3,11},{4,12},{5,13},{6,14},{7,15},{8,0},{9,1},... | collective-permute-start | bytes 405512 | tf_op jit(solution)/shard_map/ppermute | solution.py:500
  75.4 5.4 %affine_parts.3.refs_5_.refs_1_ = f32[768,1024]{1,0:T(8,128)S(1)} custom-call(bf16[1024,1024]{1,0:T(8,128)(2,1)S(1)} %get-tuple-element.309.mh.ah, bf16[1024,1024]{1,0:T(8,128)(2,1)S(1)} %get-tuple-element.310.ml.al, f32[1024,1024]{1,0:T(8,128)S(1)} %copy-done.3), custom_call_target="tpu_custom_call" | custom-call | flops 48318382080 | bytes 83886080 | tf_op jit(solution)/shard_map/affine_parts/pallas_call | solution.py:283
  83.2 3.2 %collective-permute-start.29 = (f32[264,128]{1,0:T(8,128)S(1)}, f32[264,128]{1,0:T(8,128)S(1)}, u32[]{:S(2)}, u32[]{:S(2)}) collective-permute-start(f32[264,128]{1,0:T(8,128)S(1)} %add.93), channel_id=1, source_target_pairs={{0,4},{1,5},{2,6},{3,7},{4,0},{5,1},{6,2},{7,3},{8,12},{9,13},{10,... | collective-permute-start | bytes 405512 | tf_op jit(solution)/shard_map/ppermute | solution.py:500
  86.4 1.4 %collective-permute-start.28 = (f32[264,128]{1,0:T(8,128)S(1)}, f32[264,128]{1,0:T(8,128)S(1)}, u32[]{:S(2)}, u32[]{:S(2)}) collective-permute-start(f32[264,128]{1,0:T(8,128)S(1)} %add.93), channel_id=1, source_target_pairs={{0,6},{1,7},{2,4},{3,5},{4,2},{5,3},{6,0},{7,1},{8,14},{9,15},{10,... | collective-permute-start | bytes 405512 | tf_op jit(solution)/shard_map/ppermute | solution.py:500
  87.8 2.9 %collective-permute-done.27 = f32[264,128]{1,0:T(8,128)S(1)} collective-permute-done((f32[264,128]{1,0:T(8,128)S(1)}, f32[264,128]{1,0:T(8,128)S(1)}, u32[]{:S(2)}, u32[]{:S(2)}) %collective-permute-start.27) | collective-permute-done | bytes 135200 | tf_op jit(solution)/shard_map/ppermute | solution.py:500
  90.8 1.5 %collective-permute-start.34 = (f32[264,128]{1,0:T(8,128)S(1)}, f32[264,128]{1,0:T(8,128)S(1)}, u32[]{:S(2)}, u32[]{:S(2)}) collective-permute-start(f32[264,128]{1,0:T(8,128)S(1)} %add.92), channel_id=1, source_target_pairs={{0,2},{1,3},{2,0},{3,1},{4,6},{5,7},{6,4},{7,5},{8,10},{9,11},{10,... | collective-permute-start | bytes 405512 | tf_op jit(solution)/shard_map/ppermute | solution.py:500
  92.2 2.1 %collective-permute-start.32 = (f32[264,128]{1,0:T(8,128)S(1)}, f32[264,128]{1,0:T(8,128)S(1)}, u32[]{:S(2)}, u32[]{:S(2)}) collective-permute-start(f32[264,128]{1,0:T(8,128)S(1)} %add.92), channel_id=1, source_target_pairs={{0,6},{1,7},{2,4},{3,5},{4,2},{5,3},{6,0},{7,1},{8,14},{9,15},{10,... | collective-permute-start | bytes 405512 | tf_op jit(solution)/shard_map/ppermute | solution.py:500
  95.2 1.5 %collective-permute-done.31.refs_1_ = f32[1056,128]{1,0:T(8,128)S(1)} collective-permute-done((f32[1056,128]{1,0:T(8,128)S(1)}, f32[1056,128]{1,0:T(8,128)S(1)}, u32[]{:S(2)}, u32[]{:S(2)}) %collective-permute-start.31) | collective-permute-done | bytes 540704 | tf_op jit(solution)/shard_map/ppermute | solution.py:500
  96.7 2.2 %first_part.3 = (f32[1024,256]{1,0:T(8,128)S(1)}, bf16[1024,1024]{1,0:T(8,128)(2,1)S(1)}, bf16[1024,1024]{1,0:T(8,128)(2,1)S(1)}) custom-call(s32[1]{0:T(128)} %bitcast.me_ref, f32[1056,128]{1,0:T(8,128)S(1)} %pad_maximum_fusion.2.refs_0_, f32[1056,128]{1,0:T(8,128)S(1)} %collective-permute-done.31.refs_1_, bf16[1024,1024]{1,0:T(8,128)(2,1)S(1)} %cut.4.refs_2_.ah, ...), custom_call_target="tpu_custom_call" | custom-call | flops 32212254720 | bytes 125829120 | tf_op jit(solution)/shard_map/first_part/pallas_call | solution.py:336
  98.9 1.5 %collective-permute-done.32 = f32[264,128]{1,0:T(8,128)S(1)} collective-permute-done((f32[264,128]{1,0:T(8,128)S(1)}, f32[264,128]{1,0:T(8,128)S(1)}, u32[]{:S(2)}, u32[]{:S(2)}) %collective-permute-start.32) | collective-permute-done | bytes 135200 | tf_op jit(solution)/shard_map/ppermute | solution.py:500
  100.5 1.8 %other_part.1.refs_5_ = f32[1024,768]{1,0:T(8,128)S(1)} custom-call(bf16[1024,1024]{1,0:T(8,128)(2,1)S(1)} %cut.4.refs_2_.ah, bf16[1024,1024]{1,0:T(8,128)(2,1)S(1)} %cut.5.refs_3_.al, bf16[1024,1024]{1,0:T(8,128)(2,1)S(1)} %get-tuple-element.356.hi, bf16[1024,1024]{1,0:T(8,128)(2,1)S(1)} %get-tuple-element.357.lo, ...), custom_call_target="tpu_custom_call" | custom-call | flops 16106127360 | bytes 125829120 | tf_op jit(solution)/shard_map/other_part/pallas_call | solution.py:351
  102.4 4.9 %last.1 = f32[1024,1024]{1,0:T(8,128)} custom-call(s32[1]{0:T(128)} %bitcast.me_ref, f32[1056,128]{1,0:T(8,128)S(1)} %pad_maximum_fusion.3.refs_0_, f32[1056,128]{1,0:T(8,128)S(1)} %collective-permute-done.35.refs_1_, bf16[1024,1024]{1,0:T(8,128)(2,1)S(1)} %cut.4.refs_2_.ah, bf16[1024,1024]{1,0:T(8,128)(2,1)S(1)} %cut.5.refs_3_.al, ...), custom_call_target="tpu_custom_call" | custom-call | flops 32212254720 | bytes 125829120 | tf_op jit(solution)/shard_map/last/pallas_call | solution.py:477
  (89 shorter events, 14.5 us)
Async XLA Ops:
  6.9 4.2 %collective-permute-start = (f32[1056,128]{1,0:T(8,128)S(1)}, f32[1056,128]{1,0:T(8,128)S(1)}, u32[]{:S(2)}, u32[]{:S(2)}) collective-permute-start(f32[1056,128]{1,0:T(8,128)S(1)} %get-tuple-element.190), channel_id=1, source_target_pairs={{0,1},{1,0},{2,3},{3,2},{4,5},{5,4},{6,7},{7,6},{8,9},{9,8},{10,11... | collective-permute-start | bytes 1622024 | tf_op jit(solution)/shard_map/ppermute | solution.py:500
  11.2 11.1 %collective-permute-start.4 = (f32[264,128]{1,0:T(8,128)S(1)}, f32[264,128]{1,0:T(8,128)S(1)}, u32[]{:S(2)}, u32[]{:S(2)}) collective-permute-start(f32[264,128]{1,0:T(8,128)S(1)} %get-tuple-element.372), channel_id=1, source_target_pairs={{0,2},{1,3},{2,0},{3,1},{4,6},{5,7},{6,4},{7,5},{8,10},{9,11},{10,... | collective-permute-start | bytes 405512 | tf_op jit(solution)/shard_map/ppermute | solution.py:500
  13.8 8.7 %collective-permute-start.3 = (f32[264,128]{1,0:T(8,128)S(1)}, f32[264,128]{1,0:T(8,128)S(1)}, u32[]{:S(2)}, u32[]{:S(2)}) collective-permute-start(f32[264,128]{1,0:T(8,128)S(1)} %get-tuple-element.373), channel_id=1, source_target_pairs={{0,4},{1,5},{2,6},{3,7},{4,0},{5,1},{6,2},{7,3},{8,12},{9,13},{10,... | collective-permute-start | bytes 405512 | tf_op jit(solution)/shard_map/ppermute | solution.py:500
  15.4 7.2 %collective-permute-start.2 = (f32[264,128]{1,0:T(8,128)S(1)}, f32[264,128]{1,0:T(8,128)S(1)}, u32[]{:S(2)}, u32[]{:S(2)}) collective-permute-start(f32[264,128]{1,0:T(8,128)S(1)} %get-tuple-element.374), channel_id=1, source_target_pairs={{0,6},{1,7},{2,4},{3,5},{4,2},{5,3},{6,0},{7,1},{8,14},{9,15},{10,... | collective-permute-start | bytes 405512 | tf_op jit(solution)/shard_map/ppermute | solution.py:500
  15.4 2.6 %collective-permute-start.1 = (f32[1056,128]{1,0:T(8,128)S(1)}, f32[1056,128]{1,0:T(8,128)S(1)}, u32[]{:S(2)}, u32[]{:S(2)}) collective-permute-start(f32[1056,128]{1,0:T(8,128)S(1)} %get-tuple-element.196), channel_id=1, source_target_pairs={{0,1},{1,0},{2,3},{3,2},{4,5},{5,4},{6,7},{7,6},{8,9},{9,8},{10,11... | collective-permute-start | bytes 1622024 | tf_op jit(solution)/shard_map/ppermute | solution.py:500
  18.1 13.3 %collective-permute-start.7 = (f32[264,128]{1,0:T(8,128)S(1)}, f32[264,128]{1,0:T(8,128)S(1)}, u32[]{:S(2)}, u32[]{:S(2)}) collective-permute-start(f32[264,128]{1,0:T(8,128)S(1)} %get-tuple-element.369), channel_id=1, source_target_pairs={{0,6},{1,7},{2,4},{3,5},{4,2},{5,3},{6,0},{7,1},{8,14},{9,15},{10,... | collective-permute-start | bytes 405512 | tf_op jit(solution)/shard_map/ppermute | solution.py:500
  21.1 10.3 %collective-permute-start.6 = (f32[264,128]{1,0:T(8,128)S(1)}, f32[264,128]{1,0:T(8,128)S(1)}, u32[]{:S(2)}, u32[]{:S(2)}) collective-permute-start(f32[264,128]{1,0:T(8,128)S(1)} %get-tuple-element.370), channel_id=1, source_target_pairs={{0,4},{1,5},{2,6},{3,7},{4,0},{5,1},{6,2},{7,3},{8,12},{9,13},{10,... | collective-permute-start | bytes 405512 | tf_op jit(solution)/shard_map/ppermute | solution.py:500
  22.3 9.1 %collective-permute-start.5 = (f32[264,128]{1,0:T(8,128)S(1)}, f32[264,128]{1,0:T(8,128)S(1)}, u32[]{:S(2)}, u32[]{:S(2)}) collective-permute-start(f32[264,128]{1,0:T(8,128)S(1)} %get-tuple-element.371), channel_id=1, source_target_pairs={{0,2},{1,3},{2,0},{3,1},{4,6},{5,7},{6,4},{7,5},{8,10},{9,11},{10,... | collective-permute-start | bytes 405512 | tf_op jit(solution)/shard_map/ppermute | solution.py:500
  22.6 9.7 %collective-permute-start.8 = (f32[264,128]{1,0:T(8,128)S(1)}, f32[264,128]{1,0:T(8,128)S(1)}, u32[]{:S(2)}, u32[]{:S(2)}) collective-permute-start(f32[264,128]{1,0:T(8,128)S(1)} %fusion.7), channel_id=1, source_target_pairs={{0,8},{1,9},{2,10},{3,11},{4,12},{5,13},{6,14},{7,15},{8,0},{9,1},... | collective-permute-start | bytes 405512 | tf_op jit(solution)/shard_map/ppermute | solution.py:500
  31.5 9.0 %collective-permute-start.9 = (f32[264,128]{1,0:T(8,128)S(1)}, f32[264,128]{1,0:T(8,128)S(1)}, u32[]{:S(2)}, u32[]{:S(2)}) collective-permute-start(f32[264,128]{1,0:T(8,128)S(1)} %fusion.5), channel_id=1, source_target_pairs={{0,8},{1,9},{2,10},{3,11},{4,12},{5,13},{6,14},{7,15},{8,0},{9,1},... | collective-permute-start | bytes 405512 | tf_op jit(solution)/shard_map/ppermute | solution.py:500
  32.3 9.8 %collective-permute-start.12 = (f32[264,128]{1,0:T(8,128)S(1)}, f32[264,128]{1,0:T(8,128)S(1)}, u32[]{:S(2)}, u32[]{:S(2)}) collective-permute-start(f32[264,128]{1,0:T(8,128)S(1)} %add.82), channel_id=1, source_target_pairs={{0,2},{1,3},{2,0},{3,1},{4,6},{5,7},{6,4},{7,5},{8,10},{9,11},{10,... | collective-permute-start | bytes 405512 | tf_op jit(solution)/shard_map/ppermute | solution.py:500
  33.5 10.6 %collective-permute-start.11 = (f32[264,128]{1,0:T(8,128)S(1)}, f32[264,128]{1,0:T(8,128)S(1)}, u32[]{:S(2)}, u32[]{:S(2)}) collective-permute-start(f32[264,128]{1,0:T(8,128)S(1)} %add.82), channel_id=1, source_target_pairs={{0,4},{1,5},{2,6},{3,7},{4,0},{5,1},{6,2},{7,3},{8,12},{9,13},{10,... | collective-permute-start | bytes 405512 | tf_op jit(solution)/shard_map/ppermute | solution.py:500
  35.1 10.0 %collective-permute-start.10 = (f32[264,128]{1,0:T(8,128)S(1)}, f32[264,128]{1,0:T(8,128)S(1)}, u32[]{:S(2)}, u32[]{:S(2)}) collective-permute-start(f32[264,128]{1,0:T(8,128)S(1)} %add.82), channel_id=1, source_target_pairs={{0,6},{1,7},{2,4},{3,5},{4,2},{5,3},{6,0},{7,1},{8,14},{9,15},{10,... | collective-permute-start | bytes 405512 | tf_op jit(solution)/shard_map/ppermute | solution.py:500
  40.5 10.4 %collective-permute-start.16 = (f32[264,128]{1,0:T(8,128)S(1)}, f32[264,128]{1,0:T(8,128)S(1)}, u32[]{:S(2)}, u32[]{:S(2)}) collective-permute-start(f32[264,128]{1,0:T(8,128)S(1)} %add.83), channel_id=1, source_target_pairs={{0,2},{1,3},{2,0},{3,1},{4,6},{5,7},{6,4},{7,5},{8,10},{9,11},{10,... | collective-permute-start | bytes 405512 | tf_op jit(solution)/shard_map/ppermute | solution.py:500
  41.8 9.1 %collective-permute-start.15 = (f32[264,128]{1,0:T(8,128)S(1)}, f32[264,128]{1,0:T(8,128)S(1)}, u32[]{:S(2)}, u32[]{:S(2)}) collective-permute-start(f32[264,128]{1,0:T(8,128)S(1)} %add.83), channel_id=1, source_target_pairs={{0,4},{1,5},{2,6},{3,7},{4,0},{5,1},{6,2},{7,3},{8,12},{9,13},{10,... | collective-permute-start | bytes 405512 | tf_op jit(solution)/shard_map/ppermute | solution.py:500
  42.2 8.7 %collective-permute-start.14 = (f32[264,128]{1,0:T(8,128)S(1)}, f32[264,128]{1,0:T(8,128)S(1)}, u32[]{:S(2)}, u32[]{:S(2)}) collective-permute-start(f32[264,128]{1,0:T(8,128)S(1)} %add.83), channel_id=1, source_target_pairs={{0,6},{1,7},{2,4},{3,5},{4,2},{5,3},{6,0},{7,1},{8,14},{9,15},{10,... | collective-permute-start | bytes 405512 | tf_op jit(solution)/shard_map/ppermute | solution.py:500
  59.3 4.2 %collective-permute-start.18 = (f32[1056,128]{1,0:T(8,128)S(1)}, f32[1056,128]{1,0:T(8,128)S(1)}, u32[]{:S(2)}, u32[]{:S(2)}) collective-permute-start(f32[1056,128]{1,0:T(8,128)S(1)} %get-tuple-element.292), channel_id=1, source_target_pairs={{0,1},{1,0},{2,3},{3,2},{4,5},{5,4},{6,7},{7,6},{8,9},{9,8},{10,11... | collective-permute-start | bytes 1622024 | tf_op jit(solution)/shard_map/ppermute | solution.py:500
  63.6 8.8 %collective-permute-start.22 = (f32[264,128]{1,0:T(8,128)S(1)}, f32[264,128]{1,0:T(8,128)S(1)}, u32[]{:S(2)}, u32[]{:S(2)}) collective-permute-start(f32[264,128]{1,0:T(8,128)S(1)} %get-tuple-element.366), channel_id=1, source_target_pairs={{0,2},{1,3},{2,0},{3,1},{4,6},{5,7},{6,4},{7,5},{8,10},{9,11},{10,... | collective-permute-start | bytes 405512 | tf_op jit(solution)/shard_map/ppermute | solution.py:500
  64.5 9.1 %collective-permute-start.21 = (f32[264,128]{1,0:T(8,128)S(1)}, f32[264,128]{1,0:T(8,128)S(1)}, u32[]{:S(2)}, u32[]{:S(2)}) collective-permute-start(f32[264,128]{1,0:T(8,128)S(1)} %get-tuple-element.367), channel_id=1, source_target_pairs={{0,4},{1,5},{2,6},{3,7},{4,0},{5,1},{6,2},{7,3},{8,12},{9,13},{10,... | collective-permute-start | bytes 405512 | tf_op jit(solution)/shard_map/ppermute | solution.py:500
  64.5 9.1 %collective-permute-start.20 = (f32[264,128]{1,0:T(8,128)S(1)}, f32[264,128]{1,0:T(8,128)S(1)}, u32[]{:S(2)}, u32[]{:S(2)}) collective-permute-start(f32[264,128]{1,0:T(8,128)S(1)} %get-tuple-element.368), channel_id=1, source_target_pairs={{0,6},{1,7},{2,4},{3,5},{4,2},{5,3},{6,0},{7,1},{8,14},{9,15},{10,... | collective-permute-start | bytes 405512 | tf_op jit(solution)/shard_map/ppermute | solution.py:500
  67.1 2.5 %collective-permute-start.19 = (f32[1056,128]{1,0:T(8,128)S(1)}, f32[1056,128]{1,0:T(8,128)S(1)}, u32[]{:S(2)}, u32[]{:S(2)}) collective-permute-start(f32[1056,128]{1,0:T(8,128)S(1)} %get-tuple-element.298), channel_id=1, source_target_pairs={{0,1},{1,0},{2,3},{3,2},{4,5},{5,4},{6,7},{7,6},{8,9},{9,8},{10,11... | collective-permute-start | bytes 1622024 | tf_op jit(solution)/shard_map/ppermute | solution.py:500
  69.7 11.1 %collective-permute-start.25 = (f32[264,128]{1,0:T(8,128)S(1)}, f32[264,128]{1,0:T(8,128)S(1)}, u32[]{:S(2)}, u32[]{:S(2)}) collective-permute-start(f32[264,128]{1,0:T(8,128)S(1)} %get-tuple-element.363), channel_id=1, source_target_pairs={{0,6},{1,7},{2,4},{3,5},{4,2},{5,3},{6,0},{7,1},{8,14},{9,15},{10,... | collective-permute-start | bytes 405512 | tf_op jit(solution)/shard_map/ppermute | solution.py:500
  70.1 11.8 %collective-permute-start.24 = (f32[264,128]{1,0:T(8,128)S(1)}, f32[264,128]{1,0:T(8,128)S(1)}, u32[]{:S(2)}, u32[]{:S(2)}) collective-permute-start(f32[264,128]{1,0:T(8,128)S(1)} %get-tuple-element.364), channel_id=1, source_target_pairs={{0,4},{1,5},{2,6},{3,7},{4,0},{5,1},{6,2},{7,3},{8,12},{9,13},{10,... | collective-permute-start | bytes 405512 | tf_op jit(solution)/shard_map/ppermute | solution.py:500
  72.3 9.5 %collective-permute-start.23 = (f32[264,128]{1,0:T(8,128)S(1)}, f32[264,128]{1,0:T(8,128)S(1)}, u32[]{:S(2)}, u32[]{:S(2)}) collective-permute-start(f32[264,128]{1,0:T(8,128)S(1)} %get-tuple-element.365), channel_id=1, source_target_pairs={{0,2},{1,3},{2,0},{3,1},{4,6},{5,7},{6,4},{7,5},{8,10},{9,11},{10,... | collective-permute-start | bytes 405512 | tf_op jit(solution)/shard_map/ppermute | solution.py:500
  73.6 8.5 %collective-permute-start.26 = (f32[264,128]{1,0:T(8,128)S(1)}, f32[264,128]{1,0:T(8,128)S(1)}, u32[]{:S(2)}, u32[]{:S(2)}) collective-permute-start(f32[264,128]{1,0:T(8,128)S(1)} %fusion.1), channel_id=1, source_target_pairs={{0,8},{1,9},{2,10},{3,11},{4,12},{5,13},{6,14},{7,15},{8,0},{9,1},... | collective-permute-start | bytes 405512 | tf_op jit(solution)/shard_map/ppermute | solution.py:500
  81.9 8.8 %collective-permute-start.27 = (f32[264,128]{1,0:T(8,128)S(1)}, f32[264,128]{1,0:T(8,128)S(1)}, u32[]{:S(2)}, u32[]{:S(2)}) collective-permute-start(f32[264,128]{1,0:T(8,128)S(1)} %fusion.3), channel_id=1, source_target_pairs={{0,8},{1,9},{2,10},{3,11},{4,12},{5,13},{6,14},{7,15},{8,0},{9,1},... | collective-permute-start | bytes 405512 | tf_op jit(solution)/shard_map/ppermute | solution.py:500
  82.2 10.0 %collective-permute-start.30 = (f32[264,128]{1,0:T(8,128)S(1)}, f32[264,128]{1,0:T(8,128)S(1)}, u32[]{:S(2)}, u32[]{:S(2)}) collective-permute-start(f32[264,128]{1,0:T(8,128)S(1)} %add.93), channel_id=1, source_target_pairs={{0,2},{1,3},{2,0},{3,1},{4,6},{5,7},{6,4},{7,5},{8,10},{9,11},{10,... | collective-permute-start | bytes 405512 | tf_op jit(solution)/shard_map/ppermute | solution.py:500
  83.2 11.1 %collective-permute-start.29 = (f32[264,128]{1,0:T(8,128)S(1)}, f32[264,128]{1,0:T(8,128)S(1)}, u32[]{:S(2)}, u32[]{:S(2)}) collective-permute-start(f32[264,128]{1,0:T(8,128)S(1)} %add.93), channel_id=1, source_target_pairs={{0,4},{1,5},{2,6},{3,7},{4,0},{5,1},{6,2},{7,3},{8,12},{9,13},{10,... | collective-permute-start | bytes 405512 | tf_op jit(solution)/shard_map/ppermute | solution.py:500
  86.4 8.2 %collective-permute-start.28 = (f32[264,128]{1,0:T(8,128)S(1)}, f32[264,128]{1,0:T(8,128)S(1)}, u32[]{:S(2)}, u32[]{:S(2)}) collective-permute-start(f32[264,128]{1,0:T(8,128)S(1)} %add.93), channel_id=1, source_target_pairs={{0,6},{1,7},{2,4},{3,5},{4,2},{5,3},{6,0},{7,1},{8,14},{9,15},{10,... | collective-permute-start | bytes 405512 | tf_op jit(solution)/shard_map/ppermute | solution.py:500
  90.8 8.1 %collective-permute-start.34 = (f32[264,128]{1,0:T(8,128)S(1)}, f32[264,128]{1,0:T(8,128)S(1)}, u32[]{:S(2)}, u32[]{:S(2)}) collective-permute-start(f32[264,128]{1,0:T(8,128)S(1)} %add.92), channel_id=1, source_target_pairs={{0,2},{1,3},{2,0},{3,1},{4,6},{5,7},{6,4},{7,5},{8,10},{9,11},{10,... | collective-permute-start | bytes 405512 | tf_op jit(solution)/shard_map/ppermute | solution.py:500
  92.2 6.6 %collective-permute-start.33 = (f32[264,128]{1,0:T(8,128)S(1)}, f32[264,128]{1,0:T(8,128)S(1)}, u32[]{:S(2)}, u32[]{:S(2)}) collective-permute-start(f32[264,128]{1,0:T(8,128)S(1)} %add.92), channel_id=1, source_target_pairs={{0,4},{1,5},{2,6},{3,7},{4,0},{5,1},{6,2},{7,3},{8,12},{9,13},{10,... | collective-permute-start | bytes 405512 | tf_op jit(solution)/shard_map/ppermute | solution.py:500
  92.2 8.2 %collective-permute-start.32 = (f32[264,128]{1,0:T(8,128)S(1)}, f32[264,128]{1,0:T(8,128)S(1)}, u32[]{:S(2)}, u32[]{:S(2)}) collective-permute-start(f32[264,128]{1,0:T(8,128)S(1)} %add.92), channel_id=1, source_target_pairs={{0,6},{1,7},{2,4},{3,5},{4,2},{5,3},{6,0},{7,1},{8,14},{9,15},{10,... | collective-permute-start | bytes 405512 | tf_op jit(solution)/shard_map/ppermute | solution.py:500
  (10 other events, 62.4 us)

commit v15 on v14

--- a/solution.py
+++ b/solution.py
@@ -564,12 +564,12 @@
     got_a = a.gather_plane()
     b.own(close(env, *got_b))
 
-    got_b = b.gather_plane()
+    got_b = b.gather_plane()[::-1]
     got_a = a.gather_core(close(env, *got_a))
     work()
     (got_a,) = close(env, got_a)
     late[0](env, [a.mine, got_a])
-    got_b = b.gather_core(close(env, *got_b))
+    got_b = b.gather_core(close(env, *got_b)[::-1])
     late[1](env)
     (got_b,) = close(env, got_b)
     return [b.mine, got_b]

time: 108 us -> 108 us (level)
  waiting for transfers between devices: 12.9 us -> 14.6 us
  starting transfers between devices: 38.9 us -> 37.5 us
    ppermute x36, waiting for transfers between devices: 12.9 us -> 14.6 us  [swap(): return lax.ppermute(x, 'row', [(i, i ^ offset) for i in range(self.count)])]
    ppermute x36, starting transfers between devices: 38.9 us -> 37.5 us  [swap(): return lax.ppermute(x, 'row', [(i, i ^ offset) for i in range(self.count)])]
  transfers between devices with their start and end apart: 36 -> 36, of which waited for: 9 -> 10; matrix products, arithmetic and copies ran while one was open for 0% -> 0% of each run, Pallas kernels for 34% -> 34%
where the time goes in v15:
time: 108 us
  Pallas kernels  54.3 us (50%)
  starting transfers between devices  37.5 us (35%)
  waiting for transfers between devices  14.6 us (14%)
    ppermute x36, starting transfers between devices, swap(): return lax.ppermute(x, 'row', [(i, i ^ offset) for i in range(self.count)])  37.5 us
    ppermute x36, waiting for transfers between devices, swap(): return lax.ppermute(x, 'row', [(i, i ^ offset) for i in range(self.count)])  14.6 us
    pallas_call x2, Pallas kernels, affine(): call(functools.partial(affine_kernel, part), 'affine', struct(height, siz...  8.39 us
    pallas_call x2, Pallas kernels, affine_parts(): call(functools.partial(affine_parts_kernel, part), 'affine_parts', struct...  7.86 us
    pallas_call x1, Pallas kernels, first_gram(): call(functools.partial(first_gram_kernel, shards), 'first_gram', halves(s...  6.9 us
    pallas_call x1, Pallas kernels, second_gram(): call(functools.partial(second_gram_kernel, shards, len(pieces)), 'second_...  6.15 us
    pallas_call x2, Pallas kernels, first_part(): call(functools.partial(first_part_kernel, shards, len(pieces), columns),...  5.92 us
    pallas_call x1, Pallas kernels, last_step(): call(functools.partial(last_kernel, shards, len(pieces)), 'last', struct(...  4.89 us
  transfers between devices with their start and end apart: 36, of which 10 were waited for; matrix products, arithmetic and copies ran while one was open for 0% of the time, Pallas kernels for 34%

profile of v15, /device:TPU:0, one launch (start us, length us, event | category | flops | bytes accessed | tf_op | source)
XLA Modules:
  0.0 107.8 jit_solution(13094058982718344820)
XLA Ops:
  0.0 6.9 %first_gram.1 = (f32[1056,128]{1,0:T(8,128)S(1)}, f32[1056,128]{1,0:T(8,128)S(1)}, bf16[1024,1024]{1,0:T(8,128)(2,1)S(1)}, bf16[1024,1024]{1,0:T(8,128)(2,1)S(1)...) custom-call(s32[1]{0:T(128)} %bitcast.me_ref, f32[1024,1024]{1,0:T(8,128)} %x_ref, f32[1024,1024]{1,0:T(8,128)} %a_ref.1), custom_call_target="tpu_custom_call" | custom-call | flops 32212254720 | bytes 167772160 | tf_op jit(solution)/shard_map/first_gram/pallas_call | solution.py:198
  7.4 3.6 %other_gram.1 = (f32[1056,128]{1,0:T(8,128)S(1)}, f32[1056,128]{1,0:T(8,128)S(1)}) custom-call(s32[1]{0:T(128)} %bitcast.me_ref, bf16[1024,1024]{1,0:T(8,128)(2,1)S(1)} %get-tuple-element.184.ah, bf16[1024,1024]{1,0:T(8,128)(2,1)S(1)} %get-tuple-element.185.al, bf16[1024,1024]{1,0:T(8,128)(2,1)S(1)} %get-tuple-element.186.bh, ...), custom_call_target="tpu_custom_call" | custom-call | flops 32212254720 | bytes 83886080 | tf_op jit(solution)/shard_map/other_gram/pallas_call | solution.py:228
  11.2 2.6 %collective-permute-start.4 = (f32[264,128]{1,0:T(8,128)S(1)}, f32[264,128]{1,0:T(8,128)S(1)}, u32[]{:S(2)}, u32[]{:S(2)}) collective-permute-start(f32[264,128]{1,0:T(8,128)S(1)} %get-tuple-element.372), channel_id=1, source_target_pairs={{0,2},{1,3},{2,0},{3,1},{4,6},{5,7},{6,4},{7,5},{8,10},{9,11},{10,... | collective-permute-start | bytes 405512 | tf_op jit(solution)/shard_map/ppermute | solution.py:500
  13.8 1.6 %collective-permute-start.3 = (f32[264,128]{1,0:T(8,128)S(1)}, f32[264,128]{1,0:T(8,128)S(1)}, u32[]{:S(2)}, u32[]{:S(2)}) collective-permute-start(f32[264,128]{1,0:T(8,128)S(1)} %get-tuple-element.373), channel_id=1, source_target_pairs={{0,4},{1,5},{2,6},{3,7},{4,0},{5,1},{6,2},{7,3},{8,12},{9,13},{10,... | collective-permute-start | bytes 405512 | tf_op jit(solution)/shard_map/ppermute | solution.py:500
  15.4 2.6 %affine.2.refs_4_ = f32[256,1024]{1,0:T(8,128)S(1)} custom-call(f32[1024,1024]{1,0:T(8,128)S(1)} %copy-done.1, f32[1024,1024]{1,0:T(8,128)S(1)} %copy-done.2), custom_call_target="tpu_custom_call" | custom-call | flops 16106127360 | bytes 83886080 | tf_op jit(solution)/shard_map/affine/pallas_call | solution.py:261
  18.1 3.0 %collective-permute-start.7 = (f32[264,128]{1,0:T(8,128)S(1)}, f32[264,128]{1,0:T(8,128)S(1)}, u32[]{:S(2)}, u32[]{:S(2)}) collective-permute-start(f32[264,128]{1,0:T(8,128)S(1)} %get-tuple-element.369), channel_id=1, source_target_pairs={{0,6},{1,7},{2,4},{3,5},{4,2},{5,3},{6,0},{7,1},{8,14},{9,15},{10,... | collective-permute-start | bytes 405512 | tf_op jit(solution)/shard_map/ppermute | solution.py:500
  22.6 3.0 %collective-permute-start.8 = (f32[264,128]{1,0:T(8,128)S(1)}, f32[264,128]{1,0:T(8,128)S(1)}, u32[]{:S(2)}, u32[]{:S(2)}) collective-permute-start(f32[264,128]{1,0:T(8,128)S(1)} %fusion.7), channel_id=1, source_target_pairs={{0,8},{1,9},{2,10},{3,11},{4,12},{5,13},{6,14},{7,15},{8,0},{9,1},... | collective-permute-start | bytes 405512 | tf_op jit(solution)/shard_map/ppermute | solution.py:500
  25.6 5.8 %affine.3.refs_5_ = f32[768,1024]{1,0:T(8,128)S(1)} custom-call(f32[1024,1024]{1,0:T(8,128)S(1)} %copy-done.1, f32[1024,1024]{1,0:T(8,128)S(1)} %copy-done.2), custom_call_target="tpu_custom_call" | custom-call | flops 48318382080 | bytes 83886080 | tf_op jit(solution)/shard_map/affine/pallas_call | solution.py:261
  32.3 1.2 %collective-permute-start.12 = (f32[264,128]{1,0:T(8,128)S(1)}, f32[264,128]{1,0:T(8,128)S(1)}, u32[]{:S(2)}, u32[]{:S(2)}) collective-permute-start(f32[264,128]{1,0:T(8,128)S(1)} %add.82), channel_id=1, source_target_pairs={{0,2},{1,3},{2,0},{3,1},{4,6},{5,7},{6,4},{7,5},{8,10},{9,11},{10,... | collective-permute-start | bytes 405512 | tf_op jit(solution)/shard_map/ppermute | solution.py:500
  33.5 1.5 %collective-permute-start.11 = (f32[264,128]{1,0:T(8,128)S(1)}, f32[264,128]{1,0:T(8,128)S(1)}, u32[]{:S(2)}, u32[]{:S(2)}) collective-permute-start(f32[264,128]{1,0:T(8,128)S(1)} %add.82), channel_id=1, source_target_pairs={{0,4},{1,5},{2,6},{3,7},{4,0},{5,1},{6,2},{7,3},{8,12},{9,13},{10,... | collective-permute-start | bytes 405512 | tf_op jit(solution)/shard_map/ppermute | solution.py:500
  35.1 1.3 %collective-permute-start.10 = (f32[264,128]{1,0:T(8,128)S(1)}, f32[264,128]{1,0:T(8,128)S(1)}, u32[]{:S(2)}, u32[]{:S(2)}) collective-permute-start(f32[264,128]{1,0:T(8,128)S(1)} %add.82), channel_id=1, source_target_pairs={{0,6},{1,7},{2,4},{3,5},{4,2},{5,3},{6,0},{7,1},{8,14},{9,15},{10,... | collective-permute-start | bytes 405512 | tf_op jit(solution)/shard_map/ppermute | solution.py:500
  36.3 4.2 %collective-permute-done.9 = f32[264,128]{1,0:T(8,128)S(1)} collective-permute-done((f32[264,128]{1,0:T(8,128)S(1)}, f32[264,128]{1,0:T(8,128)S(1)}, u32[]{:S(2)}, u32[]{:S(2)}) %collective-permute-start.9) | collective-permute-done | bytes 135200 | tf_op jit(solution)/shard_map/ppermute | solution.py:500
  41.6 1.7 %collective-permute-start.15 = (f32[264,128]{1,0:T(8,128)S(1)}, f32[264,128]{1,0:T(8,128)S(1)}, u32[]{:S(2)}, u32[]{:S(2)}) collective-permute-start(f32[264,128]{1,0:T(8,128)S(1)} %add.83), channel_id=1, source_target_pairs={{0,4},{1,5},{2,6},{3,7},{4,0},{5,1},{6,2},{7,3},{8,12},{9,13},{10,... | collective-permute-start | bytes 405512 | tf_op jit(solution)/shard_map/ppermute | solution.py:500
  44.1 1.4 %collective-permute-done.10 = f32[264,128]{1,0:T(8,128)S(1)} collective-permute-done((f32[264,128]{1,0:T(8,128)S(1)}, f32[264,128]{1,0:T(8,128)S(1)}, u32[]{:S(2)}, u32[]{:S(2)}) %collective-permute-start.10) | collective-permute-done | bytes 135200 | tf_op jit(solution)/shard_map/ppermute | solution.py:500
  45.6 1.7 %turn.1 = (bf16[1024,1024]{1,0:T(8,128)(2,1)S(1)}, bf16[1024,1024]{1,0:T(8,128)(2,1)S(1)}) custom-call(f32[1024,1024]{1,0:T(8,128)S(1)} %copy-done.4), custom_call_target="tpu_custom_call" | custom-call | flops 6442450944 | bytes 83886080 | tf_op jit(solution)/shard_map/turn/pallas_call | solution.py:382
  47.5 3.8 %first_part.2.mid_ref.refs_4_ = f32[1024,1024]{1,0:T(8,128)S(1)} custom-call(s32[1]{0:T(128)} %bitcast.me_ref, f32[1056,128]{1,0:T(8,128)S(1)} %pad_maximum_fusion.refs_0_, f32[1056,128]{1,0:T(8,128)S(1)} %collective-permute-done.13.refs_1_, bf16[1024,1024]{1,0:T(8,128)(2,1)S(1)} %get-tuple-element.281.refs_2_, ...), custom_call_target="tpu_custom_call" | custom-call | flops 32212254720 | bytes 125829120 | tf_op jit(solution)/shard_map/first_part/pallas_call | solution.py:336
  51.7 1.8 %column_product.1.refs_7_ = f32[1024,256]{1,0:T(8,128)S(1)} custom-call(bf16[1024,1024]{1,0:T(8,128)(2,1)S(1)} %get-tuple-element.283.xh.refs_5_, bf16[1024,1024]{1,0:T(8,128)(2,1)S(1)} %get-tuple-element.284.xl.refs_6_, f32[1024,1024]{1,0:T(8,128)S(1)} %first_part.2.mid_ref.refs_4_), custom_call_target="tpu_custom_call" | custom-call | flops 16106127360 | bytes 83886080 | tf_op jit(solution)/shard_map/column_product/pallas_call | solution.py:367
  53.5 6.1 %second_gram.1 = (f32[1056,128]{1,0:T(8,128)S(1)}, f32[1056,128]{1,0:T(8,128)S(1)}, bf16[1024,1024]{1,0:T(8,128)(2,1)S(1)}, bf16[1024,1024]{1,0:T(8,128)(2,1)S(1)}) custom-call(s32[1]{0:T(128)} %bitcast.me_ref, f32[1056,128]{1,0:T(8,128)S(1)} %pad_maximum_fusion.1.refs_0_, f32[1056,128]{1,0:T(8,128)S(1)} %collective-permute-done.17.refs_1_, ...), custom_call_target="tpu_custom_call" | custom-call | flops 51539607552 | bytes 209715200 | tf_op jit(solution)/shard_map/second_gram/pallas_call | solution.py:425
  60.0 3.9 %fourth_gram.1 = (f32[1056,128]{1,0:T(8,128)S(1)}, f32[1056,128]{1,0:T(8,128)S(1)}) custom-call(s32[1]{0:T(128)} %bitcast.me_ref, bf16[1024,1024]{1,0:T(8,128)(2,1)S(1)} %get-tuple-element.283.xh.refs_5_, bf16[1024,1024]{1,0:T(8,128)(2,1)S(1)} %get-tuple-element.284.xl.refs_6_, bf16[1024,1024]{1,0:T(8,128)(2,1)S(1)} %get-tuple-element.309.mh.ah, ...), custom_call_target="tpu_custom_call" | custom-call | flops 32212254720 | bytes 83886080 | tf_op jit(solution)/shard_map/fourth_gram/pallas_call | solution.py:442
  64.6 2.9 %collective-permute-start.20 = (f32[264,128]{1,0:T(8,128)S(1)}, f32[264,128]{1,0:T(8,128)S(1)}, u32[]{:S(2)}, u32[]{:S(2)}) collective-permute-start(f32[264,128]{1,0:T(8,128)S(1)} %get-tuple-element.368), channel_id=1, source_target_pairs={{0,6},{1,7},{2,4},{3,5},{4,2},{5,3},{6,0},{7,1},{8,14},{9,15},{10,... | collective-permute-start | bytes 405512 | tf_op jit(solution)/shard_map/ppermute | solution.py:500
  67.5 2.5 %affine_parts.2.refs_4_.refs_0_ = f32[256,1024]{1,0:T(8,128)S(1)} custom-call(bf16[1024,1024]{1,0:T(8,128)(2,1)S(1)} %get-tuple-element.309.mh.ah, bf16[1024,1024]{1,0:T(8,128)(2,1)S(1)} %get-tuple-element.310.ml.al, f32[1024,1024]{1,0:T(8,128)S(1)} %copy-done.3), custom_call_target="tpu_custom_call" | custom-call | flops 16106127360 | bytes 83886080 | tf_op jit(solution)/shard_map/affine_parts/pallas_call | solution.py:283
  70.2 2.0 %collective-permute-start.24 = (f32[264,128]{1,0:T(8,128)S(1)}, f32[264,128]{1,0:T(8,128)S(1)}, u32[]{:S(2)}, u32[]{:S(2)}) collective-permute-start(f32[264,128]{1,0:T(8,128)S(1)} %get-tuple-element.364), channel_id=1, source_target_pairs={{0,4},{1,5},{2,6},{3,7},{4,0},{5,1},{6,2},{7,3},{8,12},{9,13},{10,... | collective-permute-start | bytes 405512 | tf_op jit(solution)/shard_map/ppermute | solution.py:500
  72.4 1.5 %collective-permute-start.23 = (f32[264,128]{1,0:T(8,128)S(1)}, f32[264,128]{1,0:T(8,128)S(1)}, u32[]{:S(2)}, u32[]{:S(2)}) collective-permute-start(f32[264,128]{1,0:T(8,128)S(1)} %get-tuple-element.365), channel_id=1, source_target_pairs={{0,2},{1,3},{2,0},{3,1},{4,6},{5,7},{6,4},{7,5},{8,10},{9,11},{10,... | collective-permute-start | bytes 405512 | tf_op jit(solution)/shard_map/ppermute | solution.py:500
  74.0 1.9 %collective-permute-start.26 = (f32[264,128]{1,0:T(8,128)S(1)}, f32[264,128]{1,0:T(8,128)S(1)}, u32[]{:S(2)}, u32[]{:S(2)}) collective-permute-start(f32[264,128]{1,0:T(8,128)S(1)} %fusion.1), channel_id=1, source_target_pairs={{0,8},{1,9},{2,10},{3,11},{4,12},{5,13},{6,14},{7,15},{8,0},{9,1},... | collective-permute-start | bytes 405512 | tf_op jit(solution)/shard_map/ppermute | solution.py:500
  76.0 5.4 %affine_parts.3.refs_5_.refs_1_ = f32[768,1024]{1,0:T(8,128)S(1)} custom-call(bf16[1024,1024]{1,0:T(8,128)(2,1)S(1)} %get-tuple-element.309.mh.ah, bf16[1024,1024]{1,0:T(8,128)(2,1)S(1)} %get-tuple-element.310.ml.al, f32[1024,1024]{1,0:T(8,128)S(1)} %copy-done.3), custom_call_target="tpu_custom_call" | custom-call | flops 48318382080 | bytes 83886080 | tf_op jit(solution)/shard_map/affine_parts/pallas_call | solution.py:283
  83.6 1.7 %collective-permute-start.29 = (f32[264,128]{1,0:T(8,128)S(1)}, f32[264,128]{1,0:T(8,128)S(1)}, u32[]{:S(2)}, u32[]{:S(2)}) collective-permute-start(f32[264,128]{1,0:T(8,128)S(1)} %add.93), channel_id=1, source_target_pairs={{0,4},{1,5},{2,6},{3,7},{4,0},{5,1},{6,2},{7,3},{8,12},{9,13},{10,... | collective-permute-start | bytes 405512 | tf_op jit(solution)/shard_map/ppermute | solution.py:500
  86.3 4.7 %collective-permute-done.27 = f32[264,128]{1,0:T(8,128)S(1)} collective-permute-done((f32[264,128]{1,0:T(8,128)S(1)}, f32[264,128]{1,0:T(8,128)S(1)}, u32[]{:S(2)}, u32[]{:S(2)}) %collective-permute-start.27) | collective-permute-done | bytes 135200 | tf_op jit(solution)/shard_map/ppermute | solution.py:500
  91.3 2.7 %collective-permute-start.33 = (f32[264,128]{1,0:T(8,128)S(1)}, f32[264,128]{1,0:T(8,128)S(1)}, u32[]{:S(2)}, u32[]{:S(2)}) collective-permute-start(f32[264,128]{1,0:T(8,128)S(1)} %add.92), channel_id=1, source_target_pairs={{0,4},{1,5},{2,6},{3,7},{4,0},{5,1},{6,2},{7,3},{8,12},{9,13},{10,... | collective-permute-start | bytes 405512 | tf_op jit(solution)/shard_map/ppermute | solution.py:500
  95.7 1.5 %collective-permute-done.31.refs_1_ = f32[1056,128]{1,0:T(8,128)S(1)} collective-permute-done((f32[1056,128]{1,0:T(8,128)S(1)}, f32[1056,128]{1,0:T(8,128)S(1)}, u32[]{:S(2)}, u32[]{:S(2)}) %collective-permute-start.31) | collective-permute-done | bytes 540704 | tf_op jit(solution)/shard_map/ppermute | solution.py:500
  97.1 2.2 %first_part.3 = (f32[1024,256]{1,0:T(8,128)S(1)}, bf16[1024,1024]{1,0:T(8,128)(2,1)S(1)}, bf16[1024,1024]{1,0:T(8,128)(2,1)S(1)}) custom-call(s32[1]{0:T(128)} %bitcast.me_ref, f32[1056,128]{1,0:T(8,128)S(1)} %pad_maximum_fusion.2.refs_0_, f32[1056,128]{1,0:T(8,128)S(1)} %collective-permute-done.31.refs_1_, bf16[1024,1024]{1,0:T(8,128)(2,1)S(1)} %cut.4.refs_2_.ah, ...), custom_call_target="tpu_custom_call" | custom-call | flops 32212254720 | bytes 125829120 | tf_op jit(solution)/shard_map/first_part/pallas_call | solution.py:336
  100.8 1.8 %other_part.1.refs_5_ = f32[1024,768]{1,0:T(8,128)S(1)} custom-call(bf16[1024,1024]{1,0:T(8,128)(2,1)S(1)} %cut.4.refs_2_.ah, bf16[1024,1024]{1,0:T(8,128)(2,1)S(1)} %cut.5.refs_3_.al, bf16[1024,1024]{1,0:T(8,128)(2,1)S(1)} %get-tuple-element.356.hi, bf16[1024,1024]{1,0:T(8,128)(2,1)S(1)} %get-tuple-element.357.lo, ...), custom_call_target="tpu_custom_call" | custom-call | flops 16106127360 | bytes 125829120 | tf_op jit(solution)/shard_map/other_part/pallas_call | solution.py:351
  102.7 4.9 %last.1 = f32[1024,1024]{1,0:T(8,128)} custom-call(s32[1]{0:T(128)} %bitcast.me_ref, f32[1056,128]{1,0:T(8,128)S(1)} %pad_maximum_fusion.3.refs_0_, f32[1056,128]{1,0:T(8,128)S(1)} %collective-permute-done.35.refs_1_, bf16[1024,1024]{1,0:T(8,128)(2,1)S(1)} %cut.4.refs_2_.ah, bf16[1024,1024]{1,0:T(8,128)(2,1)S(1)} %cut.5.refs_3_.al, ...), custom_call_target="tpu_custom_call" | custom-call | flops 32212254720 | bytes 125829120 | tf_op jit(solution)/shard_map/last/pallas_call | solution.py:477
  (89 shorter events, 13.9 us)
Async XLA Ops:
  6.9 4.2 %collective-permute-start = (f32[1056,128]{1,0:T(8,128)S(1)}, f32[1056,128]{1,0:T(8,128)S(1)}, u32[]{:S(2)}, u32[]{:S(2)}) collective-permute-start(f32[1056,128]{1,0:T(8,128)S(1)} %get-tuple-element.190), channel_id=1, source_target_pairs={{0,1},{1,0},{2,3},{3,2},{4,5},{5,4},{6,7},{7,6},{8,9},{9,8},{10,11... | collective-permute-start | bytes 1622024 | tf_op jit(solution)/shard_map/ppermute | solution.py:500
  11.2 11.1 %collective-permute-start.4 = (f32[264,128]{1,0:T(8,128)S(1)}, f32[264,128]{1,0:T(8,128)S(1)}, u32[]{:S(2)}, u32[]{:S(2)}) collective-permute-start(f32[264,128]{1,0:T(8,128)S(1)} %get-tuple-element.372), channel_id=1, source_target_pairs={{0,2},{1,3},{2,0},{3,1},{4,6},{5,7},{6,4},{7,5},{8,10},{9,11},{10,... | collective-permute-start | bytes 405512 | tf_op jit(solution)/shard_map/ppermute | solution.py:500
  13.8 8.7 %collective-permute-start.3 = (f32[264,128]{1,0:T(8,128)S(1)}, f32[264,128]{1,0:T(8,128)S(1)}, u32[]{:S(2)}, u32[]{:S(2)}) collective-permute-start(f32[264,128]{1,0:T(8,128)S(1)} %get-tuple-element.373), channel_id=1, source_target_pairs={{0,4},{1,5},{2,6},{3,7},{4,0},{5,1},{6,2},{7,3},{8,12},{9,13},{10,... | collective-permute-start | bytes 405512 | tf_op jit(solution)/shard_map/ppermute | solution.py:500
  15.4 7.2 %collective-permute-start.2 = (f32[264,128]{1,0:T(8,128)S(1)}, f32[264,128]{1,0:T(8,128)S(1)}, u32[]{:S(2)}, u32[]{:S(2)}) collective-permute-start(f32[264,128]{1,0:T(8,128)S(1)} %get-tuple-element.374), channel_id=1, source_target_pairs={{0,6},{1,7},{2,4},{3,5},{4,2},{5,3},{6,0},{7,1},{8,14},{9,15},{10,... | collective-permute-start | bytes 405512 | tf_op jit(solution)/shard_map/ppermute | solution.py:500
  15.4 2.6 %collective-permute-start.1 = (f32[1056,128]{1,0:T(8,128)S(1)}, f32[1056,128]{1,0:T(8,128)S(1)}, u32[]{:S(2)}, u32[]{:S(2)}) collective-permute-start(f32[1056,128]{1,0:T(8,128)S(1)} %get-tuple-element.196), channel_id=1, source_target_pairs={{0,1},{1,0},{2,3},{3,2},{4,5},{5,4},{6,7},{7,6},{8,9},{9,8},{10,11... | collective-permute-start | bytes 1622024 | tf_op jit(solution)/shard_map/ppermute | solution.py:500
  18.1 13.3 %collective-permute-start.7 = (f32[264,128]{1,0:T(8,128)S(1)}, f32[264,128]{1,0:T(8,128)S(1)}, u32[]{:S(2)}, u32[]{:S(2)}) collective-permute-start(f32[264,128]{1,0:T(8,128)S(1)} %get-tuple-element.369), channel_id=1, source_target_pairs={{0,6},{1,7},{2,4},{3,5},{4,2},{5,3},{6,0},{7,1},{8,14},{9,15},{10,... | collective-permute-start | bytes 405512 | tf_op jit(solution)/shard_map/ppermute | solution.py:500
  21.1 10.3 %collective-permute-start.6 = (f32[264,128]{1,0:T(8,128)S(1)}, f32[264,128]{1,0:T(8,128)S(1)}, u32[]{:S(2)}, u32[]{:S(2)}) collective-permute-start(f32[264,128]{1,0:T(8,128)S(1)} %get-tuple-element.370), channel_id=1, source_target_pairs={{0,4},{1,5},{2,6},{3,7},{4,0},{5,1},{6,2},{7,3},{8,12},{9,13},{10,... | collective-permute-start | bytes 405512 | tf_op jit(solution)/shard_map/ppermute | solution.py:500
  22.3 9.1 %collective-permute-start.5 = (f32[264,128]{1,0:T(8,128)S(1)}, f32[264,128]{1,0:T(8,128)S(1)}, u32[]{:S(2)}, u32[]{:S(2)}) collective-permute-start(f32[264,128]{1,0:T(8,128)S(1)} %get-tuple-element.371), channel_id=1, source_target_pairs={{0,2},{1,3},{2,0},{3,1},{4,6},{5,7},{6,4},{7,5},{8,10},{9,11},{10,... | collective-permute-start | bytes 405512 | tf_op jit(solution)/shard_map/ppermute | solution.py:500
  22.6 9.7 %collective-permute-start.8 = (f32[264,128]{1,0:T(8,128)S(1)}, f32[264,128]{1,0:T(8,128)S(1)}, u32[]{:S(2)}, u32[]{:S(2)}) collective-permute-start(f32[264,128]{1,0:T(8,128)S(1)} %fusion.7), channel_id=1, source_target_pairs={{0,8},{1,9},{2,10},{3,11},{4,12},{5,13},{6,14},{7,15},{8,0},{9,1},... | collective-permute-start | bytes 405512 | tf_op jit(solution)/shard_map/ppermute | solution.py:500
  31.5 9.0 %collective-permute-start.9 = (f32[264,128]{1,0:T(8,128)S(1)}, f32[264,128]{1,0:T(8,128)S(1)}, u32[]{:S(2)}, u32[]{:S(2)}) collective-permute-start(f32[264,128]{1,0:T(8,128)S(1)} %fusion.5), channel_id=1, source_target_pairs={{0,8},{1,9},{2,10},{3,11},{4,12},{5,13},{6,14},{7,15},{8,0},{9,1},... | collective-permute-start | bytes 405512 | tf_op jit(solution)/shard_map/ppermute | solution.py:500
  32.3 11.0 %collective-permute-start.12 = (f32[264,128]{1,0:T(8,128)S(1)}, f32[264,128]{1,0:T(8,128)S(1)}, u32[]{:S(2)}, u32[]{:S(2)}) collective-permute-start(f32[264,128]{1,0:T(8,128)S(1)} %add.82), channel_id=1, source_target_pairs={{0,2},{1,3},{2,0},{3,1},{4,6},{5,7},{6,4},{7,5},{8,10},{9,11},{10,... | collective-permute-start | bytes 405512 | tf_op jit(solution)/shard_map/ppermute | solution.py:500
  33.5 10.6 %collective-permute-start.11 = (f32[264,128]{1,0:T(8,128)S(1)}, f32[264,128]{1,0:T(8,128)S(1)}, u32[]{:S(2)}, u32[]{:S(2)}) collective-permute-start(f32[264,128]{1,0:T(8,128)S(1)} %add.82), channel_id=1, source_target_pairs={{0,4},{1,5},{2,6},{3,7},{4,0},{5,1},{6,2},{7,3},{8,12},{9,13},{10,... | collective-permute-start | bytes 405512 | tf_op jit(solution)/shard_map/ppermute | solution.py:500
  35.1 10.4 %collective-permute-start.10 = (f32[264,128]{1,0:T(8,128)S(1)}, f32[264,128]{1,0:T(8,128)S(1)}, u32[]{:S(2)}, u32[]{:S(2)}) collective-permute-start(f32[264,128]{1,0:T(8,128)S(1)} %add.82), channel_id=1, source_target_pairs={{0,6},{1,7},{2,4},{3,5},{4,2},{5,3},{6,0},{7,1},{8,14},{9,15},{10,... | collective-permute-start | bytes 405512 | tf_op jit(solution)/shard_map/ppermute | solution.py:500
  40.5 10.7 %collective-permute-start.16 = (f32[264,128]{1,0:T(8,128)S(1)}, f32[264,128]{1,0:T(8,128)S(1)}, u32[]{:S(2)}, u32[]{:S(2)}) collective-permute-start(f32[264,128]{1,0:T(8,128)S(1)} %add.83), channel_id=1, source_target_pairs={{0,6},{1,7},{2,4},{3,5},{4,2},{5,3},{6,0},{7,1},{8,14},{9,15},{10,... | collective-permute-start | bytes 405512 | tf_op jit(solution)/shard_map/ppermute | solution.py:500
  41.6 9.7 %collective-permute-start.15 = (f32[264,128]{1,0:T(8,128)S(1)}, f32[264,128]{1,0:T(8,128)S(1)}, u32[]{:S(2)}, u32[]{:S(2)}) collective-permute-start(f32[264,128]{1,0:T(8,128)S(1)} %add.83), channel_id=1, source_target_pairs={{0,4},{1,5},{2,6},{3,7},{4,0},{5,1},{6,2},{7,3},{8,12},{9,13},{10,... | collective-permute-start | bytes 405512 | tf_op jit(solution)/shard_map/ppermute | solution.py:500
  43.3 8.0 %collective-permute-start.14 = (f32[264,128]{1,0:T(8,128)S(1)}, f32[264,128]{1,0:T(8,128)S(1)}, u32[]{:S(2)}, u32[]{:S(2)}) collective-permute-start(f32[264,128]{1,0:T(8,128)S(1)} %add.83), channel_id=1, source_target_pairs={{0,2},{1,3},{2,0},{3,1},{4,6},{5,7},{6,4},{7,5},{8,10},{9,11},{10,... | collective-permute-start | bytes 405512 | tf_op jit(solution)/shard_map/ppermute | solution.py:500
  59.7 4.2 %collective-permute-start.18 = (f32[1056,128]{1,0:T(8,128)S(1)}, f32[1056,128]{1,0:T(8,128)S(1)}, u32[]{:S(2)}, u32[]{:S(2)}) collective-permute-start(f32[1056,128]{1,0:T(8,128)S(1)} %get-tuple-element.292), channel_id=1, source_target_pairs={{0,1},{1,0},{2,3},{3,2},{4,5},{5,4},{6,7},{7,6},{8,9},{9,8},{10,11... | collective-permute-start | bytes 1622024 | tf_op jit(solution)/shard_map/ppermute | solution.py:500
  64.0 8.5 %collective-permute-start.22 = (f32[264,128]{1,0:T(8,128)S(1)}, f32[264,128]{1,0:T(8,128)S(1)}, u32[]{:S(2)}, u32[]{:S(2)}) collective-permute-start(f32[264,128]{1,0:T(8,128)S(1)} %get-tuple-element.366), channel_id=1, source_target_pairs={{0,2},{1,3},{2,0},{3,1},{4,6},{5,7},{6,4},{7,5},{8,10},{9,11},{10,... | collective-permute-start | bytes 405512 | tf_op jit(solution)/shard_map/ppermute | solution.py:500
  64.6 9.4 %collective-permute-start.21 = (f32[264,128]{1,0:T(8,128)S(1)}, f32[264,128]{1,0:T(8,128)S(1)}, u32[]{:S(2)}, u32[]{:S(2)}) collective-permute-start(f32[264,128]{1,0:T(8,128)S(1)} %get-tuple-element.367), channel_id=1, source_target_pairs={{0,4},{1,5},{2,6},{3,7},{4,0},{5,1},{6,2},{7,3},{8,12},{9,13},{10,... | collective-permute-start | bytes 405512 | tf_op jit(solution)/shard_map/ppermute | solution.py:500
  64.6 9.4 %collective-permute-start.20 = (f32[264,128]{1,0:T(8,128)S(1)}, f32[264,128]{1,0:T(8,128)S(1)}, u32[]{:S(2)}, u32[]{:S(2)}) collective-permute-start(f32[264,128]{1,0:T(8,128)S(1)} %get-tuple-element.368), channel_id=1, source_target_pairs={{0,6},{1,7},{2,4},{3,5},{4,2},{5,3},{6,0},{7,1},{8,14},{9,15},{10,... | collective-permute-start | bytes 405512 | tf_op jit(solution)/shard_map/ppermute | solution.py:500
  67.5 2.5 %collective-permute-start.19 = (f32[1056,128]{1,0:T(8,128)S(1)}, f32[1056,128]{1,0:T(8,128)S(1)}, u32[]{:S(2)}, u32[]{:S(2)}) collective-permute-start(f32[1056,128]{1,0:T(8,128)S(1)} %get-tuple-element.298), channel_id=1, source_target_pairs={{0,1},{1,0},{2,3},{3,2},{4,5},{5,4},{6,7},{7,6},{8,9},{9,8},{10,11... | collective-permute-start | bytes 1622024 | tf_op jit(solution)/shard_map/ppermute | solution.py:500
  70.1 11.3 %collective-permute-start.25 = (f32[264,128]{1,0:T(8,128)S(1)}, f32[264,128]{1,0:T(8,128)S(1)}, u32[]{:S(2)}, u32[]{:S(2)}) collective-permute-start(f32[264,128]{1,0:T(8,128)S(1)} %get-tuple-element.363), channel_id=1, source_target_pairs={{0,6},{1,7},{2,4},{3,5},{4,2},{5,3},{6,0},{7,1},{8,14},{9,15},{10,... | collective-permute-start | bytes 405512 | tf_op jit(solution)/shard_map/ppermute | solution.py:500
  70.2 11.8 %collective-permute-start.24 = (f32[264,128]{1,0:T(8,128)S(1)}, f32[264,128]{1,0:T(8,128)S(1)}, u32[]{:S(2)}, u32[]{:S(2)}) collective-permute-start(f32[264,128]{1,0:T(8,128)S(1)} %get-tuple-element.364), channel_id=1, source_target_pairs={{0,4},{1,5},{2,6},{3,7},{4,0},{5,1},{6,2},{7,3},{8,12},{9,13},{10,... | collective-permute-start | bytes 405512 | tf_op jit(solution)/shard_map/ppermute | solution.py:500
  72.4 9.5 %collective-permute-start.23 = (f32[264,128]{1,0:T(8,128)S(1)}, f32[264,128]{1,0:T(8,128)S(1)}, u32[]{:S(2)}, u32[]{:S(2)}) collective-permute-start(f32[264,128]{1,0:T(8,128)S(1)} %get-tuple-element.365), channel_id=1, source_target_pairs={{0,2},{1,3},{2,0},{3,1},{4,6},{5,7},{6,4},{7,5},{8,10},{9,11},{10,... | collective-permute-start | bytes 405512 | tf_op jit(solution)/shard_map/ppermute | solution.py:500
  74.0 8.5 %collective-permute-start.26 = (f32[264,128]{1,0:T(8,128)S(1)}, f32[264,128]{1,0:T(8,128)S(1)}, u32[]{:S(2)}, u32[]{:S(2)}) collective-permute-start(f32[264,128]{1,0:T(8,128)S(1)} %fusion.1), channel_id=1, source_target_pairs={{0,8},{1,9},{2,10},{3,11},{4,12},{5,13},{6,14},{7,15},{8,0},{9,1},... | collective-permute-start | bytes 405512 | tf_op jit(solution)/shard_map/ppermute | solution.py:500
  82.0 9.0 %collective-permute-start.27 = (f32[264,128]{1,0:T(8,128)S(1)}, f32[264,128]{1,0:T(8,128)S(1)}, u32[]{:S(2)}, u32[]{:S(2)}) collective-permute-start(f32[264,128]{1,0:T(8,128)S(1)} %fusion.3), channel_id=1, source_target_pairs={{0,8},{1,9},{2,10},{3,11},{4,12},{5,13},{6,14},{7,15},{8,0},{9,1},... | collective-permute-start | bytes 405512 | tf_op jit(solution)/shard_map/ppermute | solution.py:500
  82.6 11.5 %collective-permute-start.30 = (f32[264,128]{1,0:T(8,128)S(1)}, f32[264,128]{1,0:T(8,128)S(1)}, u32[]{:S(2)}, u32[]{:S(2)}) collective-permute-start(f32[264,128]{1,0:T(8,128)S(1)} %add.93), channel_id=1, source_target_pairs={{0,2},{1,3},{2,0},{3,1},{4,6},{5,7},{6,4},{7,5},{8,10},{9,11},{10,... | collective-permute-start | bytes 405512 | tf_op jit(solution)/shard_map/ppermute | solution.py:500
  83.6 10.9 %collective-permute-start.29 = (f32[264,128]{1,0:T(8,128)S(1)}, f32[264,128]{1,0:T(8,128)S(1)}, u32[]{:S(2)}, u32[]{:S(2)}) collective-permute-start(f32[264,128]{1,0:T(8,128)S(1)} %add.93), channel_id=1, source_target_pairs={{0,4},{1,5},{2,6},{3,7},{4,0},{5,1},{6,2},{7,3},{8,12},{9,13},{10,... | collective-permute-start | bytes 405512 | tf_op jit(solution)/shard_map/ppermute | solution.py:500
  85.4 9.7 %collective-permute-start.28 = (f32[264,128]{1,0:T(8,128)S(1)}, f32[264,128]{1,0:T(8,128)S(1)}, u32[]{:S(2)}, u32[]{:S(2)}) collective-permute-start(f32[264,128]{1,0:T(8,128)S(1)} %add.93), channel_id=1, source_target_pairs={{0,6},{1,7},{2,4},{3,5},{4,2},{5,3},{6,0},{7,1},{8,14},{9,15},{10,... | collective-permute-start | bytes 405512 | tf_op jit(solution)/shard_map/ppermute | solution.py:500
  91.0 8.3 %collective-permute-start.34 = (f32[264,128]{1,0:T(8,128)S(1)}, f32[264,128]{1,0:T(8,128)S(1)}, u32[]{:S(2)}, u32[]{:S(2)}) collective-permute-start(f32[264,128]{1,0:T(8,128)S(1)} %add.92), channel_id=1, source_target_pairs={{0,6},{1,7},{2,4},{3,5},{4,2},{5,3},{6,0},{7,1},{8,14},{9,15},{10,... | collective-permute-start | bytes 405512 | tf_op jit(solution)/shard_map/ppermute | solution.py:500
  91.3 9.1 %collective-permute-start.33 = (f32[264,128]{1,0:T(8,128)S(1)}, f32[264,128]{1,0:T(8,128)S(1)}, u32[]{:S(2)}, u32[]{:S(2)}) collective-permute-start(f32[264,128]{1,0:T(8,128)S(1)} %add.92), channel_id=1, source_target_pairs={{0,4},{1,5},{2,6},{3,7},{4,0},{5,1},{6,2},{7,3},{8,12},{9,13},{10,... | collective-permute-start | bytes 405512 | tf_op jit(solution)/shard_map/ppermute | solution.py:500
  94.1 6.6 %collective-permute-start.32 = (f32[264,128]{1,0:T(8,128)S(1)}, f32[264,128]{1,0:T(8,128)S(1)}, u32[]{:S(2)}, u32[]{:S(2)}) collective-permute-start(f32[264,128]{1,0:T(8,128)S(1)} %add.92), channel_id=1, source_target_pairs={{0,2},{1,3},{2,0},{3,1},{4,6},{5,7},{6,4},{7,5},{8,10},{9,11},{10,... | collective-permute-start | bytes 405512 | tf_op jit(solution)/shard_map/ppermute | solution.py:500
  (10 other events, 62.5 us)

commit v16 on v14

--- a/solution.py
+++ b/solution.py
@@ -561,11 +561,14 @@
         got_b = [b.exchange(offset)]
         a.own(close(env, got_a))
 
-    got_a = a.gather_plane()
+    side_a, near_a = [a.swap(a.keep, offset) for offset in PLANE[:2]]
+    (near_a,) = close(env, near_a)
+    diagonal_a = a.swap(near_a, PLANE[0])
     b.own(close(env, *got_b))
 
     got_b = b.gather_plane()
-    got_a = a.gather_core(close(env, *got_a))
+    side_a, diagonal_a = close(env, side_a, diagonal_a)
+    got_a = a.gather_core([side_a, near_a, diagonal_a])
     work()
     (got_a,) = close(env, got_a)
     late[0](env, [a.mine, got_a])

time: 108 us -> 110 us (1.019)
  starting transfers between devices: 38.9 us -> 43.2 us
  waiting for transfers between devices: 12.9 us -> 11 us
    ppermute x36, starting transfers between devices: 38.9 us -> 43.2 us  [swap(): return lax.ppermute(x, 'row', [(i, i ^ offset) for i in range(self.count)])]
    ppermute x36, waiting for transfers between devices: 12.9 us -> 11 us  [swap(): return lax.ppermute(x, 'row', [(i, i ^ offset) for i in range(self.count)])]
  transfers between devices with their start and end apart: 36 -> 36, of which waited for: 9 -> 9; matrix products, arithmetic and copies ran while one was open for 0% -> 0% of each run, Pallas kernels for 34% -> 33%
where the time goes in v16:
time: 110 us
  Pallas kernels  54.3 us (49%)
  starting transfers between devices  43.2 us (39%)
  waiting for transfers between devices  11 us (10%)
    ppermute x36, starting transfers between devices, swap(): return lax.ppermute(x, 'row', [(i, i ^ offset) for i in range(self.count)])  43.2 us
    ppermute x36, waiting for transfers between devices, swap(): return lax.ppermute(x, 'row', [(i, i ^ offset) for i in range(self.count)])  11 us
    pallas_call x2, Pallas kernels, affine(): call(functools.partial(affine_kernel, part), 'affine', struct(height, siz...  8.39 us
    pallas_call x2, Pallas kernels, affine_parts(): call(functools.partial(affine_parts_kernel, part), 'affine_parts', struct...  7.87 us
    pallas_call x1, Pallas kernels, first_gram(): call(functools.partial(first_gram_kernel, shards), 'first_gram', halves(s...  6.9 us
    pallas_call x1, Pallas kernels, second_gram(): call(functools.partial(second_gram_kernel, shards, len(pieces)), 'second_...  6.15 us
    pallas_call x2, Pallas kernels, first_part(): call(functools.partial(first_part_kernel, shards, len(pieces), columns),...  5.92 us
    pallas_call x1, Pallas kernels, last_step(): call(functools.partial(last_kernel, shards, len(pieces)), 'last', struct(...  4.88 us
  transfers between devices with their start and end apart: 36, of which 9 were waited for; matrix products, arithmetic and copies ran while one was open for 0% of the time, Pallas kernels for 33%

profile of v16, /device:TPU:0, one launch (start us, length us, event | category | flops | bytes accessed | tf_op | source)
XLA Modules:
  0.0 109.9 jit_solution(7847990700341212594)
XLA Ops:
  0.0 6.9 %first_gram.1 = (f32[1056,128]{1,0:T(8,128)S(1)}, f32[1056,128]{1,0:T(8,128)S(1)}, bf16[1024,1024]{1,0:T(8,128)(2,1)S(1)}, bf16[1024,1024]{1,0:T(8,128)(2,1)S(1)...) custom-call(s32[1]{0:T(128)} %bitcast.me_ref, f32[1024,1024]{1,0:T(8,128)} %x_ref, f32[1024,1024]{1,0:T(8,128)} %a_ref.1), custom_call_target="tpu_custom_call" | custom-call | flops 32212254720 | bytes 167772160 | tf_op jit(solution)/shard_map/first_gram/pallas_call | solution.py:198
  7.4 3.6 %other_gram.1 = (f32[1056,128]{1,0:T(8,128)S(1)}, f32[1056,128]{1,0:T(8,128)S(1)}) custom-call(s32[1]{0:T(128)} %bitcast.me_ref, bf16[1024,1024]{1,0:T(8,128)(2,1)S(1)} %get-tuple-element.200.ah, bf16[1024,1024]{1,0:T(8,128)(2,1)S(1)} %get-tuple-element.201.al, bf16[1024,1024]{1,0:T(8,128)(2,1)S(1)} %get-tuple-element.202.bh, ...), custom_call_target="tpu_custom_call" | custom-call | flops 32212254720 | bytes 83886080 | tf_op jit(solution)/shard_map/other_gram/pallas_call | solution.py:228
  11.2 2.6 %collective-permute-start.4 = (f32[264,128]{1,0:T(8,128)S(1)}, f32[264,128]{1,0:T(8,128)S(1)}, u32[]{:S(2)}, u32[]{:S(2)}) collective-permute-start(f32[264,128]{1,0:T(8,128)S(1)} %get-tuple-element.404), channel_id=1, source_target_pairs={{0,2},{1,3},{2,0},{3,1},{4,6},{5,7},{6,4},{7,5},{8,10},{9,11},{10,... | collective-permute-start | bytes 405512 | tf_op jit(solution)/shard_map/ppermute | solution.py:500
  13.8 1.6 %collective-permute-start.3 = (f32[264,128]{1,0:T(8,128)S(1)}, f32[264,128]{1,0:T(8,128)S(1)}, u32[]{:S(2)}, u32[]{:S(2)}) collective-permute-start(f32[264,128]{1,0:T(8,128)S(1)} %get-tuple-element.405), channel_id=1, source_target_pairs={{0,4},{1,5},{2,6},{3,7},{4,0},{5,1},{6,2},{7,3},{8,12},{9,13},{10,... | collective-permute-start | bytes 405512 | tf_op jit(solution)/shard_map/ppermute | solution.py:500
  15.4 2.6 %affine.2.refs_4_ = f32[256,1024]{1,0:T(8,128)S(1)} custom-call(f32[1024,1024]{1,0:T(8,128)S(1)} %copy-done.1, f32[1024,1024]{1,0:T(8,128)S(1)} %copy-done.2), custom_call_target="tpu_custom_call" | custom-call | flops 16106127360 | bytes 83886080 | tf_op jit(solution)/shard_map/affine/pallas_call | solution.py:261
  18.1 3.0 %collective-permute-start.7 = (f32[264,128]{1,0:T(8,128)S(1)}, f32[264,128]{1,0:T(8,128)S(1)}, u32[]{:S(2)}, u32[]{:S(2)}) collective-permute-start(f32[264,128]{1,0:T(8,128)S(1)} %get-tuple-element.401), channel_id=1, source_target_pairs={{0,6},{1,7},{2,4},{3,5},{4,2},{5,3},{6,0},{7,1},{8,14},{9,15},{10,... | collective-permute-start | bytes 405512 | tf_op jit(solution)/shard_map/ppermute | solution.py:500
  22.6 3.0 %collective-permute-start.8 = (f32[264,128]{1,0:T(8,128)S(1)}, f32[264,128]{1,0:T(8,128)S(1)}, u32[]{:S(2)}, u32[]{:S(2)}) collective-permute-start(f32[264,128]{1,0:T(8,128)S(1)} %fusion.7), channel_id=1, source_target_pairs={{0,8},{1,9},{2,10},{3,11},{4,12},{5,13},{6,14},{7,15},{8,0},{9,1},... | collective-permute-start | bytes 405512 | tf_op jit(solution)/shard_map/ppermute | solution.py:500
  25.6 5.8 %affine.3.refs_5_ = f32[768,1024]{1,0:T(8,128)S(1)} custom-call(f32[1024,1024]{1,0:T(8,128)S(1)} %copy-done.1, f32[1024,1024]{1,0:T(8,128)S(1)} %copy-done.2), custom_call_target="tpu_custom_call" | custom-call | flops 48318382080 | bytes 83886080 | tf_op jit(solution)/shard_map/affine/pallas_call | solution.py:261
  31.5 2.5 %collective-permute-start.9 = (f32[264,128]{1,0:T(8,128)S(1)}, f32[264,128]{1,0:T(8,128)S(1)}, u32[]{:S(2)}, u32[]{:S(2)}) collective-permute-start(f32[264,128]{1,0:T(8,128)S(1)} %add.79), channel_id=1, source_target_pairs={{0,4},{1,5},{2,6},{3,7},{4,0},{5,1},{6,2},{7,3},{8,12},{9,13},{10,... | collective-permute-start | bytes 405512 | tf_op jit(solution)/shard_map/ppermute | solution.py:500
  34.0 2.3 %collective-permute-start.10 = (f32[264,128]{1,0:T(8,128)S(1)}, f32[264,128]{1,0:T(8,128)S(1)}, u32[]{:S(2)}, u32[]{:S(2)}) collective-permute-start(f32[264,128]{1,0:T(8,128)S(1)} %fusion.5), channel_id=1, source_target_pairs={{0,8},{1,9},{2,10},{3,11},{4,12},{5,13},{6,14},{7,15},{8,0},{9,1},... | collective-permute-start | bytes 405512 | tf_op jit(solution)/shard_map/ppermute | solution.py:500
  36.3 1.5 %collective-permute-start.12 = (f32[264,128]{1,0:T(8,128)S(1)}, f32[264,128]{1,0:T(8,128)S(1)}, u32[]{:S(2)}, u32[]{:S(2)}) collective-permute-start(f32[264,128]{1,0:T(8,128)S(1)} %add.79), channel_id=1, source_target_pairs={{0,2},{1,3},{2,0},{3,1},{4,6},{5,7},{6,4},{7,5},{8,10},{9,11},{10,... | collective-permute-start | bytes 405512 | tf_op jit(solution)/shard_map/ppermute | solution.py:500
  39.3 3.5 %collective-permute-done.10 = f32[264,128]{1,0:T(8,128)S(1)} collective-permute-done((f32[264,128]{1,0:T(8,128)S(1)}, f32[264,128]{1,0:T(8,128)S(1)}, u32[]{:S(2)}, u32[]{:S(2)}) %collective-permute-start.10) | collective-permute-done | bytes 135200 | tf_op jit(solution)/shard_map/ppermute | solution.py:500
  43.6 2.8 %collective-permute-start.14 = (f32[264,128]{1,0:T(8,128)S(1)}, f32[264,128]{1,0:T(8,128)S(1)}, u32[]{:S(2)}, u32[]{:S(2)}) collective-permute-start(f32[264,128]{1,0:T(8,128)S(1)} %add.83), channel_id=1, source_target_pairs={{0,6},{1,7},{2,4},{3,5},{4,2},{5,3},{6,0},{7,1},{8,14},{9,15},{10,... | collective-permute-start | bytes 405512 | tf_op jit(solution)/shard_map/ppermute | solution.py:500
  46.5 1.7 %turn.1 = (bf16[1024,1024]{1,0:T(8,128)(2,1)S(1)}, bf16[1024,1024]{1,0:T(8,128)(2,1)S(1)}) custom-call(f32[1024,1024]{1,0:T(8,128)S(1)} %copy-done.4), custom_call_target="tpu_custom_call" | custom-call | flops 6442450944 | bytes 83886080 | tf_op jit(solution)/shard_map/turn/pallas_call | solution.py:382
  48.4 3.8 %first_part.2.mid_ref.refs_4_ = f32[1024,1024]{1,0:T(8,128)S(1)} custom-call(s32[1]{0:T(128)} %bitcast.me_ref, f32[1056,128]{1,0:T(8,128)S(1)} %pad_maximum_fusion.refs_0_, f32[1056,128]{1,0:T(8,128)S(1)} %collective-permute-done.13.refs_1_, bf16[1024,1024]{1,0:T(8,128)(2,1)S(1)} %get-tuple-element.309.refs_2_, ...), custom_call_target="tpu_custom_call" | custom-call | flops 32212254720 | bytes 125829120 | tf_op jit(solution)/shard_map/first_part/pallas_call | solution.py:336
  52.6 1.8 %column_product.1.refs_7_ = f32[1024,256]{1,0:T(8,128)S(1)} custom-call(bf16[1024,1024]{1,0:T(8,128)(2,1)S(1)} %get-tuple-element.311.xh.refs_5_, bf16[1024,1024]{1,0:T(8,128)(2,1)S(1)} %get-tuple-element.312.xl.refs_6_, f32[1024,1024]{1,0:T(8,128)S(1)} %first_part.2.mid_ref.refs_4_), custom_call_target="tpu_custom_call" | custom-call | flops 16106127360 | bytes 83886080 | tf_op jit(solution)/shard_map/column_product/pallas_call | solution.py:367
  54.5 6.1 %second_gram.1 = (f32[1056,128]{1,0:T(8,128)S(1)}, f32[1056,128]{1,0:T(8,128)S(1)}, bf16[1024,1024]{1,0:T(8,128)(2,1)S(1)}, bf16[1024,1024]{1,0:T(8,128)(2,1)S(1)}) custom-call(s32[1]{0:T(128)} %bitcast.me_ref, f32[1056,128]{1,0:T(8,128)S(1)} %pad_maximum_fusion.1.refs_0_, f32[1056,128]{1,0:T(8,128)S(1)} %collective-permute-done.17.refs_1_, ...), custom_call_target="tpu_custom_call" | custom-call | flops 51539607552 | bytes 209715200 | tf_op jit(solution)/shard_map/second_gram/pallas_call | solution.py:425
  60.9 3.9 %fourth_gram.1 = (f32[1056,128]{1,0:T(8,128)S(1)}, f32[1056,128]{1,0:T(8,128)S(1)}) custom-call(s32[1]{0:T(128)} %bitcast.me_ref, bf16[1024,1024]{1,0:T(8,128)(2,1)S(1)} %get-tuple-element.311.xh.refs_5_, bf16[1024,1024]{1,0:T(8,128)(2,1)S(1)} %get-tuple-element.312.xl.refs_6_, bf16[1024,1024]{1,0:T(8,128)(2,1)S(1)} %get-tuple-element.337.mh.ah, ...), custom_call_target="tpu_custom_call" | custom-call | flops 32212254720 | bytes 83886080 | tf_op jit(solution)/shard_map/fourth_gram/pallas_call | solution.py:442
  65.6 2.8 %collective-permute-start.20 = (f32[264,128]{1,0:T(8,128)S(1)}, f32[264,128]{1,0:T(8,128)S(1)}, u32[]{:S(2)}, u32[]{:S(2)}) collective-permute-start(f32[264,128]{1,0:T(8,128)S(1)} %get-tuple-element.400), channel_id=1, source_target_pairs={{0,6},{1,7},{2,4},{3,5},{4,2},{5,3},{6,0},{7,1},{8,14},{9,15},{10,... | collective-permute-start | bytes 405512 | tf_op jit(solution)/shard_map/ppermute | solution.py:500
  68.5 2.5 %affine_parts.2.refs_4_.refs_0_ = f32[256,1024]{1,0:T(8,128)S(1)} custom-call(bf16[1024,1024]{1,0:T(8,128)(2,1)S(1)} %get-tuple-element.337.mh.ah, bf16[1024,1024]{1,0:T(8,128)(2,1)S(1)} %get-tuple-element.338.ml.al, f32[1024,1024]{1,0:T(8,128)S(1)} %copy-done.3), custom_call_target="tpu_custom_call" | custom-call | flops 16106127360 | bytes 83886080 | tf_op jit(solution)/shard_map/affine_parts/pallas_call | solution.py:283
  71.2 1.9 %collective-permute-start.24 = (f32[264,128]{1,0:T(8,128)S(1)}, f32[264,128]{1,0:T(8,128)S(1)}, u32[]{:S(2)}, u32[]{:S(2)}) collective-permute-start(f32[264,128]{1,0:T(8,128)S(1)} %get-tuple-element.396), channel_id=1, source_target_pairs={{0,4},{1,5},{2,6},{3,7},{4,0},{5,1},{6,2},{7,3},{8,12},{9,13},{10,... | collective-permute-start | bytes 405512 | tf_op jit(solution)/shard_map/ppermute | solution.py:500
  73.4 1.5 %collective-permute-start.23 = (f32[264,128]{1,0:T(8,128)S(1)}, f32[264,128]{1,0:T(8,128)S(1)}, u32[]{:S(2)}, u32[]{:S(2)}) collective-permute-start(f32[264,128]{1,0:T(8,128)S(1)} %get-tuple-element.397), channel_id=1, source_target_pairs={{0,2},{1,3},{2,0},{3,1},{4,6},{5,7},{6,4},{7,5},{8,10},{9,11},{10,... | collective-permute-start | bytes 405512 | tf_op jit(solution)/shard_map/ppermute | solution.py:500
  75.0 1.6 %collective-permute-start.26 = (f32[264,128]{1,0:T(8,128)S(1)}, f32[264,128]{1,0:T(8,128)S(1)}, u32[]{:S(2)}, u32[]{:S(2)}) collective-permute-start(f32[264,128]{1,0:T(8,128)S(1)} %fusion.1), channel_id=1, source_target_pairs={{0,8},{1,9},{2,10},{3,11},{4,12},{5,13},{6,14},{7,15},{8,0},{9,1},... | collective-permute-start | bytes 405512 | tf_op jit(solution)/shard_map/ppermute | solution.py:500
  76.5 5.4 %affine_parts.3.refs_5_.refs_1_ = f32[768,1024]{1,0:T(8,128)S(1)} custom-call(bf16[1024,1024]{1,0:T(8,128)(2,1)S(1)} %get-tuple-element.337.mh.ah, bf16[1024,1024]{1,0:T(8,128)(2,1)S(1)} %get-tuple-element.338.ml.al, f32[1024,1024]{1,0:T(8,128)S(1)} %copy-done.3), custom_call_target="tpu_custom_call" | custom-call | flops 48318382080 | bytes 83886080 | tf_op jit(solution)/shard_map/affine_parts/pallas_call | solution.py:283
  82.9 2.4 %collective-permute-start.27 = (f32[264,128]{1,0:T(8,128)S(1)}, f32[264,128]{1,0:T(8,128)S(1)}, u32[]{:S(2)}, u32[]{:S(2)}) collective-permute-start(f32[264,128]{1,0:T(8,128)S(1)} %add.92), channel_id=1, source_target_pairs={{0,4},{1,5},{2,6},{3,7},{4,0},{5,1},{6,2},{7,3},{8,12},{9,13},{10,... | collective-permute-start | bytes 405512 | tf_op jit(solution)/shard_map/ppermute | solution.py:500
  85.3 2.1 %collective-permute-start.28 = (f32[264,128]{1,0:T(8,128)S(1)}, f32[264,128]{1,0:T(8,128)S(1)}, u32[]{:S(2)}, u32[]{:S(2)}) collective-permute-start(f32[264,128]{1,0:T(8,128)S(1)} %fusion.3), channel_id=1, source_target_pairs={{0,8},{1,9},{2,10},{3,11},{4,12},{5,13},{6,14},{7,15},{8,0},{9,1},... | collective-permute-start | bytes 405512 | tf_op jit(solution)/shard_map/ppermute | solution.py:500
  87.4 1.6 %collective-permute-start.30 = (f32[264,128]{1,0:T(8,128)S(1)}, f32[264,128]{1,0:T(8,128)S(1)}, u32[]{:S(2)}, u32[]{:S(2)}) collective-permute-start(f32[264,128]{1,0:T(8,128)S(1)} %add.92), channel_id=1, source_target_pairs={{0,2},{1,3},{2,0},{3,1},{4,6},{5,7},{6,4},{7,5},{8,10},{9,11},{10,... | collective-permute-start | bytes 405512 | tf_op jit(solution)/shard_map/ppermute | solution.py:500
  90.7 3.2 %collective-permute-done.28 = f32[264,128]{1,0:T(8,128)S(1)} collective-permute-done((f32[264,128]{1,0:T(8,128)S(1)}, f32[264,128]{1,0:T(8,128)S(1)}, u32[]{:S(2)}, u32[]{:S(2)}) %collective-permute-start.28) | collective-permute-done | bytes 135200 | tf_op jit(solution)/shard_map/ppermute | solution.py:500
  95.2 2.2 %collective-permute-start.32 = (f32[264,128]{1,0:T(8,128)S(1)}, f32[264,128]{1,0:T(8,128)S(1)}, u32[]{:S(2)}, u32[]{:S(2)}) collective-permute-start(f32[264,128]{1,0:T(8,128)S(1)} %add.93), channel_id=1, source_target_pairs={{0,6},{1,7},{2,4},{3,5},{4,2},{5,3},{6,0},{7,1},{8,14},{9,15},{10,... | collective-permute-start | bytes 405512 | tf_op jit(solution)/shard_map/ppermute | solution.py:500
  99.5 2.2 %first_part.3 = (f32[1024,256]{1,0:T(8,128)S(1)}, bf16[1024,1024]{1,0:T(8,128)(2,1)S(1)}, bf16[1024,1024]{1,0:T(8,128)(2,1)S(1)}) custom-call(s32[1]{0:T(128)} %bitcast.me_ref, f32[1056,128]{1,0:T(8,128)S(1)} %pad_maximum_fusion.2.refs_0_, f32[1056,128]{1,0:T(8,128)S(1)} %collective-permute-done.31.refs_1_, bf16[1024,1024]{1,0:T(8,128)(2,1)S(1)} %cut.4.refs_2_.ah, ...), custom_call_target="tpu_custom_call" | custom-call | flops 32212254720 | bytes 125829120 | tf_op jit(solution)/shard_map/first_part/pallas_call | solution.py:336
  103.0 1.8 %other_part.1.refs_5_ = f32[1024,768]{1,0:T(8,128)S(1)} custom-call(bf16[1024,1024]{1,0:T(8,128)(2,1)S(1)} %cut.4.refs_2_.ah, bf16[1024,1024]{1,0:T(8,128)(2,1)S(1)} %cut.5.refs_3_.al, bf16[1024,1024]{1,0:T(8,128)(2,1)S(1)} %get-tuple-element.388.hi, bf16[1024,1024]{1,0:T(8,128)(2,1)S(1)} %get-tuple-element.389.lo, ...), custom_call_target="tpu_custom_call" | custom-call | flops 16106127360 | bytes 125829120 | tf_op jit(solution)/shard_map/other_part/pallas_call | solution.py:351
  104.9 4.9 %last.1 = f32[1024,1024]{1,0:T(8,128)} custom-call(s32[1]{0:T(128)} %bitcast.me_ref, f32[1056,128]{1,0:T(8,128)S(1)} %pad_maximum_fusion.3.refs_0_, f32[1056,128]{1,0:T(8,128)S(1)} %collective-permute-done.35.refs_1_, bf16[1024,1024]{1,0:T(8,128)(2,1)S(1)} %cut.4.refs_2_.ah, bf16[1024,1024]{1,0:T(8,128)(2,1)S(1)} %cut.5.refs_3_.al, ...), custom_call_target="tpu_custom_call" | custom-call | flops 32212254720 | bytes 125829120 | tf_op jit(solution)/shard_map/last/pallas_call | solution.py:477
  (89 shorter events, 14.3 us)
Async XLA Ops:
  6.9 4.2 %collective-permute-start = (f32[1056,128]{1,0:T(8,128)S(1)}, f32[1056,128]{1,0:T(8,128)S(1)}, u32[]{:S(2)}, u32[]{:S(2)}) collective-permute-start(f32[1056,128]{1,0:T(8,128)S(1)} %get-tuple-element.206), channel_id=1, source_target_pairs={{0,1},{1,0},{2,3},{3,2},{4,5},{5,4},{6,7},{7,6},{8,9},{9,8},{10,11... | collective-permute-start | bytes 1622024 | tf_op jit(solution)/shard_map/ppermute | solution.py:500
  11.2 11.1 %collective-permute-start.4 = (f32[264,128]{1,0:T(8,128)S(1)}, f32[264,128]{1,0:T(8,128)S(1)}, u32[]{:S(2)}, u32[]{:S(2)}) collective-permute-start(f32[264,128]{1,0:T(8,128)S(1)} %get-tuple-element.404), channel_id=1, source_target_pairs={{0,2},{1,3},{2,0},{3,1},{4,6},{5,7},{6,4},{7,5},{8,10},{9,11},{10,... | collective-permute-start | bytes 405512 | tf_op jit(solution)/shard_map/ppermute | solution.py:500
  13.8 8.7 %collective-permute-start.3 = (f32[264,128]{1,0:T(8,128)S(1)}, f32[264,128]{1,0:T(8,128)S(1)}, u32[]{:S(2)}, u32[]{:S(2)}) collective-permute-start(f32[264,128]{1,0:T(8,128)S(1)} %get-tuple-element.405), channel_id=1, source_target_pairs={{0,4},{1,5},{2,6},{3,7},{4,0},{5,1},{6,2},{7,3},{8,12},{9,13},{10,... | collective-permute-start | bytes 405512 | tf_op jit(solution)/shard_map/ppermute | solution.py:500
  15.4 7.2 %collective-permute-start.2 = (f32[264,128]{1,0:T(8,128)S(1)}, f32[264,128]{1,0:T(8,128)S(1)}, u32[]{:S(2)}, u32[]{:S(2)}) collective-permute-start(f32[264,128]{1,0:T(8,128)S(1)} %get-tuple-element.406), channel_id=1, source_target_pairs={{0,6},{1,7},{2,4},{3,5},{4,2},{5,3},{6,0},{7,1},{8,14},{9,15},{10,... | collective-permute-start | bytes 405512 | tf_op jit(solution)/shard_map/ppermute | solution.py:500
  15.4 2.6 %collective-permute-start.1 = (f32[1056,128]{1,0:T(8,128)S(1)}, f32[1056,128]{1,0:T(8,128)S(1)}, u32[]{:S(2)}, u32[]{:S(2)}) collective-permute-start(f32[1056,128]{1,0:T(8,128)S(1)} %get-tuple-element.212), channel_id=1, source_target_pairs={{0,1},{1,0},{2,3},{3,2},{4,5},{5,4},{6,7},{7,6},{8,9},{9,8},{10,11... | collective-permute-start | bytes 1622024 | tf_op jit(solution)/shard_map/ppermute | solution.py:500
  18.1 13.3 %collective-permute-start.7 = (f32[264,128]{1,0:T(8,128)S(1)}, f32[264,128]{1,0:T(8,128)S(1)}, u32[]{:S(2)}, u32[]{:S(2)}) collective-permute-start(f32[264,128]{1,0:T(8,128)S(1)} %get-tuple-element.401), channel_id=1, source_target_pairs={{0,6},{1,7},{2,4},{3,5},{4,2},{5,3},{6,0},{7,1},{8,14},{9,15},{10,... | collective-permute-start | bytes 405512 | tf_op jit(solution)/shard_map/ppermute | solution.py:500
  21.1 10.3 %collective-permute-start.6 = (f32[264,128]{1,0:T(8,128)S(1)}, f32[264,128]{1,0:T(8,128)S(1)}, u32[]{:S(2)}, u32[]{:S(2)}) collective-permute-start(f32[264,128]{1,0:T(8,128)S(1)} %get-tuple-element.402), channel_id=1, source_target_pairs={{0,4},{1,5},{2,6},{3,7},{4,0},{5,1},{6,2},{7,3},{8,12},{9,13},{10,... | collective-permute-start | bytes 405512 | tf_op jit(solution)/shard_map/ppermute | solution.py:500
  22.3 9.1 %collective-permute-start.5 = (f32[264,128]{1,0:T(8,128)S(1)}, f32[264,128]{1,0:T(8,128)S(1)}, u32[]{:S(2)}, u32[]{:S(2)}) collective-permute-start(f32[264,128]{1,0:T(8,128)S(1)} %get-tuple-element.403), channel_id=1, source_target_pairs={{0,2},{1,3},{2,0},{3,1},{4,6},{5,7},{6,4},{7,5},{8,10},{9,11},{10,... | collective-permute-start | bytes 405512 | tf_op jit(solution)/shard_map/ppermute | solution.py:500
  22.6 8.8 %collective-permute-start.8 = (f32[264,128]{1,0:T(8,128)S(1)}, f32[264,128]{1,0:T(8,128)S(1)}, u32[]{:S(2)}, u32[]{:S(2)}) collective-permute-start(f32[264,128]{1,0:T(8,128)S(1)} %fusion.7), channel_id=1, source_target_pairs={{0,8},{1,9},{2,10},{3,11},{4,12},{5,13},{6,14},{7,15},{8,0},{9,1},... | collective-permute-start | bytes 405512 | tf_op jit(solution)/shard_map/ppermute | solution.py:500
  31.5 6.5 %collective-permute-start.9 = (f32[264,128]{1,0:T(8,128)S(1)}, f32[264,128]{1,0:T(8,128)S(1)}, u32[]{:S(2)}, u32[]{:S(2)}) collective-permute-start(f32[264,128]{1,0:T(8,128)S(1)} %add.79), channel_id=1, source_target_pairs={{0,4},{1,5},{2,6},{3,7},{4,0},{5,1},{6,2},{7,3},{8,12},{9,13},{10,... | collective-permute-start | bytes 405512 | tf_op jit(solution)/shard_map/ppermute | solution.py:500
  34.0 8.8 %collective-permute-start.10 = (f32[264,128]{1,0:T(8,128)S(1)}, f32[264,128]{1,0:T(8,128)S(1)}, u32[]{:S(2)}, u32[]{:S(2)}) collective-permute-start(f32[264,128]{1,0:T(8,128)S(1)} %fusion.5), channel_id=1, source_target_pairs={{0,8},{1,9},{2,10},{3,11},{4,12},{5,13},{6,14},{7,15},{8,0},{9,1},... | collective-permute-start | bytes 405512 | tf_op jit(solution)/shard_map/ppermute | solution.py:500
  36.3 10.0 %collective-permute-start.12 = (f32[264,128]{1,0:T(8,128)S(1)}, f32[264,128]{1,0:T(8,128)S(1)}, u32[]{:S(2)}, u32[]{:S(2)}) collective-permute-start(f32[264,128]{1,0:T(8,128)S(1)} %add.79), channel_id=1, source_target_pairs={{0,2},{1,3},{2,0},{3,1},{4,6},{5,7},{6,4},{7,5},{8,10},{9,11},{10,... | collective-permute-start | bytes 405512 | tf_op jit(solution)/shard_map/ppermute | solution.py:500
  38.0 8.4 %collective-permute-start.11 = (f32[264,128]{1,0:T(8,128)S(1)}, f32[264,128]{1,0:T(8,128)S(1)}, u32[]{:S(2)}, u32[]{:S(2)}) collective-permute-start(f32[264,128]{1,0:T(8,128)S(1)} %collective-permute-done.9), channel_id=1, source_target_pairs={{0,2},{1,3},{2,0},{3,1},{4,6},{5,7},{6,4},{7,5},{8,10},{9,11},{10,... | collective-permute-start | bytes 405512 | tf_op jit(solution)/shard_map/ppermute | solution.py:500
  42.8 9.4 %collective-permute-start.16 = (f32[264,128]{1,0:T(8,128)S(1)}, f32[264,128]{1,0:T(8,128)S(1)}, u32[]{:S(2)}, u32[]{:S(2)}) collective-permute-start(f32[264,128]{1,0:T(8,128)S(1)} %add.83), channel_id=1, source_target_pairs={{0,2},{1,3},{2,0},{3,1},{4,6},{5,7},{6,4},{7,5},{8,10},{9,11},{10,... | collective-permute-start | bytes 405512 | tf_op jit(solution)/shard_map/ppermute | solution.py:500
  43.4 8.8 %collective-permute-start.15 = (f32[264,128]{1,0:T(8,128)S(1)}, f32[264,128]{1,0:T(8,128)S(1)}, u32[]{:S(2)}, u32[]{:S(2)}) collective-permute-start(f32[264,128]{1,0:T(8,128)S(1)} %add.83), channel_id=1, source_target_pairs={{0,4},{1,5},{2,6},{3,7},{4,0},{5,1},{6,2},{7,3},{8,12},{9,13},{10,... | collective-permute-start | bytes 405512 | tf_op jit(solution)/shard_map/ppermute | solution.py:500
  43.6 8.7 %collective-permute-start.14 = (f32[264,128]{1,0:T(8,128)S(1)}, f32[264,128]{1,0:T(8,128)S(1)}, u32[]{:S(2)}, u32[]{:S(2)}) collective-permute-start(f32[264,128]{1,0:T(8,128)S(1)} %add.83), channel_id=1, source_target_pairs={{0,6},{1,7},{2,4},{3,5},{4,2},{5,3},{6,0},{7,1},{8,14},{9,15},{10,... | collective-permute-start | bytes 405512 | tf_op jit(solution)/shard_map/ppermute | solution.py:500
  60.6 4.2 %collective-permute-start.18 = (f32[1056,128]{1,0:T(8,128)S(1)}, f32[1056,128]{1,0:T(8,128)S(1)}, u32[]{:S(2)}, u32[]{:S(2)}) collective-permute-start(f32[1056,128]{1,0:T(8,128)S(1)} %get-tuple-element.320), channel_id=1, source_target_pairs={{0,1},{1,0},{2,3},{3,2},{4,5},{5,4},{6,7},{7,6},{8,9},{9,8},{10,11... | collective-permute-start | bytes 1622024 | tf_op jit(solution)/shard_map/ppermute | solution.py:500
  64.9 8.5 %collective-permute-start.22 = (f32[264,128]{1,0:T(8,128)S(1)}, f32[264,128]{1,0:T(8,128)S(1)}, u32[]{:S(2)}, u32[]{:S(2)}) collective-permute-start(f32[264,128]{1,0:T(8,128)S(1)} %get-tuple-element.398), channel_id=1, source_target_pairs={{0,2},{1,3},{2,0},{3,1},{4,6},{5,7},{6,4},{7,5},{8,10},{9,11},{10,... | collective-permute-start | bytes 405512 | tf_op jit(solution)/shard_map/ppermute | solution.py:500
  65.5 9.4 %collective-permute-start.21 = (f32[264,128]{1,0:T(8,128)S(1)}, f32[264,128]{1,0:T(8,128)S(1)}, u32[]{:S(2)}, u32[]{:S(2)}) collective-permute-start(f32[264,128]{1,0:T(8,128)S(1)} %get-tuple-element.399), channel_id=1, source_target_pairs={{0,4},{1,5},{2,6},{3,7},{4,0},{5,1},{6,2},{7,3},{8,12},{9,13},{10,... | collective-permute-start | bytes 405512 | tf_op jit(solution)/shard_map/ppermute | solution.py:500
  65.6 9.3 %collective-permute-start.20 = (f32[264,128]{1,0:T(8,128)S(1)}, f32[264,128]{1,0:T(8,128)S(1)}, u32[]{:S(2)}, u32[]{:S(2)}) collective-permute-start(f32[264,128]{1,0:T(8,128)S(1)} %get-tuple-element.400), channel_id=1, source_target_pairs={{0,6},{1,7},{2,4},{3,5},{4,2},{5,3},{6,0},{7,1},{8,14},{9,15},{10,... | collective-permute-start | bytes 405512 | tf_op jit(solution)/shard_map/ppermute | solution.py:500
  68.4 2.5 %collective-permute-start.19 = (f32[1056,128]{1,0:T(8,128)S(1)}, f32[1056,128]{1,0:T(8,128)S(1)}, u32[]{:S(2)}, u32[]{:S(2)}) collective-permute-start(f32[1056,128]{1,0:T(8,128)S(1)} %get-tuple-element.326), channel_id=1, source_target_pairs={{0,1},{1,0},{2,3},{3,2},{4,5},{5,4},{6,7},{7,6},{8,9},{9,8},{10,11... | collective-permute-start | bytes 1622024 | tf_op jit(solution)/shard_map/ppermute | solution.py:500
  71.0 10.9 %collective-permute-start.25 = (f32[264,128]{1,0:T(8,128)S(1)}, f32[264,128]{1,0:T(8,128)S(1)}, u32[]{:S(2)}, u32[]{:S(2)}) collective-permute-start(f32[264,128]{1,0:T(8,128)S(1)} %get-tuple-element.395), channel_id=1, source_target_pairs={{0,6},{1,7},{2,4},{3,5},{4,2},{5,3},{6,0},{7,1},{8,14},{9,15},{10,... | collective-permute-start | bytes 405512 | tf_op jit(solution)/shard_map/ppermute | solution.py:500
  71.2 11.7 %collective-permute-start.24 = (f32[264,128]{1,0:T(8,128)S(1)}, f32[264,128]{1,0:T(8,128)S(1)}, u32[]{:S(2)}, u32[]{:S(2)}) collective-permute-start(f32[264,128]{1,0:T(8,128)S(1)} %get-tuple-element.396), channel_id=1, source_target_pairs={{0,4},{1,5},{2,6},{3,7},{4,0},{5,1},{6,2},{7,3},{8,12},{9,13},{10,... | collective-permute-start | bytes 405512 | tf_op jit(solution)/shard_map/ppermute | solution.py:500
  73.4 9.5 %collective-permute-start.23 = (f32[264,128]{1,0:T(8,128)S(1)}, f32[264,128]{1,0:T(8,128)S(1)}, u32[]{:S(2)}, u32[]{:S(2)}) collective-permute-start(f32[264,128]{1,0:T(8,128)S(1)} %get-tuple-element.397), channel_id=1, source_target_pairs={{0,2},{1,3},{2,0},{3,1},{4,6},{5,7},{6,4},{7,5},{8,10},{9,11},{10,... | collective-permute-start | bytes 405512 | tf_op jit(solution)/shard_map/ppermute | solution.py:500
  75.0 7.9 %collective-permute-start.26 = (f32[264,128]{1,0:T(8,128)S(1)}, f32[264,128]{1,0:T(8,128)S(1)}, u32[]{:S(2)}, u32[]{:S(2)}) collective-permute-start(f32[264,128]{1,0:T(8,128)S(1)} %fusion.1), channel_id=1, source_target_pairs={{0,8},{1,9},{2,10},{3,11},{4,12},{5,13},{6,14},{7,15},{8,0},{9,1},... | collective-permute-start | bytes 405512 | tf_op jit(solution)/shard_map/ppermute | solution.py:500
  82.9 6.4 %collective-permute-start.27 = (f32[264,128]{1,0:T(8,128)S(1)}, f32[264,128]{1,0:T(8,128)S(1)}, u32[]{:S(2)}, u32[]{:S(2)}) collective-permute-start(f32[264,128]{1,0:T(8,128)S(1)} %add.92), channel_id=1, source_target_pairs={{0,4},{1,5},{2,6},{3,7},{4,0},{5,1},{6,2},{7,3},{8,12},{9,13},{10,... | collective-permute-start | bytes 405512 | tf_op jit(solution)/shard_map/ppermute | solution.py:500
  85.3 8.6 %collective-permute-start.28 = (f32[264,128]{1,0:T(8,128)S(1)}, f32[264,128]{1,0:T(8,128)S(1)}, u32[]{:S(2)}, u32[]{:S(2)}) collective-permute-start(f32[264,128]{1,0:T(8,128)S(1)} %fusion.3), channel_id=1, source_target_pairs={{0,8},{1,9},{2,10},{3,11},{4,12},{5,13},{6,14},{7,15},{8,0},{9,1},... | collective-permute-start | bytes 405512 | tf_op jit(solution)/shard_map/ppermute | solution.py:500
  87.4 10.0 %collective-permute-start.30 = (f32[264,128]{1,0:T(8,128)S(1)}, f32[264,128]{1,0:T(8,128)S(1)}, u32[]{:S(2)}, u32[]{:S(2)}) collective-permute-start(f32[264,128]{1,0:T(8,128)S(1)} %add.92), channel_id=1, source_target_pairs={{0,2},{1,3},{2,0},{3,1},{4,6},{5,7},{6,4},{7,5},{8,10},{9,11},{10,... | collective-permute-start | bytes 405512 | tf_op jit(solution)/shard_map/ppermute | solution.py:500
  89.3 8.2 %collective-permute-start.29 = (f32[264,128]{1,0:T(8,128)S(1)}, f32[264,128]{1,0:T(8,128)S(1)}, u32[]{:S(2)}, u32[]{:S(2)}) collective-permute-start(f32[264,128]{1,0:T(8,128)S(1)} %collective-permute-done.27), channel_id=1, source_target_pairs={{0,2},{1,3},{2,0},{3,1},{4,6},{5,7},{6,4},{7,5},{8,10},{9,11},{10,... | collective-permute-start | bytes 405512 | tf_op jit(solution)/shard_map/ppermute | solution.py:500
  93.9 7.8 %collective-permute-start.34 = (f32[264,128]{1,0:T(8,128)S(1)}, f32[264,128]{1,0:T(8,128)S(1)}, u32[]{:S(2)}, u32[]{:S(2)}) collective-permute-start(f32[264,128]{1,0:T(8,128)S(1)} %add.93), channel_id=1, source_target_pairs={{0,2},{1,3},{2,0},{3,1},{4,6},{5,7},{6,4},{7,5},{8,10},{9,11},{10,... | collective-permute-start | bytes 405512 | tf_op jit(solution)/shard_map/ppermute | solution.py:500
  95.2 6.4 %collective-permute-start.33 = (f32[264,128]{1,0:T(8,128)S(1)}, f32[264,128]{1,0:T(8,128)S(1)}, u32[]{:S(2)}, u32[]{:S(2)}) collective-permute-start(f32[264,128]{1,0:T(8,128)S(1)} %add.93), channel_id=1, source_target_pairs={{0,4},{1,5},{2,6},{3,7},{4,0},{5,1},{6,2},{7,3},{8,12},{9,13},{10,... | collective-permute-start | bytes 405512 | tf_op jit(solution)/shard_map/ppermute | solution.py:500
  95.2 7.6 %collective-permute-start.32 = (f32[264,128]{1,0:T(8,128)S(1)}, f32[264,128]{1,0:T(8,128)S(1)}, u32[]{:S(2)}, u32[]{:S(2)}) collective-permute-start(f32[264,128]{1,0:T(8,128)S(1)} %add.93), channel_id=1, source_target_pairs={{0,6},{1,7},{2,4},{3,5},{4,2},{5,3},{6,0},{7,1},{8,14},{9,15},{10,... | collective-permute-start | bytes 405512 | tf_op jit(solution)/shard_map/ppermute | solution.py:500
  (10 other events, 63.4 us)

commit v17 on v14

--- a/solution.py
+++ b/solution.py
@@ -184,11 +184,8 @@
             start(step + 2)
         ah[:, r], al[:, r] = split(a_buf[r].T)
         bh[r], bl[r] = split(b_buf[r])
-        for r0, r1, c0, c1 in [(0, q, 0, size), (q, size, 0, q), (3 * q, size, 3 * q, size)]:
-            product = mm((ah[r0:r1, r], al[r0:r1, r]), (bh[r, c0:c1], bl[r, c0:c1]))
-            if step:
-                product += g[r0:r1, c0:c1]
-            g[r0:r1, c0:c1] = product
+    for r0, r1, c0, c1 in [(0, size, 0, q), (0, q, q, size), (3 * q, size, 3 * q, size)]:
+        g[r0:r1, c0:c1] = mm((ah[r0:r1, :], al[r0:r1, :]), (bh[:, c0:c1], bl[:, c0:c1]))
     pack(g, packed, keep_ref, send_ref, me_ref[0], shards, 0)
 
 

time: 108 us -> 109 us (level)
  no operation moved by 1% of the time
where the time goes in v17:
time: 109 us; the launch traced here: 108 us
  Pallas kernels  55.1 us (51%)
  starting transfers between devices  38.9 us (36%)
  waiting for transfers between devices  13.1 us (12%)
    ppermute x36, starting transfers between devices, swap(): return lax.ppermute(x, 'row', [(i, i ^ offset) for i in range(self.count)])  38.9 us
    ppermute x36, waiting for transfers between devices, swap(): return lax.ppermute(x, 'row', [(i, i ^ offset) for i in range(self.count)])  13.1 us
    pallas_call x2, Pallas kernels, affine(): call(functools.partial(affine_kernel, part), 'affine', struct(height, siz...  8.57 us
    pallas_call x2, Pallas kernels, affine_parts(): call(functools.partial(affine_parts_kernel, part), 'affine_parts', struct...  7.87 us
    pallas_call x1, Pallas kernels, first_gram(): call(functools.partial(first_gram_kernel, shards), 'first_gram', halves(s...  7.64 us
    pallas_call x1, Pallas kernels, second_gram(): call(functools.partial(second_gram_kernel, shards, len(pieces)), 'second_...  6.15 us
    pallas_call x2, Pallas kernels, first_part(): call(functools.partial(first_part_kernel, shards, len(pieces), columns),...  5.92 us
    pallas_call x1, Pallas kernels, last_step(): call(functools.partial(last_kernel, shards, len(pieces)), 'last', struct(...  4.89 us
  transfers between devices with their start and end apart: 36, of which 9 were waited for; matrix products, arithmetic and copies ran while one was open for 0% of the time, Pallas kernels for 34%

profile of v17, /device:TPU:0, one launch (start us, length us, event | category | flops | bytes accessed | tf_op | source)
XLA Modules:
  0.0 108.4 jit_solution(7130029528688729654)
XLA Ops:
  0.0 7.6 %first_gram.1 = (f32[1056,128]{1,0:T(8,128)S(1)}, f32[1056,128]{1,0:T(8,128)S(1)}, bf16[1024,1024]{1,0:T(8,128)(2,1)S(1)}, bf16[1024,1024]{1,0:T(8,128)(2,1)S(1)...) custom-call(s32[1]{0:T(128)} %bitcast.me_ref, f32[1024,1024]{1,0:T(8,128)} %x_ref, f32[1024,1024]{1,0:T(8,128)} %a_ref.1), custom_call_target="tpu_custom_call" | custom-call | flops 32212254720 | bytes 167772160 | tf_op jit(solution)/shard_map/first_gram/pallas_call | solution.py:195
  8.2 3.6 %other_gram.1 = (f32[1056,128]{1,0:T(8,128)S(1)}, f32[1056,128]{1,0:T(8,128)S(1)}) custom-call(s32[1]{0:T(128)} %bitcast.me_ref, bf16[1024,1024]{1,0:T(8,128)(2,1)S(1)} %get-tuple-element.184.ah, bf16[1024,1024]{1,0:T(8,128)(2,1)S(1)} %get-tuple-element.185.al, bf16[1024,1024]{1,0:T(8,128)(2,1)S(1)} %get-tuple-element.186.bh, ...), custom_call_target="tpu_custom_call" | custom-call | flops 32212254720 | bytes 83886080 | tf_op jit(solution)/shard_map/other_gram/pallas_call | solution.py:225
  11.9 2.6 %collective-permute-start.4 = (f32[264,128]{1,0:T(8,128)S(1)}, f32[264,128]{1,0:T(8,128)S(1)}, u32[]{:S(2)}, u32[]{:S(2)}) collective-permute-start(f32[264,128]{1,0:T(8,128)S(1)} %get-tuple-element.372), channel_id=1, source_target_pairs={{0,2},{1,3},{2,0},{3,1},{4,6},{5,7},{6,4},{7,5},{8,10},{9,11},{10,... | collective-permute-start | bytes 405512 | tf_op jit(solution)/shard_map/ppermute | solution.py:497
  14.6 1.6 %collective-permute-start.3 = (f32[264,128]{1,0:T(8,128)S(1)}, f32[264,128]{1,0:T(8,128)S(1)}, u32[]{:S(2)}, u32[]{:S(2)}) collective-permute-start(f32[264,128]{1,0:T(8,128)S(1)} %get-tuple-element.373), channel_id=1, source_target_pairs={{0,4},{1,5},{2,6},{3,7},{4,0},{5,1},{6,2},{7,3},{8,12},{9,13},{10,... | collective-permute-start | bytes 405512 | tf_op jit(solution)/shard_map/ppermute | solution.py:497
  16.2 2.8 %affine.2.refs_4_ = f32[256,1024]{1,0:T(8,128)S(1)} custom-call(f32[1024,1024]{1,0:T(8,128)S(1)} %copy-done.1, f32[1024,1024]{1,0:T(8,128)S(1)} %copy-done.2), custom_call_target="tpu_custom_call" | custom-call | flops 16106127360 | bytes 83886080 | tf_op jit(solution)/shard_map/affine/pallas_call | solution.py:258
  19.0 3.0 %collective-permute-start.7 = (f32[264,128]{1,0:T(8,128)S(1)}, f32[264,128]{1,0:T(8,128)S(1)}, u32[]{:S(2)}, u32[]{:S(2)}) collective-permute-start(f32[264,128]{1,0:T(8,128)S(1)} %get-tuple-element.369), channel_id=1, source_target_pairs={{0,6},{1,7},{2,4},{3,5},{4,2},{5,3},{6,0},{7,1},{8,14},{9,15},{10,... | collective-permute-start | bytes 405512 | tf_op jit(solution)/shard_map/ppermute | solution.py:497
  23.5 3.0 %collective-permute-start.8 = (f32[264,128]{1,0:T(8,128)S(1)}, f32[264,128]{1,0:T(8,128)S(1)}, u32[]{:S(2)}, u32[]{:S(2)}) collective-permute-start(f32[264,128]{1,0:T(8,128)S(1)} %fusion.7), channel_id=1, source_target_pairs={{0,8},{1,9},{2,10},{3,11},{4,12},{5,13},{6,14},{7,15},{8,0},{9,1},... | collective-permute-start | bytes 405512 | tf_op jit(solution)/shard_map/ppermute | solution.py:497
  26.5 5.8 %affine.3.refs_5_ = f32[768,1024]{1,0:T(8,128)S(1)} custom-call(f32[1024,1024]{1,0:T(8,128)S(1)} %copy-done.1, f32[1024,1024]{1,0:T(8,128)S(1)} %copy-done.2), custom_call_target="tpu_custom_call" | custom-call | flops 48318382080 | bytes 83886080 | tf_op jit(solution)/shard_map/affine/pallas_call | solution.py:258
  34.4 1.6 %collective-permute-start.11 = (f32[264,128]{1,0:T(8,128)S(1)}, f32[264,128]{1,0:T(8,128)S(1)}, u32[]{:S(2)}, u32[]{:S(2)}) collective-permute-start(f32[264,128]{1,0:T(8,128)S(1)} %add.82), channel_id=1, source_target_pairs={{0,4},{1,5},{2,6},{3,7},{4,0},{5,1},{6,2},{7,3},{8,12},{9,13},{10,... | collective-permute-start | bytes 405512 | tf_op jit(solution)/shard_map/ppermute | solution.py:497
  37.3 4.2 %collective-permute-done.9 = f32[264,128]{1,0:T(8,128)S(1)} collective-permute-done((f32[264,128]{1,0:T(8,128)S(1)}, f32[264,128]{1,0:T(8,128)S(1)}, u32[]{:S(2)}, u32[]{:S(2)}) %collective-permute-start.9) | collective-permute-done | bytes 135200 | tf_op jit(solution)/shard_map/ppermute | solution.py:497
  41.5 1.3 %collective-permute-start.16 = (f32[264,128]{1,0:T(8,128)S(1)}, f32[264,128]{1,0:T(8,128)S(1)}, u32[]{:S(2)}, u32[]{:S(2)}) collective-permute-start(f32[264,128]{1,0:T(8,128)S(1)} %add.83), channel_id=1, source_target_pairs={{0,2},{1,3},{2,0},{3,1},{4,6},{5,7},{6,4},{7,5},{8,10},{9,11},{10,... | collective-permute-start | bytes 405512 | tf_op jit(solution)/shard_map/ppermute | solution.py:497
  43.1 1.9 %collective-permute-start.14 = (f32[264,128]{1,0:T(8,128)S(1)}, f32[264,128]{1,0:T(8,128)S(1)}, u32[]{:S(2)}, u32[]{:S(2)}) collective-permute-start(f32[264,128]{1,0:T(8,128)S(1)} %add.83), channel_id=1, source_target_pairs={{0,6},{1,7},{2,4},{3,5},{4,2},{5,3},{6,0},{7,1},{8,14},{9,15},{10,... | collective-permute-start | bytes 405512 | tf_op jit(solution)/shard_map/ppermute | solution.py:497
  46.1 1.5 %turn.1 = (bf16[1024,1024]{1,0:T(8,128)(2,1)S(1)}, bf16[1024,1024]{1,0:T(8,128)(2,1)S(1)}) custom-call(f32[1024,1024]{1,0:T(8,128)S(1)} %copy-done.4), custom_call_target="tpu_custom_call" | custom-call | flops 6442450944 | bytes 83886080 | tf_op jit(solution)/shard_map/turn/pallas_call | solution.py:379
  48.1 3.8 %first_part.2.mid_ref.refs_4_ = f32[1024,1024]{1,0:T(8,128)S(1)} custom-call(s32[1]{0:T(128)} %bitcast.me_ref, f32[1056,128]{1,0:T(8,128)S(1)} %pad_maximum_fusion.refs_0_, f32[1056,128]{1,0:T(8,128)S(1)} %collective-permute-done.13.refs_1_, bf16[1024,1024]{1,0:T(8,128)(2,1)S(1)} %get-tuple-element.281.refs_2_, ...), custom_call_target="tpu_custom_call" | custom-call | flops 32212254720 | bytes 125829120 | tf_op jit(solution)/shard_map/first_part/pallas_call | solution.py:333
  52.1 1.8 %column_product.1.refs_7_ = f32[1024,256]{1,0:T(8,128)S(1)} custom-call(bf16[1024,1024]{1,0:T(8,128)(2,1)S(1)} %get-tuple-element.283.xh.refs_5_, bf16[1024,1024]{1,0:T(8,128)(2,1)S(1)} %get-tuple-element.284.xl.refs_6_, f32[1024,1024]{1,0:T(8,128)S(1)} %first_part.2.mid_ref.refs_4_), custom_call_target="tpu_custom_call" | custom-call | flops 16106127360 | bytes 83886080 | tf_op jit(solution)/shard_map/column_product/pallas_call | solution.py:364
  53.9 6.2 %second_gram.1 = (f32[1056,128]{1,0:T(8,128)S(1)}, f32[1056,128]{1,0:T(8,128)S(1)}, bf16[1024,1024]{1,0:T(8,128)(2,1)S(1)}, bf16[1024,1024]{1,0:T(8,128)(2,1)S(1)}) custom-call(s32[1]{0:T(128)} %bitcast.me_ref, f32[1056,128]{1,0:T(8,128)S(1)} %pad_maximum_fusion.1.refs_0_, f32[1056,128]{1,0:T(8,128)S(1)} %collective-permute-done.17.refs_1_, ...), custom_call_target="tpu_custom_call" | custom-call | flops 51539607552 | bytes 209715200 | tf_op jit(solution)/shard_map/second_gram/pallas_call | solution.py:422
  60.5 3.9 %fourth_gram.1 = (f32[1056,128]{1,0:T(8,128)S(1)}, f32[1056,128]{1,0:T(8,128)S(1)}) custom-call(s32[1]{0:T(128)} %bitcast.me_ref, bf16[1024,1024]{1,0:T(8,128)(2,1)S(1)} %get-tuple-element.283.xh.refs_5_, bf16[1024,1024]{1,0:T(8,128)(2,1)S(1)} %get-tuple-element.284.xl.refs_6_, bf16[1024,1024]{1,0:T(8,128)(2,1)S(1)} %get-tuple-element.309.mh.ah, ...), custom_call_target="tpu_custom_call" | custom-call | flops 32212254720 | bytes 83886080 | tf_op jit(solution)/shard_map/fourth_gram/pallas_call | solution.py:439
  65.4 2.6 %collective-permute-start.20 = (f32[264,128]{1,0:T(8,128)S(1)}, f32[264,128]{1,0:T(8,128)S(1)}, u32[]{:S(2)}, u32[]{:S(2)}) collective-permute-start(f32[264,128]{1,0:T(8,128)S(1)} %get-tuple-element.368), channel_id=1, source_target_pairs={{0,6},{1,7},{2,4},{3,5},{4,2},{5,3},{6,0},{7,1},{8,14},{9,15},{10,... | collective-permute-start | bytes 405512 | tf_op jit(solution)/shard_map/ppermute | solution.py:497
  68.1 2.5 %affine_parts.2.refs_4_.refs_0_ = f32[256,1024]{1,0:T(8,128)S(1)} custom-call(bf16[1024,1024]{1,0:T(8,128)(2,1)S(1)} %get-tuple-element.309.mh.ah, bf16[1024,1024]{1,0:T(8,128)(2,1)S(1)} %get-tuple-element.310.ml.al, f32[1024,1024]{1,0:T(8,128)S(1)} %copy-done.3), custom_call_target="tpu_custom_call" | custom-call | flops 16106127360 | bytes 83886080 | tf_op jit(solution)/shard_map/affine_parts/pallas_call | solution.py:280
  71.0 2.0 %collective-permute-start.24 = (f32[264,128]{1,0:T(8,128)S(1)}, f32[264,128]{1,0:T(8,128)S(1)}, u32[]{:S(2)}, u32[]{:S(2)}) collective-permute-start(f32[264,128]{1,0:T(8,128)S(1)} %get-tuple-element.364), channel_id=1, source_target_pairs={{0,4},{1,5},{2,6},{3,7},{4,0},{5,1},{6,2},{7,3},{8,12},{9,13},{10,... | collective-permute-start | bytes 405512 | tf_op jit(solution)/shard_map/ppermute | solution.py:497
  74.6 1.7 %collective-permute-start.26 = (f32[264,128]{1,0:T(8,128)S(1)}, f32[264,128]{1,0:T(8,128)S(1)}, u32[]{:S(2)}, u32[]{:S(2)}) collective-permute-start(f32[264,128]{1,0:T(8,128)S(1)} %fusion.1), channel_id=1, source_target_pairs={{0,8},{1,9},{2,10},{3,11},{4,12},{5,13},{6,14},{7,15},{8,0},{9,1},... | collective-permute-start | bytes 405512 | tf_op jit(solution)/shard_map/ppermute | solution.py:497
  76.3 5.4 %affine_parts.3.refs_5_.refs_1_ = f32[768,1024]{1,0:T(8,128)S(1)} custom-call(bf16[1024,1024]{1,0:T(8,128)(2,1)S(1)} %get-tuple-element.309.mh.ah, bf16[1024,1024]{1,0:T(8,128)(2,1)S(1)} %get-tuple-element.310.ml.al, f32[1024,1024]{1,0:T(8,128)S(1)} %copy-done.3), custom_call_target="tpu_custom_call" | custom-call | flops 48318382080 | bytes 83886080 | tf_op jit(solution)/shard_map/affine_parts/pallas_call | solution.py:280
  84.2 3.1 %collective-permute-start.29 = (f32[264,128]{1,0:T(8,128)S(1)}, f32[264,128]{1,0:T(8,128)S(1)}, u32[]{:S(2)}, u32[]{:S(2)}) collective-permute-start(f32[264,128]{1,0:T(8,128)S(1)} %add.93), channel_id=1, source_target_pairs={{0,4},{1,5},{2,6},{3,7},{4,0},{5,1},{6,2},{7,3},{8,12},{9,13},{10,... | collective-permute-start | bytes 405512 | tf_op jit(solution)/shard_map/ppermute | solution.py:497
  87.3 1.4 %collective-permute-start.28 = (f32[264,128]{1,0:T(8,128)S(1)}, f32[264,128]{1,0:T(8,128)S(1)}, u32[]{:S(2)}, u32[]{:S(2)}) collective-permute-start(f32[264,128]{1,0:T(8,128)S(1)} %add.93), channel_id=1, source_target_pairs={{0,6},{1,7},{2,4},{3,5},{4,2},{5,3},{6,0},{7,1},{8,14},{9,15},{10,... | collective-permute-start | bytes 405512 | tf_op jit(solution)/shard_map/ppermute | solution.py:497
  88.7 2.9 %collective-permute-done.27 = f32[264,128]{1,0:T(8,128)S(1)} collective-permute-done((f32[264,128]{1,0:T(8,128)S(1)}, f32[264,128]{1,0:T(8,128)S(1)}, u32[]{:S(2)}, u32[]{:S(2)}) %collective-permute-start.27) | collective-permute-done | bytes 135200 | tf_op jit(solution)/shard_map/ppermute | solution.py:497
  91.7 1.6 %collective-permute-start.34 = (f32[264,128]{1,0:T(8,128)S(1)}, f32[264,128]{1,0:T(8,128)S(1)}, u32[]{:S(2)}, u32[]{:S(2)}) collective-permute-start(f32[264,128]{1,0:T(8,128)S(1)} %add.92), channel_id=1, source_target_pairs={{0,2},{1,3},{2,0},{3,1},{4,6},{5,7},{6,4},{7,5},{8,10},{9,11},{10,... | collective-permute-start | bytes 405512 | tf_op jit(solution)/shard_map/ppermute | solution.py:497
  93.3 2.0 %collective-permute-start.32 = (f32[264,128]{1,0:T(8,128)S(1)}, f32[264,128]{1,0:T(8,128)S(1)}, u32[]{:S(2)}, u32[]{:S(2)}) collective-permute-start(f32[264,128]{1,0:T(8,128)S(1)} %add.92), channel_id=1, source_target_pairs={{0,6},{1,7},{2,4},{3,5},{4,2},{5,3},{6,0},{7,1},{8,14},{9,15},{10,... | collective-permute-start | bytes 405512 | tf_op jit(solution)/shard_map/ppermute | solution.py:497
  96.2 1.5 %collective-permute-done.31.refs_1_ = f32[1056,128]{1,0:T(8,128)S(1)} collective-permute-done((f32[1056,128]{1,0:T(8,128)S(1)}, f32[1056,128]{1,0:T(8,128)S(1)}, u32[]{:S(2)}, u32[]{:S(2)}) %collective-permute-start.31) | collective-permute-done | bytes 540704 | tf_op jit(solution)/shard_map/ppermute | solution.py:497
  97.6 2.2 %first_part.3 = (f32[1024,256]{1,0:T(8,128)S(1)}, bf16[1024,1024]{1,0:T(8,128)(2,1)S(1)}, bf16[1024,1024]{1,0:T(8,128)(2,1)S(1)}) custom-call(s32[1]{0:T(128)} %bitcast.me_ref, f32[1056,128]{1,0:T(8,128)S(1)} %pad_maximum_fusion.2.refs_0_, f32[1056,128]{1,0:T(8,128)S(1)} %collective-permute-done.31.refs_1_, bf16[1024,1024]{1,0:T(8,128)(2,1)S(1)} %cut.4.refs_2_.ah, ...), custom_call_target="tpu_custom_call" | custom-call | flops 32212254720 | bytes 125829120 | tf_op jit(solution)/shard_map/first_part/pallas_call | solution.py:333
  99.8 1.5 %collective-permute-done.32 = f32[264,128]{1,0:T(8,128)S(1)} collective-permute-done((f32[264,128]{1,0:T(8,128)S(1)}, f32[264,128]{1,0:T(8,128)S(1)}, u32[]{:S(2)}, u32[]{:S(2)}) %collective-permute-start.32) | collective-permute-done | bytes 135200 | tf_op jit(solution)/shard_map/ppermute | solution.py:497
  101.5 1.8 %other_part.1.refs_5_ = f32[1024,768]{1,0:T(8,128)S(1)} custom-call(bf16[1024,1024]{1,0:T(8,128)(2,1)S(1)} %cut.4.refs_2_.ah, bf16[1024,1024]{1,0:T(8,128)(2,1)S(1)} %cut.5.refs_3_.al, bf16[1024,1024]{1,0:T(8,128)(2,1)S(1)} %get-tuple-element.356.hi, bf16[1024,1024]{1,0:T(8,128)(2,1)S(1)} %get-tuple-element.357.lo, ...), custom_call_target="tpu_custom_call" | custom-call | flops 16106127360 | bytes 125829120 | tf_op jit(solution)/shard_map/other_part/pallas_call | solution.py:348
  103.4 4.9 %last.1 = f32[1024,1024]{1,0:T(8,128)} custom-call(s32[1]{0:T(128)} %bitcast.me_ref, f32[1056,128]{1,0:T(8,128)S(1)} %pad_maximum_fusion.3.refs_0_, f32[1056,128]{1,0:T(8,128)S(1)} %collective-permute-done.35.refs_1_, bf16[1024,1024]{1,0:T(8,128)(2,1)S(1)} %cut.4.refs_2_.ah, bf16[1024,1024]{1,0:T(8,128)(2,1)S(1)} %cut.5.refs_3_.al, ...), custom_call_target="tpu_custom_call" | custom-call | flops 32212254720 | bytes 125829120 | tf_op jit(solution)/shard_map/last/pallas_call | solution.py:474
  (89 shorter events, 14.6 us)
Async XLA Ops:
  7.6 4.2 %collective-permute-start = (f32[1056,128]{1,0:T(8,128)S(1)}, f32[1056,128]{1,0:T(8,128)S(1)}, u32[]{:S(2)}, u32[]{:S(2)}) collective-permute-start(f32[1056,128]{1,0:T(8,128)S(1)} %get-tuple-element.190), channel_id=1, source_target_pairs={{0,1},{1,0},{2,3},{3,2},{4,5},{5,4},{6,7},{7,6},{8,9},{9,8},{10,11... | collective-permute-start | bytes 1622024 | tf_op jit(solution)/shard_map/ppermute | solution.py:497
  11.9 11.3 %collective-permute-start.4 = (f32[264,128]{1,0:T(8,128)S(1)}, f32[264,128]{1,0:T(8,128)S(1)}, u32[]{:S(2)}, u32[]{:S(2)}) collective-permute-start(f32[264,128]{1,0:T(8,128)S(1)} %get-tuple-element.372), channel_id=1, source_target_pairs={{0,2},{1,3},{2,0},{3,1},{4,6},{5,7},{6,4},{7,5},{8,10},{9,11},{10,... | collective-permute-start | bytes 405512 | tf_op jit(solution)/shard_map/ppermute | solution.py:497
  14.6 8.9 %collective-permute-start.3 = (f32[264,128]{1,0:T(8,128)S(1)}, f32[264,128]{1,0:T(8,128)S(1)}, u32[]{:S(2)}, u32[]{:S(2)}) collective-permute-start(f32[264,128]{1,0:T(8,128)S(1)} %get-tuple-element.373), channel_id=1, source_target_pairs={{0,4},{1,5},{2,6},{3,7},{4,0},{5,1},{6,2},{7,3},{8,12},{9,13},{10,... | collective-permute-start | bytes 405512 | tf_op jit(solution)/shard_map/ppermute | solution.py:497
  16.1 7.4 %collective-permute-start.2 = (f32[264,128]{1,0:T(8,128)S(1)}, f32[264,128]{1,0:T(8,128)S(1)}, u32[]{:S(2)}, u32[]{:S(2)}) collective-permute-start(f32[264,128]{1,0:T(8,128)S(1)} %get-tuple-element.374), channel_id=1, source_target_pairs={{0,6},{1,7},{2,4},{3,5},{4,2},{5,3},{6,0},{7,1},{8,14},{9,15},{10,... | collective-permute-start | bytes 405512 | tf_op jit(solution)/shard_map/ppermute | solution.py:497
  16.1 2.8 %collective-permute-start.1 = (f32[1056,128]{1,0:T(8,128)S(1)}, f32[1056,128]{1,0:T(8,128)S(1)}, u32[]{:S(2)}, u32[]{:S(2)}) collective-permute-start(f32[1056,128]{1,0:T(8,128)S(1)} %get-tuple-element.196), channel_id=1, source_target_pairs={{0,1},{1,0},{2,3},{3,2},{4,5},{5,4},{6,7},{7,6},{8,9},{9,8},{10,11... | collective-permute-start | bytes 1622024 | tf_op jit(solution)/shard_map/ppermute | solution.py:497
  19.0 13.3 %collective-permute-start.7 = (f32[264,128]{1,0:T(8,128)S(1)}, f32[264,128]{1,0:T(8,128)S(1)}, u32[]{:S(2)}, u32[]{:S(2)}) collective-permute-start(f32[264,128]{1,0:T(8,128)S(1)} %get-tuple-element.369), channel_id=1, source_target_pairs={{0,6},{1,7},{2,4},{3,5},{4,2},{5,3},{6,0},{7,1},{8,14},{9,15},{10,... | collective-permute-start | bytes 405512 | tf_op jit(solution)/shard_map/ppermute | solution.py:497
  22.0 10.3 %collective-permute-start.6 = (f32[264,128]{1,0:T(8,128)S(1)}, f32[264,128]{1,0:T(8,128)S(1)}, u32[]{:S(2)}, u32[]{:S(2)}) collective-permute-start(f32[264,128]{1,0:T(8,128)S(1)} %get-tuple-element.370), channel_id=1, source_target_pairs={{0,4},{1,5},{2,6},{3,7},{4,0},{5,1},{6,2},{7,3},{8,12},{9,13},{10,... | collective-permute-start | bytes 405512 | tf_op jit(solution)/shard_map/ppermute | solution.py:497
  23.2 9.1 %collective-permute-start.5 = (f32[264,128]{1,0:T(8,128)S(1)}, f32[264,128]{1,0:T(8,128)S(1)}, u32[]{:S(2)}, u32[]{:S(2)}) collective-permute-start(f32[264,128]{1,0:T(8,128)S(1)} %get-tuple-element.371), channel_id=1, source_target_pairs={{0,2},{1,3},{2,0},{3,1},{4,6},{5,7},{6,4},{7,5},{8,10},{9,11},{10,... | collective-permute-start | bytes 405512 | tf_op jit(solution)/shard_map/ppermute | solution.py:497
  23.5 9.7 %collective-permute-start.8 = (f32[264,128]{1,0:T(8,128)S(1)}, f32[264,128]{1,0:T(8,128)S(1)}, u32[]{:S(2)}, u32[]{:S(2)}) collective-permute-start(f32[264,128]{1,0:T(8,128)S(1)} %fusion.7), channel_id=1, source_target_pairs={{0,8},{1,9},{2,10},{3,11},{4,12},{5,13},{6,14},{7,15},{8,0},{9,1},... | collective-permute-start | bytes 405512 | tf_op jit(solution)/shard_map/ppermute | solution.py:497
  32.4 9.0 %collective-permute-start.9 = (f32[264,128]{1,0:T(8,128)S(1)}, f32[264,128]{1,0:T(8,128)S(1)}, u32[]{:S(2)}, u32[]{:S(2)}) collective-permute-start(f32[264,128]{1,0:T(8,128)S(1)} %fusion.5), channel_id=1, source_target_pairs={{0,8},{1,9},{2,10},{3,11},{4,12},{5,13},{6,14},{7,15},{8,0},{9,1},... | collective-permute-start | bytes 405512 | tf_op jit(solution)/shard_map/ppermute | solution.py:497
  33.2 9.9 %collective-permute-start.12 = (f32[264,128]{1,0:T(8,128)S(1)}, f32[264,128]{1,0:T(8,128)S(1)}, u32[]{:S(2)}, u32[]{:S(2)}) collective-permute-start(f32[264,128]{1,0:T(8,128)S(1)} %add.82), channel_id=1, source_target_pairs={{0,2},{1,3},{2,0},{3,1},{4,6},{5,7},{6,4},{7,5},{8,10},{9,11},{10,... | collective-permute-start | bytes 405512 | tf_op jit(solution)/shard_map/ppermute | solution.py:497
  34.4 10.6 %collective-permute-start.11 = (f32[264,128]{1,0:T(8,128)S(1)}, f32[264,128]{1,0:T(8,128)S(1)}, u32[]{:S(2)}, u32[]{:S(2)}) collective-permute-start(f32[264,128]{1,0:T(8,128)S(1)} %add.82), channel_id=1, source_target_pairs={{0,4},{1,5},{2,6},{3,7},{4,0},{5,1},{6,2},{7,3},{8,12},{9,13},{10,... | collective-permute-start | bytes 405512 | tf_op jit(solution)/shard_map/ppermute | solution.py:497
  36.0 10.0 %collective-permute-start.10 = (f32[264,128]{1,0:T(8,128)S(1)}, f32[264,128]{1,0:T(8,128)S(1)}, u32[]{:S(2)}, u32[]{:S(2)}) collective-permute-start(f32[264,128]{1,0:T(8,128)S(1)} %add.82), channel_id=1, source_target_pairs={{0,6},{1,7},{2,4},{3,5},{4,2},{5,3},{6,0},{7,1},{8,14},{9,15},{10,... | collective-permute-start | bytes 405512 | tf_op jit(solution)/shard_map/ppermute | solution.py:497
  41.5 10.4 %collective-permute-start.16 = (f32[264,128]{1,0:T(8,128)S(1)}, f32[264,128]{1,0:T(8,128)S(1)}, u32[]{:S(2)}, u32[]{:S(2)}) collective-permute-start(f32[264,128]{1,0:T(8,128)S(1)} %add.83), channel_id=1, source_target_pairs={{0,2},{1,3},{2,0},{3,1},{4,6},{5,7},{6,4},{7,5},{8,10},{9,11},{10,... | collective-permute-start | bytes 405512 | tf_op jit(solution)/shard_map/ppermute | solution.py:497
  42.7 9.1 %collective-permute-start.15 = (f32[264,128]{1,0:T(8,128)S(1)}, f32[264,128]{1,0:T(8,128)S(1)}, u32[]{:S(2)}, u32[]{:S(2)}) collective-permute-start(f32[264,128]{1,0:T(8,128)S(1)} %add.83), channel_id=1, source_target_pairs={{0,4},{1,5},{2,6},{3,7},{4,0},{5,1},{6,2},{7,3},{8,12},{9,13},{10,... | collective-permute-start | bytes 405512 | tf_op jit(solution)/shard_map/ppermute | solution.py:497
  43.1 8.8 %collective-permute-start.14 = (f32[264,128]{1,0:T(8,128)S(1)}, f32[264,128]{1,0:T(8,128)S(1)}, u32[]{:S(2)}, u32[]{:S(2)}) collective-permute-start(f32[264,128]{1,0:T(8,128)S(1)} %add.83), channel_id=1, source_target_pairs={{0,6},{1,7},{2,4},{3,5},{4,2},{5,3},{6,0},{7,1},{8,14},{9,15},{10,... | collective-permute-start | bytes 405512 | tf_op jit(solution)/shard_map/ppermute | solution.py:497
  60.1 4.3 %collective-permute-start.18 = (f32[1056,128]{1,0:T(8,128)S(1)}, f32[1056,128]{1,0:T(8,128)S(1)}, u32[]{:S(2)}, u32[]{:S(2)}) collective-permute-start(f32[1056,128]{1,0:T(8,128)S(1)} %get-tuple-element.292), channel_id=1, source_target_pairs={{0,1},{1,0},{2,3},{3,2},{4,5},{5,4},{6,7},{7,6},{8,9},{9,8},{10,11... | collective-permute-start | bytes 1622024 | tf_op jit(solution)/shard_map/ppermute | solution.py:497
  64.5 8.7 %collective-permute-start.22 = (f32[264,128]{1,0:T(8,128)S(1)}, f32[264,128]{1,0:T(8,128)S(1)}, u32[]{:S(2)}, u32[]{:S(2)}) collective-permute-start(f32[264,128]{1,0:T(8,128)S(1)} %get-tuple-element.366), channel_id=1, source_target_pairs={{0,2},{1,3},{2,0},{3,1},{4,6},{5,7},{6,4},{7,5},{8,10},{9,11},{10,... | collective-permute-start | bytes 405512 | tf_op jit(solution)/shard_map/ppermute | solution.py:497
  65.4 9.1 %collective-permute-start.21 = (f32[264,128]{1,0:T(8,128)S(1)}, f32[264,128]{1,0:T(8,128)S(1)}, u32[]{:S(2)}, u32[]{:S(2)}) collective-permute-start(f32[264,128]{1,0:T(8,128)S(1)} %get-tuple-element.367), channel_id=1, source_target_pairs={{0,4},{1,5},{2,6},{3,7},{4,0},{5,1},{6,2},{7,3},{8,12},{9,13},{10,... | collective-permute-start | bytes 405512 | tf_op jit(solution)/shard_map/ppermute | solution.py:497
  65.4 9.1 %collective-permute-start.20 = (f32[264,128]{1,0:T(8,128)S(1)}, f32[264,128]{1,0:T(8,128)S(1)}, u32[]{:S(2)}, u32[]{:S(2)}) collective-permute-start(f32[264,128]{1,0:T(8,128)S(1)} %get-tuple-element.368), channel_id=1, source_target_pairs={{0,6},{1,7},{2,4},{3,5},{4,2},{5,3},{6,0},{7,1},{8,14},{9,15},{10,... | collective-permute-start | bytes 405512 | tf_op jit(solution)/shard_map/ppermute | solution.py:497
  68.1 2.5 %collective-permute-start.19 = (f32[1056,128]{1,0:T(8,128)S(1)}, f32[1056,128]{1,0:T(8,128)S(1)}, u32[]{:S(2)}, u32[]{:S(2)}) collective-permute-start(f32[1056,128]{1,0:T(8,128)S(1)} %get-tuple-element.298), channel_id=1, source_target_pairs={{0,1},{1,0},{2,3},{3,2},{4,5},{5,4},{6,7},{7,6},{8,9},{9,8},{10,11... | collective-permute-start | bytes 1622024 | tf_op jit(solution)/shard_map/ppermute | solution.py:497
  70.7 11.1 %collective-permute-start.25 = (f32[264,128]{1,0:T(8,128)S(1)}, f32[264,128]{1,0:T(8,128)S(1)}, u32[]{:S(2)}, u32[]{:S(2)}) collective-permute-start(f32[264,128]{1,0:T(8,128)S(1)} %get-tuple-element.363), channel_id=1, source_target_pairs={{0,6},{1,7},{2,4},{3,5},{4,2},{5,3},{6,0},{7,1},{8,14},{9,15},{10,... | collective-permute-start | bytes 405512 | tf_op jit(solution)/shard_map/ppermute | solution.py:497
  71.0 11.8 %collective-permute-start.24 = (f32[264,128]{1,0:T(8,128)S(1)}, f32[264,128]{1,0:T(8,128)S(1)}, u32[]{:S(2)}, u32[]{:S(2)}) collective-permute-start(f32[264,128]{1,0:T(8,128)S(1)} %get-tuple-element.364), channel_id=1, source_target_pairs={{0,4},{1,5},{2,6},{3,7},{4,0},{5,1},{6,2},{7,3},{8,12},{9,13},{10,... | collective-permute-start | bytes 405512 | tf_op jit(solution)/shard_map/ppermute | solution.py:497
  73.3 9.5 %collective-permute-start.23 = (f32[264,128]{1,0:T(8,128)S(1)}, f32[264,128]{1,0:T(8,128)S(1)}, u32[]{:S(2)}, u32[]{:S(2)}) collective-permute-start(f32[264,128]{1,0:T(8,128)S(1)} %get-tuple-element.365), channel_id=1, source_target_pairs={{0,2},{1,3},{2,0},{3,1},{4,6},{5,7},{6,4},{7,5},{8,10},{9,11},{10,... | collective-permute-start | bytes 405512 | tf_op jit(solution)/shard_map/ppermute | solution.py:497
  74.6 8.5 %collective-permute-start.26 = (f32[264,128]{1,0:T(8,128)S(1)}, f32[264,128]{1,0:T(8,128)S(1)}, u32[]{:S(2)}, u32[]{:S(2)}) collective-permute-start(f32[264,128]{1,0:T(8,128)S(1)} %fusion.1), channel_id=1, source_target_pairs={{0,8},{1,9},{2,10},{3,11},{4,12},{5,13},{6,14},{7,15},{8,0},{9,1},... | collective-permute-start | bytes 405512 | tf_op jit(solution)/shard_map/ppermute | solution.py:497
  82.8 8.9 %collective-permute-start.27 = (f32[264,128]{1,0:T(8,128)S(1)}, f32[264,128]{1,0:T(8,128)S(1)}, u32[]{:S(2)}, u32[]{:S(2)}) collective-permute-start(f32[264,128]{1,0:T(8,128)S(1)} %fusion.3), channel_id=1, source_target_pairs={{0,8},{1,9},{2,10},{3,11},{4,12},{5,13},{6,14},{7,15},{8,0},{9,1},... | collective-permute-start | bytes 405512 | tf_op jit(solution)/shard_map/ppermute | solution.py:497
  83.2 10.1 %collective-permute-start.30 = (f32[264,128]{1,0:T(8,128)S(1)}, f32[264,128]{1,0:T(8,128)S(1)}, u32[]{:S(2)}, u32[]{:S(2)}) collective-permute-start(f32[264,128]{1,0:T(8,128)S(1)} %add.93), channel_id=1, source_target_pairs={{0,2},{1,3},{2,0},{3,1},{4,6},{5,7},{6,4},{7,5},{8,10},{9,11},{10,... | collective-permute-start | bytes 405512 | tf_op jit(solution)/shard_map/ppermute | solution.py:497
  84.2 11.1 %collective-permute-start.29 = (f32[264,128]{1,0:T(8,128)S(1)}, f32[264,128]{1,0:T(8,128)S(1)}, u32[]{:S(2)}, u32[]{:S(2)}) collective-permute-start(f32[264,128]{1,0:T(8,128)S(1)} %add.93), channel_id=1, source_target_pairs={{0,4},{1,5},{2,6},{3,7},{4,0},{5,1},{6,2},{7,3},{8,12},{9,13},{10,... | collective-permute-start | bytes 405512 | tf_op jit(solution)/shard_map/ppermute | solution.py:497
  87.3 8.3 %collective-permute-start.28 = (f32[264,128]{1,0:T(8,128)S(1)}, f32[264,128]{1,0:T(8,128)S(1)}, u32[]{:S(2)}, u32[]{:S(2)}) collective-permute-start(f32[264,128]{1,0:T(8,128)S(1)} %add.93), channel_id=1, source_target_pairs={{0,6},{1,7},{2,4},{3,5},{4,2},{5,3},{6,0},{7,1},{8,14},{9,15},{10,... | collective-permute-start | bytes 405512 | tf_op jit(solution)/shard_map/ppermute | solution.py:497
  91.7 8.1 %collective-permute-start.34 = (f32[264,128]{1,0:T(8,128)S(1)}, f32[264,128]{1,0:T(8,128)S(1)}, u32[]{:S(2)}, u32[]{:S(2)}) collective-permute-start(f32[264,128]{1,0:T(8,128)S(1)} %add.92), channel_id=1, source_target_pairs={{0,2},{1,3},{2,0},{3,1},{4,6},{5,7},{6,4},{7,5},{8,10},{9,11},{10,... | collective-permute-start | bytes 405512 | tf_op jit(solution)/shard_map/ppermute | solution.py:497
  93.3 6.5 %collective-permute-start.33 = (f32[264,128]{1,0:T(8,128)S(1)}, f32[264,128]{1,0:T(8,128)S(1)}, u32[]{:S(2)}, u32[]{:S(2)}) collective-permute-start(f32[264,128]{1,0:T(8,128)S(1)} %add.92), channel_id=1, source_target_pairs={{0,4},{1,5},{2,6},{3,7},{4,0},{5,1},{6,2},{7,3},{8,12},{9,13},{10,... | collective-permute-start | bytes 405512 | tf_op jit(solution)/shard_map/ppermute | solution.py:497
  93.3 8.1 %collective-permute-start.32 = (f32[264,128]{1,0:T(8,128)S(1)}, f32[264,128]{1,0:T(8,128)S(1)}, u32[]{:S(2)}, u32[]{:S(2)}) collective-permute-start(f32[264,128]{1,0:T(8,128)S(1)} %add.92), channel_id=1, source_target_pairs={{0,6},{1,7},{2,4},{3,5},{4,2},{5,3},{6,0},{7,1},{8,14},{9,15},{10,... | collective-permute-start | bytes 405512 | tf_op jit(solution)/shard_map/ppermute | solution.py:497
  (10 other events, 62.4 us)
